TPU v7x, 32 devices: a whole 2x2x4 slice. The times are simulated.
32 devices in a mesh: grp: 2 (over x), seq: 8 (over z, y), col: 2 (over core).
Axes of the slice: x: 2, y: 2, z: 4, core: 2. Of those that a mesh axis runs over, the one named last changes fastest.
Arguments:
- signal: bfloat16 [8192, 1408], P(('grp', 'seq'), 'col'), parts along dimension 0, may hold values from -6 to 6
- conv_weight: bfloat16 [5, 1408, 1408], P(None, None, 'col'), may hold values from -0.15625 to 0.15625
- conv_gain: float32 [1408], replicated, may hold values from 0.1 to 1.9
- embed_weight: bfloat16 [1408, 1536], P('col', 'seq'), may hold values from -0.15625 to 0.15625
- attn_gain: float32 [1536], replicated, may hold values from 0.1 to 1.9
- query_weight: bfloat16 [1536, 1024], P('seq'), may hold values from -4 to 4
- keyvalue_weight: bfloat16 [1536, 320], P('seq'), may hold values from -4 to 4
- output_weight: bfloat16 [1536, 1536], P(None, 'seq'), may hold values from -0.15625 to 0.15625
- rowcol_weight: bfloat16 [1536, 256], replicated, may hold values from -0.15625 to 0.15625
- pair_weight: bfloat16 [128, 128], replicated, may hold values from -0.5 to 0.5
Outputs:
- tokens: bfloat16 [2048, 1536], P(('grp', 'seq', 'col')), parts along dimension 0
- pair_out: bfloat16 [128, 64, 128], P(('grp', 'seq'), 'col'), parts along dimension 0
There are 2 independent parts, one for each index of `grp`. A program takes and returns all parts, laid end to end along the dimension named above; an argument that names none is the same for every part. Nothing has to cross between parts.
All inputs are finite; a program needn't handle non-finite values.
Results may differ from a plain program's by a relative error of at most 0.015.
Values may be sent and summed in bfloat16 or wider, within the bound.
No kernel may reach another device: no remote copies, remote signals or barrier semaphores. Data moves between devices by JAX's collectives and lax.ppermute only.
A program may use at most 128 MiB of HBM per device.

v0:
```python
import jax
import jax.numpy as jnp
from jax import lax
from jax.sharding import PartitionSpec as P

DK = 128
DV = 192
POOL = 4
PAIR_POOL = 16


def with_halo(array, sides, width):
    for axis, dim in sides:
        size, length = (lax.axis_size(axis), array.shape[dim])
        up = [(i, (i + 1) % size) for i in range(size - 1)]
        down = [(j, i) for i, j in up]
        last = lax.slice_in_dim(array, length - width, length, axis=dim)
        first = lax.slice_in_dim(array, 0, width, axis=dim)
        before = lax.ppermute(last, axis, up)
        after = lax.ppermute(first, axis, down)
        array = jnp.concatenate([before, array, after], axis=dim)
    return array


def rms_scale(values, gain_vector):
    return (
        values * lax.rsqrt(jnp.mean(values * values, axis=-1, keepdims=True) + 1e-06) * gain_vector
    )


def attention_parts(queries, head_count):
    query_rows = queries.reshape(queries.shape[0] * head_count, DK)

    def absorb(running, pieces, first_row):
        running_max, running_sum, accumulated = running
        key_piece, value_piece = pieces
        scores = lax.dot_general(
            query_rows, key_piece, (((1,), (1,)), ((), ())), preferred_element_type=jnp.float32
        )
        newest_max = jnp.maximum(running_max, jnp.max(scores, axis=1))
        weights = jnp.exp(scores - newest_max[:, None])
        running_sum = jnp.sum(weights, axis=1)
        accumulated = jnp.dot(
            weights.astype(jnp.bfloat16), value_piece, preferred_element_type=jnp.float32
        )
        return (newest_max, running_sum, accumulated)

    row_count = query_rows.shape[0]
    initial = (
        jnp.full((row_count,), -1e30, jnp.float32),
        jnp.zeros((row_count,), jnp.float32),
        jnp.zeros((row_count, DV), jnp.float32),
    )
    return (absorb, initial)


def finish_attention(result, token_count):
    running_max, running_sum, accumulated = result
    return (accumulated / running_sum[:, None]).astype(jnp.bfloat16).reshape(token_count, -1)


def on_device(
    signal,
    conv_weight,
    conv_gain,
    embed_weight,
    attn_gain,
    query_weight,
    keyvalue_weight,
    output_weight,
    rowcol_weight,
    pair_weight,
):
    positions = signal.shape[0]
    tap_count = conv_weight.shape[0]
    halo_width = tap_count // 2
    padded = with_halo(signal, (("seq", 0),), halo_width)
    widened = lax.all_gather(padded, "col", axis=1, tiled=True)
    activated = jax.nn.gelu(
        rms_scale(widened.astype(jnp.float32), conv_gain), approximate=True
    ).astype(jnp.bfloat16)
    summed = signal.astype(jnp.float32)
    for tap_index in range(tap_count):
        summed = summed + jnp.dot(
            activated[tap_index : tap_index + positions],
            conv_weight[tap_index],
            preferred_element_type=jnp.float32,
        )
    pooled = jnp.mean(summed.reshape(positions // POOL, POOL, -1), axis=1).astype(jnp.bfloat16)
    embed_full = lax.all_gather(embed_weight, "seq", axis=1, tiled=True)
    col_count = lax.axis_size("col")
    embedded = lax.psum_scatter(
        jnp.dot(pooled, embed_full, preferred_element_type=jnp.float32).astype(jnp.bfloat16),
        "col",
        scatter_dimension=0,
        tiled=True,
    )
    normed = rms_scale(embedded.astype(jnp.float32), attn_gain).astype(jnp.bfloat16)
    head_count = query_weight.shape[1] // DK
    scaling = DK ** (-0.5)
    col_index = lax.axis_index("col")
    local_heads = head_count // col_count
    group_tokens = lax.all_gather(normed, "col", axis=0, tiled=True)
    group_count = group_tokens.shape[0]
    query_half = lax.dynamic_slice_in_dim(
        query_weight, col_index * local_heads * DK, local_heads * DK, 1
    )
    query_sum = jnp.dot(
        group_tokens,
        lax.all_gather(query_half, "seq", axis=0, tiled=True),
        preferred_element_type=jnp.float32,
    )
    keyvalue_sum = jnp.dot(
        group_tokens,
        lax.all_gather(keyvalue_weight, "seq", axis=0, tiled=True),
        preferred_element_type=jnp.float32,
    )
    queries = (query_sum * scaling).astype(jnp.bfloat16)
    keyvalue = keyvalue_sum.astype(jnp.bfloat16)
    absorb, initial = attention_parts(queries, local_heads)
    result = absorb(
        initial,
        (
            lax.all_gather(keyvalue[:, :DK], "seq", axis=0, tiled=True),
            lax.all_gather(keyvalue[:, DK:], "seq", axis=0, tiled=True),
        ),
        jnp.int32(0),
    )
    attended = finish_attention(result, group_count)
    output_half = lax.dynamic_slice_in_dim(
        output_weight, col_index * local_heads * DV, local_heads * DV, 0
    )
    partial_out = jnp.dot(
        attended,
        lax.all_gather(output_half, "seq", axis=1, tiled=True),
        preferred_element_type=jnp.float32,
    )
    attention_out = lax.psum_scatter(
        partial_out.astype(jnp.bfloat16), "col", scatter_dimension=0, tiled=True
    ).astype(jnp.float32)
    tokens = (embedded.astype(jnp.float32) + attention_out).astype(jnp.bfloat16)
    pair_pool = jnp.mean(
        tokens.astype(jnp.float32).reshape(-1, PAIR_POOL, tokens.shape[1]), axis=1
    ).astype(jnp.bfloat16)
    projected = jnp.dot(pair_pool, rowcol_weight, preferred_element_type=jnp.float32).astype(
        jnp.bfloat16
    )
    features = pair_weight.shape[0]
    row_block = lax.all_gather(projected, "col", axis=0, tiled=True)
    column_all = lax.all_gather(row_block[:, features:], "seq", axis=0, tiled=True)
    row_part = row_block[:, :features]
    column_span = column_all.shape[0] // col_count
    column_part = lax.dynamic_slice_in_dim(
        column_all, lax.axis_index("col") * column_span, column_span, 0
    )
    hidden = jax.nn.gelu(
        row_part.astype(jnp.float32)[:, None, :] + column_part.astype(jnp.float32)[None, :, :],
        approximate=True,
    ).astype(jnp.bfloat16)
    pair_out = jnp.dot(
        hidden.reshape(-1, features), pair_weight, preferred_element_type=jnp.float32
    ).astype(jnp.bfloat16)
    return (tokens, pair_out.reshape(row_part.shape[0], column_span, features))


def solution(mesh):
    placed = (
        P(("grp", "seq"), "col"),
        P(None, None, "col"),
        P(),
        P("col", "seq"),
        P(),
        P("seq", None),
        P("seq", None),
        P(None, "seq"),
        P(),
        P(),
    )
    return jax.shard_map(
        on_device,
        mesh=mesh,
        in_specs=placed,
        out_specs=(P(("grp", "seq", "col"), None), P(("grp", "seq"), "col", None)),
        check_vma=False,
    )
```

profile of v0, /device:TPU:0, one launch (start us, length us, event | category | flops | bytes accessed | tf_op | source)
XLA Modules:
  0.0 257.4 jit_solution(12248278608278916954)
XLA Ops:
  7.2 1.4 copy.19
  8.7 4.9 %collective-permute-start = (bf16[2,704]{1,0:T(2,128)(2,1)S(1)}, bf16[2,704]{1,0:T(2,128)(2,1)S(1)}, u32[]{:S(2)}, u32[]{:S(2)}) collective-permute-start(bf16[2,704]{1,0:T(2,128)(2,1)S(1)} %get-tuple-element.4), channel_id=1, source_target_pairs={{0,2},{2,4},{4,6},{6,8},{8,10},{10,12},{12,14},{1,3},{3,5},{5,7},{... | collective-permute-start | bytes 8456 | tf_op jit(solution)/shard_map/ppermute | solution.py:19
  13.6 1.3 collective-permute-start.1
  14.9 4.2 %collective-permute-done.1 = bf16[2,704]{1,0:T(2,128)(2,1)S(1)} collective-permute-done((bf16[2,704]{1,0:T(2,128)(2,1)S(1)}, bf16[2,704]{1,0:T(2,128)(2,1)S(1)}, u32[]{:S(2)}, u32[]{:S(2)}) %collective-permute-start.1) | collective-permute-done | bytes 2848 | tf_op jit(solution)/shard_map/ppermute | solution.py:20
  19.1 1.1 maximum_bitcast_fusion
  20.2 0.7 all-gather.7.cloned.1.call-update
  21.0 10.3 %all-gather.13.cloned.1.call-done = bf16[2,704,516]{1,2,0:T(8,128)(2,1)} async-done(((bf16[1,704,516]{1,2,0:T(8,128)(2,1)}), bf16[2,704,516]{1,2,0:T(8,128)(2,1)}) %all-gather.13.cloned.1.call-update) | async-done | bytes 1453072 | tf_op jit(solution)/shard_map/all_gather | solution.py:78
  31.3 4.3 %copy.22 = f32[2,704,516]{1,0,2:T(2,128)} copy(bf16[2,704,516]{1,2,0:T(8,128)(2,1)} %all-gather.13.cloned.1.call-done) | data formatting | bytes 4359168 | tf_op jit(solution)/shard_map/convert_element_type | solution.py:80
  35.6 5.3 %reshape.62 = f32[1408,516]{0,1:T(8,128)} reshape(f32[2,704,516]{1,0,2:T(2,128)} %copy.22) | data formatting | bytes 5812224 | tf_op jit(solution)/shard_map/convert_element_type | solution.py:80
  40.9 2.4 multiply_reduce_fusion
  43.3 0.5 copy-done.1
  43.9 1.2 fusion.7
  45.1 3.0 %fusion.16 = f32[512,704]{0,1:T(8,128)S(1)} fusion(bf16[5,1408,704]{1,2,0:T(8,128)(2,1)} %param.11, bf16[516,1408]{1,0:T(8,128)(2,1)S(1)} %fusion.7), kind=kOutput, calls=%fused_computation.21 | convolution fusion | flops 1015021568 | bytes 4866048 | tf_op jit(solution)/shard_map/dot_general | solution.py:84
  48.1 1.4 copy-done.4
  49.5 1.3 fusion.12
  50.9 1.3 fusion.10
  52.2 1.3 fusion.8
  53.6 1.5 add_add_fusion
  55.1 1.6 copy.23
  56.7 1.8 reshape.50
  58.5 0.9 reduce_sum.46
  59.5 27.3 %all-gather.7.cloned.1.call-done = bf16[704,1536]{0,1:T(8,128)(2,1)} async-done(((bf16[704,192]{0,1:T(8,128)(2,1)}), bf16[704,1536]{0,1:T(8,128)(2,1)}) %all-gather.7.cloned.1.call-update) | async-done | bytes 2162704 | tf_op jit(solution)/shard_map/all_gather | solution.py:90
  86.8 3.3 %convolution_convert_fusion.1 = bf16[128,1536]{1,0:T(8,128)(2,1)} fusion(bf16[704,1536]{0,1:T(8,128)(2,1)} %all-gather.7.cloned.1.call-done, f32[128,704]{1,0:T(8,128)S(1)} %reduce_sum.46), kind=kOutput, calls=%fused_computation.11 | convolution fusion | flops 277200896 | bytes 2916352 | tf_op jit(solution)/shard_map/dot_general | solution.py:93
  90.2 0.7 constant_dynamic-slice_fusion.1
  91.0 0.8 constant_dynamic-slice_fusion
  91.8 34.5 %all_gather.34 = bf16[1536,320]{1,0:T(8,128)(2,1)S(1)} all-gather(bf16[192,320]{1,0:T(8,128)(2,1)S(1)} %copy-done.6), channel_id=1, replica_groups=mesh['grp'=2,'seq'=8,'col'=2] {'seq'}, dimensions={0}, use_global_device_ids=true | all-gather | bytes 1105920 | tf_op jit(solution)/shard_map/all_gather | solution.py:115
  126.3 1.1 fusion.39
  127.4 1.0 fusion.41
  128.4 2.3 all_gather.32
  130.7 0.5 convolution_convert_fusion.2
  131.3 17.6 %all-gather.9.cloned.1.call-done = bf16[1536,512]{1,0:T(8,128)(2,1)} async-done(((bf16[192,512]{1,0:T(8,128)(2,1)}), bf16[1536,512]{1,0:T(8,128)(2,1)}) %all-gather.9.cloned.1.call-update) | async-done | bytes 1572880 | tf_op jit(solution)/shard_map/all_gather | solution.py:110
  148.9 1.8 fusion.35
  150.7 0.1 reshape.51
  150.8 27.4 %all_gather.35 = bf16[1024,128]{0,1:T(8,128)(2,1)S(1)} all-gather(bf16[128,128]{0,1:T(8,128)(2,1)S(1)} %slice.71), channel_id=1, replica_groups=mesh['grp'=2,'seq'=8,'col'=2] {'seq'}, dimensions={0}, use_global_device_ids=true | all-gather | bytes 294912 | tf_op jit(solution)/shard_map/all_gather | solution.py:124
  178.1 29.0 %all_gather.36 = bf16[1024,192]{0,1:T(8,128)(2,1)S(1)} all-gather(bf16[128,192]{0,1:T(8,128)(2,1)S(1)} %slice.72), channel_id=1, replica_groups=mesh['grp'=2,'seq'=8,'col'=2] {'seq'}, dimensions={0}, use_global_device_ids=true | all-gather | bytes 442368 | tf_op jit(solution)/shard_map/all_gather | solution.py:125
  207.1 0.5 fusion.57
  207.6 0.5 fusion.23
  208.1 0.6 fusion.34
  208.7 0.1 copy.24
  208.8 0.3 reshape.52
  209.1 3.3 %convolution_convert_fusion = bf16[128,1536]{1,0:T(8,128)(2,1)} fusion(bf16[128,768]{1,0:T(8,128)(2,1)S(1)} %reshape.52, bf16[768,1536]{0,1:T(8,128)(2,1)} %all-gather.11.cloned.1.call-done), kind=kOutput, calls=%fused_computation.10 | convolution fusion | flops 302186496 | bytes 2949120 | tf_op jit(solution)/shard_map/dot_general | solution.py:133
  212.5 7.2 %reduce-scatter.5.cloned.1.call-done = bf16[64,1536]{1,0:T(8,128)(2,1)} async-done(((bf16[128,1536]{1,0:T(8,128)(2,1)}), bf16[64,1536]{1,0:T(8,128)(2,1)}) %reduce-scatter.5.cloned.1.call-update) | async-done | bytes 196624 | tf_op jit(solution)/shard_map/reduce_scatter | solution.py:138
  219.7 1.7 convert_reduce_fusion
  221.3 0.2 fusion.36
  221.6 1.8 all-gather.1
  223.3 26.3 %all_gather.39 = bf16[64,128]{1,0:T(8,128)(2,1)S(1)} all-gather(bf16[8,128]{1,0:T(8,128)(2,1)S(1)} %get-tuple-element.7), channel_id=1, replica_groups=mesh['grp'=2,'seq'=8,'col'=2] {'seq'}, dimensions={0}, use_global_device_ids=true | all-gather | bytes 18432 | tf_op jit(solution)/shard_map/all_gather | solution.py:150
  249.7 0.1 fusion.51
  249.8 0.8 convolution_convert_fusion.3
  (44 shorter events, 0.5 us)
Async XLA Ops:
  7.2 214.2 %copy-start = (bf16[1536,256]{1,0:T(8,128)(2,1)S(1)}, bf16[1536,256]{1,0:T(8,128)(2,1)}, u32[]{:S(2)}) copy-start(bf16[1536,256]{1,0:T(8,128)(2,1)} %param.18) | copy-start | bytes 2359300
  7.2 24.2 %all-gather.13.cloned.1.call-start = ((), (), s32[]{:S(2)}) async-start(), calls=%async_computation.7 | async-start | bytes 2396160 | tf_op jit(solution)/shard_map/all_gather | solution.py:78
  8.7 6.2 %collective-permute-start = (bf16[2,704]{1,0:T(2,128)(2,1)S(1)}, bf16[2,704]{1,0:T(2,128)(2,1)S(1)}, u32[]{:S(2)}, u32[]{:S(2)}) collective-permute-start(bf16[2,704]{1,0:T(2,128)(2,1)S(1)} %get-tuple-element.4), channel_id=1, source_target_pairs={{0,2},{2,4},{4,6},{6,8},{8,10},{10,12},{12,14},{1,3},{3,5},{5,7},{... | collective-permute-start | bytes 8456 | tf_op jit(solution)/shard_map/ppermute | solution.py:19
  13.6 5.5 %collective-permute-start.1 = (bf16[2,704]{1,0:T(2,128)(2,1)S(1)}, bf16[2,704]{1,0:T(2,128)(2,1)S(1)}, u32[]{:S(2)}, u32[]{:S(2)}) collective-permute-start(bf16[2,704]{1,0:T(2,128)(2,1)S(1)} %get-tuple-element.5), channel_id=1, source_target_pairs={{2,0},{4,2},{6,4},{8,6},{10,8},{12,10},{14,12},{3,1},{5,3},{7,5},{... | collective-permute-start | bytes 8456 | tf_op jit(solution)/shard_map/ppermute | solution.py:20
  20.2 66.6 %all-gather.7.cloned.1.call-start = ((), (), s32[]{:S(2)}) async-start(), calls=%async_computation.2 | async-start | bytes 2654208 | tf_op jit(solution)/shard_map/all_gather | solution.py:90
  20.9 105.4 %reduce-scatter.3.cloned.1.call-start = ((), (), s32[]{:S(2)}) async-start(), calls=%async_computation.3 | async-start | bytes 589824 | tf_op jit(solution)/shard_map/reduce_scatter | solution.py:92
  40.9 2.9 %copy-start.1 = (f32[1408,516]{0,1:T(8,128)S(1)}, f32[1408,516]{0,1:T(8,128)}, u32[]{:S(2)}) copy-start(f32[1408,516]{0,1:T(8,128)} %reshape.62) | copy-start | bytes 8718340
  40.9 2.9 %copy-start.9 = (f32[1408]{0:T(1024)S(1)}, f32[1408]{0:T(1024)}, u32[]{:S(2)}) copy-start(f32[1408]{0:T(1024)} %param.12) | copy-start | bytes 16900
  45.1 4.4 %copy-start.4 = (bf16[5,1408,704]{1,2,0:T(8,128)(2,1)S(1)}, bf16[5,1408,704]{1,2,0:T(8,128)(2,1)}, u32[]{:S(2)}) copy-start(bf16[5,1408,704]{1,2,0:T(8,128)(2,1)} %param.11) | copy-start | bytes 29736964
  52.2 1.4 copy-start.2
  59.4 30.8 %copy-start.7 = (bf16[192,1024]{1,0:T(8,128)(2,1)S(1)}, bf16[192,1024]{1,0:T(8,128)(2,1)}, u32[]{:S(2)}) copy-start(bf16[192,1024]{1,0:T(8,128)(2,1)} %param.15) | copy-start | bytes 1179652
  59.4 31.5 %copy-start.5 = (bf16[1536,192]{0,1:T(8,128)(2,1)S(1)}, bf16[1536,192]{0,1:T(8,128)(2,1)}, u32[]{:S(2)}) copy-start(bf16[1536,192]{0,1:T(8,128)(2,1)} %param.17) | copy-start | bytes 1769476
  59.4 32.4 %copy-start.6 = (bf16[192,320]{1,0:T(8,128)(2,1)S(1)}, bf16[192,320]{1,0:T(8,128)(2,1)}, u32[]{:S(2)}) copy-start(bf16[192,320]{1,0:T(8,128)(2,1)} %param.16) | copy-start | bytes 368644
  90.1 37.3 %copy-start.10 = (f32[1536]{0:T(1024)S(1)}, f32[1536]{0:T(1024)}, u32[]{:S(2)}) copy-start(f32[1536]{0:T(1024)} %param.14) | copy-start | bytes 18436
  90.1 58.7 %all-gather.9.cloned.1.call-start = ((), (), s32[]{:S(2)}) async-start(), calls=%async_computation.4 | async-start | bytes 1769472 | tf_op jit(solution)/shard_map/all_gather | solution.py:110
  90.9 118.2 %all-gather.11.cloned.1.call-start = ((), (), s32[]{:S(2)}) async-start(), calls=%async_computation.5 | async-start | bytes 2654208 | tf_op jit(solution)/shard_map/all_gather | solution.py:135
  91.8 127.9 %reduce-scatter.5.cloned.1.call-start = ((), (), s32[]{:S(2)}) async-start(), calls=%async_computation.6 | async-start | bytes 589824 | tf_op jit(solution)/shard_map/reduce_scatter | solution.py:138
  208.8 10.8 %copy-start.3 = (bf16[64,1536]{1,0:T(8,128)(2,1)S(1)}, bf16[64,1536]{1,0:T(8,128)(2,1)}, u32[]{:S(2)}) copy-start(bf16[64,1536]{1,0:T(8,128)(2,1)} %reduce-scatter.3.cloned.1.call-done) | copy-start | bytes 589828
  209.1 40.6 %copy-start.8 = (bf16[128,128]{1,0:T(8,128)(2,1)S(1)}, bf16[128,128]{1,0:T(8,128)(2,1)}, u32[]{:S(2)}) copy-start(bf16[128,128]{1,0:T(8,128)(2,1)} %param.19) | copy-start | bytes 98308
Sparse Core Ops, SparseCore 0:
  20.3 10.9 all-gather.12
  33.5 53.2 all-gather.6
  90.2 6.3 reduce-scatter.2
  99.4 49.3 all-gather.8
  151.1 57.5 all-gather.10
  212.6 7.0 reduce-scatter.4
where the time goes:
time: 258 us; the launch traced here: 257 us
  blocking collectives  121 us (47%)
  waiting for transfers between devices  67.5 us (26%)
  matrix products  19.5 us (8%)
  local copies, waits for them, and re-layouts  18.4 us (7%)
  between operations  14.4 us (6%)
  other arithmetic  10.1 us (4%)
  starting transfers between devices  6.41 us (2%)
    all_gather x1, blocking collectives, on_device(): lax.all_gather(keyvalue_weight, 'seq', axis=0, tiled=True)  34.5 us
    all_gather x1, blocking collectives, on_device(): lax.all_gather(keyvalue[:, DK:], 'seq', axis=0, tiled=True)  29 us
    all_gather x1, blocking collectives, on_device(): lax.all_gather(keyvalue[:, :DK], 'seq', axis=0, tiled=True)  27.4 us
    all_gather x1, waiting for transfers between devices, on_device(): embed_full = lax.all_gather(embed_weight, 'seq', axis=1, tiled=True)  27.3 us
    all_gather x1, blocking collectives, on_device(): lax.all_gather(row_block[:, features:], 'seq', axis=0, tiled=True)  26.3 us
    all_gather x1, waiting for transfers between devices, on_device(): lax.all_gather(query_half, 'seq', axis=0, tiled=True)  17.6 us
    all_gather x1, waiting for transfers between devices, on_device(): widened = lax.all_gather(padded, 'col', axis=1, tiled=True)  10.3 us
    convert_element_type x2, local copies, waits for them, and re-layouts, on_device(): widened.astype(jnp.float32)  9.6 us
  transfers between devices with their start and end apart: 8, of which 5 were waited for; matrix products, arithmetic and copies ran while one was open for 13% of the time, Pallas kernels for 0%

commit v1 on v0

v1 whole, which is shorter than its diff:
```python
import functools
import math

import jax
import jax.numpy as jnp
import numpy as np
from jax import lax
from jax.experimental import pallas as pl
from jax.experimental.pallas import tpu as pltpu
from jax.sharding import PartitionSpec as P

DK = 128
DV = 192
POOL = 4
PAIR_POOL = 16
EPS = 1e-06
VMEM = pltpu.VMEM
F32 = jnp.float32
BF16 = jnp.bfloat16


def gelu(x):
    return 0.5 * x * (1.0 + jnp.tanh(math.sqrt(2.0 / math.pi) * (x + 0.044715 * (x * x * x))))


def dot_nt(a, b):
    return lax.dot_general(a, b, (((1,), (1,)), ((), ())), preferred_element_type=F32)


def dot_nn(a, b):
    return lax.dot_general(a, b, (((1,), (0,)), ((), ())), preferred_element_type=F32)


def params(mib, **kw):
    return pltpu.CompilerParams(vmem_limit_bytes=mib << 20, **kw)


def vspec(n):
    return [pl.BlockSpec(memory_space=VMEM)] * n


def ring_order(rows):
    evens = [i for i in range(rows) if i % 2 == 1]
    odds = [i for i in range(rows) if i % 2 == 0 and i > 0]
    return [0] + evens + odds[::-1]


def gather_plan(count):
    if count % 2 or count > 16:
        return None
    return ring_order(count // 2)


def pick(index, table):
    value = jnp.int32(table[0])
    for i, entry in enumerate(table[1:], 1):
        value = jnp.where(index == i, jnp.int32(entry), value)
    return value


def owners(count):
    ring = gather_plan(count)
    if ring is None:
        return [jnp.int32(0)]
    me = lax.axis_index("seq")
    row, side = me // 2, me % 2
    rows = len(ring)
    place = pick(row, [ring.index(i) for i in range(rows)])
    result = []
    for step in range(rows):
        source = pick(lax.rem(place + rows - step, rows), ring)
        result.append(source * 2 + side)
        result.append(source * 2 + 1 - side)
    return result


def gather_blocks(own, count):
    ring = gather_plan(count)
    if ring is None:
        return [lax.all_gather(own, "seq", axis=0, tiled=True)]
    rows = len(ring)
    step_pairs = []
    for k in range(rows):
        a, b = ring[k], ring[(k + 1) % rows]
        step_pairs += [(2 * a + s, 2 * b + s) for s in range(2)]
    side_pairs = [(i, i ^ 1) for i in range(count)]
    pieces = []
    held = own
    for step in range(rows):
        ahead = lax.ppermute(held, "seq", step_pairs) if step < rows - 1 else None
        pieces += [held, lax.ppermute(held, "seq", side_pairs)]
        held = ahead
    return pieces


def conv_kernel(own_ref, other_ref, halo_ref, gaincol_ref, gainrow_ref, pool_ref, poolhalo_ref, weight_hbm,
                out_ref, act, slabs, weights, sems):
    taps, width, channels = weights.shape
    copies = [pltpu.make_async_copy(weight_hbm.at[t], weights.at[t], sems.at[t]) for t in range(taps)]
    for c in copies:
        c.start()
    col = lax.axis_index("col")
    half, positions = own_ref.shape
    tokens = out_ref.shape[0]
    step = 64
    halves = ((own_ref, col), (other_ref, 1 - col))
    squares = jnp.zeros((8, positions), F32)
    for ref, _ in halves:
        for j in range(half // step):
            x = ref[j * step:(j + 1) * step, :].astype(F32)
            x = x * x
            for i in range(step // 8):
                squares = squares + x[i * 8:(i + 1) * 8]
    scale = lax.rsqrt(jnp.sum(squares, axis=0, keepdims=True) / channels + EPS)
    for ref, index in halves:
        for j in range(half // step):
            start = pl.multiple_of(index * half + j * step, step)
            x = ref[j * step:(j + 1) * step, :].astype(F32)
            x = x * scale * gaincol_ref[pl.ds(start, step), :]
            act[pl.ds(start, step), :] = gelu(x).astype(BF16)
    h = halo_ref[...].astype(F32)
    h = h * lax.rsqrt(jnp.sum(h * h, axis=1, keepdims=True) / channels + EPS) * gainrow_ref[...]
    h = gelu(h).astype(BF16)
    for t in range(taps):
        rows = slice(t * tokens, (t + 1) * tokens)
        slabs[t] = (dot_nt(pool_ref[rows], act[...]) + dot_nn(poolhalo_ref[rows], h)).astype(BF16)
    total = dot_nt(pool_ref[(taps // 2) * tokens:(taps // 2 + 1) * tokens], own_ref[...])
    for t in range(taps):
        copies[t].wait()
        total = total + dot_nt(slabs[t], weights[t])
    out_ref[...] = total.astype(BF16)


def embed_kernel(pieces, pooled_ref, *refs):
    blocks, out_ref = refs[:pieces], refs[pieces]
    for ref, owner in zip(blocks, owners(lax.axis_size("seq"))):
        out_ref[owner] = dot_nt(pooled_ref[...], ref[...]).astype(BF16)


def embedded_of(a_ref, b_ref, rows=slice(None)):
    return (a_ref[:, rows].astype(F32) + b_ref[:, rows].astype(F32)).astype(BF16).astype(F32)


def query_kernel(pieces, features, part_ref, other_ref, gain_ref, *refs):
    blocks, (query_ref, kv_ref, normed) = refs[:pieces], refs[pieces:]
    embedded = embedded_of(part_ref, other_ref)
    count, _, width = embedded.shape
    squares = jnp.sum(jnp.sum(embedded * embedded, axis=0), axis=1, keepdims=True)
    scale = lax.rsqrt(squares / (count * width) + EPS)
    normed[...] = (embedded * scale[None] * gain_ref[...]).astype(BF16)
    total = None
    for ref, owner in zip(blocks, owners(lax.axis_size("seq"))):
        part = dot_nn(normed[owner], ref[...])
        total = part if total is None else total + part
    query_ref[...] = (total[:, :features] * DK ** (-0.5)).astype(BF16)
    kv = total[:, features:].astype(BF16)
    for i in range(kv_ref.shape[0]):
        kv_ref[i] = kv


def attend_kernel(query_ref, key_ref, value_ref, out_ref):
    tokens, features = query_ref.shape
    keys = key_ref[:, :DK]
    values = value_ref[...]
    for h in range(features // DK):
        scores = dot_nt(query_ref[:, h * DK:(h + 1) * DK], keys)
        weights = jnp.exp(scores - jnp.max(scores, axis=1, keepdims=True))
        total = jnp.sum(weights, axis=1, keepdims=True)
        out_ref[h] = (dot_nn(weights.astype(BF16), values) / total).astype(BF16)


def output_kernel(pieces, attended_ref, *refs):
    blocks, (mine_ref, theirs_ref, whole) = refs[:pieces], refs[pieces:]
    heads = attended_ref.shape[0]
    flat = jnp.concatenate([attended_ref[h] for h in range(heads)], axis=1)
    for ref, owner in zip(blocks, owners(lax.axis_size("seq"))):
        whole[owner] = dot_nt(flat, ref[...])
    col = lax.axis_index("col")
    rows = mine_ref.shape[1]
    mine_ref[...] = whole[:, pl.ds(pl.multiple_of(col * rows, rows), rows)]
    theirs_ref[...] = whole[:, pl.ds(pl.multiple_of((1 - col) * rows, rows), rows)].astype(BF16)


def token_kernel(part_ref, other_ref, mine_ref, theirs_ref, weight_ref, token_ref, send_ref):
    col = lax.axis_index("col")
    count, rows, width = mine_ref.shape
    rows_here = pl.ds(pl.multiple_of(col * rows, rows), rows)
    embedded = embedded_of(part_ref, other_ref, rows_here)
    tokens = (embedded + mine_ref[...] + theirs_ref[...].astype(F32)).astype(BF16)
    token_ref[...] = jnp.concatenate([tokens[s] for s in range(count)], axis=1)
    projected = None
    for s in range(count):
        pooled = jnp.mean(tokens[s].astype(F32).reshape(rows // PAIR_POOL, PAIR_POOL, width), axis=1).astype(BF16)
        part = dot_nn(pooled, weight_ref[s * width:(s + 1) * width])
        projected = part if projected is None else projected + part
    projected = projected.astype(BF16)
    for i in range(send_ref.shape[0]):
        send_ref[i] = projected


def pair_kernel(all_ref, weight_ref, out_ref, rows_here, columns_here):
    seq, col = lax.axis_index("seq"), lax.axis_index("col")
    devices, each, _ = all_ref.shape
    features = weight_ref.shape[0]
    cols = lax.axis_size("col")
    for c in range(cols):
        rows_here[c * each:(c + 1) * each] = all_ref[seq * cols + c].astype(F32)[:, :features]
    span = devices // cols
    for j in range(span):
        columns_here[j * each:(j + 1) * each] = all_ref[col * span + j].astype(F32)[:, features:]
    hidden = gelu(rows_here[...][:, None, :] + columns_here[...][None, :, :])
    r, c, f = hidden.shape
    out_ref[...] = dot_nn(hidden.reshape(r * c, f).astype(BF16), weight_ref[...]).reshape(r, c, f).astype(BF16)


def pooling_matrices(positions, taps):
    tokens, reach = positions // POOL, taps // 2
    main = np.zeros((taps, tokens, positions), np.float32)
    halo = np.zeros((taps, tokens, 16), np.float32)
    for t in range(taps):
        for i in range(tokens):
            for j in range(POOL):
                p = POOL * i + j + t - reach
                if p < 0:
                    halo[t, i, p + reach] += 1.0 / POOL
                elif p >= positions:
                    halo[t, i, reach + p - positions] += 1.0 / POOL
                else:
                    main[t, i, p] += 1.0 / POOL
    as_rows = lambda a: jnp.asarray(a.reshape(taps * tokens, -1), BF16)
    return as_rows(main), as_rows(halo)


def cost(flops, size):
    return pl.CostEstimate(flops=int(flops), bytes_accessed=int(size), transcendentals=0)


def on_device(signal, conv_weight, conv_gain, embed_weight, attn_gain, query_weight, keyvalue_weight,
              output_weight, rowcol_weight, pair_weight):
    col = lax.axis_index("col")
    count, cols = lax.axis_size("seq"), lax.axis_size("col")
    positions, half = signal.shape
    taps, channels, _ = conv_weight.shape
    reach = taps // 2
    tokens = positions // POOL
    width = embed_weight.shape[1] * count
    features = query_weight.shape[1] // cols
    heads = features // DK
    swap = [(i, (i + 1) % cols) for i in range(cols)]
    shape = jax.ShapeDtypeStruct

    signal_t = signal.T
    other_t = lax.ppermute(signal_t, "col", swap)
    first, last = signal[:reach], signal[positions - reach:]

    def shifted(rows, by, across):
        pairs = [
            (s * cols + c, (s + by) * cols + ((c + 1) % cols if across else c))
            for s in range(count) for c in range(cols) if 0 <= s + by < count
        ]
        return lax.ppermute(rows, ("seq", "col"), pairs)

    own_halo = jnp.concatenate([shifted(last, 1, False), shifted(first, -1, False)], axis=0)
    other_halo = jnp.concatenate([shifted(last, 1, True), shifted(first, -1, True)], axis=0)
    halo = jnp.where(
        col == 0, jnp.concatenate([own_halo, other_halo], axis=1), jnp.concatenate([other_halo, own_halo], axis=1)
    )
    halo = jnp.pad(halo, ((0, 16 - 2 * reach), (0, 0)))

    embed_blocks = gather_blocks(embed_weight.T, count)
    query_own = jnp.concatenate(
        [
            lax.dynamic_slice_in_dim(query_weight, col * features, features, 1),
            lax.dynamic_slice_in_dim(keyvalue_weight, col * DK, DV, 1),
        ],
        axis=1,
    )
    query_blocks = gather_blocks(query_own, count)
    output_own = lax.dynamic_slice_in_dim(output_weight.T, col * heads * DV, heads * DV, 1)
    output_blocks = gather_blocks(output_own, count)
    pieces = len(embed_blocks)
    block = width // pieces

    pool_main, pool_halo = pooling_matrices(positions, taps)
    pooled = pl.pallas_call(
        conv_kernel,
        out_shape=shape((tokens, half), BF16),
        in_specs=vspec(7) + [pl.BlockSpec(memory_space=pl.ANY)],
        out_specs=pl.BlockSpec(memory_space=VMEM),
        scratch_shapes=[
            pltpu.VMEM((channels, positions), BF16),
            pltpu.VMEM((taps, tokens, channels), BF16),
            pltpu.VMEM((taps, half, channels), BF16),
            pltpu.SemaphoreType.DMA((taps,)),
        ],
        compiler_params=params(36),
        cost_estimate=cost(2 * taps * tokens * channels * (half + positions), 2 * taps * channels * half * 2),
        name="conv",
    )(
        signal_t, other_t, halo, conv_gain.reshape(channels, 1), conv_gain.reshape(1, channels),
        pool_main, pool_halo, conv_weight.transpose(0, 2, 1),
    )

    part = pl.pallas_call(
        functools.partial(embed_kernel, pieces),
        out_shape=shape((pieces, tokens, block), BF16),
        in_specs=vspec(1 + pieces),
        out_specs=pl.BlockSpec(memory_space=VMEM),
        compiler_params=params(16),
        cost_estimate=cost(2 * tokens * half * width, 2 * half * width),
        name="embed",
    )(pooled, *embed_blocks)
    other_part = lax.ppermute(part, "col", swap)

    queries, keyvalue = pl.pallas_call(
        functools.partial(query_kernel, pieces, features),
        out_shape=(shape((tokens, features), BF16), shape((count, tokens, DV), BF16)),
        in_specs=vspec(3 + pieces),
        out_specs=vspec(2),
        scratch_shapes=[pltpu.VMEM((pieces, tokens, block), BF16)],
        compiler_params=params(32),
        cost_estimate=cost(2 * tokens * width * (features + DV), 2 * width * (features + DV)),
        name="query",
    )(part, other_part, attn_gain.reshape(pieces, 1, block), *query_blocks)

    gathered = lax.all_to_all(keyvalue, "seq", 0, 0).reshape(count * tokens, DV)
    gathered_other = lax.ppermute(gathered, "col", swap)
    keys = jnp.where(col == 0, gathered, gathered_other)
    values = jnp.where(col == 0, gathered_other, gathered)

    attended = pl.pallas_call(
        attend_kernel,
        out_shape=shape((heads, tokens, DV), BF16),
        in_specs=vspec(3),
        out_specs=pl.BlockSpec(memory_space=VMEM),
        compiler_params=params(48),
        cost_estimate=cost(2 * tokens * heads * count * tokens * (DK + DV), 4 * count * tokens * DV),
        name="attend",
    )(queries, keys, values)

    own_rows = tokens // cols
    mine, theirs = pl.pallas_call(
        functools.partial(output_kernel, pieces),
        out_shape=(shape((pieces, own_rows, block), F32), shape((pieces, own_rows, block), BF16)),
        in_specs=vspec(1 + pieces),
        out_specs=vspec(2),
        scratch_shapes=[pltpu.VMEM((pieces, tokens, block), F32)],
        compiler_params=params(32),
        cost_estimate=cost(2 * tokens * heads * DV * width, 2 * heads * DV * width),
        name="output",
    )(attended, *output_blocks)
    theirs = lax.ppermute(theirs, "col", swap)

    out_width = rowcol_weight.shape[1]
    each = own_rows // PAIR_POOL
    out_tokens, projected = pl.pallas_call(
        token_kernel,
        out_shape=(shape((own_rows, width), BF16), shape((count * cols, each, out_width), BF16)),
        in_specs=vspec(5),
        out_specs=vspec(2),
        compiler_params=params(16),
        cost_estimate=cost(2 * each * width * out_width, 2 * width * out_width),
        name="tokens",
    )(part, other_part, mine, theirs, rowcol_weight)
    all_projected = lax.all_to_all(projected, ("seq", "col"), 0, 0)

    pair_rows, span = each * cols, each * count
    pair_features = pair_weight.shape[0]
    pair_out = pl.pallas_call(
        pair_kernel,
        out_shape=shape((pair_rows, span, pair_features), BF16),
        in_specs=vspec(2),
        out_specs=pl.BlockSpec(memory_space=VMEM),
        scratch_shapes=[pltpu.VMEM((pair_rows, pair_features), F32), pltpu.VMEM((span, pair_features), F32)],
        compiler_params=params(16),
        cost_estimate=cost(2 * pair_rows * span * pair_features**2, 2 * pair_rows * span * pair_features),
        name="pair",
    )(all_projected, pair_weight)
    return out_tokens, pair_out


def solution(mesh):
    placed = (
        P(("grp", "seq"), "col"),
        P(None, None, "col"),
        P(),
        P("col", "seq"),
        P(),
        P("seq", None),
        P("seq", None),
        P(None, "seq"),
        P(),
        P(),
    )
    return jax.shard_map(
        on_device,
        mesh=mesh,
        in_specs=placed,
        out_specs=(P(("grp", "seq", "col"), None), P(("grp", "seq"), "col", None)),
        check_vma=False,
    )
```

time: 258 us -> 183 us (0.71)
  blocking collectives: 121 us -> 11.9 us
  starting transfers between devices: 6.41 us -> 47.8 us
  matrix products: 19.5 us -> 0 us
  Pallas kernels: 0 us -> 17.5 us
  waiting for transfers between devices: 67.5 us -> 82.8 us
  between operations: 14.4 us -> 0.92 us
  other arithmetic: 10.1 us -> 1.23 us
    all_gather x6 -> x0, blocking collectives: 121 us -> none  [the longest x1 34.5 us: on_device(): lax.all_gather(keyvalue_weight, 'seq', axis=0, tiled=True)]
    ppermute x2 -> x29, waiting for transfers between devices: 4.18 us -> 82.8 us  [the longest x9 40.8 us: gather_blocks(): ahead = lax.ppermute(held, 'seq', step_pairs) if step < rows - 1 else None]
    all_gather x4 -> x0, waiting for transfers between devices: 55.3 us -> none  [the longest x1 27.3 us: on_device(): embed_full = lax.all_gather(embed_weight, 'seq', axis=1, tiled=True)]
    ppermute x2 -> x29, starting transfers between devices: 6.16 us -> 42.1 us  [the longest x12 17.2 us: gather_blocks(): pieces += [held, lax.ppermute(held, 'seq', side_pairs)]]
    dot_general x13 -> x0, matrix products: 19.5 us -> none  [the longest x5 8.5 us: on_device(): jnp.dot(activated[tap_index:tap_index + positions], conv_weight[tap_index...]
    pallas_call x0 -> x7, Pallas kernels: none -> 17.5 us  [the longest x1 10.5 us: on_device(): pl.pallas_call(conv_kernel, out_shape=shape((tokens, half), BF16), in_spe...]
    all_to_all x0 -> x1, blocking collectives: none -> 11.9 us  [on_device(): all_projected = lax.all_to_all(projected, ('seq', 'col'), 0, 0)]
    convert_element_type x3 -> x0, local copies, waits for them, and re-layouts: 9.74 us -> none  [the longest x2 9.6 us: on_device(): widened.astype(jnp.float32)]
  transfers between devices with their start and end apart: 8 -> 30, of which waited for: 5 -> 17; matrix products, arithmetic and copies ran while one was open for 13% -> 5% of each run, Pallas kernels for 0% -> 7%
where the time goes in v1:
time: 183 us; the launch traced here: 182 us
  waiting for transfers between devices  82.8 us (45%)
  starting transfers between devices  47.8 us (26%)
  local copies, waits for them, and re-layouts  19.9 us (11%)
  Pallas kernels  17.5 us (10%)
  blocking collectives  11.9 us (7%)
    ppermute x9, waiting for transfers between devices, gather_blocks(): ahead = lax.ppermute(held, 'seq', step_pairs) if step < rows - 1 else None  40.8 us
    ppermute x12, waiting for transfers between devices, gather_blocks(): pieces += [held, lax.ppermute(held, 'seq', side_pairs)]  39.2 us
    ppermute x12, starting transfers between devices, gather_blocks(): pieces += [held, lax.ppermute(held, 'seq', side_pairs)]  17.2 us
    ppermute x9, starting transfers between devices, gather_blocks(): ahead = lax.ppermute(held, 'seq', step_pairs) if step < rows - 1 else None  13.5 us
    unnamed x32, local copies, waits for them, and re-layouts  12.1 us
    all_to_all x1, blocking collectives, on_device(): all_projected = lax.all_to_all(projected, ('seq', 'col'), 0, 0)  11.9 us
    ppermute x4, starting transfers between devices, shifted(): return lax.ppermute(rows, ('seq', 'col'), pairs)  10.8 us
    pallas_call x1, Pallas kernels, on_device(): pl.pallas_call(conv_kernel, out_shape=shape((tokens, half), BF16), in_spe...  10.5 us
  transfers between devices with their start and end apart: 30, of which 17 were waited for; matrix products, arithmetic and copies ran while one was open for 5% of the time, Pallas kernels for 7%

profile of v1, /device:TPU:0, one launch (start us, length us, event | category | flops | bytes accessed | tf_op | source)
XLA Modules:
  0.0 182.1 jit_solution(13699156414171752163)
XLA Ops:
  0.7 3.1 %collective-permute-start.6 = (bf16[192,704]{1,0:T(8,128)(2,1)}, bf16[192,704]{1,0:T(8,128)(2,1)S(1)}, u32[]{:S(2)}, u32[]{:S(2)}) collective-permute-start(bf16[192,704]{1,0:T(8,128)(2,1)} %bitcast.11), channel_id=1, source_target_pairs={{0,4},{2,6},{4,12},{6,14},{12,8},{14,10},{8,0},{10,2},{1,5},{3,7},... | collective-permute-start | bytes 811016 | tf_op jit(solution)/shard_map/ppermute | solution.py:90
  3.7 1.0 constant_dynamic-slice_fusion
  5.7 2.6 %collective-permute-start.14 = (bf16[192,704]{1,0:T(8,128)(2,1)S(1)}, bf16[192,704]{1,0:T(8,128)(2,1)}, u32[]{:S(2)}, u32[]{:S(2)}) collective-permute-start(bf16[192,704]{1,0:T(8,128)(2,1)S(1)} %pad_maximum_fusion.refs_0_), channel_id=1, source_target_pairs={{0,4},{2,6},{4,12},{6,14},{12,8},{14,10},{8,0},{10,2},{1,5},{3,7},... | collective-permute-start | bytes 811016 | tf_op jit(solution)/shard_map/ppermute | solution.py:90
  8.4 4.4 %collective-permute-done.6.refs_2_ = bf16[192,704]{1,0:T(8,128)(2,1)S(1)} collective-permute-done((bf16[192,704]{1,0:T(8,128)(2,1)}, bf16[192,704]{1,0:T(8,128)(2,1)S(1)}, u32[]{:S(2)}, u32[]{:S(2)}) %collective-permute-start.6) | collective-permute-done | bytes 270368 | tf_op jit(solution)/shard_map/ppermute | solution.py:90
  12.8 1.3 collective-permute-start.8
  14.1 5.2 %collective-permute-done.14.refs_2_ = bf16[192,704]{1,0:T(8,128)(2,1)} collective-permute-done((bf16[192,704]{1,0:T(8,128)(2,1)S(1)}, bf16[192,704]{1,0:T(8,128)(2,1)}, u32[]{:S(2)}, u32[]{:S(2)}) %collective-permute-start.14) | collective-permute-done | bytes 270368 | tf_op jit(solution)/shard_map/ppermute | solution.py:90
  19.2 1.0 collective-permute-start.16
  20.3 5.2 %collective-permute-done.8.refs_4_ = bf16[192,704]{1,0:T(8,128)(2,1)S(1)} collective-permute-done((bf16[192,704]{1,0:T(8,128)(2,1)S(1)}, bf16[192,704]{1,0:T(8,128)(2,1)S(1)}, u32[]{:S(2)}, u32[]{:S(2)}) %collective-permute-start.8) | collective-permute-done | bytes 270368 | tf_op jit(solution)/shard_map/ppermute | solution.py:90
  25.4 1.2 collective-permute-start.10
  26.6 1.1 fusion
  27.8 3.4 %collective-permute-start.1 = (bf16[2,704]{1,0:T(2,128)(2,1)S(1)}, bf16[2,704]{1,0:T(2,128)(2,1)S(1)}, u32[]{:S(2)}, u32[]{:S(2)}) collective-permute-start(bf16[2,704]{1,0:T(2,128)(2,1)S(1)} %copy.24), channel_id=1, source_target_pairs={{0,2},{1,3},{2,4},{3,5},{4,6},{5,7},{6,8},{7,9},{8,10},{9,11},{10,... | collective-permute-start | bytes 8456 | tf_op jit(solution)/shard_map/ppermute | solution.py:261
  31.4 1.3 collective-permute-start.2
  32.7 4.8 %collective-permute-start.3 = (bf16[2,704]{1,0:T(2,128)(2,1)S(1)}, bf16[2,704]{1,0:T(2,128)(2,1)S(1)}, u32[]{:S(2)}, u32[]{:S(2)}) collective-permute-start(bf16[2,704]{1,0:T(2,128)(2,1)S(1)} %copy.24), channel_id=1, source_target_pairs={{0,3},{1,2},{2,5},{3,4},{4,7},{5,6},{6,9},{7,8},{8,11},{9,10},{10,... | collective-permute-start | bytes 8456 | tf_op jit(solution)/shard_map/ppermute | solution.py:261
  38.2 1.3 collective-permute-start.4
  41.2 3.6 %collective-permute-start.5 = (bf16[192,704]{1,0:T(8,128)(2,1)}, bf16[192,704]{1,0:T(8,128)(2,1)S(1)}, u32[]{:S(2)}, u32[]{:S(2)}) collective-permute-start(bf16[192,704]{1,0:T(8,128)(2,1)} %bitcast.12), channel_id=1, source_target_pairs={{0,2},{2,0},{4,6},{6,4},{8,10},{10,8},{12,14},{14,12},{1,3},{3,1},... | collective-permute-start | bytes 811016 | tf_op jit(solution)/shard_map/ppermute | solution.py:91
  45.3 1.7 collective-permute-start.7
  47.3 1.7 collective-permute-start.11
  49.1 2.3 %collective-permute-start.18 = (bf16[192,704]{1,0:T(8,128)(2,1)}, bf16[192,704]{1,0:T(8,128)(2,1)}, u32[]{:S(2)}, u32[]{:S(2)}) collective-permute-start(bf16[192,704]{1,0:T(8,128)(2,1)} %collective-permute-done.16.refs_4_), channel_id=1, source_target_pairs={{0,4},{2,6},{4,12},{6,14},{12,8},{14,10},{8,0},{10,2},{1,5},{3,7},... | collective-permute-start | bytes 811016 | tf_op jit(solution)/shard_map/ppermute | solution.py:90
  51.4 3.8 %copy-done.1 = bf16[5,1408,704]{1,2,0:T(8,128)(2,1)S(1)} copy-done((bf16[5,1408,704]{1,2,0:T(8,128)(2,1)S(1)}, bf16[5,1408,704]{1,2,0:T(8,128)(2,1)}, u32[]{:S(2)}) %copy-start.1) | copy-done | bytes 9912344
  55.2 1.1 copy-done.2
  56.3 1.1 copy-done.4
  58.3 10.5 %conv.1.pooled_ref = bf16[128,704]{1,0:T(8,128)(2,1)S(1)} custom-call(bf16[704,512]{1,0:T(8,128)(2,1)S(1)} %bitcast.10, bf16[704,512]{1,0:T(8,128)(2,1)S(1)} %collective-permute-done.other_ref, bf16[16,1408]{1,0:T(8,128)(2,1)S(1)} %pad.4.halo_ref, f32[1408,1]{1,0:T(8,128)S(1)} %reshape.20.gaincol_ref, f32[1,1408]{1,0:T(1,128)S(1)} %reshape.17.gainrow_ref, ...), custom_call_target="tpu_custom_call" | custom-call | flops 2191523840 | bytes 19824640 | tf_op jit(solution)/shard_map/conv/pallas_call | solution.py:285
  68.8 2.3 %collective-permute-done.11.refs_7_ = bf16[192,704]{1,0:T(8,128)(2,1)S(1)} collective-permute-done((bf16[192,704]{1,0:T(8,128)(2,1)S(1)}, bf16[192,704]{1,0:T(8,128)(2,1)S(1)}, u32[]{:S(2)}, u32[]{:S(2)}) %collective-permute-start.11) | collective-permute-done | bytes 270368 | tf_op jit(solution)/shard_map/ppermute | solution.py:91
  73.5 2.1 %collective-permute-start.13 = (bf16[192,704]{1,0:T(8,128)(2,1)S(1)}, bf16[192,704]{1,0:T(8,128)(2,1)S(1)}, u32[]{:S(2)}, u32[]{:S(2)}) collective-permute-start(bf16[192,704]{1,0:T(8,128)(2,1)S(1)} %pad_maximum_fusion.refs_0_), channel_id=1, source_target_pairs={{0,2},{2,0},{4,6},{6,4},{8,10},{10,8},{12,14},{14,12},{1,3},{3,1},... | collective-permute-start | bytes 811016 | tf_op jit(solution)/shard_map/ppermute | solution.py:91
  75.6 2.0 %collective-permute-start.17 = (bf16[192,704]{1,0:T(8,128)(2,1)}, bf16[192,704]{1,0:T(8,128)(2,1)}, u32[]{:S(2)}, u32[]{:S(2)}) collective-permute-start(bf16[192,704]{1,0:T(8,128)(2,1)} %collective-permute-done.16.refs_4_), channel_id=1, source_target_pairs={{0,2},{2,0},{4,6},{6,4},{8,10},{10,8},{12,14},{14,12},{1,3},{3,1},... | collective-permute-start | bytes 811016 | tf_op jit(solution)/shard_map/ppermute | solution.py:91
  77.8 5.7 %collective-permute-done.13.refs_1_ = bf16[192,704]{1,0:T(8,128)(2,1)S(1)} collective-permute-done((bf16[192,704]{1,0:T(8,128)(2,1)S(1)}, bf16[192,704]{1,0:T(8,128)(2,1)S(1)}, u32[]{:S(2)}, u32[]{:S(2)}) %collective-permute-start.13) | collective-permute-done | bytes 270368 | tf_op jit(solution)/shard_map/ppermute | solution.py:91
  83.4 6.3 %collective-permute-done.15.refs_3_ = bf16[192,704]{1,0:T(8,128)(2,1)S(1)} collective-permute-done((bf16[192,704]{1,0:T(8,128)(2,1)}, bf16[192,704]{1,0:T(8,128)(2,1)S(1)}, u32[]{:S(2)}, u32[]{:S(2)}) %collective-permute-start.15) | collective-permute-done | bytes 270368 | tf_op jit(solution)/shard_map/ppermute | solution.py:91
  90.5 5.7 %collective-permute-done.17.refs_5_ = bf16[192,704]{1,0:T(8,128)(2,1)} collective-permute-done((bf16[192,704]{1,0:T(8,128)(2,1)}, bf16[192,704]{1,0:T(8,128)(2,1)}, u32[]{:S(2)}, u32[]{:S(2)}) %collective-permute-start.17) | collective-permute-done | bytes 270368 | tf_op jit(solution)/shard_map/ppermute | solution.py:91
  96.2 6.0 %collective-permute-done.19.refs_7_ = bf16[192,704]{1,0:T(8,128)(2,1)} collective-permute-done((bf16[192,704]{1,0:T(8,128)(2,1)}, bf16[192,704]{1,0:T(8,128)(2,1)}, u32[]{:S(2)}, u32[]{:S(2)}) %collective-permute-start.19) | collective-permute-done | bytes 270368 | tf_op jit(solution)/shard_map/ppermute | solution.py:91
  103.2 2.2 %query.1 = (bf16[128,512]{1,0:T(8,128)(2,1)S(1)}, bf16[8,128,192]{2,1,0:T(8,128)(2,1)S(1)}) custom-call(bf16[8,128,192]{2,1,0:T(8,128)(2,1)S(1)} %embed.1.part_ref, bf16[8,128,192]{2,1,0:T(8,128)(2,1)S(1)} %collective-permute-done.12.other_ref, f32[8,1,192]{2,1,0:T(1,128)S(1)} %reshape.18.gain_ref, bf16[192,704]{1,0:T(8,128)(2,1)S(1)} %pad_maximum_fusion.refs_0_, ...), custom_call_target="tpu_custom_call" | custom-call | flops 276824064 | bytes 2162688 | tf_op jit(solution)/shard_map/query/pallas_call | solution.py:315
  107.0 5.7 %all-to-all-start = ((bf16[8,128,192]{1,2,0:T(8,128)(2,1)}), bf16[8,128,192]{1,2,0:T(8,128)(2,1)}, u32[]{:S(2)}, u32[]{:S(2)}) async-start(bf16[8,128,192]{1,2,0:T(8,128)(2,1)} %copy.22), calls=%async_computation | async-start | bytes 786432 | tf_op jit(solution)/shard_map/all_to_all | solution.py:326
  112.8 2.1 %collective-permute-start.22 = (bf16[192,768]{1,0:T(8,128)(2,1)S(1)}, bf16[192,768]{1,0:T(8,128)(2,1)S(1)}, u32[]{:S(2)}, u32[]{:S(2)}) collective-permute-start(bf16[192,768]{1,0:T(8,128)(2,1)S(1)} %dynamic-slice_bitcast_fusion.refs_0_), channel_id=1, source_target_pairs={{0,4},{2,6},{4,12},{6,14},{12,8},{14,10},{8,0},{10,2},{1,5},{3,7},... | collective-permute-start | bytes 884744 | tf_op jit(solution)/shard_map/ppermute | solution.py:90
  114.8 15.8 %collective-permute-done.22.refs_2_ = bf16[192,768]{1,0:T(8,128)(2,1)S(1)} collective-permute-done((bf16[192,768]{1,0:T(8,128)(2,1)S(1)}, bf16[192,768]{1,0:T(8,128)(2,1)S(1)}, u32[]{:S(2)}, u32[]{:S(2)}) %collective-permute-start.22) | collective-permute-done | bytes 294944 | tf_op jit(solution)/shard_map/ppermute | solution.py:90
  130.7 2.0 %copy.23 = bf16[8,128,192]{2,1,0:T(8,128)(2,1)} copy(bf16[8,128,192]{1,2,0:T(8,128)(2,1)} %all-to-all-done) | data formatting | bytes 786432 | tf_op jit(solution)/shard_map/all_to_all | solution.py:326
  132.7 6.4 %collective-permute-done.24.refs_4_ = bf16[192,768]{1,0:T(8,128)(2,1)S(1)} collective-permute-done((bf16[192,768]{1,0:T(8,128)(2,1)S(1)}, bf16[192,768]{1,0:T(8,128)(2,1)S(1)}, u32[]{:S(2)}, u32[]{:S(2)}) %collective-permute-start.24) | collective-permute-done | bytes 294944 | tf_op jit(solution)/shard_map/ppermute | solution.py:90
  139.1 1.8 collective-permute-start.21
  141.1 1.8 collective-permute-start.25
  142.8 3.8 %collective-permute-done.26.refs_6_ = bf16[192,768]{1,0:T(8,128)(2,1)S(1)} collective-permute-done((bf16[192,768]{1,0:T(8,128)(2,1)S(1)}, bf16[192,768]{1,0:T(8,128)(2,1)S(1)}, u32[]{:S(2)}, u32[]{:S(2)}) %collective-permute-start.26) | collective-permute-done | bytes 294944 | tf_op jit(solution)/shard_map/ppermute | solution.py:90
  146.7 2.0 %collective-permute-start.27 = (bf16[192,768]{1,0:T(8,128)(2,1)S(1)}, bf16[192,768]{1,0:T(8,128)(2,1)S(1)}, u32[]{:S(2)}, u32[]{:S(2)}) collective-permute-start(bf16[192,768]{1,0:T(8,128)(2,1)S(1)} %collective-permute-done.26.refs_6_), channel_id=1, source_target_pairs={{0,2},{2,0},{4,6},{6,4},{8,10},{10,8},{12,14},{14,12},{1,3},{3,1},... | collective-permute-start | bytes 884744 | tf_op jit(solution)/shard_map/ppermute | solution.py:91
  148.7 1.1 broadcast_select_fusion
  150.7 1.1 attend.1.attended_ref
  151.8 3.5 %collective-permute-done.23.refs_3_ = bf16[192,768]{1,0:T(8,128)(2,1)S(1)} collective-permute-done((bf16[192,768]{1,0:T(8,128)(2,1)S(1)}, bf16[192,768]{1,0:T(8,128)(2,1)S(1)}, u32[]{:S(2)}, u32[]{:S(2)}) %collective-permute-start.23) | collective-permute-done | bytes 294944 | tf_op jit(solution)/shard_map/ppermute | solution.py:91
  155.3 6.3 %collective-permute-done.25.refs_5_ = bf16[192,768]{1,0:T(8,128)(2,1)S(1)} collective-permute-done((bf16[192,768]{1,0:T(8,128)(2,1)S(1)}, bf16[192,768]{1,0:T(8,128)(2,1)S(1)}, u32[]{:S(2)}, u32[]{:S(2)}) %collective-permute-start.25) | collective-permute-done | bytes 294944 | tf_op jit(solution)/shard_map/ppermute | solution.py:91
  161.6 3.4 %collective-permute-done.27.refs_7_ = bf16[192,768]{1,0:T(8,128)(2,1)S(1)} collective-permute-done((bf16[192,768]{1,0:T(8,128)(2,1)S(1)}, bf16[192,768]{1,0:T(8,128)(2,1)S(1)}, u32[]{:S(2)}, u32[]{:S(2)}) %collective-permute-start.27) | collective-permute-done | bytes 294944 | tf_op jit(solution)/shard_map/ppermute | solution.py:91
  165.0 1.0 output.1
  166.1 1.5 collective-permute-done.28.theirs_ref
  167.6 1.0 tokens.1
  168.6 11.9 %all_to_all.10.all_ref = bf16[16,4,256]{2,1,0:T(4,128)(2,1)S(1)} all-to-all(bf16[16,4,256]{2,1,0:T(4,128)(2,1)S(1)} %get-tuple-element.13), channel_id=1, replica_groups=mesh['grp'=2,'seq'=8,'col'=2] {'seq','col'}, dimensions={0} | all-to-all | bytes 65536 | tf_op jit(solution)/shard_map/all_to_all | solution.py:365
  (65 shorter events, 14.1 us)
Async XLA Ops:
  0.6 112.1 %copy-start = (bf16[1536,192]{0,1:T(8,128)(2,1)S(1)}, bf16[1536,192]{0,1:T(8,128)(2,1)}, u32[]{:S(2)}) copy-start(bf16[1536,192]{0,1:T(8,128)(2,1)} %param.19) | copy-start | bytes 1769476
  0.6 70.5 %copy-start.5 = (bf16[704,192]{0,1:T(8,128)(2,1)S(1)}, bf16[704,192]{0,1:T(8,128)(2,1)}, u32[]{:S(2)}) copy-start(bf16[704,192]{0,1:T(8,128)(2,1)} %param.15) | copy-start | bytes 811012
  0.7 77.0 %copy-start.14 = (f32[1536]{0:T(1024)S(1)}, f32[1536]{0:T(1024)}, u32[]{:S(2)}) copy-start(f32[1536]{0:T(1024)} %param.16) | copy-start | bytes 18436
  0.7 12.1 %collective-permute-start.6 = (bf16[192,704]{1,0:T(8,128)(2,1)}, bf16[192,704]{1,0:T(8,128)(2,1)S(1)}, u32[]{:S(2)}, u32[]{:S(2)}) collective-permute-start(bf16[192,704]{1,0:T(8,128)(2,1)} %bitcast.11), channel_id=1, source_target_pairs={{0,4},{2,6},{4,12},{6,14},{12,8},{14,10},{8,0},{10,2},{1,5},{3,7},... | collective-permute-start | bytes 811016 | tf_op jit(solution)/shard_map/ppermute | solution.py:90
  5.7 13.5 %collective-permute-start.14 = (bf16[192,704]{1,0:T(8,128)(2,1)S(1)}, bf16[192,704]{1,0:T(8,128)(2,1)}, u32[]{:S(2)}, u32[]{:S(2)}) collective-permute-start(bf16[192,704]{1,0:T(8,128)(2,1)S(1)} %pad_maximum_fusion.refs_0_), channel_id=1, source_target_pairs={{0,4},{2,6},{4,12},{6,14},{12,8},{14,10},{8,0},{10,2},{1,5},{3,7},... | collective-permute-start | bytes 811016 | tf_op jit(solution)/shard_map/ppermute | solution.py:90
  12.8 12.6 %collective-permute-start.8 = (bf16[192,704]{1,0:T(8,128)(2,1)S(1)}, bf16[192,704]{1,0:T(8,128)(2,1)S(1)}, u32[]{:S(2)}, u32[]{:S(2)}) collective-permute-start(bf16[192,704]{1,0:T(8,128)(2,1)S(1)} %collective-permute-done.6.refs_2_), channel_id=1, source_target_pairs={{0,4},{2,6},{4,12},{6,14},{12,8},{14,10},{8,0},{10,2},{1,5},{3,7},... | collective-permute-start | bytes 811016 | tf_op jit(solution)/shard_map/ppermute | solution.py:90
  14.1 35.1 %collective-permute-start = (bf16[704,512]{1,0:T(8,128)(2,1)}, bf16[704,512]{1,0:T(8,128)(2,1)S(1)}, u32[]{:S(2)}, u32[]{:S(2)}) collective-permute-start(bf16[704,512]{1,0:T(8,128)(2,1)} %bitcast.9), channel_id=1, source_target_pairs={{0,1},{1,0},{2,3},{3,2},{4,5},{5,4},{6,7},{7,6},{8,9},{9,8},{10,11... | collective-permute-start | bytes 2162696 | tf_op jit(solution)/shard_map/ppermute | solution.py:253
  19.2 27.7 %collective-permute-start.16 = (bf16[192,704]{1,0:T(8,128)(2,1)}, bf16[192,704]{1,0:T(8,128)(2,1)}, u32[]{:S(2)}, u32[]{:S(2)}) collective-permute-start(bf16[192,704]{1,0:T(8,128)(2,1)} %collective-permute-done.14.refs_2_), channel_id=1, source_target_pairs={{0,4},{2,6},{4,12},{6,14},{12,8},{14,10},{8,0},{10,2},{1,5},{3,7},... | collective-permute-start | bytes 811016 | tf_op jit(solution)/shard_map/ppermute | solution.py:90
  25.4 21.9 %collective-permute-start.10 = (bf16[192,704]{1,0:T(8,128)(2,1)S(1)}, bf16[192,704]{1,0:T(8,128)(2,1)S(1)}, u32[]{:S(2)}, u32[]{:S(2)}) collective-permute-start(bf16[192,704]{1,0:T(8,128)(2,1)S(1)} %collective-permute-done.8.refs_4_), channel_id=1, source_target_pairs={{0,4},{2,6},{4,12},{6,14},{12,8},{14,10},{8,0},{10,2},{1,5},{3,7},... | collective-permute-start | bytes 811016 | tf_op jit(solution)/shard_map/ppermute | solution.py:90
  27.8 4.9 %collective-permute-start.1 = (bf16[2,704]{1,0:T(2,128)(2,1)S(1)}, bf16[2,704]{1,0:T(2,128)(2,1)S(1)}, u32[]{:S(2)}, u32[]{:S(2)}) collective-permute-start(bf16[2,704]{1,0:T(2,128)(2,1)S(1)} %copy.24), channel_id=1, source_target_pairs={{0,2},{1,3},{2,4},{3,5},{4,6},{5,7},{6,8},{7,9},{8,10},{9,11},{10,... | collective-permute-start | bytes 8456 | tf_op jit(solution)/shard_map/ppermute | solution.py:261
  31.4 6.8 %collective-permute-start.2 = (bf16[2,704]{1,0:T(2,128)(2,1)S(1)}, bf16[2,704]{1,0:T(2,128)(2,1)S(1)}, u32[]{:S(2)}, u32[]{:S(2)}) collective-permute-start(bf16[2,704]{1,0:T(2,128)(2,1)S(1)} %copy.25), channel_id=1, source_target_pairs={{2,0},{3,1},{4,2},{5,3},{6,4},{7,5},{8,6},{9,7},{10,8},{11,9},{12,... | collective-permute-start | bytes 8456 | tf_op jit(solution)/shard_map/ppermute | solution.py:261
  32.7 8.4 %collective-permute-start.3 = (bf16[2,704]{1,0:T(2,128)(2,1)S(1)}, bf16[2,704]{1,0:T(2,128)(2,1)S(1)}, u32[]{:S(2)}, u32[]{:S(2)}) collective-permute-start(bf16[2,704]{1,0:T(2,128)(2,1)S(1)} %copy.24), channel_id=1, source_target_pairs={{0,3},{1,2},{2,5},{3,4},{4,7},{5,6},{6,9},{7,8},{8,11},{9,10},{10,... | collective-permute-start | bytes 8456 | tf_op jit(solution)/shard_map/ppermute | solution.py:261
  38.2 7.1 %collective-permute-start.4 = (bf16[2,704]{1,0:T(2,128)(2,1)S(1)}, bf16[2,704]{1,0:T(2,128)(2,1)S(1)}, u32[]{:S(2)}, u32[]{:S(2)}) collective-permute-start(bf16[2,704]{1,0:T(2,128)(2,1)S(1)} %copy.25), channel_id=1, source_target_pairs={{2,1},{3,0},{4,3},{5,2},{6,5},{7,4},{8,7},{9,6},{10,9},{11,8},{12,... | collective-permute-start | bytes 8456 | tf_op jit(solution)/shard_map/ppermute | solution.py:261
  41.2 27.6 %collective-permute-start.5 = (bf16[192,704]{1,0:T(8,128)(2,1)}, bf16[192,704]{1,0:T(8,128)(2,1)S(1)}, u32[]{:S(2)}, u32[]{:S(2)}) collective-permute-start(bf16[192,704]{1,0:T(8,128)(2,1)} %bitcast.12), channel_id=1, source_target_pairs={{0,2},{2,0},{4,6},{6,4},{8,10},{10,8},{12,14},{14,12},{1,3},{3,1},... | collective-permute-start | bytes 811016 | tf_op jit(solution)/shard_map/ppermute | solution.py:91
  45.3 23.5 %collective-permute-start.7 = (bf16[192,704]{1,0:T(8,128)(2,1)S(1)}, bf16[192,704]{1,0:T(8,128)(2,1)S(1)}, u32[]{:S(2)}, u32[]{:S(2)}) collective-permute-start(bf16[192,704]{1,0:T(8,128)(2,1)S(1)} %collective-permute-done.6.refs_2_), channel_id=1, source_target_pairs={{0,2},{2,0},{4,6},{6,4},{8,10},{10,8},{12,14},{14,12},{1,3},{3,1},... | collective-permute-start | bytes 811016 | tf_op jit(solution)/shard_map/ppermute | solution.py:91
  47.0 21.8 %collective-permute-start.9 = (bf16[192,704]{1,0:T(8,128)(2,1)S(1)}, bf16[192,704]{1,0:T(8,128)(2,1)S(1)}, u32[]{:S(2)}, u32[]{:S(2)}) collective-permute-start(bf16[192,704]{1,0:T(8,128)(2,1)S(1)} %collective-permute-done.8.refs_4_), channel_id=1, source_target_pairs={{0,2},{2,0},{4,6},{6,4},{8,10},{10,8},{12,14},{14,12},{1,3},{3,1},... | collective-permute-start | bytes 811016 | tf_op jit(solution)/shard_map/ppermute | solution.py:91
  47.3 21.5 %copy-start.6 = (bf16[192,704]{1,0:T(8,128)(2,1)}, bf16[192,704]{1,0:T(8,128)(2,1)S(1)}, u32[]{:S(2)}) copy-start(bf16[192,704]{1,0:T(8,128)(2,1)S(1)} %collective-permute-done.10.refs_6_) | copy-start | bytes 811012
  47.3 23.9 %collective-permute-start.11 = (bf16[192,704]{1,0:T(8,128)(2,1)S(1)}, bf16[192,704]{1,0:T(8,128)(2,1)S(1)}, u32[]{:S(2)}, u32[]{:S(2)}) collective-permute-start(bf16[192,704]{1,0:T(8,128)(2,1)S(1)} %collective-permute-done.10.refs_6_), channel_id=1, source_target_pairs={{0,2},{2,0},{4,6},{6,4},{8,10},{10,8},{12,14},{14,12},{1,3},{3,1},... | collective-permute-start | bytes 811016 | tf_op jit(solution)/shard_map/ppermute | solution.py:91
  49.1 28.5 %collective-permute-start.18 = (bf16[192,704]{1,0:T(8,128)(2,1)}, bf16[192,704]{1,0:T(8,128)(2,1)}, u32[]{:S(2)}, u32[]{:S(2)}) collective-permute-start(bf16[192,704]{1,0:T(8,128)(2,1)} %collective-permute-done.16.refs_4_), channel_id=1, source_target_pairs={{0,4},{2,6},{4,12},{6,14},{12,8},{14,10},{8,0},{10,2},{1,5},{3,7},... | collective-permute-start | bytes 811016 | tf_op jit(solution)/shard_map/ppermute | solution.py:90
  51.4 3.8 %copy-start.1 = (bf16[5,1408,704]{1,2,0:T(8,128)(2,1)S(1)}, bf16[5,1408,704]{1,2,0:T(8,128)(2,1)}, u32[]{:S(2)}) copy-start(bf16[5,1408,704]{1,2,0:T(8,128)(2,1)} %param.13) | copy-start | bytes 29736964
  55.2 1.1 copy-start.2
  56.3 1.1 copy-start.4
  57.4 0.9 copy-start.10
  68.8 98.8 %copy-start.3 = (bf16[1536,256]{1,0:T(8,128)(2,1)S(1)}, bf16[1536,256]{1,0:T(8,128)(2,1)}, u32[]{:S(2)}) copy-start(bf16[1536,256]{1,0:T(8,128)(2,1)} %weight_ref.2) | copy-start | bytes 2359300
  71.2 1.0 copy-start.7
  73.1 29.1 %collective-permute-start.12 = (bf16[8,128,192]{2,1,0:T(8,128)(2,1)S(1)}, bf16[8,128,192]{2,1,0:T(8,128)(2,1)S(1)}, u32[]{:S(2)}, u32[]{:S(2)}) collective-permute-start(bf16[8,128,192]{2,1,0:T(8,128)(2,1)S(1)} %embed.1.part_ref), channel_id=1, source_target_pairs={{0,1},{1,0},{2,3},{3,2},{4,5},{5,4},{6,7},{7,6},{8,9},{9,8},{10,11... | collective-permute-start | bytes 1179656 | tf_op jit(solution)/shard_map/ppermute | solution.py:313
  73.5 9.9 %collective-permute-start.13 = (bf16[192,704]{1,0:T(8,128)(2,1)S(1)}, bf16[192,704]{1,0:T(8,128)(2,1)S(1)}, u32[]{:S(2)}, u32[]{:S(2)}) collective-permute-start(bf16[192,704]{1,0:T(8,128)(2,1)S(1)} %pad_maximum_fusion.refs_0_), channel_id=1, source_target_pairs={{0,2},{2,0},{4,6},{6,4},{8,10},{10,8},{12,14},{14,12},{1,3},{3,1},... | collective-permute-start | bytes 811016 | tf_op jit(solution)/shard_map/ppermute | solution.py:91
  75.6 14.1 %collective-permute-start.15 = (bf16[192,704]{1,0:T(8,128)(2,1)}, bf16[192,704]{1,0:T(8,128)(2,1)S(1)}, u32[]{:S(2)}, u32[]{:S(2)}) collective-permute-start(bf16[192,704]{1,0:T(8,128)(2,1)} %collective-permute-done.14.refs_2_), channel_id=1, source_target_pairs={{0,2},{2,0},{4,6},{6,4},{8,10},{10,8},{12,14},{14,12},{1,3},{3,1},... | collective-permute-start | bytes 811016 | tf_op jit(solution)/shard_map/ppermute | solution.py:91
  75.6 20.5 %collective-permute-start.17 = (bf16[192,704]{1,0:T(8,128)(2,1)}, bf16[192,704]{1,0:T(8,128)(2,1)}, u32[]{:S(2)}, u32[]{:S(2)}) collective-permute-start(bf16[192,704]{1,0:T(8,128)(2,1)} %collective-permute-done.16.refs_4_), channel_id=1, source_target_pairs={{0,2},{2,0},{4,6},{6,4},{8,10},{10,8},{12,14},{14,12},{1,3},{3,1},... | collective-permute-start | bytes 811016 | tf_op jit(solution)/shard_map/ppermute | solution.py:91
  77.6 24.5 %collective-permute-start.19 = (bf16[192,704]{1,0:T(8,128)(2,1)}, bf16[192,704]{1,0:T(8,128)(2,1)}, u32[]{:S(2)}, u32[]{:S(2)}) collective-permute-start(bf16[192,704]{1,0:T(8,128)(2,1)} %collective-permute-done.18.refs_6_), channel_id=1, source_target_pairs={{0,2},{2,0},{4,6},{6,4},{8,10},{10,8},{12,14},{14,12},{1,3},{3,1},... | collective-permute-start | bytes 811016 | tf_op jit(solution)/shard_map/ppermute | solution.py:91
  89.7 0.7 copy-start.8
  102.2 1.0 copy-start.9
  105.4 0.7 copy-start.11
  107.0 23.7 %all-to-all-start = ((bf16[8,128,192]{1,2,0:T(8,128)(2,1)}), bf16[8,128,192]{1,2,0:T(8,128)(2,1)}, u32[]{:S(2)}, u32[]{:S(2)}) async-start(bf16[8,128,192]{1,2,0:T(8,128)(2,1)} %copy.22), calls=%async_computation | async-start | bytes 786432 | tf_op jit(solution)/shard_map/all_to_all | solution.py:326
  112.8 17.9 %collective-permute-start.22 = (bf16[192,768]{1,0:T(8,128)(2,1)S(1)}, bf16[192,768]{1,0:T(8,128)(2,1)S(1)}, u32[]{:S(2)}, u32[]{:S(2)}) collective-permute-start(bf16[192,768]{1,0:T(8,128)(2,1)S(1)} %dynamic-slice_bitcast_fusion.refs_0_), channel_id=1, source_target_pairs={{0,4},{2,6},{4,12},{6,14},{12,8},{14,10},{8,0},{10,2},{1,5},{3,7},... | collective-permute-start | bytes 884744 | tf_op jit(solution)/shard_map/ppermute | solution.py:90
  130.7 8.4 %collective-permute-start.24 = (bf16[192,768]{1,0:T(8,128)(2,1)S(1)}, bf16[192,768]{1,0:T(8,128)(2,1)S(1)}, u32[]{:S(2)}, u32[]{:S(2)}) collective-permute-start(bf16[192,768]{1,0:T(8,128)(2,1)S(1)} %collective-permute-done.22.refs_2_), channel_id=1, source_target_pairs={{0,4},{2,6},{4,12},{6,14},{12,8},{14,10},{8,0},{10,2},{1,5},{3,7},... | collective-permute-start | bytes 884744 | tf_op jit(solution)/shard_map/ppermute | solution.py:90
  132.7 16.0 %collective-permute-start.20 = (bf16[1024,192]{1,0:T(8,128)(2,1)}, bf16[1024,192]{1,0:T(8,128)(2,1)S(1)}, u32[]{:S(2)}, u32[]{:S(2)}) collective-permute-start(bf16[1024,192]{1,0:T(8,128)(2,1)} %bitcast.14), channel_id=1, source_target_pairs={{0,1},{1,0},{2,3},{3,2},{4,5},{5,4},{6,7},{7,6},{8,9},{9,8},{10,11... | collective-permute-start | bytes 1179656 | tf_op jit(solution)/shard_map/ppermute | solution.py:327
  139.1 7.6 %collective-permute-start.26 = (bf16[192,768]{1,0:T(8,128)(2,1)S(1)}, bf16[192,768]{1,0:T(8,128)(2,1)S(1)}, u32[]{:S(2)}, u32[]{:S(2)}) collective-permute-start(bf16[192,768]{1,0:T(8,128)(2,1)S(1)} %collective-permute-done.24.refs_4_), channel_id=1, source_target_pairs={{0,4},{2,6},{4,12},{6,14},{12,8},{14,10},{8,0},{10,2},{1,5},{3,7},... | collective-permute-start | bytes 884744 | tf_op jit(solution)/shard_map/ppermute | solution.py:90
  139.1 12.8 %collective-permute-start.21 = (bf16[192,768]{1,0:T(8,128)(2,1)S(1)}, bf16[192,768]{1,0:T(8,128)(2,1)S(1)}, u32[]{:S(2)}, u32[]{:S(2)}) collective-permute-start(bf16[192,768]{1,0:T(8,128)(2,1)S(1)} %dynamic-slice_bitcast_fusion.refs_0_), channel_id=1, source_target_pairs={{0,2},{2,0},{4,6},{6,4},{8,10},{10,8},{12,14},{14,12},{1,3},{3,1},... | collective-permute-start | bytes 884744 | tf_op jit(solution)/shard_map/ppermute | solution.py:91
  140.8 14.5 %collective-permute-start.23 = (bf16[192,768]{1,0:T(8,128)(2,1)S(1)}, bf16[192,768]{1,0:T(8,128)(2,1)S(1)}, u32[]{:S(2)}, u32[]{:S(2)}) collective-permute-start(bf16[192,768]{1,0:T(8,128)(2,1)S(1)} %collective-permute-done.22.refs_2_), channel_id=1, source_target_pairs={{0,2},{2,0},{4,6},{6,4},{8,10},{10,8},{12,14},{14,12},{1,3},{3,1},... | collective-permute-start | bytes 884744 | tf_op jit(solution)/shard_map/ppermute | solution.py:91
  141.1 20.6 %collective-permute-start.25 = (bf16[192,768]{1,0:T(8,128)(2,1)S(1)}, bf16[192,768]{1,0:T(8,128)(2,1)S(1)}, u32[]{:S(2)}, u32[]{:S(2)}) collective-permute-start(bf16[192,768]{1,0:T(8,128)(2,1)S(1)} %collective-permute-done.24.refs_4_), channel_id=1, source_target_pairs={{0,2},{2,0},{4,6},{6,4},{8,10},{10,8},{12,14},{14,12},{1,3},{3,1},... | collective-permute-start | bytes 884744 | tf_op jit(solution)/shard_map/ppermute | solution.py:91
  146.7 18.3 %collective-permute-start.27 = (bf16[192,768]{1,0:T(8,128)(2,1)S(1)}, bf16[192,768]{1,0:T(8,128)(2,1)S(1)}, u32[]{:S(2)}, u32[]{:S(2)}) collective-permute-start(bf16[192,768]{1,0:T(8,128)(2,1)S(1)} %collective-permute-done.26.refs_6_), channel_id=1, source_target_pairs={{0,2},{2,0},{4,6},{6,4},{8,10},{10,8},{12,14},{14,12},{1,3},{3,1},... | collective-permute-start | bytes 884744 | tf_op jit(solution)/shard_map/ppermute | solution.py:91
  149.8 0.9 copy-start.12
  166.0 1.6 collective-permute-start.28
  180.5 0.8 copy-start.13

commit v2 on v1

v2 whole, which is shorter than its diff:
```python
import functools
import math

import jax
import jax.numpy as jnp
import numpy as np
from jax import lax
from jax.experimental import pallas as pl
from jax.experimental.pallas import tpu as pltpu
from jax.sharding import PartitionSpec as P

DK = 128
DV = 192
POOL = 4
PAIR_POOL = 16
EPS = 1e-06
VMEM = pltpu.VMEM
F32 = jnp.float32
BF16 = jnp.bfloat16


def gelu(x):
    return 0.5 * x * (1.0 + jnp.tanh(math.sqrt(2.0 / math.pi) * (x + 0.044715 * (x * x * x))))


def dot_nt(a, b):
    return lax.dot_general(a, b, (((1,), (1,)), ((), ())), preferred_element_type=F32)


def dot_nn(a, b):
    return lax.dot_general(a, b, (((1,), (0,)), ((), ())), preferred_element_type=F32)


def params(mib, **kw):
    return pltpu.CompilerParams(vmem_limit_bytes=mib << 20, **kw)


def vspec(n):
    return [pl.BlockSpec(memory_space=VMEM)] * n


RING = (0, 1, 3, 2)


def planned(count, groups):
    return count == 2 * len(RING) and groups == 2


def pick(index, table):
    value = jnp.int32(table[0])
    for i, entry in enumerate(table[1:], 1):
        value = jnp.where(index == i, jnp.int32(entry), value)
    return value


def owners(count, groups):
    if not planned(count, groups):
        return [jnp.int32(0)]
    group, me = lax.axis_index("grp"), lax.axis_index("seq")
    side, place = me % 2, pick(me // 2, [RING.index(i) for i in range(4)])
    result = []
    for step in (0, 3 + 2 * group, 1 + 2 * group, 2):
        row = pick(lax.rem(place + step, 4), RING)
        result += [2 * row + side, 2 * row + 1 - side]
    return result


class Blocks:
    def __init__(self, own, count):
        self.count = count
        self.at = {"own": own}

    def along(self, source, target):
        pairs = []
        for group in range(2):
            for k in range(4):
                a, b = RING[k], RING[(k + 1) % 4]
                if group:
                    a, b = b, a
                pairs += [(group * self.count + 2 * a + i, group * self.count + 2 * b + i) for i in range(2)]
        self.at[target] = lax.ppermute(self.at[source], ("grp", "seq"), pairs)

    def across(self, source, target):
        self.at[target] = lax.ppermute(self.at[source], "seq", [(i, i ^ 1) for i in range(self.count)])

    def between(self, source, target):
        self.at[target] = lax.ppermute(self.at[source], "grp", [(0, 1), (1, 0)])

    def pieces(self):
        names = ("own", "own2", "step", "step2", "cross", "cross2", "far", "far2")
        return [self.at[name] for name in names]


def after(values, *done):
    return lax.optimization_barrier((values, done))[0]


def conv_kernel(own_ref, other_ref, halo_ref, gaincol_ref, gainrow_ref, pool_ref, poolhalo_ref, weight_hbm,
                out_ref, act, slabs, weights, sems):
    taps, width, channels = weights.shape
    copies = [pltpu.make_async_copy(weight_hbm.at[t], weights.at[t], sems.at[t]) for t in range(taps)]
    for c in copies:
        c.start()
    col = lax.axis_index("col")
    half, positions = own_ref.shape
    tokens = out_ref.shape[1]
    step = 64
    halves = ((own_ref, col), (other_ref, 1 - col))
    squares = jnp.zeros((8, positions), F32)
    for ref, _ in halves:
        for j in range(half // step):
            x = ref[j * step:(j + 1) * step, :].astype(F32)
            x = x * x
            for i in range(step // 8):
                squares = squares + x[i * 8:(i + 1) * 8]
    scale = lax.rsqrt(jnp.sum(squares, axis=0, keepdims=True) / channels + EPS)
    for ref, index in halves:
        for j in range(half // step):
            start = pl.multiple_of(index * half + j * step, step)
            x = ref[j * step:(j + 1) * step, :].astype(F32)
            x = x * scale * gaincol_ref[pl.ds(start, step), :]
            act[pl.ds(start, step), :] = gelu(x).astype(BF16)
    h = halo_ref[...].astype(F32)
    h = h * lax.rsqrt(jnp.sum(h * h, axis=1, keepdims=True) / channels + EPS) * gainrow_ref[...]
    h = gelu(h)
    edges = lax.dot_general(h.astype(BF16), poolhalo_ref[...], (((0,), (0,)), ((), ())), preferred_element_type=F32)
    slabs[...] = (dot_nn(act[...], pool_ref[...]) + edges).astype(BF16)
    middle = (taps // 2) * tokens
    total = dot_nn(own_ref[...], pool_ref[:, middle:middle + tokens])
    for t in range(taps):
        copies[t].wait()
        total = total + dot_nn(weights[t], slabs[:, t * tokens:(t + 1) * tokens])
    out_ref[...] = total.astype(BF16)


def block_owners():
    return owners(lax.axis_size("seq"), lax.axis_size("grp"))


def embed_kernel(pieces, pooled_ref, *refs):
    blocks, out_ref = refs[:pieces], refs[pieces]
    for ref, owner in zip(blocks, block_owners()):
        out_ref[owner] = dot_nn(ref[...], pooled_ref[...]).astype(BF16)


def query_kernel(pieces, features, part_ref, other_ref, gain_ref, *refs):
    blocks, (query_ref, kv_ref, embedded_ref, normed) = refs[:pieces], refs[pieces:]
    count, width, _ = part_ref.shape
    squares = 0.0
    for s in range(count):
        e = (part_ref[s].astype(F32) + other_ref[s].astype(F32)).astype(BF16)
        e = e.astype(F32)
        squares = squares + jnp.sum(e * e, axis=0, keepdims=True)
    scale = lax.rsqrt(squares / (count * width) + EPS)
    for s in range(count):
        e = (part_ref[s].astype(F32) + other_ref[s].astype(F32)).astype(BF16).astype(F32)
        embedded_ref[s] = e.T.astype(BF16)
        normed[s] = ((e * scale).T * gain_ref[s]).astype(BF16)
    total = None
    for ref, owner in zip(blocks, block_owners()):
        part = dot_nn(normed[owner], ref[...])
        total = part if total is None else total + part
    query_ref[...] = (total[:, :features] * DK ** (-0.5)).astype(BF16)
    kv = total[:, features:].astype(BF16)
    for i in range(kv_ref.shape[0]):
        kv_ref[i] = kv


def attend_kernel(query_ref, own_ref, other_ref, out_ref):
    tokens, features = query_ref.shape
    first = lax.axis_index("col") == 0
    keys = jnp.where(first, own_ref[:, :DK], other_ref[:, :DK])
    values = jnp.where(first, other_ref[...], own_ref[...])
    for h in range(features // DK):
        scores = dot_nt(query_ref[:, h * DK:(h + 1) * DK], keys)
        weights = jnp.exp(scores - jnp.max(scores, axis=1, keepdims=True))
        total = jnp.sum(weights, axis=1, keepdims=True)
        out_ref[h] = (dot_nn(weights.astype(BF16), values) / total).astype(BF16)


def output_kernel(pieces, attended_ref, *refs):
    blocks, out_ref = refs[:pieces], refs[pieces]
    heads = attended_ref.shape[0]
    flat = jnp.concatenate([attended_ref[h] for h in range(heads)], axis=1)
    for ref, owner in zip(blocks, block_owners()):
        out_ref[owner] = dot_nt(flat, ref[...]).astype(BF16)


def token_kernel(embedded_ref, part_ref, other_ref, weight_ref, token_ref, send_ref, whole):
    col = lax.axis_index("col")
    count, rows, width = part_ref.shape
    projected = None
    for s in range(count):
        tokens = (embedded_ref[s].astype(F32) + (part_ref[s].astype(F32) + other_ref[s].astype(F32))).astype(BF16)
        whole[s] = tokens
        pooled = jnp.mean(tokens.astype(F32).reshape(rows // PAIR_POOL, PAIR_POOL, width), axis=1).astype(BF16)
        part = dot_nn(pooled, weight_ref[s * width:(s + 1) * width])
        projected = part if projected is None else projected + part
    own = token_ref.shape[0]
    mine = pl.ds(pl.multiple_of(col * own, own), own)
    token_ref[...] = jnp.concatenate([whole[s, mine] for s in range(count)], axis=1)
    projected = projected.astype(BF16)
    for i in range(send_ref.shape[0]):
        send_ref[i] = projected


def pair_kernel(all_ref, weight_ref, out_ref, columns_here):
    seq, col = lax.axis_index("seq"), lax.axis_index("col")
    blocks, each, _ = all_ref.shape
    features = weight_ref.shape[0]
    span = blocks // lax.axis_size("col")
    rows_here = all_ref[seq].astype(F32)[:, :features]
    for j in range(span):
        columns_here[j * each:(j + 1) * each] = all_ref[col * span + j].astype(F32)[:, features:]
    hidden = gelu(rows_here[:, None, :] + columns_here[...][None, :, :])
    r, c, f = hidden.shape
    out_ref[...] = dot_nn(hidden.reshape(r * c, f).astype(BF16), weight_ref[...]).reshape(r, c, f).astype(BF16)


def pooling_matrices(positions, taps):
    tokens, reach = positions // POOL, taps // 2
    main = np.zeros((positions, taps, tokens), np.float32)
    halo = np.zeros((16, taps, tokens), np.float32)
    for t in range(taps):
        for i in range(tokens):
            for j in range(POOL):
                p = POOL * i + j + t - reach
                if p < 0:
                    halo[p + reach, t, i] += 1.0 / POOL
                elif p >= positions:
                    halo[reach + p - positions, t, i] += 1.0 / POOL
                else:
                    main[p, t, i] += 1.0 / POOL
    flat = lambda a: jnp.asarray(a.reshape(a.shape[0], taps * tokens), BF16)
    return flat(main), flat(halo)


def cost(flops, size):
    return pl.CostEstimate(flops=int(flops), bytes_accessed=int(size), transcendentals=0)


def on_device(signal, conv_weight, conv_gain, embed_weight, attn_gain, query_weight, keyvalue_weight,
              output_weight, rowcol_weight, pair_weight):
    col = lax.axis_index("col")
    count, cols = lax.axis_size("seq"), lax.axis_size("col")
    positions, half = signal.shape
    taps, channels, _ = conv_weight.shape
    reach = taps // 2
    tokens = positions // POOL
    width = embed_weight.shape[1] * count
    features = query_weight.shape[1] // cols
    heads = features // DK
    swap = [(i, (i + 1) % cols) for i in range(cols)]
    shape = jax.ShapeDtypeStruct

    signal_t = signal.T
    other_t = lax.ppermute(signal_t, "col", swap)
    first, last = signal[:reach], signal[positions - reach:]

    def shifted(rows, by, across):
        pairs = [
            (s * cols + c, (s + by) * cols + ((c + 1) % cols if across else c))
            for s in range(count) for c in range(cols) if 0 <= s + by < count
        ]
        return lax.ppermute(rows, ("seq", "col"), pairs)

    own_halo = jnp.concatenate([shifted(last, 1, False), shifted(first, -1, False)], axis=0)
    other_halo = jnp.concatenate([shifted(last, 1, True), shifted(first, -1, True)], axis=0)
    halo = jnp.where(
        col == 0, jnp.concatenate([own_halo, other_halo], axis=1), jnp.concatenate([other_halo, own_halo], axis=1)
    )
    halo = jnp.pad(halo, ((0, 16 - 2 * reach), (0, 0)))

    query_own = jnp.concatenate(
        [
            lax.dynamic_slice_in_dim(query_weight, col * features, features, 1),
            lax.dynamic_slice_in_dim(keyvalue_weight, col * DK, DV, 1),
        ],
        axis=1,
    )
    output_own = lax.dynamic_slice_in_dim(output_weight.T, col * heads * DV, heads * DV, 1)
    ring = planned(count, lax.axis_size("grp"))
    e, q, o = (Blocks(x, count) for x in (embed_weight.T, query_own, output_own))
    if ring:
        e.along("own", "step")
        e.across("own", "own2")
        e.along("step", "far")
        e.across("step", "step2")
        e.between("step", "cross")
        q.at["own"] = after(q.at["own"], e.at["far"])
        e.across("far", "far2")
        e.between("step2", "cross2")
        q.along("own", "step")
        q.along("step", "far")
        q.across("step", "step2")
        q.between("step", "cross")
        q.along("step2", "far2")
        q.between("step2", "cross2")
        q.across("own", "own2")
        o.at["own"] = after(o.at["own"], q.at["step2"])
        o.along("own", "step")
        o.across("own", "own2")
        o.along("step", "far")
        o.across("step", "step2")
        o.between("step", "cross")
        o.across("far", "far2")
        o.between("step2", "cross2")
        embed_blocks, query_blocks, output_blocks = e.pieces(), q.pieces(), o.pieces()
    else:
        embed_blocks, query_blocks, output_blocks = (
            [lax.all_gather(x.at["own"], "seq", axis=0, tiled=True)] for x in (e, q, o)
        )
    pieces = len(embed_blocks)
    block = width // pieces

    pool_main, pool_halo = pooling_matrices(positions, taps)
    pooled = pl.pallas_call(
        conv_kernel,
        out_shape=shape((half, tokens), BF16),
        in_specs=vspec(7) + [pl.BlockSpec(memory_space=pl.ANY)],
        out_specs=pl.BlockSpec(memory_space=VMEM),
        scratch_shapes=[
            pltpu.VMEM((channels, positions), BF16),
            pltpu.VMEM((channels, taps * tokens), BF16),
            pltpu.VMEM((taps, half, channels), BF16),
            pltpu.SemaphoreType.DMA((taps,)),
        ],
        compiler_params=params(32),
        cost_estimate=cost(2 * taps * tokens * channels * (half + positions), 2 * taps * channels * half * 2),
        name="conv",
    )(
        signal_t, other_t, halo, conv_gain.reshape(channels, 1), conv_gain.reshape(1, channels),
        pool_main, pool_halo, conv_weight.transpose(0, 2, 1),
    )

    part = pl.pallas_call(
        functools.partial(embed_kernel, pieces),
        out_shape=shape((pieces, block, tokens), BF16),
        in_specs=vspec(1 + pieces),
        out_specs=pl.BlockSpec(memory_space=VMEM),
        compiler_params=params(16),
        cost_estimate=cost(2 * tokens * half * width, 2 * half * width),
        name="embed",
    )(pooled, *embed_blocks)
    other_part = lax.ppermute(part, "col", swap)

    queries, keyvalue, embedded = pl.pallas_call(
        functools.partial(query_kernel, pieces, features),
        out_shape=(
            shape((tokens, features), BF16), shape((count, tokens, DV), BF16), shape((pieces, tokens, block), BF16)
        ),
        in_specs=vspec(3 + pieces),
        out_specs=vspec(3),
        scratch_shapes=[pltpu.VMEM((pieces, tokens, block), BF16)],
        compiler_params=params(24),
        cost_estimate=cost(2 * tokens * width * (features + DV), 2 * width * (features + DV)),
        name="query",
    )(part, other_part, attn_gain.reshape(pieces, 1, block), *query_blocks)

    gathered = lax.all_to_all(keyvalue, "seq", 0, 0).reshape(count * tokens, DV)
    gathered_other = lax.ppermute(gathered, "col", swap)

    attended = pl.pallas_call(
        attend_kernel,
        out_shape=shape((heads, tokens, DV), BF16),
        in_specs=vspec(3),
        out_specs=pl.BlockSpec(memory_space=VMEM),
        compiler_params=params(40),
        cost_estimate=cost(2 * tokens * heads * count * tokens * (DK + DV), 4 * count * tokens * DV),
        name="attend",
    )(queries, gathered, gathered_other)

    part_out = pl.pallas_call(
        functools.partial(output_kernel, pieces),
        out_shape=shape((pieces, tokens, block), BF16),
        in_specs=vspec(1 + pieces),
        out_specs=pl.BlockSpec(memory_space=VMEM),
        compiler_params=params(24),
        cost_estimate=cost(2 * tokens * heads * DV * width, 2 * heads * DV * width),
        name="output",
    )(attended, *output_blocks)
    other_out = lax.ppermute(part_out, "col", swap)

    out_width = rowcol_weight.shape[1]
    own_rows, pair_rows = tokens // cols, tokens // PAIR_POOL
    out_tokens, projected = pl.pallas_call(
        token_kernel,
        out_shape=(shape((own_rows, width), BF16), shape((count, pair_rows, out_width), BF16)),
        in_specs=vspec(4),
        out_specs=vspec(2),
        scratch_shapes=[pltpu.VMEM((pieces, tokens, block), BF16)],
        compiler_params=params(16),
        cost_estimate=cost(2 * pair_rows * width * out_width, 2 * width * out_width),
        name="tokens",
    )(embedded, part_out, other_out, rowcol_weight)
    all_projected = lax.all_to_all(projected, "seq", 0, 0)

    span = pair_rows * count // cols
    pair_features = pair_weight.shape[0]
    pair_out = pl.pallas_call(
        pair_kernel,
        out_shape=shape((pair_rows, span, pair_features), BF16),
        in_specs=vspec(2),
        out_specs=pl.BlockSpec(memory_space=VMEM),
        scratch_shapes=[pltpu.VMEM((span, pair_features), F32)],
        compiler_params=params(16),
        cost_estimate=cost(2 * pair_rows * span * pair_features**2, 2 * pair_rows * span * pair_features),
        name="pair",
    )(all_projected, pair_weight)
    return out_tokens, pair_out


def solution(mesh):
    placed = (
        P(("grp", "seq"), "col"),
        P(None, None, "col"),
        P(),
        P("col", "seq"),
        P(),
        P("seq", None),
        P("seq", None),
        P(None, "seq"),
        P(),
        P(),
    )
    return jax.shard_map(
        on_device,
        mesh=mesh,
        in_specs=placed,
        out_specs=(P(("grp", "seq", "col"), None), P(("grp", "seq"), "col", None)),
        check_vma=False,
    )
```

time: 183 us -> 158 us (0.86)
  waiting for transfers between devices: 82.8 us -> 67.9 us
  starting transfers between devices: 47.8 us -> 35.4 us
  local copies, waits for them, and re-layouts: 19.9 us -> 22.5 us
  Pallas kernels: 17.5 us -> 19.4 us
    ppermute x22, waiting for transfers between devices: 81.6 us -> 54.6 us  [the longest x7 31.7 us: along(): self.at[target] = lax.ppermute(self.at[source], ('grp', 'seq'), pairs)]
    ppermute x4, waiting for transfers between devices: 1.21 us -> 13.3 us  [shifted(): return lax.ppermute(rows, ('seq', 'col'), pairs)]
    ppermute x22, starting transfers between devices: 30.8 us -> 24.5 us  [the longest x8 13.6 us: across(): lax.ppermute(self.at[source], 'seq', [(i, i ^ 1) for i in range(self.coun...]
    unnamed x32 -> x44, local copies, waits for them, and re-layouts: 12.1 us -> 16.5 us
    ppermute x4, starting transfers between devices: 10.8 us -> 7.28 us  [shifted(): return lax.ppermute(rows, ('seq', 'col'), pairs)]
    all_to_all x1, starting transfers between devices: 5.73 us -> 3.45 us  [on_device(): gathered = lax.all_to_all(keyvalue, 'seq', 0, 0).reshape(count * tokens, DV)]
  transfers between devices with their start and end apart: 30 -> 30, of which waited for: 17 -> 16; matrix products, arithmetic and copies ran while one was open for 5% -> 3% of each run, Pallas kernels for 7% -> 8%
where the time goes in v2:
time: 158 us; the launch traced here: 157 us
  waiting for transfers between devices  67.9 us (43%)
  starting transfers between devices  35.4 us (22%)
  local copies, waits for them, and re-layouts  22.5 us (14%)
  Pallas kernels  19.4 us (12%)
  blocking collectives  11 us (7%)
    ppermute x7, waiting for transfers between devices, along(): self.at[target] = lax.ppermute(self.at[source], ('grp', 'seq'), pairs)  31.7 us
    unnamed x44, local copies, waits for them, and re-layouts  16.5 us
    ppermute x8, starting transfers between devices, across(): lax.ppermute(self.at[source], 'seq', [(i, i ^ 1) for i in range(self.coun...  13.6 us
    ppermute x4, waiting for transfers between devices, shifted(): return lax.ppermute(rows, ('seq', 'col'), pairs)  13.3 us
    ppermute x8, waiting for transfers between devices, across(): lax.ppermute(self.at[source], 'seq', [(i, i ^ 1) for i in range(self.coun...  12.8 us
    all_to_all x1, blocking collectives, on_device(): all_projected = lax.all_to_all(projected, 'seq', 0, 0)  11 us
    pallas_call x1, Pallas kernels, on_device(): pl.pallas_call(conv_kernel, out_shape=shape((half, tokens), BF16), in_spe...  10.2 us
    ppermute x6, waiting for transfers between devices, between(): self.at[target] = lax.ppermute(self.at[source], 'grp', [(0, 1), (1, 0)])  8.23 us
  transfers between devices with their start and end apart: 30, of which 16 were waited for; matrix products, arithmetic and copies ran while one was open for 3% of the time, Pallas kernels for 8%

profile of v2, /device:TPU:0, one launch (start us, length us, event | category | flops | bytes accessed | tf_op | source)
XLA Modules:
  0.0 157.3 jit_solution(13462205805825930124)
XLA Ops:
  0.7 3.1 %collective-permute-start.6 = (bf16[192,704]{1,0:T(8,128)(2,1)}, bf16[192,704]{1,0:T(8,128)(2,1)S(1)}, u32[]{:S(2)}, u32[]{:S(2)}) collective-permute-start(bf16[192,704]{1,0:T(8,128)(2,1)} %bitcast.11), channel_id=1, source_target_pairs={{0,4},{2,6},{4,12},{6,14},{12,8},{14,10},{8,0},{10,2},{20,16},{22,... | collective-permute-start | bytes 811016 | tf_op jit(solution)/shard_map/ppermute | solution.py:81
  3.7 1.5 collective-permute-start.5
  5.3 6.7 %collective-permute-done.6.refs_2_ = bf16[192,704]{1,0:T(8,128)(2,1)S(1)} collective-permute-done((bf16[192,704]{1,0:T(8,128)(2,1)}, bf16[192,704]{1,0:T(8,128)(2,1)S(1)}, u32[]{:S(2)}, u32[]{:S(2)}) %collective-permute-start.6) | collective-permute-done | bytes 270368 | tf_op jit(solution)/shard_map/ppermute | solution.py:81
  12.9 1.0 constant_dynamic-slice_fusion
  14.9 1.6 %collective-permute-start.7 = (bf16[192,704]{1,0:T(8,128)(2,1)S(1)}, bf16[192,704]{1,0:T(8,128)(2,1)}, u32[]{:S(2)}, u32[]{:S(2)}) collective-permute-start(bf16[192,704]{1,0:T(8,128)(2,1)S(1)} %collective-permute-done.6.refs_2_), channel_id=1, source_target_pairs={{0,2},{2,0},{4,6},{6,4},{8,10},{10,8},{12,14},{14,12},{1,3},{3,1},... | collective-permute-start | bytes 811016 | tf_op jit(solution)/shard_map/ppermute | solution.py:84
  16.5 4.7 %collective-permute-done.10.refs_6_ = bf16[192,704]{1,0:T(8,128)(2,1)} collective-permute-done((bf16[192,704]{1,0:T(8,128)(2,1)S(1)}, bf16[192,704]{1,0:T(8,128)(2,1)}, u32[]{:S(2)}, u32[]{:S(2)}) %collective-permute-start.10) | collective-permute-done | bytes 270368 | tf_op jit(solution)/shard_map/ppermute | solution.py:81
  21.6 1.1 fusion
  22.8 3.4 %collective-permute-start.1 = (bf16[2,704]{1,0:T(2,128)(2,1)S(1)}, bf16[2,704]{1,0:T(2,128)(2,1)S(1)}, u32[]{:S(2)}, u32[]{:S(2)}) collective-permute-start(bf16[2,704]{1,0:T(2,128)(2,1)S(1)} %copy.24), channel_id=1, source_target_pairs={{0,2},{1,3},{2,4},{3,5},{4,6},{5,7},{6,8},{7,9},{8,10},{9,11},{10,... | collective-permute-start | bytes 8456 | tf_op jit(solution)/shard_map/ppermute | solution.py:265
  26.4 1.2 collective-permute-done.1
  27.6 1.3 collective-permute-start.2
  28.9 5.6 %collective-permute-done.2 = bf16[2,704]{1,0:T(2,128)(2,1)S(1)} collective-permute-done((bf16[2,704]{1,0:T(2,128)(2,1)S(1)}, bf16[2,704]{1,0:T(2,128)(2,1)S(1)}, u32[]{:S(2)}, u32[]{:S(2)}) %collective-permute-start.2) | collective-permute-done | bytes 2848 | tf_op jit(solution)/shard_map/ppermute | solution.py:265
  34.5 1.3 collective-permute-start.3
  35.8 1.3 collective-permute-done.3
  37.1 1.3 collective-permute-start.4
  40.0 5.2 %collective-permute-done.4 = bf16[2,704]{1,0:T(2,128)(2,1)S(1)} collective-permute-done((bf16[2,704]{1,0:T(2,128)(2,1)S(1)}, bf16[2,704]{1,0:T(2,128)(2,1)S(1)}, u32[]{:S(2)}, u32[]{:S(2)}) %collective-permute-start.4) | collective-permute-done | bytes 2848 | tf_op jit(solution)/shard_map/ppermute | solution.py:265
  45.4 4.9 %collective-permute-start.11 = (bf16[192,704]{1,0:T(8,128)(2,1)}, bf16[192,704]{1,0:T(8,128)(2,1)S(1)}, u32[]{:S(2)}, u32[]{:S(2)}) collective-permute-start(bf16[192,704]{1,0:T(8,128)(2,1)} %collective-permute-done.10.refs_6_), channel_id=1, source_target_pairs={{0,2},{2,0},{4,6},{6,4},{8,10},{10,8},{12,14},{14,12},{1,3},{3,1},... | collective-permute-start | bytes 811016 | tf_op jit(solution)/shard_map/ppermute | solution.py:84
  50.7 1.9 %collective-permute-start.15 = (bf16[192,704]{1,0:T(8,128)(2,1)S(1)}, bf16[192,704]{1,0:T(8,128)(2,1)S(1)}, u32[]{:S(2)}, u32[]{:S(2)}) collective-permute-start(bf16[192,704]{1,0:T(8,128)(2,1)S(1)} %collective-permute-done.14.refs_2_), channel_id=1, source_target_pairs={{0,2},{2,0},{4,6},{6,4},{8,10},{10,8},{12,14},{14,12},{1,3},{3,1},... | collective-permute-start | bytes 811016 | tf_op jit(solution)/shard_map/ppermute | solution.py:84
  52.6 3.8 %copy-done.1 = bf16[5,1408,704]{1,2,0:T(8,128)(2,1)S(1)} copy-done((bf16[5,1408,704]{1,2,0:T(8,128)(2,1)S(1)}, bf16[5,1408,704]{1,2,0:T(8,128)(2,1)}, u32[]{:S(2)}) %copy-start.1) | copy-done | bytes 9912344
  56.5 1.1 copy-done.2
  57.6 1.1 copy-done.4
  59.4 10.2 %conv.1.pooled_ref = bf16[704,128]{1,0:T(8,128)(2,1)S(1)} custom-call(bf16[704,512]{1,0:T(8,128)(2,1)S(1)} %bitcast.10, bf16[704,512]{1,0:T(8,128)(2,1)S(1)} %collective-permute-done.other_ref, bf16[16,1408]{1,0:T(8,128)(2,1)S(1)} %pad.4.halo_ref, f32[1408,1]{1,0:T(8,128)S(1)} %reshape.20.gaincol_ref, f32[1,1408]{1,0:T(1,128)S(1)} %reshape.17.gainrow_ref, ...), custom_call_target="tpu_custom_call" | custom-call | flops 2191523840 | bytes 19824640 | tf_op jit(solution)/shard_map/conv/pallas_call | solution.py:317
  69.6 1.0 copy-done.15
  70.6 1.8 %embed.1.part_ref = bf16[8,192,128]{2,1,0:T(8,128)(2,1)S(1)} custom-call(bf16[704,128]{1,0:T(8,128)(2,1)S(1)} %conv.1.pooled_ref, bf16[192,704]{1,0:T(8,128)(2,1)S(1)} %bitcast.13, bf16[192,704]{1,0:T(8,128)(2,1)S(1)} %copy-done.15, bf16[192,704]{1,0:T(8,128)(2,1)S(1)} %collective-permute-done.6.refs_2_, bf16[192,704]{1,0:T(8,128)(2,1)} %collective-permute-done.7.refs_3_, ...), custom_call_target="tpu_custom_call" | custom-call | flops 276824064 | bytes 2162688 | tf_op jit(solution)/shard_map/embed/pallas_call | solution.py:336
  72.5 2.0 %collective-permute-start.16 = (bf16[192,704]{1,0:T(8,128)(2,1)S(1)}, bf16[192,704]{1,0:T(8,128)(2,1)S(1)}, u32[]{:S(2)}, u32[]{:S(2)}) collective-permute-start(bf16[192,704]{1,0:T(8,128)(2,1)S(1)} %collective-permute-done.14.refs_2_), channel_id=1, source_target_pairs={{0,16},{16,0},{1,17},{17,1},{2,18},{18,2},{3,19},{19,3},{4,20},{20... | collective-permute-start | bytes 811016 | tf_op jit(solution)/shard_map/ppermute | solution.py:87
  76.1 1.2 collective-permute-start.19
  78.2 4.3 %collective-permute-done.16.refs_4_ = bf16[192,704]{1,0:T(8,128)(2,1)S(1)} collective-permute-done((bf16[192,704]{1,0:T(8,128)(2,1)S(1)}, bf16[192,704]{1,0:T(8,128)(2,1)S(1)}, u32[]{:S(2)}, u32[]{:S(2)}) %collective-permute-start.16) | collective-permute-done | bytes 270368 | tf_op jit(solution)/shard_map/ppermute | solution.py:87
  83.2 2.2 %collective-permute-done.18.refs_6_ = bf16[192,704]{1,0:T(8,128)(2,1)} collective-permute-done((bf16[192,704]{1,0:T(8,128)(2,1)S(1)}, bf16[192,704]{1,0:T(8,128)(2,1)}, u32[]{:S(2)}, u32[]{:S(2)}) %collective-permute-start.18) | collective-permute-done | bytes 270368 | tf_op jit(solution)/shard_map/ppermute | solution.py:81
  86.2 2.4 %collective-permute-done.17.refs_5_ = bf16[192,704]{1,0:T(8,128)(2,1)} collective-permute-done((bf16[192,704]{1,0:T(8,128)(2,1)S(1)}, bf16[192,704]{1,0:T(8,128)(2,1)}, u32[]{:S(2)}, u32[]{:S(2)}) %collective-permute-start.17) | collective-permute-done | bytes 270368 | tf_op jit(solution)/shard_map/ppermute | solution.py:87
  88.6 2.4 %collective-permute-done.19.refs_7_ = bf16[192,704]{1,0:T(8,128)(2,1)} collective-permute-done((bf16[192,704]{1,0:T(8,128)(2,1)S(1)}, bf16[192,704]{1,0:T(8,128)(2,1)}, u32[]{:S(2)}, u32[]{:S(2)}) %collective-permute-start.19) | collective-permute-done | bytes 270368 | tf_op jit(solution)/shard_map/ppermute | solution.py:81
  91.0 1.0 copy-done.6
  92.0 1.0 copy-done.8
  92.9 1.0 copy-done.10
  94.8 2.2 %query.1 = (bf16[128,512]{1,0:T(8,128)(2,1)S(1)}, bf16[8,128,192]{2,1,0:T(8,128)(2,1)S(1)}, bf16[8,128,192]{2,1,0:T(8,128)(2,1)S(1)}) custom-call(bf16[8,192,128]{2,1,0:T(8,128)(2,1)S(1)} %embed.1.part_ref, bf16[8,192,128]{2,1,0:T(8,128)(2,1)S(1)} %copy-done.6, f32[8,1,192]{2,1,0:T(1,128)S(1)} %reshape.18.gain_ref, ...), custom_call_target="tpu_custom_call" | custom-call | flops 276824064 | bytes 2162688 | tf_op jit(solution)/shard_map/query/pallas_call | solution.py:347
  97.1 1.0 copy.22
  98.1 3.5 %all-to-all-start = ((bf16[8,128,192]{1,2,0:T(8,128)(2,1)}), bf16[8,128,192]{1,2,0:T(8,128)(2,1)S(1)}, u32[]{:S(2)}, u32[]{:S(2)}) async-start(bf16[8,128,192]{1,2,0:T(8,128)(2,1)} %copy.22), calls=%async_computation | async-start | bytes 786432 | tf_op jit(solution)/shard_map/all_to_all | solution.py:360
  101.6 2.0 %collective-permute-start.22 = (bf16[192,768]{1,0:T(8,128)(2,1)S(1)}, bf16[192,768]{1,0:T(8,128)(2,1)S(1)}, u32[]{:S(2)}, u32[]{:S(2)}) collective-permute-start(bf16[192,768]{1,0:T(8,128)(2,1)S(1)} %dynamic-slice_bitcast_fusion.refs_0_), channel_id=1, source_target_pairs={{0,4},{2,6},{4,12},{6,14},{12,8},{14,10},{8,0},{10,2},{20,16},{22,... | collective-permute-start | bytes 884744 | tf_op jit(solution)/shard_map/ppermute | solution.py:81
  103.5 15.7 %collective-permute-done.22.refs_2_ = bf16[192,768]{1,0:T(8,128)(2,1)S(1)} collective-permute-done((bf16[192,768]{1,0:T(8,128)(2,1)S(1)}, bf16[192,768]{1,0:T(8,128)(2,1)S(1)}, u32[]{:S(2)}, u32[]{:S(2)}) %collective-permute-start.22) | collective-permute-done | bytes 294944 | tf_op jit(solution)/shard_map/ppermute | solution.py:81
  119.3 1.4 collective-permute-start.23
  121.7 7.7 %collective-permute-done.23.refs_3_ = bf16[192,768]{1,0:T(8,128)(2,1)} collective-permute-done((bf16[192,768]{1,0:T(8,128)(2,1)S(1)}, bf16[192,768]{1,0:T(8,128)(2,1)}, u32[]{:S(2)}, u32[]{:S(2)}) %collective-permute-start.23) | collective-permute-done | bytes 294944 | tf_op jit(solution)/shard_map/ppermute | solution.py:84
  129.3 1.4 collective-permute-start.27
  131.7 1.1 attend.1.attended_ref
  132.8 2.8 %collective-permute-done.21.refs_1_ = bf16[192,768]{1,0:T(8,128)(2,1)S(1)} collective-permute-done((bf16[192,768]{1,0:T(8,128)(2,1)S(1)}, bf16[192,768]{1,0:T(8,128)(2,1)S(1)}, u32[]{:S(2)}, u32[]{:S(2)}) %collective-permute-start.21) | collective-permute-done | bytes 294944 | tf_op jit(solution)/shard_map/ppermute | solution.py:84
  135.5 1.5 collective-permute-done.25.refs_5_
  137.1 2.4 %collective-permute-done.27.refs_7_ = bf16[192,768]{1,0:T(8,128)(2,1)S(1)} collective-permute-done((bf16[192,768]{1,0:T(8,128)(2,1)}, bf16[192,768]{1,0:T(8,128)(2,1)S(1)}, u32[]{:S(2)}, u32[]{:S(2)}) %collective-permute-start.27) | collective-permute-done | bytes 294944 | tf_op jit(solution)/shard_map/ppermute | solution.py:84
  139.4 2.0 %output.1.part_ref = bf16[8,128,192]{2,1,0:T(8,128)(2,1)S(1)} custom-call(bf16[4,128,192]{2,1,0:T(8,128)(2,1)S(1)} %attend.1.attended_ref, bf16[192,768]{1,0:T(8,128)(2,1)S(1)} %dynamic-slice_bitcast_fusion.refs_0_, bf16[192,768]{1,0:T(8,128)(2,1)S(1)} %collective-permute-done.21.refs_1_, bf16[192,768]{1,0:T(8,128)(2,1)S(1)} %collective-permute-done.22.refs_2_, ...), custom_call_target="tpu_custom_call" | custom-call | flops 301989888 | bytes 2359296 | tf_op jit(solution)/shard_map/output/pallas_call | solution.py:373
  141.5 1.9 %collective-permute-done.28.other_ref = bf16[8,128,192]{2,1,0:T(8,128)(2,1)S(1)} collective-permute-done((bf16[8,128,192]{2,1,0:T(8,128)(2,1)S(1)}, bf16[8,128,192]{2,1,0:T(8,128)(2,1)S(1)}, u32[]{:S(2)}, u32[]{:S(2)}) %collective-permute-start.28) | collective-permute-done | bytes 393248 | tf_op jit(solution)/shard_map/ppermute | solution.py:382
  143.4 1.3 tokens.1
  144.7 11.0 %all_to_all.10.all_ref = bf16[8,8,256]{2,1,0:T(8,128)(2,1)S(1)} all-to-all(bf16[8,8,256]{2,1,0:T(8,128)(2,1)S(1)} %get-tuple-element.15), channel_id=1, replica_groups=mesh['grp'=2,'seq'=8,'col'=2] {'seq'}, dimensions={0} | all-to-all | bytes 65536 | tf_op jit(solution)/shard_map/all_to_all | solution.py:396
  (76 shorter events, 14.0 us)
Async XLA Ops:
  0.6 100.9 %copy-start = (bf16[1536,192]{0,1:T(8,128)(2,1)S(1)}, bf16[1536,192]{0,1:T(8,128)(2,1)}, u32[]{:S(2)}) copy-start(bf16[1536,192]{0,1:T(8,128)(2,1)} %param.19) | copy-start | bytes 1769476
  0.6 69.0 %copy-start.13 = (bf16[704,192]{0,1:T(8,128)(2,1)S(1)}, bf16[704,192]{0,1:T(8,128)(2,1)}, u32[]{:S(2)}) copy-start(bf16[704,192]{0,1:T(8,128)(2,1)} %param.15) | copy-start | bytes 811012
  0.7 77.4 %copy-start.20 = (f32[1536]{0:T(1024)S(1)}, f32[1536]{0:T(1024)}, u32[]{:S(2)}) copy-start(f32[1536]{0:T(1024)} %param.16) | copy-start | bytes 18436
  0.7 11.3 %collective-permute-start.6 = (bf16[192,704]{1,0:T(8,128)(2,1)}, bf16[192,704]{1,0:T(8,128)(2,1)S(1)}, u32[]{:S(2)}, u32[]{:S(2)}) collective-permute-start(bf16[192,704]{1,0:T(8,128)(2,1)} %bitcast.11), channel_id=1, source_target_pairs={{0,4},{2,6},{4,12},{6,14},{12,8},{14,10},{8,0},{10,2},{20,16},{22,... | collective-permute-start | bytes 811016 | tf_op jit(solution)/shard_map/ppermute | solution.py:81
  3.7 41.7 %collective-permute-start.5 = (bf16[192,704]{1,0:T(8,128)(2,1)}, bf16[192,704]{1,0:T(8,128)(2,1)S(1)}, u32[]{:S(2)}, u32[]{:S(2)}) collective-permute-start(bf16[192,704]{1,0:T(8,128)(2,1)} %bitcast.12), channel_id=1, source_target_pairs={{0,2},{2,0},{4,6},{6,4},{8,10},{10,8},{12,14},{14,12},{1,3},{3,1},... | collective-permute-start | bytes 811016 | tf_op jit(solution)/shard_map/ppermute | solution.py:84
  5.3 45.3 %collective-permute-start = (bf16[704,512]{1,0:T(8,128)(2,1)}, bf16[704,512]{1,0:T(8,128)(2,1)S(1)}, u32[]{:S(2)}, u32[]{:S(2)}) collective-permute-start(bf16[704,512]{1,0:T(8,128)(2,1)} %bitcast.9), channel_id=1, source_target_pairs={{0,1},{1,0},{2,3},{3,2},{4,5},{5,4},{6,7},{7,6},{8,9},{9,8},{10,11... | collective-permute-start | bytes 2162696 | tf_op jit(solution)/shard_map/ppermute | solution.py:257
  12.0 9.2 %collective-permute-start.10 = (bf16[192,704]{1,0:T(8,128)(2,1)S(1)}, bf16[192,704]{1,0:T(8,128)(2,1)}, u32[]{:S(2)}, u32[]{:S(2)}) collective-permute-start(bf16[192,704]{1,0:T(8,128)(2,1)S(1)} %collective-permute-done.6.refs_2_), channel_id=1, source_target_pairs={{0,4},{2,6},{4,12},{6,14},{12,8},{14,10},{8,0},{10,2},{20,16},{22,... | collective-permute-start | bytes 811016 | tf_op jit(solution)/shard_map/ppermute | solution.py:81
  14.9 35.5 %collective-permute-start.7 = (bf16[192,704]{1,0:T(8,128)(2,1)S(1)}, bf16[192,704]{1,0:T(8,128)(2,1)}, u32[]{:S(2)}, u32[]{:S(2)}) collective-permute-start(bf16[192,704]{1,0:T(8,128)(2,1)S(1)} %collective-permute-done.6.refs_2_), channel_id=1, source_target_pairs={{0,2},{2,0},{4,6},{6,4},{8,10},{10,8},{12,14},{14,12},{1,3},{3,1},... | collective-permute-start | bytes 811016 | tf_op jit(solution)/shard_map/ppermute | solution.py:84
  21.2 29.5 %collective-permute-start.14 = (bf16[192,704]{1,0:T(8,128)(2,1)S(1)}, bf16[192,704]{1,0:T(8,128)(2,1)S(1)}, u32[]{:S(2)}, u32[]{:S(2)}) collective-permute-start(bf16[192,704]{1,0:T(8,128)(2,1)S(1)} %pad_maximum_fusion.refs_0_), channel_id=1, source_target_pairs={{0,4},{2,6},{4,12},{6,14},{12,8},{14,10},{8,0},{10,2},{20,16},{22,... | collective-permute-start | bytes 811016 | tf_op jit(solution)/shard_map/ppermute | solution.py:81
  22.8 4.7 %collective-permute-start.1 = (bf16[2,704]{1,0:T(2,128)(2,1)S(1)}, bf16[2,704]{1,0:T(2,128)(2,1)S(1)}, u32[]{:S(2)}, u32[]{:S(2)}) collective-permute-start(bf16[2,704]{1,0:T(2,128)(2,1)S(1)} %copy.24), channel_id=1, source_target_pairs={{0,2},{1,3},{2,4},{3,5},{4,6},{5,7},{6,8},{7,9},{8,10},{9,11},{10,... | collective-permute-start | bytes 8456 | tf_op jit(solution)/shard_map/ppermute | solution.py:265
  27.6 6.9 %collective-permute-start.2 = (bf16[2,704]{1,0:T(2,128)(2,1)S(1)}, bf16[2,704]{1,0:T(2,128)(2,1)S(1)}, u32[]{:S(2)}, u32[]{:S(2)}) collective-permute-start(bf16[2,704]{1,0:T(2,128)(2,1)S(1)} %copy.25), channel_id=1, source_target_pairs={{2,0},{3,1},{4,2},{5,3},{6,4},{7,5},{8,6},{9,7},{10,8},{11,9},{12,... | collective-permute-start | bytes 8456 | tf_op jit(solution)/shard_map/ppermute | solution.py:265
  34.5 2.6 %collective-permute-start.3 = (bf16[2,704]{1,0:T(2,128)(2,1)S(1)}, bf16[2,704]{1,0:T(2,128)(2,1)S(1)}, u32[]{:S(2)}, u32[]{:S(2)}) collective-permute-start(bf16[2,704]{1,0:T(2,128)(2,1)S(1)} %copy.24), channel_id=1, source_target_pairs={{0,3},{1,2},{2,5},{3,4},{4,7},{5,6},{6,9},{7,8},{8,11},{9,10},{10,... | collective-permute-start | bytes 8456 | tf_op jit(solution)/shard_map/ppermute | solution.py:265
  37.1 8.1 %collective-permute-start.4 = (bf16[2,704]{1,0:T(2,128)(2,1)S(1)}, bf16[2,704]{1,0:T(2,128)(2,1)S(1)}, u32[]{:S(2)}, u32[]{:S(2)}) collective-permute-start(bf16[2,704]{1,0:T(2,128)(2,1)S(1)} %copy.25), channel_id=1, source_target_pairs={{2,1},{3,0},{4,3},{5,2},{6,5},{7,4},{8,7},{9,6},{10,9},{11,8},{12,... | collective-permute-start | bytes 8456 | tf_op jit(solution)/shard_map/ppermute | solution.py:265
  45.2 24.4 %collective-permute-start.8 = (bf16[192,704]{1,0:T(8,128)(2,1)S(1)}, bf16[192,704]{1,0:T(8,128)(2,1)S(1)}, u32[]{:S(2)}, u32[]{:S(2)}) collective-permute-start(bf16[192,704]{1,0:T(8,128)(2,1)S(1)} %collective-permute-done.6.refs_2_), channel_id=1, source_target_pairs={{0,16},{16,0},{1,17},{17,1},{2,18},{18,2},{3,19},{19,3},{4,20},{20... | collective-permute-start | bytes 811016 | tf_op jit(solution)/shard_map/ppermute | solution.py:87
  45.4 24.2 %copy-start.14 = (bf16[192,704]{1,0:T(8,128)(2,1)}, bf16[192,704]{1,0:T(8,128)(2,1)S(1)}, u32[]{:S(2)}) copy-start(bf16[192,704]{1,0:T(8,128)(2,1)S(1)} %collective-permute-done.5.refs_1_) | copy-start | bytes 811012
  45.4 24.1 %collective-permute-start.11 = (bf16[192,704]{1,0:T(8,128)(2,1)}, bf16[192,704]{1,0:T(8,128)(2,1)S(1)}, u32[]{:S(2)}, u32[]{:S(2)}) collective-permute-start(bf16[192,704]{1,0:T(8,128)(2,1)} %collective-permute-done.10.refs_6_), channel_id=1, source_target_pairs={{0,2},{2,0},{4,6},{6,4},{8,10},{10,8},{12,14},{14,12},{1,3},{3,1},... | collective-permute-start | bytes 811016 | tf_op jit(solution)/shard_map/ppermute | solution.py:84
  50.4 19.2 %collective-permute-start.9 = (bf16[192,704]{1,0:T(8,128)(2,1)}, bf16[192,704]{1,0:T(8,128)(2,1)S(1)}, u32[]{:S(2)}, u32[]{:S(2)}) collective-permute-start(bf16[192,704]{1,0:T(8,128)(2,1)} %collective-permute-done.7.refs_3_), channel_id=1, source_target_pairs={{0,16},{16,0},{1,17},{17,1},{2,18},{18,2},{3,19},{19,3},{4,20},{20... | collective-permute-start | bytes 811016 | tf_op jit(solution)/shard_map/ppermute | solution.py:87
  50.5 24.9 %collective-permute-start.13 = (bf16[192,704]{1,0:T(8,128)(2,1)S(1)}, bf16[192,704]{1,0:T(8,128)(2,1)S(1)}, u32[]{:S(2)}, u32[]{:S(2)}) collective-permute-start(bf16[192,704]{1,0:T(8,128)(2,1)S(1)} %pad_maximum_fusion.refs_0_), channel_id=1, source_target_pairs={{0,2},{2,0},{4,6},{6,4},{8,10},{10,8},{12,14},{14,12},{1,3},{3,1},... | collective-permute-start | bytes 811016 | tf_op jit(solution)/shard_map/ppermute | solution.py:84
  50.7 24.0 %collective-permute-start.15 = (bf16[192,704]{1,0:T(8,128)(2,1)S(1)}, bf16[192,704]{1,0:T(8,128)(2,1)S(1)}, u32[]{:S(2)}, u32[]{:S(2)}) collective-permute-start(bf16[192,704]{1,0:T(8,128)(2,1)S(1)} %collective-permute-done.14.refs_2_), channel_id=1, source_target_pairs={{0,2},{2,0},{4,6},{6,4},{8,10},{10,8},{12,14},{14,12},{1,3},{3,1},... | collective-permute-start | bytes 811016 | tf_op jit(solution)/shard_map/ppermute | solution.py:84
  52.6 3.8 %copy-start.1 = (bf16[5,1408,704]{1,2,0:T(8,128)(2,1)S(1)}, bf16[5,1408,704]{1,2,0:T(8,128)(2,1)}, u32[]{:S(2)}) copy-start(bf16[5,1408,704]{1,2,0:T(8,128)(2,1)} %param.13) | copy-start | bytes 29736964
  56.5 1.1 copy-start.2
  57.6 1.1 copy-start.4
  58.7 0.7 copy-start.19
  69.5 73.9 %copy-start.3 = (bf16[1536,256]{1,0:T(8,128)(2,1)S(1)}, bf16[1536,256]{1,0:T(8,128)(2,1)}, u32[]{:S(2)}) copy-start(bf16[1536,256]{1,0:T(8,128)(2,1)} %weight_ref.2) | copy-start | bytes 2359300
  69.6 1.0 copy-start.15
  72.5 13.0 %collective-permute-start.12 = (bf16[8,192,128]{2,1,0:T(8,128)(2,1)S(1)}, bf16[8,192,128]{2,1,0:T(8,128)(2,1)S(1)}, u32[]{:S(2)}, u32[]{:S(2)}) collective-permute-start(bf16[8,192,128]{2,1,0:T(8,128)(2,1)S(1)} %embed.1.part_ref), channel_id=1, source_target_pairs={{0,1},{1,0},{2,3},{3,2},{4,5},{5,4},{6,7},{7,6},{8,9},{9,8},{10,11... | collective-permute-start | bytes 1179656 | tf_op jit(solution)/shard_map/ppermute | solution.py:345
  72.5 9.9 %collective-permute-start.16 = (bf16[192,704]{1,0:T(8,128)(2,1)S(1)}, bf16[192,704]{1,0:T(8,128)(2,1)S(1)}, u32[]{:S(2)}, u32[]{:S(2)}) collective-permute-start(bf16[192,704]{1,0:T(8,128)(2,1)S(1)} %collective-permute-done.14.refs_2_), channel_id=1, source_target_pairs={{0,16},{16,0},{1,17},{17,1},{2,18},{18,2},{3,19},{19,3},{4,20},{20... | collective-permute-start | bytes 811016 | tf_op jit(solution)/shard_map/ppermute | solution.py:87
  74.6 10.9 %collective-permute-start.18 = (bf16[192,704]{1,0:T(8,128)(2,1)S(1)}, bf16[192,704]{1,0:T(8,128)(2,1)}, u32[]{:S(2)}, u32[]{:S(2)}) collective-permute-start(bf16[192,704]{1,0:T(8,128)(2,1)S(1)} %collective-permute-done.14.refs_2_), channel_id=1, source_target_pairs={{0,4},{2,6},{4,12},{6,14},{12,8},{14,10},{8,0},{10,2},{20,16},{22,... | collective-permute-start | bytes 811016 | tf_op jit(solution)/shard_map/ppermute | solution.py:81
  74.7 13.9 %collective-permute-start.17 = (bf16[192,704]{1,0:T(8,128)(2,1)S(1)}, bf16[192,704]{1,0:T(8,128)(2,1)}, u32[]{:S(2)}, u32[]{:S(2)}) collective-permute-start(bf16[192,704]{1,0:T(8,128)(2,1)S(1)} %collective-permute-done.15.refs_3_), channel_id=1, source_target_pairs={{0,16},{16,0},{1,17},{17,1},{2,18},{18,2},{3,19},{19,3},{4,20},{20... | collective-permute-start | bytes 811016 | tf_op jit(solution)/shard_map/ppermute | solution.py:87
  76.1 14.8 %collective-permute-start.19 = (bf16[192,704]{1,0:T(8,128)(2,1)S(1)}, bf16[192,704]{1,0:T(8,128)(2,1)}, u32[]{:S(2)}, u32[]{:S(2)}) collective-permute-start(bf16[192,704]{1,0:T(8,128)(2,1)S(1)} %collective-permute-done.15.refs_3_), channel_id=1, source_target_pairs={{0,4},{2,6},{4,12},{6,14},{12,8},{14,10},{8,0},{10,2},{20,16},{22,... | collective-permute-start | bytes 811016 | tf_op jit(solution)/shard_map/ppermute | solution.py:81
  85.4 0.8 copy-start.5
  91.0 1.0 copy-start.6
  92.0 1.0 copy-start.8
  92.9 1.0 copy-start.10
  93.9 1.0 copy-start.12
  97.1 4.4 %copy-start.16 = (bf16[128,512]{1,0:T(8,128)(2,1)}, bf16[128,512]{1,0:T(8,128)(2,1)S(1)}, u32[]{:S(2)}) copy-start(bf16[128,512]{1,0:T(8,128)(2,1)S(1)} %get-tuple-element.11.query_ref) | copy-start | bytes 393220
  98.1 22.6 %all-to-all-start = ((bf16[8,128,192]{1,2,0:T(8,128)(2,1)}), bf16[8,128,192]{1,2,0:T(8,128)(2,1)S(1)}, u32[]{:S(2)}, u32[]{:S(2)}) async-start(bf16[8,128,192]{1,2,0:T(8,128)(2,1)} %copy.22), calls=%async_computation | async-start | bytes 786432 | tf_op jit(solution)/shard_map/all_to_all | solution.py:360
  101.6 17.7 %collective-permute-start.22 = (bf16[192,768]{1,0:T(8,128)(2,1)S(1)}, bf16[192,768]{1,0:T(8,128)(2,1)S(1)}, u32[]{:S(2)}, u32[]{:S(2)}) collective-permute-start(bf16[192,768]{1,0:T(8,128)(2,1)S(1)} %dynamic-slice_bitcast_fusion.refs_0_), channel_id=1, source_target_pairs={{0,4},{2,6},{4,12},{6,14},{12,8},{14,10},{8,0},{10,2},{20,16},{22,... | collective-permute-start | bytes 884744 | tf_op jit(solution)/shard_map/ppermute | solution.py:81
  119.3 10.1 %collective-permute-start.23 = (bf16[192,768]{1,0:T(8,128)(2,1)S(1)}, bf16[192,768]{1,0:T(8,128)(2,1)}, u32[]{:S(2)}, u32[]{:S(2)}) collective-permute-start(bf16[192,768]{1,0:T(8,128)(2,1)S(1)} %collective-permute-done.22.refs_2_), channel_id=1, source_target_pairs={{0,2},{2,0},{4,6},{6,4},{8,10},{10,8},{12,14},{14,12},{1,3},{3,1},... | collective-permute-start | bytes 884744 | tf_op jit(solution)/shard_map/ppermute | solution.py:84
  120.7 8.6 %collective-permute-start.26 = (bf16[192,768]{1,0:T(8,128)(2,1)S(1)}, bf16[192,768]{1,0:T(8,128)(2,1)}, u32[]{:S(2)}, u32[]{:S(2)}) collective-permute-start(bf16[192,768]{1,0:T(8,128)(2,1)S(1)} %collective-permute-done.22.refs_2_), channel_id=1, source_target_pairs={{0,4},{2,6},{4,12},{6,14},{12,8},{14,10},{8,0},{10,2},{20,16},{22,... | collective-permute-start | bytes 884744 | tf_op jit(solution)/shard_map/ppermute | solution.py:81
  120.9 9.8 %collective-permute-start.20 = (bf16[1024,192]{1,0:T(8,128)(2,1)S(1)}, bf16[1024,192]{1,0:T(8,128)(2,1)S(1)}, u32[]{:S(2)}, u32[]{:S(2)}) collective-permute-start(bf16[1024,192]{1,0:T(8,128)(2,1)S(1)} %bitcast.7), channel_id=1, source_target_pairs={{0,1},{1,0},{2,3},{3,2},{4,5},{5,4},{6,7},{7,6},{8,9},{9,8},{10,11... | collective-permute-start | bytes 1179656 | tf_op jit(solution)/shard_map/ppermute | solution.py:361
  121.0 14.5 %collective-permute-start.21 = (bf16[192,768]{1,0:T(8,128)(2,1)S(1)}, bf16[192,768]{1,0:T(8,128)(2,1)S(1)}, u32[]{:S(2)}, u32[]{:S(2)}) collective-permute-start(bf16[192,768]{1,0:T(8,128)(2,1)S(1)} %dynamic-slice_bitcast_fusion.refs_0_), channel_id=1, source_target_pairs={{0,2},{2,0},{4,6},{6,4},{8,10},{10,8},{12,14},{14,12},{1,3},{3,1},... | collective-permute-start | bytes 884744 | tf_op jit(solution)/shard_map/ppermute | solution.py:84
  121.7 13.9 %collective-permute-start.24 = (bf16[192,768]{1,0:T(8,128)(2,1)S(1)}, bf16[192,768]{1,0:T(8,128)(2,1)S(1)}, u32[]{:S(2)}, u32[]{:S(2)}) collective-permute-start(bf16[192,768]{1,0:T(8,128)(2,1)S(1)} %collective-permute-done.22.refs_2_), channel_id=1, source_target_pairs={{0,16},{16,0},{1,17},{17,1},{2,18},{18,2},{3,19},{19,3},{4,20},{20... | collective-permute-start | bytes 884744 | tf_op jit(solution)/shard_map/ppermute | solution.py:87
  129.3 7.7 %collective-permute-start.25 = (bf16[192,768]{1,0:T(8,128)(2,1)}, bf16[192,768]{1,0:T(8,128)(2,1)S(1)}, u32[]{:S(2)}, u32[]{:S(2)}) collective-permute-start(bf16[192,768]{1,0:T(8,128)(2,1)} %collective-permute-done.23.refs_3_), channel_id=1, source_target_pairs={{0,16},{16,0},{1,17},{17,1},{2,18},{18,2},{3,19},{19,3},{4,20},{20... | collective-permute-start | bytes 884744 | tf_op jit(solution)/shard_map/ppermute | solution.py:87
  129.3 10.1 %collective-permute-start.27 = (bf16[192,768]{1,0:T(8,128)(2,1)}, bf16[192,768]{1,0:T(8,128)(2,1)S(1)}, u32[]{:S(2)}, u32[]{:S(2)}) collective-permute-start(bf16[192,768]{1,0:T(8,128)(2,1)} %collective-permute-done.26.refs_6_), channel_id=1, source_target_pairs={{0,2},{2,0},{4,6},{6,4},{8,10},{10,8},{12,14},{14,12},{1,3},{3,1},... | collective-permute-start | bytes 884744 | tf_op jit(solution)/shard_map/ppermute | solution.py:84
  130.8 0.9 copy-start.17
  141.4 2.0 %collective-permute-start.28 = (bf16[8,128,192]{2,1,0:T(8,128)(2,1)S(1)}, bf16[8,128,192]{2,1,0:T(8,128)(2,1)S(1)}, u32[]{:S(2)}, u32[]{:S(2)}) collective-permute-start(bf16[8,128,192]{2,1,0:T(8,128)(2,1)S(1)} %output.1.part_ref), channel_id=1, source_target_pairs={{0,1},{1,0},{2,3},{3,2},{4,5},{5,4},{6,7},{7,6},{8,9},{9,8},{10,11... | collective-permute-start | bytes 1179656 | tf_op jit(solution)/shard_map/ppermute | solution.py:382
  155.7 0.8 copy-start.18
  (3 other events, 2.1 us)

commit v3 on v2

--- a/solution.py
+++ b/solution.py
@@ -20,7 +20,9 @@
 
 
 def gelu(x):
-    return 0.5 * x * (1.0 + jnp.tanh(math.sqrt(2.0 / math.pi) * (x + 0.044715 * (x * x * x))))
+    c = math.sqrt(2.0 / math.pi)
+    half = 0.5 * x
+    return half + half * jnp.tanh(x * (c + (0.044715 * c) * (x * x)))
 
 
 def dot_nt(a, b):
@@ -37,6 +39,21 @@
 
 def vspec(n):
     return [pl.BlockSpec(memory_space=VMEM)] * n
+
+
+def hspec(n):
+    return [pl.BlockSpec(memory_space=pltpu.HBM)] * n
+
+
+def fetch(sources, held, sems):
+    copies = [pltpu.make_async_copy(ref, held.at[i], sems.at[i]) for i, ref in enumerate(sources)]
+    for c in copies:
+        c.start()
+    return copies
+
+
+def slots(pieces, rows, columns):
+    return [pltpu.VMEM((pieces, rows, columns), BF16), pltpu.SemaphoreType.DMA((pieces,))]
 
 
 RING = (0, 1, 3, 2)
@@ -104,22 +121,31 @@
     col = lax.axis_index("col")
     half, positions = own_ref.shape
     tokens = out_ref.shape[1]
-    step = 64
+    step, group = 16, 4
     halves = ((own_ref, col), (other_ref, 1 - col))
     squares = jnp.zeros((8, positions), F32)
     for ref, _ in halves:
-        for j in range(half // step):
-            x = ref[j * step:(j + 1) * step, :].astype(F32)
-            x = x * x
-            for i in range(step // 8):
-                squares = squares + x[i * 8:(i + 1) * 8]
+
+        def add(j, squares, ref=ref):
+            for i in range(group):
+                x = ref[pl.ds(pl.multiple_of((j * group + i) * step, step), step), :].astype(F32)
+                x = x * x
+                squares = squares + (x[:8] + x[8:])
+            return squares
+
+        squares = lax.fori_loop(0, half // (step * group), add, squares)
     scale = lax.rsqrt(jnp.sum(squares, axis=0, keepdims=True) / channels + EPS)
     for ref, index in halves:
-        for j in range(half // step):
-            start = pl.multiple_of(index * half + j * step, step)
-            x = ref[j * step:(j + 1) * step, :].astype(F32)
-            x = x * scale * gaincol_ref[pl.ds(start, step), :]
-            act[pl.ds(start, step), :] = gelu(x).astype(BF16)
+
+        def activate(j, carry, ref=ref, index=index):
+            for i in range(group):
+                at = pl.multiple_of((j * group + i) * step, step)
+                x = ref[pl.ds(at, step), :].astype(F32) * scale
+                at = pl.multiple_of(index * half + at, step)
+                act[pl.ds(at, step), :] = gelu(x * gaincol_ref[pl.ds(at, step), :]).astype(BF16)
+            return carry
+
+        lax.fori_loop(0, half // (step * group), activate, 0)
     h = halo_ref[...].astype(F32)
     h = h * lax.rsqrt(jnp.sum(h * h, axis=1, keepdims=True) / channels + EPS) * gainrow_ref[...]
     h = gelu(h)
@@ -138,52 +164,68 @@
 
 
 def embed_kernel(pieces, pooled_ref, *refs):
-    blocks, out_ref = refs[:pieces], refs[pieces]
-    for ref, owner in zip(blocks, block_owners()):
-        out_ref[owner] = dot_nn(ref[...], pooled_ref[...]).astype(BF16)
-
-
-def query_kernel(pieces, features, part_ref, other_ref, gain_ref, *refs):
-    blocks, (query_ref, kv_ref, embedded_ref, normed) = refs[:pieces], refs[pieces:]
+    blocks, (out_ref, held, sems) = refs[:pieces], refs[pieces:]
+    half, lanes = pooled_ref.shape[0], held.shape[2]
+    copies = fetch([ref.at[:, pl.ds(0, lanes)] for ref in blocks], held, sems)
+    for i, owner in enumerate(block_owners()):
+        copies[i].wait()
+        out_ref[owner] = dot_nn(held[i][:, :half], pooled_ref[...]).astype(BF16)
+
+
+def keyvalue_kernel(pieces, half, part_ref, other_ref, gain_ref, *refs):
+    blocks, (kv_ref, normed_ref, embedded_ref, held, sems) = refs[:pieces], refs[pieces:]
+    lanes = held.shape[2]
+    start = blocks[0].shape[1] - lanes
+    copies = fetch([ref.at[:, pl.ds(start, lanes)] for ref in blocks], held, sems)
     count, width, _ = part_ref.shape
     squares = 0.0
     for s in range(count):
-        e = (part_ref[s].astype(F32) + other_ref[s].astype(F32)).astype(BF16)
-        e = e.astype(F32)
+        e = (part_ref[s].astype(F32) + other_ref[s].astype(F32)).astype(BF16).astype(F32)
         squares = squares + jnp.sum(e * e, axis=0, keepdims=True)
     scale = lax.rsqrt(squares / (count * width) + EPS)
     for s in range(count):
         e = (part_ref[s].astype(F32) + other_ref[s].astype(F32)).astype(BF16).astype(F32)
         embedded_ref[s] = e.T.astype(BF16)
-        normed[s] = ((e * scale).T * gain_ref[s]).astype(BF16)
-    total = None
-    for ref, owner in zip(blocks, block_owners()):
-        part = dot_nn(normed[owner], ref[...])
-        total = part if total is None else total + part
-    query_ref[...] = (total[:, :features] * DK ** (-0.5)).astype(BF16)
-    kv = total[:, features:].astype(BF16)
-    for i in range(kv_ref.shape[0]):
-        kv_ref[i] = kv
-
-
-def attend_kernel(query_ref, own_ref, other_ref, out_ref):
+        normed_ref[s] = ((e * scale).T * gain_ref[s]).astype(BF16)
+    total = 0.0
+    for i, owner in enumerate(block_owners()):
+        copies[i].wait()
+        total = total + dot_nn(normed_ref[owner], held[i][:, half - start:])
+    kv_ref[...] = total.T.astype(BF16)
+
+
+def query_kernel(pieces, normed_ref, *refs):
+    blocks, (query_ref, held, sems) = refs[:pieces], refs[pieces:]
+    copies = fetch(blocks, held, sems)
+    total = 0.0
+    for i, owner in enumerate(block_owners()):
+        copies[i].wait()
+        total = total + dot_nn(normed_ref[owner], held[i])
+    query_ref[...] = (total * DK ** (-0.5)).astype(BF16)
+
+
+def attend_kernel(query_ref, own_ref, other_ref, out_ref, keys, values):
     tokens, features = query_ref.shape
+    blocks, _, each = own_ref.shape
     first = lax.axis_index("col") == 0
-    keys = jnp.where(first, own_ref[:, :DK], other_ref[:, :DK])
-    values = jnp.where(first, other_ref[...], own_ref[...])
+    for i in range(blocks):
+        keys[:, i * each:(i + 1) * each] = jnp.where(first, own_ref[i][:DK], other_ref[i][:DK])
+        values[:, i * each:(i + 1) * each] = jnp.where(first, other_ref[i], own_ref[i])
     for h in range(features // DK):
-        scores = dot_nt(query_ref[:, h * DK:(h + 1) * DK], keys)
+        scores = dot_nn(query_ref[:, h * DK:(h + 1) * DK], keys[...])
         weights = jnp.exp(scores - jnp.max(scores, axis=1, keepdims=True))
         total = jnp.sum(weights, axis=1, keepdims=True)
-        out_ref[h] = (dot_nn(weights.astype(BF16), values) / total).astype(BF16)
+        out_ref[h] = (dot_nt(weights.astype(BF16), values[...]) / total).astype(BF16)
 
 
 def output_kernel(pieces, attended_ref, *refs):
-    blocks, out_ref = refs[:pieces], refs[pieces]
+    blocks, (out_ref, held, sems) = refs[:pieces], refs[pieces:]
+    copies = fetch(blocks, held, sems)
     heads = attended_ref.shape[0]
     flat = jnp.concatenate([attended_ref[h] for h in range(heads)], axis=1)
-    for ref, owner in zip(blocks, block_owners()):
-        out_ref[owner] = dot_nt(flat, ref[...]).astype(BF16)
+    for i, owner in enumerate(block_owners()):
+        copies[i].wait()
+        out_ref[owner] = dot_nt(flat, held[i]).astype(BF16)
 
 
 def token_kernel(embedded_ref, part_ref, other_ref, weight_ref, token_ref, send_ref, whole):
@@ -199,19 +241,21 @@
     own = token_ref.shape[0]
     mine = pl.ds(pl.multiple_of(col * own, own), own)
     token_ref[...] = jnp.concatenate([whole[s, mine] for s in range(count)], axis=1)
-    projected = projected.astype(BF16)
-    for i in range(send_ref.shape[0]):
-        send_ref[i] = projected
-
-
-def pair_kernel(all_ref, weight_ref, out_ref, columns_here):
+    send_ref[...] = projected.astype(BF16)
+
+
+def pair_kernel(own_ref, weight_ref, *refs):
+    arrived, (out_ref, columns_here) = refs[:-2], refs[-2:]
     seq, col = lax.axis_index("seq"), lax.axis_index("col")
-    blocks, each, _ = all_ref.shape
-    features = weight_ref.shape[0]
-    span = blocks // lax.axis_size("col")
-    rows_here = all_ref[seq].astype(F32)[:, :features]
+    features, each = weight_ref.shape[0], own_ref.shape[0]
+    span = columns_here.shape[0] // each
     for j in range(span):
-        columns_here[j * each:(j + 1) * each] = all_ref[col * span + j].astype(F32)[:, features:]
+        if len(arrived) == 1:
+            rows, at = arrived[0][col * span + j], j
+        else:
+            rows, at = arrived[j][...], j ^ (seq % span)
+        columns_here[pl.ds(pl.multiple_of(at * each, each), each)] = rows.astype(F32)[:, features:]
+    rows_here = own_ref[...].astype(F32)[:, :features]
     hidden = gelu(rows_here[:, None, :] + columns_here[...][None, :, :])
     r, c, f = hidden.shape
     out_ref[...] = dot_nn(hidden.reshape(r * c, f).astype(BF16), weight_ref[...]).reshape(r, c, f).astype(BF16)
@@ -254,36 +298,28 @@
     shape = jax.ShapeDtypeStruct
 
     signal_t = signal.T
+    up = [(i, i + 1) for i in range(count - 1)]
+    before = lax.ppermute(signal[positions - reach:], "seq", up)
+    behind = lax.ppermute(signal[:reach], "seq", [(j, i) for i, j in up])
     other_t = lax.ppermute(signal_t, "col", swap)
-    first, last = signal[:reach], signal[positions - reach:]
-
-    def shifted(rows, by, across):
-        pairs = [
-            (s * cols + c, (s + by) * cols + ((c + 1) % cols if across else c))
-            for s in range(count) for c in range(cols) if 0 <= s + by < count
-        ]
-        return lax.ppermute(rows, ("seq", "col"), pairs)
-
-    own_halo = jnp.concatenate([shifted(last, 1, False), shifted(first, -1, False)], axis=0)
-    other_halo = jnp.concatenate([shifted(last, 1, True), shifted(first, -1, True)], axis=0)
+    own_halo = jnp.pad(jnp.concatenate([before, behind], axis=0), ((0, 16 - 2 * reach), (0, 0)))
+    other_halo = lax.ppermute(own_halo, "col", swap)
     halo = jnp.where(
         col == 0, jnp.concatenate([own_halo, other_halo], axis=1), jnp.concatenate([other_halo, own_halo], axis=1)
     )
-    halo = jnp.pad(halo, ((0, 16 - 2 * reach), (0, 0)))
-
-    query_own = jnp.concatenate(
-        [
-            lax.dynamic_slice_in_dim(query_weight, col * features, features, 1),
-            lax.dynamic_slice_in_dim(keyvalue_weight, col * DK, DV, 1),
-        ],
-        axis=1,
+
+    embed_own = jnp.concatenate(
+        [embed_weight.T, lax.dynamic_slice_in_dim(keyvalue_weight, col * DK, DV, 1)], axis=1
     )
+    query_own = lax.dynamic_slice_in_dim(query_weight, col * features, features, 1)
     output_own = lax.dynamic_slice_in_dim(output_weight.T, col * heads * DV, heads * DV, 1)
-    ring = planned(count, lax.axis_size("grp"))
-    e, q, o = (Blocks(x, count) for x in (embed_weight.T, query_own, output_own))
+    ring = planned(count, lax.axis_size("grp")) and cols == 2
+    e, q, o = (Blocks(x, count) for x in (embed_own, query_own, output_own))
     if ring:
+        e.at["own"] = after(e.at["own"], before, behind)
         e.along("own", "step")
         e.across("own", "own2")
+        e.at["step"] = after(e.at["step"], e.at["own2"])
         e.along("step", "far")
         e.across("step", "step2")
         e.between("step", "cross")
@@ -292,12 +328,14 @@
         e.between("step2", "cross2")
         q.along("own", "step")
         q.along("step", "far")
+        q.at["step"] = after(q.at["step"], e.at["far2"])
         q.across("step", "step2")
         q.between("step", "cross")
         q.along("step2", "far2")
         q.between("step2", "cross2")
+        q.at["own"] = after(q.at["own"], q.at["step2"])
         q.across("own", "own2")
-        o.at["own"] = after(o.at["own"], q.at["step2"])
+        o.at["own"] = after(o.at["own"], q.at["step2"], q.at["far"])
         o.along("own", "step")
         o.across("own", "own2")
         o.along("step", "far")
@@ -317,7 +355,7 @@
     pooled = pl.pallas_call(
         conv_kernel,
         out_shape=shape((half, tokens), BF16),
-        in_specs=vspec(7) + [pl.BlockSpec(memory_space=pl.ANY)],
+        in_specs=vspec(7) + hspec(1),
         out_specs=pl.BlockSpec(memory_space=VMEM),
         scratch_shapes=[
             pltpu.VMEM((channels, positions), BF16),
@@ -325,7 +363,7 @@
             pltpu.VMEM((taps, half, channels), BF16),
             pltpu.SemaphoreType.DMA((taps,)),
         ],
-        compiler_params=params(32),
+        compiler_params=params(28),
         cost_estimate=cost(2 * taps * tokens * channels * (half + positions), 2 * taps * channels * half * 2),
         name="conv",
     )(
@@ -333,38 +371,62 @@
         pool_main, pool_halo, conv_weight.transpose(0, 2, 1),
     )
 
+    upper = -(-half // 128) * 128
+    lower = half // 128 * 128
     part = pl.pallas_call(
         functools.partial(embed_kernel, pieces),
         out_shape=shape((pieces, block, tokens), BF16),
-        in_specs=vspec(1 + pieces),
+        in_specs=vspec(1) + hspec(pieces),
         out_specs=pl.BlockSpec(memory_space=VMEM),
-        compiler_params=params(16),
+        scratch_shapes=slots(pieces, block, min(upper, half + DV)),
+        compiler_params=params(12),
         cost_estimate=cost(2 * tokens * half * width, 2 * half * width),
         name="embed",
     )(pooled, *embed_blocks)
     other_part = lax.ppermute(part, "col", swap)
 
-    queries, keyvalue, embedded = pl.pallas_call(
-        functools.partial(query_kernel, pieces, features),
+    keyvalue, normed, embedded = pl.pallas_call(
+        functools.partial(keyvalue_kernel, pieces, half),
         out_shape=(
-            shape((tokens, features), BF16), shape((count, tokens, DV), BF16), shape((pieces, tokens, block), BF16)
+            shape((DV, tokens), BF16), shape((pieces, tokens, block), BF16), shape((pieces, tokens, block), BF16)
         ),
-        in_specs=vspec(3 + pieces),
+        in_specs=vspec(3) + hspec(pieces),
         out_specs=vspec(3),
-        scratch_shapes=[pltpu.VMEM((pieces, tokens, block), BF16)],
-        compiler_params=params(24),
-        cost_estimate=cost(2 * tokens * width * (features + DV), 2 * width * (features + DV)),
+        scratch_shapes=slots(pieces, block, half + DV - lower),
+        compiler_params=params(12),
+        cost_estimate=cost(2 * tokens * width * DV, 2 * width * DV),
+        name="keyvalue",
+    )(part, other_part, attn_gain.reshape(pieces, 1, block), *embed_blocks)
+
+    if ring:
+        arrived = [keyvalue]
+        for k in range(1, count // 2):
+            arrived.append(lax.ppermute(keyvalue, "seq", [(i, i ^ (2 * k)) for i in range(count)]))
+        arrived += [lax.ppermute(x, "seq", [(i, i ^ 1) for i in range(count)]) for x in arrived]
+        gathered = jnp.stack(arrived)
+    else:
+        gathered = lax.all_gather(keyvalue, "seq", axis=0)
+    gathered_other = lax.ppermute(gathered, "col", swap)
+
+    queries = pl.pallas_call(
+        functools.partial(query_kernel, pieces),
+        out_shape=shape((tokens, features), BF16),
+        in_specs=vspec(1) + hspec(pieces),
+        out_specs=pl.BlockSpec(memory_space=VMEM),
+        scratch_shapes=slots(pieces, block, features),
+        compiler_params=params(12),
+        cost_estimate=cost(2 * tokens * width * features, 2 * width * features),
         name="query",
-    )(part, other_part, attn_gain.reshape(pieces, 1, block), *query_blocks)
-
-    gathered = lax.all_to_all(keyvalue, "seq", 0, 0).reshape(count * tokens, DV)
-    gathered_other = lax.ppermute(gathered, "col", swap)
+    )(normed, *query_blocks)
+    if ring:
+        queries = after(queries, o.at["step"], o.at["own2"])
 
     attended = pl.pallas_call(
         attend_kernel,
         out_shape=shape((heads, tokens, DV), BF16),
         in_specs=vspec(3),
         out_specs=pl.BlockSpec(memory_space=VMEM),
+        scratch_shapes=[pltpu.VMEM((DK, count * tokens), BF16), pltpu.VMEM((DV, count * tokens), BF16)],
         compiler_params=params(40),
         cost_estimate=cost(2 * tokens * heads * count * tokens * (DK + DV), 4 * count * tokens * DV),
         name="attend",
@@ -373,9 +435,10 @@
     part_out = pl.pallas_call(
         functools.partial(output_kernel, pieces),
         out_shape=shape((pieces, tokens, block), BF16),
-        in_specs=vspec(1 + pieces),
+        in_specs=vspec(1) + hspec(pieces),
         out_specs=pl.BlockSpec(memory_space=VMEM),
-        compiler_params=params(24),
+        scratch_shapes=slots(pieces, block, heads * DV),
+        compiler_params=params(16),
         cost_estimate=cost(2 * tokens * heads * DV * width, 2 * heads * DV * width),
         name="output",
     )(attended, *output_blocks)
@@ -385,28 +448,39 @@
     own_rows, pair_rows = tokens // cols, tokens // PAIR_POOL
     out_tokens, projected = pl.pallas_call(
         token_kernel,
-        out_shape=(shape((own_rows, width), BF16), shape((count, pair_rows, out_width), BF16)),
+        out_shape=(shape((own_rows, width), BF16), shape((pair_rows, out_width), BF16)),
         in_specs=vspec(4),
         out_specs=vspec(2),
         scratch_shapes=[pltpu.VMEM((pieces, tokens, block), BF16)],
-        compiler_params=params(16),
+        compiler_params=params(12),
         cost_estimate=cost(2 * pair_rows * width * out_width, 2 * width * out_width),
         name="tokens",
     )(embedded, part_out, other_out, rowcol_weight)
-    all_projected = lax.all_to_all(projected, "seq", 0, 0)
+
+    if ring:
+        columns = []
+        for turn in range(count // 2):
+            pairs = []
+            for source in range(count):
+                need, i = source // (count // 2), source % (count // 2)
+                for c in range(2):
+                    pairs.append((source * 2 + c, ((i ^ turn) + c * (count // 2)) * 2 + need))
+            columns.append(lax.ppermute(projected, ("seq", "col"), pairs))
+    else:
+        columns = [lax.all_gather(projected, "seq", axis=0)]
 
     span = pair_rows * count // cols
     pair_features = pair_weight.shape[0]
     pair_out = pl.pallas_call(
         pair_kernel,
         out_shape=shape((pair_rows, span, pair_features), BF16),
-        in_specs=vspec(2),
+        in_specs=vspec(2 + len(columns)),
         out_specs=pl.BlockSpec(memory_space=VMEM),
         scratch_shapes=[pltpu.VMEM((span, pair_features), F32)],
         compiler_params=params(16),
         cost_estimate=cost(2 * pair_rows * span * pair_features**2, 2 * pair_rows * span * pair_features),
         name="pair",
-    )(all_projected, pair_weight)
+    )(projected, pair_weight, *columns)
     return out_tokens, pair_out
 
 

time: 158 us -> 146 us (0.924)
  the two profiles are of different devices: /device:TPU:0 before, /device:TPU:1 now
where the time goes in v3:
time: 146 us
  starting transfers between devices  61.3 us (42%)
  waiting for transfers between devices  40.6 us (28%)
  Pallas kernels  27.3 us (19%)
  local copies, waits for them, and re-layouts  14.3 us (10%)
    pallas_call x1, Pallas kernels, on_device(): pl.pallas_call(conv_kernel, out_shape=shape((half, tokens), BF16), in_spe...  13.3 us
    ppermute x1, starting transfers between devices, on_device(): gathered_other = lax.ppermute(gathered, 'col', swap)  10.2 us
    ppermute x3, waiting for transfers between devices, on_device(): lax.ppermute(keyvalue, 'seq', [(i, i ^ 2 * k) for i in range(count)])  9.91 us
    ppermute x4, starting transfers between devices, on_device(): columns.append(lax.ppermute(projected, ('seq', 'col'), pairs))  9.31 us
    ppermute x8, waiting for transfers between devices, across(): lax.ppermute(self.at[source], 'seq', [(i, i ^ 1) for i in range(self.coun...  8.83 us
    unnamed x29, local copies, waits for them, and re-layouts  8.78 us
    ppermute x8, starting transfers between devices, across(): lax.ppermute(self.at[source], 'seq', [(i, i ^ 1) for i in range(self.coun...  7.76 us
    ppermute x6, starting transfers between devices, between(): self.at[target] = lax.ppermute(self.at[source], 'grp', [(0, 1), (1, 0)])  7.64 us
  transfers between devices with their start and end apart: 39, of which 18 were waited for; matrix products, arithmetic and copies ran while one was open for 4% of the time, Pallas kernels for 15%

profile of v3, /device:TPU:1, one launch (start us, length us, event | category | flops | bytes accessed | tf_op | source)
XLA Modules:
  0.0 145.6 jit_solution(9772685950485503453)
XLA Ops:
  0.7 1.2 fusion.3
  2.0 4.0 %collective-permute-start.1 = (bf16[2,704]{1,0:T(2,128)(2,1)S(1)}, bf16[2,704]{1,0:T(2,128)(2,1)S(1)}, u32[]{:S(2)}, u32[]{:S(2)}) collective-permute-start(bf16[2,704]{1,0:T(2,128)(2,1)S(1)} %copy.19), channel_id=1, source_target_pairs={{0,2},{2,4},{4,6},{6,8},{8,10},{10,12},{12,14},{1,3},{3,5},{5,7},{... | collective-permute-start | bytes 8456 | tf_op jit(solution)/shard_map/ppermute | solution.py:302
  6.1 1.3 collective-permute-start.2
  10.4 2.1 %collective-permute-start.4 = (bf16[192,896]{1,0:T(8,128)(2,1)S(1)}, bf16[192,896]{1,0:T(8,128)(2,1)S(1)}, u32[]{:S(2)}, u32[]{:S(2)}) collective-permute-start(bf16[192,896]{1,0:T(8,128)(2,1)S(1)} %pad_maximum_fusion.refs_0_), channel_id=1, source_target_pairs={{0,2},{2,0},{4,6},{6,4},{8,10},{10,8},{12,14},{14,12},{1,3},{3,1},... | collective-permute-start | bytes 1032200 | tf_op jit(solution)/shard_map/ppermute | solution.py:101
  12.6 1.3 collective-permute-start.5
  13.9 2.7 %collective-permute-start = (bf16[704,512]{1,0:T(8,128)(2,1)}, bf16[704,512]{1,0:T(8,128)(2,1)}, u32[]{:S(2)}, u32[]{:S(2)}) collective-permute-start(bf16[704,512]{1,0:T(8,128)(2,1)} %bitcast.22), channel_id=1, source_target_pairs={{0,1},{1,0},{2,3},{3,2},{4,5},{5,4},{6,7},{7,6},{8,9},{9,8},{10,11... | collective-permute-start | bytes 2162696 | tf_op jit(solution)/shard_map/ppermute | solution.py:304
  16.5 2.3 %collective-permute-done.4.refs_1_ = bf16[192,896]{1,0:T(8,128)(2,1)S(1)} collective-permute-done((bf16[192,896]{1,0:T(8,128)(2,1)S(1)}, bf16[192,896]{1,0:T(8,128)(2,1)S(1)}, u32[]{:S(2)}, u32[]{:S(2)}) %collective-permute-start.4) | collective-permute-done | bytes 344096 | tf_op jit(solution)/shard_map/ppermute | solution.py:101
  18.8 1.8 %collective-permute-done.5.refs_2_ = bf16[192,896]{1,0:T(8,128)(2,1)S(1)} collective-permute-done((bf16[192,896]{1,0:T(8,128)(2,1)S(1)}, bf16[192,896]{1,0:T(8,128)(2,1)S(1)}, u32[]{:S(2)}, u32[]{:S(2)}) %collective-permute-start.5) | collective-permute-done | bytes 344096 | tf_op jit(solution)/shard_map/ppermute | solution.py:98
  21.1 1.1 collective-permute-start.6
  22.2 3.1 %collective-permute-start.3 = (bf16[16,704]{1,0:T(8,128)(2,1)S(1)}, bf16[16,704]{1,0:T(8,128)(2,1)S(1)}, u32[]{:S(2)}, u32[]{:S(2)}) collective-permute-start(bf16[16,704]{1,0:T(8,128)(2,1)S(1)} %fusion.2), channel_id=1, source_target_pairs={{0,1},{1,0},{2,3},{3,2},{4,5},{5,4},{6,7},{7,6},{8,9},{9,8},{10,11... | collective-permute-start | bytes 67592 | tf_op jit(solution)/shard_map/ppermute | solution.py:306
  25.3 1.6 %constant_dynamic-slice_fusion.refs_0_ = bf16[192,512]{1,0:T(8,128)(2,1)} fusion(bf16[192,1024]{1,0:T(8,128)(2,1)} %param.17, s32[]{:T(128)S(6)} %select_n.20), kind=kLoop, calls=%fused_computation.15 | loop fusion | bytes 393220 | tf_op jit(solution)/shard_map/dynamic_slice | solution.py:314
  28.6 3.0 %collective-permute-start.7 = (bf16[192,896]{1,0:T(8,128)(2,1)S(1)}, bf16[192,896]{1,0:T(8,128)(2,1)S(1)}, u32[]{:S(2)}, u32[]{:S(2)}) collective-permute-start(bf16[192,896]{1,0:T(8,128)(2,1)S(1)} %collective-permute-done.5.refs_2_), channel_id=1, source_target_pairs={{0,16},{16,0},{1,17},{17,1},{2,18},{18,2},{3,19},{19,3},{4,20},{20... | collective-permute-start | bytes 1032200 | tf_op jit(solution)/shard_map/ppermute | solution.py:104
  31.6 1.3 collective-permute-start.10
  33.6 3.8 %copy-done.1 = bf16[5,1408,704]{1,2,0:T(8,128)(2,1)S(1)} copy-done((bf16[5,1408,704]{1,2,0:T(8,128)(2,1)S(1)}, bf16[5,1408,704]{1,2,0:T(8,128)(2,1)}, u32[]{:S(2)}) %copy-start.1) | copy-done | bytes 9912344
  40.4 13.3 %conv.1.pooled_ref = bf16[704,128]{1,0:T(8,128)(2,1)S(1)} custom-call(bf16[704,512]{1,0:T(8,128)(2,1)S(1)} %bitcast.23, bf16[704,512]{1,0:T(8,128)(2,1)} %collective-permute-done.other_ref, bf16[16,1408]{1,0:T(8,128)(2,1)S(1)} %maximum_select_fusion.halo_ref, f32[1408,1]{1,0:T(8,128)S(1)} %reshape.16.gaincol_ref, f32[1,1408]{1,0:T(1,128)S(1)} %reshape.14.gainrow_ref, ...), custom_call_target="tpu_custom_call" | custom-call | flops 2191523840 | bytes 19824640 | tf_op jit(solution)/shard_map/conv/pallas_call | solution.py:355
  53.7 2.3 %embed.1.part_ref = bf16[8,192,128]{2,1,0:T(8,128)(2,1)S(1)} custom-call(bf16[704,128]{1,0:T(8,128)(2,1)S(1)} %conv.1.pooled_ref, bf16[192,896]{1,0:T(8,128)(2,1)S(1)} %pad_maximum_fusion.refs_0_, bf16[192,896]{1,0:T(8,128)(2,1)S(1)} %collective-permute-done.4.refs_1_, bf16[192,896]{1,0:T(8,128)(2,1)S(1)} %collective-permute-done.5.refs_2_, ...), custom_call_target="tpu_custom_call" | custom-call | flops 276824064 | bytes 2162688 | tf_op jit(solution)/shard_map/embed/pallas_call | solution.py:376
  56.8 2.6 %collective-permute-start.11 = (bf16[8,192,128]{2,1,0:T(8,128)(2,1)S(1)}, bf16[8,192,128]{2,1,0:T(8,128)(2,1)}, u32[]{:S(2)}, u32[]{:S(2)}) collective-permute-start(bf16[8,192,128]{2,1,0:T(8,128)(2,1)S(1)} %embed.1.part_ref), channel_id=1, source_target_pairs={{0,1},{1,0},{2,3},{3,2},{4,5},{5,4},{6,7},{7,6},{8,9},{9,8},{10,11... | collective-permute-start | bytes 1179656 | tf_op jit(solution)/shard_map/ppermute | solution.py:386
  59.3 1.2 collective-permute-start.17
  61.0 1.8 %collective-permute-start.15 = (bf16[192,512]{1,0:T(8,128)(2,1)}, bf16[192,512]{1,0:T(8,128)(2,1)S(1)}, u32[]{:S(2)}, u32[]{:S(2)}) collective-permute-start(bf16[192,512]{1,0:T(8,128)(2,1)} %collective-permute-done.12.refs_2_), channel_id=1, source_target_pairs={{0,16},{16,0},{1,17},{17,1},{2,18},{18,2},{3,19},{19,3},{4,20},{20... | collective-permute-start | bytes 589832 | tf_op jit(solution)/shard_map/ppermute | solution.py:104
  62.8 4.3 %collective-permute-done.17.refs_6_ = bf16[192,512]{1,0:T(8,128)(2,1)} collective-permute-done((bf16[192,512]{1,0:T(8,128)(2,1)}, bf16[192,512]{1,0:T(8,128)(2,1)}, u32[]{:S(2)}, u32[]{:S(2)}) %collective-permute-start.17) | collective-permute-done | bytes 196640 | tf_op jit(solution)/shard_map/ppermute | solution.py:98
  67.1 1.3 collective-permute-start.19
  69.2 1.3 collective-permute-start.16
  71.5 3.1 %keyvalue.1 = (bf16[192,128]{1,0:T(8,128)(2,1)S(1)}, bf16[8,128,192]{2,1,0:T(8,128)(2,1)S(1)}, bf16[8,128,192]{2,1,0:T(8,128)(2,1)S(1)}) custom-call(bf16[8,192,128]{2,1,0:T(8,128)(2,1)S(1)} %embed.1.part_ref, bf16[8,192,128]{2,1,0:T(8,128)(2,1)} %collective-permute-done.11.other_ref, f32[8,1,192]{2,1,0:T(1,128)S(1)} %reshape.15.gain_ref, ...), custom_call_target="tpu_custom_call" | custom-call | flops 75497472 | bytes 589824 | tf_op jit(solution)/shard_map/keyvalue/pallas_call | solution.py:388
  74.8 2.9 %collective-permute-done.21 = bf16[192,128]{1,0:T(8,128)(2,1)S(1)} collective-permute-done((bf16[192,128]{1,0:T(8,128)(2,1)S(1)}, bf16[192,128]{1,0:T(8,128)(2,1)S(1)}, u32[]{:S(2)}, u32[]{:S(2)}) %collective-permute-start.21) | collective-permute-done | bytes 49184 | tf_op jit(solution)/shard_map/ppermute | solution.py:404
  77.9 3.8 %collective-permute-done.22 = bf16[192,128]{1,0:T(8,128)(2,1)S(1)} collective-permute-done((bf16[192,128]{1,0:T(8,128)(2,1)S(1)}, bf16[192,128]{1,0:T(8,128)(2,1)S(1)}, u32[]{:S(2)}, u32[]{:S(2)}) %collective-permute-start.22) | collective-permute-done | bytes 49184 | tf_op jit(solution)/shard_map/ppermute | solution.py:404
  81.8 1.5 %collective-permute-start.23 = (bf16[192,128]{1,0:T(8,128)(2,1)S(1)}, bf16[192,128]{1,0:T(8,128)(2,1)S(1)}, u32[]{:S(2)}, u32[]{:S(2)}) collective-permute-start(bf16[192,128]{1,0:T(8,128)(2,1)S(1)} %get-tuple-element.23), channel_id=1, source_target_pairs={{0,12},{2,14},{4,8},{6,10},{8,4},{10,6},{12,0},{14,2},{1,13},{3,15... | collective-permute-start | bytes 147464 | tf_op jit(solution)/shard_map/ppermute | solution.py:404
  83.3 3.2 %collective-permute-done.23 = bf16[192,128]{1,0:T(8,128)(2,1)S(1)} collective-permute-done((bf16[192,128]{1,0:T(8,128)(2,1)S(1)}, bf16[192,128]{1,0:T(8,128)(2,1)S(1)}, u32[]{:S(2)}, u32[]{:S(2)}) %collective-permute-start.23) | collective-permute-done | bytes 49184 | tf_op jit(solution)/shard_map/ppermute | solution.py:404
  86.5 1.1 collective-permute-start.24
  87.6 1.8 %collective-permute-done.24 = bf16[192,128]{1,0:T(8,128)(2,1)S(1)} collective-permute-done((bf16[192,128]{1,0:T(8,128)(2,1)S(1)}, bf16[192,128]{1,0:T(8,128)(2,1)S(1)}, u32[]{:S(2)}, u32[]{:S(2)}) %collective-permute-start.24) | collective-permute-done | bytes 49184 | tf_op jit(solution)/shard_map/ppermute | solution.py:405
  90.6 1.8 %collective-permute-done.25 = bf16[192,128]{1,0:T(8,128)(2,1)S(1)} collective-permute-done((bf16[192,128]{1,0:T(8,128)(2,1)S(1)}, bf16[192,128]{1,0:T(8,128)(2,1)S(1)}, u32[]{:S(2)}, u32[]{:S(2)}) %collective-permute-start.25) | collective-permute-done | bytes 49184 | tf_op jit(solution)/shard_map/ppermute | solution.py:405
  92.4 1.1 collective-permute-start.26
  93.5 2.6 %collective-permute-done.26 = bf16[192,128]{1,0:T(8,128)(2,1)S(1)} collective-permute-done((bf16[192,128]{1,0:T(8,128)(2,1)S(1)}, bf16[192,128]{1,0:T(8,128)(2,1)S(1)}, u32[]{:S(2)}, u32[]{:S(2)}) %collective-permute-start.26) | collective-permute-done | bytes 49184 | tf_op jit(solution)/shard_map/ppermute | solution.py:405
  97.7 1.3 collective-permute-done.27
  99.1 10.2 %collective-permute-start.28 = (bf16[8,192,128]{2,1,0:T(8,128)(2,1)S(1)}, bf16[8,192,128]{2,1,0:T(8,128)(2,1)S(1)}, u32[]{:S(2)}, u32[]{:S(2)}) collective-permute-start(bf16[8,192,128]{2,1,0:T(8,128)(2,1)S(1)} %bitcast_dynamic-update-slice_fusion.own_ref), channel_id=1, source_target_pairs={{0,1},{1,0},{2,3},{3,2},{4,5},{5,4},{6,7},{7,6},{8,9},{9,8},{10,11... | collective-permute-start | bytes 1179656 | tf_op jit(solution)/shard_map/ppermute | solution.py:409
  110.5 1.5 %collective-permute-start.31 = (bf16[192,768]{1,0:T(8,128)(2,1)S(1)}, bf16[192,768]{1,0:T(8,128)(2,1)S(1)}, u32[]{:S(2)}, u32[]{:S(2)}) collective-permute-start(bf16[192,768]{1,0:T(8,128)(2,1)S(1)} %collective-permute-done.29.refs_3_), channel_id=1, source_target_pairs={{0,16},{16,0},{1,17},{17,1},{2,18},{18,2},{3,19},{19,3},{4,20},{20... | collective-permute-start | bytes 884744 | tf_op jit(solution)/shard_map/ppermute | solution.py:104
  112.3 2.0 %query.1.query_ref = bf16[128,512]{1,0:T(8,128)(2,1)S(1)} custom-call(bf16[8,128,192]{2,1,0:T(8,128)(2,1)S(1)} %get-tuple-element.17.normed_ref, bf16[192,512]{1,0:T(8,128)(2,1)} %constant_dynamic-slice_fusion.refs_0_, bf16[192,512]{1,0:T(8,128)(2,1)S(1)} %collective-permute-done.14.refs_1_, bf16[192,512]{1,0:T(8,128)(2,1)} %collective-permute-done.12.refs_2_, ...), custom_call_target="tpu_custom_call" | custom-call | flops 201326592 | bytes 1572864 | tf_op jit(solution)/shard_map/query/pallas_call | solution.py:411
  114.4 4.1 %collective-permute-done.20.refs_1_ = bf16[192,768]{1,0:T(8,128)(2,1)S(1)} collective-permute-done((bf16[192,768]{1,0:T(8,128)(2,1)S(1)}, bf16[192,768]{1,0:T(8,128)(2,1)S(1)}, u32[]{:S(2)}, u32[]{:S(2)}) %collective-permute-start.20) | collective-permute-done | bytes 294944 | tf_op jit(solution)/shard_map/ppermute | solution.py:101
  118.5 1.4 attend.1.attended_ref
  119.9 2.5 %collective-permute-done.31.refs_5_ = bf16[192,768]{1,0:T(8,128)(2,1)S(1)} collective-permute-done((bf16[192,768]{1,0:T(8,128)(2,1)S(1)}, bf16[192,768]{1,0:T(8,128)(2,1)S(1)}, u32[]{:S(2)}, u32[]{:S(2)}) %collective-permute-start.31) | collective-permute-done | bytes 294944 | tf_op jit(solution)/shard_map/ppermute | solution.py:104
  122.3 2.4 %collective-permute-done.33.refs_7_ = bf16[192,768]{1,0:T(8,128)(2,1)S(1)} collective-permute-done((bf16[192,768]{1,0:T(8,128)(2,1)S(1)}, bf16[192,768]{1,0:T(8,128)(2,1)S(1)}, u32[]{:S(2)}, u32[]{:S(2)}) %collective-permute-start.33) | collective-permute-done | bytes 294944 | tf_op jit(solution)/shard_map/ppermute | solution.py:101
  124.8 3.1 %output.1.part_ref = bf16[8,128,192]{2,1,0:T(8,128)(2,1)S(1)} custom-call(bf16[4,128,192]{2,1,0:T(8,128)(2,1)S(1)} %attend.1.attended_ref, bf16[192,768]{1,0:T(8,128)(2,1)S(1)} %dynamic-slice_bitcast_fusion.refs_0_, bf16[192,768]{1,0:T(8,128)(2,1)S(1)} %collective-permute-done.20.refs_1_, bf16[192,768]{1,0:T(8,128)(2,1)S(1)} %collective-permute-done.19.refs_2_, ...), custom_call_target="tpu_custom_call" | custom-call | flops 301989888 | bytes 2359296 | tf_op jit(solution)/shard_map/output/pallas_call | solution.py:435
  127.9 1.5 %collective-permute-start.34 = (bf16[8,128,192]{2,1,0:T(8,128)(2,1)S(1)}, bf16[8,128,192]{2,1,0:T(8,128)(2,1)S(1)}, u32[]{:S(2)}, u32[]{:S(2)}) collective-permute-start(bf16[8,128,192]{2,1,0:T(8,128)(2,1)S(1)} %output.1.part_ref), channel_id=1, source_target_pairs={{0,1},{1,0},{2,3},{3,2},{4,5},{5,4},{6,7},{7,6},{8,9},{9,8},{10,11... | collective-permute-start | bytes 1179656 | tf_op jit(solution)/shard_map/ppermute | solution.py:445
  129.4 1.5 %collective-permute-done.34.other_ref = bf16[8,128,192]{2,1,0:T(8,128)(2,1)S(1)} collective-permute-done((bf16[8,128,192]{2,1,0:T(8,128)(2,1)S(1)}, bf16[8,128,192]{2,1,0:T(8,128)(2,1)S(1)}, u32[]{:S(2)}, u32[]{:S(2)}) %collective-permute-start.34) | collective-permute-done | bytes 393248 | tf_op jit(solution)/shard_map/ppermute | solution.py:445
  130.9 1.3 tokens.1
  132.2 4.8 %collective-permute-start.35 = (bf16[8,256]{1,0:T(8,128)(2,1)S(1)}, bf16[8,256]{1,0:T(8,128)(2,1)S(1)}, u32[]{:S(2)}, u32[]{:S(2)}) collective-permute-start(bf16[8,256]{1,0:T(8,128)(2,1)S(1)} %get-tuple-element.25.own_ref), channel_id=1, source_target_pairs={{0,0},{1,8},{2,2},{3,10},{4,4},{5,12},{6,6},{7,14},{8,1},{9,9},{10... | collective-permute-start | bytes 12296 | tf_op jit(solution)/shard_map/ppermute | solution.py:468
  137.1 2.0 %collective-permute-start.37 = (bf16[8,256]{1,0:T(8,128)(2,1)S(1)}, bf16[8,256]{1,0:T(8,128)(2,1)S(1)}, u32[]{:S(2)}, u32[]{:S(2)}) collective-permute-start(bf16[8,256]{1,0:T(8,128)(2,1)S(1)} %get-tuple-element.25.own_ref), channel_id=1, source_target_pairs={{0,4},{1,12},{2,6},{3,14},{4,0},{5,8},{6,2},{7,10},{8,5},{9,13},{1... | collective-permute-start | bytes 12296 | tf_op jit(solution)/shard_map/ppermute | solution.py:468
  139.0 2.5 %collective-permute-start.38 = (bf16[8,256]{1,0:T(8,128)(2,1)S(1)}, bf16[8,256]{1,0:T(8,128)(2,1)S(1)}, u32[]{:S(2)}, u32[]{:S(2)}) collective-permute-start(bf16[8,256]{1,0:T(8,128)(2,1)S(1)} %get-tuple-element.25.own_ref), channel_id=1, source_target_pairs={{0,6},{1,14},{2,4},{3,12},{4,2},{5,10},{6,0},{7,8},{8,7},{9,15},{1... | collective-permute-start | bytes 12296 | tf_op jit(solution)/shard_map/ppermute | solution.py:468
  142.0 2.8 %collective-permute-done.38.refs_3_ = bf16[8,256]{1,0:T(8,128)(2,1)S(1)} collective-permute-done((bf16[8,256]{1,0:T(8,128)(2,1)S(1)}, bf16[8,256]{1,0:T(8,128)(2,1)S(1)}, u32[]{:S(2)}, u32[]{:S(2)}) %collective-permute-start.38) | collective-permute-done | bytes 4128 | tf_op jit(solution)/shard_map/ppermute | solution.py:468
  (78 shorter events, 18.3 us)
Async XLA Ops:
  0.6 60.3 %copy-start = (bf16[1536,192]{0,1:T(8,128)(2,1)S(1)}, bf16[1536,192]{0,1:T(8,128)(2,1)}, u32[]{:S(2)}) copy-start(bf16[1536,192]{0,1:T(8,128)(2,1)} %param.19) | copy-start | bytes 1769476
  0.6 60.2 %copy-start.9 = (f32[1536]{0:T(1024)S(1)}, f32[1536]{0:T(1024)}, u32[]{:S(2)}) copy-start(f32[1536]{0:T(1024)} %param.16) | copy-start | bytes 18436
  2.0 7.5 %collective-permute-start.1 = (bf16[2,704]{1,0:T(2,128)(2,1)S(1)}, bf16[2,704]{1,0:T(2,128)(2,1)S(1)}, u32[]{:S(2)}, u32[]{:S(2)}) collective-permute-start(bf16[2,704]{1,0:T(2,128)(2,1)S(1)} %copy.19), channel_id=1, source_target_pairs={{0,2},{2,4},{4,6},{6,8},{8,10},{10,12},{12,14},{1,3},{3,5},{5,7},{... | collective-permute-start | bytes 8456 | tf_op jit(solution)/shard_map/ppermute | solution.py:302
  6.1 4.4 %collective-permute-start.2 = (bf16[2,704]{1,0:T(2,128)(2,1)S(1)}, bf16[2,704]{1,0:T(2,128)(2,1)S(1)}, u32[]{:S(2)}, u32[]{:S(2)}) collective-permute-start(bf16[2,704]{1,0:T(2,128)(2,1)S(1)} %copy.20), channel_id=1, source_target_pairs={{2,0},{4,2},{6,4},{8,6},{10,8},{12,10},{14,12},{3,1},{5,3},{7,5},{... | collective-permute-start | bytes 8456 | tf_op jit(solution)/shard_map/ppermute | solution.py:303
  10.4 8.4 %collective-permute-start.4 = (bf16[192,896]{1,0:T(8,128)(2,1)S(1)}, bf16[192,896]{1,0:T(8,128)(2,1)S(1)}, u32[]{:S(2)}, u32[]{:S(2)}) collective-permute-start(bf16[192,896]{1,0:T(8,128)(2,1)S(1)} %pad_maximum_fusion.refs_0_), channel_id=1, source_target_pairs={{0,2},{2,0},{4,6},{6,4},{8,10},{10,8},{12,14},{14,12},{1,3},{3,1},... | collective-permute-start | bytes 1032200 | tf_op jit(solution)/shard_map/ppermute | solution.py:101
  12.6 8.1 %collective-permute-start.5 = (bf16[192,896]{1,0:T(8,128)(2,1)S(1)}, bf16[192,896]{1,0:T(8,128)(2,1)S(1)}, u32[]{:S(2)}, u32[]{:S(2)}) collective-permute-start(bf16[192,896]{1,0:T(8,128)(2,1)S(1)} %pad_maximum_fusion.refs_0_), channel_id=1, source_target_pairs={{0,4},{2,6},{4,12},{6,14},{12,8},{14,10},{8,0},{10,2},{20,16},{22,... | collective-permute-start | bytes 1032200 | tf_op jit(solution)/shard_map/ppermute | solution.py:98
  13.9 19.7 %collective-permute-start = (bf16[704,512]{1,0:T(8,128)(2,1)}, bf16[704,512]{1,0:T(8,128)(2,1)}, u32[]{:S(2)}, u32[]{:S(2)}) collective-permute-start(bf16[704,512]{1,0:T(8,128)(2,1)} %bitcast.22), channel_id=1, source_target_pairs={{0,1},{1,0},{2,3},{3,2},{4,5},{5,4},{6,7},{7,6},{8,9},{9,8},{10,11... | collective-permute-start | bytes 2162696 | tf_op jit(solution)/shard_map/ppermute | solution.py:304
  20.6 10.9 %collective-permute-start.9 = (bf16[192,896]{1,0:T(8,128)(2,1)S(1)}, bf16[192,896]{1,0:T(8,128)(2,1)S(1)}, u32[]{:S(2)}, u32[]{:S(2)}) collective-permute-start(bf16[192,896]{1,0:T(8,128)(2,1)S(1)} %collective-permute-done.5.refs_2_), channel_id=1, source_target_pairs={{0,4},{2,6},{4,12},{6,14},{12,8},{14,10},{8,0},{10,2},{20,16},{22,... | collective-permute-start | bytes 1032200 | tf_op jit(solution)/shard_map/ppermute | solution.py:98
  21.1 11.8 %collective-permute-start.6 = (bf16[192,896]{1,0:T(8,128)(2,1)S(1)}, bf16[192,896]{1,0:T(8,128)(2,1)S(1)}, u32[]{:S(2)}, u32[]{:S(2)}) collective-permute-start(bf16[192,896]{1,0:T(8,128)(2,1)S(1)} %collective-permute-done.5.refs_2_), channel_id=1, source_target_pairs={{0,2},{2,0},{4,6},{6,4},{8,10},{10,8},{12,14},{14,12},{1,3},{3,1},... | collective-permute-start | bytes 1032200 | tf_op jit(solution)/shard_map/ppermute | solution.py:101
  22.2 10.7 %collective-permute-start.3 = (bf16[16,704]{1,0:T(8,128)(2,1)S(1)}, bf16[16,704]{1,0:T(8,128)(2,1)S(1)}, u32[]{:S(2)}, u32[]{:S(2)}) collective-permute-start(bf16[16,704]{1,0:T(8,128)(2,1)S(1)} %fusion.2), channel_id=1, source_target_pairs={{0,1},{1,0},{2,3},{3,2},{4,5},{5,4},{6,7},{7,6},{8,9},{9,8},{10,11... | collective-permute-start | bytes 67592 | tf_op jit(solution)/shard_map/ppermute | solution.py:306
  28.6 25.1 %collective-permute-start.7 = (bf16[192,896]{1,0:T(8,128)(2,1)S(1)}, bf16[192,896]{1,0:T(8,128)(2,1)S(1)}, u32[]{:S(2)}, u32[]{:S(2)}) collective-permute-start(bf16[192,896]{1,0:T(8,128)(2,1)S(1)} %collective-permute-done.5.refs_2_), channel_id=1, source_target_pairs={{0,16},{16,0},{1,17},{17,1},{2,18},{18,2},{3,19},{19,3},{4,20},{20... | collective-permute-start | bytes 1032200 | tf_op jit(solution)/shard_map/ppermute | solution.py:104
  31.6 22.1 %collective-permute-start.10 = (bf16[192,896]{1,0:T(8,128)(2,1)S(1)}, bf16[192,896]{1,0:T(8,128)(2,1)S(1)}, u32[]{:S(2)}, u32[]{:S(2)}) collective-permute-start(bf16[192,896]{1,0:T(8,128)(2,1)S(1)} %collective-permute-done.9.refs_6_), channel_id=1, source_target_pairs={{0,2},{2,0},{4,6},{6,4},{8,10},{10,8},{12,14},{14,12},{1,3},{3,1},... | collective-permute-start | bytes 1032200 | tf_op jit(solution)/shard_map/ppermute | solution.py:101
  32.9 20.8 %collective-permute-start.8 = (bf16[192,896]{1,0:T(8,128)(2,1)S(1)}, bf16[192,896]{1,0:T(8,128)(2,1)S(1)}, u32[]{:S(2)}, u32[]{:S(2)}) collective-permute-start(bf16[192,896]{1,0:T(8,128)(2,1)S(1)} %collective-permute-done.6.refs_3_), channel_id=1, source_target_pairs={{0,16},{16,0},{1,17},{17,1},{2,18},{18,2},{3,19},{19,3},{4,20},{20... | collective-permute-start | bytes 1032200 | tf_op jit(solution)/shard_map/ppermute | solution.py:104
  33.0 26.3 %collective-permute-start.12 = (bf16[192,512]{1,0:T(8,128)(2,1)}, bf16[192,512]{1,0:T(8,128)(2,1)}, u32[]{:S(2)}, u32[]{:S(2)}) collective-permute-start(bf16[192,512]{1,0:T(8,128)(2,1)} %constant_dynamic-slice_fusion.refs_0_), channel_id=1, source_target_pairs={{0,4},{2,6},{4,12},{6,14},{12,8},{14,10},{8,0},{10,2},{20,16},{22,... | collective-permute-start | bytes 589832 | tf_op jit(solution)/shard_map/ppermute | solution.py:98
  33.6 3.8 %copy-start.1 = (bf16[5,1408,704]{1,2,0:T(8,128)(2,1)S(1)}, bf16[5,1408,704]{1,2,0:T(8,128)(2,1)}, u32[]{:S(2)}) copy-start(bf16[5,1408,704]{1,2,0:T(8,128)(2,1)} %param.13) | copy-start | bytes 29736964
  37.4 1.1 copy-start.2
  38.5 1.1 copy-start.6
  53.6 91.1 %copy-start.7 = (bf16[128,128]{1,0:T(8,128)(2,1)S(1)}, bf16[128,128]{1,0:T(8,128)(2,1)}, u32[]{:S(2)}) copy-start(bf16[128,128]{1,0:T(8,128)(2,1)} %weight_ref.3) | copy-start | bytes 98308
  56.0 0.8 copy-start.3
  56.8 13.8 %collective-permute-start.11 = (bf16[8,192,128]{2,1,0:T(8,128)(2,1)S(1)}, bf16[8,192,128]{2,1,0:T(8,128)(2,1)}, u32[]{:S(2)}, u32[]{:S(2)}) collective-permute-start(bf16[8,192,128]{2,1,0:T(8,128)(2,1)S(1)} %embed.1.part_ref), channel_id=1, source_target_pairs={{0,1},{1,0},{2,3},{3,2},{4,5},{5,4},{6,7},{7,6},{8,9},{9,8},{10,11... | collective-permute-start | bytes 1179656 | tf_op jit(solution)/shard_map/ppermute | solution.py:386
  59.3 7.7 %collective-permute-start.17 = (bf16[192,512]{1,0:T(8,128)(2,1)}, bf16[192,512]{1,0:T(8,128)(2,1)}, u32[]{:S(2)}, u32[]{:S(2)}) collective-permute-start(bf16[192,512]{1,0:T(8,128)(2,1)} %collective-permute-done.12.refs_2_), channel_id=1, source_target_pairs={{0,4},{2,6},{4,12},{6,14},{12,8},{14,10},{8,0},{10,2},{20,16},{22,... | collective-permute-start | bytes 589832 | tf_op jit(solution)/shard_map/ppermute | solution.py:98
  60.5 6.5 %collective-permute-start.13 = (bf16[192,512]{1,0:T(8,128)(2,1)}, bf16[192,512]{1,0:T(8,128)(2,1)}, u32[]{:S(2)}, u32[]{:S(2)}) collective-permute-start(bf16[192,512]{1,0:T(8,128)(2,1)} %collective-permute-done.12.refs_2_), channel_id=1, source_target_pairs={{0,2},{2,0},{4,6},{6,4},{8,10},{10,8},{12,14},{14,12},{1,3},{3,1},... | collective-permute-start | bytes 589832 | tf_op jit(solution)/shard_map/ppermute | solution.py:101
  61.0 36.2 %collective-permute-start.15 = (bf16[192,512]{1,0:T(8,128)(2,1)}, bf16[192,512]{1,0:T(8,128)(2,1)S(1)}, u32[]{:S(2)}, u32[]{:S(2)}) collective-permute-start(bf16[192,512]{1,0:T(8,128)(2,1)} %collective-permute-done.12.refs_2_), channel_id=1, source_target_pairs={{0,16},{16,0},{1,17},{17,1},{2,18},{18,2},{3,19},{19,3},{4,20},{20... | collective-permute-start | bytes 589832 | tf_op jit(solution)/shard_map/ppermute | solution.py:104
  67.1 30.2 %collective-permute-start.19 = (bf16[192,768]{1,0:T(8,128)(2,1)S(1)}, bf16[192,768]{1,0:T(8,128)(2,1)S(1)}, u32[]{:S(2)}, u32[]{:S(2)}) collective-permute-start(bf16[192,768]{1,0:T(8,128)(2,1)S(1)} %dynamic-slice_bitcast_fusion.refs_0_), channel_id=1, source_target_pairs={{0,4},{2,6},{4,12},{6,14},{12,8},{14,10},{8,0},{10,2},{20,16},{22,... | collective-permute-start | bytes 884744 | tf_op jit(solution)/shard_map/ppermute | solution.py:98
  68.3 30.8 %collective-permute-start.14 = (bf16[192,512]{1,0:T(8,128)(2,1)}, bf16[192,512]{1,0:T(8,128)(2,1)S(1)}, u32[]{:S(2)}, u32[]{:S(2)}) collective-permute-start(bf16[192,512]{1,0:T(8,128)(2,1)} %constant_dynamic-slice_fusion.refs_0_), channel_id=1, source_target_pairs={{0,2},{2,0},{4,6},{6,4},{8,10},{10,8},{12,14},{14,12},{1,3},{3,1},... | collective-permute-start | bytes 589832 | tf_op jit(solution)/shard_map/ppermute | solution.py:101
  69.2 40.1 %collective-permute-start.16 = (bf16[192,512]{1,0:T(8,128)(2,1)}, bf16[192,512]{1,0:T(8,128)(2,1)S(1)}, u32[]{:S(2)}, u32[]{:S(2)}) collective-permute-start(bf16[192,512]{1,0:T(8,128)(2,1)} %collective-permute-done.13.refs_3_), channel_id=1, source_target_pairs={{0,16},{16,0},{1,17},{17,1},{2,18},{18,2},{3,19},{19,3},{4,20},{20... | collective-permute-start | bytes 589832 | tf_op jit(solution)/shard_map/ppermute | solution.py:104
  70.5 1.0 copy-start.4
  71.5 59.4 %copy-start.5 = (bf16[1536,256]{1,0:T(8,128)(2,1)S(1)}, bf16[1536,256]{1,0:T(8,128)(2,1)}, u32[]{:S(2)}) copy-start(bf16[1536,256]{1,0:T(8,128)(2,1)} %weight_ref.2) | copy-start | bytes 2359300
  74.6 3.0 %collective-permute-start.21 = (bf16[192,128]{1,0:T(8,128)(2,1)S(1)}, bf16[192,128]{1,0:T(8,128)(2,1)S(1)}, u32[]{:S(2)}, u32[]{:S(2)}) collective-permute-start(bf16[192,128]{1,0:T(8,128)(2,1)S(1)} %get-tuple-element.23), channel_id=1, source_target_pairs={{0,4},{2,6},{4,0},{6,2},{8,12},{10,14},{12,8},{14,10},{1,5},{3,7},... | collective-permute-start | bytes 147464 | tf_op jit(solution)/shard_map/ppermute | solution.py:404
  77.6 4.2 %collective-permute-start.22 = (bf16[192,128]{1,0:T(8,128)(2,1)S(1)}, bf16[192,128]{1,0:T(8,128)(2,1)S(1)}, u32[]{:S(2)}, u32[]{:S(2)}) collective-permute-start(bf16[192,128]{1,0:T(8,128)(2,1)S(1)} %get-tuple-element.23), channel_id=1, source_target_pairs={{0,8},{2,10},{4,12},{6,14},{8,0},{10,2},{12,4},{14,6},{1,9},{3,11}... | collective-permute-start | bytes 147464 | tf_op jit(solution)/shard_map/ppermute | solution.py:404
  81.8 4.7 %collective-permute-start.23 = (bf16[192,128]{1,0:T(8,128)(2,1)S(1)}, bf16[192,128]{1,0:T(8,128)(2,1)S(1)}, u32[]{:S(2)}, u32[]{:S(2)}) collective-permute-start(bf16[192,128]{1,0:T(8,128)(2,1)S(1)} %get-tuple-element.23), channel_id=1, source_target_pairs={{0,12},{2,14},{4,8},{6,10},{8,4},{10,6},{12,0},{14,2},{1,13},{3,15... | collective-permute-start | bytes 147464 | tf_op jit(solution)/shard_map/ppermute | solution.py:404
  86.5 2.9 %collective-permute-start.24 = (bf16[192,128]{1,0:T(8,128)(2,1)S(1)}, bf16[192,128]{1,0:T(8,128)(2,1)S(1)}, u32[]{:S(2)}, u32[]{:S(2)}) collective-permute-start(bf16[192,128]{1,0:T(8,128)(2,1)S(1)} %get-tuple-element.23), channel_id=1, source_target_pairs={{0,2},{2,0},{4,6},{6,4},{8,10},{10,8},{12,14},{14,12},{1,3},{3,1},... | collective-permute-start | bytes 147464 | tf_op jit(solution)/shard_map/ppermute | solution.py:405
  89.5 2.9 %collective-permute-start.25 = (bf16[192,128]{1,0:T(8,128)(2,1)S(1)}, bf16[192,128]{1,0:T(8,128)(2,1)S(1)}, u32[]{:S(2)}, u32[]{:S(2)}) collective-permute-start(bf16[192,128]{1,0:T(8,128)(2,1)S(1)} %collective-permute-done.21), channel_id=1, source_target_pairs={{0,2},{2,0},{4,6},{6,4},{8,10},{10,8},{12,14},{14,12},{1,3},{3,1},... | collective-permute-start | bytes 147464 | tf_op jit(solution)/shard_map/ppermute | solution.py:405
  92.4 3.7 %collective-permute-start.26 = (bf16[192,128]{1,0:T(8,128)(2,1)S(1)}, bf16[192,128]{1,0:T(8,128)(2,1)S(1)}, u32[]{:S(2)}, u32[]{:S(2)}) collective-permute-start(bf16[192,128]{1,0:T(8,128)(2,1)S(1)} %collective-permute-done.22), channel_id=1, source_target_pairs={{0,2},{2,0},{4,6},{6,4},{8,10},{10,8},{12,14},{14,12},{1,3},{3,1},... | collective-permute-start | bytes 147464 | tf_op jit(solution)/shard_map/ppermute | solution.py:405
  96.1 2.9 %collective-permute-start.27 = (bf16[192,128]{1,0:T(8,128)(2,1)S(1)}, bf16[192,128]{1,0:T(8,128)(2,1)S(1)}, u32[]{:S(2)}, u32[]{:S(2)}) collective-permute-start(bf16[192,128]{1,0:T(8,128)(2,1)S(1)} %collective-permute-done.23), channel_id=1, source_target_pairs={{0,2},{2,0},{4,6},{6,4},{8,10},{10,8},{12,14},{14,12},{1,3},{3,1},... | collective-permute-start | bytes 147464 | tf_op jit(solution)/shard_map/ppermute | solution.py:405
  97.2 13.3 %collective-permute-start.18 = (bf16[192,512]{1,0:T(8,128)(2,1)}, bf16[192,512]{1,0:T(8,128)(2,1)S(1)}, u32[]{:S(2)}, u32[]{:S(2)}) collective-permute-start(bf16[192,512]{1,0:T(8,128)(2,1)} %collective-permute-done.13.refs_3_), channel_id=1, source_target_pairs={{0,4},{2,6},{4,12},{6,14},{12,8},{14,10},{8,0},{10,2},{20,16},{22,... | collective-permute-start | bytes 589832 | tf_op jit(solution)/shard_map/ppermute | solution.py:98
  97.2 13.2 %collective-permute-start.29 = (bf16[192,768]{1,0:T(8,128)(2,1)S(1)}, bf16[192,768]{1,0:T(8,128)(2,1)S(1)}, u32[]{:S(2)}, u32[]{:S(2)}) collective-permute-start(bf16[192,768]{1,0:T(8,128)(2,1)S(1)} %collective-permute-done.19.refs_2_), channel_id=1, source_target_pairs={{0,2},{2,0},{4,6},{6,4},{8,10},{10,8},{12,14},{14,12},{1,3},{3,1},... | collective-permute-start | bytes 884744 | tf_op jit(solution)/shard_map/ppermute | solution.py:101
  99.0 12.9 %collective-permute-start.32 = (bf16[192,768]{1,0:T(8,128)(2,1)S(1)}, bf16[192,768]{1,0:T(8,128)(2,1)S(1)}, u32[]{:S(2)}, u32[]{:S(2)}) collective-permute-start(bf16[192,768]{1,0:T(8,128)(2,1)S(1)} %collective-permute-done.19.refs_2_), channel_id=1, source_target_pairs={{0,4},{2,6},{4,12},{6,14},{12,8},{14,10},{8,0},{10,2},{20,16},{22,... | collective-permute-start | bytes 884744 | tf_op jit(solution)/shard_map/ppermute | solution.py:98
  99.1 19.3 %collective-permute-start.28 = (bf16[8,192,128]{2,1,0:T(8,128)(2,1)S(1)}, bf16[8,192,128]{2,1,0:T(8,128)(2,1)S(1)}, u32[]{:S(2)}, u32[]{:S(2)}) collective-permute-start(bf16[8,192,128]{2,1,0:T(8,128)(2,1)S(1)} %bitcast_dynamic-update-slice_fusion.own_ref), channel_id=1, source_target_pairs={{0,1},{1,0},{2,3},{3,2},{4,5},{5,4},{6,7},{7,6},{8,9},{9,8},{10,11... | collective-permute-start | bytes 1179656 | tf_op jit(solution)/shard_map/ppermute | solution.py:409
  109.3 9.1 %collective-permute-start.20 = (bf16[192,768]{1,0:T(8,128)(2,1)S(1)}, bf16[192,768]{1,0:T(8,128)(2,1)S(1)}, u32[]{:S(2)}, u32[]{:S(2)}) collective-permute-start(bf16[192,768]{1,0:T(8,128)(2,1)S(1)} %dynamic-slice_bitcast_fusion.refs_0_), channel_id=1, source_target_pairs={{0,2},{2,0},{4,6},{6,4},{8,10},{10,8},{12,14},{14,12},{1,3},{3,1},... | collective-permute-start | bytes 884744 | tf_op jit(solution)/shard_map/ppermute | solution.py:101
  110.4 9.4 %collective-permute-start.30 = (bf16[192,768]{1,0:T(8,128)(2,1)S(1)}, bf16[192,768]{1,0:T(8,128)(2,1)S(1)}, u32[]{:S(2)}, u32[]{:S(2)}) collective-permute-start(bf16[192,768]{1,0:T(8,128)(2,1)S(1)} %collective-permute-done.19.refs_2_), channel_id=1, source_target_pairs={{0,16},{16,0},{1,17},{17,1},{2,18},{18,2},{3,19},{19,3},{4,20},{20... | collective-permute-start | bytes 884744 | tf_op jit(solution)/shard_map/ppermute | solution.py:104
  110.5 11.9 %collective-permute-start.31 = (bf16[192,768]{1,0:T(8,128)(2,1)S(1)}, bf16[192,768]{1,0:T(8,128)(2,1)S(1)}, u32[]{:S(2)}, u32[]{:S(2)}) collective-permute-start(bf16[192,768]{1,0:T(8,128)(2,1)S(1)} %collective-permute-done.29.refs_3_), channel_id=1, source_target_pairs={{0,16},{16,0},{1,17},{17,1},{2,18},{18,2},{3,19},{19,3},{4,20},{20... | collective-permute-start | bytes 884744 | tf_op jit(solution)/shard_map/ppermute | solution.py:104
  111.9 12.8 %collective-permute-start.33 = (bf16[192,768]{1,0:T(8,128)(2,1)S(1)}, bf16[192,768]{1,0:T(8,128)(2,1)S(1)}, u32[]{:S(2)}, u32[]{:S(2)}) collective-permute-start(bf16[192,768]{1,0:T(8,128)(2,1)S(1)} %collective-permute-done.32.refs_6_), channel_id=1, source_target_pairs={{0,2},{2,0},{4,6},{6,4},{8,10},{10,8},{12,14},{14,12},{1,3},{3,1},... | collective-permute-start | bytes 884744 | tf_op jit(solution)/shard_map/ppermute | solution.py:101
  127.9 3.0 %collective-permute-start.34 = (bf16[8,128,192]{2,1,0:T(8,128)(2,1)S(1)}, bf16[8,128,192]{2,1,0:T(8,128)(2,1)S(1)}, u32[]{:S(2)}, u32[]{:S(2)}) collective-permute-start(bf16[8,128,192]{2,1,0:T(8,128)(2,1)S(1)} %output.1.part_ref), channel_id=1, source_target_pairs={{0,1},{1,0},{2,3},{3,2},{4,5},{5,4},{6,7},{7,6},{8,9},{9,8},{10,11... | collective-permute-start | bytes 1179656 | tf_op jit(solution)/shard_map/ppermute | solution.py:445
  132.2 9.3 %collective-permute-start.35 = (bf16[8,256]{1,0:T(8,128)(2,1)S(1)}, bf16[8,256]{1,0:T(8,128)(2,1)S(1)}, u32[]{:S(2)}, u32[]{:S(2)}) collective-permute-start(bf16[8,256]{1,0:T(8,128)(2,1)S(1)} %get-tuple-element.25.own_ref), channel_id=1, source_target_pairs={{0,0},{1,8},{2,2},{3,10},{4,4},{5,12},{6,6},{7,14},{8,1},{9,9},{10... | collective-permute-start | bytes 12296 | tf_op jit(solution)/shard_map/ppermute | solution.py:468
  137.0 4.9 %collective-permute-start.36 = (bf16[8,256]{1,0:T(8,128)(2,1)S(1)}, bf16[8,256]{1,0:T(8,128)(2,1)S(1)}, u32[]{:S(2)}, u32[]{:S(2)}) collective-permute-start(bf16[8,256]{1,0:T(8,128)(2,1)S(1)} %get-tuple-element.25.own_ref), channel_id=1, source_target_pairs={{0,2},{1,10},{2,0},{3,8},{4,6},{5,14},{6,4},{7,12},{8,3},{9,11},{1... | collective-permute-start | bytes 12296 | tf_op jit(solution)/shard_map/ppermute | solution.py:468
  137.1 4.9 %collective-permute-start.37 = (bf16[8,256]{1,0:T(8,128)(2,1)S(1)}, bf16[8,256]{1,0:T(8,128)(2,1)S(1)}, u32[]{:S(2)}, u32[]{:S(2)}) collective-permute-start(bf16[8,256]{1,0:T(8,128)(2,1)S(1)} %get-tuple-element.25.own_ref), channel_id=1, source_target_pairs={{0,4},{1,12},{2,6},{3,14},{4,0},{5,8},{6,2},{7,10},{8,5},{9,13},{1... | collective-permute-start | bytes 12296 | tf_op jit(solution)/shard_map/ppermute | solution.py:468
  139.0 5.7 %collective-permute-start.38 = (bf16[8,256]{1,0:T(8,128)(2,1)S(1)}, bf16[8,256]{1,0:T(8,128)(2,1)S(1)}, u32[]{:S(2)}, u32[]{:S(2)}) collective-permute-start(bf16[8,256]{1,0:T(8,128)(2,1)S(1)} %get-tuple-element.25.own_ref), channel_id=1, source_target_pairs={{0,6},{1,14},{2,4},{3,12},{4,2},{5,10},{6,0},{7,8},{8,7},{9,15},{1... | collective-permute-start | bytes 12296 | tf_op jit(solution)/shard_map/ppermute | solution.py:468
  (1 other events, 0.7 us)

commit v4 on v3

--- a/solution.py
+++ b/solution.py
@@ -43,17 +43,6 @@
 
 def hspec(n):
     return [pl.BlockSpec(memory_space=pltpu.HBM)] * n
-
-
-def fetch(sources, held, sems):
-    copies = [pltpu.make_async_copy(ref, held.at[i], sems.at[i]) for i, ref in enumerate(sources)]
-    for c in copies:
-        c.start()
-    return copies
-
-
-def slots(pieces, rows, columns):
-    return [pltpu.VMEM((pieces, rows, columns), BF16), pltpu.SemaphoreType.DMA((pieces,))]
 
 
 RING = (0, 1, 3, 2)
@@ -112,50 +101,42 @@
     return lax.optimization_barrier((values, done))[0]
 
 
-def conv_kernel(own_ref, other_ref, halo_ref, gaincol_ref, gainrow_ref, pool_ref, poolhalo_ref, weight_hbm,
-                out_ref, act, slabs, weights, sems):
-    taps, width, channels = weights.shape
+def act_kernel(own_ref, other_ref, halo_ref, gaincol_ref, gainrow_ref, pool_ref, poolhalo_ref, out_ref, act):
+    channels, positions = act.shape
+    half = own_ref.shape[0]
+    col = lax.axis_index("col")
+    step = 64
+    halves = ((own_ref, col), (other_ref, 1 - col))
+    squares = jnp.zeros((8, positions), F32)
+    for ref, _ in halves:
+        for j in range(half // step):
+            x = ref[j * step:(j + 1) * step, :].astype(F32)
+            x = x * x
+            for i in range(step // 8):
+                squares = squares + x[i * 8:(i + 1) * 8]
+    scale = lax.rsqrt(jnp.sum(squares, axis=0, keepdims=True) / channels + EPS)
+    for ref, index in halves:
+        for j in range(half // step):
+            at = pl.multiple_of(index * half + j * step, step)
+            x = ref[j * step:(j + 1) * step, :].astype(F32) * scale
+            act[pl.ds(at, step), :] = gelu(x * gaincol_ref[pl.ds(at, step), :]).astype(BF16)
+    h = halo_ref[...].astype(F32)
+    h = h * lax.rsqrt(jnp.sum(h * h, axis=1, keepdims=True) / channels + EPS) * gainrow_ref[...]
+    h = gelu(h).astype(BF16)
+    out_ref[...] = (dot_nt(pool_ref[...], act[...]) + dot_nn(poolhalo_ref[...], h)).astype(BF16)
+
+
+def conv_kernel(windows_ref, own_ref, pool_ref, weight_hbm, out_ref, weights, sems):
+    taps = weights.shape[0]
     copies = [pltpu.make_async_copy(weight_hbm.at[t], weights.at[t], sems.at[t]) for t in range(taps)]
     for c in copies:
         c.start()
-    col = lax.axis_index("col")
-    half, positions = own_ref.shape
-    tokens = out_ref.shape[1]
-    step, group = 16, 4
-    halves = ((own_ref, col), (other_ref, 1 - col))
-    squares = jnp.zeros((8, positions), F32)
-    for ref, _ in halves:
-
-        def add(j, squares, ref=ref):
-            for i in range(group):
-                x = ref[pl.ds(pl.multiple_of((j * group + i) * step, step), step), :].astype(F32)
-                x = x * x
-                squares = squares + (x[:8] + x[8:])
-            return squares
-
-        squares = lax.fori_loop(0, half // (step * group), add, squares)
-    scale = lax.rsqrt(jnp.sum(squares, axis=0, keepdims=True) / channels + EPS)
-    for ref, index in halves:
-
-        def activate(j, carry, ref=ref, index=index):
-            for i in range(group):
-                at = pl.multiple_of((j * group + i) * step, step)
-                x = ref[pl.ds(at, step), :].astype(F32) * scale
-                at = pl.multiple_of(index * half + at, step)
-                act[pl.ds(at, step), :] = gelu(x * gaincol_ref[pl.ds(at, step), :]).astype(BF16)
-            return carry
-
-        lax.fori_loop(0, half // (step * group), activate, 0)
-    h = halo_ref[...].astype(F32)
-    h = h * lax.rsqrt(jnp.sum(h * h, axis=1, keepdims=True) / channels + EPS) * gainrow_ref[...]
-    h = gelu(h)
-    edges = lax.dot_general(h.astype(BF16), poolhalo_ref[...], (((0,), (0,)), ((), ())), preferred_element_type=F32)
-    slabs[...] = (dot_nn(act[...], pool_ref[...]) + edges).astype(BF16)
+    tokens = out_ref.shape[0]
     middle = (taps // 2) * tokens
-    total = dot_nn(own_ref[...], pool_ref[:, middle:middle + tokens])
+    total = dot_nt(pool_ref[middle:middle + tokens], own_ref[...])
     for t in range(taps):
         copies[t].wait()
-        total = total + dot_nn(weights[t], slabs[:, t * tokens:(t + 1) * tokens])
+        total = total + dot_nt(windows_ref[t * tokens:(t + 1) * tokens], weights[t])
     out_ref[...] = total.astype(BF16)
 
 
@@ -164,43 +145,34 @@
 
 
 def embed_kernel(pieces, pooled_ref, *refs):
-    blocks, (out_ref, held, sems) = refs[:pieces], refs[pieces:]
-    half, lanes = pooled_ref.shape[0], held.shape[2]
-    copies = fetch([ref.at[:, pl.ds(0, lanes)] for ref in blocks], held, sems)
-    for i, owner in enumerate(block_owners()):
-        copies[i].wait()
-        out_ref[owner] = dot_nn(held[i][:, :half], pooled_ref[...]).astype(BF16)
+    blocks, out_ref = refs[:pieces], refs[pieces]
+    half = pooled_ref.shape[1]
+    for ref, owner in zip(blocks, block_owners()):
+        out_ref[owner] = dot_nt(pooled_ref[...], ref[:, :half]).astype(BF16)
 
 
 def keyvalue_kernel(pieces, half, part_ref, other_ref, gain_ref, *refs):
-    blocks, (kv_ref, normed_ref, embedded_ref, held, sems) = refs[:pieces], refs[pieces:]
-    lanes = held.shape[2]
-    start = blocks[0].shape[1] - lanes
-    copies = fetch([ref.at[:, pl.ds(start, lanes)] for ref in blocks], held, sems)
-    count, width, _ = part_ref.shape
-    squares = 0.0
-    for s in range(count):
-        e = (part_ref[s].astype(F32) + other_ref[s].astype(F32)).astype(BF16).astype(F32)
-        squares = squares + jnp.sum(e * e, axis=0, keepdims=True)
+    blocks, (kv_ref, normed_ref, embedded_ref) = refs[:pieces], refs[pieces:]
+    count, _, width = part_ref.shape
+    e = (part_ref[...].astype(F32) + other_ref[...].astype(F32)).astype(BF16)
+    embedded_ref[...] = e
+    e = e.astype(F32)
+    squares = jnp.sum(jnp.sum(e * e, axis=0), axis=1, keepdims=True)
     scale = lax.rsqrt(squares / (count * width) + EPS)
-    for s in range(count):
-        e = (part_ref[s].astype(F32) + other_ref[s].astype(F32)).astype(BF16).astype(F32)
-        embedded_ref[s] = e.T.astype(BF16)
-        normed_ref[s] = ((e * scale).T * gain_ref[s]).astype(BF16)
+    normed_ref[...] = (e * scale[None] * gain_ref[...]).astype(BF16)
     total = 0.0
-    for i, owner in enumerate(block_owners()):
-        copies[i].wait()
-        total = total + dot_nn(normed_ref[owner], held[i][:, half - start:])
-    kv_ref[...] = total.T.astype(BF16)
+    for ref, owner in zip(blocks, block_owners()):
+        total = total + dot_nn(normed_ref[owner], ref[:, half:])
+    kv = total.T.astype(BF16)
+    for i in range(kv_ref.shape[0]):
+        kv_ref[i] = kv
 
 
 def query_kernel(pieces, normed_ref, *refs):
-    blocks, (query_ref, held, sems) = refs[:pieces], refs[pieces:]
-    copies = fetch(blocks, held, sems)
+    blocks, query_ref = refs[:pieces], refs[pieces]
     total = 0.0
-    for i, owner in enumerate(block_owners()):
-        copies[i].wait()
-        total = total + dot_nn(normed_ref[owner], held[i])
+    for ref, owner in zip(blocks, block_owners()):
+        total = total + dot_nn(normed_ref[owner], ref[...])
     query_ref[...] = (total * DK ** (-0.5)).astype(BF16)
 
 
@@ -219,13 +191,11 @@
 
 
 def output_kernel(pieces, attended_ref, *refs):
-    blocks, (out_ref, held, sems) = refs[:pieces], refs[pieces:]
-    copies = fetch(blocks, held, sems)
+    blocks, out_ref = refs[:pieces], refs[pieces]
     heads = attended_ref.shape[0]
     flat = jnp.concatenate([attended_ref[h] for h in range(heads)], axis=1)
-    for i, owner in enumerate(block_owners()):
-        copies[i].wait()
-        out_ref[owner] = dot_nt(flat, held[i]).astype(BF16)
+    for ref, owner in zip(blocks, block_owners()):
+        out_ref[owner] = dot_nt(flat, ref[...]).astype(BF16)
 
 
 def token_kernel(embedded_ref, part_ref, other_ref, weight_ref, token_ref, send_ref, whole):
@@ -263,19 +233,19 @@
 
 def pooling_matrices(positions, taps):
     tokens, reach = positions // POOL, taps // 2
-    main = np.zeros((positions, taps, tokens), np.float32)
-    halo = np.zeros((16, taps, tokens), np.float32)
+    main = np.zeros((taps, tokens, positions), np.float32)
+    halo = np.zeros((taps, tokens, 16), np.float32)
     for t in range(taps):
         for i in range(tokens):
             for j in range(POOL):
                 p = POOL * i + j + t - reach
                 if p < 0:
-                    halo[p + reach, t, i] += 1.0 / POOL
+                    halo[t, i, p + reach] += 1.0 / POOL
                 elif p >= positions:
-                    halo[reach + p - positions, t, i] += 1.0 / POOL
+                    halo[t, i, reach + p - positions] += 1.0 / POOL
                 else:
-                    main[p, t, i] += 1.0 / POOL
-    flat = lambda a: jnp.asarray(a.reshape(a.shape[0], taps * tokens), BF16)
+                    main[t, i, p] += 1.0 / POOL
+    flat = lambda a: jnp.asarray(a.reshape(taps * tokens, -1), BF16)
     return flat(main), flat(halo)
 
 
@@ -315,26 +285,53 @@
     output_own = lax.dynamic_slice_in_dim(output_weight.T, col * heads * DV, heads * DV, 1)
     ring = planned(count, lax.axis_size("grp")) and cols == 2
     e, q, o = (Blocks(x, count) for x in (embed_own, query_own, output_own))
+    pool_main, pool_halo = pooling_matrices(positions, taps)
     if ring:
         e.at["own"] = after(e.at["own"], before, behind)
         e.along("own", "step")
         e.across("own", "own2")
-        e.at["step"] = after(e.at["step"], e.at["own2"])
+    windows = pl.pallas_call(
+        act_kernel,
+        out_shape=shape((taps * tokens, channels), BF16),
+        in_specs=vspec(7),
+        out_specs=pl.BlockSpec(memory_space=VMEM),
+        scratch_shapes=[pltpu.VMEM((channels, positions), BF16)],
+        compiler_params=params(24),
+        cost_estimate=cost(2 * taps * tokens * channels * positions, 4 * channels * positions),
+        name="act",
+    )(
+        signal_t, other_t, halo, conv_gain.reshape(channels, 1), conv_gain.reshape(1, channels), pool_main, pool_halo
+    )
+    if ring:
+        e.at["step"] = after(e.at["step"], e.at["own2"], windows)
         e.along("step", "far")
         e.across("step", "step2")
         e.between("step", "cross")
-        q.at["own"] = after(q.at["own"], e.at["far"])
+    pooled = pl.pallas_call(
+        conv_kernel,
+        out_shape=shape((tokens, half), BF16),
+        in_specs=vspec(3) + hspec(1),
+        out_specs=pl.BlockSpec(memory_space=VMEM),
+        scratch_shapes=[pltpu.VMEM((taps, half, channels), BF16), pltpu.SemaphoreType.DMA((taps,))],
+        compiler_params=params(56),
+        cost_estimate=cost(2 * taps * tokens * channels * half, 2 * taps * channels * half),
+        name="conv",
+    )(windows, signal_t, pool_main, conv_weight.transpose(0, 2, 1))
+    if ring:
+        e.at["far"] = after(e.at["far"], pooled)
+        e.at["step2"] = after(e.at["step2"], pooled)
         e.across("far", "far2")
         e.between("step2", "cross2")
+        q.at["own"] = after(q.at["own"], pooled, e.at["far"])
         q.along("own", "step")
+        q.at["step"] = after(q.at["step"], e.at["far2"], e.at["cross2"])
         q.along("step", "far")
-        q.at["step"] = after(q.at["step"], e.at["far2"])
         q.across("step", "step2")
         q.between("step", "cross")
+        q.at["own"] = after(q.at["own"], q.at["step2"])
         q.along("step2", "far2")
+        q.across("own", "own2")
         q.between("step2", "cross2")
-        q.at["own"] = after(q.at["own"], q.at["step2"])
-        q.across("own", "own2")
         o.at["own"] = after(o.at["own"], q.at["step2"], q.at["far"])
         o.along("own", "step")
         o.across("own", "own2")
@@ -351,69 +348,40 @@
     pieces = len(embed_blocks)
     block = width // pieces
 
-    pool_main, pool_halo = pooling_matrices(positions, taps)
-    pooled = pl.pallas_call(
-        conv_kernel,
-        out_shape=shape((half, tokens), BF16),
-        in_specs=vspec(7) + hspec(1),
-        out_specs=pl.BlockSpec(memory_space=VMEM),
-        scratch_shapes=[
-            pltpu.VMEM((channels, positions), BF16),
-            pltpu.VMEM((channels, taps * tokens), BF16),
-            pltpu.VMEM((taps, half, channels), BF16),
-            pltpu.SemaphoreType.DMA((taps,)),
-        ],
-        compiler_params=params(28),
-        cost_estimate=cost(2 * taps * tokens * channels * (half + positions), 2 * taps * channels * half * 2),
-        name="conv",
-    )(
-        signal_t, other_t, halo, conv_gain.reshape(channels, 1), conv_gain.reshape(1, channels),
-        pool_main, pool_halo, conv_weight.transpose(0, 2, 1),
-    )
-
-    upper = -(-half // 128) * 128
-    lower = half // 128 * 128
     part = pl.pallas_call(
         functools.partial(embed_kernel, pieces),
-        out_shape=shape((pieces, block, tokens), BF16),
-        in_specs=vspec(1) + hspec(pieces),
-        out_specs=pl.BlockSpec(memory_space=VMEM),
-        scratch_shapes=slots(pieces, block, min(upper, half + DV)),
+        out_shape=shape((pieces, tokens, block), BF16),
+        in_specs=vspec(1 + pieces),
+        out_specs=pl.BlockSpec(memory_space=VMEM),
         compiler_params=params(12),
         cost_estimate=cost(2 * tokens * half * width, 2 * half * width),
         name="embed",
     )(pooled, *embed_blocks)
     other_part = lax.ppermute(part, "col", swap)
+    if ring:
+        other_part = after(other_part, q.at["step2"], q.at["far"])
 
     keyvalue, normed, embedded = pl.pallas_call(
         functools.partial(keyvalue_kernel, pieces, half),
         out_shape=(
-            shape((DV, tokens), BF16), shape((pieces, tokens, block), BF16), shape((pieces, tokens, block), BF16)
+            shape((count, DV, tokens), BF16),
+            shape((pieces, tokens, block), BF16),
+            shape((pieces, tokens, block), BF16),
         ),
-        in_specs=vspec(3) + hspec(pieces),
+        in_specs=vspec(3 + pieces),
         out_specs=vspec(3),
-        scratch_shapes=slots(pieces, block, half + DV - lower),
-        compiler_params=params(12),
+        compiler_params=params(16),
         cost_estimate=cost(2 * tokens * width * DV, 2 * width * DV),
         name="keyvalue",
     )(part, other_part, attn_gain.reshape(pieces, 1, block), *embed_blocks)
-
-    if ring:
-        arrived = [keyvalue]
-        for k in range(1, count // 2):
-            arrived.append(lax.ppermute(keyvalue, "seq", [(i, i ^ (2 * k)) for i in range(count)]))
-        arrived += [lax.ppermute(x, "seq", [(i, i ^ 1) for i in range(count)]) for x in arrived]
-        gathered = jnp.stack(arrived)
-    else:
-        gathered = lax.all_gather(keyvalue, "seq", axis=0)
+    gathered = lax.all_to_all(keyvalue, "seq", 0, 0)
     gathered_other = lax.ppermute(gathered, "col", swap)
 
     queries = pl.pallas_call(
         functools.partial(query_kernel, pieces),
         out_shape=shape((tokens, features), BF16),
-        in_specs=vspec(1) + hspec(pieces),
-        out_specs=pl.BlockSpec(memory_space=VMEM),
-        scratch_shapes=slots(pieces, block, features),
+        in_specs=vspec(1 + pieces),
+        out_specs=pl.BlockSpec(memory_space=VMEM),
         compiler_params=params(12),
         cost_estimate=cost(2 * tokens * width * features, 2 * width * features),
         name="query",
@@ -435,9 +403,8 @@
     part_out = pl.pallas_call(
         functools.partial(output_kernel, pieces),
         out_shape=shape((pieces, tokens, block), BF16),
-        in_specs=vspec(1) + hspec(pieces),
-        out_specs=pl.BlockSpec(memory_space=VMEM),
-        scratch_shapes=slots(pieces, block, heads * DV),
+        in_specs=vspec(1 + pieces),
+        out_specs=pl.BlockSpec(memory_space=VMEM),
         compiler_params=params(16),
         cost_estimate=cost(2 * tokens * heads * DV * width, 2 * heads * DV * width),
         name="output",

time: 146 us -> 136 us (0.932)
  starting transfers between devices: 61.3 us -> 47.2 us
  Pallas kernels: 27.3 us -> 20.9 us
  local copies, waits for them, and re-layouts: 14.3 us -> 19.6 us
  waiting for transfers between devices: 40.6 us -> 45.2 us
    ppermute x7 -> x0, waiting for transfers between devices: 17.4 us -> none  [the longest x3 9.91 us: on_device(): lax.ppermute(keyvalue, 'seq', [(i, i ^ 2 * k) for i in range(count)])]
    ppermute x7, waiting for transfers between devices: 6.09 us -> 20.2 us  [along(): self.at[target] = lax.ppermute(self.at[source], ('grp', 'seq'), pairs)]
    ppermute x6, waiting for transfers between devices: 2.49 us -> 13.6 us  [between(): self.at[target] = lax.ppermute(self.at[source], 'grp', [(0, 1), (1, 0)])]
    ppermute x1, starting transfers between devices: 10.2 us -> 1.8 us  [on_device(): gathered_other = lax.ppermute(gathered, 'col', swap)]
    ppermute x7 -> x0, starting transfers between devices: 6.41 us -> none  [the longest x4 4.44 us: on_device(): lax.ppermute(x, 'seq', [(i, i ^ 1) for i in range(count)])]
    unnamed x29 -> x40, local copies, waits for them, and re-layouts: 8.78 us -> 14.7 us
    all_to_all x0 -> x1, starting transfers between devices: none -> 3.58 us  [on_device(): gathered = lax.all_to_all(keyvalue, 'seq', 0, 0)]
    ppermute x7, starting transfers between devices: 4.88 us -> 8.3 us  [along(): self.at[target] = lax.ppermute(self.at[source], ('grp', 'seq'), pairs)]
  transfers between devices with their start and end apart: 39 -> 33, of which waited for: 18 -> 9; matrix products, arithmetic and copies ran while one was open for 4% -> 5% of each run, Pallas kernels for 15% -> 12%
where the time goes in v4:
time: 136 us; the launch traced here: 135 us
  starting transfers between devices  47.2 us (35%)
  waiting for transfers between devices  45.2 us (33%)
  Pallas kernels  20.9 us (15%)
  local copies, waits for them, and re-layouts  19.6 us (14%)
    ppermute x7, waiting for transfers between devices, along(): self.at[target] = lax.ppermute(self.at[source], ('grp', 'seq'), pairs)  20.2 us
    unnamed x40, local copies, waits for them, and re-layouts  14.7 us
    ppermute x6, waiting for transfers between devices, between(): self.at[target] = lax.ppermute(self.at[source], 'grp', [(0, 1), (1, 0)])  13.6 us
    ppermute x4, starting transfers between devices, on_device(): columns.append(lax.ppermute(projected, ('seq', 'col'), pairs))  9.05 us
    pallas_call x1, Pallas kernels, on_device(): pl.pallas_call(conv_kernel, out_shape=shape((tokens, half), BF16), in_spe...  8.42 us
    ppermute x7, starting transfers between devices, along(): self.at[target] = lax.ppermute(self.at[source], ('grp', 'seq'), pairs)  8.3 us
    ppermute x8, starting transfers between devices, across(): lax.ppermute(self.at[source], 'seq', [(i, i ^ 1) for i in range(self.coun...  6.32 us
    ppermute x8, waiting for transfers between devices, across(): lax.ppermute(self.at[source], 'seq', [(i, i ^ 1) for i in range(self.coun...  6.08 us
  transfers between devices with their start and end apart: 33, of which 9 were waited for; matrix products, arithmetic and copies ran while one was open for 5% of the time, Pallas kernels for 12%

profile of v4, /device:TPU:1, one launch (start us, length us, event | category | flops | bytes accessed | tf_op | source)
XLA Modules:
  0.0 134.9 jit_solution(18388516124954071594)
XLA Ops:
  0.8 1.2 fusion.3
  2.1 1.3 collective-permute-start.2
  3.5 5.2 %collective-permute-start.1 = (bf16[2,704]{1,0:T(2,128)(2,1)S(1)}, bf16[2,704]{1,0:T(2,128)(2,1)S(1)}, u32[]{:S(2)}, u32[]{:S(2)}) collective-permute-start(bf16[2,704]{1,0:T(2,128)(2,1)S(1)} %copy.19), channel_id=1, source_target_pairs={{0,2},{2,4},{4,6},{6,8},{8,10},{10,12},{12,14},{1,3},{3,5},{5,7},{... | collective-permute-start | bytes 8456 | tf_op jit(solution)/shard_map/ppermute | solution.py:272
  8.7 1.0 constant_dynamic-slice_fusion.1
  9.7 1.1 pad_maximum_fusion.refs_0_
  10.8 2.4 %collective-permute-start.4 = (bf16[192,896]{1,0:T(8,128)(2,1)S(1)}, bf16[192,896]{1,0:T(8,128)(2,1)S(1)}, u32[]{:S(2)}, u32[]{:S(2)}) collective-permute-start(bf16[192,896]{1,0:T(8,128)(2,1)S(1)} %pad_maximum_fusion.refs_0_), channel_id=1, source_target_pairs={{0,2},{2,0},{4,6},{6,4},{8,10},{10,8},{12,14},{14,12},{1,3},{3,1},... | collective-permute-start | bytes 1032200 | tf_op jit(solution)/shard_map/ppermute | solution.py:90
  13.2 1.3 collective-permute-start.5
  14.5 1.3 collective-permute-start.3
  17.5 1.1 copy-done.2
  18.7 1.1 copy-done.3
  20.7 3.8 %act.1.windows_ref = bf16[640,1408]{1,0:T(8,128)(2,1)S(1)} custom-call(bf16[704,512]{1,0:T(8,128)(2,1)S(1)} %bitcast.7, bf16[704,512]{1,0:T(8,128)(2,1)S(1)} %collective-permute-done.other_ref, bf16[16,1408]{1,0:T(8,128)(2,1)S(1)} %maximum_select_fusion.halo_ref, f32[1408,1]{1,0:T(8,128)S(1)} %reshape.16.gaincol_ref, f32[1,1408]{1,0:T(1,128)S(1)} %reshape.14.gainrow_ref, ...), custom_call_target="tpu_custom_call" | custom-call | flops 922746880 | bytes 2883584 | tf_op jit(solution)/shard_map/act/pallas_call | solution.py:293
  24.4 1.3 copy-done.1
  25.7 1.0 collective-permute-start.6
  26.7 2.3 %collective-permute-start.9 = (bf16[192,896]{1,0:T(8,128)(2,1)S(1)}, bf16[192,896]{1,0:T(8,128)(2,1)S(1)}, u32[]{:S(2)}, u32[]{:S(2)}) collective-permute-start(bf16[192,896]{1,0:T(8,128)(2,1)S(1)} %collective-permute-done.5.refs_2_), channel_id=1, source_target_pairs={{0,4},{2,6},{4,12},{6,14},{12,8},{14,10},{8,0},{10,2},{20,16},{22,... | collective-permute-start | bytes 1032200 | tf_op jit(solution)/shard_map/ppermute | solution.py:87
  29.0 1.2 collective-permute-start.7
  30.2 8.4 %conv.1.pooled_ref = bf16[128,704]{1,0:T(8,128)(2,1)} custom-call(bf16[640,1408]{1,0:T(8,128)(2,1)} %copy-done.1, bf16[704,512]{1,0:T(8,128)(2,1)} %bitcast.6, bf16[640,512]{1,0:T(8,128)(2,1)} %constant.26.clone.pool_ref, bf16[5,704,1408]{2,1,0:T(8,128)(2,1)} %bitcast.8), custom_call_target="tpu_custom_call" | custom-call | flops 1268776960 | bytes 9912320 | tf_op jit(solution)/shard_map/conv/pallas_call | solution.py:310
  39.1 0.9 constant_dynamic-slice_fusion.refs_0_
  40.6 6.9 %collective-permute-done.8.refs_5_ = bf16[192,896]{1,0:T(8,128)(2,1)S(1)} collective-permute-done((bf16[192,896]{1,0:T(8,128)(2,1)S(1)}, bf16[192,896]{1,0:T(8,128)(2,1)S(1)}, u32[]{:S(2)}, u32[]{:S(2)}) %collective-permute-start.8) | collective-permute-done | bytes 344096 | tf_op jit(solution)/shard_map/ppermute | solution.py:93
  48.3 1.0 copy-done.5
  51.1 2.0 %collective-permute-start.11 = (bf16[8,128,192]{2,1,0:T(8,128)(2,1)S(1)}, bf16[8,128,192]{2,1,0:T(8,128)(2,1)}, u32[]{:S(2)}, u32[]{:S(2)}) collective-permute-start(bf16[8,128,192]{2,1,0:T(8,128)(2,1)S(1)} %embed.1.part_ref), channel_id=1, source_target_pairs={{0,1},{1,0},{2,3},{3,2},{4,5},{5,4},{6,7},{7,6},{8,9},{9,8},{10,11... | collective-permute-start | bytes 1179656 | tf_op jit(solution)/shard_map/ppermute | solution.py:360
  53.9 6.1 %collective-permute-done.13.refs_3_ = bf16[192,512]{1,0:T(8,128)(2,1)} collective-permute-done((bf16[192,512]{1,0:T(8,128)(2,1)}, bf16[192,512]{1,0:T(8,128)(2,1)}, u32[]{:S(2)}, u32[]{:S(2)}) %collective-permute-start.13) | collective-permute-done | bytes 196640 | tf_op jit(solution)/shard_map/ppermute | solution.py:90
  60.6 1.0 copy-done.6
  61.5 1.9 %keyvalue.1 = (bf16[8,192,128]{2,1,0:T(8,128)(2,1)S(1)}, bf16[8,128,192]{2,1,0:T(8,128)(2,1)S(1)}, bf16[8,128,192]{2,1,0:T(8,128)(2,1)S(1)}) custom-call(bf16[8,128,192]{2,1,0:T(8,128)(2,1)S(1)} %embed.1.part_ref, bf16[8,128,192]{2,1,0:T(8,128)(2,1)} %collective-permute-done.11.other_ref, f32[8,1,192]{2,1,0:T(1,128)S(1)} %reshape.15.gain_ref, ...), custom_call_target="tpu_custom_call" | custom-call | flops 75497472 | bytes 589824 | tf_op jit(solution)/shard_map/keyvalue/pallas_call | solution.py:364
  65.8 3.6 %all-to-all-start = ((bf16[8,192,128]{2,1,0:T(8,128)(2,1)}), bf16[8,192,128]{2,1,0:T(8,128)(2,1)S(1)}, u32[]{:S(2)}, u32[]{:S(2)}) async-start(bf16[8,192,128]{2,1,0:T(8,128)(2,1)} %copy-done.15), calls=%async_computation | async-start | bytes 786432 | tf_op jit(solution)/shard_map/all_to_all | solution.py:377
  69.4 1.4 %collective-permute-start.19 = (bf16[192,768]{1,0:T(8,128)(2,1)S(1)}, bf16[192,768]{1,0:T(8,128)(2,1)S(1)}, u32[]{:S(2)}, u32[]{:S(2)}) collective-permute-start(bf16[192,768]{1,0:T(8,128)(2,1)S(1)} %dynamic-slice_bitcast_fusion.refs_0_), channel_id=1, source_target_pairs={{0,4},{2,6},{4,12},{6,14},{12,8},{14,10},{8,0},{10,2},{20,16},{22,... | collective-permute-start | bytes 884744 | tf_op jit(solution)/shard_map/ppermute | solution.py:87
  70.8 1.5 %collective-permute-start.16 = (bf16[192,512]{1,0:T(8,128)(2,1)}, bf16[192,512]{1,0:T(8,128)(2,1)S(1)}, u32[]{:S(2)}, u32[]{:S(2)}) collective-permute-start(bf16[192,512]{1,0:T(8,128)(2,1)} %collective-permute-done.12.refs_2_), channel_id=1, source_target_pairs={{0,16},{16,0},{1,17},{17,1},{2,18},{18,2},{3,19},{19,3},{4,20},{20... | collective-permute-start | bytes 589832 | tf_op jit(solution)/shard_map/ppermute | solution.py:93
  72.3 1.2 collective-permute-start.15
  73.5 12.8 %collective-permute-done.19.refs_2_ = bf16[192,768]{1,0:T(8,128)(2,1)S(1)} collective-permute-done((bf16[192,768]{1,0:T(8,128)(2,1)S(1)}, bf16[192,768]{1,0:T(8,128)(2,1)S(1)}, u32[]{:S(2)}, u32[]{:S(2)}) %collective-permute-start.19) | collective-permute-done | bytes 294944 | tf_op jit(solution)/shard_map/ppermute | solution.py:87
  86.3 1.6 %collective-permute-start.22 = (bf16[192,768]{1,0:T(8,128)(2,1)S(1)}, bf16[192,768]{1,0:T(8,128)(2,1)S(1)}, u32[]{:S(2)}, u32[]{:S(2)}) collective-permute-start(bf16[192,768]{1,0:T(8,128)(2,1)S(1)} %collective-permute-done.19.refs_2_), channel_id=1, source_target_pairs={{0,2},{2,0},{4,6},{6,4},{8,10},{10,8},{12,14},{14,12},{1,3},{3,1},... | collective-permute-start | bytes 884744 | tf_op jit(solution)/shard_map/ppermute | solution.py:90
  87.9 2.1 %collective-permute-start.18 = (bf16[192,512]{1,0:T(8,128)(2,1)}, bf16[192,512]{1,0:T(8,128)(2,1)S(1)}, u32[]{:S(2)}, u32[]{:S(2)}) collective-permute-start(bf16[192,512]{1,0:T(8,128)(2,1)} %collective-permute-done.13.refs_3_), channel_id=1, source_target_pairs={{0,4},{2,6},{4,12},{6,14},{12,8},{14,10},{8,0},{10,2},{20,16},{22,... | collective-permute-start | bytes 589832 | tf_op jit(solution)/shard_map/ppermute | solution.py:87
  90.0 1.8 %collective-permute-start.21 = (bf16[8,192,128]{2,1,0:T(8,128)(2,1)S(1)}, bf16[8,192,128]{2,1,0:T(8,128)(2,1)S(1)}, u32[]{:S(2)}, u32[]{:S(2)}) collective-permute-start(bf16[8,192,128]{2,1,0:T(8,128)(2,1)S(1)} %all-to-all-done.own_ref), channel_id=1, source_target_pairs={{0,1},{1,0},{2,3},{3,2},{4,5},{5,4},{6,7},{7,6},{8,9},{9,8},{10,11... | collective-permute-start | bytes 1179656 | tf_op jit(solution)/shard_map/ppermute | solution.py:378
  91.8 1.1 collective-permute-done.17.refs_5_
  92.9 6.7 %collective-permute-done.18.refs_7_ = bf16[192,512]{1,0:T(8,128)(2,1)S(1)} collective-permute-done((bf16[192,512]{1,0:T(8,128)(2,1)}, bf16[192,512]{1,0:T(8,128)(2,1)S(1)}, u32[]{:S(2)}, u32[]{:S(2)}) %collective-permute-start.18) | collective-permute-done | bytes 196640 | tf_op jit(solution)/shard_map/ppermute | solution.py:87
  99.6 1.5 %collective-permute-start.24 = (bf16[192,768]{1,0:T(8,128)(2,1)S(1)}, bf16[192,768]{1,0:T(8,128)(2,1)S(1)}, u32[]{:S(2)}, u32[]{:S(2)}) collective-permute-start(bf16[192,768]{1,0:T(8,128)(2,1)S(1)} %collective-permute-done.22.refs_3_), channel_id=1, source_target_pairs={{0,16},{16,0},{1,17},{17,1},{2,18},{18,2},{3,19},{19,3},{4,20},{20... | collective-permute-start | bytes 884744 | tf_op jit(solution)/shard_map/ppermute | solution.py:93
  102.0 1.0 copy-done.12
  103.0 1.5 %query.1.query_ref = bf16[128,512]{1,0:T(8,128)(2,1)S(1)} custom-call(bf16[8,128,192]{2,1,0:T(8,128)(2,1)S(1)} %copy-done.12, bf16[192,512]{1,0:T(8,128)(2,1)S(1)} %copy-done.8, bf16[192,512]{1,0:T(8,128)(2,1)S(1)} %collective-permute-done.15.refs_1_, bf16[192,512]{1,0:T(8,128)(2,1)} %collective-permute-done.12.refs_2_, ...), custom_call_target="tpu_custom_call" | custom-call | flops 201326592 | bytes 1572864 | tf_op jit(solution)/shard_map/query/pallas_call | solution.py:380
  104.6 1.4 %attend.1.attended_ref = bf16[4,128,192]{2,1,0:T(8,128)(2,1)S(1)} custom-call(bf16[128,512]{1,0:T(8,128)(2,1)S(1)} %query.1.query_ref, bf16[8,192,128]{2,1,0:T(8,128)(2,1)S(1)} %all-to-all-done.own_ref, bf16[8,192,128]{2,1,0:T(8,128)(2,1)S(1)} %collective-permute-done.21.other_ref), custom_call_target="tpu_custom_call" | custom-call | flops 335544320 | bytes 786432 | tf_op jit(solution)/shard_map/attend/pallas_call | solution.py:392
  106.0 5.6 %collective-permute-done.24.refs_5_ = bf16[192,768]{1,0:T(8,128)(2,1)S(1)} collective-permute-done((bf16[192,768]{1,0:T(8,128)(2,1)S(1)}, bf16[192,768]{1,0:T(8,128)(2,1)S(1)}, u32[]{:S(2)}, u32[]{:S(2)}) %collective-permute-start.24) | collective-permute-done | bytes 294944 | tf_op jit(solution)/shard_map/ppermute | solution.py:93
  112.6 3.8 %collective-permute-start.27 = (bf16[8,128,192]{2,1,0:T(8,128)(2,1)S(1)}, bf16[8,128,192]{2,1,0:T(8,128)(2,1)S(1)}, u32[]{:S(2)}, u32[]{:S(2)}) collective-permute-start(bf16[8,128,192]{2,1,0:T(8,128)(2,1)S(1)} %output.1.part_ref), channel_id=1, source_target_pairs={{0,1},{1,0},{2,3},{3,2},{4,5},{5,4},{6,7},{7,6},{8,9},{9,8},{10,11... | collective-permute-start | bytes 1179656 | tf_op jit(solution)/shard_map/ppermute | solution.py:412
  116.3 1.5 %collective-permute-done.27.other_ref = bf16[8,128,192]{2,1,0:T(8,128)(2,1)S(1)} collective-permute-done((bf16[8,128,192]{2,1,0:T(8,128)(2,1)S(1)}, bf16[8,128,192]{2,1,0:T(8,128)(2,1)S(1)}, u32[]{:S(2)}, u32[]{:S(2)}) %collective-permute-start.27) | collective-permute-done | bytes 393248 | tf_op jit(solution)/shard_map/ppermute | solution.py:412
  117.9 1.1 copy-done.9
  119.0 1.0 copy-done.14
  120.1 1.3 tokens.1
  121.3 2.8 %collective-permute-start.28 = (bf16[8,256]{1,0:T(8,128)(2,1)S(1)}, bf16[8,256]{1,0:T(8,128)(2,1)S(1)}, u32[]{:S(2)}, u32[]{:S(2)}) collective-permute-start(bf16[8,256]{1,0:T(8,128)(2,1)S(1)} %get-tuple-element.31.own_ref), channel_id=1, source_target_pairs={{0,0},{1,8},{2,2},{3,10},{4,4},{5,12},{6,6},{7,14},{8,1},{9,9},{10... | collective-permute-start | bytes 12296 | tf_op jit(solution)/shard_map/ppermute | solution.py:435
  124.2 1.2 collective-permute-start.29
  125.3 3.0 %collective-permute-start.30 = (bf16[8,256]{1,0:T(8,128)(2,1)S(1)}, bf16[8,256]{1,0:T(8,128)(2,1)S(1)}, u32[]{:S(2)}, u32[]{:S(2)}) collective-permute-start(bf16[8,256]{1,0:T(8,128)(2,1)S(1)} %get-tuple-element.31.own_ref), channel_id=1, source_target_pairs={{0,4},{1,12},{2,6},{3,14},{4,0},{5,8},{6,2},{7,10},{8,5},{9,13},{1... | collective-permute-start | bytes 12296 | tf_op jit(solution)/shard_map/ppermute | solution.py:435
  128.4 2.0 %collective-permute-start.31 = (bf16[8,256]{1,0:T(8,128)(2,1)S(1)}, bf16[8,256]{1,0:T(8,128)(2,1)S(1)}, u32[]{:S(2)}, u32[]{:S(2)}) collective-permute-start(bf16[8,256]{1,0:T(8,128)(2,1)S(1)} %get-tuple-element.31.own_ref), channel_id=1, source_target_pairs={{0,6},{1,14},{2,4},{3,12},{4,2},{5,10},{6,0},{7,8},{8,7},{9,15},{1... | collective-permute-start | bytes 12296 | tf_op jit(solution)/shard_map/ppermute | solution.py:435
  130.4 3.7 %collective-permute-done.31.refs_3_ = bf16[8,256]{1,0:T(8,128)(2,1)S(1)} collective-permute-done((bf16[8,256]{1,0:T(8,128)(2,1)S(1)}, bf16[8,256]{1,0:T(8,128)(2,1)S(1)}, u32[]{:S(2)}, u32[]{:S(2)}) %collective-permute-start.31) | collective-permute-done | bytes 4128 | tf_op jit(solution)/shard_map/ppermute | solution.py:435
  (77 shorter events, 13.1 us)
Async XLA Ops:
  0.6 68.7 %copy-start = (bf16[1536,192]{0,1:T(8,128)(2,1)S(1)}, bf16[1536,192]{0,1:T(8,128)(2,1)}, u32[]{:S(2)}) copy-start(bf16[1536,192]{0,1:T(8,128)(2,1)} %param.19) | copy-start | bytes 1769476
  0.6 16.9 %collective-permute-start = (bf16[704,512]{1,0:T(8,128)(2,1)}, bf16[704,512]{1,0:T(8,128)(2,1)S(1)}, u32[]{:S(2)}, u32[]{:S(2)}) collective-permute-start(bf16[704,512]{1,0:T(8,128)(2,1)} %bitcast.5), channel_id=1, source_target_pairs={{0,1},{1,0},{2,3},{3,2},{4,5},{5,4},{6,7},{7,6},{8,9},{9,8},{10,11... | collective-permute-start | bytes 2162696 | tf_op jit(solution)/shard_map/ppermute | solution.py:274
  2.1 8.7 %collective-permute-start.2 = (bf16[2,704]{1,0:T(2,128)(2,1)S(1)}, bf16[2,704]{1,0:T(2,128)(2,1)S(1)}, u32[]{:S(2)}, u32[]{:S(2)}) collective-permute-start(bf16[2,704]{1,0:T(2,128)(2,1)S(1)} %copy.20), channel_id=1, source_target_pairs={{2,0},{4,2},{6,4},{8,6},{10,8},{12,10},{14,12},{3,1},{5,3},{7,5},{... | collective-permute-start | bytes 8456 | tf_op jit(solution)/shard_map/ppermute | solution.py:273
  3.5 7.3 %collective-permute-start.1 = (bf16[2,704]{1,0:T(2,128)(2,1)S(1)}, bf16[2,704]{1,0:T(2,128)(2,1)S(1)}, u32[]{:S(2)}, u32[]{:S(2)}) collective-permute-start(bf16[2,704]{1,0:T(2,128)(2,1)S(1)} %copy.19), channel_id=1, source_target_pairs={{0,2},{2,4},{4,6},{6,8},{8,10},{10,12},{12,14},{1,3},{3,5},{5,7},{... | collective-permute-start | bytes 8456 | tf_op jit(solution)/shard_map/ppermute | solution.py:272
  10.8 14.9 %collective-permute-start.4 = (bf16[192,896]{1,0:T(8,128)(2,1)S(1)}, bf16[192,896]{1,0:T(8,128)(2,1)S(1)}, u32[]{:S(2)}, u32[]{:S(2)}) collective-permute-start(bf16[192,896]{1,0:T(8,128)(2,1)S(1)} %pad_maximum_fusion.refs_0_), channel_id=1, source_target_pairs={{0,2},{2,0},{4,6},{6,4},{8,10},{10,8},{12,14},{14,12},{1,3},{3,1},... | collective-permute-start | bytes 1032200 | tf_op jit(solution)/shard_map/ppermute | solution.py:90
  13.2 12.5 %collective-permute-start.5 = (bf16[192,896]{1,0:T(8,128)(2,1)S(1)}, bf16[192,896]{1,0:T(8,128)(2,1)S(1)}, u32[]{:S(2)}, u32[]{:S(2)}) collective-permute-start(bf16[192,896]{1,0:T(8,128)(2,1)S(1)} %pad_maximum_fusion.refs_0_), channel_id=1, source_target_pairs={{0,4},{2,6},{4,12},{6,14},{12,8},{14,10},{8,0},{10,2},{20,16},{22,... | collective-permute-start | bytes 1032200 | tf_op jit(solution)/shard_map/ppermute | solution.py:87
  14.5 2.9 %collective-permute-start.3 = (bf16[16,704]{1,0:T(8,128)(2,1)S(1)}, bf16[16,704]{1,0:T(8,128)(2,1)S(1)}, u32[]{:S(2)}, u32[]{:S(2)}) collective-permute-start(bf16[16,704]{1,0:T(8,128)(2,1)S(1)} %fusion.2), channel_id=1, source_target_pairs={{0,1},{1,0},{2,3},{3,2},{4,5},{5,4},{6,7},{7,6},{8,9},{9,8},{10,11... | collective-permute-start | bytes 67592 | tf_op jit(solution)/shard_map/ppermute | solution.py:276
  17.5 1.1 copy-start.2
  18.7 1.1 copy-start.3
  19.7 0.9 copy-start.16
  20.7 33.1 %copy-start.18 = (f32[1536]{0:T(1024)S(1)}, f32[1536]{0:T(1024)}, u32[]{:S(2)}) copy-start(f32[1536]{0:T(1024)} %param.16) | copy-start | bytes 18436
  24.4 1.3 copy-start.1
  25.7 13.0 %collective-permute-start.6 = (bf16[192,896]{1,0:T(8,128)(2,1)S(1)}, bf16[192,896]{1,0:T(8,128)(2,1)S(1)}, u32[]{:S(2)}, u32[]{:S(2)}) collective-permute-start(bf16[192,896]{1,0:T(8,128)(2,1)S(1)} %collective-permute-done.5.refs_2_), channel_id=1, source_target_pairs={{0,2},{2,0},{4,6},{6,4},{8,10},{10,8},{12,14},{14,12},{1,3},{3,1},... | collective-permute-start | bytes 1032200 | tf_op jit(solution)/shard_map/ppermute | solution.py:90
  26.7 12.3 %collective-permute-start.9 = (bf16[192,896]{1,0:T(8,128)(2,1)S(1)}, bf16[192,896]{1,0:T(8,128)(2,1)S(1)}, u32[]{:S(2)}, u32[]{:S(2)}) collective-permute-start(bf16[192,896]{1,0:T(8,128)(2,1)S(1)} %collective-permute-done.5.refs_2_), channel_id=1, source_target_pairs={{0,4},{2,6},{4,12},{6,14},{12,8},{14,10},{8,0},{10,2},{20,16},{22,... | collective-permute-start | bytes 1032200 | tf_op jit(solution)/shard_map/ppermute | solution.py:87
  29.0 11.6 %collective-permute-start.7 = (bf16[192,896]{1,0:T(8,128)(2,1)S(1)}, bf16[192,896]{1,0:T(8,128)(2,1)S(1)}, u32[]{:S(2)}, u32[]{:S(2)}) collective-permute-start(bf16[192,896]{1,0:T(8,128)(2,1)S(1)} %collective-permute-done.5.refs_2_), channel_id=1, source_target_pairs={{0,16},{16,0},{1,17},{17,1},{2,18},{18,2},{3,19},{19,3},{4,20},{20... | collective-permute-start | bytes 1032200 | tf_op jit(solution)/shard_map/ppermute | solution.py:93
  38.7 8.9 %collective-permute-start.8 = (bf16[192,896]{1,0:T(8,128)(2,1)S(1)}, bf16[192,896]{1,0:T(8,128)(2,1)S(1)}, u32[]{:S(2)}, u32[]{:S(2)}) collective-permute-start(bf16[192,896]{1,0:T(8,128)(2,1)S(1)} %collective-permute-done.6.refs_3_), channel_id=1, source_target_pairs={{0,16},{16,0},{1,17},{17,1},{2,18},{18,2},{3,19},{19,3},{4,20},{20... | collective-permute-start | bytes 1032200 | tf_op jit(solution)/shard_map/ppermute | solution.py:93
  39.0 8.5 %collective-permute-start.10 = (bf16[192,896]{1,0:T(8,128)(2,1)S(1)}, bf16[192,896]{1,0:T(8,128)(2,1)S(1)}, u32[]{:S(2)}, u32[]{:S(2)}) collective-permute-start(bf16[192,896]{1,0:T(8,128)(2,1)S(1)} %collective-permute-done.9.refs_6_), channel_id=1, source_target_pairs={{0,2},{2,0},{4,6},{6,4},{8,10},{10,8},{12,14},{14,12},{1,3},{3,1},... | collective-permute-start | bytes 1032200 | tf_op jit(solution)/shard_map/ppermute | solution.py:90
  40.0 11.1 %copy-start.7 = (bf16[192,512]{1,0:T(8,128)(2,1)}, bf16[192,512]{1,0:T(8,128)(2,1)S(1)}, u32[]{:S(2)}) copy-start(bf16[192,512]{1,0:T(8,128)(2,1)S(1)} %constant_dynamic-slice_fusion.refs_0_) | copy-start | bytes 589828
  40.0 13.1 %collective-permute-start.12 = (bf16[192,512]{1,0:T(8,128)(2,1)S(1)}, bf16[192,512]{1,0:T(8,128)(2,1)}, u32[]{:S(2)}, u32[]{:S(2)}) collective-permute-start(bf16[192,512]{1,0:T(8,128)(2,1)S(1)} %constant_dynamic-slice_fusion.refs_0_), channel_id=1, source_target_pairs={{0,4},{2,6},{4,12},{6,14},{12,8},{14,10},{8,0},{10,2},{20,16},{22,... | collective-permute-start | bytes 589832 | tf_op jit(solution)/shard_map/ppermute | solution.py:87
  48.3 1.0 copy-start.5
  49.3 0.9 copy-start.10
  51.1 9.4 %collective-permute-start.11 = (bf16[8,128,192]{2,1,0:T(8,128)(2,1)S(1)}, bf16[8,128,192]{2,1,0:T(8,128)(2,1)}, u32[]{:S(2)}, u32[]{:S(2)}) collective-permute-start(bf16[8,128,192]{2,1,0:T(8,128)(2,1)S(1)} %embed.1.part_ref), channel_id=1, source_target_pairs={{0,1},{1,0},{2,3},{3,2},{4,5},{5,4},{6,7},{7,6},{8,9},{9,8},{10,11... | collective-permute-start | bytes 1179656 | tf_op jit(solution)/shard_map/ppermute | solution.py:360
  53.1 6.8 %collective-permute-start.13 = (bf16[192,512]{1,0:T(8,128)(2,1)}, bf16[192,512]{1,0:T(8,128)(2,1)}, u32[]{:S(2)}, u32[]{:S(2)}) collective-permute-start(bf16[192,512]{1,0:T(8,128)(2,1)} %collective-permute-done.12.refs_2_), channel_id=1, source_target_pairs={{0,2},{2,0},{4,6},{6,4},{8,10},{10,8},{12,14},{14,12},{1,3},{3,1},... | collective-permute-start | bytes 589832 | tf_op jit(solution)/shard_map/ppermute | solution.py:90
  53.2 7.3 %collective-permute-start.14 = (bf16[192,512]{1,0:T(8,128)(2,1)}, bf16[192,512]{1,0:T(8,128)(2,1)}, u32[]{:S(2)}, u32[]{:S(2)}) collective-permute-start(bf16[192,512]{1,0:T(8,128)(2,1)} %collective-permute-done.12.refs_2_), channel_id=1, source_target_pairs={{0,4},{2,6},{4,12},{6,14},{12,8},{14,10},{8,0},{10,2},{20,16},{22,... | collective-permute-start | bytes 589832 | tf_op jit(solution)/shard_map/ppermute | solution.py:87
  60.6 1.0 copy-start.6
  65.8 68.3 %copy-start.17 = (bf16[128,128]{1,0:T(8,128)(2,1)S(1)}, bf16[128,128]{1,0:T(8,128)(2,1)}, u32[]{:S(2)}) copy-start(bf16[128,128]{1,0:T(8,128)(2,1)} %weight_ref.3) | copy-start | bytes 98308
  65.8 24.2 %all-to-all-start = ((bf16[8,192,128]{2,1,0:T(8,128)(2,1)}), bf16[8,192,128]{2,1,0:T(8,128)(2,1)S(1)}, u32[]{:S(2)}, u32[]{:S(2)}) async-start(bf16[8,192,128]{2,1,0:T(8,128)(2,1)} %copy-done.15), calls=%async_computation | async-start | bytes 786432 | tf_op jit(solution)/shard_map/all_to_all | solution.py:377
  69.4 16.9 %collective-permute-start.19 = (bf16[192,768]{1,0:T(8,128)(2,1)S(1)}, bf16[192,768]{1,0:T(8,128)(2,1)S(1)}, u32[]{:S(2)}, u32[]{:S(2)}) collective-permute-start(bf16[192,768]{1,0:T(8,128)(2,1)S(1)} %dynamic-slice_bitcast_fusion.refs_0_), channel_id=1, source_target_pairs={{0,4},{2,6},{4,12},{6,14},{12,8},{14,10},{8,0},{10,2},{20,16},{22,... | collective-permute-start | bytes 884744 | tf_op jit(solution)/shard_map/ppermute | solution.py:87
  70.8 17.0 %collective-permute-start.16 = (bf16[192,512]{1,0:T(8,128)(2,1)}, bf16[192,512]{1,0:T(8,128)(2,1)S(1)}, u32[]{:S(2)}, u32[]{:S(2)}) collective-permute-start(bf16[192,512]{1,0:T(8,128)(2,1)} %collective-permute-done.12.refs_2_), channel_id=1, source_target_pairs={{0,16},{16,0},{1,17},{17,1},{2,18},{18,2},{3,19},{19,3},{4,20},{20... | collective-permute-start | bytes 589832 | tf_op jit(solution)/shard_map/ppermute | solution.py:93
  72.3 17.7 %collective-permute-start.15 = (bf16[192,512]{1,0:T(8,128)(2,1)}, bf16[192,512]{1,0:T(8,128)(2,1)S(1)}, u32[]{:S(2)}, u32[]{:S(2)}) collective-permute-start(bf16[192,512]{1,0:T(8,128)(2,1)} %copy-done.7), channel_id=1, source_target_pairs={{0,2},{2,0},{4,6},{6,4},{8,10},{10,8},{12,14},{14,12},{1,3},{3,1},... | collective-permute-start | bytes 589832 | tf_op jit(solution)/shard_map/ppermute | solution.py:90
  86.3 13.3 %collective-permute-start.22 = (bf16[192,768]{1,0:T(8,128)(2,1)S(1)}, bf16[192,768]{1,0:T(8,128)(2,1)S(1)}, u32[]{:S(2)}, u32[]{:S(2)}) collective-permute-start(bf16[192,768]{1,0:T(8,128)(2,1)S(1)} %collective-permute-done.19.refs_2_), channel_id=1, source_target_pairs={{0,2},{2,0},{4,6},{6,4},{8,10},{10,8},{12,14},{14,12},{1,3},{3,1},... | collective-permute-start | bytes 884744 | tf_op jit(solution)/shard_map/ppermute | solution.py:90
  87.8 13.2 %collective-permute-start.25 = (bf16[192,768]{1,0:T(8,128)(2,1)S(1)}, bf16[192,768]{1,0:T(8,128)(2,1)S(1)}, u32[]{:S(2)}, u32[]{:S(2)}) collective-permute-start(bf16[192,768]{1,0:T(8,128)(2,1)S(1)} %collective-permute-done.19.refs_2_), channel_id=1, source_target_pairs={{0,4},{2,6},{4,12},{6,14},{12,8},{14,10},{8,0},{10,2},{20,16},{22,... | collective-permute-start | bytes 884744 | tf_op jit(solution)/shard_map/ppermute | solution.py:87
  87.8 5.0 %collective-permute-start.17 = (bf16[192,512]{1,0:T(8,128)(2,1)}, bf16[192,512]{1,0:T(8,128)(2,1)S(1)}, u32[]{:S(2)}, u32[]{:S(2)}) collective-permute-start(bf16[192,512]{1,0:T(8,128)(2,1)} %collective-permute-done.13.refs_3_), channel_id=1, source_target_pairs={{0,16},{16,0},{1,17},{17,1},{2,18},{18,2},{3,19},{19,3},{4,20},{20... | collective-permute-start | bytes 589832 | tf_op jit(solution)/shard_map/ppermute | solution.py:93
  87.9 11.7 %collective-permute-start.18 = (bf16[192,512]{1,0:T(8,128)(2,1)}, bf16[192,512]{1,0:T(8,128)(2,1)S(1)}, u32[]{:S(2)}, u32[]{:S(2)}) collective-permute-start(bf16[192,512]{1,0:T(8,128)(2,1)} %collective-permute-done.13.refs_3_), channel_id=1, source_target_pairs={{0,4},{2,6},{4,12},{6,14},{12,8},{14,10},{8,0},{10,2},{20,16},{22,... | collective-permute-start | bytes 589832 | tf_op jit(solution)/shard_map/ppermute | solution.py:87
  90.0 14.6 %collective-permute-start.21 = (bf16[8,192,128]{2,1,0:T(8,128)(2,1)S(1)}, bf16[8,192,128]{2,1,0:T(8,128)(2,1)S(1)}, u32[]{:S(2)}, u32[]{:S(2)}) collective-permute-start(bf16[8,192,128]{2,1,0:T(8,128)(2,1)S(1)} %all-to-all-done.own_ref), channel_id=1, source_target_pairs={{0,1},{1,0},{2,3},{3,2},{4,5},{5,4},{6,7},{7,6},{8,9},{9,8},{10,11... | collective-permute-start | bytes 1179656 | tf_op jit(solution)/shard_map/ppermute | solution.py:378
  92.9 11.7 %collective-permute-start.20 = (bf16[192,768]{1,0:T(8,128)(2,1)S(1)}, bf16[192,768]{1,0:T(8,128)(2,1)S(1)}, u32[]{:S(2)}, u32[]{:S(2)}) collective-permute-start(bf16[192,768]{1,0:T(8,128)(2,1)S(1)} %dynamic-slice_bitcast_fusion.refs_0_), channel_id=1, source_target_pairs={{0,2},{2,0},{4,6},{6,4},{8,10},{10,8},{12,14},{14,12},{1,3},{3,1},... | collective-permute-start | bytes 884744 | tf_op jit(solution)/shard_map/ppermute | solution.py:90
  99.6 6.4 %collective-permute-start.23 = (bf16[192,768]{1,0:T(8,128)(2,1)S(1)}, bf16[192,768]{1,0:T(8,128)(2,1)S(1)}, u32[]{:S(2)}, u32[]{:S(2)}) collective-permute-start(bf16[192,768]{1,0:T(8,128)(2,1)S(1)} %collective-permute-done.19.refs_2_), channel_id=1, source_target_pairs={{0,16},{16,0},{1,17},{17,1},{2,18},{18,2},{3,19},{19,3},{4,20},{20... | collective-permute-start | bytes 884744 | tf_op jit(solution)/shard_map/ppermute | solution.py:93
  99.6 12.0 %collective-permute-start.24 = (bf16[192,768]{1,0:T(8,128)(2,1)S(1)}, bf16[192,768]{1,0:T(8,128)(2,1)S(1)}, u32[]{:S(2)}, u32[]{:S(2)}) collective-permute-start(bf16[192,768]{1,0:T(8,128)(2,1)S(1)} %collective-permute-done.22.refs_3_), channel_id=1, source_target_pairs={{0,16},{16,0},{1,17},{17,1},{2,18},{18,2},{3,19},{19,3},{4,20},{20... | collective-permute-start | bytes 884744 | tf_op jit(solution)/shard_map/ppermute | solution.py:93
  101.1 10.6 %collective-permute-start.26 = (bf16[192,768]{1,0:T(8,128)(2,1)S(1)}, bf16[192,768]{1,0:T(8,128)(2,1)S(1)}, u32[]{:S(2)}, u32[]{:S(2)}) collective-permute-start(bf16[192,768]{1,0:T(8,128)(2,1)S(1)} %collective-permute-done.25.refs_6_), channel_id=1, source_target_pairs={{0,2},{2,0},{4,6},{6,4},{8,10},{10,8},{12,14},{14,12},{1,3},{3,1},... | collective-permute-start | bytes 884744 | tf_op jit(solution)/shard_map/ppermute | solution.py:90
  101.1 0.9 copy-start.8
  102.0 1.0 copy-start.12
  112.6 5.3 %collective-permute-start.27 = (bf16[8,128,192]{2,1,0:T(8,128)(2,1)S(1)}, bf16[8,128,192]{2,1,0:T(8,128)(2,1)S(1)}, u32[]{:S(2)}, u32[]{:S(2)}) collective-permute-start(bf16[8,128,192]{2,1,0:T(8,128)(2,1)S(1)} %output.1.part_ref), channel_id=1, source_target_pairs={{0,1},{1,0},{2,3},{3,2},{4,5},{5,4},{6,7},{7,6},{8,9},{9,8},{10,11... | collective-permute-start | bytes 1179656 | tf_op jit(solution)/shard_map/ppermute | solution.py:412
  117.9 1.1 copy-start.9
  119.0 1.0 copy-start.14
  121.3 9.1 %collective-permute-start.28 = (bf16[8,256]{1,0:T(8,128)(2,1)S(1)}, bf16[8,256]{1,0:T(8,128)(2,1)S(1)}, u32[]{:S(2)}, u32[]{:S(2)}) collective-permute-start(bf16[8,256]{1,0:T(8,128)(2,1)S(1)} %get-tuple-element.31.own_ref), channel_id=1, source_target_pairs={{0,0},{1,8},{2,2},{3,10},{4,4},{5,12},{6,6},{7,14},{8,1},{9,9},{10... | collective-permute-start | bytes 12296 | tf_op jit(solution)/shard_map/ppermute | solution.py:435
  124.2 6.2 %collective-permute-start.29 = (bf16[8,256]{1,0:T(8,128)(2,1)S(1)}, bf16[8,256]{1,0:T(8,128)(2,1)S(1)}, u32[]{:S(2)}, u32[]{:S(2)}) collective-permute-start(bf16[8,256]{1,0:T(8,128)(2,1)S(1)} %get-tuple-element.31.own_ref), channel_id=1, source_target_pairs={{0,2},{1,10},{2,0},{3,8},{4,6},{5,14},{6,4},{7,12},{8,3},{9,11},{1... | collective-permute-start | bytes 12296 | tf_op jit(solution)/shard_map/ppermute | solution.py:435
  125.3 5.1 %collective-permute-start.30 = (bf16[8,256]{1,0:T(8,128)(2,1)S(1)}, bf16[8,256]{1,0:T(8,128)(2,1)S(1)}, u32[]{:S(2)}, u32[]{:S(2)}) collective-permute-start(bf16[8,256]{1,0:T(8,128)(2,1)S(1)} %get-tuple-element.31.own_ref), channel_id=1, source_target_pairs={{0,4},{1,12},{2,6},{3,14},{4,0},{5,8},{6,2},{7,10},{8,5},{9,13},{1... | collective-permute-start | bytes 12296 | tf_op jit(solution)/shard_map/ppermute | solution.py:435
  128.4 5.7 %collective-permute-start.31 = (bf16[8,256]{1,0:T(8,128)(2,1)S(1)}, bf16[8,256]{1,0:T(8,128)(2,1)S(1)}, u32[]{:S(2)}, u32[]{:S(2)}) collective-permute-start(bf16[8,256]{1,0:T(8,128)(2,1)S(1)} %get-tuple-element.31.own_ref), channel_id=1, source_target_pairs={{0,6},{1,14},{2,4},{3,12},{4,2},{5,10},{6,0},{7,8},{8,7},{9,15},{1... | collective-permute-start | bytes 12296 | tf_op jit(solution)/shard_map/ppermute | solution.py:435
  (4 other events, 3.1 us)

commit v5 on v4

--- a/solution.py
+++ b/solution.py
@@ -3,7 +3,6 @@
 
 import jax
 import jax.numpy as jnp
-import numpy as np
 from jax import lax
 from jax.experimental import pallas as pl
 from jax.experimental.pallas import tpu as pltpu
@@ -101,10 +100,22 @@
     return lax.optimization_barrier((values, done))[0]
 
 
-def act_kernel(own_ref, other_ref, halo_ref, gaincol_ref, gainrow_ref, pool_ref, poolhalo_ref, out_ref, act):
+def window_means(first_row, rows, tokens, taps, positions, columns):
+    r = lax.broadcasted_iota(jnp.int32, (rows, columns), 0) + first_row
+    k = lax.broadcasted_iota(jnp.int32, (rows, columns), 1)
+    reach = taps // 2
+    if columns != positions:
+        k = jnp.where(k < 2 * reach, jnp.where(k < reach, k - reach, k - reach + positions), -positions)
+    tap = r // tokens
+    gap = k - (POOL * (r - tap * tokens) + tap - reach)
+    return jnp.where((gap >= 0) & (gap < POOL), 1.0 / POOL, 0.0).astype(BF16)
+
+
+def act_kernel(taps, own_ref, other_ref, halo_ref, gain_ref, out_ref, act, gaincol):
     channels, positions = act.shape
     half = own_ref.shape[0]
     col = lax.axis_index("col")
+    gaincol[...] = jnp.broadcast_to(gain_ref[...], (8, channels)).T
     step = 64
     halves = ((own_ref, col), (other_ref, 1 - col))
     squares = jnp.zeros((8, positions), F32)
@@ -119,23 +130,29 @@
         for j in range(half // step):
             at = pl.multiple_of(index * half + j * step, step)
             x = ref[j * step:(j + 1) * step, :].astype(F32) * scale
-            act[pl.ds(at, step), :] = gelu(x * gaincol_ref[pl.ds(at, step), :]).astype(BF16)
+            act[pl.ds(at, step), :] = gelu(x * gaincol[pl.ds(at, step), :1]).astype(BF16)
     h = halo_ref[...].astype(F32)
-    h = h * lax.rsqrt(jnp.sum(h * h, axis=1, keepdims=True) / channels + EPS) * gainrow_ref[...]
+    h = h * lax.rsqrt(jnp.sum(h * h, axis=1, keepdims=True) / channels + EPS) * gain_ref[...]
     h = gelu(h).astype(BF16)
-    out_ref[...] = (dot_nt(pool_ref[...], act[...]) + dot_nn(poolhalo_ref[...], h)).astype(BF16)
-
-
-def conv_kernel(windows_ref, own_ref, pool_ref, weight_hbm, out_ref, weights, sems):
+    rows = out_ref.shape[0]
+    shape = (0, rows, rows // taps, taps, positions)
+    out_ref[...] = (
+        dot_nt(window_means(*shape, positions), act[...]) + dot_nn(window_means(*shape, h.shape[0]), h)
+    ).astype(BF16)
+
+
+def conv_kernel(windows_ref, own_ref, weight_hbm, out_ref, weights, sems):
     taps = weights.shape[0]
     copies = [pltpu.make_async_copy(weight_hbm.at[t], weights.at[t], sems.at[t]) for t in range(taps)]
-    for c in copies:
+    ahead = 2
+    for c in copies[:ahead]:
         c.start()
-    tokens = out_ref.shape[0]
-    middle = (taps // 2) * tokens
-    total = dot_nt(pool_ref[middle:middle + tokens], own_ref[...])
+    tokens, positions = out_ref.shape[0], own_ref.shape[1]
+    total = dot_nt(window_means((taps // 2) * tokens, tokens, tokens, taps, positions, positions), own_ref[...])
     for t in range(taps):
         copies[t].wait()
+        if t + ahead < taps:
+            copies[t + ahead].start()
         total = total + dot_nt(windows_ref[t * tokens:(t + 1) * tokens], weights[t])
     out_ref[...] = total.astype(BF16)
 
@@ -190,12 +207,12 @@
         out_ref[h] = (dot_nt(weights.astype(BF16), values[...]) / total).astype(BF16)
 
 
-def output_kernel(pieces, attended_ref, *refs):
-    blocks, out_ref = refs[:pieces], refs[pieces]
+def output_kernel(attended_ref, weight_ref, out_ref):
     heads = attended_ref.shape[0]
     flat = jnp.concatenate([attended_ref[h] for h in range(heads)], axis=1)
-    for ref, owner in zip(blocks, block_owners()):
-        out_ref[owner] = dot_nt(flat, ref[...]).astype(BF16)
+    count, _, block = out_ref.shape
+    for s in range(count):
+        out_ref[s] = dot_nt(flat, weight_ref[s * block:(s + 1) * block]).astype(BF16)
 
 
 def token_kernel(embedded_ref, part_ref, other_ref, weight_ref, token_ref, send_ref, whole):
@@ -214,39 +231,22 @@
     send_ref[...] = projected.astype(BF16)
 
 
-def pair_kernel(own_ref, weight_ref, *refs):
-    arrived, (out_ref, columns_here) = refs[:-2], refs[-2:]
+def pair_kernel(own_ref, all_ref, weight_ref, out_ref, columns_here):
     seq, col = lax.axis_index("seq"), lax.axis_index("col")
     features, each = weight_ref.shape[0], own_ref.shape[0]
     span = columns_here.shape[0] // each
-    for j in range(span):
-        if len(arrived) == 1:
-            rows, at = arrived[0][col * span + j], j
-        else:
-            rows, at = arrived[j][...], j ^ (seq % span)
-        columns_here[pl.ds(pl.multiple_of(at * each, each), each)] = rows.astype(F32)[:, features:]
+    rows = all_ref[...].astype(F32)[:, features:]
+    if rows.shape[0] == columns_here.shape[0]:
+        for j in range(span):
+            at = pl.multiple_of((j ^ (seq % span)) * each, each)
+            columns_here[pl.ds(at, each)] = rows[j * each:(j + 1) * each]
+    else:
+        half = columns_here.shape[0]
+        columns_here[...] = jnp.where(col == 0, rows[:half], rows[half:])
     rows_here = own_ref[...].astype(F32)[:, :features]
     hidden = gelu(rows_here[:, None, :] + columns_here[...][None, :, :])
     r, c, f = hidden.shape
     out_ref[...] = dot_nn(hidden.reshape(r * c, f).astype(BF16), weight_ref[...]).reshape(r, c, f).astype(BF16)
-
-
-def pooling_matrices(positions, taps):
-    tokens, reach = positions // POOL, taps // 2
-    main = np.zeros((taps, tokens, positions), np.float32)
-    halo = np.zeros((taps, tokens, 16), np.float32)
-    for t in range(taps):
-        for i in range(tokens):
-            for j in range(POOL):
-                p = POOL * i + j + t - reach
-                if p < 0:
-                    halo[t, i, p + reach] += 1.0 / POOL
-                elif p >= positions:
-                    halo[t, i, reach + p - positions] += 1.0 / POOL
-                else:
-                    main[t, i, p] += 1.0 / POOL
-    flat = lambda a: jnp.asarray(a.reshape(taps * tokens, -1), BF16)
-    return flat(main), flat(halo)
 
 
 def cost(flops, size):
@@ -284,24 +284,22 @@
     query_own = lax.dynamic_slice_in_dim(query_weight, col * features, features, 1)
     output_own = lax.dynamic_slice_in_dim(output_weight.T, col * heads * DV, heads * DV, 1)
     ring = planned(count, lax.axis_size("grp")) and cols == 2
-    e, q, o = (Blocks(x, count) for x in (embed_own, query_own, output_own))
-    pool_main, pool_halo = pooling_matrices(positions, taps)
+    e, q = (Blocks(x, count) for x in (embed_own, query_own))
+    output_all = lax.all_gather(output_own, "seq", axis=0, tiled=True)
     if ring:
         e.at["own"] = after(e.at["own"], before, behind)
         e.along("own", "step")
         e.across("own", "own2")
     windows = pl.pallas_call(
-        act_kernel,
+        functools.partial(act_kernel, taps),
         out_shape=shape((taps * tokens, channels), BF16),
-        in_specs=vspec(7),
-        out_specs=pl.BlockSpec(memory_space=VMEM),
-        scratch_shapes=[pltpu.VMEM((channels, positions), BF16)],
-        compiler_params=params(24),
+        in_specs=vspec(4),
+        out_specs=pl.BlockSpec(memory_space=VMEM),
+        scratch_shapes=[pltpu.VMEM((channels, positions), BF16), pltpu.VMEM((channels, 8), F32)],
+        compiler_params=params(20),
         cost_estimate=cost(2 * taps * tokens * channels * positions, 4 * channels * positions),
         name="act",
-    )(
-        signal_t, other_t, halo, conv_gain.reshape(channels, 1), conv_gain.reshape(1, channels), pool_main, pool_halo
-    )
+    )(signal_t, other_t, halo, conv_gain.reshape(1, channels))
     if ring:
         e.at["step"] = after(e.at["step"], e.at["own2"], windows)
         e.along("step", "far")
@@ -310,13 +308,13 @@
     pooled = pl.pallas_call(
         conv_kernel,
         out_shape=shape((tokens, half), BF16),
-        in_specs=vspec(3) + hspec(1),
+        in_specs=vspec(2) + hspec(1),
         out_specs=pl.BlockSpec(memory_space=VMEM),
         scratch_shapes=[pltpu.VMEM((taps, half, channels), BF16), pltpu.SemaphoreType.DMA((taps,))],
-        compiler_params=params(56),
+        compiler_params=params(52),
         cost_estimate=cost(2 * taps * tokens * channels * half, 2 * taps * channels * half),
         name="conv",
-    )(windows, signal_t, pool_main, conv_weight.transpose(0, 2, 1))
+    )(windows, signal_t, conv_weight.transpose(0, 2, 1))
     if ring:
         e.at["far"] = after(e.at["far"], pooled)
         e.at["step2"] = after(e.at["step2"], pooled)
@@ -332,19 +330,9 @@
         q.along("step2", "far2")
         q.across("own", "own2")
         q.between("step2", "cross2")
-        o.at["own"] = after(o.at["own"], q.at["step2"], q.at["far"])
-        o.along("own", "step")
-        o.across("own", "own2")
-        o.along("step", "far")
-        o.across("step", "step2")
-        o.between("step", "cross")
-        o.across("far", "far2")
-        o.between("step2", "cross2")
-        embed_blocks, query_blocks, output_blocks = e.pieces(), q.pieces(), o.pieces()
+        embed_blocks, query_blocks = e.pieces(), q.pieces()
     else:
-        embed_blocks, query_blocks, output_blocks = (
-            [lax.all_gather(x.at["own"], "seq", axis=0, tiled=True)] for x in (e, q, o)
-        )
+        embed_blocks, query_blocks = ([lax.all_gather(x.at["own"], "seq", axis=0, tiled=True)] for x in (e, q))
     pieces = len(embed_blocks)
     block = width // pieces
 
@@ -358,8 +346,6 @@
         name="embed",
     )(pooled, *embed_blocks)
     other_part = lax.ppermute(part, "col", swap)
-    if ring:
-        other_part = after(other_part, q.at["step2"], q.at["far"])
 
     keyvalue, normed, embedded = pl.pallas_call(
         functools.partial(keyvalue_kernel, pieces, half),
@@ -386,8 +372,6 @@
         cost_estimate=cost(2 * tokens * width * features, 2 * width * features),
         name="query",
     )(normed, *query_blocks)
-    if ring:
-        queries = after(queries, o.at["step"], o.at["own2"])
 
     attended = pl.pallas_call(
         attend_kernel,
@@ -395,20 +379,20 @@
         in_specs=vspec(3),
         out_specs=pl.BlockSpec(memory_space=VMEM),
         scratch_shapes=[pltpu.VMEM((DK, count * tokens), BF16), pltpu.VMEM((DV, count * tokens), BF16)],
-        compiler_params=params(40),
+        compiler_params=params(24),
         cost_estimate=cost(2 * tokens * heads * count * tokens * (DK + DV), 4 * count * tokens * DV),
         name="attend",
     )(queries, gathered, gathered_other)
 
     part_out = pl.pallas_call(
-        functools.partial(output_kernel, pieces),
+        output_kernel,
         out_shape=shape((pieces, tokens, block), BF16),
-        in_specs=vspec(1 + pieces),
+        in_specs=vspec(2),
         out_specs=pl.BlockSpec(memory_space=VMEM),
         compiler_params=params(16),
         cost_estimate=cost(2 * tokens * heads * DV * width, 2 * heads * DV * width),
         name="output",
-    )(attended, *output_blocks)
+    )(attended, output_all)
     other_out = lax.ppermute(part_out, "col", swap)
 
     out_width = rowcol_weight.shape[1]
@@ -425,29 +409,27 @@
     )(embedded, part_out, other_out, rowcol_weight)
 
     if ring:
-        columns = []
-        for turn in range(count // 2):
-            pairs = []
-            for source in range(count):
-                need, i = source // (count // 2), source % (count // 2)
-                for c in range(2):
-                    pairs.append((source * 2 + c, ((i ^ turn) + c * (count // 2)) * 2 + need))
-            columns.append(lax.ppermute(projected, ("seq", "col"), pairs))
+        rows_all = projected
+        for bit in (1, 2):
+            rows_all = jnp.concatenate([rows_all, lax.ppermute(rows_all, "seq", [(i, i ^ bit) for i in range(count)])])
+        pairs = [(i * cols + i // 4, (i ^ 4) * cols + i // 4) for i in range(count)]
+        far_rows = lax.ppermute(rows_all, ("seq", "col"), pairs)
+        rows_all = jnp.where(lax.axis_index("seq") // 4 == col, rows_all, far_rows)
     else:
-        columns = [lax.all_gather(projected, "seq", axis=0)]
+        rows_all = lax.all_gather(projected, "seq", axis=0, tiled=True)
 
     span = pair_rows * count // cols
     pair_features = pair_weight.shape[0]
     pair_out = pl.pallas_call(
         pair_kernel,
         out_shape=shape((pair_rows, span, pair_features), BF16),
-        in_specs=vspec(2 + len(columns)),
+        in_specs=vspec(3),
         out_specs=pl.BlockSpec(memory_space=VMEM),
         scratch_shapes=[pltpu.VMEM((span, pair_features), F32)],
         compiler_params=params(16),
         cost_estimate=cost(2 * pair_rows * span * pair_features**2, 2 * pair_rows * span * pair_features),
         name="pair",
-    )(projected, pair_weight, *columns)
+    )(projected, rows_all, pair_weight)
     return out_tokens, pair_out
 
 

time: 136 us -> 142 us (1.044)
  the two profiles are of different devices: /device:TPU:1 before, /device:TPU:0 now
where the time goes in v5:
time: 142 us; the launch traced here: 141 us
  waiting for transfers between devices  59.9 us (42%)
  starting transfers between devices  34.8 us (25%)
  Pallas kernels  18 us (13%)
  between operations  14.4 us (10%)
  local copies, waits for them, and re-layouts  14.2 us (10%)
    ppermute x5, waiting for transfers between devices, along(): self.at[target] = lax.ppermute(self.at[source], ('grp', 'seq'), pairs)  29 us
    ppermute x5, waiting for transfers between devices, across(): lax.ppermute(self.at[source], 'seq', [(i, i ^ 1) for i in range(self.coun...  16.6 us
    unnamed x40, local copies, waits for them, and re-layouts  10.3 us
    ppermute x5, starting transfers between devices, along(): self.at[target] = lax.ppermute(self.at[source], ('grp', 'seq'), pairs)  8.36 us
    pallas_call x1, Pallas kernels, on_device(): pl.pallas_call(conv_kernel, out_shape=shape((tokens, half), BF16), in_spe...  7.59 us
    ppermute x5, starting transfers between devices, across(): lax.ppermute(self.at[source], 'seq', [(i, i ^ 1) for i in range(self.coun...  7.48 us
    ppermute x2, waiting for transfers between devices, on_device(): lax.ppermute(rows_all, 'seq', [(i, i ^ bit) for i in range(count)])  5.47 us
    ppermute x1, starting transfers between devices, on_device(): before = lax.ppermute(signal[positions - reach:], 'seq', up)  5.05 us
  transfers between devices with their start and end apart: 26, of which 18 were waited for; matrix products, arithmetic and copies ran while one was open for 3% of the time, Pallas kernels for 11%

profile of v5, /device:TPU:0, one launch (start us, length us, event | category | flops | bytes accessed | tf_op | source)
XLA Modules:
  0.0 141.5 jit_solution(5259191460311816709)
XLA Ops:
  7.3 1.1 copy-done
  9.6 1.1 fusion.3
  10.9 1.3 collective-permute-start.2
  12.3 5.1 %collective-permute-start.1 = (bf16[2,704]{1,0:T(2,128)(2,1)S(1)}, bf16[2,704]{1,0:T(2,128)(2,1)S(1)}, u32[]{:S(2)}, u32[]{:S(2)}) collective-permute-start(bf16[2,704]{1,0:T(2,128)(2,1)S(1)} %copy.14), channel_id=1, source_target_pairs={{0,2},{2,4},{4,6},{6,8},{8,10},{10,12},{12,14},{1,3},{3,5},{5,7},{... | collective-permute-start | bytes 8456 | tf_op jit(solution)/shard_map/ppermute | solution.py:272
  17.4 1.0 constant_dynamic-slice_fusion.1
  18.7 2.9 %collective-permute-start.4 = (bf16[192,896]{1,0:T(8,128)(2,1)S(1)}, bf16[192,896]{1,0:T(8,128)(2,1)S(1)}, u32[]{:S(2)}, u32[]{:S(2)}) collective-permute-start(bf16[192,896]{1,0:T(8,128)(2,1)S(1)} %pad_maximum_fusion.refs_0_), channel_id=1, source_target_pairs={{0,2},{2,0},{4,6},{6,4},{8,10},{10,8},{12,14},{14,12},{1,3},{3,1},... | collective-permute-start | bytes 1032200 | tf_op jit(solution)/shard_map/ppermute | solution.py:89
  21.6 1.7 %collective-permute-start.5 = (bf16[192,896]{1,0:T(8,128)(2,1)S(1)}, bf16[192,896]{1,0:T(8,128)(2,1)S(1)}, u32[]{:S(2)}, u32[]{:S(2)}) collective-permute-start(bf16[192,896]{1,0:T(8,128)(2,1)S(1)} %pad_maximum_fusion.refs_0_), channel_id=1, source_target_pairs={{0,4},{2,6},{4,12},{6,14},{12,8},{14,10},{8,0},{10,2},{20,16},{22,... | collective-permute-start | bytes 1032200 | tf_op jit(solution)/shard_map/ppermute | solution.py:86
  23.4 1.2 collective-permute-done.3
  24.7 2.8 %act.1.windows_ref = bf16[640,1408]{1,0:T(8,128)(2,1)S(1)} custom-call(bf16[704,512]{1,0:T(8,128)(2,1)S(1)} %bitcast.6, bf16[704,512]{1,0:T(8,128)(2,1)S(1)} %collective-permute-done.other_ref, bf16[16,1408]{1,0:T(8,128)(2,1)S(1)} %maximum_select_fusion.halo_ref, f32[1,1408]{1,0:T(1,128)S(1)} %reshape.10.gain_ref), custom_call_target="tpu_custom_call" | custom-call | flops 922746880 | bytes 2883584 | tf_op jit(solution)/shard_map/act/pallas_call | solution.py:293
  27.5 1.2 copy-done.2
  28.7 4.1 %collective-permute-done.4.refs_1_ = bf16[192,896]{1,0:T(8,128)(2,1)S(1)} collective-permute-done((bf16[192,896]{1,0:T(8,128)(2,1)S(1)}, bf16[192,896]{1,0:T(8,128)(2,1)S(1)}, u32[]{:S(2)}, u32[]{:S(2)}) %collective-permute-start.4) | collective-permute-done | bytes 344096 | tf_op jit(solution)/shard_map/ppermute | solution.py:89
  32.8 8.0 %collective-permute-done.5.refs_2_ = bf16[192,896]{1,0:T(8,128)(2,1)S(1)} collective-permute-done((bf16[192,896]{1,0:T(8,128)(2,1)S(1)}, bf16[192,896]{1,0:T(8,128)(2,1)S(1)}, u32[]{:S(2)}, u32[]{:S(2)}) %collective-permute-start.5) | collective-permute-done | bytes 344096 | tf_op jit(solution)/shard_map/ppermute | solution.py:86
  40.8 1.6 %collective-permute-start.6 = (bf16[192,896]{1,0:T(8,128)(2,1)S(1)}, bf16[192,896]{1,0:T(8,128)(2,1)S(1)}, u32[]{:S(2)}, u32[]{:S(2)}) collective-permute-start(bf16[192,896]{1,0:T(8,128)(2,1)S(1)} %collective-permute-done.5.refs_2_), channel_id=1, source_target_pairs={{0,2},{2,0},{4,6},{6,4},{8,10},{10,8},{12,14},{14,12},{1,3},{3,1},... | collective-permute-start | bytes 1032200 | tf_op jit(solution)/shard_map/ppermute | solution.py:89
  42.6 2.4 %collective-permute-start.7 = (bf16[192,896]{1,0:T(8,128)(2,1)S(1)}, bf16[192,896]{1,0:T(8,128)(2,1)S(1)}, u32[]{:S(2)}, u32[]{:S(2)}) collective-permute-start(bf16[192,896]{1,0:T(8,128)(2,1)S(1)} %collective-permute-done.5.refs_2_), channel_id=1, source_target_pairs={{0,16},{16,0},{1,17},{17,1},{2,18},{18,2},{3,19},{19,3},{4,20},{20... | collective-permute-start | bytes 1032200 | tf_op jit(solution)/shard_map/ppermute | solution.py:92
  45.1 7.6 %conv.1.pooled_ref = bf16[128,704]{1,0:T(8,128)(2,1)S(1)} custom-call(bf16[640,1408]{1,0:T(8,128)(2,1)} %copy-done.2, bf16[704,512]{1,0:T(8,128)(2,1)S(1)} %bitcast.7, bf16[5,704,1408]{2,1,0:T(8,128)(2,1)} %bitcast.8), custom_call_target="tpu_custom_call" | custom-call | flops 1268776960 | bytes 9912320 | tf_op jit(solution)/shard_map/conv/pallas_call | solution.py:308
  52.7 1.5 %collective-permute-start.8 = (bf16[192,896]{1,0:T(8,128)(2,1)S(1)}, bf16[192,896]{1,0:T(8,128)(2,1)S(1)}, u32[]{:S(2)}, u32[]{:S(2)}) collective-permute-start(bf16[192,896]{1,0:T(8,128)(2,1)S(1)} %collective-permute-done.6.refs_3_), channel_id=1, source_target_pairs={{0,16},{16,0},{1,17},{17,1},{2,18},{18,2},{3,19},{19,3},{4,20},{20... | collective-permute-start | bytes 1032200 | tf_op jit(solution)/shard_map/ppermute | solution.py:92
  54.1 6.2 %collective-permute-done.9.refs_6_ = bf16[192,896]{1,0:T(8,128)(2,1)S(1)} collective-permute-done((bf16[192,896]{1,0:T(8,128)(2,1)S(1)}, bf16[192,896]{1,0:T(8,128)(2,1)S(1)}, u32[]{:S(2)}, u32[]{:S(2)}) %collective-permute-start.9) | collective-permute-done | bytes 344096 | tf_op jit(solution)/shard_map/ppermute | solution.py:86
  61.0 8.8 %collective-permute-done.10.refs_7_ = bf16[192,896]{1,0:T(8,128)(2,1)S(1)} collective-permute-done((bf16[192,896]{1,0:T(8,128)(2,1)S(1)}, bf16[192,896]{1,0:T(8,128)(2,1)S(1)}, u32[]{:S(2)}, u32[]{:S(2)}) %collective-permute-start.10) | collective-permute-done | bytes 344096 | tf_op jit(solution)/shard_map/ppermute | solution.py:89
  69.9 0.9 embed.1.part_ref
  71.6 2.0 %collective-permute-done.11.other_ref = bf16[8,128,192]{2,1,0:T(8,128)(2,1)} collective-permute-done((bf16[8,128,192]{2,1,0:T(8,128)(2,1)S(1)}, bf16[8,128,192]{2,1,0:T(8,128)(2,1)}, u32[]{:S(2)}, u32[]{:S(2)}) %collective-permute-start.11) | collective-permute-done | bytes 393248 | tf_op jit(solution)/shard_map/ppermute | solution.py:348
  73.6 1.0 copy-done.5
  74.5 1.0 copy-done.7
  75.5 1.9 %keyvalue.1 = (bf16[8,192,128]{2,1,0:T(8,128)(2,1)S(1)}, bf16[8,128,192]{2,1,0:T(8,128)(2,1)S(1)}, bf16[8,128,192]{2,1,0:T(8,128)(2,1)S(1)}) custom-call(bf16[8,128,192]{2,1,0:T(8,128)(2,1)S(1)} %embed.1.part_ref, bf16[8,128,192]{2,1,0:T(8,128)(2,1)} %collective-permute-done.11.other_ref, f32[8,1,192]{2,1,0:T(1,128)S(1)} %reshape.11.gain_ref, ...), custom_call_target="tpu_custom_call" | custom-call | flops 75497472 | bytes 589824 | tf_op jit(solution)/shard_map/keyvalue/pallas_call | solution.py:350
  77.4 0.8 copy-done.9
  79.7 3.5 %all-to-all-start = ((bf16[8,192,128]{2,1,0:T(8,128)(2,1)}), bf16[8,192,128]{2,1,0:T(8,128)(2,1)S(1)}, u32[]{:S(2)}, u32[]{:S(2)}) async-start(bf16[8,192,128]{2,1,0:T(8,128)(2,1)} %copy-done.13), calls=%async_computation | async-start | bytes 786432 | tf_op jit(solution)/shard_map/all_to_all | solution.py:363
  83.3 0.9 constant_dynamic-slice_fusion.refs_0_
  84.2 2.1 %collective-permute-start.12 = (bf16[192,512]{1,0:T(8,128)(2,1)S(1)}, bf16[192,512]{1,0:T(8,128)(2,1)S(1)}, u32[]{:S(2)}, u32[]{:S(2)}) collective-permute-start(bf16[192,512]{1,0:T(8,128)(2,1)S(1)} %constant_dynamic-slice_fusion.refs_0_), channel_id=1, source_target_pairs={{0,4},{2,6},{4,12},{6,14},{12,8},{14,10},{8,0},{10,2},{20,16},{22,... | collective-permute-start | bytes 589832 | tf_op jit(solution)/shard_map/ppermute | solution.py:86
  86.3 13.3 %collective-permute-done.12.refs_2_ = bf16[192,512]{1,0:T(8,128)(2,1)S(1)} collective-permute-done((bf16[192,512]{1,0:T(8,128)(2,1)S(1)}, bf16[192,512]{1,0:T(8,128)(2,1)S(1)}, u32[]{:S(2)}, u32[]{:S(2)}) %collective-permute-start.12) | collective-permute-done | bytes 196640 | tf_op jit(solution)/shard_map/ppermute | solution.py:86
  99.6 1.5 %collective-permute-start.13 = (bf16[192,512]{1,0:T(8,128)(2,1)S(1)}, bf16[192,512]{1,0:T(8,128)(2,1)S(1)}, u32[]{:S(2)}, u32[]{:S(2)}) collective-permute-start(bf16[192,512]{1,0:T(8,128)(2,1)S(1)} %collective-permute-done.12.refs_2_), channel_id=1, source_target_pairs={{0,2},{2,0},{4,6},{6,4},{8,10},{10,8},{12,14},{14,12},{1,3},{3,1},... | collective-permute-start | bytes 589832 | tf_op jit(solution)/shard_map/ppermute | solution.py:89
  101.1 2.3 %collective-permute-start.17 = (bf16[192,512]{1,0:T(8,128)(2,1)S(1)}, bf16[192,512]{1,0:T(8,128)(2,1)S(1)}, u32[]{:S(2)}, u32[]{:S(2)}) collective-permute-start(bf16[192,512]{1,0:T(8,128)(2,1)S(1)} %collective-permute-done.12.refs_2_), channel_id=1, source_target_pairs={{0,4},{2,6},{4,12},{6,14},{12,8},{14,10},{8,0},{10,2},{20,16},{22,... | collective-permute-start | bytes 589832 | tf_op jit(solution)/shard_map/ppermute | solution.py:86
  103.3 2.2 %collective-permute-done.13.refs_3_ = bf16[192,512]{1,0:T(8,128)(2,1)S(1)} collective-permute-done((bf16[192,512]{1,0:T(8,128)(2,1)S(1)}, bf16[192,512]{1,0:T(8,128)(2,1)S(1)}, u32[]{:S(2)}, u32[]{:S(2)}) %collective-permute-start.13) | collective-permute-done | bytes 196640 | tf_op jit(solution)/shard_map/ppermute | solution.py:89
  105.5 1.5 %collective-permute-start.14 = (bf16[192,512]{1,0:T(8,128)(2,1)S(1)}, bf16[192,512]{1,0:T(8,128)(2,1)S(1)}, u32[]{:S(2)}, u32[]{:S(2)}) collective-permute-start(bf16[192,512]{1,0:T(8,128)(2,1)S(1)} %constant_dynamic-slice_fusion.refs_0_), channel_id=1, source_target_pairs={{0,2},{2,0},{4,6},{6,4},{8,10},{10,8},{12,14},{14,12},{1,3},{3,1},... | collective-permute-start | bytes 589832 | tf_op jit(solution)/shard_map/ppermute | solution.py:89
  107.0 2.1 %collective-permute-start.18 = (bf16[192,512]{1,0:T(8,128)(2,1)S(1)}, bf16[192,512]{1,0:T(8,128)(2,1)S(1)}, u32[]{:S(2)}, u32[]{:S(2)}) collective-permute-start(bf16[192,512]{1,0:T(8,128)(2,1)S(1)} %collective-permute-done.13.refs_3_), channel_id=1, source_target_pairs={{0,4},{2,6},{4,12},{6,14},{12,8},{14,10},{8,0},{10,2},{20,16},{22,... | collective-permute-start | bytes 589832 | tf_op jit(solution)/shard_map/ppermute | solution.py:86
  109.7 1.5 %collective-permute-done.14.refs_1_ = bf16[192,512]{1,0:T(8,128)(2,1)S(1)} collective-permute-done((bf16[192,512]{1,0:T(8,128)(2,1)S(1)}, bf16[192,512]{1,0:T(8,128)(2,1)S(1)}, u32[]{:S(2)}, u32[]{:S(2)}) %collective-permute-start.14) | collective-permute-done | bytes 196640 | tf_op jit(solution)/shard_map/ppermute | solution.py:89
  111.2 1.5 %collective-permute-done.16.refs_5_ = bf16[192,512]{1,0:T(8,128)(2,1)S(1)} collective-permute-done((bf16[192,512]{1,0:T(8,128)(2,1)S(1)}, bf16[192,512]{1,0:T(8,128)(2,1)S(1)}, u32[]{:S(2)}, u32[]{:S(2)}) %collective-permute-start.16) | collective-permute-done | bytes 196640 | tf_op jit(solution)/shard_map/ppermute | solution.py:92
  112.7 0.9 collective-permute-done.18.refs_7_
  113.6 1.0 copy-done.10
  115.1 1.4 attend.1.attended_ref
  116.5 1.7 %copy-done.1 = bf16[1536,768]{1,0:T(8,128)(2,1)S(1)} copy-done((bf16[1536,768]{1,0:T(8,128)(2,1)S(1)}, bf16[1536,768]{1,0:T(8,128)(2,1)}, u32[]{:S(2)}) %copy-start.1) | copy-done | bytes 2359320
  118.2 0.9 output.1.part_ref
  119.2 1.9 %collective-permute-done.20.other_ref = bf16[8,128,192]{2,1,0:T(8,128)(2,1)S(1)} collective-permute-done((bf16[8,128,192]{2,1,0:T(8,128)(2,1)S(1)}, bf16[8,128,192]{2,1,0:T(8,128)(2,1)S(1)}, u32[]{:S(2)}, u32[]{:S(2)}) %collective-permute-start.20) | collective-permute-done | bytes 393248 | tf_op jit(solution)/shard_map/ppermute | solution.py:396
  121.1 1.3 tokens.1
  122.9 3.1 %collective-permute-done.21 = bf16[8,256]{1,0:T(8,128)(2,1)S(1)} collective-permute-done((bf16[8,256]{1,0:T(8,128)(2,1)S(1)}, bf16[8,256]{1,0:T(8,128)(2,1)S(1)}, u32[]{:S(2)}, u32[]{:S(2)}) %collective-permute-start.21) | collective-permute-done | bytes 4128 | tf_op jit(solution)/shard_map/ppermute | solution.py:414
  126.0 1.3 collective-permute-start.22
  127.3 2.4 %collective-permute-done.22 = bf16[16,256]{1,0:T(8,128)(2,1)S(1)} collective-permute-done((bf16[16,256]{1,0:T(8,128)(2,1)S(1)}, bf16[16,256]{1,0:T(8,128)(2,1)S(1)}, u32[]{:S(2)}, u32[]{:S(2)}) %collective-permute-start.22) | collective-permute-done | bytes 8224 | tf_op jit(solution)/shard_map/ppermute | solution.py:414
  129.6 2.7 %collective-permute-start.23 = (bf16[32,256]{1,0:T(8,128)(2,1)S(1)}, bf16[32,256]{1,0:T(8,128)(2,1)S(1)}, u32[]{:S(2)}, u32[]{:S(2)}) collective-permute-start(bf16[32,256]{1,0:T(8,128)(2,1)S(1)} %constant_dynamic-update-slice_fusion), channel_id=1, source_target_pairs={{0,8},{2,10},{4,12},{6,14},{9,1},{11,3},{13,5},{15,7},{16,24},{18,... | collective-permute-start | bytes 49160 | tf_op jit(solution)/shard_map/ppermute | solution.py:416
  132.4 1.4 collective-permute-done.23
  133.8 0.8 pair.1
  (66 shorter events, 7.0 us)
Async XLA Ops:
  7.2 1.2 copy-start
  7.2 17.5 %copy-start.3 = (bf16[512,704]{0,1:T(8,128)(2,1)S(1)}, bf16[512,704]{0,1:T(8,128)(2,1)}, u32[]{:S(2)}) copy-start(bf16[512,704]{0,1:T(8,128)(2,1)} %param.10) | copy-start | bytes 2162692
  7.2 11.2 %copy-start.15 = (bf16[704,192]{0,1:T(8,128)(2,1)S(1)}, bf16[704,192]{0,1:T(8,128)(2,1)}, u32[]{:S(2)}) copy-start(bf16[704,192]{0,1:T(8,128)(2,1)} %param.13) | copy-start | bytes 811012
  7.2 16.2 %copy-start.16 = (f32[1408]{0:T(1024)S(1)}, f32[1408]{0:T(1024)}, u32[]{:S(2)}) copy-start(f32[1408]{0:T(1024)} %param.12) | copy-start | bytes 16900
  7.2 109.3 %all-gather.2.cloned.1.call-start = ((), (), s32[]{:S(2)}) async-start(), calls=%async_computation.1 | async-start | bytes 2654208 | tf_op jit(solution)/shard_map/all_gather | solution.py:288
  9.1 15.6 %collective-permute-start = (bf16[704,512]{1,0:T(8,128)(2,1)}, bf16[704,512]{1,0:T(8,128)(2,1)S(1)}, u32[]{:S(2)}, u32[]{:S(2)}) collective-permute-start(bf16[704,512]{1,0:T(8,128)(2,1)} %bitcast.5), channel_id=1, source_target_pairs={{0,1},{1,0},{2,3},{3,2},{4,5},{5,4},{6,7},{7,6},{8,9},{9,8},{10,11... | collective-permute-start | bytes 2162696 | tf_op jit(solution)/shard_map/ppermute | solution.py:274
  10.9 7.7 %collective-permute-start.2 = (bf16[2,704]{1,0:T(2,128)(2,1)S(1)}, bf16[2,704]{1,0:T(2,128)(2,1)S(1)}, u32[]{:S(2)}, u32[]{:S(2)}) collective-permute-start(bf16[2,704]{1,0:T(2,128)(2,1)S(1)} %copy.15), channel_id=1, source_target_pairs={{2,0},{4,2},{6,4},{8,6},{10,8},{12,10},{14,12},{3,1},{5,3},{7,5},{... | collective-permute-start | bytes 8456 | tf_op jit(solution)/shard_map/ppermute | solution.py:273
  12.3 6.4 %collective-permute-start.1 = (bf16[2,704]{1,0:T(2,128)(2,1)S(1)}, bf16[2,704]{1,0:T(2,128)(2,1)S(1)}, u32[]{:S(2)}, u32[]{:S(2)}) collective-permute-start(bf16[2,704]{1,0:T(2,128)(2,1)S(1)} %copy.14), channel_id=1, source_target_pairs={{0,2},{2,4},{4,6},{6,8},{8,10},{10,12},{12,14},{1,3},{3,5},{5,7},{... | collective-permute-start | bytes 8456 | tf_op jit(solution)/shard_map/ppermute | solution.py:272
  18.7 14.1 %collective-permute-start.4 = (bf16[192,896]{1,0:T(8,128)(2,1)S(1)}, bf16[192,896]{1,0:T(8,128)(2,1)S(1)}, u32[]{:S(2)}, u32[]{:S(2)}) collective-permute-start(bf16[192,896]{1,0:T(8,128)(2,1)S(1)} %pad_maximum_fusion.refs_0_), channel_id=1, source_target_pairs={{0,2},{2,0},{4,6},{6,4},{8,10},{10,8},{12,14},{14,12},{1,3},{3,1},... | collective-permute-start | bytes 1032200 | tf_op jit(solution)/shard_map/ppermute | solution.py:89
  21.6 19.2 %collective-permute-start.5 = (bf16[192,896]{1,0:T(8,128)(2,1)S(1)}, bf16[192,896]{1,0:T(8,128)(2,1)S(1)}, u32[]{:S(2)}, u32[]{:S(2)}) collective-permute-start(bf16[192,896]{1,0:T(8,128)(2,1)S(1)} %pad_maximum_fusion.refs_0_), channel_id=1, source_target_pairs={{0,4},{2,6},{4,12},{6,14},{12,8},{14,10},{8,0},{10,2},{20,16},{22,... | collective-permute-start | bytes 1032200 | tf_op jit(solution)/shard_map/ppermute | solution.py:86
  23.3 1.3 collective-permute-start.3
  27.5 1.2 copy-start.2
  40.8 11.9 %collective-permute-start.6 = (bf16[192,896]{1,0:T(8,128)(2,1)S(1)}, bf16[192,896]{1,0:T(8,128)(2,1)S(1)}, u32[]{:S(2)}, u32[]{:S(2)}) collective-permute-start(bf16[192,896]{1,0:T(8,128)(2,1)S(1)} %collective-permute-done.5.refs_2_), channel_id=1, source_target_pairs={{0,2},{2,0},{4,6},{6,4},{8,10},{10,8},{12,14},{14,12},{1,3},{3,1},... | collective-permute-start | bytes 1032200 | tf_op jit(solution)/shard_map/ppermute | solution.py:89
  42.4 17.9 %collective-permute-start.9 = (bf16[192,896]{1,0:T(8,128)(2,1)S(1)}, bf16[192,896]{1,0:T(8,128)(2,1)S(1)}, u32[]{:S(2)}, u32[]{:S(2)}) collective-permute-start(bf16[192,896]{1,0:T(8,128)(2,1)S(1)} %collective-permute-done.5.refs_2_), channel_id=1, source_target_pairs={{0,4},{2,6},{4,12},{6,14},{12,8},{14,10},{8,0},{10,2},{20,16},{22,... | collective-permute-start | bytes 1032200 | tf_op jit(solution)/shard_map/ppermute | solution.py:86
  42.6 17.7 %collective-permute-start.7 = (bf16[192,896]{1,0:T(8,128)(2,1)S(1)}, bf16[192,896]{1,0:T(8,128)(2,1)S(1)}, u32[]{:S(2)}, u32[]{:S(2)}) collective-permute-start(bf16[192,896]{1,0:T(8,128)(2,1)S(1)} %collective-permute-done.5.refs_2_), channel_id=1, source_target_pairs={{0,16},{16,0},{1,17},{17,1},{2,18},{18,2},{3,19},{19,3},{4,20},{20... | collective-permute-start | bytes 1032200 | tf_op jit(solution)/shard_map/ppermute | solution.py:92
  52.6 18.9 %copy-start.17 = (f32[1536]{0:T(1024)S(1)}, f32[1536]{0:T(1024)}, u32[]{:S(2)}) copy-start(f32[1536]{0:T(1024)} %param.14) | copy-start | bytes 18436
  52.7 8.3 %collective-permute-start.8 = (bf16[192,896]{1,0:T(8,128)(2,1)S(1)}, bf16[192,896]{1,0:T(8,128)(2,1)S(1)}, u32[]{:S(2)}, u32[]{:S(2)}) collective-permute-start(bf16[192,896]{1,0:T(8,128)(2,1)S(1)} %collective-permute-done.6.refs_3_), channel_id=1, source_target_pairs={{0,16},{16,0},{1,17},{17,1},{2,18},{18,2},{3,19},{19,3},{4,20},{20... | collective-permute-start | bytes 1032200 | tf_op jit(solution)/shard_map/ppermute | solution.py:92
  60.3 9.5 %collective-permute-start.10 = (bf16[192,896]{1,0:T(8,128)(2,1)S(1)}, bf16[192,896]{1,0:T(8,128)(2,1)S(1)}, u32[]{:S(2)}, u32[]{:S(2)}) collective-permute-start(bf16[192,896]{1,0:T(8,128)(2,1)S(1)} %collective-permute-done.9.refs_6_), channel_id=1, source_target_pairs={{0,2},{2,0},{4,6},{6,4},{8,10},{10,8},{12,14},{14,12},{1,3},{3,1},... | collective-permute-start | bytes 1032200 | tf_op jit(solution)/shard_map/ppermute | solution.py:89
  69.9 0.9 copy-start.6
  70.8 0.7 copy-start.4
  71.5 2.0 %collective-permute-start.11 = (bf16[8,128,192]{2,1,0:T(8,128)(2,1)S(1)}, bf16[8,128,192]{2,1,0:T(8,128)(2,1)}, u32[]{:S(2)}, u32[]{:S(2)}) collective-permute-start(bf16[8,128,192]{2,1,0:T(8,128)(2,1)S(1)} %embed.1.part_ref), channel_id=1, source_target_pairs={{0,1},{1,0},{2,3},{3,2},{4,5},{5,4},{6,7},{7,6},{8,9},{9,8},{10,11... | collective-permute-start | bytes 1179656 | tf_op jit(solution)/shard_map/ppermute | solution.py:348
  73.6 1.0 copy-start.5
  74.5 1.0 copy-start.7
  77.4 0.8 copy-start.9
  78.2 0.8 copy-start.11
  79.0 0.7 copy-start.13
  79.7 21.3 %all-to-all-start = ((bf16[8,192,128]{2,1,0:T(8,128)(2,1)}), bf16[8,192,128]{2,1,0:T(8,128)(2,1)S(1)}, u32[]{:S(2)}, u32[]{:S(2)}) async-start(bf16[8,192,128]{2,1,0:T(8,128)(2,1)} %copy-done.13), calls=%async_computation | async-start | bytes 786432 | tf_op jit(solution)/shard_map/all_to_all | solution.py:363
  84.2 15.4 %collective-permute-start.12 = (bf16[192,512]{1,0:T(8,128)(2,1)S(1)}, bf16[192,512]{1,0:T(8,128)(2,1)S(1)}, u32[]{:S(2)}, u32[]{:S(2)}) collective-permute-start(bf16[192,512]{1,0:T(8,128)(2,1)S(1)} %constant_dynamic-slice_fusion.refs_0_), channel_id=1, source_target_pairs={{0,4},{2,6},{4,12},{6,14},{12,8},{14,10},{8,0},{10,2},{20,16},{22,... | collective-permute-start | bytes 589832 | tf_op jit(solution)/shard_map/ppermute | solution.py:86
  99.6 5.9 %collective-permute-start.13 = (bf16[192,512]{1,0:T(8,128)(2,1)S(1)}, bf16[192,512]{1,0:T(8,128)(2,1)S(1)}, u32[]{:S(2)}, u32[]{:S(2)}) collective-permute-start(bf16[192,512]{1,0:T(8,128)(2,1)S(1)} %collective-permute-done.12.refs_2_), channel_id=1, source_target_pairs={{0,2},{2,0},{4,6},{6,4},{8,10},{10,8},{12,14},{14,12},{1,3},{3,1},... | collective-permute-start | bytes 589832 | tf_op jit(solution)/shard_map/ppermute | solution.py:89
  101.0 6.0 %collective-permute-start.15 = (bf16[192,512]{1,0:T(8,128)(2,1)S(1)}, bf16[192,512]{1,0:T(8,128)(2,1)S(1)}, u32[]{:S(2)}, u32[]{:S(2)}) collective-permute-start(bf16[192,512]{1,0:T(8,128)(2,1)S(1)} %collective-permute-done.12.refs_2_), channel_id=1, source_target_pairs={{0,16},{16,0},{1,17},{17,1},{2,18},{18,2},{3,19},{19,3},{4,20},{20... | collective-permute-start | bytes 589832 | tf_op jit(solution)/shard_map/ppermute | solution.py:92
  101.1 14.0 %collective-permute-start.19 = (bf16[8,192,128]{2,1,0:T(8,128)(2,1)S(1)}, bf16[8,192,128]{2,1,0:T(8,128)(2,1)S(1)}, u32[]{:S(2)}, u32[]{:S(2)}) collective-permute-start(bf16[8,192,128]{2,1,0:T(8,128)(2,1)S(1)} %all-to-all-done.own_ref), channel_id=1, source_target_pairs={{0,1},{1,0},{2,3},{3,2},{4,5},{5,4},{6,7},{7,6},{8,9},{9,8},{10,11... | collective-permute-start | bytes 1179656 | tf_op jit(solution)/shard_map/ppermute | solution.py:364
  101.1 8.7 %collective-permute-start.17 = (bf16[192,512]{1,0:T(8,128)(2,1)S(1)}, bf16[192,512]{1,0:T(8,128)(2,1)S(1)}, u32[]{:S(2)}, u32[]{:S(2)}) collective-permute-start(bf16[192,512]{1,0:T(8,128)(2,1)S(1)} %collective-permute-done.12.refs_2_), channel_id=1, source_target_pairs={{0,4},{2,6},{4,12},{6,14},{12,8},{14,10},{8,0},{10,2},{20,16},{22,... | collective-permute-start | bytes 589832 | tf_op jit(solution)/shard_map/ppermute | solution.py:86
  105.5 5.7 %collective-permute-start.14 = (bf16[192,512]{1,0:T(8,128)(2,1)S(1)}, bf16[192,512]{1,0:T(8,128)(2,1)S(1)}, u32[]{:S(2)}, u32[]{:S(2)}) collective-permute-start(bf16[192,512]{1,0:T(8,128)(2,1)S(1)} %constant_dynamic-slice_fusion.refs_0_), channel_id=1, source_target_pairs={{0,2},{2,0},{4,6},{6,4},{8,10},{10,8},{12,14},{14,12},{1,3},{3,1},... | collective-permute-start | bytes 589832 | tf_op jit(solution)/shard_map/ppermute | solution.py:89
  107.0 5.7 %collective-permute-start.16 = (bf16[192,512]{1,0:T(8,128)(2,1)S(1)}, bf16[192,512]{1,0:T(8,128)(2,1)S(1)}, u32[]{:S(2)}, u32[]{:S(2)}) collective-permute-start(bf16[192,512]{1,0:T(8,128)(2,1)S(1)} %collective-permute-done.13.refs_3_), channel_id=1, source_target_pairs={{0,16},{16,0},{1,17},{17,1},{2,18},{18,2},{3,19},{19,3},{4,20},{20... | collective-permute-start | bytes 589832 | tf_op jit(solution)/shard_map/ppermute | solution.py:92
  107.0 6.6 %collective-permute-start.18 = (bf16[192,512]{1,0:T(8,128)(2,1)S(1)}, bf16[192,512]{1,0:T(8,128)(2,1)S(1)}, u32[]{:S(2)}, u32[]{:S(2)}) collective-permute-start(bf16[192,512]{1,0:T(8,128)(2,1)S(1)} %collective-permute-done.13.refs_3_), channel_id=1, source_target_pairs={{0,4},{2,6},{4,12},{6,14},{12,8},{14,10},{8,0},{10,2},{20,16},{22,... | collective-permute-start | bytes 589832 | tf_op jit(solution)/shard_map/ppermute | solution.py:86
  113.6 1.0 copy-start.10
  114.6 6.5 %copy-start.12 = (bf16[8,128,192]{2,1,0:T(8,128)(2,1)S(1)}, bf16[8,128,192]{2,1,0:T(8,128)(2,1)}, u32[]{:S(2)}) copy-start(bf16[8,128,192]{2,1,0:T(8,128)(2,1)} %copy-done.11) | copy-start | bytes 1179652
  115.1 6.1 %copy-start.8 = (bf16[1536,256]{1,0:T(8,128)(2,1)S(1)}, bf16[1536,256]{1,0:T(8,128)(2,1)}, u32[]{:S(2)}) copy-start(bf16[1536,256]{1,0:T(8,128)(2,1)} %weight_ref.2) | copy-start | bytes 2359300
  116.5 1.7 %copy-start.1 = (bf16[1536,768]{1,0:T(8,128)(2,1)S(1)}, bf16[1536,768]{1,0:T(8,128)(2,1)}, u32[]{:S(2)}) copy-start(bf16[1536,768]{1,0:T(8,128)(2,1)} %all-gather.2.cloned.1.call-done.weight_ref) | copy-start | bytes 7077892
  118.2 15.6 %copy-start.14 = (bf16[128,128]{1,0:T(8,128)(2,1)S(1)}, bf16[128,128]{1,0:T(8,128)(2,1)}, u32[]{:S(2)}) copy-start(bf16[128,128]{1,0:T(8,128)(2,1)} %weight_ref.3) | copy-start | bytes 98308
  119.1 2.0 %collective-permute-start.20 = (bf16[8,128,192]{2,1,0:T(8,128)(2,1)S(1)}, bf16[8,128,192]{2,1,0:T(8,128)(2,1)S(1)}, u32[]{:S(2)}, u32[]{:S(2)}) collective-permute-start(bf16[8,128,192]{2,1,0:T(8,128)(2,1)S(1)} %output.1.part_ref), channel_id=1, source_target_pairs={{0,1},{1,0},{2,3},{3,2},{4,5},{5,4},{6,7},{7,6},{8,9},{9,8},{10,11... | collective-permute-start | bytes 1179656 | tf_op jit(solution)/shard_map/ppermute | solution.py:396
  122.4 3.6 %collective-permute-start.21 = (bf16[8,256]{1,0:T(8,128)(2,1)S(1)}, bf16[8,256]{1,0:T(8,128)(2,1)S(1)}, u32[]{:S(2)}, u32[]{:S(2)}) collective-permute-start(bf16[8,256]{1,0:T(8,128)(2,1)S(1)} %get-tuple-element.25.own_ref), channel_id=1, source_target_pairs={{0,2},{2,0},{4,6},{6,4},{8,10},{10,8},{12,14},{14,12},{1,3},{3,1},... | collective-permute-start | bytes 12296 | tf_op jit(solution)/shard_map/ppermute | solution.py:414
  126.0 3.7 %collective-permute-start.22 = (bf16[16,256]{1,0:T(8,128)(2,1)S(1)}, bf16[16,256]{1,0:T(8,128)(2,1)S(1)}, u32[]{:S(2)}, u32[]{:S(2)}) collective-permute-start(bf16[16,256]{1,0:T(8,128)(2,1)S(1)} %pad_maximum_fusion.1), channel_id=1, source_target_pairs={{0,4},{2,6},{4,0},{6,2},{8,12},{10,14},{12,8},{14,10},{1,5},{3,7},... | collective-permute-start | bytes 24584 | tf_op jit(solution)/shard_map/ppermute | solution.py:414
  129.6 4.2 %collective-permute-start.23 = (bf16[32,256]{1,0:T(8,128)(2,1)S(1)}, bf16[32,256]{1,0:T(8,128)(2,1)S(1)}, u32[]{:S(2)}, u32[]{:S(2)}) collective-permute-start(bf16[32,256]{1,0:T(8,128)(2,1)S(1)} %constant_dynamic-update-slice_fusion), channel_id=1, source_target_pairs={{0,8},{2,10},{4,12},{6,14},{9,1},{11,3},{13,5},{15,7},{16,24},{18,... | collective-permute-start | bytes 49160 | tf_op jit(solution)/shard_map/ppermute | solution.py:416
Sparse Core Ops, SparseCore 0:
  10.2 66.0 all-gather.1

commit v6 on v5

--- a/solution.py
+++ b/solution.py
@@ -111,7 +111,7 @@
     return jnp.where((gap >= 0) & (gap < POOL), 1.0 / POOL, 0.0).astype(BF16)
 
 
-def act_kernel(taps, own_ref, other_ref, halo_ref, gain_ref, out_ref, act, gaincol):
+def act_kernel(taps, own_ref, other_ref, gain_ref, out_ref, act, gaincol):
     channels, positions = act.shape
     half = own_ref.shape[0]
     col = lax.axis_index("col")
@@ -131,29 +131,30 @@
             at = pl.multiple_of(index * half + j * step, step)
             x = ref[j * step:(j + 1) * step, :].astype(F32) * scale
             act[pl.ds(at, step), :] = gelu(x * gaincol[pl.ds(at, step), :1]).astype(BF16)
-    h = halo_ref[...].astype(F32)
-    h = h * lax.rsqrt(jnp.sum(h * h, axis=1, keepdims=True) / channels + EPS) * gain_ref[...]
-    h = gelu(h).astype(BF16)
     rows = out_ref.shape[0]
-    shape = (0, rows, rows // taps, taps, positions)
-    out_ref[...] = (
-        dot_nt(window_means(*shape, positions), act[...]) + dot_nn(window_means(*shape, h.shape[0]), h)
-    ).astype(BF16)
-
-
-def conv_kernel(windows_ref, own_ref, weight_hbm, out_ref, weights, sems):
-    taps = weights.shape[0]
+    out_ref[...] = dot_nt(window_means(0, rows, rows // taps, taps, positions, positions), act[...]).astype(BF16)
+
+
+def conv_kernel(windows_ref, own_ref, halo_ref, gain_ref, weight_hbm, out_ref, weights, sems):
+    taps, _, channels = weights.shape
     copies = [pltpu.make_async_copy(weight_hbm.at[t], weights.at[t], sems.at[t]) for t in range(taps)]
     ahead = 2
     for c in copies[:ahead]:
         c.start()
     tokens, positions = out_ref.shape[0], own_ref.shape[1]
+    h = halo_ref[...].astype(F32)
+    h = h * lax.rsqrt(jnp.sum(h * h, axis=1, keepdims=True) / channels + EPS) * gain_ref[...]
+    h = gelu(h).astype(BF16)
     total = dot_nt(window_means((taps // 2) * tokens, tokens, tokens, taps, positions, positions), own_ref[...])
     for t in range(taps):
+        window = windows_ref[t * tokens:(t + 1) * tokens]
+        if t != taps // 2:
+            edges = dot_nn(window_means(t * tokens, tokens, tokens, taps, positions, h.shape[0]), h)
+            window = (window.astype(F32) + edges).astype(BF16)
         copies[t].wait()
         if t + ahead < taps:
             copies[t + ahead].start()
-        total = total + dot_nt(windows_ref[t * tokens:(t + 1) * tokens], weights[t])
+        total = total + dot_nt(window, weights[t])
     out_ref[...] = total.astype(BF16)
 
 
@@ -181,15 +182,15 @@
     for ref, owner in zip(blocks, block_owners()):
         total = total + dot_nn(normed_ref[owner], ref[:, half:])
     kv = total.T.astype(BF16)
-    for i in range(kv_ref.shape[0]):
-        kv_ref[i] = kv
+    kv_ref[...] = kv
 
 
 def query_kernel(pieces, normed_ref, *refs):
     blocks, query_ref = refs[:pieces], refs[pieces]
+    features = query_ref.shape[1]
     total = 0.0
     for ref, owner in zip(blocks, block_owners()):
-        total = total + dot_nn(normed_ref[owner], ref[...])
+        total = total + dot_nn(normed_ref[owner], ref[:, :features])
     query_ref[...] = (total * DK ** (-0.5)).astype(BF16)
 
 
@@ -207,12 +208,12 @@
         out_ref[h] = (dot_nt(weights.astype(BF16), values[...]) / total).astype(BF16)
 
 
-def output_kernel(attended_ref, weight_ref, out_ref):
+def output_kernel(pieces, features, attended_ref, *refs):
+    blocks, out_ref = refs[:pieces], refs[pieces]
     heads = attended_ref.shape[0]
     flat = jnp.concatenate([attended_ref[h] for h in range(heads)], axis=1)
-    count, _, block = out_ref.shape
-    for s in range(count):
-        out_ref[s] = dot_nt(flat, weight_ref[s * block:(s + 1) * block]).astype(BF16)
+    for ref, owner in zip(blocks, block_owners()):
+        out_ref[owner] = dot_nt(flat, ref[:, features:]).astype(BF16)
 
 
 def token_kernel(embedded_ref, part_ref, other_ref, weight_ref, token_ref, send_ref, whole):
@@ -267,39 +268,43 @@
     swap = [(i, (i + 1) % cols) for i in range(cols)]
     shape = jax.ShapeDtypeStruct
 
+    embed_own = jnp.concatenate(
+        [embed_weight.T, lax.dynamic_slice_in_dim(keyvalue_weight, col * DK, DV, 1)], axis=1
+    )
+    later_own = jnp.concatenate(
+        [
+            lax.dynamic_slice_in_dim(query_weight, col * features, features, 1),
+            lax.dynamic_slice_in_dim(output_weight.T, col * heads * DV, heads * DV, 1),
+        ],
+        axis=1,
+    )
+    ring = planned(count, lax.axis_size("grp")) and cols == 2
+    e, q = (Blocks(x, count) for x in (embed_own, later_own))
+
     signal_t = signal.T
     up = [(i, i + 1) for i in range(count - 1)]
+    if ring:
+        e.along("own", "step")
+        e.across("own", "own2")
+    other_t = lax.ppermute(signal_t, "col", swap)
     before = lax.ppermute(signal[positions - reach:], "seq", up)
     behind = lax.ppermute(signal[:reach], "seq", [(j, i) for i, j in up])
-    other_t = lax.ppermute(signal_t, "col", swap)
     own_halo = jnp.pad(jnp.concatenate([before, behind], axis=0), ((0, 16 - 2 * reach), (0, 0)))
     other_halo = lax.ppermute(own_halo, "col", swap)
     halo = jnp.where(
         col == 0, jnp.concatenate([own_halo, other_halo], axis=1), jnp.concatenate([other_halo, own_halo], axis=1)
     )
-
-    embed_own = jnp.concatenate(
-        [embed_weight.T, lax.dynamic_slice_in_dim(keyvalue_weight, col * DK, DV, 1)], axis=1
-    )
-    query_own = lax.dynamic_slice_in_dim(query_weight, col * features, features, 1)
-    output_own = lax.dynamic_slice_in_dim(output_weight.T, col * heads * DV, heads * DV, 1)
-    ring = planned(count, lax.axis_size("grp")) and cols == 2
-    e, q = (Blocks(x, count) for x in (embed_own, query_own))
-    output_all = lax.all_gather(output_own, "seq", axis=0, tiled=True)
-    if ring:
-        e.at["own"] = after(e.at["own"], before, behind)
-        e.along("own", "step")
-        e.across("own", "own2")
+    gain_row = conv_gain.reshape(1, channels)
     windows = pl.pallas_call(
         functools.partial(act_kernel, taps),
         out_shape=shape((taps * tokens, channels), BF16),
-        in_specs=vspec(4),
+        in_specs=vspec(3),
         out_specs=pl.BlockSpec(memory_space=VMEM),
         scratch_shapes=[pltpu.VMEM((channels, positions), BF16), pltpu.VMEM((channels, 8), F32)],
         compiler_params=params(20),
         cost_estimate=cost(2 * taps * tokens * channels * positions, 4 * channels * positions),
         name="act",
-    )(signal_t, other_t, halo, conv_gain.reshape(1, channels))
+    )(signal_t, other_t, gain_row)
     if ring:
         e.at["step"] = after(e.at["step"], e.at["own2"], windows)
         e.along("step", "far")
@@ -308,13 +313,13 @@
     pooled = pl.pallas_call(
         conv_kernel,
         out_shape=shape((tokens, half), BF16),
-        in_specs=vspec(2) + hspec(1),
+        in_specs=vspec(4) + hspec(1),
         out_specs=pl.BlockSpec(memory_space=VMEM),
         scratch_shapes=[pltpu.VMEM((taps, half, channels), BF16), pltpu.SemaphoreType.DMA((taps,))],
-        compiler_params=params(52),
+        compiler_params=params(50),
         cost_estimate=cost(2 * taps * tokens * channels * half, 2 * taps * channels * half),
         name="conv",
-    )(windows, signal_t, conv_weight.transpose(0, 2, 1))
+    )(windows, signal_t, halo, gain_row, conv_weight.transpose(0, 2, 1))
     if ring:
         e.at["far"] = after(e.at["far"], pooled)
         e.at["step2"] = after(e.at["step2"], pooled)
@@ -330,9 +335,9 @@
         q.along("step2", "far2")
         q.across("own", "own2")
         q.between("step2", "cross2")
-        embed_blocks, query_blocks = e.pieces(), q.pieces()
+        embed_blocks, later_blocks = e.pieces(), q.pieces()
     else:
-        embed_blocks, query_blocks = ([lax.all_gather(x.at["own"], "seq", axis=0, tiled=True)] for x in (e, q))
+        embed_blocks, later_blocks = ([lax.all_gather(x.at["own"], "seq", axis=0, tiled=True)] for x in (e, q))
     pieces = len(embed_blocks)
     block = width // pieces
 
@@ -350,7 +355,7 @@
     keyvalue, normed, embedded = pl.pallas_call(
         functools.partial(keyvalue_kernel, pieces, half),
         out_shape=(
-            shape((count, DV, tokens), BF16),
+            shape((DV, tokens), BF16),
             shape((pieces, tokens, block), BF16),
             shape((pieces, tokens, block), BF16),
         ),
@@ -360,7 +365,14 @@
         cost_estimate=cost(2 * tokens * width * DV, 2 * width * DV),
         name="keyvalue",
     )(part, other_part, attn_gain.reshape(pieces, 1, block), *embed_blocks)
-    gathered = lax.all_to_all(keyvalue, "seq", 0, 0)
+    if ring:
+        here = jnp.stack([keyvalue, lax.ppermute(keyvalue, "seq", [(i, i ^ 1) for i in range(count)])])
+        onward = [(2 * RING[k] + i, 2 * RING[(k + 1) % 4] + i) for k in range(4) for i in range(2)]
+        ahead = lax.ppermute(here, "seq", onward)
+        back = lax.ppermute(here, "seq", [(j, i) for i, j in onward])
+        gathered = jnp.concatenate([here, ahead, back, lax.ppermute(ahead, "seq", onward)])
+    else:
+        gathered = lax.all_gather(keyvalue, "seq", axis=0)
     gathered_other = lax.ppermute(gathered, "col", swap)
 
     queries = pl.pallas_call(
@@ -371,7 +383,7 @@
         compiler_params=params(12),
         cost_estimate=cost(2 * tokens * width * features, 2 * width * features),
         name="query",
-    )(normed, *query_blocks)
+    )(normed, *later_blocks)
 
     attended = pl.pallas_call(
         attend_kernel,
@@ -385,14 +397,14 @@
     )(queries, gathered, gathered_other)
 
     part_out = pl.pallas_call(
-        output_kernel,
+        functools.partial(output_kernel, pieces, features),
         out_shape=shape((pieces, tokens, block), BF16),
-        in_specs=vspec(2),
+        in_specs=vspec(1 + pieces),
         out_specs=pl.BlockSpec(memory_space=VMEM),
         compiler_params=params(16),
         cost_estimate=cost(2 * tokens * heads * DV * width, 2 * heads * DV * width),
         name="output",
-    )(attended, output_all)
+    )(attended, *later_blocks)
     other_out = lax.ppermute(part_out, "col", swap)
 
     out_width = rowcol_weight.shape[1]

time: 142 us -> 105 us (0.74); the launches traced: 141 us -> 103 us
  waiting for transfers between devices: 59.9 us -> 39.9 us
  between operations: 14.4 us -> 1 us
  local copies, waits for them, and re-layouts: 14.2 us -> 9.42 us
    ppermute x5, waiting for transfers between devices: 29 us -> 9.42 us  [along(): self.at[target] = lax.ppermute(self.at[source], ('grp', 'seq'), pairs)]
    ppermute x5, waiting for transfers between devices: 16.6 us -> 3.6 us  [across(): lax.ppermute(self.at[source], 'seq', [(i, i ^ 1) for i in range(self.coun...]
    ppermute x0 -> x4, waiting for transfers between devices: none -> 9 us  [the longest x1 3.45 us: on_device(): lax.ppermute(ahead, 'seq', onward)]
    ppermute x4, waiting for transfers between devices: 2.19 us -> 8.56 us  [between(): self.at[target] = lax.ppermute(self.at[source], 'grp', [(0, 1), (1, 0)])]
    ppermute x0 -> x4, starting transfers between devices: none -> 4.41 us  [the longest x1 2.55 us: on_device(): back = lax.ppermute(here, 'seq', [(j, i) for i, j in onward])]
    unnamed x40 -> x38, local copies, waits for them, and re-layouts: 10.3 us -> 6.44 us
    all_to_all x1 -> x0, starting transfers between devices: 3.53 us -> none  [on_device(): gathered = lax.all_to_all(keyvalue, 'seq', 0, 0)]
    ppermute x1, waiting for transfers between devices: 1.95 us -> 0.01 us  [on_device(): other_part = lax.ppermute(part, 'col', swap)]
  transfers between devices with their start and end apart: 26 -> 28, of which waited for: 18 -> 14; matrix products, arithmetic and copies ran while one was open for 3% -> 4% of each run, Pallas kernels for 11% -> 12%
where the time goes in v6:
time: 105 us; the launch traced here: 103 us
  waiting for transfers between devices  39.9 us (38%)
  starting transfers between devices  34.6 us (33%)
  Pallas kernels  16.8 us (16%)
  local copies, waits for them, and re-layouts  9.42 us (9%)
  other arithmetic  1.22 us (1%)
    ppermute x5, waiting for transfers between devices, along(): self.at[target] = lax.ppermute(self.at[source], ('grp', 'seq'), pairs)  9.42 us
    ppermute x4, waiting for transfers between devices, between(): self.at[target] = lax.ppermute(self.at[source], 'grp', [(0, 1), (1, 0)])  8.56 us
    ppermute x5, starting transfers between devices, across(): lax.ppermute(self.at[source], 'seq', [(i, i ^ 1) for i in range(self.coun...  8.52 us
    ppermute x5, starting transfers between devices, along(): self.at[target] = lax.ppermute(self.at[source], ('grp', 'seq'), pairs)  7.15 us
    unnamed x38, local copies, waits for them, and re-layouts  6.44 us
    pallas_call x1, Pallas kernels, on_device(): pl.pallas_call(conv_kernel, out_shape=shape((tokens, half), BF16), in_spe...  6.38 us
    ppermute x2, waiting for transfers between devices, on_device(): lax.ppermute(rows_all, 'seq', [(i, i ^ bit) for i in range(count)])  5.49 us
    ppermute x1, starting transfers between devices, on_device(): before = lax.ppermute(signal[positions - reach:], 'seq', up)  4.56 us
  transfers between devices with their start and end apart: 28, of which 14 were waited for; matrix products, arithmetic and copies ran while one was open for 4% of the time, Pallas kernels for 12%

profile of v6, /device:TPU:0, one launch (start us, length us, event | category | flops | bytes accessed | tf_op | source)
XLA Modules:
  0.0 103.0 jit_solution(10300652244827112594)
XLA Ops:
  1.2 1.0 constant_dynamic-slice_fusion.1
  2.2 1.1 %pad_maximum_fusion.1.refs_0_ = bf16[192,896]{1,0:T(8,128)(2,1)S(1)} fusion(bf16[192,192]{1,0:T(8,128)(2,1)S(1)} %constant_dynamic-slice_fusion.1, bf16[192,704]{1,0:T(8,128)(2,1)} %bitcast.14), kind=kLoop, calls=%fused_computation.1 | loop fusion | flops 688128 | bytes 688128 | tf_op jit(solution)/shard_map/concatenate | solution.py:271
  3.2 2.7 %collective-permute-start.4 = (bf16[192,896]{1,0:T(8,128)(2,1)S(1)}, bf16[192,896]{1,0:T(8,128)(2,1)S(1)}, u32[]{:S(2)}, u32[]{:S(2)}) collective-permute-start(bf16[192,896]{1,0:T(8,128)(2,1)S(1)} %pad_maximum_fusion.1.refs_0_), channel_id=1, source_target_pairs={{0,2},{2,0},{4,6},{6,4},{8,10},{10,8},{12,14},{14,12},{1,3},{3,1},... | collective-permute-start | bytes 1032200 | tf_op jit(solution)/shard_map/ppermute | solution.py:89
  5.9 1.6 %collective-permute-start.5 = (bf16[192,896]{1,0:T(8,128)(2,1)S(1)}, bf16[192,896]{1,0:T(8,128)(2,1)S(1)}, u32[]{:S(2)}, u32[]{:S(2)}) collective-permute-start(bf16[192,896]{1,0:T(8,128)(2,1)S(1)} %pad_maximum_fusion.1.refs_0_), channel_id=1, source_target_pairs={{0,4},{2,6},{4,12},{6,14},{12,8},{14,10},{8,0},{10,2},{20,16},{22,... | collective-permute-start | bytes 1032200 | tf_op jit(solution)/shard_map/ppermute | solution.py:86
  7.5 1.1 %fusion.3 = (bf16[2,704]{0,1:T(8,128)(2,1)S(1)}, bf16[2,704]{0,1:T(8,128)(2,1)S(1)}) fusion(bf16[512,704]{0,1:T(8,128)(2,1)} %param.10), kind=kLoop, calls=%fused_computation.21 | loop fusion | bytes 11264 | tf_op jit(solution)/shard_map/slice | solution.py:290
  8.7 1.4 %collective-permute-start.2 = (bf16[2,704]{1,0:T(2,128)(2,1)S(1)}, bf16[2,704]{1,0:T(2,128)(2,1)S(1)}, u32[]{:S(2)}, u32[]{:S(2)}) collective-permute-start(bf16[2,704]{1,0:T(2,128)(2,1)S(1)} %copy.15), channel_id=1, source_target_pairs={{2,0},{4,2},{6,4},{8,6},{10,8},{12,10},{14,12},{3,1},{5,3},{7,5},{... | collective-permute-start | bytes 8456 | tf_op jit(solution)/shard_map/ppermute | solution.py:291
  10.3 4.6 %collective-permute-start.1 = (bf16[2,704]{1,0:T(2,128)(2,1)S(1)}, bf16[2,704]{1,0:T(2,128)(2,1)S(1)}, u32[]{:S(2)}, u32[]{:S(2)}) collective-permute-start(bf16[2,704]{1,0:T(2,128)(2,1)S(1)} %copy.14), channel_id=1, source_target_pairs={{0,2},{2,4},{4,6},{6,8},{8,10},{10,12},{12,14},{1,3},{3,5},{5,7},{... | collective-permute-start | bytes 8456 | tf_op jit(solution)/shard_map/ppermute | solution.py:290
  14.9 0.7 reshape.10.gain_ref
  16.3 1.1 %copy-done.1 = bf16[512,704]{0,1:T(8,128)(2,1)S(1)} copy-done((bf16[512,704]{0,1:T(8,128)(2,1)S(1)}, bf16[512,704]{0,1:T(8,128)(2,1)}, u32[]{:S(2)}) %copy-start.1) | copy-done | bytes 720920
  17.4 2.7 %act.1.windows_ref = bf16[640,1408]{1,0:T(8,128)(2,1)S(1)} custom-call(bf16[704,512]{1,0:T(8,128)(2,1)S(1)} %bitcast.10, bf16[704,512]{1,0:T(8,128)(2,1)S(1)} %collective-permute-done.other_ref, f32[1,1408]{1,0:T(1,128)S(1)} %reshape.10.gain_ref), custom_call_target="tpu_custom_call" | custom-call | flops 922746880 | bytes 2883584 | tf_op jit(solution)/shard_map/act/pallas_call | solution.py:298
  20.1 2.3 %collective-permute-start.6 = (bf16[192,896]{1,0:T(8,128)(2,1)S(1)}, bf16[192,896]{1,0:T(8,128)(2,1)S(1)}, u32[]{:S(2)}, u32[]{:S(2)}) collective-permute-start(bf16[192,896]{1,0:T(8,128)(2,1)S(1)} %collective-permute-done.5.refs_2_), channel_id=1, source_target_pairs={{0,2},{2,0},{4,6},{6,4},{8,10},{10,8},{12,14},{14,12},{1,3},{3,1},... | collective-permute-start | bytes 1032200 | tf_op jit(solution)/shard_map/ppermute | solution.py:89
  22.4 2.6 %collective-permute-start.9 = (bf16[192,896]{1,0:T(8,128)(2,1)S(1)}, bf16[192,896]{1,0:T(8,128)(2,1)S(1)}, u32[]{:S(2)}, u32[]{:S(2)}) collective-permute-start(bf16[192,896]{1,0:T(8,128)(2,1)S(1)} %collective-permute-done.5.refs_2_), channel_id=1, source_target_pairs={{0,4},{2,6},{4,12},{6,14},{12,8},{14,10},{8,0},{10,2},{20,16},{22,... | collective-permute-start | bytes 1032200 | tf_op jit(solution)/shard_map/ppermute | solution.py:86
  25.1 1.6 %collective-permute-start.7 = (bf16[192,896]{1,0:T(8,128)(2,1)S(1)}, bf16[192,896]{1,0:T(8,128)(2,1)S(1)}, u32[]{:S(2)}, u32[]{:S(2)}) collective-permute-start(bf16[192,896]{1,0:T(8,128)(2,1)S(1)} %collective-permute-done.5.refs_2_), channel_id=1, source_target_pairs={{0,16},{16,0},{1,17},{17,1},{2,18},{18,2},{3,19},{19,3},{4,20},{20... | collective-permute-start | bytes 1032200 | tf_op jit(solution)/shard_map/ppermute | solution.py:92
  26.7 1.1 %copy-done.2 = bf16[512,704]{0,1:T(8,128)(2,1)S(1)} copy-done((bf16[512,704]{0,1:T(8,128)(2,1)S(1)}, bf16[512,704]{0,1:T(8,128)(2,1)}, u32[]{:S(2)}) %copy-start.2) | copy-done | bytes 720920
  27.8 6.4 %conv.1.pooled_ref = bf16[128,704]{1,0:T(8,128)(2,1)S(1)} custom-call(bf16[640,1408]{1,0:T(8,128)(2,1)S(1)} %act.1.windows_ref, bf16[704,512]{1,0:T(8,128)(2,1)S(1)} %bitcast.11, bf16[16,1408]{1,0:T(8,128)(2,1)S(1)} %maximum_select_fusion.halo_ref, f32[1,1408]{1,0:T(1,128)S(1)} %reshape.10.gain_ref, bf16[5,704,1408]{2,1,0:T(8,128)(2,1)} %bitcast.13), custom_call_target="tpu_custom_call" | custom-call | flops 1268776960 | bytes 9912320 | tf_op jit(solution)/shard_map/conv/pallas_call | solution.py:313
  34.2 0.6 collective-permute-start.8
  34.8 1.0 collective-permute-start.10
  35.8 0.8 collective-permute-start.12
  36.7 7.2 %collective-permute-done.8.refs_5_ = bf16[192,896]{1,0:T(8,128)(2,1)S(1)} collective-permute-done((bf16[192,896]{1,0:T(8,128)(2,1)S(1)}, bf16[192,896]{1,0:T(8,128)(2,1)S(1)}, u32[]{:S(2)}, u32[]{:S(2)}) %collective-permute-start.8) | collective-permute-done | bytes 344096 | tf_op jit(solution)/shard_map/ppermute | solution.py:92
  44.1 1.0 embed.1.part_ref
  45.3 4.0 %collective-permute-done.12.refs_2_ = bf16[192,1280]{1,0:T(8,128)(2,1)S(1)} collective-permute-done((bf16[192,1280]{1,0:T(8,128)(2,1)S(1)}, bf16[192,1280]{1,0:T(8,128)(2,1)S(1)}, u32[]{:S(2)}, u32[]{:S(2)}) %collective-permute-start.12) | collective-permute-done | bytes 491552 | tf_op jit(solution)/shard_map/ppermute | solution.py:86
  49.3 0.7 collective-permute-start.13
  50.1 0.6 collective-permute-start.15
  50.6 2.2 %collective-permute-start.17 = (bf16[192,1280]{1,0:T(8,128)(2,1)S(1)}, bf16[192,1280]{1,0:T(8,128)(2,1)S(1)}, u32[]{:S(2)}, u32[]{:S(2)}) collective-permute-start(bf16[192,1280]{1,0:T(8,128)(2,1)S(1)} %collective-permute-done.12.refs_2_), channel_id=1, source_target_pairs={{0,4},{2,6},{4,12},{6,14},{12,8},{14,10},{8,0},{10,2},{20,16},{22,... | collective-permute-start | bytes 1474568 | tf_op jit(solution)/shard_map/ppermute | solution.py:86
  52.8 1.0 copy-done.4
  53.8 1.0 copy-done.6
  54.8 1.0 copy-done.8
  55.8 1.0 copy-done.10
  56.7 1.9 %keyvalue.1 = (bf16[192,128]{1,0:T(8,128)(2,1)S(1)}, bf16[8,128,192]{2,1,0:T(8,128)(2,1)S(1)}, bf16[8,128,192]{2,1,0:T(8,128)(2,1)S(1)}) custom-call(bf16[8,128,192]{2,1,0:T(8,128)(2,1)S(1)} %embed.1.part_ref, bf16[8,128,192]{2,1,0:T(8,128)(2,1)} %collective-permute-done.11.other_ref, f32[8,1,192]{2,1,0:T(1,128)S(1)} %reshape.11.gain_ref, ...), custom_call_target="tpu_custom_call" | custom-call | flops 75497472 | bytes 589824 | tf_op jit(solution)/shard_map/keyvalue/pallas_call | solution.py:355
  58.7 1.4 %collective-permute-start.19 = (bf16[192,128]{1,0:T(8,128)(2,1)S(1)}, bf16[192,128]{1,0:T(8,128)(2,1)S(1)}, u32[]{:S(2)}, u32[]{:S(2)}) collective-permute-start(bf16[192,128]{1,0:T(8,128)(2,1)S(1)} %get-tuple-element.21), channel_id=1, source_target_pairs={{0,2},{2,0},{4,6},{6,4},{8,10},{10,8},{12,14},{14,12},{1,3},{3,1},... | collective-permute-start | bytes 147464 | tf_op jit(solution)/shard_map/ppermute | solution.py:369
  60.1 2.7 %collective-permute-done.19 = bf16[192,128]{1,0:T(8,128)(2,1)S(1)} collective-permute-done((bf16[192,128]{1,0:T(8,128)(2,1)S(1)}, bf16[192,128]{1,0:T(8,128)(2,1)S(1)}, u32[]{:S(2)}, u32[]{:S(2)}) %collective-permute-start.19) | collective-permute-done | bytes 49184 | tf_op jit(solution)/shard_map/ppermute | solution.py:369
  63.3 2.6 %collective-permute-start.21 = (bf16[2,192,128]{2,1,0:T(8,128)(2,1)S(1)}, bf16[2,192,128]{2,1,0:T(8,128)(2,1)S(1)}, u32[]{:S(2)}, u32[]{:S(2)}) collective-permute-start(bf16[2,192,128]{2,1,0:T(8,128)(2,1)S(1)} %pad_maximum_fusion.2), channel_id=1, source_target_pairs={{4,0},{6,2},{12,4},{14,6},{8,12},{10,14},{0,8},{2,10},{5,1},{7,3},... | collective-permute-start | bytes 294920 | tf_op jit(solution)/shard_map/ppermute | solution.py:372
  65.8 2.8 %collective-permute-done.20 = bf16[2,192,128]{2,1,0:T(8,128)(2,1)S(1)} collective-permute-done((bf16[2,192,128]{2,1,0:T(8,128)(2,1)S(1)}, bf16[2,192,128]{2,1,0:T(8,128)(2,1)S(1)}, u32[]{:S(2)}, u32[]{:S(2)}) %collective-permute-start.20) | collective-permute-done | bytes 98336 | tf_op jit(solution)/shard_map/ppermute | solution.py:371
  68.7 1.8 %collective-permute-start.14 = (bf16[192,1280]{1,0:T(8,128)(2,1)S(1)}, bf16[192,1280]{1,0:T(8,128)(2,1)S(1)}, u32[]{:S(2)}, u32[]{:S(2)}) collective-permute-start(bf16[192,1280]{1,0:T(8,128)(2,1)S(1)} %pad_maximum_fusion.refs_0_), channel_id=1, source_target_pairs={{0,2},{2,0},{4,6},{6,4},{8,10},{10,8},{12,14},{14,12},{1,3},{3,1},... | collective-permute-start | bytes 1474568 | tf_op jit(solution)/shard_map/ppermute | solution.py:89
  71.1 3.4 %collective-permute-done.22 = bf16[2,192,128]{2,1,0:T(8,128)(2,1)S(1)} collective-permute-done((bf16[2,192,128]{2,1,0:T(8,128)(2,1)S(1)}, bf16[2,192,128]{2,1,0:T(8,128)(2,1)S(1)}, u32[]{:S(2)}, u32[]{:S(2)}) %collective-permute-start.22) | collective-permute-done | bytes 98336 | tf_op jit(solution)/shard_map/ppermute | solution.py:373
  74.7 3.3 %collective-permute-done.14.refs_1_ = bf16[192,1280]{1,0:T(8,128)(2,1)S(1)} collective-permute-done((bf16[192,1280]{1,0:T(8,128)(2,1)S(1)}, bf16[192,1280]{1,0:T(8,128)(2,1)S(1)}, u32[]{:S(2)}, u32[]{:S(2)}) %collective-permute-start.14) | collective-permute-done | bytes 491552 | tf_op jit(solution)/shard_map/ppermute | solution.py:89
  78.0 1.4 %collective-permute-done.16.refs_5_ = bf16[192,1280]{1,0:T(8,128)(2,1)S(1)} collective-permute-done((bf16[192,1280]{1,0:T(8,128)(2,1)S(1)}, bf16[192,1280]{1,0:T(8,128)(2,1)S(1)}, u32[]{:S(2)}, u32[]{:S(2)}) %collective-permute-start.16) | collective-permute-done | bytes 491552 | tf_op jit(solution)/shard_map/ppermute | solution.py:92
  79.3 5.4 %collective-permute-done.18.refs_7_ = bf16[192,1280]{1,0:T(8,128)(2,1)S(1)} collective-permute-done((bf16[192,1280]{1,0:T(8,128)(2,1)S(1)}, bf16[192,1280]{1,0:T(8,128)(2,1)S(1)}, u32[]{:S(2)}, u32[]{:S(2)}) %collective-permute-start.18) | collective-permute-done | bytes 491552 | tf_op jit(solution)/shard_map/ppermute | solution.py:86
  85.2 1.4 %attend.1.attended_ref = bf16[4,128,192]{2,1,0:T(8,128)(2,1)S(1)} custom-call(bf16[128,512]{1,0:T(8,128)(2,1)S(1)} %query.1.query_ref, bf16[8,192,128]{2,1,0:T(8,128)(2,1)S(1)} %constant_dynamic-update-slice_fusion.own_ref, bf16[8,192,128]{2,1,0:T(8,128)(2,1)S(1)} %collective-permute-done.23.other_ref), custom_call_target="tpu_custom_call" | custom-call | flops 335544320 | bytes 786432 | tf_op jit(solution)/shard_map/attend/pallas_call | solution.py:388
  86.6 0.9 output.1.part_ref
  87.6 1.9 %collective-permute-done.24.other_ref = bf16[8,128,192]{2,1,0:T(8,128)(2,1)S(1)} collective-permute-done((bf16[8,128,192]{2,1,0:T(8,128)(2,1)S(1)}, bf16[8,128,192]{2,1,0:T(8,128)(2,1)S(1)}, u32[]{:S(2)}, u32[]{:S(2)}) %collective-permute-start.24) | collective-permute-done | bytes 393248 | tf_op jit(solution)/shard_map/ppermute | solution.py:408
  89.5 1.3 %tokens.1 = (bf16[64,1536]{1,0:T(8,128)(2,1)}, bf16[8,256]{1,0:T(8,128)(2,1)S(1)}) custom-call(bf16[8,128,192]{2,1,0:T(8,128)(2,1)S(1)} %get-tuple-element.16.embedded_ref, bf16[8,128,192]{2,1,0:T(8,128)(2,1)S(1)} %output.1.part_ref, bf16[8,128,192]{2,1,0:T(8,128)(2,1)S(1)} %collective-permute-done.24.other_ref, bf16[1536,256]{1,0:T(8,128)(2,1)S(1)} %copy-done.11), custom_call_target="tpu_custom_call" | custom-call | flops 6291456 | bytes 786432 | tf_op jit(solution)/shard_map/tokens/pallas_call | solution.py:412
  90.7 1.8 %collective-permute-start.25 = (bf16[8,256]{1,0:T(8,128)(2,1)S(1)}, bf16[8,256]{1,0:T(8,128)(2,1)S(1)}, u32[]{:S(2)}, u32[]{:S(2)}) collective-permute-start(bf16[8,256]{1,0:T(8,128)(2,1)S(1)} %get-tuple-element.23.own_ref), channel_id=1, source_target_pairs={{0,2},{2,0},{4,6},{6,4},{8,10},{10,8},{12,14},{14,12},{1,3},{3,1},... | collective-permute-start | bytes 12296 | tf_op jit(solution)/shard_map/ppermute | solution.py:426
  92.5 1.9 %collective-permute-done.25 = bf16[8,256]{1,0:T(8,128)(2,1)S(1)} collective-permute-done((bf16[8,256]{1,0:T(8,128)(2,1)S(1)}, bf16[8,256]{1,0:T(8,128)(2,1)S(1)}, u32[]{:S(2)}, u32[]{:S(2)}) %collective-permute-start.25) | collective-permute-done | bytes 4128 | tf_op jit(solution)/shard_map/ppermute | solution.py:426
  94.4 3.6 %collective-permute-done.26 = bf16[16,256]{1,0:T(8,128)(2,1)S(1)} collective-permute-done((bf16[16,256]{1,0:T(8,128)(2,1)S(1)}, bf16[16,256]{1,0:T(8,128)(2,1)S(1)}, u32[]{:S(2)}, u32[]{:S(2)}) %collective-permute-start.26) | collective-permute-done | bytes 8224 | tf_op jit(solution)/shard_map/ppermute | solution.py:426
  98.0 2.7 %collective-permute-start.27 = (bf16[32,256]{1,0:T(8,128)(2,1)S(1)}, bf16[32,256]{1,0:T(8,128)(2,1)S(1)}, u32[]{:S(2)}, u32[]{:S(2)}) collective-permute-start(bf16[32,256]{1,0:T(8,128)(2,1)S(1)} %constant_dynamic-update-slice_fusion.5), channel_id=1, source_target_pairs={{0,8},{2,10},{4,12},{6,14},{9,1},{11,3},{13,5},{15,7},{16,24},{18,... | collective-permute-start | bytes 49160 | tf_op jit(solution)/shard_map/ppermute | solution.py:428
  100.7 1.4 %collective-permute-done.27 = bf16[32,256]{1,0:T(8,128)(2,1)S(1)} collective-permute-done((bf16[32,256]{1,0:T(8,128)(2,1)S(1)}, bf16[32,256]{1,0:T(8,128)(2,1)S(1)}, u32[]{:S(2)}, u32[]{:S(2)}) %collective-permute-start.27) | collective-permute-done | bytes 16416 | tf_op jit(solution)/shard_map/ppermute | solution.py:428
  102.2 0.8 pair.1
  (70 shorter events, 3.7 us)
Async XLA Ops:
  0.6 14.2 %copy-start = (bf16[1536,192]{0,1:T(8,128)(2,1)S(1)}, bf16[1536,192]{0,1:T(8,128)(2,1)}, u32[]{:S(2)}) copy-start(bf16[1536,192]{0,1:T(8,128)(2,1)} %param.17) | copy-start | bytes 1769476
  0.6 15.6 %collective-permute-start = (bf16[704,512]{1,0:T(8,128)(2,1)}, bf16[704,512]{1,0:T(8,128)(2,1)S(1)}, u32[]{:S(2)}, u32[]{:S(2)}) collective-permute-start(bf16[704,512]{1,0:T(8,128)(2,1)} %bitcast.9), channel_id=1, source_target_pairs={{0,1},{1,0},{2,3},{3,2},{4,5},{5,4},{6,7},{7,6},{8,9},{9,8},{10,11... | collective-permute-start | bytes 2162696 | tf_op jit(solution)/shard_map/ppermute | solution.py:289
  3.2 16.8 %collective-permute-start.4 = (bf16[192,896]{1,0:T(8,128)(2,1)S(1)}, bf16[192,896]{1,0:T(8,128)(2,1)S(1)}, u32[]{:S(2)}, u32[]{:S(2)}) collective-permute-start(bf16[192,896]{1,0:T(8,128)(2,1)S(1)} %pad_maximum_fusion.1.refs_0_), channel_id=1, source_target_pairs={{0,2},{2,0},{4,6},{6,4},{8,10},{10,8},{12,14},{14,12},{1,3},{3,1},... | collective-permute-start | bytes 1032200 | tf_op jit(solution)/shard_map/ppermute | solution.py:89
  5.9 14.2 %collective-permute-start.5 = (bf16[192,896]{1,0:T(8,128)(2,1)S(1)}, bf16[192,896]{1,0:T(8,128)(2,1)S(1)}, u32[]{:S(2)}, u32[]{:S(2)}) collective-permute-start(bf16[192,896]{1,0:T(8,128)(2,1)S(1)} %pad_maximum_fusion.1.refs_0_), channel_id=1, source_target_pairs={{0,4},{2,6},{4,12},{6,14},{12,8},{14,10},{8,0},{10,2},{20,16},{22,... | collective-permute-start | bytes 1032200 | tf_op jit(solution)/shard_map/ppermute | solution.py:86
  8.7 27.0 %copy-start.13 = (bf16[192,1024]{1,0:T(8,128)(2,1)S(1)}, bf16[192,1024]{1,0:T(8,128)(2,1)}, u32[]{:S(2)}) copy-start(bf16[192,1024]{1,0:T(8,128)(2,1)} %param.15) | copy-start | bytes 1179652
  8.7 6.9 %collective-permute-start.2 = (bf16[2,704]{1,0:T(2,128)(2,1)S(1)}, bf16[2,704]{1,0:T(2,128)(2,1)S(1)}, u32[]{:S(2)}, u32[]{:S(2)}) collective-permute-start(bf16[2,704]{1,0:T(2,128)(2,1)S(1)} %copy.15), channel_id=1, source_target_pairs={{2,0},{4,2},{6,4},{8,6},{10,8},{12,10},{14,12},{3,1},{5,3},{7,5},{... | collective-permute-start | bytes 8456 | tf_op jit(solution)/shard_map/ppermute | solution.py:291
  10.3 5.9 %collective-permute-start.1 = (bf16[2,704]{1,0:T(2,128)(2,1)S(1)}, bf16[2,704]{1,0:T(2,128)(2,1)S(1)}, u32[]{:S(2)}, u32[]{:S(2)}) collective-permute-start(bf16[2,704]{1,0:T(2,128)(2,1)S(1)} %copy.14), channel_id=1, source_target_pairs={{0,2},{2,4},{4,6},{6,8},{8,10},{10,12},{12,14},{1,3},{3,5},{5,7},{... | collective-permute-start | bytes 8456 | tf_op jit(solution)/shard_map/ppermute | solution.py:290
  16.2 29.0 %copy-start.14 = (f32[1536]{0:T(1024)S(1)}, f32[1536]{0:T(1024)}, u32[]{:S(2)}) copy-start(f32[1536]{0:T(1024)} %param.14) | copy-start | bytes 18436
  16.2 8.8 %collective-permute-start.3 = (bf16[16,704]{1,0:T(8,128)(2,1)S(1)}, bf16[16,704]{1,0:T(8,128)(2,1)S(1)}, u32[]{:S(2)}, u32[]{:S(2)}) collective-permute-start(bf16[16,704]{1,0:T(8,128)(2,1)S(1)} %fusion.2), channel_id=1, source_target_pairs={{0,1},{1,0},{2,3},{3,2},{4,5},{5,4},{6,7},{7,6},{8,9},{9,8},{10,11... | collective-permute-start | bytes 67592 | tf_op jit(solution)/shard_map/ppermute | solution.py:293
  16.3 1.1 %copy-start.1 = (bf16[512,704]{0,1:T(8,128)(2,1)S(1)}, bf16[512,704]{0,1:T(8,128)(2,1)}, u32[]{:S(2)}) copy-start(bf16[512,704]{0,1:T(8,128)(2,1)} %param.10) | copy-start | bytes 2162692
  20.1 14.1 %collective-permute-start.6 = (bf16[192,896]{1,0:T(8,128)(2,1)S(1)}, bf16[192,896]{1,0:T(8,128)(2,1)S(1)}, u32[]{:S(2)}, u32[]{:S(2)}) collective-permute-start(bf16[192,896]{1,0:T(8,128)(2,1)S(1)} %collective-permute-done.5.refs_2_), channel_id=1, source_target_pairs={{0,2},{2,0},{4,6},{6,4},{8,10},{10,8},{12,14},{14,12},{1,3},{3,1},... | collective-permute-start | bytes 1032200 | tf_op jit(solution)/shard_map/ppermute | solution.py:89
  22.4 12.4 %collective-permute-start.9 = (bf16[192,896]{1,0:T(8,128)(2,1)S(1)}, bf16[192,896]{1,0:T(8,128)(2,1)S(1)}, u32[]{:S(2)}, u32[]{:S(2)}) collective-permute-start(bf16[192,896]{1,0:T(8,128)(2,1)S(1)} %collective-permute-done.5.refs_2_), channel_id=1, source_target_pairs={{0,4},{2,6},{4,12},{6,14},{12,8},{14,10},{8,0},{10,2},{20,16},{22,... | collective-permute-start | bytes 1032200 | tf_op jit(solution)/shard_map/ppermute | solution.py:86
  25.1 11.5 %collective-permute-start.7 = (bf16[192,896]{1,0:T(8,128)(2,1)S(1)}, bf16[192,896]{1,0:T(8,128)(2,1)S(1)}, u32[]{:S(2)}, u32[]{:S(2)}) collective-permute-start(bf16[192,896]{1,0:T(8,128)(2,1)S(1)} %collective-permute-done.5.refs_2_), channel_id=1, source_target_pairs={{0,16},{16,0},{1,17},{17,1},{2,18},{18,2},{3,19},{19,3},{4,20},{20... | collective-permute-start | bytes 1032200 | tf_op jit(solution)/shard_map/ppermute | solution.py:92
  26.7 1.1 %copy-start.2 = (bf16[512,704]{0,1:T(8,128)(2,1)S(1)}, bf16[512,704]{0,1:T(8,128)(2,1)}, u32[]{:S(2)}) copy-start(bf16[512,704]{0,1:T(8,128)(2,1)} %param.10) | copy-start | bytes 2162692
  34.2 9.7 %collective-permute-start.8 = (bf16[192,896]{1,0:T(8,128)(2,1)S(1)}, bf16[192,896]{1,0:T(8,128)(2,1)S(1)}, u32[]{:S(2)}, u32[]{:S(2)}) collective-permute-start(bf16[192,896]{1,0:T(8,128)(2,1)S(1)} %collective-permute-done.6.refs_3_), channel_id=1, source_target_pairs={{0,16},{16,0},{1,17},{17,1},{2,18},{18,2},{3,19},{19,3},{4,20},{20... | collective-permute-start | bytes 1032200 | tf_op jit(solution)/shard_map/ppermute | solution.py:92
  34.8 9.3 %copy-start.3 = (bf16[192,896]{1,0:T(8,128)(2,1)}, bf16[192,896]{1,0:T(8,128)(2,1)S(1)}, u32[]{:S(2)}) copy-start(bf16[192,896]{1,0:T(8,128)(2,1)S(1)} %collective-permute-done.9.refs_6_) | copy-start | bytes 1032196
  34.8 9.3 %collective-permute-start.10 = (bf16[192,896]{1,0:T(8,128)(2,1)S(1)}, bf16[192,896]{1,0:T(8,128)(2,1)S(1)}, u32[]{:S(2)}, u32[]{:S(2)}) collective-permute-start(bf16[192,896]{1,0:T(8,128)(2,1)S(1)} %collective-permute-done.9.refs_6_), channel_id=1, source_target_pairs={{0,2},{2,0},{4,6},{6,4},{8,10},{10,8},{12,14},{14,12},{1,3},{3,1},... | collective-permute-start | bytes 1032200 | tf_op jit(solution)/shard_map/ppermute | solution.py:89
  35.8 66.3 %copy-start.12 = (bf16[128,128]{1,0:T(8,128)(2,1)S(1)}, bf16[128,128]{1,0:T(8,128)(2,1)}, u32[]{:S(2)}) copy-start(bf16[128,128]{1,0:T(8,128)(2,1)} %weight_ref.3) | copy-start | bytes 98308
  35.8 13.5 %collective-permute-start.12 = (bf16[192,1280]{1,0:T(8,128)(2,1)S(1)}, bf16[192,1280]{1,0:T(8,128)(2,1)S(1)}, u32[]{:S(2)}, u32[]{:S(2)}) collective-permute-start(bf16[192,1280]{1,0:T(8,128)(2,1)S(1)} %pad_maximum_fusion.refs_0_), channel_id=1, source_target_pairs={{0,4},{2,6},{4,12},{6,14},{12,8},{14,10},{8,0},{10,2},{20,16},{22,... | collective-permute-start | bytes 1474568 | tf_op jit(solution)/shard_map/ppermute | solution.py:86
  36.7 8.4 %copy-start.5 = (bf16[192,896]{1,0:T(8,128)(2,1)}, bf16[192,896]{1,0:T(8,128)(2,1)S(1)}, u32[]{:S(2)}) copy-start(bf16[192,896]{1,0:T(8,128)(2,1)S(1)} %collective-permute-done.7.refs_4_) | copy-start | bytes 1032196
  43.9 1.2 %copy-start.7 = (bf16[192,896]{1,0:T(8,128)(2,1)}, bf16[192,896]{1,0:T(8,128)(2,1)S(1)}, u32[]{:S(2)}) copy-start(bf16[192,896]{1,0:T(8,128)(2,1)S(1)} %collective-permute-done.8.refs_5_) | copy-start | bytes 1032196
  44.1 1.0 copy-start.9
  45.1 7.7 %collective-permute-start.11 = (bf16[8,128,192]{2,1,0:T(8,128)(2,1)S(1)}, bf16[8,128,192]{2,1,0:T(8,128)(2,1)}, u32[]{:S(2)}, u32[]{:S(2)}) collective-permute-start(bf16[8,128,192]{2,1,0:T(8,128)(2,1)S(1)} %embed.1.part_ref), channel_id=1, source_target_pairs={{0,1},{1,0},{2,3},{3,2},{4,5},{5,4},{6,7},{7,6},{8,9},{9,8},{10,11... | collective-permute-start | bytes 1179656 | tf_op jit(solution)/shard_map/ppermute | solution.py:353
  49.3 19.3 %collective-permute-start.13 = (bf16[192,1280]{1,0:T(8,128)(2,1)S(1)}, bf16[192,1280]{1,0:T(8,128)(2,1)S(1)}, u32[]{:S(2)}, u32[]{:S(2)}) collective-permute-start(bf16[192,1280]{1,0:T(8,128)(2,1)S(1)} %collective-permute-done.12.refs_2_), channel_id=1, source_target_pairs={{0,2},{2,0},{4,6},{6,4},{8,10},{10,8},{12,14},{14,12},{1,3},{3,1},... | collective-permute-start | bytes 1474568 | tf_op jit(solution)/shard_map/ppermute | solution.py:89
  50.1 24.5 %collective-permute-start.15 = (bf16[192,1280]{1,0:T(8,128)(2,1)S(1)}, bf16[192,1280]{1,0:T(8,128)(2,1)S(1)}, u32[]{:S(2)}, u32[]{:S(2)}) collective-permute-start(bf16[192,1280]{1,0:T(8,128)(2,1)S(1)} %collective-permute-done.12.refs_2_), channel_id=1, source_target_pairs={{0,16},{16,0},{1,17},{17,1},{2,18},{18,2},{3,19},{19,3},{4,20},{20... | collective-permute-start | bytes 1474568 | tf_op jit(solution)/shard_map/ppermute | solution.py:92
  50.6 24.0 %collective-permute-start.17 = (bf16[192,1280]{1,0:T(8,128)(2,1)S(1)}, bf16[192,1280]{1,0:T(8,128)(2,1)S(1)}, u32[]{:S(2)}, u32[]{:S(2)}) collective-permute-start(bf16[192,1280]{1,0:T(8,128)(2,1)S(1)} %collective-permute-done.12.refs_2_), channel_id=1, source_target_pairs={{0,4},{2,6},{4,12},{6,14},{12,8},{14,10},{8,0},{10,2},{20,16},{22,... | collective-permute-start | bytes 1474568 | tf_op jit(solution)/shard_map/ppermute | solution.py:86
  52.8 1.0 copy-start.4
  53.8 1.0 copy-start.6
  54.8 1.0 copy-start.8
  55.8 1.0 copy-start.10
  56.7 32.7 %copy-start.11 = (bf16[1536,256]{1,0:T(8,128)(2,1)S(1)}, bf16[1536,256]{1,0:T(8,128)(2,1)}, u32[]{:S(2)}) copy-start(bf16[1536,256]{1,0:T(8,128)(2,1)} %weight_ref.2) | copy-start | bytes 2359300
  58.7 4.2 %collective-permute-start.19 = (bf16[192,128]{1,0:T(8,128)(2,1)S(1)}, bf16[192,128]{1,0:T(8,128)(2,1)S(1)}, u32[]{:S(2)}, u32[]{:S(2)}) collective-permute-start(bf16[192,128]{1,0:T(8,128)(2,1)S(1)} %get-tuple-element.21), channel_id=1, source_target_pairs={{0,2},{2,0},{4,6},{6,4},{8,10},{10,8},{12,14},{14,12},{1,3},{3,1},... | collective-permute-start | bytes 147464 | tf_op jit(solution)/shard_map/ppermute | solution.py:369
  62.8 5.8 %collective-permute-start.20 = (bf16[2,192,128]{2,1,0:T(8,128)(2,1)S(1)}, bf16[2,192,128]{2,1,0:T(8,128)(2,1)S(1)}, u32[]{:S(2)}, u32[]{:S(2)}) collective-permute-start(bf16[2,192,128]{2,1,0:T(8,128)(2,1)S(1)} %pad_maximum_fusion.2), channel_id=1, source_target_pairs={{0,4},{2,6},{4,12},{6,14},{12,8},{14,10},{8,0},{10,2},{1,5},{3,7},... | collective-permute-start | bytes 294920 | tf_op jit(solution)/shard_map/ppermute | solution.py:371
  63.3 7.3 %collective-permute-start.21 = (bf16[2,192,128]{2,1,0:T(8,128)(2,1)S(1)}, bf16[2,192,128]{2,1,0:T(8,128)(2,1)S(1)}, u32[]{:S(2)}, u32[]{:S(2)}) collective-permute-start(bf16[2,192,128]{2,1,0:T(8,128)(2,1)S(1)} %pad_maximum_fusion.2), channel_id=1, source_target_pairs={{4,0},{6,2},{12,4},{14,6},{8,12},{10,14},{0,8},{2,10},{5,1},{7,3},... | collective-permute-start | bytes 294920 | tf_op jit(solution)/shard_map/ppermute | solution.py:372
  68.7 5.9 %collective-permute-start.22 = (bf16[2,192,128]{2,1,0:T(8,128)(2,1)S(1)}, bf16[2,192,128]{2,1,0:T(8,128)(2,1)S(1)}, u32[]{:S(2)}, u32[]{:S(2)}) collective-permute-start(bf16[2,192,128]{2,1,0:T(8,128)(2,1)S(1)} %collective-permute-done.20), channel_id=1, source_target_pairs={{0,4},{2,6},{4,12},{6,14},{12,8},{14,10},{8,0},{10,2},{1,5},{3,7},... | collective-permute-start | bytes 294920 | tf_op jit(solution)/shard_map/ppermute | solution.py:373
  68.7 9.3 %collective-permute-start.14 = (bf16[192,1280]{1,0:T(8,128)(2,1)S(1)}, bf16[192,1280]{1,0:T(8,128)(2,1)S(1)}, u32[]{:S(2)}, u32[]{:S(2)}) collective-permute-start(bf16[192,1280]{1,0:T(8,128)(2,1)S(1)} %pad_maximum_fusion.refs_0_), channel_id=1, source_target_pairs={{0,2},{2,0},{4,6},{6,4},{8,10},{10,8},{12,14},{14,12},{1,3},{3,1},... | collective-permute-start | bytes 1474568 | tf_op jit(solution)/shard_map/ppermute | solution.py:89
  70.5 8.8 %collective-permute-start.16 = (bf16[192,1280]{1,0:T(8,128)(2,1)S(1)}, bf16[192,1280]{1,0:T(8,128)(2,1)S(1)}, u32[]{:S(2)}, u32[]{:S(2)}) collective-permute-start(bf16[192,1280]{1,0:T(8,128)(2,1)S(1)} %collective-permute-done.13.refs_3_), channel_id=1, source_target_pairs={{0,16},{16,0},{1,17},{17,1},{2,18},{18,2},{3,19},{19,3},{4,20},{20... | collective-permute-start | bytes 1474568 | tf_op jit(solution)/shard_map/ppermute | solution.py:92
  74.5 10.2 %collective-permute-start.18 = (bf16[192,1280]{1,0:T(8,128)(2,1)S(1)}, bf16[192,1280]{1,0:T(8,128)(2,1)S(1)}, u32[]{:S(2)}, u32[]{:S(2)}) collective-permute-start(bf16[192,1280]{1,0:T(8,128)(2,1)S(1)} %collective-permute-done.13.refs_3_), channel_id=1, source_target_pairs={{0,4},{2,6},{4,12},{6,14},{12,8},{14,10},{8,0},{10,2},{20,16},{22,... | collective-permute-start | bytes 1474568 | tf_op jit(solution)/shard_map/ppermute | solution.py:86
  74.6 10.6 %collective-permute-start.23 = (bf16[8,192,128]{2,1,0:T(8,128)(2,1)S(1)}, bf16[8,192,128]{2,1,0:T(8,128)(2,1)S(1)}, u32[]{:S(2)}, u32[]{:S(2)}) collective-permute-start(bf16[8,192,128]{2,1,0:T(8,128)(2,1)S(1)} %constant_dynamic-update-slice_fusion.own_ref), channel_id=1, source_target_pairs={{0,1},{1,0},{2,3},{3,2},{4,5},{5,4},{6,7},{7,6},{8,9},{9,8},{10,11... | collective-permute-start | bytes 1179656 | tf_op jit(solution)/shard_map/ppermute | solution.py:376
  87.5 2.0 %collective-permute-start.24 = (bf16[8,128,192]{2,1,0:T(8,128)(2,1)S(1)}, bf16[8,128,192]{2,1,0:T(8,128)(2,1)S(1)}, u32[]{:S(2)}, u32[]{:S(2)}) collective-permute-start(bf16[8,128,192]{2,1,0:T(8,128)(2,1)S(1)} %output.1.part_ref), channel_id=1, source_target_pairs={{0,1},{1,0},{2,3},{3,2},{4,5},{5,4},{6,7},{7,6},{8,9},{9,8},{10,11... | collective-permute-start | bytes 1179656 | tf_op jit(solution)/shard_map/ppermute | solution.py:408
  90.7 3.6 %collective-permute-start.25 = (bf16[8,256]{1,0:T(8,128)(2,1)S(1)}, bf16[8,256]{1,0:T(8,128)(2,1)S(1)}, u32[]{:S(2)}, u32[]{:S(2)}) collective-permute-start(bf16[8,256]{1,0:T(8,128)(2,1)S(1)} %get-tuple-element.23.own_ref), channel_id=1, source_target_pairs={{0,2},{2,0},{4,6},{6,4},{8,10},{10,8},{12,14},{14,12},{1,3},{3,1},... | collective-permute-start | bytes 12296 | tf_op jit(solution)/shard_map/ppermute | solution.py:426
  94.4 3.7 %collective-permute-start.26 = (bf16[16,256]{1,0:T(8,128)(2,1)S(1)}, bf16[16,256]{1,0:T(8,128)(2,1)S(1)}, u32[]{:S(2)}, u32[]{:S(2)}) collective-permute-start(bf16[16,256]{1,0:T(8,128)(2,1)S(1)} %pad_maximum_fusion.3), channel_id=1, source_target_pairs={{0,4},{2,6},{4,0},{6,2},{8,12},{10,14},{12,8},{14,10},{1,5},{3,7},... | collective-permute-start | bytes 24584 | tf_op jit(solution)/shard_map/ppermute | solution.py:426
  98.0 4.1 %collective-permute-start.27 = (bf16[32,256]{1,0:T(8,128)(2,1)S(1)}, bf16[32,256]{1,0:T(8,128)(2,1)S(1)}, u32[]{:S(2)}, u32[]{:S(2)}) collective-permute-start(bf16[32,256]{1,0:T(8,128)(2,1)S(1)} %constant_dynamic-update-slice_fusion.5), channel_id=1, source_target_pairs={{0,8},{2,10},{4,12},{6,14},{9,1},{11,3},{13,5},{15,7},{16,24},{18,... | collective-permute-start | bytes 49160 | tf_op jit(solution)/shard_map/ppermute | solution.py:428

commit v7 on v6

--- a/solution.py
+++ b/solution.py
@@ -111,7 +111,7 @@
     return jnp.where((gap >= 0) & (gap < POOL), 1.0 / POOL, 0.0).astype(BF16)
 
 
-def act_kernel(taps, own_ref, other_ref, gain_ref, out_ref, act, gaincol):
+def act_kernel(taps, own_ref, other_ref, gain_ref, out_ref, residual_ref, act, gaincol):
     channels, positions = act.shape
     half = own_ref.shape[0]
     col = lax.axis_index("col")
@@ -131,21 +131,24 @@
             at = pl.multiple_of(index * half + j * step, step)
             x = ref[j * step:(j + 1) * step, :].astype(F32) * scale
             act[pl.ds(at, step), :] = gelu(x * gaincol[pl.ds(at, step), :1]).astype(BF16)
-    rows = out_ref.shape[0]
-    out_ref[...] = dot_nt(window_means(0, rows, rows // taps, taps, positions, positions), act[...]).astype(BF16)
-
-
-def conv_kernel(windows_ref, own_ref, halo_ref, gain_ref, weight_hbm, out_ref, weights, sems):
+    rows, tokens = out_ref.shape[0], residual_ref.shape[0]
+    means = window_means(0, rows, tokens, taps, positions, positions)
+    out_ref[...] = dot_nt(means, act[...]).astype(BF16)
+    middle = (taps // 2) * tokens
+    residual_ref[...] = dot_nt(means[middle:middle + tokens], own_ref[...])
+
+
+def conv_kernel(positions, windows_ref, residual_ref, halo_ref, gain_ref, weight_hbm, out_ref, weights, sems):
     taps, _, channels = weights.shape
     copies = [pltpu.make_async_copy(weight_hbm.at[t], weights.at[t], sems.at[t]) for t in range(taps)]
     ahead = 2
     for c in copies[:ahead]:
         c.start()
-    tokens, positions = out_ref.shape[0], own_ref.shape[1]
+    tokens = out_ref.shape[0]
     h = halo_ref[...].astype(F32)
     h = h * lax.rsqrt(jnp.sum(h * h, axis=1, keepdims=True) / channels + EPS) * gain_ref[...]
     h = gelu(h).astype(BF16)
-    total = dot_nt(window_means((taps // 2) * tokens, tokens, tokens, taps, positions, positions), own_ref[...])
+    total = residual_ref[...]
     for t in range(taps):
         window = windows_ref[t * tokens:(t + 1) * tokens]
         if t != taps // 2:
@@ -163,14 +166,14 @@
 
 
 def embed_kernel(pieces, pooled_ref, *refs):
-    blocks, out_ref = refs[:pieces], refs[pieces]
+    blocks, (out_ref, rest_ref) = refs[:pieces], refs[pieces:]
     half = pooled_ref.shape[1]
     for ref, owner in zip(blocks, block_owners()):
         out_ref[owner] = dot_nt(pooled_ref[...], ref[:, :half]).astype(BF16)
-
-
-def keyvalue_kernel(pieces, half, part_ref, other_ref, gain_ref, *refs):
-    blocks, (kv_ref, normed_ref, embedded_ref) = refs[:pieces], refs[pieces:]
+        rest_ref[owner] = ref[:, half:]
+
+
+def keyvalue_kernel(part_ref, other_ref, gain_ref, weight_ref, kv_ref, normed_ref, embedded_ref):
     count, _, width = part_ref.shape
     e = (part_ref[...].astype(F32) + other_ref[...].astype(F32)).astype(BF16)
     embedded_ref[...] = e
@@ -179,8 +182,8 @@
     scale = lax.rsqrt(squares / (count * width) + EPS)
     normed_ref[...] = (e * scale[None] * gain_ref[...]).astype(BF16)
     total = 0.0
-    for ref, owner in zip(blocks, block_owners()):
-        total = total + dot_nn(normed_ref[owner], ref[:, half:])
+    for s in range(count):
+        total = total + dot_nn(normed_ref[s], weight_ref[s])
     kv = total.T.astype(BF16)
     kv_ref[...] = kv
 
@@ -208,28 +211,32 @@
         out_ref[h] = (dot_nt(weights.astype(BF16), values[...]) / total).astype(BF16)
 
 
-def output_kernel(pieces, features, attended_ref, *refs):
-    blocks, out_ref = refs[:pieces], refs[pieces]
+def output_kernel(pieces, features, attended_ref, embedded_ref, pair_weight_ref, *refs):
+    blocks, (out_ref, pair_ref) = refs[:pieces], refs[pieces:]
     heads = attended_ref.shape[0]
     flat = jnp.concatenate([attended_ref[h] for h in range(heads)], axis=1)
+    _, rows, width = out_ref.shape
+    share = jnp.where(lax.axis_index("col") == 0, 1.0, 0.0)
+    projected = 0.0
     for ref, owner in zip(blocks, block_owners()):
-        out_ref[owner] = dot_nt(flat, ref[:, features:]).astype(BF16)
-
-
-def token_kernel(embedded_ref, part_ref, other_ref, weight_ref, token_ref, send_ref, whole):
+        part = dot_nt(flat, ref[:, features:])
+        out_ref[owner] = part.astype(BF16)
+        part = part + share * embedded_ref[owner].astype(F32)
+        pooled = jnp.mean(part.reshape(rows // PAIR_POOL, PAIR_POOL, width), axis=1).astype(BF16)
+        weight = pair_weight_ref[pl.ds(pl.multiple_of(owner * width, width), width)]
+        projected = projected + dot_nn(pooled, weight)
+    pair_ref[...] = projected.astype(BF16)
+
+
+def token_kernel(embedded_ref, part_ref, other_ref, token_ref):
     col = lax.axis_index("col")
-    count, rows, width = part_ref.shape
-    projected = None
-    for s in range(count):
-        tokens = (embedded_ref[s].astype(F32) + (part_ref[s].astype(F32) + other_ref[s].astype(F32))).astype(BF16)
-        whole[s] = tokens
-        pooled = jnp.mean(tokens.astype(F32).reshape(rows // PAIR_POOL, PAIR_POOL, width), axis=1).astype(BF16)
-        part = dot_nn(pooled, weight_ref[s * width:(s + 1) * width])
-        projected = part if projected is None else projected + part
     own = token_ref.shape[0]
     mine = pl.ds(pl.multiple_of(col * own, own), own)
-    token_ref[...] = jnp.concatenate([whole[s, mine] for s in range(count)], axis=1)
-    send_ref[...] = projected.astype(BF16)
+    blocks = [
+        embedded_ref[s, mine].astype(F32) + (part_ref[s, mine].astype(F32) + other_ref[s, mine].astype(F32))
+        for s in range(part_ref.shape[0])
+    ]
+    token_ref[...] = jnp.concatenate(blocks, axis=1).astype(BF16)
 
 
 def pair_kernel(own_ref, all_ref, weight_ref, out_ref, columns_here):
@@ -295,11 +302,11 @@
         col == 0, jnp.concatenate([own_halo, other_halo], axis=1), jnp.concatenate([other_halo, own_halo], axis=1)
     )
     gain_row = conv_gain.reshape(1, channels)
-    windows = pl.pallas_call(
+    windows, residual = pl.pallas_call(
         functools.partial(act_kernel, taps),
-        out_shape=shape((taps * tokens, channels), BF16),
+        out_shape=(shape((taps * tokens, channels), BF16), shape((tokens, half), F32)),
         in_specs=vspec(3),
-        out_specs=pl.BlockSpec(memory_space=VMEM),
+        out_specs=vspec(2),
         scratch_shapes=[pltpu.VMEM((channels, positions), BF16), pltpu.VMEM((channels, 8), F32)],
         compiler_params=params(20),
         cost_estimate=cost(2 * taps * tokens * channels * positions, 4 * channels * positions),
@@ -311,7 +318,7 @@
         e.across("step", "step2")
         e.between("step", "cross")
     pooled = pl.pallas_call(
-        conv_kernel,
+        functools.partial(conv_kernel, positions),
         out_shape=shape((tokens, half), BF16),
         in_specs=vspec(4) + hspec(1),
         out_specs=pl.BlockSpec(memory_space=VMEM),
@@ -319,21 +326,20 @@
         compiler_params=params(50),
         cost_estimate=cost(2 * taps * tokens * channels * half, 2 * taps * channels * half),
         name="conv",
-    )(windows, signal_t, halo, gain_row, conv_weight.transpose(0, 2, 1))
-    if ring:
-        e.at["far"] = after(e.at["far"], pooled)
-        e.at["step2"] = after(e.at["step2"], pooled)
+    )(windows, residual, halo, gain_row, conv_weight.transpose(0, 2, 1))
+    if ring:
+        e.at["far"] = after(e.at["far"], pooled, e.at["cross"])
+        e.at["step2"] = after(e.at["step2"], pooled, e.at["cross"])
         e.across("far", "far2")
         e.between("step2", "cross2")
         q.at["own"] = after(q.at["own"], pooled, e.at["far"])
         q.along("own", "step")
+        q.across("own", "own2")
         q.at["step"] = after(q.at["step"], e.at["far2"], e.at["cross2"])
         q.along("step", "far")
         q.across("step", "step2")
         q.between("step", "cross")
-        q.at["own"] = after(q.at["own"], q.at["step2"])
-        q.along("step2", "far2")
-        q.across("own", "own2")
+        q.across("far", "far2")
         q.between("step2", "cross2")
         embed_blocks, later_blocks = e.pieces(), q.pieces()
     else:
@@ -341,32 +347,35 @@
     pieces = len(embed_blocks)
     block = width // pieces
 
-    part = pl.pallas_call(
+    part, keyvalue_blocks = pl.pallas_call(
         functools.partial(embed_kernel, pieces),
-        out_shape=shape((pieces, tokens, block), BF16),
+        out_shape=(shape((pieces, tokens, block), BF16), shape((pieces, block, DV), BF16)),
         in_specs=vspec(1 + pieces),
-        out_specs=pl.BlockSpec(memory_space=VMEM),
+        out_specs=vspec(2),
         compiler_params=params(12),
         cost_estimate=cost(2 * tokens * half * width, 2 * half * width),
         name="embed",
     )(pooled, *embed_blocks)
     other_part = lax.ppermute(part, "col", swap)
+    if ring:
+        other_part = after(other_part, q.at["own2"])
 
     keyvalue, normed, embedded = pl.pallas_call(
-        functools.partial(keyvalue_kernel, pieces, half),
+        keyvalue_kernel,
         out_shape=(
             shape((DV, tokens), BF16),
             shape((pieces, tokens, block), BF16),
             shape((pieces, tokens, block), BF16),
         ),
-        in_specs=vspec(3 + pieces),
+        in_specs=vspec(4),
         out_specs=vspec(3),
         compiler_params=params(16),
         cost_estimate=cost(2 * tokens * width * DV, 2 * width * DV),
         name="keyvalue",
-    )(part, other_part, attn_gain.reshape(pieces, 1, block), *embed_blocks)
+    )(part, other_part, attn_gain.reshape(pieces, 1, block), keyvalue_blocks)
     if ring:
         here = jnp.stack([keyvalue, lax.ppermute(keyvalue, "seq", [(i, i ^ 1) for i in range(count)])])
+        here = after(here, q.at["far"], q.at["step2"], q.at["cross"])
         onward = [(2 * RING[k] + i, 2 * RING[(k + 1) % 4] + i) for k in range(4) for i in range(2)]
         ahead = lax.ppermute(here, "seq", onward)
         back = lax.ppermute(here, "seq", [(j, i) for i, j in onward])
@@ -396,29 +405,29 @@
         name="attend",
     )(queries, gathered, gathered_other)
 
-    part_out = pl.pallas_call(
+    out_width = rowcol_weight.shape[1]
+    own_rows, pair_rows = tokens // cols, tokens // PAIR_POOL
+    part_out, part_pair = pl.pallas_call(
         functools.partial(output_kernel, pieces, features),
-        out_shape=shape((pieces, tokens, block), BF16),
-        in_specs=vspec(1 + pieces),
-        out_specs=pl.BlockSpec(memory_space=VMEM),
+        out_shape=(shape((pieces, tokens, block), BF16), shape((pair_rows, out_width), BF16)),
+        in_specs=vspec(3 + pieces),
+        out_specs=vspec(2),
         compiler_params=params(16),
         cost_estimate=cost(2 * tokens * heads * DV * width, 2 * heads * DV * width),
         name="output",
-    )(attended, *later_blocks)
+    )(attended, embedded, rowcol_weight, *later_blocks)
+    other_pair = lax.ppermute(part_pair, "col", swap)
     other_out = lax.ppermute(part_out, "col", swap)
-
-    out_width = rowcol_weight.shape[1]
-    own_rows, pair_rows = tokens // cols, tokens // PAIR_POOL
-    out_tokens, projected = pl.pallas_call(
+    projected = (part_pair.astype(F32) + other_pair.astype(F32)).astype(BF16)
+    out_tokens = pl.pallas_call(
         token_kernel,
-        out_shape=(shape((own_rows, width), BF16), shape((pair_rows, out_width), BF16)),
-        in_specs=vspec(4),
-        out_specs=vspec(2),
-        scratch_shapes=[pltpu.VMEM((pieces, tokens, block), BF16)],
+        out_shape=shape((own_rows, width), BF16),
+        in_specs=vspec(3),
+        out_specs=pl.BlockSpec(memory_space=VMEM),
         compiler_params=params(12),
-        cost_estimate=cost(2 * pair_rows * width * out_width, 2 * width * out_width),
+        cost_estimate=cost(3 * own_rows * width, 8 * own_rows * width),
         name="tokens",
-    )(embedded, part_out, other_out, rowcol_weight)
+    )(embedded, part_out, other_out)
 
     if ring:
         rows_all = projected

time: 105 us -> 107 us (1.019)
  Pallas kernels: 16.8 us -> 21.4 us
  waiting for transfers between devices: 39.9 us -> 37.6 us
    ppermute x5 -> x4, waiting for transfers between devices: 9.42 us -> 2.37 us  [along(): self.at[target] = lax.ppermute(self.at[source], ('grp', 'seq'), pairs)]
    ppermute x5 -> x6, waiting for transfers between devices: 3.6 us -> 8.13 us  [across(): lax.ppermute(self.at[source], 'seq', [(i, i ^ 1) for i in range(self.coun...]
    ppermute x5 -> x4, starting transfers between devices: 7.15 us -> 4.85 us  [along(): self.at[target] = lax.ppermute(self.at[source], ('grp', 'seq'), pairs)]
    pallas_call x1, Pallas kernels: 0.92 us -> 3.2 us  [on_device(): pl.pallas_call(functools.partial(output_kernel, pieces, features), out_sh...]
    ppermute x1, waiting for transfers between devices: 1.9 us -> 0.01 us  [on_device(): other_out = lax.ppermute(part_out, 'col', swap)]
    ppermute x5 -> x6, starting transfers between devices: 8.52 us -> 10.4 us  [across(): lax.ppermute(self.at[source], 'seq', [(i, i ^ 1) for i in range(self.coun...]
    ppermute x1, waiting for transfers between devices: 3.45 us -> 5.19 us  [on_device(): lax.ppermute(ahead, 'seq', onward)]
    ppermute x1, waiting for transfers between devices: 2.83 us -> 1.11 us  [on_device(): ahead = lax.ppermute(here, 'seq', onward)]
  transfers between devices with their start and end apart: 28 -> 29, of which waited for: 14 -> 15; matrix products, arithmetic and copies ran while one was open for 4% -> 3% of each run, Pallas kernels for 12% -> 14%
where the time goes in v7:
time: 107 us; the launch traced here: 106 us
  waiting for transfers between devices  37.6 us (35%)
  starting transfers between devices  34.5 us (32%)
  Pallas kernels  21.4 us (20%)
  local copies, waits for them, and re-layouts  10.4 us (10%)
  other arithmetic  1.23 us (1%)
    ppermute x6, starting transfers between devices, across(): lax.ppermute(self.at[source], 'seq', [(i, i ^ 1) for i in range(self.coun...  10.4 us
    ppermute x4, waiting for transfers between devices, between(): self.at[target] = lax.ppermute(self.at[source], 'grp', [(0, 1), (1, 0)])  8.88 us
    ppermute x6, waiting for transfers between devices, across(): lax.ppermute(self.at[source], 'seq', [(i, i ^ 1) for i in range(self.coun...  8.13 us
    unnamed x23, local copies, waits for them, and re-layouts  6.39 us
    pallas_call x1, Pallas kernels, on_device(): pl.pallas_call(functools.partial(conv_kernel, positions), out_shape=shape...  6.14 us
    ppermute x2, waiting for transfers between devices, on_device(): lax.ppermute(rows_all, 'seq', [(i, i ^ bit) for i in range(count)])  5.67 us
    ppermute x1, waiting for transfers between devices, on_device(): lax.ppermute(ahead, 'seq', onward)  5.19 us
    ppermute x4, starting transfers between devices, along(): self.at[target] = lax.ppermute(self.at[source], ('grp', 'seq'), pairs)  4.85 us
  transfers between devices with their start and end apart: 29, of which 15 were waited for; matrix products, arithmetic and copies ran while one was open for 3% of the time, Pallas kernels for 14%

profile of v7, /device:TPU:0, one launch (start us, length us, event | category | flops | bytes accessed | tf_op | source)
XLA Modules:
  0.0 105.9 jit_solution(9803810619263923972)
XLA Ops:
  0.7 1.1 %constant_dynamic-slice_fusion.1 = bf16[192,192]{1,0:T(8,128)(2,1)S(1)} fusion(bf16[192,320]{1,0:T(8,128)(2,1)} %param.16, s32[]{:T(128)S(6)} %select_n.32), kind=kLoop, calls=%fused_computation.18 | loop fusion | bytes 147460 | tf_op jit(solution)/shard_map/dynamic_slice | solution.py:279
  1.7 1.1 %pad_maximum_fusion.1.refs_0_ = bf16[192,896]{1,0:T(8,128)(2,1)S(1)} fusion(bf16[192,192]{1,0:T(8,128)(2,1)S(1)} %constant_dynamic-slice_fusion.1, bf16[192,704]{1,0:T(8,128)(2,1)} %bitcast.11), kind=kLoop, calls=%fused_computation.1 | loop fusion | flops 688128 | bytes 688128 | tf_op jit(solution)/shard_map/concatenate | solution.py:278
  2.8 3.0 %collective-permute-start.4 = (bf16[192,896]{1,0:T(8,128)(2,1)S(1)}, bf16[192,896]{1,0:T(8,128)(2,1)S(1)}, u32[]{:S(2)}, u32[]{:S(2)}) collective-permute-start(bf16[192,896]{1,0:T(8,128)(2,1)S(1)} %pad_maximum_fusion.1.refs_0_), channel_id=1, source_target_pairs={{0,2},{2,0},{4,6},{6,4},{8,10},{10,8},{12,14},{14,12},{1,3},{3,1},... | collective-permute-start | bytes 1032200 | tf_op jit(solution)/shard_map/ppermute | solution.py:89
  5.8 1.6 %collective-permute-start.5 = (bf16[192,896]{1,0:T(8,128)(2,1)S(1)}, bf16[192,896]{1,0:T(8,128)(2,1)S(1)}, u32[]{:S(2)}, u32[]{:S(2)}) collective-permute-start(bf16[192,896]{1,0:T(8,128)(2,1)S(1)} %pad_maximum_fusion.1.refs_0_), channel_id=1, source_target_pairs={{0,4},{2,6},{4,12},{6,14},{12,8},{14,10},{8,0},{10,2},{20,16},{22,... | collective-permute-start | bytes 1032200 | tf_op jit(solution)/shard_map/ppermute | solution.py:86
  7.4 1.1 %fusion.3 = (bf16[2,704]{0,1:T(8,128)(2,1)S(1)}, bf16[2,704]{0,1:T(8,128)(2,1)S(1)}) fusion(bf16[512,704]{0,1:T(8,128)(2,1)} %param.10), kind=kLoop, calls=%fused_computation.19 | loop fusion | bytes 11264 | tf_op jit(solution)/shard_map/slice | solution.py:297
  8.6 1.3 %collective-permute-start.2 = (bf16[2,704]{1,0:T(2,128)(2,1)S(1)}, bf16[2,704]{1,0:T(2,128)(2,1)S(1)}, u32[]{:S(2)}, u32[]{:S(2)}) collective-permute-start(bf16[2,704]{1,0:T(2,128)(2,1)S(1)} %copy.15), channel_id=1, source_target_pairs={{2,0},{4,2},{6,4},{8,6},{10,8},{12,10},{14,12},{3,1},{5,3},{7,5},{... | collective-permute-start | bytes 8456 | tf_op jit(solution)/shard_map/ppermute | solution.py:298
  10.1 4.6 %collective-permute-start.1 = (bf16[2,704]{1,0:T(2,128)(2,1)S(1)}, bf16[2,704]{1,0:T(2,128)(2,1)S(1)}, u32[]{:S(2)}, u32[]{:S(2)}) collective-permute-start(bf16[2,704]{1,0:T(2,128)(2,1)S(1)} %copy.14), channel_id=1, source_target_pairs={{0,2},{2,4},{4,6},{6,8},{8,10},{10,12},{12,14},{1,3},{3,5},{5,7},{... | collective-permute-start | bytes 8456 | tf_op jit(solution)/shard_map/ppermute | solution.py:297
  14.7 0.9 constant_dynamic-slice_fusion
  16.5 1.1 %copy-done.6 = bf16[512,704]{0,1:T(8,128)(2,1)S(1)} copy-done((bf16[512,704]{0,1:T(8,128)(2,1)S(1)}, bf16[512,704]{0,1:T(8,128)(2,1)}, u32[]{:S(2)}) %copy-start.6) | copy-done | bytes 720920
  17.6 2.9 %act.1 = (bf16[640,1408]{1,0:T(8,128)(2,1)S(1)}, f32[128,704]{1,0:T(8,128)S(1)}) custom-call(bf16[704,512]{1,0:T(8,128)(2,1)S(1)} %bitcast.8, bf16[704,512]{1,0:T(8,128)(2,1)S(1)} %collective-permute-done.other_ref, f32[1,1408]{1,0:T(1,128)S(1)} %reshape.10.gain_ref), custom_call_target="tpu_custom_call" | custom-call | flops 922746880 | bytes 2883584 | tf_op jit(solution)/shard_map/act/pallas_call | solution.py:305
  20.5 2.3 %collective-permute-start.6 = (bf16[192,896]{1,0:T(8,128)(2,1)S(1)}, bf16[192,896]{1,0:T(8,128)(2,1)S(1)}, u32[]{:S(2)}, u32[]{:S(2)}) collective-permute-start(bf16[192,896]{1,0:T(8,128)(2,1)S(1)} %collective-permute-done.5.refs_2_), channel_id=1, source_target_pairs={{0,2},{2,0},{4,6},{6,4},{8,10},{10,8},{12,14},{14,12},{1,3},{3,1},... | collective-permute-start | bytes 1032200 | tf_op jit(solution)/shard_map/ppermute | solution.py:89
  22.8 2.1 %collective-permute-start.7 = (bf16[192,896]{1,0:T(8,128)(2,1)S(1)}, bf16[192,896]{1,0:T(8,128)(2,1)S(1)}, u32[]{:S(2)}, u32[]{:S(2)}) collective-permute-start(bf16[192,896]{1,0:T(8,128)(2,1)S(1)} %collective-permute-done.5.refs_2_), channel_id=1, source_target_pairs={{0,16},{16,0},{1,17},{17,1},{2,18},{18,2},{3,19},{19,3},{4,20},{20... | collective-permute-start | bytes 1032200 | tf_op jit(solution)/shard_map/ppermute | solution.py:92
  24.9 0.9 collective-permute-start.9
  25.9 6.1 %conv.1.pooled_ref = bf16[128,704]{1,0:T(8,128)(2,1)S(1)} custom-call(bf16[640,1408]{1,0:T(8,128)(2,1)S(1)} %get-tuple-element.18.windows_ref, f32[128,704]{1,0:T(8,128)S(1)} %get-tuple-element.19.residual_ref, bf16[16,1408]{1,0:T(8,128)(2,1)S(1)} %maximum_select_fusion.halo_ref, f32[1,1408]{1,0:T(1,128)S(1)} %reshape.10.gain_ref, bf16[5,704,1408]{2,1,0:T(8,128)(2,1)} %bitcast.10), custom_call_target="tpu_custom_call" | custom-call | flops 1268776960 | bytes 9912320 | tf_op jit(solution)/shard_map/conv/pallas_call | solution.py:320
  32.1 1.3 %collective-permute-done.7.refs_4_ = bf16[192,896]{1,0:T(8,128)(2,1)S(1)} collective-permute-done((bf16[192,896]{1,0:T(8,128)(2,1)S(1)}, bf16[192,896]{1,0:T(8,128)(2,1)S(1)}, u32[]{:S(2)}, u32[]{:S(2)}) %collective-permute-start.7) | collective-permute-done | bytes 344096 | tf_op jit(solution)/shard_map/ppermute | solution.py:92
  33.3 2.4 %collective-permute-done.9.refs_6_ = bf16[192,896]{1,0:T(8,128)(2,1)S(1)} collective-permute-done((bf16[192,896]{1,0:T(8,128)(2,1)S(1)}, bf16[192,896]{1,0:T(8,128)(2,1)S(1)}, u32[]{:S(2)}, u32[]{:S(2)}) %collective-permute-start.9) | collective-permute-done | bytes 344096 | tf_op jit(solution)/shard_map/ppermute | solution.py:86
  36.0 2.5 %collective-permute-start.8 = (bf16[192,896]{1,0:T(8,128)(2,1)S(1)}, bf16[192,896]{1,0:T(8,128)(2,1)S(1)}, u32[]{:S(2)}, u32[]{:S(2)}) collective-permute-start(bf16[192,896]{1,0:T(8,128)(2,1)S(1)} %collective-permute-done.6.refs_3_), channel_id=1, source_target_pairs={{0,16},{16,0},{1,17},{17,1},{2,18},{18,2},{3,19},{19,3},{4,20},{20... | collective-permute-start | bytes 1032200 | tf_op jit(solution)/shard_map/ppermute | solution.py:92
  38.4 1.7 %collective-permute-start.10 = (bf16[192,896]{1,0:T(8,128)(2,1)S(1)}, bf16[192,896]{1,0:T(8,128)(2,1)S(1)}, u32[]{:S(2)}, u32[]{:S(2)}) collective-permute-start(bf16[192,896]{1,0:T(8,128)(2,1)S(1)} %collective-permute-done.9.refs_6_), channel_id=1, source_target_pairs={{0,2},{2,0},{4,6},{6,4},{8,10},{10,8},{12,14},{14,12},{1,3},{3,1},... | collective-permute-start | bytes 1032200 | tf_op jit(solution)/shard_map/ppermute | solution.py:89
  40.5 5.3 %collective-permute-done.8.refs_5_ = bf16[192,896]{1,0:T(8,128)(2,1)S(1)} collective-permute-done((bf16[192,896]{1,0:T(8,128)(2,1)S(1)}, bf16[192,896]{1,0:T(8,128)(2,1)S(1)}, u32[]{:S(2)}, u32[]{:S(2)}) %collective-permute-start.8) | collective-permute-done | bytes 344096 | tf_op jit(solution)/shard_map/ppermute | solution.py:92
  45.8 3.7 %collective-permute-done.10.refs_7_ = bf16[192,896]{1,0:T(8,128)(2,1)S(1)} collective-permute-done((bf16[192,896]{1,0:T(8,128)(2,1)S(1)}, bf16[192,896]{1,0:T(8,128)(2,1)S(1)}, u32[]{:S(2)}, u32[]{:S(2)}) %collective-permute-start.10) | collective-permute-done | bytes 344096 | tf_op jit(solution)/shard_map/ppermute | solution.py:89
  49.4 1.8 %embed.1 = (bf16[8,128,192]{2,1,0:T(8,128)(2,1)}, bf16[8,192,192]{2,1,0:T(8,128)(2,1)S(1)}) custom-call(bf16[128,704]{1,0:T(8,128)(2,1)S(1)} %conv.1.pooled_ref, bf16[192,896]{1,0:T(8,128)(2,1)S(1)} %pad_maximum_fusion.1.refs_0_, bf16[192,896]{1,0:T(8,128)(2,1)S(1)} %collective-permute-done.4.refs_1_, bf16[192,896]{1,0:T(8,128)(2,1)S(1)} %collective-permute-done.5.refs_2_, ...), custom_call_target="tpu_custom_call" | custom-call | flops 276824064 | bytes 2162688 | tf_op jit(solution)/shard_map/embed/pallas_call | solution.py:350
  51.2 0.9 copy-done.1
  52.1 1.7 %collective-permute-start.14 = (bf16[192,1280]{1,0:T(8,128)(2,1)S(1)}, bf16[192,1280]{1,0:T(8,128)(2,1)S(1)}, u32[]{:S(2)}, u32[]{:S(2)}) collective-permute-start(bf16[192,1280]{1,0:T(8,128)(2,1)S(1)} %collective-permute-done.13.refs_2_), channel_id=1, source_target_pairs={{0,2},{2,0},{4,6},{6,4},{8,10},{10,8},{12,14},{14,12},{1,3},{3,1},... | collective-permute-start | bytes 1474568 | tf_op jit(solution)/shard_map/ppermute | solution.py:89
  53.8 2.1 %collective-permute-start.17 = (bf16[192,1280]{1,0:T(8,128)(2,1)S(1)}, bf16[192,1280]{1,0:T(8,128)(2,1)}, u32[]{:S(2)}, u32[]{:S(2)}) collective-permute-start(bf16[192,1280]{1,0:T(8,128)(2,1)S(1)} %collective-permute-done.13.refs_2_), channel_id=1, source_target_pairs={{0,4},{2,6},{4,12},{6,14},{12,8},{14,10},{8,0},{10,2},{20,16},{22,... | collective-permute-start | bytes 1474568 | tf_op jit(solution)/shard_map/ppermute | solution.py:86
  56.0 4.0 %collective-permute-done.12.refs_1_ = bf16[192,1280]{1,0:T(8,128)(2,1)S(1)} collective-permute-done((bf16[192,1280]{1,0:T(8,128)(2,1)S(1)}, bf16[192,1280]{1,0:T(8,128)(2,1)S(1)}, u32[]{:S(2)}, u32[]{:S(2)}) %collective-permute-start.12) | collective-permute-done | bytes 491552 | tf_op jit(solution)/shard_map/ppermute | solution.py:89
  60.0 0.8 copy-done.4
  60.8 1.1 %copy-done.2 = bf16[8,192,192]{2,1,0:T(8,128)(2,1)S(1)} copy-done((bf16[8,192,192]{2,1,0:T(8,128)(2,1)S(1)}, bf16[8,192,192]{2,1,0:T(8,128)(2,1)}, u32[]{:S(2)}) %copy-start.2) | copy-done | bytes 589848
  61.9 1.0 copy-done.5
  63.0 1.7 %keyvalue.1 = (bf16[192,128]{1,0:T(8,128)(2,1)S(1)}, bf16[8,128,192]{2,1,0:T(8,128)(2,1)S(1)}, bf16[8,128,192]{2,1,0:T(8,128)(2,1)S(1)}) custom-call(bf16[8,128,192]{2,1,0:T(8,128)(2,1)} %get-tuple-element.23.part_ref, bf16[8,128,192]{2,1,0:T(8,128)(2,1)S(1)} %copy-done.5, f32[8,1,192]{2,1,0:T(1,128)S(1)} %reshape.11.gain_ref, bf16[8,192,192]{2,1,0:T(8,128)(2,1)S(1)} %copy-done.2), custom_call_target="tpu_custom_call" | custom-call | flops 75497472 | bytes 589824 | tf_op jit(solution)/shard_map/keyvalue/pallas_call | solution.py:363
  64.6 1.4 %collective-permute-start.19 = (bf16[192,128]{1,0:T(8,128)(2,1)S(1)}, bf16[192,128]{1,0:T(8,128)(2,1)S(1)}, u32[]{:S(2)}, u32[]{:S(2)}) collective-permute-start(bf16[192,128]{1,0:T(8,128)(2,1)S(1)} %get-tuple-element.30), channel_id=1, source_target_pairs={{0,2},{2,0},{4,6},{6,4},{8,10},{10,8},{12,14},{14,12},{1,3},{3,1},... | collective-permute-start | bytes 147464 | tf_op jit(solution)/shard_map/ppermute | solution.py:377
  66.0 3.3 %collective-permute-done.19 = bf16[192,128]{1,0:T(8,128)(2,1)S(1)} collective-permute-done((bf16[192,128]{1,0:T(8,128)(2,1)S(1)}, bf16[192,128]{1,0:T(8,128)(2,1)S(1)}, u32[]{:S(2)}, u32[]{:S(2)}) %collective-permute-start.19) | collective-permute-done | bytes 49184 | tf_op jit(solution)/shard_map/ppermute | solution.py:377
  69.8 2.6 %collective-permute-start.21 = (bf16[2,192,128]{2,1,0:T(8,128)(2,1)S(1)}, bf16[2,192,128]{2,1,0:T(8,128)(2,1)S(1)}, u32[]{:S(2)}, u32[]{:S(2)}) collective-permute-start(bf16[2,192,128]{2,1,0:T(8,128)(2,1)S(1)} %pad_maximum_fusion.2), channel_id=1, source_target_pairs={{4,0},{6,2},{12,4},{14,6},{8,12},{10,14},{0,8},{2,10},{5,1},{7,3},... | collective-permute-start | bytes 294920 | tf_op jit(solution)/shard_map/ppermute | solution.py:381
  72.7 1.3 %collective-permute-start.18 = (bf16[192,1280]{1,0:T(8,128)(2,1)}, bf16[192,1280]{1,0:T(8,128)(2,1)S(1)}, u32[]{:S(2)}, u32[]{:S(2)}) collective-permute-start(bf16[192,1280]{1,0:T(8,128)(2,1)} %collective-permute-done.17.refs_6_), channel_id=1, source_target_pairs={{0,2},{2,0},{4,6},{6,4},{8,10},{10,8},{12,14},{14,12},{1,3},{3,1},... | collective-permute-start | bytes 1474568 | tf_op jit(solution)/shard_map/ppermute | solution.py:89
  74.0 1.1 %collective-permute-done.20 = bf16[2,192,128]{2,1,0:T(8,128)(2,1)S(1)} collective-permute-done((bf16[2,192,128]{2,1,0:T(8,128)(2,1)S(1)}, bf16[2,192,128]{2,1,0:T(8,128)(2,1)S(1)}, u32[]{:S(2)}, u32[]{:S(2)}) %collective-permute-start.20) | collective-permute-done | bytes 98336 | tf_op jit(solution)/shard_map/ppermute | solution.py:380
  75.5 5.2 %collective-permute-done.22 = bf16[2,192,128]{2,1,0:T(8,128)(2,1)S(1)} collective-permute-done((bf16[2,192,128]{2,1,0:T(8,128)(2,1)S(1)}, bf16[2,192,128]{2,1,0:T(8,128)(2,1)S(1)}, u32[]{:S(2)}, u32[]{:S(2)}) %collective-permute-start.22) | collective-permute-done | bytes 98336 | tf_op jit(solution)/shard_map/ppermute | solution.py:382
  80.8 2.3 %collective-permute-done.16.refs_5_ = bf16[192,1280]{1,0:T(8,128)(2,1)S(1)} collective-permute-done((bf16[192,1280]{1,0:T(8,128)(2,1)S(1)}, bf16[192,1280]{1,0:T(8,128)(2,1)S(1)}, u32[]{:S(2)}, u32[]{:S(2)}) %collective-permute-start.16) | collective-permute-done | bytes 491552 | tf_op jit(solution)/shard_map/ppermute | solution.py:92
  83.5 1.6 %query.1.query_ref = bf16[128,512]{1,0:T(8,128)(2,1)S(1)} custom-call(bf16[8,128,192]{2,1,0:T(8,128)(2,1)S(1)} %get-tuple-element.28.normed_ref, bf16[192,1280]{1,0:T(8,128)(2,1)S(1)} %pad_maximum_fusion.refs_0_, bf16[192,1280]{1,0:T(8,128)(2,1)S(1)} %collective-permute-done.12.refs_1_, bf16[192,1280]{1,0:T(8,128)(2,1)S(1)} %collective-permute-done.13.refs_2_, ...), custom_call_target="tpu_custom_call" | custom-call | flops 201326592 | bytes 1572864 | tf_op jit(solution)/shard_map/query/pallas_call | solution.py:387
  85.2 1.4 %attend.1.attended_ref = bf16[4,128,192]{2,1,0:T(8,128)(2,1)S(1)} custom-call(bf16[128,512]{1,0:T(8,128)(2,1)S(1)} %query.1.query_ref, bf16[8,192,128]{2,1,0:T(8,128)(2,1)S(1)} %constant_dynamic-update-slice_fusion.own_ref, bf16[8,192,128]{2,1,0:T(8,128)(2,1)S(1)} %collective-permute-done.23.other_ref), custom_call_target="tpu_custom_call" | custom-call | flops 335544320 | bytes 786432 | tf_op jit(solution)/shard_map/attend/pallas_call | solution.py:397
  86.6 1.1 %copy-done.3 = bf16[1536,256]{1,0:T(8,128)(2,1)S(1)} copy-done((bf16[1536,256]{1,0:T(8,128)(2,1)S(1)}, bf16[1536,256]{1,0:T(8,128)(2,1)}, u32[]{:S(2)}) %copy-start.3) | copy-done | bytes 786456
  87.7 3.2 %output.1 = (bf16[8,128,192]{2,1,0:T(8,128)(2,1)}, bf16[8,256]{1,0:T(8,128)(2,1)S(1)}) custom-call(bf16[4,128,192]{2,1,0:T(8,128)(2,1)S(1)} %attend.1.attended_ref, bf16[8,128,192]{2,1,0:T(8,128)(2,1)S(1)} %get-tuple-element.27.embedded_ref, bf16[1536,256]{1,0:T(8,128)(2,1)S(1)} %copy-done.3, bf16[192,1280]{1,0:T(8,128)(2,1)S(1)} %pad_maximum_fusion.refs_0_, ...), custom_call_target="tpu_custom_call" | custom-call | flops 301989888 | bytes 2359296 | tf_op jit(solution)/shard_map/output/pallas_call | solution.py:410
  90.9 1.2 %collective-permute-done.25 = bf16[8,256]{1,0:T(8,128)(2,1)S(1)} collective-permute-done((bf16[8,256]{1,0:T(8,128)(2,1)S(1)}, bf16[8,256]{1,0:T(8,128)(2,1)S(1)}, u32[]{:S(2)}, u32[]{:S(2)}) %collective-permute-start.25) | collective-permute-done | bytes 4128 | tf_op jit(solution)/shard_map/ppermute | solution.py:419
  92.1 1.0 collective-permute-start.26
  93.1 2.6 %collective-permute-done.26 = bf16[8,256]{1,0:T(8,128)(2,1)S(1)} collective-permute-done((bf16[8,256]{1,0:T(8,128)(2,1)S(1)}, bf16[8,256]{1,0:T(8,128)(2,1)S(1)}, u32[]{:S(2)}, u32[]{:S(2)}) %collective-permute-start.26) | collective-permute-done | bytes 4128 | tf_op jit(solution)/shard_map/ppermute | solution.py:435
  96.3 3.0 %collective-permute-done.27 = bf16[16,256]{1,0:T(8,128)(2,1)S(1)} collective-permute-done((bf16[16,256]{1,0:T(8,128)(2,1)S(1)}, bf16[16,256]{1,0:T(8,128)(2,1)S(1)}, u32[]{:S(2)}, u32[]{:S(2)}) %collective-permute-start.27) | collective-permute-done | bytes 8224 | tf_op jit(solution)/shard_map/ppermute | solution.py:435
  99.4 2.5 %collective-permute-start.28 = (bf16[32,256]{1,0:T(8,128)(2,1)S(1)}, bf16[32,256]{1,0:T(8,128)(2,1)S(1)}, u32[]{:S(2)}, u32[]{:S(2)}) collective-permute-start(bf16[32,256]{1,0:T(8,128)(2,1)S(1)} %pad_maximum_fusion.3), channel_id=1, source_target_pairs={{0,8},{2,10},{4,12},{6,14},{9,1},{11,3},{13,5},{15,7},{16,24},{18,... | collective-permute-start | bytes 49160 | tf_op jit(solution)/shard_map/ppermute | solution.py:437
  101.8 1.4 %collective-permute-done.28 = bf16[32,256]{1,0:T(8,128)(2,1)S(1)} collective-permute-done((bf16[32,256]{1,0:T(8,128)(2,1)S(1)}, bf16[32,256]{1,0:T(8,128)(2,1)S(1)}, u32[]{:S(2)}, u32[]{:S(2)}) %collective-permute-start.28) | collective-permute-done | bytes 16416 | tf_op jit(solution)/shard_map/ppermute | solution.py:437
  103.3 0.8 pair.1
  104.1 1.8 %tokens.1 = bf16[64,1536]{1,0:T(8,128)(2,1)} custom-call(bf16[8,128,192]{2,1,0:T(8,128)(2,1)S(1)} %get-tuple-element.27.embedded_ref, bf16[8,128,192]{2,1,0:T(8,128)(2,1)} %get-tuple-element.32.part_ref, bf16[8,128,192]{2,1,0:T(8,128)(2,1)S(1)} %collective-permute-done.24.other_ref), custom_call_target="tpu_custom_call" | custom-call | flops 294912 | bytes 786432 | tf_op jit(solution)/shard_map/tokens/pallas_call | solution.py:422
  (58 shorter events, 4.2 us)
Async XLA Ops:
  0.6 15.0 %copy-start = (bf16[1536,192]{0,1:T(8,128)(2,1)S(1)}, bf16[1536,192]{0,1:T(8,128)(2,1)}, u32[]{:S(2)}) copy-start(bf16[1536,192]{0,1:T(8,128)(2,1)} %param.17) | copy-start | bytes 1769476
  2.8 17.7 %collective-permute-start.4 = (bf16[192,896]{1,0:T(8,128)(2,1)S(1)}, bf16[192,896]{1,0:T(8,128)(2,1)S(1)}, u32[]{:S(2)}, u32[]{:S(2)}) collective-permute-start(bf16[192,896]{1,0:T(8,128)(2,1)S(1)} %pad_maximum_fusion.1.refs_0_), channel_id=1, source_target_pairs={{0,2},{2,0},{4,6},{6,4},{8,10},{10,8},{12,14},{14,12},{1,3},{3,1},... | collective-permute-start | bytes 1032200 | tf_op jit(solution)/shard_map/ppermute | solution.py:89
  5.8 14.7 %collective-permute-start.5 = (bf16[192,896]{1,0:T(8,128)(2,1)S(1)}, bf16[192,896]{1,0:T(8,128)(2,1)S(1)}, u32[]{:S(2)}, u32[]{:S(2)}) collective-permute-start(bf16[192,896]{1,0:T(8,128)(2,1)S(1)} %pad_maximum_fusion.1.refs_0_), channel_id=1, source_target_pairs={{0,4},{2,6},{4,12},{6,14},{12,8},{14,10},{8,0},{10,2},{20,16},{22,... | collective-permute-start | bytes 1032200 | tf_op jit(solution)/shard_map/ppermute | solution.py:86
  7.4 9.1 %collective-permute-start = (bf16[704,512]{1,0:T(8,128)(2,1)}, bf16[704,512]{1,0:T(8,128)(2,1)S(1)}, u32[]{:S(2)}, u32[]{:S(2)}) collective-permute-start(bf16[704,512]{1,0:T(8,128)(2,1)} %bitcast.7), channel_id=1, source_target_pairs={{0,1},{1,0},{2,3},{3,2},{4,5},{5,4},{6,7},{7,6},{8,9},{9,8},{10,11... | collective-permute-start | bytes 2162696 | tf_op jit(solution)/shard_map/ppermute | solution.py:296
  8.6 7.8 %collective-permute-start.2 = (bf16[2,704]{1,0:T(2,128)(2,1)S(1)}, bf16[2,704]{1,0:T(2,128)(2,1)S(1)}, u32[]{:S(2)}, u32[]{:S(2)}) collective-permute-start(bf16[2,704]{1,0:T(2,128)(2,1)S(1)} %copy.15), channel_id=1, source_target_pairs={{2,0},{4,2},{6,4},{8,6},{10,8},{12,10},{14,12},{3,1},{5,3},{7,5},{... | collective-permute-start | bytes 8456 | tf_op jit(solution)/shard_map/ppermute | solution.py:298
  10.1 6.3 %collective-permute-start.1 = (bf16[2,704]{1,0:T(2,128)(2,1)S(1)}, bf16[2,704]{1,0:T(2,128)(2,1)S(1)}, u32[]{:S(2)}, u32[]{:S(2)}) collective-permute-start(bf16[2,704]{1,0:T(2,128)(2,1)S(1)} %copy.14), channel_id=1, source_target_pairs={{0,2},{2,4},{4,6},{6,8},{8,10},{10,12},{12,14},{1,3},{3,5},{5,7},{... | collective-permute-start | bytes 8456 | tf_op jit(solution)/shard_map/ppermute | solution.py:297
  15.6 40.2 %copy-start.8 = (f32[1536]{0:T(1024)S(1)}, f32[1536]{0:T(1024)}, u32[]{:S(2)}) copy-start(f32[1536]{0:T(1024)} %param.14) | copy-start | bytes 18436
  16.4 9.4 %collective-permute-start.3 = (bf16[16,704]{1,0:T(8,128)(2,1)S(1)}, bf16[16,704]{1,0:T(8,128)(2,1)S(1)}, u32[]{:S(2)}, u32[]{:S(2)}) collective-permute-start(bf16[16,704]{1,0:T(8,128)(2,1)S(1)} %fusion.2), channel_id=1, source_target_pairs={{0,1},{1,0},{2,3},{3,2},{4,5},{5,4},{6,7},{7,6},{8,9},{9,8},{10,11... | collective-permute-start | bytes 67592 | tf_op jit(solution)/shard_map/ppermute | solution.py:300
  16.5 1.1 %copy-start.6 = (bf16[512,704]{0,1:T(8,128)(2,1)S(1)}, bf16[512,704]{0,1:T(8,128)(2,1)}, u32[]{:S(2)}) copy-start(bf16[512,704]{0,1:T(8,128)(2,1)} %param.10) | copy-start | bytes 2162692
  20.5 15.5 %collective-permute-start.6 = (bf16[192,896]{1,0:T(8,128)(2,1)S(1)}, bf16[192,896]{1,0:T(8,128)(2,1)S(1)}, u32[]{:S(2)}, u32[]{:S(2)}) collective-permute-start(bf16[192,896]{1,0:T(8,128)(2,1)S(1)} %collective-permute-done.5.refs_2_), channel_id=1, source_target_pairs={{0,2},{2,0},{4,6},{6,4},{8,10},{10,8},{12,14},{14,12},{1,3},{3,1},... | collective-permute-start | bytes 1032200 | tf_op jit(solution)/shard_map/ppermute | solution.py:89
  22.8 10.5 %collective-permute-start.7 = (bf16[192,896]{1,0:T(8,128)(2,1)S(1)}, bf16[192,896]{1,0:T(8,128)(2,1)S(1)}, u32[]{:S(2)}, u32[]{:S(2)}) collective-permute-start(bf16[192,896]{1,0:T(8,128)(2,1)S(1)} %collective-permute-done.5.refs_2_), channel_id=1, source_target_pairs={{0,16},{16,0},{1,17},{17,1},{2,18},{18,2},{3,19},{19,3},{4,20},{20... | collective-permute-start | bytes 1032200 | tf_op jit(solution)/shard_map/ppermute | solution.py:92
  24.9 10.8 %collective-permute-start.9 = (bf16[192,896]{1,0:T(8,128)(2,1)S(1)}, bf16[192,896]{1,0:T(8,128)(2,1)S(1)}, u32[]{:S(2)}, u32[]{:S(2)}) collective-permute-start(bf16[192,896]{1,0:T(8,128)(2,1)S(1)} %collective-permute-done.5.refs_2_), channel_id=1, source_target_pairs={{0,4},{2,6},{4,12},{6,14},{12,8},{14,10},{8,0},{10,2},{20,16},{22,... | collective-permute-start | bytes 1032200 | tf_op jit(solution)/shard_map/ppermute | solution.py:86
  32.1 71.2 %copy-start.7 = (bf16[128,128]{1,0:T(8,128)(2,1)S(1)}, bf16[128,128]{1,0:T(8,128)(2,1)}, u32[]{:S(2)}) copy-start(bf16[128,128]{1,0:T(8,128)(2,1)} %weight_ref.1) | copy-start | bytes 98308
  35.7 16.5 %collective-permute-start.13 = (bf16[192,1280]{1,0:T(8,128)(2,1)S(1)}, bf16[192,1280]{1,0:T(8,128)(2,1)S(1)}, u32[]{:S(2)}, u32[]{:S(2)}) collective-permute-start(bf16[192,1280]{1,0:T(8,128)(2,1)S(1)} %pad_maximum_fusion.refs_0_), channel_id=1, source_target_pairs={{0,4},{2,6},{4,12},{6,14},{12,8},{14,10},{8,0},{10,2},{20,16},{22,... | collective-permute-start | bytes 1474568 | tf_op jit(solution)/shard_map/ppermute | solution.py:86
  36.0 9.8 %collective-permute-start.8 = (bf16[192,896]{1,0:T(8,128)(2,1)S(1)}, bf16[192,896]{1,0:T(8,128)(2,1)S(1)}, u32[]{:S(2)}, u32[]{:S(2)}) collective-permute-start(bf16[192,896]{1,0:T(8,128)(2,1)S(1)} %collective-permute-done.6.refs_3_), channel_id=1, source_target_pairs={{0,16},{16,0},{1,17},{17,1},{2,18},{18,2},{3,19},{19,3},{4,20},{20... | collective-permute-start | bytes 1032200 | tf_op jit(solution)/shard_map/ppermute | solution.py:92
  38.4 11.0 %collective-permute-start.10 = (bf16[192,896]{1,0:T(8,128)(2,1)S(1)}, bf16[192,896]{1,0:T(8,128)(2,1)S(1)}, u32[]{:S(2)}, u32[]{:S(2)}) collective-permute-start(bf16[192,896]{1,0:T(8,128)(2,1)S(1)} %collective-permute-done.9.refs_6_), channel_id=1, source_target_pairs={{0,2},{2,0},{4,6},{6,4},{8,10},{10,8},{12,14},{14,12},{1,3},{3,1},... | collective-permute-start | bytes 1032200 | tf_op jit(solution)/shard_map/ppermute | solution.py:89
  40.1 19.9 %collective-permute-start.12 = (bf16[192,1280]{1,0:T(8,128)(2,1)S(1)}, bf16[192,1280]{1,0:T(8,128)(2,1)S(1)}, u32[]{:S(2)}, u32[]{:S(2)}) collective-permute-start(bf16[192,1280]{1,0:T(8,128)(2,1)S(1)} %pad_maximum_fusion.refs_0_), channel_id=1, source_target_pairs={{0,2},{2,0},{4,6},{6,4},{8,10},{10,8},{12,14},{14,12},{1,3},{3,1},... | collective-permute-start | bytes 1474568 | tf_op jit(solution)/shard_map/ppermute | solution.py:89
  51.2 0.9 copy-start.1
  52.1 7.8 %collective-permute-start.11 = (bf16[8,128,192]{2,1,0:T(8,128)(2,1)}, bf16[8,128,192]{2,1,0:T(8,128)(2,1)S(1)}, u32[]{:S(2)}, u32[]{:S(2)}) collective-permute-start(bf16[8,128,192]{2,1,0:T(8,128)(2,1)} %get-tuple-element.23.part_ref), channel_id=1, source_target_pairs={{0,1},{1,0},{2,3},{3,2},{4,5},{5,4},{6,7},{7,6},{8,9},{9,8},{10,11... | collective-permute-start | bytes 1179656 | tf_op jit(solution)/shard_map/ppermute | solution.py:359
  52.1 17.2 %collective-permute-start.14 = (bf16[192,1280]{1,0:T(8,128)(2,1)S(1)}, bf16[192,1280]{1,0:T(8,128)(2,1)S(1)}, u32[]{:S(2)}, u32[]{:S(2)}) collective-permute-start(bf16[192,1280]{1,0:T(8,128)(2,1)S(1)} %collective-permute-done.13.refs_2_), channel_id=1, source_target_pairs={{0,2},{2,0},{4,6},{6,4},{8,10},{10,8},{12,14},{14,12},{1,3},{3,1},... | collective-permute-start | bytes 1474568 | tf_op jit(solution)/shard_map/ppermute | solution.py:89
  53.8 15.6 %collective-permute-start.15 = (bf16[192,1280]{1,0:T(8,128)(2,1)S(1)}, bf16[192,1280]{1,0:T(8,128)(2,1)}, u32[]{:S(2)}, u32[]{:S(2)}) collective-permute-start(bf16[192,1280]{1,0:T(8,128)(2,1)S(1)} %collective-permute-done.13.refs_2_), channel_id=1, source_target_pairs={{0,16},{16,0},{1,17},{17,1},{2,18},{18,2},{3,19},{19,3},{4,20},{20... | collective-permute-start | bytes 1474568 | tf_op jit(solution)/shard_map/ppermute | solution.py:92
  53.8 15.6 %collective-permute-start.17 = (bf16[192,1280]{1,0:T(8,128)(2,1)S(1)}, bf16[192,1280]{1,0:T(8,128)(2,1)}, u32[]{:S(2)}, u32[]{:S(2)}) collective-permute-start(bf16[192,1280]{1,0:T(8,128)(2,1)S(1)} %collective-permute-done.13.refs_2_), channel_id=1, source_target_pairs={{0,4},{2,6},{4,12},{6,14},{12,8},{14,10},{8,0},{10,2},{20,16},{22,... | collective-permute-start | bytes 1474568 | tf_op jit(solution)/shard_map/ppermute | solution.py:86
  60.0 0.8 copy-start.4
  60.8 1.1 %copy-start.2 = (bf16[8,192,192]{2,1,0:T(8,128)(2,1)S(1)}, bf16[8,192,192]{2,1,0:T(8,128)(2,1)}, u32[]{:S(2)}) copy-start(bf16[8,192,192]{2,1,0:T(8,128)(2,1)} %copy-done.1) | copy-start | bytes 1769476
  61.9 1.0 copy-start.5
  64.6 4.7 %collective-permute-start.19 = (bf16[192,128]{1,0:T(8,128)(2,1)S(1)}, bf16[192,128]{1,0:T(8,128)(2,1)S(1)}, u32[]{:S(2)}, u32[]{:S(2)}) collective-permute-start(bf16[192,128]{1,0:T(8,128)(2,1)S(1)} %get-tuple-element.30), channel_id=1, source_target_pairs={{0,2},{2,0},{4,6},{6,4},{8,10},{10,8},{12,14},{14,12},{1,3},{3,1},... | collective-permute-start | bytes 147464 | tf_op jit(solution)/shard_map/ppermute | solution.py:377
  69.4 5.7 %collective-permute-start.20 = (bf16[2,192,128]{2,1,0:T(8,128)(2,1)S(1)}, bf16[2,192,128]{2,1,0:T(8,128)(2,1)S(1)}, u32[]{:S(2)}, u32[]{:S(2)}) collective-permute-start(bf16[2,192,128]{2,1,0:T(8,128)(2,1)S(1)} %pad_maximum_fusion.2), channel_id=1, source_target_pairs={{0,4},{2,6},{4,12},{6,14},{12,8},{14,10},{8,0},{10,2},{1,5},{3,7},... | collective-permute-start | bytes 294920 | tf_op jit(solution)/shard_map/ppermute | solution.py:380
  69.8 5.7 %collective-permute-start.21 = (bf16[2,192,128]{2,1,0:T(8,128)(2,1)S(1)}, bf16[2,192,128]{2,1,0:T(8,128)(2,1)S(1)}, u32[]{:S(2)}, u32[]{:S(2)}) collective-permute-start(bf16[2,192,128]{2,1,0:T(8,128)(2,1)S(1)} %pad_maximum_fusion.2), channel_id=1, source_target_pairs={{4,0},{6,2},{12,4},{14,6},{8,12},{10,14},{0,8},{2,10},{5,1},{7,3},... | collective-permute-start | bytes 294920 | tf_op jit(solution)/shard_map/ppermute | solution.py:381
  72.4 10.7 %collective-permute-start.16 = (bf16[192,1280]{1,0:T(8,128)(2,1)S(1)}, bf16[192,1280]{1,0:T(8,128)(2,1)S(1)}, u32[]{:S(2)}, u32[]{:S(2)}) collective-permute-start(bf16[192,1280]{1,0:T(8,128)(2,1)S(1)} %collective-permute-done.14.refs_3_), channel_id=1, source_target_pairs={{0,16},{16,0},{1,17},{17,1},{2,18},{18,2},{3,19},{19,3},{4,20},{20... | collective-permute-start | bytes 1474568 | tf_op jit(solution)/shard_map/ppermute | solution.py:92
  72.7 10.9 %collective-permute-start.18 = (bf16[192,1280]{1,0:T(8,128)(2,1)}, bf16[192,1280]{1,0:T(8,128)(2,1)S(1)}, u32[]{:S(2)}, u32[]{:S(2)}) collective-permute-start(bf16[192,1280]{1,0:T(8,128)(2,1)} %collective-permute-done.17.refs_6_), channel_id=1, source_target_pairs={{0,2},{2,0},{4,6},{6,4},{8,10},{10,8},{12,14},{14,12},{1,3},{3,1},... | collective-permute-start | bytes 1474568 | tf_op jit(solution)/shard_map/ppermute | solution.py:89
  75.1 5.5 %collective-permute-start.22 = (bf16[2,192,128]{2,1,0:T(8,128)(2,1)S(1)}, bf16[2,192,128]{2,1,0:T(8,128)(2,1)S(1)}, u32[]{:S(2)}, u32[]{:S(2)}) collective-permute-start(bf16[2,192,128]{2,1,0:T(8,128)(2,1)S(1)} %collective-permute-done.20), channel_id=1, source_target_pairs={{0,4},{2,6},{4,12},{6,14},{12,8},{14,10},{8,0},{10,2},{1,5},{3,7},... | collective-permute-start | bytes 294920 | tf_op jit(solution)/shard_map/ppermute | solution.py:382
  80.7 4.5 %collective-permute-start.23 = (bf16[8,192,128]{2,1,0:T(8,128)(2,1)S(1)}, bf16[8,192,128]{2,1,0:T(8,128)(2,1)S(1)}, u32[]{:S(2)}, u32[]{:S(2)}) collective-permute-start(bf16[8,192,128]{2,1,0:T(8,128)(2,1)S(1)} %constant_dynamic-update-slice_fusion.own_ref), channel_id=1, source_target_pairs={{0,1},{1,0},{2,3},{3,2},{4,5},{5,4},{6,7},{7,6},{8,9},{9,8},{10,11... | collective-permute-start | bytes 1179656 | tf_op jit(solution)/shard_map/ppermute | solution.py:385
  86.6 1.1 %copy-start.3 = (bf16[1536,256]{1,0:T(8,128)(2,1)S(1)}, bf16[1536,256]{1,0:T(8,128)(2,1)}, u32[]{:S(2)}) copy-start(bf16[1536,256]{1,0:T(8,128)(2,1)} %pair_weight_ref.1) | copy-start | bytes 2359300
  90.9 1.2 %collective-permute-start.25 = (bf16[8,256]{1,0:T(8,128)(2,1)S(1)}, bf16[8,256]{1,0:T(8,128)(2,1)S(1)}, u32[]{:S(2)}, u32[]{:S(2)}) collective-permute-start(bf16[8,256]{1,0:T(8,128)(2,1)S(1)} %get-tuple-element.33), channel_id=1, source_target_pairs={{0,1},{1,0},{2,3},{3,2},{4,5},{5,4},{6,7},{7,6},{8,9},{9,8},{10,11... | collective-permute-start | bytes 12296 | tf_op jit(solution)/shard_map/ppermute | solution.py:419
  92.1 3.6 %collective-permute-start.26 = (bf16[8,256]{1,0:T(8,128)(2,1)S(1)}, bf16[8,256]{1,0:T(8,128)(2,1)S(1)}, u32[]{:S(2)}, u32[]{:S(2)}) collective-permute-start(bf16[8,256]{1,0:T(8,128)(2,1)S(1)} %add_convert_fusion.own_ref), channel_id=1, source_target_pairs={{0,2},{2,0},{4,6},{6,4},{8,10},{10,8},{12,14},{14,12},{1,3},{3,1},... | collective-permute-start | bytes 12296 | tf_op jit(solution)/shard_map/ppermute | solution.py:435
  93.0 11.0 %collective-permute-start.24 = (bf16[8,128,192]{2,1,0:T(8,128)(2,1)}, bf16[8,128,192]{2,1,0:T(8,128)(2,1)S(1)}, u32[]{:S(2)}, u32[]{:S(2)}) collective-permute-start(bf16[8,128,192]{2,1,0:T(8,128)(2,1)} %get-tuple-element.32.part_ref), channel_id=1, source_target_pairs={{0,1},{1,0},{2,3},{3,2},{4,5},{5,4},{6,7},{7,6},{8,9},{9,8},{10,11... | collective-permute-start | bytes 1179656 | tf_op jit(solution)/shard_map/ppermute | solution.py:420
  95.7 3.7 %collective-permute-start.27 = (bf16[16,256]{1,0:T(8,128)(2,1)S(1)}, bf16[16,256]{1,0:T(8,128)(2,1)S(1)}, u32[]{:S(2)}, u32[]{:S(2)}) collective-permute-start(bf16[16,256]{1,0:T(8,128)(2,1)S(1)} %pad_maximum_fusion.4), channel_id=1, source_target_pairs={{0,4},{2,6},{4,0},{6,2},{8,12},{10,14},{12,8},{14,10},{1,5},{3,7},... | collective-permute-start | bytes 24584 | tf_op jit(solution)/shard_map/ppermute | solution.py:435
  99.4 3.9 %collective-permute-start.28 = (bf16[32,256]{1,0:T(8,128)(2,1)S(1)}, bf16[32,256]{1,0:T(8,128)(2,1)S(1)}, u32[]{:S(2)}, u32[]{:S(2)}) collective-permute-start(bf16[32,256]{1,0:T(8,128)(2,1)S(1)} %pad_maximum_fusion.3), channel_id=1, source_target_pairs={{0,8},{2,10},{4,12},{6,14},{9,1},{11,3},{13,5},{15,7},{16,24},{18,... | collective-permute-start | bytes 49160 | tf_op jit(solution)/shard_map/ppermute | solution.py:437

commit v8 on v7

--- a/solution.py
+++ b/solution.py
@@ -188,13 +188,25 @@
     kv_ref[...] = kv
 
 
-def query_kernel(pieces, normed_ref, *refs):
-    blocks, query_ref = refs[:pieces], refs[pieces]
+def later_blocks_of(refs):
+    places = block_owners()
+    per = len(places) // len(refs)
+    rows = refs[0].shape[0] // per
+    for i, place in enumerate(places):
+        start = (i % per) * rows
+        yield refs[i // per], slice(start, start + rows), place
+
+
+def query_kernel(sides, *refs):
+    normed, pieces, query_ref = refs[:sides], refs[sides:-1], refs[-1]
     features = query_ref.shape[1]
-    total = 0.0
-    for ref, owner in zip(blocks, block_owners()):
-        total = total + dot_nn(normed_ref[owner], ref[:, :features])
-    query_ref[...] = (total * DK ** (-0.5)).astype(BF16)
+    tokens = normed[0].shape[1]
+    totals = [0.0] * sides
+    for ref, rows, place in later_blocks_of(pieces):
+        weight = ref[rows, :features]
+        totals = [t + dot_nn(n[place], weight) for t, n in zip(totals, normed)]
+    for i, total in enumerate(totals):
+        query_ref[i * tokens:(i + 1) * tokens] = (total * DK ** (-0.5)).astype(BF16)
 
 
 def attend_kernel(query_ref, own_ref, other_ref, out_ref, keys, values):
@@ -211,20 +223,23 @@
         out_ref[h] = (dot_nt(weights.astype(BF16), values[...]) / total).astype(BF16)
 
 
-def output_kernel(pieces, features, attended_ref, embedded_ref, pair_weight_ref, *refs):
-    blocks, (out_ref, pair_ref) = refs[:pieces], refs[pieces:]
+def output_kernel(sides, features, attended_ref, embedded_ref, pair_weight_ref, *refs):
+    pieces, outs, pair_ref = refs[:-1 - sides], refs[-1 - sides:-1], refs[-1]
     heads = attended_ref.shape[0]
     flat = jnp.concatenate([attended_ref[h] for h in range(heads)], axis=1)
-    _, rows, width = out_ref.shape
+    _, tokens, width = outs[0].shape
     share = jnp.where(lax.axis_index("col") == 0, 1.0, 0.0)
     projected = 0.0
-    for ref, owner in zip(blocks, block_owners()):
-        part = dot_nt(flat, ref[:, features:])
-        out_ref[owner] = part.astype(BF16)
-        part = part + share * embedded_ref[owner].astype(F32)
-        pooled = jnp.mean(part.reshape(rows // PAIR_POOL, PAIR_POOL, width), axis=1).astype(BF16)
-        weight = pair_weight_ref[pl.ds(pl.multiple_of(owner * width, width), width)]
-        projected = projected + dot_nn(pooled, weight)
+    for ref, rows, place in later_blocks_of(pieces):
+        part = dot_nt(flat, ref[rows, features:])
+        for i, out in enumerate(outs):
+            out[place] = part[i * tokens:(i + 1) * tokens].astype(BF16)
+        pooled = jnp.mean(part.reshape(sides * tokens // PAIR_POOL, PAIR_POOL, width), axis=1)
+        first = jnp.mean(embedded_ref[place].astype(F32).reshape(tokens // PAIR_POOL, PAIR_POOL, width), axis=1) * share
+        if sides > 1:
+            first = jnp.concatenate([first, jnp.zeros((pooled.shape[0] - first.shape[0], width), F32)], axis=0)
+        weight = pair_weight_ref[pl.ds(pl.multiple_of(place * width, width), width)]
+        projected = projected + dot_nn((pooled + first).astype(BF16), weight)
     pair_ref[...] = projected.astype(BF16)
 
 
@@ -278,15 +293,23 @@
     embed_own = jnp.concatenate(
         [embed_weight.T, lax.dynamic_slice_in_dim(keyvalue_weight, col * DK, DV, 1)], axis=1
     )
-    later_own = jnp.concatenate(
-        [
-            lax.dynamic_slice_in_dim(query_weight, col * features, features, 1),
-            lax.dynamic_slice_in_dim(output_weight.T, col * heads * DV, heads * DV, 1),
-        ],
-        axis=1,
-    )
     ring = planned(count, lax.axis_size("grp")) and cols == 2
-    e, q = (Blocks(x, count) for x in (embed_own, later_own))
+    sides = 2 if ring else 1
+    side = lax.axis_index("seq") % sides
+    pair_swap = [(i, i ^ 1) for i in range(count)]
+    heads, features = heads // sides, features // sides
+
+    def later_part(which):
+        place = col * sides + which
+        return jnp.concatenate(
+            [
+                lax.dynamic_slice_in_dim(query_weight, place * features, features, 1),
+                lax.dynamic_slice_in_dim(output_weight.T, place * heads * DV, heads * DV, 1),
+            ],
+            axis=1,
+        )
+
+    e = Blocks(embed_own, count)
 
     signal_t = signal.T
     up = [(i, i + 1) for i in range(count - 1)]
@@ -301,6 +324,8 @@
     halo = jnp.where(
         col == 0, jnp.concatenate([own_halo, other_halo], axis=1), jnp.concatenate([other_halo, own_halo], axis=1)
     )
+    if ring:
+        other_t = after(other_t, e.at["step"], e.at["own2"])
     gain_row = conv_gain.reshape(1, channels)
     windows, residual = pl.pallas_call(
         functools.partial(act_kernel, taps),
@@ -313,7 +338,7 @@
         name="act",
     )(signal_t, other_t, gain_row)
     if ring:
-        e.at["step"] = after(e.at["step"], e.at["own2"], windows)
+        e.at["step"] = after(e.at["step"], e.at["own2"])
         e.along("step", "far")
         e.across("step", "step2")
         e.between("step", "cross")
@@ -332,18 +357,20 @@
         e.at["step2"] = after(e.at["step2"], pooled, e.at["cross"])
         e.across("far", "far2")
         e.between("step2", "cross2")
-        q.at["own"] = after(q.at["own"], pooled, e.at["far"])
+        theirs = after(later_part(1 - side), pooled, e.at["cross"])
+        received = lax.ppermute(theirs, "seq", pair_swap)
+        pooled = after(pooled, received)
+        q = Blocks(jnp.concatenate([later_part(side), received]), count)
+        q.at["own"] = after(q.at["own"], e.at["far2"])
         q.along("own", "step")
-        q.across("own", "own2")
-        q.at["step"] = after(q.at["step"], e.at["far2"], e.at["cross2"])
         q.along("step", "far")
-        q.across("step", "step2")
         q.between("step", "cross")
-        q.across("far", "far2")
-        q.between("step2", "cross2")
-        embed_blocks, later_blocks = e.pieces(), q.pieces()
+        embed_blocks = e.pieces()
+        later_blocks = [q.at[name] for name in ("own", "step", "cross", "far")]
     else:
-        embed_blocks, later_blocks = ([lax.all_gather(x.at["own"], "seq", axis=0, tiled=True)] for x in (e, q))
+        embed_blocks, later_blocks = (
+            [lax.all_gather(x, "seq", axis=0, tiled=True)] for x in (embed_own, later_part(0))
+        )
     pieces = len(embed_blocks)
     block = width // pieces
 
@@ -357,8 +384,6 @@
         name="embed",
     )(pooled, *embed_blocks)
     other_part = lax.ppermute(part, "col", swap)
-    if ring:
-        other_part = after(other_part, q.at["own2"])
 
     keyvalue, normed, embedded = pl.pallas_call(
         keyvalue_kernel,
@@ -373,9 +398,10 @@
         cost_estimate=cost(2 * tokens * width * DV, 2 * width * DV),
         name="keyvalue",
     )(part, other_part, attn_gain.reshape(pieces, 1, block), keyvalue_blocks)
-    if ring:
-        here = jnp.stack([keyvalue, lax.ppermute(keyvalue, "seq", [(i, i ^ 1) for i in range(count)])])
-        here = after(here, q.at["far"], q.at["step2"], q.at["cross"])
+    both_normed = [normed]
+    if ring:
+        here = jnp.stack([keyvalue, lax.ppermute(keyvalue, "seq", pair_swap)])
+        both_normed.append(lax.ppermute(normed, "seq", pair_swap))
         onward = [(2 * RING[k] + i, 2 * RING[(k + 1) % 4] + i) for k in range(4) for i in range(2)]
         ahead = lax.ppermute(here, "seq", onward)
         back = lax.ppermute(here, "seq", [(j, i) for i, j in onward])
@@ -385,18 +411,18 @@
     gathered_other = lax.ppermute(gathered, "col", swap)
 
     queries = pl.pallas_call(
-        functools.partial(query_kernel, pieces),
-        out_shape=shape((tokens, features), BF16),
-        in_specs=vspec(1 + pieces),
+        functools.partial(query_kernel, sides),
+        out_shape=shape((sides * tokens, features), BF16),
+        in_specs=vspec(sides + len(later_blocks)),
         out_specs=pl.BlockSpec(memory_space=VMEM),
         compiler_params=params(12),
-        cost_estimate=cost(2 * tokens * width * features, 2 * width * features),
+        cost_estimate=cost(2 * sides * tokens * width * features, 2 * width * features),
         name="query",
-    )(normed, *later_blocks)
+    )(*both_normed, *later_blocks)
 
     attended = pl.pallas_call(
         attend_kernel,
-        out_shape=shape((heads, tokens, DV), BF16),
+        out_shape=shape((heads, sides * tokens, DV), BF16),
         in_specs=vspec(3),
         out_specs=pl.BlockSpec(memory_space=VMEM),
         scratch_shapes=[pltpu.VMEM((DK, count * tokens), BF16), pltpu.VMEM((DV, count * tokens), BF16)],
@@ -407,18 +433,29 @@
 
     out_width = rowcol_weight.shape[1]
     own_rows, pair_rows = tokens // cols, tokens // PAIR_POOL
-    part_out, part_pair = pl.pallas_call(
-        functools.partial(output_kernel, pieces, features),
-        out_shape=(shape((pieces, tokens, block), BF16), shape((pair_rows, out_width), BF16)),
-        in_specs=vspec(3 + pieces),
-        out_specs=vspec(2),
+    *part_outs, part_pair = pl.pallas_call(
+        functools.partial(output_kernel, sides, features),
+        out_shape=tuple(
+            [shape((pieces, tokens, block), BF16)] * sides + [shape((sides * pair_rows, out_width), BF16)]
+        ),
+        in_specs=vspec(3 + len(later_blocks)),
+        out_specs=vspec(sides + 1),
         compiler_params=params(16),
-        cost_estimate=cost(2 * tokens * heads * DV * width, 2 * heads * DV * width),
+        cost_estimate=cost(2 * sides * tokens * heads * DV * width, 2 * heads * DV * width),
         name="output",
     )(attended, embedded, rowcol_weight, *later_blocks)
-    other_pair = lax.ppermute(part_pair, "col", swap)
+
+    def total(*parts):
+        return sum(x.astype(F32) for x in parts).astype(BF16)
+
+    part_out = part_outs[0]
+    if ring:
+        turned = lax.ppermute(part_pair, "seq", pair_swap)
+        part_pair = total(part_pair, jnp.concatenate([turned[pair_rows:], turned[:pair_rows]]))
+    projected = total(part_pair, lax.ppermute(part_pair, "col", swap))
+    if ring:
+        part_out = total(part_out, lax.ppermute(part_outs[1], "seq", pair_swap))
     other_out = lax.ppermute(part_out, "col", swap)
-    projected = (part_pair.astype(F32) + other_pair.astype(F32)).astype(BF16)
     out_tokens = pl.pallas_call(
         token_kernel,
         out_shape=shape((own_rows, width), BF16),
@@ -431,8 +468,7 @@
 
     if ring:
         rows_all = projected
-        for bit in (1, 2):
-            rows_all = jnp.concatenate([rows_all, lax.ppermute(rows_all, "seq", [(i, i ^ bit) for i in range(count)])])
+        rows_all = jnp.concatenate([rows_all, lax.ppermute(rows_all, "seq", [(i, i ^ 2) for i in range(count)])])
         pairs = [(i * cols + i // 4, (i ^ 4) * cols + i // 4) for i in range(count)]
         far_rows = lax.ppermute(rows_all, ("seq", "col"), pairs)
         rows_all = jnp.where(lax.axis_index("seq") // 4 == col, rows_all, far_rows)
@@ -450,7 +486,7 @@
         compiler_params=params(16),
         cost_estimate=cost(2 * pair_rows * span * pair_features**2, 2 * pair_rows * span * pair_features),
         name="pair",
-    )(projected, rows_all, pair_weight)
+    )(projected[:pair_rows], rows_all, pair_weight)
     return out_tokens, pair_out
 
 

time: 107 us -> 114 us (1.065)
  waiting for transfers between devices: 37.6 us -> 57.6 us
  starting transfers between devices: 34.5 us -> 28.5 us
  Pallas kernels: 21.4 us -> 15.5 us
  local copies, waits for them, and re-layouts: 10.4 us -> 7.61 us
  other arithmetic: 1.23 us -> 2.43 us
    ppermute x4 -> x7, waiting for transfers between devices: 10.2 us -> 30.7 us  [the longest x1 12.4 us: on_device(): received = lax.ppermute(theirs, 'seq', pair_swap)]
    ppermute x4 -> x3, waiting for transfers between devices: 8.88 us -> 0.01 us  [between(): self.at[target] = lax.ppermute(self.at[source], 'grp', [(0, 1), (1, 0)])]
    ppermute x6 -> x3, waiting for transfers between devices: 8.13 us -> 0.01 us  [across(): lax.ppermute(self.at[source], 'seq', [(i, i ^ 1) for i in range(self.coun...]
    ppermute x1, waiting for transfers between devices: 5.19 us -> 12 us  [on_device(): lax.ppermute(ahead, 'seq', onward)]
    ppermute x6 -> x3, starting transfers between devices: 10.4 us -> 6.02 us  [across(): lax.ppermute(self.at[source], 'seq', [(i, i ^ 1) for i in range(self.coun...]
    unnamed x23 -> x18, local copies, waits for them, and re-layouts: 6.39 us -> 2.3 us
    ppermute x1, waiting for transfers between devices: 0.01 us -> 4.01 us  [on_device(): behind = lax.ppermute(signal[:reach], 'seq', [(j, i) for i, j in up])]
    ppermute x4, waiting for transfers between devices: 2.37 us -> 6.04 us  [along(): self.at[target] = lax.ppermute(self.at[source], ('grp', 'seq'), pairs)]
  transfers between devices with their start and end apart: 29 -> 28, of which waited for: 15 -> 12; matrix products, arithmetic and copies ran while one was open for 3% -> 6% of each run, Pallas kernels for 14% -> 10%
where the time goes in v8:
time: 114 us; the launch traced here: 113 us
  waiting for transfers between devices  57.6 us (51%)
  starting transfers between devices  28.5 us (25%)
  Pallas kernels  15.5 us (14%)
  local copies, waits for them, and re-layouts  7.61 us (7%)
  other arithmetic  2.43 us (2%)
    ppermute x1, waiting for transfers between devices, on_device(): received = lax.ppermute(theirs, 'seq', pair_swap)  12.4 us
    ppermute x1, waiting for transfers between devices, on_device(): lax.ppermute(ahead, 'seq', onward)  12 us
    ppermute x1, waiting for transfers between devices, on_device(): part_out = total(part_out, lax.ppermute(part_outs[1], 'seq', pair_swap))  10.3 us
    pallas_call x1, Pallas kernels, on_device(): pl.pallas_call(functools.partial(conv_kernel, positions), out_shape=shape...  6.21 us
    ppermute x4, waiting for transfers between devices, along(): self.at[target] = lax.ppermute(self.at[source], ('grp', 'seq'), pairs)  6.04 us
    ppermute x3, starting transfers between devices, across(): lax.ppermute(self.at[source], 'seq', [(i, i ^ 1) for i in range(self.coun...  6.02 us
    ppermute x4, starting transfers between devices, along(): self.at[target] = lax.ppermute(self.at[source], ('grp', 'seq'), pairs)  4.94 us
    ppermute x1, waiting for transfers between devices, on_device(): behind = lax.ppermute(signal[:reach], 'seq', [(j, i) for i, j in up])  4.01 us
  transfers between devices with their start and end apart: 28, of which 12 were waited for; matrix products, arithmetic and copies ran while one was open for 6% of the time, Pallas kernels for 10%

profile of v8, /device:TPU:0, one launch (start us, length us, event | category | flops | bytes accessed | tf_op | source)
XLA Modules:
  0.0 112.7 jit_solution(1080040439619082902)
XLA Ops:
  0.7 0.9 copy-done
  1.6 1.1 pad_maximum_fusion.1.refs_0_
  2.7 3.0 %collective-permute-start.2 = (bf16[192,896]{1,0:T(8,128)(2,1)S(1)}, bf16[192,896]{1,0:T(8,128)(2,1)S(1)}, u32[]{:S(2)}, u32[]{:S(2)}) collective-permute-start(bf16[192,896]{1,0:T(8,128)(2,1)S(1)} %pad_maximum_fusion.1.refs_0_), channel_id=1, source_target_pairs={{0,2},{2,0},{4,6},{6,4},{8,10},{10,8},{12,14},{14,12},{1,3},{3,1},... | collective-permute-start | bytes 1032200 | tf_op jit(solution)/shard_map/ppermute | solution.py:89
  5.7 1.6 %collective-permute-start.1 = (bf16[192,896]{1,0:T(8,128)(2,1)S(1)}, bf16[192,896]{1,0:T(8,128)(2,1)S(1)}, u32[]{:S(2)}, u32[]{:S(2)}) collective-permute-start(bf16[192,896]{1,0:T(8,128)(2,1)S(1)} %pad_maximum_fusion.1.refs_0_), channel_id=1, source_target_pairs={{0,4},{2,6},{4,12},{6,14},{12,8},{14,10},{8,0},{10,2},{20,16},{22,... | collective-permute-start | bytes 1032200 | tf_op jit(solution)/shard_map/ppermute | solution.py:86
  7.3 1.1 fusion.3
  8.6 2.4 %collective-permute-start.3 = (bf16[2,704]{1,0:T(2,128)(2,1)S(1)}, bf16[2,704]{1,0:T(2,128)(2,1)S(1)}, u32[]{:S(2)}, u32[]{:S(2)}) collective-permute-start(bf16[2,704]{1,0:T(2,128)(2,1)S(1)} %copy.14), channel_id=1, source_target_pairs={{0,2},{2,4},{4,6},{6,8},{8,10},{10,12},{12,14},{1,3},{3,5},{5,7},{... | collective-permute-start | bytes 8456 | tf_op jit(solution)/shard_map/ppermute | solution.py:320
  11.1 1.3 %collective-permute-start.4 = (bf16[2,704]{1,0:T(2,128)(2,1)S(1)}, bf16[2,704]{1,0:T(2,128)(2,1)S(1)}, u32[]{:S(2)}, u32[]{:S(2)}) collective-permute-start(bf16[2,704]{1,0:T(2,128)(2,1)S(1)} %copy.15), channel_id=1, source_target_pairs={{2,0},{4,2},{6,4},{8,6},{10,8},{12,10},{14,12},{3,1},{5,3},{7,5},{... | collective-permute-start | bytes 8456 | tf_op jit(solution)/shard_map/ppermute | solution.py:321
  12.5 1.7 %dynamic-slice_bitcast_fusion = (bf16[192,384]{1,0:T(8,128)(2,1)}, bf16[192,384]{1,0:T(8,128)(2,1)S(1)}) fusion(bf16[1536,192]{0,1:T(8,128)(2,1)} %param.17, s32[]{:T(128)S(6)} %select_n.49, s32[]{:T(128)S(6)} %select_n.47), kind=kLoop, calls=%fused_computation.4 | loop fusion | bytes 589832 | tf_op jit(solution)/shard_map/dynamic_slice | solution.py:307
  14.2 4.0 %collective-permute-done.4 = bf16[2,704]{1,0:T(2,128)(2,1)S(1)} collective-permute-done((bf16[2,704]{1,0:T(2,128)(2,1)S(1)}, bf16[2,704]{1,0:T(2,128)(2,1)S(1)}, u32[]{:S(2)}, u32[]{:S(2)}) %collective-permute-start.4) | collective-permute-done | bytes 2848 | tf_op jit(solution)/shard_map/ppermute | solution.py:321
  18.3 1.6 %constant_dynamic-slice_fusion = (bf16[192,256]{1,0:T(8,128)(2,1)}, bf16[192,256]{1,0:T(8,128)(2,1)S(1)}) fusion(bf16[192,1024]{1,0:T(8,128)(2,1)} %param.15, s32[]{:T(128)S(6)} %select_n.48, s32[]{:T(128)S(6)} %select_n.46), kind=kLoop, calls=%fused_computation.21 | loop fusion | bytes 393224 | tf_op jit(solution)/shard_map/dynamic_slice | solution.py:306
  19.9 0.7 reshape.10.gain_ref
  20.6 1.0 collective-permute-start.6
  21.6 1.1 collective-permute-start.10
  22.7 2.9 %collective-permute-start.8 = (bf16[192,896]{1,0:T(8,128)(2,1)S(1)}, bf16[192,896]{1,0:T(8,128)(2,1)S(1)}, u32[]{:S(2)}, u32[]{:S(2)}) collective-permute-start(bf16[192,896]{1,0:T(8,128)(2,1)S(1)} %collective-permute-done.1.refs_2_), channel_id=1, source_target_pairs={{0,2},{2,0},{4,6},{6,4},{8,10},{10,8},{12,14},{14,12},{1,3},{3,1},... | collective-permute-start | bytes 1032200 | tf_op jit(solution)/shard_map/ppermute | solution.py:89
  25.7 1.1 copy-done.2
  26.8 2.9 %act.1 = (bf16[640,1408]{1,0:T(8,128)(2,1)S(1)}, f32[128,704]{1,0:T(8,128)S(1)}) custom-call(bf16[704,512]{1,0:T(8,128)(2,1)S(1)} %bitcast.13, bf16[704,512]{1,0:T(8,128)(2,1)S(1)} %collective-permute-done.other_ref, f32[1,1408]{1,0:T(1,128)S(1)} %reshape.10.gain_ref), custom_call_target="tpu_custom_call" | custom-call | flops 922746880 | bytes 2883584 | tf_op jit(solution)/shard_map/act/pallas_call | solution.py:330
  29.7 6.2 %conv.1.pooled_ref = bf16[128,704]{1,0:T(8,128)(2,1)S(1)} custom-call(bf16[640,1408]{1,0:T(8,128)(2,1)S(1)} %get-tuple-element.20.windows_ref, f32[128,704]{1,0:T(8,128)S(1)} %get-tuple-element.21.residual_ref, bf16[16,1408]{1,0:T(8,128)(2,1)S(1)} %maximum_select_fusion.halo_ref, f32[1,1408]{1,0:T(1,128)S(1)} %reshape.10.gain_ref, bf16[5,704,1408]{2,1,0:T(8,128)(2,1)} %bitcast.14), custom_call_target="tpu_custom_call" | custom-call | flops 1268776960 | bytes 9912320 | tf_op jit(solution)/shard_map/conv/pallas_call | solution.py:345
  36.1 0.5 collective-permute-start.9
  36.6 2.0 %collective-permute-start.7 = (bf16[192,640]{1,0:T(8,128)(2,1)S(1)}, bf16[192,640]{1,0:T(8,128)(2,1)}, u32[]{:S(2)}, u32[]{:S(2)}) collective-permute-start(bf16[192,640]{1,0:T(8,128)(2,1)S(1)} %pad_maximum_fusion.2), channel_id=1, source_target_pairs={{0,2},{2,0},{4,6},{6,4},{8,10},{10,8},{12,14},{14,12},{1,3},{3,1},... | collective-permute-start | bytes 737288 | tf_op jit(solution)/shard_map/ppermute | solution.py:361
  38.6 12.4 %collective-permute-done.7 = bf16[192,640]{1,0:T(8,128)(2,1)} collective-permute-done((bf16[192,640]{1,0:T(8,128)(2,1)S(1)}, bf16[192,640]{1,0:T(8,128)(2,1)}, u32[]{:S(2)}, u32[]{:S(2)}) %collective-permute-start.7) | collective-permute-done | bytes 245792 | tf_op jit(solution)/shard_map/ppermute | solution.py:361
  51.0 1.0 embed.1
  52.2 1.1 pad_maximum_fusion.refs_2_.refs_0_
  53.2 0.3 collective-permute-start.14
  53.6 0.4 collective-permute-done.12.other_ref
  54.0 0.6 keyvalue.1
  54.6 0.4 collective-permute-start.17
  55.0 1.7 %collective-permute-start.13 = (bf16[8,128,192]{2,1,0:T(8,128)(2,1)S(1)}, bf16[8,128,192]{2,1,0:T(8,128)(2,1)S(1)}, u32[]{:S(2)}, u32[]{:S(2)}) collective-permute-start(bf16[8,128,192]{2,1,0:T(8,128)(2,1)S(1)} %get-tuple-element.30.refs_0_), channel_id=1, source_target_pairs={{0,2},{2,0},{4,6},{6,4},{8,10},{10,8},{12,14},{14,12},{1,3},{3,1},... | collective-permute-start | bytes 1179656 | tf_op jit(solution)/shard_map/ppermute | solution.py:404
  56.7 2.6 %collective-permute-done.17 = bf16[192,128]{1,0:T(8,128)(2,1)S(1)} collective-permute-done((bf16[192,128]{1,0:T(8,128)(2,1)S(1)}, bf16[192,128]{1,0:T(8,128)(2,1)S(1)}, u32[]{:S(2)}, u32[]{:S(2)}) %collective-permute-start.17) | collective-permute-done | bytes 49184 | tf_op jit(solution)/shard_map/ppermute | solution.py:403
  59.3 1.2 %collective-permute-start.18 = (bf16[2,192,128]{2,1,0:T(8,128)(2,1)S(1)}, bf16[2,192,128]{2,1,0:T(8,128)(2,1)S(1)}, u32[]{:S(2)}, u32[]{:S(2)}) collective-permute-start(bf16[2,192,128]{2,1,0:T(8,128)(2,1)S(1)} %pad_maximum_fusion.3), channel_id=1, source_target_pairs={{0,4},{2,6},{4,12},{6,14},{12,8},{14,10},{8,0},{10,2},{1,5},{3,7},... | collective-permute-start | bytes 294920 | tf_op jit(solution)/shard_map/ppermute | solution.py:406
  60.4 1.8 %collective-permute-start.19 = (bf16[2,192,128]{2,1,0:T(8,128)(2,1)S(1)}, bf16[2,192,128]{2,1,0:T(8,128)(2,1)S(1)}, u32[]{:S(2)}, u32[]{:S(2)}) collective-permute-start(bf16[2,192,128]{2,1,0:T(8,128)(2,1)S(1)} %pad_maximum_fusion.3), channel_id=1, source_target_pairs={{4,0},{6,2},{12,4},{14,6},{8,12},{10,14},{0,8},{2,10},{5,1},{7,3},... | collective-permute-start | bytes 294920 | tf_op jit(solution)/shard_map/ppermute | solution.py:407
  62.3 6.0 %collective-permute-done.14.refs_3_.refs_1_ = bf16[384,640]{1,0:T(8,128)(2,1)S(1)} collective-permute-done((bf16[384,640]{1,0:T(8,128)(2,1)S(1)}, bf16[384,640]{1,0:T(8,128)(2,1)S(1)}, u32[]{:S(2)}, u32[]{:S(2)}) %collective-permute-start.14) | collective-permute-done | bytes 491552 | tf_op jit(solution)/shard_map/ppermute | solution.py:86
  68.3 1.9 %collective-permute-start.16 = (bf16[384,640]{1,0:T(8,128)(2,1)S(1)}, bf16[384,640]{1,0:T(8,128)(2,1)S(1)}, u32[]{:S(2)}, u32[]{:S(2)}) collective-permute-start(bf16[384,640]{1,0:T(8,128)(2,1)S(1)} %collective-permute-done.14.refs_3_.refs_1_), channel_id=1, source_target_pairs={{0,4},{2,6},{4,12},{6,14},{12,8},{14,10},{8,0},{10,2},{20,16},{22,... | collective-permute-start | bytes 1474568 | tf_op jit(solution)/shard_map/ppermute | solution.py:86
  70.2 1.9 %collective-permute-done.18 = bf16[2,192,128]{2,1,0:T(8,128)(2,1)S(1)} collective-permute-done((bf16[2,192,128]{2,1,0:T(8,128)(2,1)S(1)}, bf16[2,192,128]{2,1,0:T(8,128)(2,1)S(1)}, u32[]{:S(2)}, u32[]{:S(2)}) %collective-permute-start.18) | collective-permute-done | bytes 98336 | tf_op jit(solution)/shard_map/ppermute | solution.py:406
  72.2 0.5 collective-permute-start.20
  72.7 12.0 %collective-permute-done.20 = bf16[2,192,128]{2,1,0:T(8,128)(2,1)S(1)} collective-permute-done((bf16[2,192,128]{2,1,0:T(8,128)(2,1)S(1)}, bf16[2,192,128]{2,1,0:T(8,128)(2,1)S(1)}, u32[]{:S(2)}, u32[]{:S(2)}) %collective-permute-start.20) | collective-permute-done | bytes 98336 | tf_op jit(solution)/shard_map/ppermute | solution.py:408
  84.8 0.4 query.1.query_ref
  85.3 1.2 %collective-permute-done.21.other_ref = bf16[8,192,128]{2,1,0:T(8,128)(2,1)S(1)} collective-permute-done((bf16[8,192,128]{2,1,0:T(8,128)(2,1)S(1)}, bf16[8,192,128]{2,1,0:T(8,128)(2,1)S(1)}, u32[]{:S(2)}, u32[]{:S(2)}) %collective-permute-start.21) | collective-permute-done | bytes 393248 | tf_op jit(solution)/shard_map/ppermute | solution.py:411
  86.5 1.4 %attend.1.attended_ref = bf16[2,256,192]{2,1,0:T(8,128)(2,1)S(1)} custom-call(bf16[256,256]{1,0:T(8,128)(2,1)S(1)} %query.1.query_ref, bf16[8,192,128]{2,1,0:T(8,128)(2,1)S(1)} %constant_dynamic-update-slice_fusion.own_ref, bf16[8,192,128]{2,1,0:T(8,128)(2,1)S(1)} %collective-permute-done.21.other_ref), custom_call_target="tpu_custom_call" | custom-call | flops 167772160 | bytes 786432 | tf_op jit(solution)/shard_map/attend/pallas_call | solution.py:423
  88.0 1.3 %output.1 = (bf16[8,128,192]{2,1,0:T(8,128)(2,1)S(1)}, bf16[8,128,192]{2,1,0:T(8,128)(2,1)S(1)}, bf16[16,256]{1,0:T(8,128)(2,1)S(1)}) custom-call(bf16[2,256,192]{2,1,0:T(8,128)(2,1)S(1)} %attend.1.attended_ref, bf16[8,128,192]{2,1,0:T(8,128)(2,1)S(1)} %get-tuple-element.29.embedded_ref, bf16[1536,256]{1,0:T(8,128)(2,1)S(1)} %copy-done.1, ...), custom_call_target="tpu_custom_call" | custom-call | flops 301989888 | bytes 1179648 | tf_op jit(solution)/shard_map/output/pallas_call | solution.py:436
  89.3 0.3 collective-permute-start.24
  89.6 1.7 %collective-permute-start.22 = (bf16[8,128,192]{2,1,0:T(8,128)(2,1)S(1)}, bf16[8,128,192]{2,1,0:T(8,128)(2,1)S(1)}, u32[]{:S(2)}, u32[]{:S(2)}) collective-permute-start(bf16[8,128,192]{2,1,0:T(8,128)(2,1)S(1)} %get-tuple-element.34), channel_id=1, source_target_pairs={{0,2},{2,0},{4,6},{6,4},{8,10},{10,8},{12,14},{14,12},{1,3},{3,1},... | collective-permute-start | bytes 1179656 | tf_op jit(solution)/shard_map/ppermute | solution.py:457
  91.3 1.7 %collective-permute-done.24 = bf16[16,256]{1,0:T(8,128)(2,1)S(1)} collective-permute-done((bf16[16,256]{1,0:T(8,128)(2,1)S(1)}, bf16[16,256]{1,0:T(8,128)(2,1)S(1)}, u32[]{:S(2)}, u32[]{:S(2)}) %collective-permute-start.24) | collective-permute-done | bytes 8224 | tf_op jit(solution)/shard_map/ppermute | solution.py:453
  93.1 10.3 %collective-permute-done.22 = bf16[8,128,192]{2,1,0:T(8,128)(2,1)S(1)} collective-permute-done((bf16[8,128,192]{2,1,0:T(8,128)(2,1)S(1)}, bf16[8,128,192]{2,1,0:T(8,128)(2,1)S(1)}, u32[]{:S(2)}, u32[]{:S(2)}) %collective-permute-start.22) | collective-permute-done | bytes 393248 | tf_op jit(solution)/shard_map/ppermute | solution.py:457
  103.8 3.6 %collective-permute-done.26 = bf16[16,256]{1,0:T(8,128)(2,1)S(1)} collective-permute-done((bf16[16,256]{1,0:T(8,128)(2,1)S(1)}, bf16[16,256]{1,0:T(8,128)(2,1)S(1)}, u32[]{:S(2)}, u32[]{:S(2)}) %collective-permute-start.26) | collective-permute-done | bytes 8224 | tf_op jit(solution)/shard_map/ppermute | solution.py:471
  107.4 2.2 %collective-permute-start.27 = (bf16[32,256]{1,0:T(8,128)(2,1)S(1)}, bf16[32,256]{1,0:T(8,128)(2,1)S(1)}, u32[]{:S(2)}, u32[]{:S(2)}) collective-permute-start(bf16[32,256]{1,0:T(8,128)(2,1)S(1)} %pad_maximum_fusion.4), channel_id=1, source_target_pairs={{0,8},{2,10},{4,12},{6,14},{9,1},{11,3},{13,5},{15,7},{16,24},{18,... | collective-permute-start | bytes 49160 | tf_op jit(solution)/shard_map/ppermute | solution.py:473
  109.7 1.4 %collective-permute-done.27 = bf16[32,256]{1,0:T(8,128)(2,1)S(1)} collective-permute-done((bf16[32,256]{1,0:T(8,128)(2,1)S(1)}, bf16[32,256]{1,0:T(8,128)(2,1)S(1)}, u32[]{:S(2)}, u32[]{:S(2)}) %collective-permute-start.27) | collective-permute-done | bytes 16416 | tf_op jit(solution)/shard_map/ppermute | solution.py:473
  111.1 0.8 pair.1
  111.9 0.8 tokens.1
  (55 shorter events, 1.3 us)
Async XLA Ops:
  0.6 0.9 copy-start
  2.7 17.9 %collective-permute-start.2 = (bf16[192,896]{1,0:T(8,128)(2,1)S(1)}, bf16[192,896]{1,0:T(8,128)(2,1)S(1)}, u32[]{:S(2)}, u32[]{:S(2)}) collective-permute-start(bf16[192,896]{1,0:T(8,128)(2,1)S(1)} %pad_maximum_fusion.1.refs_0_), channel_id=1, source_target_pairs={{0,2},{2,0},{4,6},{6,4},{8,10},{10,8},{12,14},{14,12},{1,3},{3,1},... | collective-permute-start | bytes 1032200 | tf_op jit(solution)/shard_map/ppermute | solution.py:89
  5.7 14.8 %collective-permute-start.1 = (bf16[192,896]{1,0:T(8,128)(2,1)S(1)}, bf16[192,896]{1,0:T(8,128)(2,1)S(1)}, u32[]{:S(2)}, u32[]{:S(2)}) collective-permute-start(bf16[192,896]{1,0:T(8,128)(2,1)S(1)} %pad_maximum_fusion.1.refs_0_), channel_id=1, source_target_pairs={{0,4},{2,6},{4,12},{6,14},{12,8},{14,10},{8,0},{10,2},{20,16},{22,... | collective-permute-start | bytes 1032200 | tf_op jit(solution)/shard_map/ppermute | solution.py:86
  7.3 18.4 %collective-permute-start = (bf16[704,512]{1,0:T(8,128)(2,1)}, bf16[704,512]{1,0:T(8,128)(2,1)S(1)}, u32[]{:S(2)}, u32[]{:S(2)}) collective-permute-start(bf16[704,512]{1,0:T(8,128)(2,1)} %bitcast.12), channel_id=1, source_target_pairs={{0,1},{1,0},{2,3},{3,2},{4,5},{5,4},{6,7},{7,6},{8,9},{9,8},{10,11... | collective-permute-start | bytes 2162696 | tf_op jit(solution)/shard_map/ppermute | solution.py:319
  8.6 5.6 %collective-permute-start.3 = (bf16[2,704]{1,0:T(2,128)(2,1)S(1)}, bf16[2,704]{1,0:T(2,128)(2,1)S(1)}, u32[]{:S(2)}, u32[]{:S(2)}) collective-permute-start(bf16[2,704]{1,0:T(2,128)(2,1)S(1)} %copy.14), channel_id=1, source_target_pairs={{0,2},{2,4},{4,6},{6,8},{8,10},{10,12},{12,14},{1,3},{3,5},{5,7},{... | collective-permute-start | bytes 8456 | tf_op jit(solution)/shard_map/ppermute | solution.py:320
  11.1 7.0 %collective-permute-start.4 = (bf16[2,704]{1,0:T(2,128)(2,1)S(1)}, bf16[2,704]{1,0:T(2,128)(2,1)S(1)}, u32[]{:S(2)}, u32[]{:S(2)}) collective-permute-start(bf16[2,704]{1,0:T(2,128)(2,1)S(1)} %copy.15), channel_id=1, source_target_pairs={{2,0},{4,2},{6,4},{8,6},{10,8},{12,10},{14,12},{3,1},{5,3},{7,5},{... | collective-permute-start | bytes 8456 | tf_op jit(solution)/shard_map/ppermute | solution.py:321
  14.1 37.9 %copy-start.5 = (f32[1536]{0:T(1024)S(1)}, f32[1536]{0:T(1024)}, u32[]{:S(2)}) copy-start(f32[1536]{0:T(1024)} %param.14) | copy-start | bytes 18436
  18.2 7.4 %collective-permute-start.5 = (bf16[16,704]{1,0:T(8,128)(2,1)S(1)}, bf16[16,704]{1,0:T(8,128)(2,1)S(1)}, u32[]{:S(2)}, u32[]{:S(2)}) collective-permute-start(bf16[16,704]{1,0:T(8,128)(2,1)S(1)} %fusion.2), channel_id=1, source_target_pairs={{0,1},{1,0},{2,3},{3,2},{4,5},{5,4},{6,7},{7,6},{8,9},{9,8},{10,11... | collective-permute-start | bytes 67592 | tf_op jit(solution)/shard_map/ppermute | solution.py:323
  20.6 15.4 %collective-permute-start.6 = (bf16[192,896]{1,0:T(8,128)(2,1)S(1)}, bf16[192,896]{1,0:T(8,128)(2,1)S(1)}, u32[]{:S(2)}, u32[]{:S(2)}) collective-permute-start(bf16[192,896]{1,0:T(8,128)(2,1)S(1)} %collective-permute-done.1.refs_2_), channel_id=1, source_target_pairs={{0,16},{16,0},{1,17},{17,1},{2,18},{18,2},{3,19},{19,3},{4,20},{20... | collective-permute-start | bytes 1032200 | tf_op jit(solution)/shard_map/ppermute | solution.py:92
  21.6 14.4 %collective-permute-start.10 = (bf16[192,896]{1,0:T(8,128)(2,1)S(1)}, bf16[192,896]{1,0:T(8,128)(2,1)S(1)}, u32[]{:S(2)}, u32[]{:S(2)}) collective-permute-start(bf16[192,896]{1,0:T(8,128)(2,1)S(1)} %collective-permute-done.1.refs_2_), channel_id=1, source_target_pairs={{0,4},{2,6},{4,12},{6,14},{12,8},{14,10},{8,0},{10,2},{20,16},{22,... | collective-permute-start | bytes 1032200 | tf_op jit(solution)/shard_map/ppermute | solution.py:86
  22.7 13.4 %collective-permute-start.8 = (bf16[192,896]{1,0:T(8,128)(2,1)S(1)}, bf16[192,896]{1,0:T(8,128)(2,1)S(1)}, u32[]{:S(2)}, u32[]{:S(2)}) collective-permute-start(bf16[192,896]{1,0:T(8,128)(2,1)S(1)} %collective-permute-done.1.refs_2_), channel_id=1, source_target_pairs={{0,2},{2,0},{4,6},{6,4},{8,10},{10,8},{12,14},{14,12},{1,3},{3,1},... | collective-permute-start | bytes 1032200 | tf_op jit(solution)/shard_map/ppermute | solution.py:89
  25.7 1.1 copy-start.2
  29.7 22.5 %copy-start.4 = (bf16[192,384]{1,0:T(8,128)(2,1)S(1)}, bf16[192,384]{1,0:T(8,128)(2,1)}, u32[]{:S(2)}) copy-start(bf16[192,384]{1,0:T(8,128)(2,1)} %get-tuple-element.38) | copy-start | bytes 442372
  29.7 58.2 %copy-start.1 = (bf16[1536,256]{1,0:T(8,128)(2,1)S(1)}, bf16[1536,256]{1,0:T(8,128)(2,1)}, u32[]{:S(2)}) copy-start(bf16[1536,256]{1,0:T(8,128)(2,1)} %pair_weight_ref.1) | copy-start | bytes 2359300
  35.9 75.1 %copy-start.3 = (bf16[128,128]{1,0:T(8,128)(2,1)S(1)}, bf16[128,128]{1,0:T(8,128)(2,1)}, u32[]{:S(2)}) copy-start(bf16[128,128]{1,0:T(8,128)(2,1)} %weight_ref.1) | copy-start | bytes 98308
  36.0 15.1 %collective-permute-start.11 = (bf16[192,896]{1,0:T(8,128)(2,1)S(1)}, bf16[192,896]{1,0:T(8,128)(2,1)S(1)}, u32[]{:S(2)}, u32[]{:S(2)}) collective-permute-start(bf16[192,896]{1,0:T(8,128)(2,1)S(1)} %collective-permute-done.10.refs_6_), channel_id=1, source_target_pairs={{0,2},{2,0},{4,6},{6,4},{8,10},{10,8},{12,14},{14,12},{1,3},{3,1},... | collective-permute-start | bytes 1032200 | tf_op jit(solution)/shard_map/ppermute | solution.py:89
  36.1 15.0 %collective-permute-start.9 = (bf16[192,896]{1,0:T(8,128)(2,1)S(1)}, bf16[192,896]{1,0:T(8,128)(2,1)S(1)}, u32[]{:S(2)}, u32[]{:S(2)}) collective-permute-start(bf16[192,896]{1,0:T(8,128)(2,1)S(1)} %collective-permute-done.8.refs_3_), channel_id=1, source_target_pairs={{0,16},{16,0},{1,17},{17,1},{2,18},{18,2},{3,19},{19,3},{4,20},{20... | collective-permute-start | bytes 1032200 | tf_op jit(solution)/shard_map/ppermute | solution.py:92
  36.6 14.5 %collective-permute-start.7 = (bf16[192,640]{1,0:T(8,128)(2,1)S(1)}, bf16[192,640]{1,0:T(8,128)(2,1)}, u32[]{:S(2)}, u32[]{:S(2)}) collective-permute-start(bf16[192,640]{1,0:T(8,128)(2,1)S(1)} %pad_maximum_fusion.2), channel_id=1, source_target_pairs={{0,2},{2,0},{4,6},{6,4},{8,10},{10,8},{12,14},{14,12},{1,3},{3,1},... | collective-permute-start | bytes 737288 | tf_op jit(solution)/shard_map/ppermute | solution.py:361
  52.0 2.0 %collective-permute-start.12 = (bf16[8,128,192]{2,1,0:T(8,128)(2,1)S(1)}, bf16[8,128,192]{2,1,0:T(8,128)(2,1)S(1)}, u32[]{:S(2)}, u32[]{:S(2)}) collective-permute-start(bf16[8,128,192]{2,1,0:T(8,128)(2,1)S(1)} %get-tuple-element.27.part_ref), channel_id=1, source_target_pairs={{0,1},{1,0},{2,3},{3,2},{4,5},{5,4},{6,7},{7,6},{8,9},{9,8},{10,11... | collective-permute-start | bytes 1179656 | tf_op jit(solution)/shard_map/ppermute | solution.py:386
  53.2 15.1 %collective-permute-start.14 = (bf16[384,640]{1,0:T(8,128)(2,1)S(1)}, bf16[384,640]{1,0:T(8,128)(2,1)S(1)}, u32[]{:S(2)}, u32[]{:S(2)}) collective-permute-start(bf16[384,640]{1,0:T(8,128)(2,1)S(1)} %pad_maximum_fusion.refs_2_.refs_0_), channel_id=1, source_target_pairs={{0,4},{2,6},{4,12},{6,14},{12,8},{14,10},{8,0},{10,2},{20,16},{22,... | collective-permute-start | bytes 1474568 | tf_op jit(solution)/shard_map/ppermute | solution.py:86
  54.6 4.7 %collective-permute-start.17 = (bf16[192,128]{1,0:T(8,128)(2,1)S(1)}, bf16[192,128]{1,0:T(8,128)(2,1)S(1)}, u32[]{:S(2)}, u32[]{:S(2)}) collective-permute-start(bf16[192,128]{1,0:T(8,128)(2,1)S(1)} %get-tuple-element.32), channel_id=1, source_target_pairs={{0,2},{2,0},{4,6},{6,4},{8,10},{10,8},{12,14},{14,12},{1,3},{3,1},... | collective-permute-start | bytes 147464 | tf_op jit(solution)/shard_map/ppermute | solution.py:403
  55.0 29.8 %collective-permute-start.13 = (bf16[8,128,192]{2,1,0:T(8,128)(2,1)S(1)}, bf16[8,128,192]{2,1,0:T(8,128)(2,1)S(1)}, u32[]{:S(2)}, u32[]{:S(2)}) collective-permute-start(bf16[8,128,192]{2,1,0:T(8,128)(2,1)S(1)} %get-tuple-element.30.refs_0_), channel_id=1, source_target_pairs={{0,2},{2,0},{4,6},{6,4},{8,10},{10,8},{12,14},{14,12},{1,3},{3,1},... | collective-permute-start | bytes 1179656 | tf_op jit(solution)/shard_map/ppermute | solution.py:404
  59.3 12.9 %collective-permute-start.18 = (bf16[2,192,128]{2,1,0:T(8,128)(2,1)S(1)}, bf16[2,192,128]{2,1,0:T(8,128)(2,1)S(1)}, u32[]{:S(2)}, u32[]{:S(2)}) collective-permute-start(bf16[2,192,128]{2,1,0:T(8,128)(2,1)S(1)} %pad_maximum_fusion.3), channel_id=1, source_target_pairs={{0,4},{2,6},{4,12},{6,14},{12,8},{14,10},{8,0},{10,2},{1,5},{3,7},... | collective-permute-start | bytes 294920 | tf_op jit(solution)/shard_map/ppermute | solution.py:406
  60.4 12.3 %collective-permute-start.19 = (bf16[2,192,128]{2,1,0:T(8,128)(2,1)S(1)}, bf16[2,192,128]{2,1,0:T(8,128)(2,1)S(1)}, u32[]{:S(2)}, u32[]{:S(2)}) collective-permute-start(bf16[2,192,128]{2,1,0:T(8,128)(2,1)S(1)} %pad_maximum_fusion.3), channel_id=1, source_target_pairs={{4,0},{6,2},{12,4},{14,6},{8,12},{10,14},{0,8},{2,10},{5,1},{7,3},... | collective-permute-start | bytes 294920 | tf_op jit(solution)/shard_map/ppermute | solution.py:407
  68.3 16.5 %collective-permute-start.15 = (bf16[384,640]{1,0:T(8,128)(2,1)S(1)}, bf16[384,640]{1,0:T(8,128)(2,1)S(1)}, u32[]{:S(2)}, u32[]{:S(2)}) collective-permute-start(bf16[384,640]{1,0:T(8,128)(2,1)S(1)} %collective-permute-done.14.refs_3_.refs_1_), channel_id=1, source_target_pairs={{0,16},{16,0},{1,17},{17,1},{2,18},{18,2},{3,19},{19,3},{4,20},{20... | collective-permute-start | bytes 1474568 | tf_op jit(solution)/shard_map/ppermute | solution.py:92
  68.3 16.5 %collective-permute-start.16 = (bf16[384,640]{1,0:T(8,128)(2,1)S(1)}, bf16[384,640]{1,0:T(8,128)(2,1)S(1)}, u32[]{:S(2)}, u32[]{:S(2)}) collective-permute-start(bf16[384,640]{1,0:T(8,128)(2,1)S(1)} %collective-permute-done.14.refs_3_.refs_1_), channel_id=1, source_target_pairs={{0,4},{2,6},{4,12},{6,14},{12,8},{14,10},{8,0},{10,2},{20,16},{22,... | collective-permute-start | bytes 1474568 | tf_op jit(solution)/shard_map/ppermute | solution.py:86
  72.2 12.5 %collective-permute-start.20 = (bf16[2,192,128]{2,1,0:T(8,128)(2,1)S(1)}, bf16[2,192,128]{2,1,0:T(8,128)(2,1)S(1)}, u32[]{:S(2)}, u32[]{:S(2)}) collective-permute-start(bf16[2,192,128]{2,1,0:T(8,128)(2,1)S(1)} %collective-permute-done.18), channel_id=1, source_target_pairs={{0,4},{2,6},{4,12},{6,14},{12,8},{14,10},{8,0},{10,2},{1,5},{3,7},... | collective-permute-start | bytes 294920 | tf_op jit(solution)/shard_map/ppermute | solution.py:408
  84.7 1.8 %collective-permute-start.21 = (bf16[8,192,128]{2,1,0:T(8,128)(2,1)S(1)}, bf16[8,192,128]{2,1,0:T(8,128)(2,1)S(1)}, u32[]{:S(2)}, u32[]{:S(2)}) collective-permute-start(bf16[8,192,128]{2,1,0:T(8,128)(2,1)S(1)} %constant_dynamic-update-slice_fusion.own_ref), channel_id=1, source_target_pairs={{0,1},{1,0},{2,3},{3,2},{4,5},{5,4},{6,7},{7,6},{8,9},{9,8},{10,11... | collective-permute-start | bytes 1179656 | tf_op jit(solution)/shard_map/ppermute | solution.py:411
  89.3 3.7 %collective-permute-start.24 = (bf16[16,256]{1,0:T(8,128)(2,1)S(1)}, bf16[16,256]{1,0:T(8,128)(2,1)S(1)}, u32[]{:S(2)}, u32[]{:S(2)}) collective-permute-start(bf16[16,256]{1,0:T(8,128)(2,1)S(1)} %get-tuple-element.35), channel_id=1, source_target_pairs={{0,2},{2,0},{4,6},{6,4},{8,10},{10,8},{12,14},{14,12},{1,3},{3,1},... | collective-permute-start | bytes 24584 | tf_op jit(solution)/shard_map/ppermute | solution.py:453
  89.6 13.9 %collective-permute-start.22 = (bf16[8,128,192]{2,1,0:T(8,128)(2,1)S(1)}, bf16[8,128,192]{2,1,0:T(8,128)(2,1)S(1)}, u32[]{:S(2)}, u32[]{:S(2)}) collective-permute-start(bf16[8,128,192]{2,1,0:T(8,128)(2,1)S(1)} %get-tuple-element.34), channel_id=1, source_target_pairs={{0,2},{2,0},{4,6},{6,4},{8,10},{10,8},{12,14},{14,12},{1,3},{3,1},... | collective-permute-start | bytes 1179656 | tf_op jit(solution)/shard_map/ppermute | solution.py:457
  93.0 10.6 %collective-permute-start.25 = (bf16[16,256]{1,0:T(8,128)(2,1)S(1)}, bf16[16,256]{1,0:T(8,128)(2,1)S(1)}, u32[]{:S(2)}, u32[]{:S(2)}) collective-permute-start(bf16[16,256]{1,0:T(8,128)(2,1)S(1)} %add_convert_fusion.2), channel_id=1, source_target_pairs={{0,1},{1,0},{2,3},{3,2},{4,5},{5,4},{6,7},{7,6},{8,9},{9,8},{10,11... | collective-permute-start | bytes 24584 | tf_op jit(solution)/shard_map/ppermute | solution.py:455
  103.6 8.3 %collective-permute-start.23 = (bf16[8,128,192]{2,1,0:T(8,128)(2,1)S(1)}, bf16[8,128,192]{2,1,0:T(8,128)(2,1)S(1)}, u32[]{:S(2)}, u32[]{:S(2)}) collective-permute-start(bf16[8,128,192]{2,1,0:T(8,128)(2,1)S(1)} %add_convert_fusion.part_ref), channel_id=1, source_target_pairs={{0,1},{1,0},{2,3},{3,2},{4,5},{5,4},{6,7},{7,6},{8,9},{9,8},{10,11... | collective-permute-start | bytes 1179656 | tf_op jit(solution)/shard_map/ppermute | solution.py:458
  103.7 3.7 %collective-permute-start.26 = (bf16[16,256]{1,0:T(8,128)(2,1)S(1)}, bf16[16,256]{1,0:T(8,128)(2,1)S(1)}, u32[]{:S(2)}, u32[]{:S(2)}) collective-permute-start(bf16[16,256]{1,0:T(8,128)(2,1)S(1)} %add_convert_fusion.1), channel_id=1, source_target_pairs={{0,4},{2,6},{4,0},{6,2},{8,12},{10,14},{12,8},{14,10},{1,5},{3,7},... | collective-permute-start | bytes 24584 | tf_op jit(solution)/shard_map/ppermute | solution.py:471
  107.4 3.6 %collective-permute-start.27 = (bf16[32,256]{1,0:T(8,128)(2,1)S(1)}, bf16[32,256]{1,0:T(8,128)(2,1)S(1)}, u32[]{:S(2)}, u32[]{:S(2)}) collective-permute-start(bf16[32,256]{1,0:T(8,128)(2,1)S(1)} %pad_maximum_fusion.4), channel_id=1, source_target_pairs={{0,8},{2,10},{4,12},{6,14},{9,1},{11,3},{13,5},{15,7},{16,24},{18,... | collective-permute-start | bytes 49160 | tf_op jit(solution)/shard_map/ppermute | solution.py:473

commit v9 on v8

--- a/solution.py
+++ b/solution.py
@@ -224,16 +224,16 @@
 
 
 def output_kernel(sides, features, attended_ref, embedded_ref, pair_weight_ref, *refs):
-    pieces, outs, pair_ref = refs[:-1 - sides], refs[-1 - sides:-1], refs[-1]
+    pieces, (keep_ref, give_ref, pair_ref, whole) = refs[:-4], refs[-4:]
     heads = attended_ref.shape[0]
     flat = jnp.concatenate([attended_ref[h] for h in range(heads)], axis=1)
-    _, tokens, width = outs[0].shape
-    share = jnp.where(lax.axis_index("col") == 0, 1.0, 0.0)
+    _, tokens, width = embedded_ref.shape
+    col = lax.axis_index("col")
+    share = jnp.where(col == 0, 1.0, 0.0)
     projected = 0.0
     for ref, rows, place in later_blocks_of(pieces):
         part = dot_nt(flat, ref[rows, features:])
-        for i, out in enumerate(outs):
-            out[place] = part[i * tokens:(i + 1) * tokens].astype(BF16)
+        whole[place] = part.astype(BF16)
         pooled = jnp.mean(part.reshape(sides * tokens // PAIR_POOL, PAIR_POOL, width), axis=1)
         first = jnp.mean(embedded_ref[place].astype(F32).reshape(tokens // PAIR_POOL, PAIR_POOL, width), axis=1) * share
         if sides > 1:
@@ -241,15 +241,20 @@
         weight = pair_weight_ref[pl.ds(pl.multiple_of(place * width, width), width)]
         projected = projected + dot_nn((pooled + first).astype(BF16), weight)
     pair_ref[...] = projected.astype(BF16)
-
-
-def token_kernel(embedded_ref, part_ref, other_ref, token_ref):
-    col = lax.axis_index("col")
+    own = keep_ref.shape[1] // sides
+    for i in range(sides):
+        rows = slice(i * own, (i + 1) * own)
+        keep_ref[:, rows] = whole[:, pl.ds(pl.multiple_of(i * tokens + col * own, own), own)]
+        give_ref[:, rows] = whole[:, pl.ds(pl.multiple_of(i * tokens + (1 - col) * own, own), own)]
+
+
+def token_kernel(embedded_ref, *refs):
+    parts, token_ref = refs[:-1], refs[-1]
     own = token_ref.shape[0]
-    mine = pl.ds(pl.multiple_of(col * own, own), own)
+    mine = pl.ds(pl.multiple_of(lax.axis_index("col") * own, own), own)
     blocks = [
-        embedded_ref[s, mine].astype(F32) + (part_ref[s, mine].astype(F32) + other_ref[s, mine].astype(F32))
-        for s in range(part_ref.shape[0])
+        embedded_ref[s, mine].astype(F32) + sum(part[s].astype(F32) for part in parts)
+        for s in range(embedded_ref.shape[0])
     ]
     token_ref[...] = jnp.concatenate(blocks, axis=1).astype(BF16)
 
@@ -319,6 +324,8 @@
     other_t = lax.ppermute(signal_t, "col", swap)
     before = lax.ppermute(signal[positions - reach:], "seq", up)
     behind = lax.ppermute(signal[:reach], "seq", [(j, i) for i, j in up])
+    if ring:
+        before, behind = after((before, behind), e.at["step"], e.at["own2"])
     own_halo = jnp.pad(jnp.concatenate([before, behind], axis=0), ((0, 16 - 2 * reach), (0, 0)))
     other_halo = lax.ppermute(own_halo, "col", swap)
     halo = jnp.where(
@@ -355,7 +362,7 @@
     if ring:
         e.at["far"] = after(e.at["far"], pooled, e.at["cross"])
         e.at["step2"] = after(e.at["step2"], pooled, e.at["cross"])
-        e.across("far", "far2")
+        e.along("step2", "far2")
         e.between("step2", "cross2")
         theirs = after(later_part(1 - side), pooled, e.at["cross"])
         received = lax.ppermute(theirs, "seq", pair_swap)
@@ -403,9 +410,9 @@
         here = jnp.stack([keyvalue, lax.ppermute(keyvalue, "seq", pair_swap)])
         both_normed.append(lax.ppermute(normed, "seq", pair_swap))
         onward = [(2 * RING[k] + i, 2 * RING[(k + 1) % 4] + i) for k in range(4) for i in range(2)]
-        ahead = lax.ppermute(here, "seq", onward)
-        back = lax.ppermute(here, "seq", [(j, i) for i, j in onward])
-        gathered = jnp.concatenate([here, ahead, back, lax.ppermute(ahead, "seq", onward)])
+        opposite = [(2 * RING[k] + i, 2 * RING[(k + 2) % 4] + i) for k in range(4) for i in range(2)]
+        turns = [onward, [(j, i) for i, j in onward], opposite]
+        gathered = jnp.concatenate([here] + [lax.ppermute(here, "seq", turn) for turn in turns])
     else:
         gathered = lax.all_gather(keyvalue, "seq", axis=0)
     gathered_other = lax.ppermute(gathered, "col", swap)
@@ -433,13 +440,13 @@
 
     out_width = rowcol_weight.shape[1]
     own_rows, pair_rows = tokens // cols, tokens // PAIR_POOL
-    *part_outs, part_pair = pl.pallas_call(
+    kept = shape((pieces, sides * own_rows, block), BF16)
+    keep, give, part_pair = pl.pallas_call(
         functools.partial(output_kernel, sides, features),
-        out_shape=tuple(
-            [shape((pieces, tokens, block), BF16)] * sides + [shape((sides * pair_rows, out_width), BF16)]
-        ),
+        out_shape=(kept, kept, shape((sides * pair_rows, out_width), BF16)),
         in_specs=vspec(3 + len(later_blocks)),
-        out_specs=vspec(sides + 1),
+        out_specs=vspec(3),
+        scratch_shapes=[pltpu.VMEM((pieces, sides * tokens, block), BF16)],
         compiler_params=params(16),
         cost_estimate=cost(2 * sides * tokens * heads * DV * width, 2 * heads * DV * width),
         name="output",
@@ -448,32 +455,33 @@
     def total(*parts):
         return sum(x.astype(F32) for x in parts).astype(BF16)
 
-    part_out = part_outs[0]
     if ring:
         turned = lax.ppermute(part_pair, "seq", pair_swap)
         part_pair = total(part_pair, jnp.concatenate([turned[pair_rows:], turned[:pair_rows]]))
     projected = total(part_pair, lax.ppermute(part_pair, "col", swap))
-    if ring:
-        part_out = total(part_out, lax.ppermute(part_outs[1], "seq", pair_swap))
-    other_out = lax.ppermute(part_out, "col", swap)
-    out_tokens = pl.pallas_call(
-        token_kernel,
-        out_shape=shape((own_rows, width), BF16),
-        in_specs=vspec(3),
-        out_specs=pl.BlockSpec(memory_space=VMEM),
-        compiler_params=params(12),
-        cost_estimate=cost(3 * own_rows * width, 8 * own_rows * width),
-        name="tokens",
-    )(embedded, part_out, other_out)
-
-    if ring:
-        rows_all = projected
+    sums = total(keep, lax.ppermute(give, "col", swap))
+
+    if ring:
+        rows_all = after(projected, sums)
         rows_all = jnp.concatenate([rows_all, lax.ppermute(rows_all, "seq", [(i, i ^ 2) for i in range(count)])])
         pairs = [(i * cols + i // 4, (i ^ 4) * cols + i // 4) for i in range(count)]
         far_rows = lax.ppermute(rows_all, ("seq", "col"), pairs)
         rows_all = jnp.where(lax.axis_index("seq") // 4 == col, rows_all, far_rows)
     else:
         rows_all = lax.all_gather(projected, "seq", axis=0, tiled=True)
+
+    parts = [sums[:, :own_rows]]
+    if ring:
+        parts.append(after(lax.ppermute(sums[:, own_rows:], "seq", pair_swap), far_rows))
+    out_tokens = pl.pallas_call(
+        token_kernel,
+        out_shape=shape((own_rows, width), BF16),
+        in_specs=vspec(1 + len(parts)),
+        out_specs=pl.BlockSpec(memory_space=VMEM),
+        compiler_params=params(12),
+        cost_estimate=cost(3 * own_rows * width, 8 * own_rows * width),
+        name="tokens",
+    )(embedded, *parts)
 
     span = pair_rows * count // cols
     pair_features = pair_weight.shape[0]

time: 114 us -> 104 us (0.912)
  waiting for transfers between devices: 57.6 us -> 51.3 us
  starting transfers between devices: 28.5 us -> 25.8 us
    ppermute x5, waiting for transfers between devices: 24.2 us -> 11 us  [the longest x3 6.49 us: on_device(): lax.ppermute(here, 'seq', turn)]
    ppermute x4 -> x5, waiting for transfers between devices: 6.04 us -> 12.2 us  [along(): self.at[target] = lax.ppermute(self.at[source], ('grp', 'seq'), pairs)]
    ppermute x1, waiting for transfers between devices: 12.4 us -> 6.6 us  [on_device(): received = lax.ppermute(theirs, 'seq', pair_swap)]
    ppermute x3, waiting for transfers between devices: 0.01 us -> 5.73 us  [between(): self.at[target] = lax.ppermute(self.at[source], 'grp', [(0, 1), (1, 0)])]
    ppermute x1, waiting for transfers between devices: 1.68 us -> 3.36 us  [on_device(): turned = lax.ppermute(part_pair, 'seq', pair_swap)]
    ppermute x4 -> x5, starting transfers between devices: 4.94 us -> 3.39 us  [along(): self.at[target] = lax.ppermute(self.at[source], ('grp', 'seq'), pairs)]
    ppermute x1, waiting for transfers between devices: 1.24 us -> 0.01 us  [on_device(): gathered_other = lax.ppermute(gathered, 'col', swap)]
    ppermute x1, starting transfers between devices: 2.01 us -> 0.8 us  [on_device(): received = lax.ppermute(theirs, 'seq', pair_swap)]
  transfers between devices with their start and end apart: 28 -> 28, of which waited for: 12 -> 15; matrix products, arithmetic and copies ran while one was open for 6% -> 7% of each run, Pallas kernels for 10% -> 11%
where the time goes in v9:
time: 104 us
  waiting for transfers between devices  51.3 us (49%)
  starting transfers between devices  25.8 us (25%)
  Pallas kernels  15.5 us (15%)
  local copies, waits for them, and re-layouts  7.66 us (7%)
  other arithmetic  2.42 us (2%)
    ppermute x5, waiting for transfers between devices, along(): self.at[target] = lax.ppermute(self.at[source], ('grp', 'seq'), pairs)  12.2 us
    ppermute x1, waiting for transfers between devices, on_device(): received = lax.ppermute(theirs, 'seq', pair_swap)  6.6 us
    ppermute x3, waiting for transfers between devices, on_device(): lax.ppermute(here, 'seq', turn)  6.49 us
    pallas_call x1, Pallas kernels, on_device(): pl.pallas_call(functools.partial(conv_kernel, positions), out_shape=shape...  6.21 us
    ppermute x2, starting transfers between devices, across(): lax.ppermute(self.at[source], 'seq', [(i, i ^ 1) for i in range(self.coun...  5.94 us
    ppermute x3, waiting for transfers between devices, between(): self.at[target] = lax.ppermute(self.at[source], 'grp', [(0, 1), (1, 0)])  5.73 us
    ppermute x3, starting transfers between devices, on_device(): lax.ppermute(here, 'seq', turn)  5.49 us
    ppermute x1, waiting for transfers between devices, on_device(): lax.ppermute(sums[:, own_rows:], 'seq', pair_swap)  4.49 us
  transfers between devices with their start and end apart: 28, of which 15 were waited for; matrix products, arithmetic and copies ran while one was open for 7% of the time, Pallas kernels for 11%

profile of v9, /device:TPU:0, one launch (start us, length us, event | category | flops | bytes accessed | tf_op | source)
XLA Modules:
  0.0 103.8 jit_solution(180387042273226262)
XLA Ops:
  0.7 0.9 copy-done
  1.6 1.1 %pad_maximum_fusion.1.refs_0_ = bf16[192,896]{1,0:T(8,128)(2,1)S(1)} fusion(bf16[192,192]{1,0:T(8,128)(2,1)S(1)} %constant_dynamic-slice_fusion.2, bf16[192,704]{1,0:T(8,128)(2,1)} %bitcast.15), kind=kLoop, calls=%fused_computation.2 | loop fusion | flops 688128 | bytes 688128 | tf_op jit(solution)/shard_map/concatenate | solution.py:298
  2.7 3.0 %collective-permute-start.2 = (bf16[192,896]{1,0:T(8,128)(2,1)S(1)}, bf16[192,896]{1,0:T(8,128)(2,1)S(1)}, u32[]{:S(2)}, u32[]{:S(2)}) collective-permute-start(bf16[192,896]{1,0:T(8,128)(2,1)S(1)} %pad_maximum_fusion.1.refs_0_), channel_id=1, source_target_pairs={{0,2},{2,0},{4,6},{6,4},{8,10},{10,8},{12,14},{14,12},{1,3},{3,1},... | collective-permute-start | bytes 1032200 | tf_op jit(solution)/shard_map/ppermute | solution.py:89
  5.7 1.6 %collective-permute-start.1 = (bf16[192,896]{1,0:T(8,128)(2,1)S(1)}, bf16[192,896]{1,0:T(8,128)(2,1)S(1)}, u32[]{:S(2)}, u32[]{:S(2)}) collective-permute-start(bf16[192,896]{1,0:T(8,128)(2,1)S(1)} %pad_maximum_fusion.1.refs_0_), channel_id=1, source_target_pairs={{0,4},{2,6},{4,12},{6,14},{12,8},{14,10},{8,0},{10,2},{20,16},{22,... | collective-permute-start | bytes 1032200 | tf_op jit(solution)/shard_map/ppermute | solution.py:86
  7.3 1.1 %fusion.3 = (bf16[2,704]{0,1:T(8,128)(2,1)S(1)}, bf16[2,704]{0,1:T(8,128)(2,1)S(1)}) fusion(bf16[512,704]{0,1:T(8,128)(2,1)} %param.10), kind=kLoop, calls=%fused_computation.25 | loop fusion | bytes 11264 | tf_op jit(solution)/shard_map/slice | solution.py:326
  8.6 2.4 %collective-permute-start.3 = (bf16[2,704]{1,0:T(2,128)(2,1)S(1)}, bf16[2,704]{1,0:T(2,128)(2,1)S(1)}, u32[]{:S(2)}, u32[]{:S(2)}) collective-permute-start(bf16[2,704]{1,0:T(2,128)(2,1)S(1)} %copy.14), channel_id=1, source_target_pairs={{0,2},{2,4},{4,6},{6,8},{8,10},{10,12},{12,14},{1,3},{3,5},{5,7},{... | collective-permute-start | bytes 8456 | tf_op jit(solution)/shard_map/ppermute | solution.py:325
  11.1 1.3 %collective-permute-start.4 = (bf16[2,704]{1,0:T(2,128)(2,1)S(1)}, bf16[2,704]{1,0:T(2,128)(2,1)S(1)}, u32[]{:S(2)}, u32[]{:S(2)}) collective-permute-start(bf16[2,704]{1,0:T(2,128)(2,1)S(1)} %copy.15), channel_id=1, source_target_pairs={{2,0},{4,2},{6,4},{8,6},{10,8},{12,10},{14,12},{3,1},{5,3},{7,5},{... | collective-permute-start | bytes 8456 | tf_op jit(solution)/shard_map/ppermute | solution.py:326
  12.5 1.7 %dynamic-slice_bitcast_fusion = (bf16[192,384]{1,0:T(8,128)(2,1)}, bf16[192,384]{1,0:T(8,128)(2,1)S(1)}) fusion(bf16[1536,192]{0,1:T(8,128)(2,1)} %param.17, s32[]{:T(128)S(6)} %select_n.49, s32[]{:T(128)S(6)} %select_n.47), kind=kLoop, calls=%fused_computation.4 | loop fusion | bytes 589832 | tf_op jit(solution)/shard_map/dynamic_slice | solution.py:312
  14.2 4.0 %collective-permute-done.4 = bf16[2,704]{1,0:T(2,128)(2,1)S(1)} collective-permute-done((bf16[2,704]{1,0:T(2,128)(2,1)S(1)}, bf16[2,704]{1,0:T(2,128)(2,1)S(1)}, u32[]{:S(2)}, u32[]{:S(2)}) %collective-permute-start.4) | collective-permute-done | bytes 2848 | tf_op jit(solution)/shard_map/ppermute | solution.py:326
  18.3 1.6 %constant_dynamic-slice_fusion = (bf16[192,256]{1,0:T(8,128)(2,1)}, bf16[192,256]{1,0:T(8,128)(2,1)S(1)}) fusion(bf16[192,1024]{1,0:T(8,128)(2,1)} %param.15, s32[]{:T(128)S(6)} %select_n.48, s32[]{:T(128)S(6)} %select_n.46), kind=kLoop, calls=%fused_computation.22 | loop fusion | bytes 393224 | tf_op jit(solution)/shard_map/dynamic_slice | solution.py:311
  19.9 0.7 reshape.10.gain_ref
  20.6 1.0 collective-permute-start.6
  21.6 1.1 %collective-permute-start.10 = (bf16[192,896]{1,0:T(8,128)(2,1)S(1)}, bf16[192,896]{1,0:T(8,128)(2,1)S(1)}, u32[]{:S(2)}, u32[]{:S(2)}) collective-permute-start(bf16[192,896]{1,0:T(8,128)(2,1)S(1)} %collective-permute-done.1.refs_2_), channel_id=1, source_target_pairs={{0,4},{2,6},{4,12},{6,14},{12,8},{14,10},{8,0},{10,2},{20,16},{22,... | collective-permute-start | bytes 1032200 | tf_op jit(solution)/shard_map/ppermute | solution.py:86
  22.6 2.9 %collective-permute-start.8 = (bf16[192,896]{1,0:T(8,128)(2,1)S(1)}, bf16[192,896]{1,0:T(8,128)(2,1)S(1)}, u32[]{:S(2)}, u32[]{:S(2)}) collective-permute-start(bf16[192,896]{1,0:T(8,128)(2,1)S(1)} %collective-permute-done.1.refs_2_), channel_id=1, source_target_pairs={{0,2},{2,0},{4,6},{6,4},{8,10},{10,8},{12,14},{14,12},{1,3},{3,1},... | collective-permute-start | bytes 1032200 | tf_op jit(solution)/shard_map/ppermute | solution.py:89
  25.7 1.1 %copy-done.2 = bf16[512,704]{0,1:T(8,128)(2,1)S(1)} copy-done((bf16[512,704]{0,1:T(8,128)(2,1)S(1)}, bf16[512,704]{0,1:T(8,128)(2,1)}, u32[]{:S(2)}) %copy-start.2) | copy-done | bytes 720920
  26.8 2.8 %act.1 = (bf16[640,1408]{1,0:T(8,128)(2,1)S(1)}, f32[128,704]{1,0:T(8,128)S(1)}) custom-call(bf16[704,512]{1,0:T(8,128)(2,1)S(1)} %bitcast.13, bf16[704,512]{1,0:T(8,128)(2,1)S(1)} %collective-permute-done.other_ref, f32[1,1408]{1,0:T(1,128)S(1)} %reshape.10.gain_ref), custom_call_target="tpu_custom_call" | custom-call | flops 922746880 | bytes 2883584 | tf_op jit(solution)/shard_map/act/pallas_call | solution.py:337
  29.6 6.2 %conv.1.pooled_ref = bf16[128,704]{1,0:T(8,128)(2,1)S(1)} custom-call(bf16[640,1408]{1,0:T(8,128)(2,1)S(1)} %get-tuple-element.24.windows_ref, f32[128,704]{1,0:T(8,128)S(1)} %get-tuple-element.25.residual_ref, bf16[16,1408]{1,0:T(8,128)(2,1)S(1)} %maximum_select_fusion.halo_ref, f32[1,1408]{1,0:T(1,128)S(1)} %reshape.10.gain_ref, bf16[5,704,1408]{2,1,0:T(8,128)(2,1)} %bitcast.14), custom_call_target="tpu_custom_call" | custom-call | flops 1268776960 | bytes 9912320 | tf_op jit(solution)/shard_map/conv/pallas_call | solution.py:352
  36.0 0.5 collective-permute-start.9
  36.5 0.8 collective-permute-start.7
  37.3 6.6 %collective-permute-done.7 = bf16[192,640]{1,0:T(8,128)(2,1)} collective-permute-done((bf16[192,640]{1,0:T(8,128)(2,1)S(1)}, bf16[192,640]{1,0:T(8,128)(2,1)}, u32[]{:S(2)}, u32[]{:S(2)}) %collective-permute-start.7) | collective-permute-done | bytes 245792 | tf_op jit(solution)/shard_map/ppermute | solution.py:368
  43.9 2.6 %collective-permute-done.11.refs_7_ = bf16[192,896]{1,0:T(8,128)(2,1)S(1)} collective-permute-done((bf16[192,896]{1,0:T(8,128)(2,1)S(1)}, bf16[192,896]{1,0:T(8,128)(2,1)S(1)}, u32[]{:S(2)}, u32[]{:S(2)}) %collective-permute-start.11) | collective-permute-done | bytes 344096 | tf_op jit(solution)/shard_map/ppermute | solution.py:86
  46.5 1.0 embed.1
  47.6 1.1 %pad_maximum_fusion.refs_2_.refs_0_ = bf16[384,640]{1,0:T(8,128)(2,1)S(1)} fusion(bf16[192,640]{1,0:T(8,128)(2,1)} %collective-permute-done.7, bf16[192,384]{1,0:T(8,128)(2,1)S(1)} %copy-done.4, bf16[192,256]{1,0:T(8,128)(2,1)} %get-tuple-element.50), kind=kLoop, calls=%fused_computation.1 | loop fusion | flops 1474560 | bytes 983040 | tf_op jit(solution)/shard_map/concatenate | solution.py:370
  48.7 0.7 collective-permute-start.14
  49.4 0.6 keyvalue.1
  50.1 0.4 collective-permute-start.17
  50.5 1.7 %collective-permute-start.13 = (bf16[8,128,192]{2,1,0:T(8,128)(2,1)S(1)}, bf16[8,128,192]{2,1,0:T(8,128)(2,1)S(1)}, u32[]{:S(2)}, u32[]{:S(2)}) collective-permute-start(bf16[8,128,192]{2,1,0:T(8,128)(2,1)S(1)} %get-tuple-element.36.refs_0_), channel_id=1, source_target_pairs={{0,2},{2,0},{4,6},{6,4},{8,10},{10,8},{12,14},{14,12},{1,3},{3,1},... | collective-permute-start | bytes 1179656 | tf_op jit(solution)/shard_map/ppermute | solution.py:411
  52.2 2.6 %collective-permute-done.17 = bf16[192,128]{1,0:T(8,128)(2,1)S(1)} collective-permute-done((bf16[192,128]{1,0:T(8,128)(2,1)S(1)}, bf16[192,128]{1,0:T(8,128)(2,1)S(1)}, u32[]{:S(2)}, u32[]{:S(2)}) %collective-permute-start.17) | collective-permute-done | bytes 49184 | tf_op jit(solution)/shard_map/ppermute | solution.py:410
  54.7 1.4 %collective-permute-start.18 = (bf16[2,192,128]{2,1,0:T(8,128)(2,1)S(1)}, bf16[2,192,128]{2,1,0:T(8,128)(2,1)S(1)}, u32[]{:S(2)}, u32[]{:S(2)}) collective-permute-start(bf16[2,192,128]{2,1,0:T(8,128)(2,1)S(1)} %pad_maximum_fusion.3), channel_id=1, source_target_pairs={{0,4},{2,6},{4,12},{6,14},{12,8},{14,10},{8,0},{10,2},{1,5},{3,7},... | collective-permute-start | bytes 294920 | tf_op jit(solution)/shard_map/ppermute | solution.py:415
  56.1 1.6 %collective-permute-start.19 = (bf16[2,192,128]{2,1,0:T(8,128)(2,1)S(1)}, bf16[2,192,128]{2,1,0:T(8,128)(2,1)S(1)}, u32[]{:S(2)}, u32[]{:S(2)}) collective-permute-start(bf16[2,192,128]{2,1,0:T(8,128)(2,1)S(1)} %pad_maximum_fusion.3), channel_id=1, source_target_pairs={{4,0},{6,2},{12,4},{14,6},{8,12},{10,14},{0,8},{2,10},{5,1},{7,3},... | collective-permute-start | bytes 294920 | tf_op jit(solution)/shard_map/ppermute | solution.py:415
  57.7 2.5 %collective-permute-start.20 = (bf16[2,192,128]{2,1,0:T(8,128)(2,1)S(1)}, bf16[2,192,128]{2,1,0:T(8,128)(2,1)S(1)}, u32[]{:S(2)}, u32[]{:S(2)}) collective-permute-start(bf16[2,192,128]{2,1,0:T(8,128)(2,1)S(1)} %pad_maximum_fusion.3), channel_id=1, source_target_pairs={{0,12},{2,14},{4,8},{6,10},{12,0},{14,2},{8,4},{10,6},{1,13},{3,15... | collective-permute-start | bytes 294920 | tf_op jit(solution)/shard_map/ppermute | solution.py:415
  60.2 3.5 %collective-permute-done.14.refs_3_.refs_1_ = bf16[384,640]{1,0:T(8,128)(2,1)S(1)} collective-permute-done((bf16[384,640]{1,0:T(8,128)(2,1)S(1)}, bf16[384,640]{1,0:T(8,128)(2,1)S(1)}, u32[]{:S(2)}, u32[]{:S(2)}) %collective-permute-start.14) | collective-permute-done | bytes 491552 | tf_op jit(solution)/shard_map/ppermute | solution.py:86
  63.7 6.0 %collective-permute-done.18 = bf16[2,192,128]{2,1,0:T(8,128)(2,1)S(1)} collective-permute-done((bf16[2,192,128]{2,1,0:T(8,128)(2,1)S(1)}, bf16[2,192,128]{2,1,0:T(8,128)(2,1)S(1)}, u32[]{:S(2)}, u32[]{:S(2)}) %collective-permute-start.18) | collective-permute-done | bytes 98336 | tf_op jit(solution)/shard_map/ppermute | solution.py:415
  69.8 0.5 collective-permute-done.20
  70.4 5.7 %collective-permute-done.15.refs_4_.refs_2_ = bf16[384,640]{1,0:T(8,128)(2,1)S(1)} collective-permute-done((bf16[384,640]{1,0:T(8,128)(2,1)S(1)}, bf16[384,640]{1,0:T(8,128)(2,1)S(1)}, u32[]{:S(2)}, u32[]{:S(2)}) %collective-permute-start.15) | collective-permute-done | bytes 491552 | tf_op jit(solution)/shard_map/ppermute | solution.py:92
  76.1 6.1 %collective-permute-done.16.refs_5_.refs_3_ = bf16[384,640]{1,0:T(8,128)(2,1)S(1)} collective-permute-done((bf16[384,640]{1,0:T(8,128)(2,1)S(1)}, bf16[384,640]{1,0:T(8,128)(2,1)S(1)}, u32[]{:S(2)}, u32[]{:S(2)}) %collective-permute-start.16) | collective-permute-done | bytes 491552 | tf_op jit(solution)/shard_map/ppermute | solution.py:86
  82.2 0.4 query.1.query_ref
  82.7 1.4 %attend.1.attended_ref = bf16[2,256,192]{2,1,0:T(8,128)(2,1)S(1)} custom-call(bf16[256,256]{1,0:T(8,128)(2,1)S(1)} %query.1.query_ref, bf16[8,192,128]{2,1,0:T(8,128)(2,1)S(1)} %constant_dynamic-update-slice_fusion.own_ref, bf16[8,192,128]{2,1,0:T(8,128)(2,1)S(1)} %collective-permute-done.21.other_ref), custom_call_target="tpu_custom_call" | custom-call | flops 167772160 | bytes 786432 | tf_op jit(solution)/shard_map/attend/pallas_call | solution.py:430
  84.1 1.4 %output.1 = (bf16[8,128,192]{2,1,0:T(8,128)(2,1)S(1)}, bf16[8,128,192]{2,1,0:T(8,128)(2,1)S(1)}, bf16[16,256]{1,0:T(8,128)(2,1)S(1)}) custom-call(bf16[2,256,192]{2,1,0:T(8,128)(2,1)S(1)} %attend.1.attended_ref, bf16[8,128,192]{2,1,0:T(8,128)(2,1)S(1)} %get-tuple-element.35.embedded_ref, bf16[1536,256]{1,0:T(8,128)(2,1)S(1)} %copy-done.1, ...), custom_call_target="tpu_custom_call" | custom-call | flops 301989888 | bytes 1179648 | tf_op jit(solution)/shard_map/output/pallas_call | solution.py:444
  85.8 3.4 %collective-permute-done.24 = bf16[16,256]{1,0:T(8,128)(2,1)S(1)} collective-permute-done((bf16[16,256]{1,0:T(8,128)(2,1)S(1)}, bf16[16,256]{1,0:T(8,128)(2,1)S(1)}, u32[]{:S(2)}, u32[]{:S(2)}) %collective-permute-start.24) | collective-permute-done | bytes 8224 | tf_op jit(solution)/shard_map/ppermute | solution.py:459
  89.3 1.1 %collective-permute-done.25 = bf16[16,256]{1,0:T(8,128)(2,1)S(1)} collective-permute-done((bf16[16,256]{1,0:T(8,128)(2,1)S(1)}, bf16[16,256]{1,0:T(8,128)(2,1)S(1)}, u32[]{:S(2)}, u32[]{:S(2)}) %collective-permute-start.25) | collective-permute-done | bytes 8224 | tf_op jit(solution)/shard_map/ppermute | solution.py:461
  90.7 3.6 %collective-permute-done.26 = bf16[16,256]{1,0:T(8,128)(2,1)S(1)} collective-permute-done((bf16[16,256]{1,0:T(8,128)(2,1)S(1)}, bf16[16,256]{1,0:T(8,128)(2,1)S(1)}, u32[]{:S(2)}, u32[]{:S(2)}) %collective-permute-start.26) | collective-permute-done | bytes 8224 | tf_op jit(solution)/shard_map/ppermute | solution.py:466
  94.3 1.9 %collective-permute-start.27 = (bf16[32,256]{1,0:T(8,128)(2,1)S(1)}, bf16[32,256]{1,0:T(8,128)(2,1)S(1)}, u32[]{:S(2)}, u32[]{:S(2)}) collective-permute-start(bf16[32,256]{1,0:T(8,128)(2,1)S(1)} %constant_dynamic-update-slice_fusion.5), channel_id=1, source_target_pairs={{0,8},{2,10},{4,12},{6,14},{9,1},{11,3},{13,5},{15,7},{16,24},{18,... | collective-permute-start | bytes 49160 | tf_op jit(solution)/shard_map/ppermute | solution.py:468
  96.2 0.4 collective-permute-start.23
  96.6 1.0 collective-permute-done.27
  97.6 0.8 pair.1
  98.5 4.5 %collective-permute-done.23.refs_1_ = bf16[8,64,192]{2,1,0:T(8,128)(2,1)S(1)} collective-permute-done((bf16[8,64,192]{2,1,0:T(8,128)(2,1)S(1)}, bf16[8,64,192]{2,1,0:T(8,128)(2,1)S(1)}, u32[]{:S(2)}, u32[]{:S(2)}) %collective-permute-start.23) | collective-permute-done | bytes 196640 | tf_op jit(solution)/shard_map/ppermute | solution.py:475
  103.0 0.8 tokens.1
  (57 shorter events, 1.7 us)
Async XLA Ops:
  0.6 0.9 copy-start
  2.7 15.5 %collective-permute-start.2 = (bf16[192,896]{1,0:T(8,128)(2,1)S(1)}, bf16[192,896]{1,0:T(8,128)(2,1)S(1)}, u32[]{:S(2)}, u32[]{:S(2)}) collective-permute-start(bf16[192,896]{1,0:T(8,128)(2,1)S(1)} %pad_maximum_fusion.1.refs_0_), channel_id=1, source_target_pairs={{0,2},{2,0},{4,6},{6,4},{8,10},{10,8},{12,14},{14,12},{1,3},{3,1},... | collective-permute-start | bytes 1032200 | tf_op jit(solution)/shard_map/ppermute | solution.py:89
  5.7 12.4 %collective-permute-start.1 = (bf16[192,896]{1,0:T(8,128)(2,1)S(1)}, bf16[192,896]{1,0:T(8,128)(2,1)S(1)}, u32[]{:S(2)}, u32[]{:S(2)}) collective-permute-start(bf16[192,896]{1,0:T(8,128)(2,1)S(1)} %pad_maximum_fusion.1.refs_0_), channel_id=1, source_target_pairs={{0,4},{2,6},{4,12},{6,14},{12,8},{14,10},{8,0},{10,2},{20,16},{22,... | collective-permute-start | bytes 1032200 | tf_op jit(solution)/shard_map/ppermute | solution.py:86
  7.3 18.3 %collective-permute-start = (bf16[704,512]{1,0:T(8,128)(2,1)}, bf16[704,512]{1,0:T(8,128)(2,1)S(1)}, u32[]{:S(2)}, u32[]{:S(2)}) collective-permute-start(bf16[704,512]{1,0:T(8,128)(2,1)} %bitcast.12), channel_id=1, source_target_pairs={{0,1},{1,0},{2,3},{3,2},{4,5},{5,4},{6,7},{7,6},{8,9},{9,8},{10,11... | collective-permute-start | bytes 2162696 | tf_op jit(solution)/shard_map/ppermute | solution.py:324
  8.6 5.6 %collective-permute-start.3 = (bf16[2,704]{1,0:T(2,128)(2,1)S(1)}, bf16[2,704]{1,0:T(2,128)(2,1)S(1)}, u32[]{:S(2)}, u32[]{:S(2)}) collective-permute-start(bf16[2,704]{1,0:T(2,128)(2,1)S(1)} %copy.14), channel_id=1, source_target_pairs={{0,2},{2,4},{4,6},{6,8},{8,10},{10,12},{12,14},{1,3},{3,5},{5,7},{... | collective-permute-start | bytes 8456 | tf_op jit(solution)/shard_map/ppermute | solution.py:325
  11.1 7.0 %collective-permute-start.4 = (bf16[2,704]{1,0:T(2,128)(2,1)S(1)}, bf16[2,704]{1,0:T(2,128)(2,1)S(1)}, u32[]{:S(2)}, u32[]{:S(2)}) collective-permute-start(bf16[2,704]{1,0:T(2,128)(2,1)S(1)} %copy.15), channel_id=1, source_target_pairs={{2,0},{4,2},{6,4},{8,6},{10,8},{12,10},{14,12},{3,1},{5,3},{7,5},{... | collective-permute-start | bytes 8456 | tf_op jit(solution)/shard_map/ppermute | solution.py:326
  14.1 33.4 %copy-start.5 = (f32[1536]{0:T(1024)S(1)}, f32[1536]{0:T(1024)}, u32[]{:S(2)}) copy-start(f32[1536]{0:T(1024)} %param.14) | copy-start | bytes 18436
  18.2 7.4 %collective-permute-start.5 = (bf16[16,704]{1,0:T(8,128)(2,1)S(1)}, bf16[16,704]{1,0:T(8,128)(2,1)S(1)}, u32[]{:S(2)}, u32[]{:S(2)}) collective-permute-start(bf16[16,704]{1,0:T(8,128)(2,1)S(1)} %fusion.2), channel_id=1, source_target_pairs={{0,1},{1,0},{2,3},{3,2},{4,5},{5,4},{6,7},{7,6},{8,9},{9,8},{10,11... | collective-permute-start | bytes 67592 | tf_op jit(solution)/shard_map/ppermute | solution.py:330
  20.6 15.3 %collective-permute-start.6 = (bf16[192,896]{1,0:T(8,128)(2,1)S(1)}, bf16[192,896]{1,0:T(8,128)(2,1)S(1)}, u32[]{:S(2)}, u32[]{:S(2)}) collective-permute-start(bf16[192,896]{1,0:T(8,128)(2,1)S(1)} %collective-permute-done.1.refs_2_), channel_id=1, source_target_pairs={{0,16},{16,0},{1,17},{17,1},{2,18},{18,2},{3,19},{19,3},{4,20},{20... | collective-permute-start | bytes 1032200 | tf_op jit(solution)/shard_map/ppermute | solution.py:92
  21.6 15.7 %collective-permute-start.10 = (bf16[192,896]{1,0:T(8,128)(2,1)S(1)}, bf16[192,896]{1,0:T(8,128)(2,1)S(1)}, u32[]{:S(2)}, u32[]{:S(2)}) collective-permute-start(bf16[192,896]{1,0:T(8,128)(2,1)S(1)} %collective-permute-done.1.refs_2_), channel_id=1, source_target_pairs={{0,4},{2,6},{4,12},{6,14},{12,8},{14,10},{8,0},{10,2},{20,16},{22,... | collective-permute-start | bytes 1032200 | tf_op jit(solution)/shard_map/ppermute | solution.py:86
  22.6 13.3 %collective-permute-start.8 = (bf16[192,896]{1,0:T(8,128)(2,1)S(1)}, bf16[192,896]{1,0:T(8,128)(2,1)S(1)}, u32[]{:S(2)}, u32[]{:S(2)}) collective-permute-start(bf16[192,896]{1,0:T(8,128)(2,1)S(1)} %collective-permute-done.1.refs_2_), channel_id=1, source_target_pairs={{0,2},{2,0},{4,6},{6,4},{8,10},{10,8},{12,14},{14,12},{1,3},{3,1},... | collective-permute-start | bytes 1032200 | tf_op jit(solution)/shard_map/ppermute | solution.py:89
  25.7 1.1 %copy-start.2 = (bf16[512,704]{0,1:T(8,128)(2,1)S(1)}, bf16[512,704]{0,1:T(8,128)(2,1)}, u32[]{:S(2)}) copy-start(bf16[512,704]{0,1:T(8,128)(2,1)} %param.10) | copy-start | bytes 2162692
  29.6 18.0 %copy-start.4 = (bf16[192,384]{1,0:T(8,128)(2,1)S(1)}, bf16[192,384]{1,0:T(8,128)(2,1)}, u32[]{:S(2)}) copy-start(bf16[192,384]{1,0:T(8,128)(2,1)} %get-tuple-element.46) | copy-start | bytes 442372
  29.6 54.5 %copy-start.1 = (bf16[1536,256]{1,0:T(8,128)(2,1)S(1)}, bf16[1536,256]{1,0:T(8,128)(2,1)}, u32[]{:S(2)}) copy-start(bf16[1536,256]{1,0:T(8,128)(2,1)} %pair_weight_ref.1) | copy-start | bytes 2359300
  35.9 61.8 %copy-start.3 = (bf16[128,128]{1,0:T(8,128)(2,1)S(1)}, bf16[128,128]{1,0:T(8,128)(2,1)}, u32[]{:S(2)}) copy-start(bf16[128,128]{1,0:T(8,128)(2,1)} %weight_ref.1) | copy-start | bytes 98308
  35.9 10.6 %collective-permute-start.11 = (bf16[192,896]{1,0:T(8,128)(2,1)S(1)}, bf16[192,896]{1,0:T(8,128)(2,1)S(1)}, u32[]{:S(2)}, u32[]{:S(2)}) collective-permute-start(bf16[192,896]{1,0:T(8,128)(2,1)S(1)} %collective-permute-done.8.refs_3_), channel_id=1, source_target_pairs={{0,4},{2,6},{4,12},{6,14},{12,8},{14,10},{8,0},{10,2},{20,16},{22,... | collective-permute-start | bytes 1032200 | tf_op jit(solution)/shard_map/ppermute | solution.py:86
  36.0 10.5 %collective-permute-start.9 = (bf16[192,896]{1,0:T(8,128)(2,1)S(1)}, bf16[192,896]{1,0:T(8,128)(2,1)S(1)}, u32[]{:S(2)}, u32[]{:S(2)}) collective-permute-start(bf16[192,896]{1,0:T(8,128)(2,1)S(1)} %collective-permute-done.8.refs_3_), channel_id=1, source_target_pairs={{0,16},{16,0},{1,17},{17,1},{2,18},{18,2},{3,19},{19,3},{4,20},{20... | collective-permute-start | bytes 1032200 | tf_op jit(solution)/shard_map/ppermute | solution.py:92
  36.5 7.4 %collective-permute-start.7 = (bf16[192,640]{1,0:T(8,128)(2,1)S(1)}, bf16[192,640]{1,0:T(8,128)(2,1)}, u32[]{:S(2)}, u32[]{:S(2)}) collective-permute-start(bf16[192,640]{1,0:T(8,128)(2,1)S(1)} %pad_maximum_fusion.2), channel_id=1, source_target_pairs={{0,2},{2,0},{4,6},{6,4},{8,10},{10,8},{12,14},{14,12},{1,3},{3,1},... | collective-permute-start | bytes 737288 | tf_op jit(solution)/shard_map/ppermute | solution.py:368
  47.4 2.0 %collective-permute-start.12 = (bf16[8,128,192]{2,1,0:T(8,128)(2,1)S(1)}, bf16[8,128,192]{2,1,0:T(8,128)(2,1)S(1)}, u32[]{:S(2)}, u32[]{:S(2)}) collective-permute-start(bf16[8,128,192]{2,1,0:T(8,128)(2,1)S(1)} %get-tuple-element.33.part_ref), channel_id=1, source_target_pairs={{0,1},{1,0},{2,3},{3,2},{4,5},{5,4},{6,7},{7,6},{8,9},{9,8},{10,11... | collective-permute-start | bytes 1179656 | tf_op jit(solution)/shard_map/ppermute | solution.py:393
  48.7 15.1 %collective-permute-start.14 = (bf16[384,640]{1,0:T(8,128)(2,1)S(1)}, bf16[384,640]{1,0:T(8,128)(2,1)S(1)}, u32[]{:S(2)}, u32[]{:S(2)}) collective-permute-start(bf16[384,640]{1,0:T(8,128)(2,1)S(1)} %pad_maximum_fusion.refs_2_.refs_0_), channel_id=1, source_target_pairs={{0,4},{2,6},{4,12},{6,14},{12,8},{14,10},{8,0},{10,2},{20,16},{22,... | collective-permute-start | bytes 1474568 | tf_op jit(solution)/shard_map/ppermute | solution.py:86
  50.1 4.7 %collective-permute-start.17 = (bf16[192,128]{1,0:T(8,128)(2,1)S(1)}, bf16[192,128]{1,0:T(8,128)(2,1)S(1)}, u32[]{:S(2)}, u32[]{:S(2)}) collective-permute-start(bf16[192,128]{1,0:T(8,128)(2,1)S(1)} %get-tuple-element.38), channel_id=1, source_target_pairs={{0,2},{2,0},{4,6},{6,4},{8,10},{10,8},{12,14},{14,12},{1,3},{3,1},... | collective-permute-start | bytes 147464 | tf_op jit(solution)/shard_map/ppermute | solution.py:410
  50.5 19.9 %collective-permute-start.13 = (bf16[8,128,192]{2,1,0:T(8,128)(2,1)S(1)}, bf16[8,128,192]{2,1,0:T(8,128)(2,1)S(1)}, u32[]{:S(2)}, u32[]{:S(2)}) collective-permute-start(bf16[8,128,192]{2,1,0:T(8,128)(2,1)S(1)} %get-tuple-element.36.refs_0_), channel_id=1, source_target_pairs={{0,2},{2,0},{4,6},{6,4},{8,10},{10,8},{12,14},{14,12},{1,3},{3,1},... | collective-permute-start | bytes 1179656 | tf_op jit(solution)/shard_map/ppermute | solution.py:411
  54.7 15.0 %collective-permute-start.18 = (bf16[2,192,128]{2,1,0:T(8,128)(2,1)S(1)}, bf16[2,192,128]{2,1,0:T(8,128)(2,1)S(1)}, u32[]{:S(2)}, u32[]{:S(2)}) collective-permute-start(bf16[2,192,128]{2,1,0:T(8,128)(2,1)S(1)} %pad_maximum_fusion.3), channel_id=1, source_target_pairs={{0,4},{2,6},{4,12},{6,14},{12,8},{14,10},{8,0},{10,2},{1,5},{3,7},... | collective-permute-start | bytes 294920 | tf_op jit(solution)/shard_map/ppermute | solution.py:415
  56.1 13.7 %collective-permute-start.19 = (bf16[2,192,128]{2,1,0:T(8,128)(2,1)S(1)}, bf16[2,192,128]{2,1,0:T(8,128)(2,1)S(1)}, u32[]{:S(2)}, u32[]{:S(2)}) collective-permute-start(bf16[2,192,128]{2,1,0:T(8,128)(2,1)S(1)} %pad_maximum_fusion.3), channel_id=1, source_target_pairs={{4,0},{6,2},{12,4},{14,6},{8,12},{10,14},{0,8},{2,10},{5,1},{7,3},... | collective-permute-start | bytes 294920 | tf_op jit(solution)/shard_map/ppermute | solution.py:415
  57.7 12.6 %collective-permute-start.20 = (bf16[2,192,128]{2,1,0:T(8,128)(2,1)S(1)}, bf16[2,192,128]{2,1,0:T(8,128)(2,1)S(1)}, u32[]{:S(2)}, u32[]{:S(2)}) collective-permute-start(bf16[2,192,128]{2,1,0:T(8,128)(2,1)S(1)} %pad_maximum_fusion.3), channel_id=1, source_target_pairs={{0,12},{2,14},{4,8},{6,10},{12,0},{14,2},{8,4},{10,6},{1,13},{3,15... | collective-permute-start | bytes 294920 | tf_op jit(solution)/shard_map/ppermute | solution.py:415
  63.7 12.4 %collective-permute-start.15 = (bf16[384,640]{1,0:T(8,128)(2,1)S(1)}, bf16[384,640]{1,0:T(8,128)(2,1)S(1)}, u32[]{:S(2)}, u32[]{:S(2)}) collective-permute-start(bf16[384,640]{1,0:T(8,128)(2,1)S(1)} %collective-permute-done.14.refs_3_.refs_1_), channel_id=1, source_target_pairs={{0,16},{16,0},{1,17},{17,1},{2,18},{18,2},{3,19},{19,3},{4,20},{20... | collective-permute-start | bytes 1474568 | tf_op jit(solution)/shard_map/ppermute | solution.py:92
  69.7 12.5 %collective-permute-start.16 = (bf16[384,640]{1,0:T(8,128)(2,1)S(1)}, bf16[384,640]{1,0:T(8,128)(2,1)S(1)}, u32[]{:S(2)}, u32[]{:S(2)}) collective-permute-start(bf16[384,640]{1,0:T(8,128)(2,1)S(1)} %collective-permute-done.14.refs_3_.refs_1_), channel_id=1, source_target_pairs={{0,4},{2,6},{4,12},{6,14},{12,8},{14,10},{8,0},{10,2},{20,16},{22,... | collective-permute-start | bytes 1474568 | tf_op jit(solution)/shard_map/ppermute | solution.py:86
  70.3 12.4 %collective-permute-start.21 = (bf16[8,192,128]{2,1,0:T(8,128)(2,1)S(1)}, bf16[8,192,128]{2,1,0:T(8,128)(2,1)S(1)}, u32[]{:S(2)}, u32[]{:S(2)}) collective-permute-start(bf16[8,192,128]{2,1,0:T(8,128)(2,1)S(1)} %constant_dynamic-update-slice_fusion.own_ref), channel_id=1, source_target_pairs={{0,1},{1,0},{2,3},{3,2},{4,5},{5,4},{6,7},{7,6},{8,9},{9,8},{10,11... | collective-permute-start | bytes 1179656 | tf_op jit(solution)/shard_map/ppermute | solution.py:418
  85.5 3.7 %collective-permute-start.24 = (bf16[16,256]{1,0:T(8,128)(2,1)S(1)}, bf16[16,256]{1,0:T(8,128)(2,1)S(1)}, u32[]{:S(2)}, u32[]{:S(2)}) collective-permute-start(bf16[16,256]{1,0:T(8,128)(2,1)S(1)} %get-tuple-element.41), channel_id=1, source_target_pairs={{0,2},{2,0},{4,6},{6,4},{8,10},{10,8},{12,14},{14,12},{1,3},{3,1},... | collective-permute-start | bytes 24584 | tf_op jit(solution)/shard_map/ppermute | solution.py:459
  85.8 4.6 %collective-permute-start.22 = (bf16[8,128,192]{2,1,0:T(8,128)(2,1)S(1)}, bf16[8,128,192]{2,1,0:T(8,128)(2,1)S(1)}, u32[]{:S(2)}, u32[]{:S(2)}) collective-permute-start(bf16[8,128,192]{2,1,0:T(8,128)(2,1)S(1)} %get-tuple-element.40), channel_id=1, source_target_pairs={{0,1},{1,0},{2,3},{3,2},{4,5},{5,4},{6,7},{7,6},{8,9},{9,8},{10,11... | collective-permute-start | bytes 1179656 | tf_op jit(solution)/shard_map/ppermute | solution.py:462
  89.2 1.2 %collective-permute-start.25 = (bf16[16,256]{1,0:T(8,128)(2,1)S(1)}, bf16[16,256]{1,0:T(8,128)(2,1)S(1)}, u32[]{:S(2)}, u32[]{:S(2)}) collective-permute-start(bf16[16,256]{1,0:T(8,128)(2,1)S(1)} %add_convert_fusion.2), channel_id=1, source_target_pairs={{0,1},{1,0},{2,3},{3,2},{4,5},{5,4},{6,7},{7,6},{8,9},{9,8},{10,11... | collective-permute-start | bytes 24584 | tf_op jit(solution)/shard_map/ppermute | solution.py:461
  90.6 3.7 %collective-permute-start.26 = (bf16[16,256]{1,0:T(8,128)(2,1)S(1)}, bf16[16,256]{1,0:T(8,128)(2,1)S(1)}, u32[]{:S(2)}, u32[]{:S(2)}) collective-permute-start(bf16[16,256]{1,0:T(8,128)(2,1)S(1)} %add_convert_fusion.1), channel_id=1, source_target_pairs={{0,4},{2,6},{4,0},{6,2},{8,12},{10,14},{12,8},{14,10},{1,5},{3,7},... | collective-permute-start | bytes 24584 | tf_op jit(solution)/shard_map/ppermute | solution.py:466
  94.3 3.3 %collective-permute-start.27 = (bf16[32,256]{1,0:T(8,128)(2,1)S(1)}, bf16[32,256]{1,0:T(8,128)(2,1)S(1)}, u32[]{:S(2)}, u32[]{:S(2)}) collective-permute-start(bf16[32,256]{1,0:T(8,128)(2,1)S(1)} %constant_dynamic-update-slice_fusion.5), channel_id=1, source_target_pairs={{0,8},{2,10},{4,12},{6,14},{9,1},{11,3},{13,5},{15,7},{16,24},{18,... | collective-permute-start | bytes 49160 | tf_op jit(solution)/shard_map/ppermute | solution.py:468
  96.2 6.7 %collective-permute-start.23 = (bf16[8,64,192]{2,1,0:T(8,128)(2,1)S(1)}, bf16[8,64,192]{2,1,0:T(8,128)(2,1)S(1)}, u32[]{:S(2)}, u32[]{:S(2)}) collective-permute-start(bf16[8,64,192]{2,1,0:T(8,128)(2,1)S(1)} %get-tuple-element.48), channel_id=1, source_target_pairs={{0,2},{2,0},{4,6},{6,4},{8,10},{10,8},{12,14},{14,12},{1,3},{3,1},... | collective-permute-start | bytes 589832 | tf_op jit(solution)/shard_map/ppermute | solution.py:475

commit v10 on v9

--- a/solution.py
+++ b/solution.py
@@ -325,13 +325,6 @@
     before = lax.ppermute(signal[positions - reach:], "seq", up)
     behind = lax.ppermute(signal[:reach], "seq", [(j, i) for i, j in up])
     if ring:
-        before, behind = after((before, behind), e.at["step"], e.at["own2"])
-    own_halo = jnp.pad(jnp.concatenate([before, behind], axis=0), ((0, 16 - 2 * reach), (0, 0)))
-    other_halo = lax.ppermute(own_halo, "col", swap)
-    halo = jnp.where(
-        col == 0, jnp.concatenate([own_halo, other_halo], axis=1), jnp.concatenate([other_halo, own_halo], axis=1)
-    )
-    if ring:
         other_t = after(other_t, e.at["step"], e.at["own2"])
     gain_row = conv_gain.reshape(1, channels)
     windows, residual = pl.pallas_call(
@@ -344,6 +337,13 @@
         cost_estimate=cost(2 * taps * tokens * channels * positions, 4 * channels * positions),
         name="act",
     )(signal_t, other_t, gain_row)
+    if ring:
+        before, behind = after((before, behind), windows)
+    own_halo = jnp.pad(jnp.concatenate([before, behind], axis=0), ((0, 16 - 2 * reach), (0, 0)))
+    other_halo = lax.ppermute(own_halo, "col", swap)
+    halo = jnp.where(
+        col == 0, jnp.concatenate([own_halo, other_halo], axis=1), jnp.concatenate([other_halo, own_halo], axis=1)
+    )
     if ring:
         e.at["step"] = after(e.at["step"], e.at["own2"])
         e.along("step", "far")
@@ -407,12 +407,10 @@
     )(part, other_part, attn_gain.reshape(pieces, 1, block), keyvalue_blocks)
     both_normed = [normed]
     if ring:
-        here = jnp.stack([keyvalue, lax.ppermute(keyvalue, "seq", pair_swap)])
         both_normed.append(lax.ppermute(normed, "seq", pair_swap))
-        onward = [(2 * RING[k] + i, 2 * RING[(k + 1) % 4] + i) for k in range(4) for i in range(2)]
-        opposite = [(2 * RING[k] + i, 2 * RING[(k + 2) % 4] + i) for k in range(4) for i in range(2)]
-        turns = [onward, [(j, i) for i, j in onward], opposite]
-        gathered = jnp.concatenate([here] + [lax.ppermute(here, "seq", turn) for turn in turns])
+        turns = [[(2 * RING[k] + i, 2 * RING[(k + t) % 4] + i) for k in range(4) for i in range(2)] for t in (1, 3, 2)]
+        row = jnp.stack([keyvalue] + [lax.ppermute(keyvalue, "seq", turn) for turn in turns])
+        gathered = jnp.concatenate([row, lax.ppermute(row, "seq", pair_swap)])
     else:
         gathered = lax.all_gather(keyvalue, "seq", axis=0)
     gathered_other = lax.ppermute(gathered, "col", swap)
@@ -462,7 +460,8 @@
     sums = total(keep, lax.ppermute(give, "col", swap))
 
     if ring:
-        rows_all = after(projected, sums)
+        sent = sums[:, own_rows:]
+        rows_all = after(projected, sent)
         rows_all = jnp.concatenate([rows_all, lax.ppermute(rows_all, "seq", [(i, i ^ 2) for i in range(count)])])
         pairs = [(i * cols + i // 4, (i ^ 4) * cols + i // 4) for i in range(count)]
         far_rows = lax.ppermute(rows_all, ("seq", "col"), pairs)
@@ -472,7 +471,7 @@
 
     parts = [sums[:, :own_rows]]
     if ring:
-        parts.append(after(lax.ppermute(sums[:, own_rows:], "seq", pair_swap), far_rows))
+        parts.append(lax.ppermute(sent, "seq", pair_swap))
     out_tokens = pl.pallas_call(
         token_kernel,
         out_shape=shape((own_rows, width), BF16),
@@ -494,7 +493,7 @@
         compiler_params=params(16),
         cost_estimate=cost(2 * pair_rows * span * pair_features**2, 2 * pair_rows * span * pair_features),
         name="pair",
-    )(projected[:pair_rows], rows_all, pair_weight)
+    )(after(projected[:pair_rows], out_tokens), rows_all, pair_weight)
     return out_tokens, pair_out
 
 

time: 104 us -> 109 us (1.048)
  starting transfers between devices: 25.8 us -> 35.2 us
  waiting for transfers between devices: 51.3 us -> 42.4 us
  local copies, waits for them, and re-layouts: 7.66 us -> 10.9 us
    ppermute x5, waiting for transfers between devices: 12.2 us -> 4.49 us  [along(): self.at[target] = lax.ppermute(self.at[source], ('grp', 'seq'), pairs)]
    ppermute x5, starting transfers between devices: 3.39 us -> 9.51 us  [along(): self.at[target] = lax.ppermute(self.at[source], ('grp', 'seq'), pairs)]
    ppermute x5, waiting for transfers between devices: 13.5 us -> 18.2 us  [the longest x3 7.95 us: on_device(): lax.ppermute(keyvalue, 'seq', turn)]
    ppermute x1, waiting for transfers between devices: 4.01 us -> 0.01 us  [on_device(): behind = lax.ppermute(signal[:reach], 'seq', [(j, i) for i, j in up])]
    ppermute x2, waiting for transfers between devices: 0.01 us -> 3.51 us  [across(): lax.ppermute(self.at[source], 'seq', [(i, i ^ 1) for i in range(self.coun...]
    unnamed x19 -> x33, local copies, waits for them, and re-layouts: 2.3 us -> 5.44 us
    ppermute x3, starting transfers between devices: 1.47 us -> 4.03 us  [between(): self.at[target] = lax.ppermute(self.at[source], 'grp', [(0, 1), (1, 0)])]
    ppermute x2, starting transfers between devices: 5.94 us -> 3.57 us  [across(): lax.ppermute(self.at[source], 'seq', [(i, i ^ 1) for i in range(self.coun...]
  transfers between devices with their start and end apart: 28 -> 28, of which waited for: 15 -> 12; matrix products, arithmetic and copies ran while one was open for 7% -> 7% of each run, Pallas kernels for 11% -> 9%
where the time goes in v10:
time: 109 us; the launch traced here: 108 us
  waiting for transfers between devices  42.4 us (39%)
  starting transfers between devices  35.2 us (32%)
  Pallas kernels  16.5 us (15%)
  local copies, waits for them, and re-layouts  10.9 us (10%)
  other arithmetic  2.4 us (2%)
    ppermute x5, starting transfers between devices, along(): self.at[target] = lax.ppermute(self.at[source], ('grp', 'seq'), pairs)  9.51 us
    ppermute x3, waiting for transfers between devices, on_device(): lax.ppermute(keyvalue, 'seq', turn)  7.95 us
    ppermute x1, waiting for transfers between devices, on_device(): received = lax.ppermute(theirs, 'seq', pair_swap)  6.27 us
    pallas_call x1, Pallas kernels, on_device(): pl.pallas_call(functools.partial(conv_kernel, positions), out_shape=shape...  6.21 us
    unnamed x33, local copies, waits for them, and re-layouts  5.44 us
    ppermute x1, waiting for transfers between devices, on_device(): gathered = jnp.concatenate([row, lax.ppermute(row, 'seq', pair_swap)])  5.24 us
    ppermute x1, waiting for transfers between devices, on_device(): parts.append(lax.ppermute(sent, 'seq', pair_swap))  4.97 us
    ppermute x3, starting transfers between devices, on_device(): lax.ppermute(keyvalue, 'seq', turn)  4.51 us
  transfers between devices with their start and end apart: 28, of which 12 were waited for; matrix products, arithmetic and copies ran while one was open for 7% of the time, Pallas kernels for 9%

profile of v10, /device:TPU:0, one launch (start us, length us, event | category | flops | bytes accessed | tf_op | source)
XLA Modules:
  0.0 108.4 jit_solution(10829651383566421596)
XLA Ops:
  1.6 1.1 pad_maximum_fusion.1.refs_0_
  2.7 3.0 %collective-permute-start.2 = (bf16[192,896]{1,0:T(8,128)(2,1)S(1)}, bf16[192,896]{1,0:T(8,128)(2,1)S(1)}, u32[]{:S(2)}, u32[]{:S(2)}) collective-permute-start(bf16[192,896]{1,0:T(8,128)(2,1)S(1)} %pad_maximum_fusion.1.refs_0_), channel_id=1, source_target_pairs={{0,2},{2,0},{4,6},{6,4},{8,10},{10,8},{12,14},{14,12},{1,3},{3,1},... | collective-permute-start | bytes 1032200 | tf_op jit(solution)/shard_map/ppermute | solution.py:89
  5.7 1.6 %collective-permute-start.1 = (bf16[192,896]{1,0:T(8,128)(2,1)S(1)}, bf16[192,896]{1,0:T(8,128)(2,1)}, u32[]{:S(2)}, u32[]{:S(2)}) collective-permute-start(bf16[192,896]{1,0:T(8,128)(2,1)S(1)} %pad_maximum_fusion.1.refs_0_), channel_id=1, source_target_pairs={{0,4},{2,6},{4,12},{6,14},{12,8},{14,10},{8,0},{10,2},{20,16},{22,... | collective-permute-start | bytes 1032200 | tf_op jit(solution)/shard_map/ppermute | solution.py:86
  7.3 1.1 %fusion.3 = (bf16[2,704]{0,1:T(8,128)(2,1)S(1)}, bf16[2,704]{0,1:T(8,128)(2,1)S(1)}) fusion(bf16[512,704]{0,1:T(8,128)(2,1)} %param.10), kind=kLoop, calls=%fused_computation.25 | loop fusion | bytes 11264 | tf_op jit(solution)/shard_map/slice | solution.py:326
  8.6 2.4 %collective-permute-start.3 = (bf16[2,704]{1,0:T(2,128)(2,1)S(1)}, bf16[2,704]{1,0:T(2,128)(2,1)S(1)}, u32[]{:S(2)}, u32[]{:S(2)}) collective-permute-start(bf16[2,704]{1,0:T(2,128)(2,1)S(1)} %copy.14), channel_id=1, source_target_pairs={{0,2},{2,4},{4,6},{6,8},{8,10},{10,12},{12,14},{1,3},{3,5},{5,7},{... | collective-permute-start | bytes 8456 | tf_op jit(solution)/shard_map/ppermute | solution.py:325
  11.1 1.3 %collective-permute-start.4 = (bf16[2,704]{1,0:T(2,128)(2,1)S(1)}, bf16[2,704]{1,0:T(2,128)(2,1)S(1)}, u32[]{:S(2)}, u32[]{:S(2)}) collective-permute-start(bf16[2,704]{1,0:T(2,128)(2,1)S(1)} %copy.15), channel_id=1, source_target_pairs={{2,0},{4,2},{6,4},{8,6},{10,8},{12,10},{14,12},{3,1},{5,3},{7,5},{... | collective-permute-start | bytes 8456 | tf_op jit(solution)/shard_map/ppermute | solution.py:326
  12.5 0.7 reshape.10.gain_ref
  13.2 1.7 %dynamic-slice_bitcast_fusion = (bf16[192,384]{1,0:T(8,128)(2,1)}, bf16[192,384]{1,0:T(8,128)(2,1)}) fusion(bf16[1536,192]{0,1:T(8,128)(2,1)} %param.17, s32[]{:T(128)S(6)} %select_n.49, s32[]{:T(128)S(6)} %select_n.47), kind=kLoop, calls=%fused_computation.5 | loop fusion | bytes 589832 | tf_op jit(solution)/shard_map/dynamic_slice | solution.py:312
  14.9 0.7 copy-done.6
  16.3 1.1 %copy-done.8 = bf16[512,704]{0,1:T(8,128)(2,1)S(1)} copy-done((bf16[512,704]{0,1:T(8,128)(2,1)S(1)}, bf16[512,704]{0,1:T(8,128)(2,1)}, u32[]{:S(2)}) %copy-start.8) | copy-done | bytes 720920
  17.4 2.9 %act.1 = (bf16[640,1408]{1,0:T(8,128)(2,1)S(1)}, f32[128,704]{1,0:T(8,128)S(1)}) custom-call(bf16[704,512]{1,0:T(8,128)(2,1)S(1)} %bitcast.17, bf16[704,512]{1,0:T(8,128)(2,1)S(1)} %collective-permute-done.other_ref, f32[1,1408]{1,0:T(1,128)S(1)} %reshape.10.gain_ref), custom_call_target="tpu_custom_call" | custom-call | flops 922746880 | bytes 2883584 | tf_op jit(solution)/shard_map/act/pallas_call | solution.py:330
  20.4 1.7 %constant_dynamic-slice_fusion = (bf16[192,256]{1,0:T(8,128)(2,1)}, bf16[192,256]{1,0:T(8,128)(2,1)}) fusion(bf16[192,1024]{1,0:T(8,128)(2,1)} %param.15, s32[]{:T(128)S(6)} %select_n.48, s32[]{:T(128)S(6)} %select_n.46), kind=kLoop, calls=%fused_computation.22 | loop fusion | bytes 393224 | tf_op jit(solution)/shard_map/dynamic_slice | solution.py:311
  22.0 1.9 %collective-permute-start.6 = (bf16[192,896]{1,0:T(8,128)(2,1)}, bf16[192,896]{1,0:T(8,128)(2,1)S(1)}, u32[]{:S(2)}, u32[]{:S(2)}) collective-permute-start(bf16[192,896]{1,0:T(8,128)(2,1)} %collective-permute-done.1.refs_2_), channel_id=1, source_target_pairs={{0,16},{16,0},{1,17},{17,1},{2,18},{18,2},{3,19},{19,3},{4,20},{20... | collective-permute-start | bytes 1032200 | tf_op jit(solution)/shard_map/ppermute | solution.py:92
  24.0 3.2 %collective-permute-start.10 = (bf16[192,896]{1,0:T(8,128)(2,1)}, bf16[192,896]{1,0:T(8,128)(2,1)S(1)}, u32[]{:S(2)}, u32[]{:S(2)}) collective-permute-start(bf16[192,896]{1,0:T(8,128)(2,1)} %collective-permute-done.1.refs_2_), channel_id=1, source_target_pairs={{0,4},{2,6},{4,12},{6,14},{12,8},{14,10},{8,0},{10,2},{20,16},{22,... | collective-permute-start | bytes 1032200 | tf_op jit(solution)/shard_map/ppermute | solution.py:86
  27.8 6.2 %conv.1.pooled_ref = bf16[128,704]{1,0:T(8,128)(2,1)S(1)} custom-call(bf16[640,1408]{1,0:T(8,128)(2,1)S(1)} %get-tuple-element.24.windows_ref, f32[128,704]{1,0:T(8,128)S(1)} %get-tuple-element.25.residual_ref, bf16[16,1408]{1,0:T(8,128)(2,1)S(1)} %maximum_select_fusion.halo_ref, f32[1,1408]{1,0:T(1,128)S(1)} %reshape.10.gain_ref, bf16[5,704,1408]{2,1,0:T(8,128)(2,1)} %bitcast.18), custom_call_target="tpu_custom_call" | custom-call | flops 1268776960 | bytes 9912320 | tf_op jit(solution)/shard_map/conv/pallas_call | solution.py:352
  34.0 3.5 %collective-permute-done.8.refs_3_ = bf16[192,896]{1,0:T(8,128)(2,1)S(1)} collective-permute-done((bf16[192,896]{1,0:T(8,128)(2,1)}, bf16[192,896]{1,0:T(8,128)(2,1)S(1)}, u32[]{:S(2)}, u32[]{:S(2)}) %collective-permute-start.8) | collective-permute-done | bytes 344096 | tf_op jit(solution)/shard_map/ppermute | solution.py:89
  37.5 1.5 %collective-permute-start.11 = (bf16[192,896]{1,0:T(8,128)(2,1)S(1)}, bf16[192,896]{1,0:T(8,128)(2,1)S(1)}, u32[]{:S(2)}, u32[]{:S(2)}) collective-permute-start(bf16[192,896]{1,0:T(8,128)(2,1)S(1)} %collective-permute-done.8.refs_3_), channel_id=1, source_target_pairs={{0,4},{2,6},{4,12},{6,14},{12,8},{14,10},{8,0},{10,2},{20,16},{22,... | collective-permute-start | bytes 1032200 | tf_op jit(solution)/shard_map/ppermute | solution.py:86
  39.0 0.6 collective-permute-start.9
  40.1 6.3 %collective-permute-done.7 = bf16[192,640]{1,0:T(8,128)(2,1)S(1)} collective-permute-done((bf16[192,640]{1,0:T(8,128)(2,1)S(1)}, bf16[192,640]{1,0:T(8,128)(2,1)S(1)}, u32[]{:S(2)}, u32[]{:S(2)}) %collective-permute-start.7) | collective-permute-done | bytes 245792 | tf_op jit(solution)/shard_map/ppermute | solution.py:368
  46.4 1.4 %collective-permute-done.11.refs_7_ = bf16[192,896]{1,0:T(8,128)(2,1)S(1)} collective-permute-done((bf16[192,896]{1,0:T(8,128)(2,1)S(1)}, bf16[192,896]{1,0:T(8,128)(2,1)S(1)}, u32[]{:S(2)}, u32[]{:S(2)}) %collective-permute-start.11) | collective-permute-done | bytes 344096 | tf_op jit(solution)/shard_map/ppermute | solution.py:86
  47.8 1.9 %embed.1 = (bf16[8,128,192]{2,1,0:T(8,128)(2,1)S(1)}, bf16[8,192,192]{2,1,0:T(8,128)(2,1)S(1)}) custom-call(bf16[128,704]{1,0:T(8,128)(2,1)S(1)} %conv.1.pooled_ref, bf16[192,896]{1,0:T(8,128)(2,1)S(1)} %pad_maximum_fusion.1.refs_0_, bf16[192,896]{1,0:T(8,128)(2,1)S(1)} %copy-done.7, bf16[192,896]{1,0:T(8,128)(2,1)} %collective-permute-done.1.refs_2_, ...), custom_call_target="tpu_custom_call" | custom-call | flops 276824064 | bytes 2162688 | tf_op jit(solution)/shard_map/embed/pallas_call | solution.py:384
  49.9 1.0 pad_maximum_fusion.refs_2_.refs_0_
  51.0 1.7 %collective-permute-start.14 = (bf16[384,640]{1,0:T(8,128)(2,1)S(1)}, bf16[384,640]{1,0:T(8,128)(2,1)S(1)}, u32[]{:S(2)}, u32[]{:S(2)}) collective-permute-start(bf16[384,640]{1,0:T(8,128)(2,1)S(1)} %pad_maximum_fusion.refs_2_.refs_0_), channel_id=1, source_target_pairs={{0,4},{2,6},{4,12},{6,14},{12,8},{14,10},{8,0},{10,2},{20,16},{22,... | collective-permute-start | bytes 1474568 | tf_op jit(solution)/shard_map/ppermute | solution.py:86
  52.7 0.8 copy-done.4
  53.5 1.0 copy-done.3
  54.5 1.0 copy-done.5
  56.2 1.2 %collective-permute-start.17 = (bf16[192,128]{1,0:T(8,128)(2,1)S(1)}, bf16[192,128]{1,0:T(8,128)(2,1)S(1)}, u32[]{:S(2)}, u32[]{:S(2)}) collective-permute-start(bf16[192,128]{1,0:T(8,128)(2,1)S(1)} %get-tuple-element.38), channel_id=1, source_target_pairs={{0,4},{2,6},{4,12},{6,14},{12,8},{14,10},{8,0},{10,2},{1,5},{3,7},... | collective-permute-start | bytes 147464 | tf_op jit(solution)/shard_map/ppermute | solution.py:412
  57.5 1.7 %collective-permute-start.18 = (bf16[192,128]{1,0:T(8,128)(2,1)S(1)}, bf16[192,128]{1,0:T(8,128)(2,1)S(1)}, u32[]{:S(2)}, u32[]{:S(2)}) collective-permute-start(bf16[192,128]{1,0:T(8,128)(2,1)S(1)} %get-tuple-element.38), channel_id=1, source_target_pairs={{0,8},{2,10},{4,0},{6,2},{12,4},{14,6},{8,12},{10,14},{1,9},{3,11}... | collective-permute-start | bytes 147464 | tf_op jit(solution)/shard_map/ppermute | solution.py:412
  59.2 1.5 %collective-permute-start.19 = (bf16[192,128]{1,0:T(8,128)(2,1)S(1)}, bf16[192,128]{1,0:T(8,128)(2,1)S(1)}, u32[]{:S(2)}, u32[]{:S(2)}) collective-permute-start(bf16[192,128]{1,0:T(8,128)(2,1)S(1)} %get-tuple-element.38), channel_id=1, source_target_pairs={{0,12},{2,14},{4,8},{6,10},{12,0},{14,2},{8,4},{10,6},{1,13},{3,15... | collective-permute-start | bytes 147464 | tf_op jit(solution)/shard_map/ppermute | solution.py:412
  61.2 7.9 %collective-permute-done.17 = bf16[192,128]{1,0:T(8,128)(2,1)S(1)} collective-permute-done((bf16[192,128]{1,0:T(8,128)(2,1)S(1)}, bf16[192,128]{1,0:T(8,128)(2,1)S(1)}, u32[]{:S(2)}, u32[]{:S(2)}) %collective-permute-start.17) | collective-permute-done | bytes 49184 | tf_op jit(solution)/shard_map/ppermute | solution.py:412
  69.2 0.7 collective-permute-start.20
  69.9 1.5 %collective-permute-start.15 = (bf16[384,640]{1,0:T(8,128)(2,1)S(1)}, bf16[384,640]{1,0:T(8,128)(2,1)S(1)}, u32[]{:S(2)}, u32[]{:S(2)}) collective-permute-start(bf16[384,640]{1,0:T(8,128)(2,1)S(1)} %collective-permute-done.14.refs_3_.refs_1_), channel_id=1, source_target_pairs={{0,16},{16,0},{1,17},{17,1},{2,18},{18,2},{3,19},{19,3},{4,20},{20... | collective-permute-start | bytes 1474568 | tf_op jit(solution)/shard_map/ppermute | solution.py:92
  71.4 1.5 %collective-permute-start.16 = (bf16[384,640]{1,0:T(8,128)(2,1)S(1)}, bf16[384,640]{1,0:T(8,128)(2,1)S(1)}, u32[]{:S(2)}, u32[]{:S(2)}) collective-permute-start(bf16[384,640]{1,0:T(8,128)(2,1)S(1)} %collective-permute-done.14.refs_3_.refs_1_), channel_id=1, source_target_pairs={{0,4},{2,6},{4,12},{6,14},{12,8},{14,10},{8,0},{10,2},{20,16},{22,... | collective-permute-start | bytes 1474568 | tf_op jit(solution)/shard_map/ppermute | solution.py:86
  72.9 5.2 %collective-permute-done.20 = bf16[4,192,128]{2,1,0:T(8,128)(2,1)S(1)} collective-permute-done((bf16[4,192,128]{2,1,0:T(8,128)(2,1)S(1)}, bf16[4,192,128]{2,1,0:T(8,128)(2,1)S(1)}, u32[]{:S(2)}, u32[]{:S(2)}) %collective-permute-start.20) | collective-permute-done | bytes 196640 | tf_op jit(solution)/shard_map/ppermute | solution.py:413
  78.3 3.9 %collective-permute-done.15.refs_4_.refs_2_ = bf16[384,640]{1,0:T(8,128)(2,1)S(1)} collective-permute-done((bf16[384,640]{1,0:T(8,128)(2,1)S(1)}, bf16[384,640]{1,0:T(8,128)(2,1)S(1)}, u32[]{:S(2)}, u32[]{:S(2)}) %collective-permute-start.15) | collective-permute-done | bytes 491552 | tf_op jit(solution)/shard_map/ppermute | solution.py:92
  82.1 2.4 %collective-permute-done.16.refs_5_.refs_3_ = bf16[384,640]{1,0:T(8,128)(2,1)S(1)} collective-permute-done((bf16[384,640]{1,0:T(8,128)(2,1)S(1)}, bf16[384,640]{1,0:T(8,128)(2,1)S(1)}, u32[]{:S(2)}, u32[]{:S(2)}) %collective-permute-start.16) | collective-permute-done | bytes 491552 | tf_op jit(solution)/shard_map/ppermute | solution.py:86
  85.0 1.4 %attend.1.attended_ref = bf16[2,256,192]{2,1,0:T(8,128)(2,1)S(1)} custom-call(bf16[256,256]{1,0:T(8,128)(2,1)S(1)} %query.1.query_ref, bf16[8,192,128]{2,1,0:T(8,128)(2,1)S(1)} %constant_dynamic-update-slice_fusion.own_ref, bf16[8,192,128]{2,1,0:T(8,128)(2,1)S(1)} %collective-permute-done.21.other_ref), custom_call_target="tpu_custom_call" | custom-call | flops 167772160 | bytes 786432 | tf_op jit(solution)/shard_map/attend/pallas_call | solution.py:428
  86.4 1.4 %output.1 = (bf16[8,128,192]{2,1,0:T(8,128)(2,1)S(1)}, bf16[8,128,192]{2,1,0:T(8,128)(2,1)S(1)}, bf16[16,256]{1,0:T(8,128)(2,1)S(1)}) custom-call(bf16[2,256,192]{2,1,0:T(8,128)(2,1)S(1)} %attend.1.attended_ref, bf16[8,128,192]{2,1,0:T(8,128)(2,1)S(1)} %get-tuple-element.35.embedded_ref, bf16[1536,256]{1,0:T(8,128)(2,1)S(1)} %copy-done.1, ...), custom_call_target="tpu_custom_call" | custom-call | flops 301989888 | bytes 1179648 | tf_op jit(solution)/shard_map/output/pallas_call | solution.py:442
  87.8 1.4 %collective-permute-start.24 = (bf16[16,256]{1,0:T(8,128)(2,1)S(1)}, bf16[16,256]{1,0:T(8,128)(2,1)S(1)}, u32[]{:S(2)}, u32[]{:S(2)}) collective-permute-start(bf16[16,256]{1,0:T(8,128)(2,1)S(1)} %get-tuple-element.41), channel_id=1, source_target_pairs={{0,2},{2,0},{4,6},{6,4},{8,10},{10,8},{12,14},{14,12},{1,3},{3,1},... | collective-permute-start | bytes 24584 | tf_op jit(solution)/shard_map/ppermute | solution.py:457
  89.2 2.3 %collective-permute-done.24 = bf16[16,256]{1,0:T(8,128)(2,1)S(1)} collective-permute-done((bf16[16,256]{1,0:T(8,128)(2,1)S(1)}, bf16[16,256]{1,0:T(8,128)(2,1)S(1)}, u32[]{:S(2)}, u32[]{:S(2)}) %collective-permute-start.24) | collective-permute-done | bytes 8224 | tf_op jit(solution)/shard_map/ppermute | solution.py:457
  91.6 1.2 %collective-permute-done.25 = bf16[16,256]{1,0:T(8,128)(2,1)S(1)} collective-permute-done((bf16[16,256]{1,0:T(8,128)(2,1)S(1)}, bf16[16,256]{1,0:T(8,128)(2,1)S(1)}, u32[]{:S(2)}, u32[]{:S(2)}) %collective-permute-start.25) | collective-permute-done | bytes 8224 | tf_op jit(solution)/shard_map/ppermute | solution.py:459
  92.9 1.0 collective-permute-start.26
  94.0 2.7 %collective-permute-done.26 = bf16[16,256]{1,0:T(8,128)(2,1)S(1)} collective-permute-done((bf16[16,256]{1,0:T(8,128)(2,1)S(1)}, bf16[16,256]{1,0:T(8,128)(2,1)S(1)}, u32[]{:S(2)}, u32[]{:S(2)}) %collective-permute-start.26) | collective-permute-done | bytes 8224 | tf_op jit(solution)/shard_map/ppermute | solution.py:465
  96.7 3.6 %collective-permute-start.27 = (bf16[32,256]{1,0:T(8,128)(2,1)S(1)}, bf16[32,256]{1,0:T(8,128)(2,1)S(1)}, u32[]{:S(2)}, u32[]{:S(2)}) collective-permute-start(bf16[32,256]{1,0:T(8,128)(2,1)S(1)} %constant_dynamic-update-slice_fusion.5), channel_id=1, source_target_pairs={{0,8},{2,10},{4,12},{6,14},{9,1},{11,3},{13,5},{15,7},{16,24},{18,... | collective-permute-start | bytes 49160 | tf_op jit(solution)/shard_map/ppermute | solution.py:467
  100.3 1.5 %collective-permute-start.23 = (bf16[8,64,192]{2,1,0:T(8,128)(2,1)S(1)}, bf16[8,64,192]{2,1,0:T(8,128)(2,1)S(1)}, u32[]{:S(2)}, u32[]{:S(2)}) collective-permute-start(bf16[8,64,192]{2,1,0:T(8,128)(2,1)S(1)} %get-tuple-element.48), channel_id=1, source_target_pairs={{0,2},{2,0},{4,6},{6,4},{8,10},{10,8},{12,14},{14,12},{1,3},{3,1},... | collective-permute-start | bytes 589832 | tf_op jit(solution)/shard_map/ppermute | solution.py:474
  101.8 5.0 %collective-permute-done.23.refs_1_ = bf16[8,64,192]{2,1,0:T(8,128)(2,1)S(1)} collective-permute-done((bf16[8,64,192]{2,1,0:T(8,128)(2,1)S(1)}, bf16[8,64,192]{2,1,0:T(8,128)(2,1)S(1)}, u32[]{:S(2)}, u32[]{:S(2)}) %collective-permute-start.23) | collective-permute-done | bytes 196640 | tf_op jit(solution)/shard_map/ppermute | solution.py:474
  106.8 0.8 tokens.1
  107.6 0.8 pair.1
  (71 shorter events, 5.2 us)
Async XLA Ops:
  0.6 0.9 copy-start
  0.6 15.6 %collective-permute-start = (bf16[704,512]{1,0:T(8,128)(2,1)}, bf16[704,512]{1,0:T(8,128)(2,1)S(1)}, u32[]{:S(2)}, u32[]{:S(2)}) collective-permute-start(bf16[704,512]{1,0:T(8,128)(2,1)} %bitcast.16), channel_id=1, source_target_pairs={{0,1},{1,0},{2,3},{3,2},{4,5},{5,4},{6,7},{7,6},{8,9},{9,8},{10,11... | collective-permute-start | bytes 2162696 | tf_op jit(solution)/shard_map/ppermute | solution.py:324
  2.7 12.2 %collective-permute-start.2 = (bf16[192,896]{1,0:T(8,128)(2,1)S(1)}, bf16[192,896]{1,0:T(8,128)(2,1)S(1)}, u32[]{:S(2)}, u32[]{:S(2)}) collective-permute-start(bf16[192,896]{1,0:T(8,128)(2,1)S(1)} %pad_maximum_fusion.1.refs_0_), channel_id=1, source_target_pairs={{0,2},{2,0},{4,6},{6,4},{8,10},{10,8},{12,14},{14,12},{1,3},{3,1},... | collective-permute-start | bytes 1032200 | tf_op jit(solution)/shard_map/ppermute | solution.py:89
  5.7 10.5 %collective-permute-start.1 = (bf16[192,896]{1,0:T(8,128)(2,1)S(1)}, bf16[192,896]{1,0:T(8,128)(2,1)}, u32[]{:S(2)}, u32[]{:S(2)}) collective-permute-start(bf16[192,896]{1,0:T(8,128)(2,1)S(1)} %pad_maximum_fusion.1.refs_0_), channel_id=1, source_target_pairs={{0,4},{2,6},{4,12},{6,14},{12,8},{14,10},{8,0},{10,2},{20,16},{22,... | collective-permute-start | bytes 1032200 | tf_op jit(solution)/shard_map/ppermute | solution.py:86
  8.6 11.7 %collective-permute-start.3 = (bf16[2,704]{1,0:T(2,128)(2,1)S(1)}, bf16[2,704]{1,0:T(2,128)(2,1)S(1)}, u32[]{:S(2)}, u32[]{:S(2)}) collective-permute-start(bf16[2,704]{1,0:T(2,128)(2,1)S(1)} %copy.14), channel_id=1, source_target_pairs={{0,2},{2,4},{4,6},{6,8},{8,10},{10,12},{12,14},{1,3},{3,5},{5,7},{... | collective-permute-start | bytes 8456 | tf_op jit(solution)/shard_map/ppermute | solution.py:325
  11.1 9.1 %collective-permute-start.4 = (bf16[2,704]{1,0:T(2,128)(2,1)S(1)}, bf16[2,704]{1,0:T(2,128)(2,1)S(1)}, u32[]{:S(2)}, u32[]{:S(2)}) collective-permute-start(bf16[2,704]{1,0:T(2,128)(2,1)S(1)} %copy.15), channel_id=1, source_target_pairs={{2,0},{4,2},{6,4},{8,6},{10,8},{12,10},{14,12},{3,1},{5,3},{7,5},{... | collective-permute-start | bytes 8456 | tf_op jit(solution)/shard_map/ppermute | solution.py:326
  13.2 36.7 %copy-start.12 = (f32[1536]{0:T(1024)S(1)}, f32[1536]{0:T(1024)}, u32[]{:S(2)}) copy-start(f32[1536]{0:T(1024)} %param.14) | copy-start | bytes 18436
  14.9 0.7 copy-start.6
  16.3 1.1 %copy-start.8 = (bf16[512,704]{0,1:T(8,128)(2,1)S(1)}, bf16[512,704]{0,1:T(8,128)(2,1)}, u32[]{:S(2)}) copy-start(bf16[512,704]{0,1:T(8,128)(2,1)} %param.10) | copy-start | bytes 2162692
  20.3 7.4 %collective-permute-start.5 = (bf16[16,704]{1,0:T(8,128)(2,1)S(1)}, bf16[16,704]{1,0:T(8,128)(2,1)S(1)}, u32[]{:S(2)}, u32[]{:S(2)}) collective-permute-start(bf16[16,704]{1,0:T(8,128)(2,1)S(1)} %fusion.2), channel_id=1, source_target_pairs={{0,1},{1,0},{2,3},{3,2},{4,5},{5,4},{6,7},{7,6},{8,9},{9,8},{10,11... | collective-permute-start | bytes 67592 | tf_op jit(solution)/shard_map/ppermute | solution.py:343
  22.0 17.6 %copy-start.10 = (bf16[192,384]{1,0:T(8,128)(2,1)S(1)}, bf16[192,384]{1,0:T(8,128)(2,1)}, u32[]{:S(2)}) copy-start(bf16[192,384]{1,0:T(8,128)(2,1)} %get-tuple-element.47) | copy-start | bytes 442372
  22.0 17.6 %copy-start.11 = (bf16[192,256]{1,0:T(8,128)(2,1)S(1)}, bf16[192,256]{1,0:T(8,128)(2,1)}, u32[]{:S(2)}) copy-start(bf16[192,256]{1,0:T(8,128)(2,1)} %get-tuple-element.51) | copy-start | bytes 294916
  22.0 25.8 %copy-start.7 = (bf16[192,896]{1,0:T(8,128)(2,1)S(1)}, bf16[192,896]{1,0:T(8,128)(2,1)}, u32[]{:S(2)}) copy-start(bf16[192,896]{1,0:T(8,128)(2,1)} %copy-done.6) | copy-start | bytes 1032196
  22.0 12.0 %collective-permute-start.6 = (bf16[192,896]{1,0:T(8,128)(2,1)}, bf16[192,896]{1,0:T(8,128)(2,1)S(1)}, u32[]{:S(2)}, u32[]{:S(2)}) collective-permute-start(bf16[192,896]{1,0:T(8,128)(2,1)} %collective-permute-done.1.refs_2_), channel_id=1, source_target_pairs={{0,16},{16,0},{1,17},{17,1},{2,18},{18,2},{3,19},{19,3},{4,20},{20... | collective-permute-start | bytes 1032200 | tf_op jit(solution)/shard_map/ppermute | solution.py:92
  24.0 16.1 %collective-permute-start.10 = (bf16[192,896]{1,0:T(8,128)(2,1)}, bf16[192,896]{1,0:T(8,128)(2,1)S(1)}, u32[]{:S(2)}, u32[]{:S(2)}) collective-permute-start(bf16[192,896]{1,0:T(8,128)(2,1)} %collective-permute-done.1.refs_2_), channel_id=1, source_target_pairs={{0,4},{2,6},{4,12},{6,14},{12,8},{14,10},{8,0},{10,2},{20,16},{22,... | collective-permute-start | bytes 1032200 | tf_op jit(solution)/shard_map/ppermute | solution.py:86
  27.2 10.4 %collective-permute-start.8 = (bf16[192,896]{1,0:T(8,128)(2,1)}, bf16[192,896]{1,0:T(8,128)(2,1)S(1)}, u32[]{:S(2)}, u32[]{:S(2)}) collective-permute-start(bf16[192,896]{1,0:T(8,128)(2,1)} %collective-permute-done.1.refs_2_), channel_id=1, source_target_pairs={{0,2},{2,0},{4,6},{6,4},{8,10},{10,8},{12,14},{14,12},{1,3},{3,1},... | collective-permute-start | bytes 1032200 | tf_op jit(solution)/shard_map/ppermute | solution.py:89
  27.8 58.6 %copy-start.1 = (bf16[1536,256]{1,0:T(8,128)(2,1)S(1)}, bf16[1536,256]{1,0:T(8,128)(2,1)}, u32[]{:S(2)}) copy-start(bf16[1536,256]{1,0:T(8,128)(2,1)} %pair_weight_ref.1) | copy-start | bytes 2359300
  34.0 73.6 %copy-start.9 = (bf16[128,128]{1,0:T(8,128)(2,1)S(1)}, bf16[128,128]{1,0:T(8,128)(2,1)}, u32[]{:S(2)}) copy-start(bf16[128,128]{1,0:T(8,128)(2,1)} %weight_ref.1) | copy-start | bytes 98308
  37.5 10.3 %collective-permute-start.11 = (bf16[192,896]{1,0:T(8,128)(2,1)S(1)}, bf16[192,896]{1,0:T(8,128)(2,1)S(1)}, u32[]{:S(2)}, u32[]{:S(2)}) collective-permute-start(bf16[192,896]{1,0:T(8,128)(2,1)S(1)} %collective-permute-done.8.refs_3_), channel_id=1, source_target_pairs={{0,4},{2,6},{4,12},{6,14},{12,8},{14,10},{8,0},{10,2},{20,16},{22,... | collective-permute-start | bytes 1032200 | tf_op jit(solution)/shard_map/ppermute | solution.py:86
  39.0 8.8 %collective-permute-start.9 = (bf16[192,896]{1,0:T(8,128)(2,1)S(1)}, bf16[192,896]{1,0:T(8,128)(2,1)S(1)}, u32[]{:S(2)}, u32[]{:S(2)}) collective-permute-start(bf16[192,896]{1,0:T(8,128)(2,1)S(1)} %collective-permute-done.8.refs_3_), channel_id=1, source_target_pairs={{0,16},{16,0},{1,17},{17,1},{2,18},{18,2},{3,19},{19,3},{4,20},{20... | collective-permute-start | bytes 1032200 | tf_op jit(solution)/shard_map/ppermute | solution.py:92
  39.7 6.7 %collective-permute-start.7 = (bf16[192,640]{1,0:T(8,128)(2,1)S(1)}, bf16[192,640]{1,0:T(8,128)(2,1)S(1)}, u32[]{:S(2)}, u32[]{:S(2)}) collective-permute-start(bf16[192,640]{1,0:T(8,128)(2,1)S(1)} %pad_maximum_fusion.2), channel_id=1, source_target_pairs={{0,2},{2,0},{4,6},{6,4},{8,10},{10,8},{12,14},{14,12},{1,3},{3,1},... | collective-permute-start | bytes 737288 | tf_op jit(solution)/shard_map/ppermute | solution.py:368
  49.8 2.9 %copy-start.2 = (bf16[8,128,192]{2,1,0:T(8,128)(2,1)}, bf16[8,128,192]{2,1,0:T(8,128)(2,1)S(1)}, u32[]{:S(2)}) copy-start(bf16[8,128,192]{2,1,0:T(8,128)(2,1)S(1)} %get-tuple-element.33.part_ref) | copy-start | bytes 1179652
  49.8 2.9 %collective-permute-start.12 = (bf16[8,128,192]{2,1,0:T(8,128)(2,1)S(1)}, bf16[8,128,192]{2,1,0:T(8,128)(2,1)S(1)}, u32[]{:S(2)}, u32[]{:S(2)}) collective-permute-start(bf16[8,128,192]{2,1,0:T(8,128)(2,1)S(1)} %get-tuple-element.33.part_ref), channel_id=1, source_target_pairs={{0,1},{1,0},{2,3},{3,2},{4,5},{5,4},{6,7},{7,6},{8,9},{9,8},{10,11... | collective-permute-start | bytes 1179656 | tf_op jit(solution)/shard_map/ppermute | solution.py:393
  51.0 18.9 %collective-permute-start.14 = (bf16[384,640]{1,0:T(8,128)(2,1)S(1)}, bf16[384,640]{1,0:T(8,128)(2,1)S(1)}, u32[]{:S(2)}, u32[]{:S(2)}) collective-permute-start(bf16[384,640]{1,0:T(8,128)(2,1)S(1)} %pad_maximum_fusion.refs_2_.refs_0_), channel_id=1, source_target_pairs={{0,4},{2,6},{4,12},{6,14},{12,8},{14,10},{8,0},{10,2},{20,16},{22,... | collective-permute-start | bytes 1474568 | tf_op jit(solution)/shard_map/ppermute | solution.py:86
  52.7 0.8 copy-start.4
  53.5 1.0 copy-start.3
  54.5 1.0 copy-start.5
  56.2 12.9 %collective-permute-start.17 = (bf16[192,128]{1,0:T(8,128)(2,1)S(1)}, bf16[192,128]{1,0:T(8,128)(2,1)S(1)}, u32[]{:S(2)}, u32[]{:S(2)}) collective-permute-start(bf16[192,128]{1,0:T(8,128)(2,1)S(1)} %get-tuple-element.38), channel_id=1, source_target_pairs={{0,4},{2,6},{4,12},{6,14},{12,8},{14,10},{8,0},{10,2},{1,5},{3,7},... | collective-permute-start | bytes 147464 | tf_op jit(solution)/shard_map/ppermute | solution.py:412
  57.5 11.7 %collective-permute-start.18 = (bf16[192,128]{1,0:T(8,128)(2,1)S(1)}, bf16[192,128]{1,0:T(8,128)(2,1)S(1)}, u32[]{:S(2)}, u32[]{:S(2)}) collective-permute-start(bf16[192,128]{1,0:T(8,128)(2,1)S(1)} %get-tuple-element.38), channel_id=1, source_target_pairs={{0,8},{2,10},{4,0},{6,2},{12,4},{14,6},{8,12},{10,14},{1,9},{3,11}... | collective-permute-start | bytes 147464 | tf_op jit(solution)/shard_map/ppermute | solution.py:412
  59.2 9.9 %collective-permute-start.19 = (bf16[192,128]{1,0:T(8,128)(2,1)S(1)}, bf16[192,128]{1,0:T(8,128)(2,1)S(1)}, u32[]{:S(2)}, u32[]{:S(2)}) collective-permute-start(bf16[192,128]{1,0:T(8,128)(2,1)S(1)} %get-tuple-element.38), channel_id=1, source_target_pairs={{0,12},{2,14},{4,8},{6,10},{12,0},{14,2},{8,4},{10,6},{1,13},{3,15... | collective-permute-start | bytes 147464 | tf_op jit(solution)/shard_map/ppermute | solution.py:412
  60.7 17.5 %collective-permute-start.13 = (bf16[8,128,192]{2,1,0:T(8,128)(2,1)S(1)}, bf16[8,128,192]{2,1,0:T(8,128)(2,1)S(1)}, u32[]{:S(2)}, u32[]{:S(2)}) collective-permute-start(bf16[8,128,192]{2,1,0:T(8,128)(2,1)S(1)} %get-tuple-element.36.refs_0_), channel_id=1, source_target_pairs={{0,2},{2,0},{4,6},{6,4},{8,10},{10,8},{12,14},{14,12},{1,3},{3,1},... | collective-permute-start | bytes 1179656 | tf_op jit(solution)/shard_map/ppermute | solution.py:410
  69.2 9.0 %collective-permute-start.20 = (bf16[4,192,128]{2,1,0:T(8,128)(2,1)S(1)}, bf16[4,192,128]{2,1,0:T(8,128)(2,1)S(1)}, u32[]{:S(2)}, u32[]{:S(2)}) collective-permute-start(bf16[4,192,128]{2,1,0:T(8,128)(2,1)S(1)} %pad_maximum_fusion.3), channel_id=1, source_target_pairs={{0,2},{2,0},{4,6},{6,4},{8,10},{10,8},{12,14},{14,12},{1,3},{3,1},... | collective-permute-start | bytes 589832 | tf_op jit(solution)/shard_map/ppermute | solution.py:413
  69.9 12.2 %collective-permute-start.15 = (bf16[384,640]{1,0:T(8,128)(2,1)S(1)}, bf16[384,640]{1,0:T(8,128)(2,1)S(1)}, u32[]{:S(2)}, u32[]{:S(2)}) collective-permute-start(bf16[384,640]{1,0:T(8,128)(2,1)S(1)} %collective-permute-done.14.refs_3_.refs_1_), channel_id=1, source_target_pairs={{0,16},{16,0},{1,17},{17,1},{2,18},{18,2},{3,19},{19,3},{4,20},{20... | collective-permute-start | bytes 1474568 | tf_op jit(solution)/shard_map/ppermute | solution.py:92
  71.4 13.2 %collective-permute-start.16 = (bf16[384,640]{1,0:T(8,128)(2,1)S(1)}, bf16[384,640]{1,0:T(8,128)(2,1)S(1)}, u32[]{:S(2)}, u32[]{:S(2)}) collective-permute-start(bf16[384,640]{1,0:T(8,128)(2,1)S(1)} %collective-permute-done.14.refs_3_.refs_1_), channel_id=1, source_target_pairs={{0,4},{2,6},{4,12},{6,14},{12,8},{14,10},{8,0},{10,2},{20,16},{22,... | collective-permute-start | bytes 1474568 | tf_op jit(solution)/shard_map/ppermute | solution.py:86
  78.2 6.8 %collective-permute-start.21 = (bf16[8,192,128]{2,1,0:T(8,128)(2,1)S(1)}, bf16[8,192,128]{2,1,0:T(8,128)(2,1)S(1)}, u32[]{:S(2)}, u32[]{:S(2)}) collective-permute-start(bf16[8,192,128]{2,1,0:T(8,128)(2,1)S(1)} %constant_dynamic-update-slice_fusion.own_ref), channel_id=1, source_target_pairs={{0,1},{1,0},{2,3},{3,2},{4,5},{5,4},{6,7},{7,6},{8,9},{9,8},{10,11... | collective-permute-start | bytes 1179656 | tf_op jit(solution)/shard_map/ppermute | solution.py:416
  87.8 3.7 %collective-permute-start.24 = (bf16[16,256]{1,0:T(8,128)(2,1)S(1)}, bf16[16,256]{1,0:T(8,128)(2,1)S(1)}, u32[]{:S(2)}, u32[]{:S(2)}) collective-permute-start(bf16[16,256]{1,0:T(8,128)(2,1)S(1)} %get-tuple-element.41), channel_id=1, source_target_pairs={{0,2},{2,0},{4,6},{6,4},{8,10},{10,8},{12,14},{14,12},{1,3},{3,1},... | collective-permute-start | bytes 24584 | tf_op jit(solution)/shard_map/ppermute | solution.py:457
  89.2 3.5 %collective-permute-start.22 = (bf16[8,128,192]{2,1,0:T(8,128)(2,1)S(1)}, bf16[8,128,192]{2,1,0:T(8,128)(2,1)S(1)}, u32[]{:S(2)}, u32[]{:S(2)}) collective-permute-start(bf16[8,128,192]{2,1,0:T(8,128)(2,1)S(1)} %get-tuple-element.40), channel_id=1, source_target_pairs={{0,1},{1,0},{2,3},{3,2},{4,5},{5,4},{6,7},{7,6},{8,9},{9,8},{10,11... | collective-permute-start | bytes 1179656 | tf_op jit(solution)/shard_map/ppermute | solution.py:460
  91.5 1.2 %collective-permute-start.25 = (bf16[16,256]{1,0:T(8,128)(2,1)S(1)}, bf16[16,256]{1,0:T(8,128)(2,1)S(1)}, u32[]{:S(2)}, u32[]{:S(2)}) collective-permute-start(bf16[16,256]{1,0:T(8,128)(2,1)S(1)} %add_convert_fusion.2), channel_id=1, source_target_pairs={{0,1},{1,0},{2,3},{3,2},{4,5},{5,4},{6,7},{7,6},{8,9},{9,8},{10,11... | collective-permute-start | bytes 24584 | tf_op jit(solution)/shard_map/ppermute | solution.py:459
  92.9 3.7 %collective-permute-start.26 = (bf16[16,256]{1,0:T(8,128)(2,1)S(1)}, bf16[16,256]{1,0:T(8,128)(2,1)S(1)}, u32[]{:S(2)}, u32[]{:S(2)}) collective-permute-start(bf16[16,256]{1,0:T(8,128)(2,1)S(1)} %add_convert_fusion.1), channel_id=1, source_target_pairs={{0,4},{2,6},{4,0},{6,2},{8,12},{10,14},{12,8},{14,10},{1,5},{3,7},... | collective-permute-start | bytes 24584 | tf_op jit(solution)/shard_map/ppermute | solution.py:465
  96.7 5.1 %collective-permute-start.27 = (bf16[32,256]{1,0:T(8,128)(2,1)S(1)}, bf16[32,256]{1,0:T(8,128)(2,1)S(1)}, u32[]{:S(2)}, u32[]{:S(2)}) collective-permute-start(bf16[32,256]{1,0:T(8,128)(2,1)S(1)} %constant_dynamic-update-slice_fusion.5), channel_id=1, source_target_pairs={{0,8},{2,10},{4,12},{6,14},{9,1},{11,3},{13,5},{15,7},{16,24},{18,... | collective-permute-start | bytes 49160 | tf_op jit(solution)/shard_map/ppermute | solution.py:467
  100.3 6.4 %collective-permute-start.23 = (bf16[8,64,192]{2,1,0:T(8,128)(2,1)S(1)}, bf16[8,64,192]{2,1,0:T(8,128)(2,1)S(1)}, u32[]{:S(2)}, u32[]{:S(2)}) collective-permute-start(bf16[8,64,192]{2,1,0:T(8,128)(2,1)S(1)} %get-tuple-element.48), channel_id=1, source_target_pairs={{0,2},{2,0},{4,6},{6,4},{8,10},{10,8},{12,14},{14,12},{1,3},{3,1},... | collective-permute-start | bytes 589832 | tf_op jit(solution)/shard_map/ppermute | solution.py:474

commit v11 on v9

--- a/solution.py
+++ b/solution.py
@@ -321,18 +321,18 @@
     if ring:
         e.along("own", "step")
         e.across("own", "own2")
-    other_t = lax.ppermute(signal_t, "col", swap)
     before = lax.ppermute(signal[positions - reach:], "seq", up)
     behind = lax.ppermute(signal[:reach], "seq", [(j, i) for i, j in up])
-    if ring:
-        before, behind = after((before, behind), e.at["step"], e.at["own2"])
+    later_mine, later_theirs = later_part(side), later_part(1 - side) if ring else None
+    ready = signal_t
+    if ring:
+        ready = after(signal_t, e.at["step"], e.at["own2"], before, behind, later_mine, later_theirs)
+    other_t = lax.ppermute(ready, "col", swap)
     own_halo = jnp.pad(jnp.concatenate([before, behind], axis=0), ((0, 16 - 2 * reach), (0, 0)))
     other_halo = lax.ppermute(own_halo, "col", swap)
     halo = jnp.where(
         col == 0, jnp.concatenate([own_halo, other_halo], axis=1), jnp.concatenate([other_halo, own_halo], axis=1)
     )
-    if ring:
-        other_t = after(other_t, e.at["step"], e.at["own2"])
     gain_row = conv_gain.reshape(1, channels)
     windows, residual = pl.pallas_call(
         functools.partial(act_kernel, taps),
@@ -364,10 +364,10 @@
         e.at["step2"] = after(e.at["step2"], pooled, e.at["cross"])
         e.along("step2", "far2")
         e.between("step2", "cross2")
-        theirs = after(later_part(1 - side), pooled, e.at["cross"])
+        theirs = after(later_theirs, pooled, e.at["cross"])
         received = lax.ppermute(theirs, "seq", pair_swap)
         pooled = after(pooled, received)
-        q = Blocks(jnp.concatenate([later_part(side), received]), count)
+        q = Blocks(jnp.concatenate([later_mine, received]), count)
         q.at["own"] = after(q.at["own"], e.at["far2"])
         q.along("own", "step")
         q.along("step", "far")
@@ -376,7 +376,7 @@
         later_blocks = [q.at[name] for name in ("own", "step", "cross", "far")]
     else:
         embed_blocks, later_blocks = (
-            [lax.all_gather(x, "seq", axis=0, tiled=True)] for x in (embed_own, later_part(0))
+            [lax.all_gather(x, "seq", axis=0, tiled=True)] for x in (embed_own, later_mine)
         )
     pieces = len(embed_blocks)
     block = width // pieces
@@ -462,8 +462,11 @@
     sums = total(keep, lax.ppermute(give, "col", swap))
 
     if ring:
-        rows_all = after(projected, sums)
+        sent = sums[:, own_rows:]
+        crossed = lax.ppermute(sent, "seq", pair_swap)
+        rows_all = after(projected, sent)
         rows_all = jnp.concatenate([rows_all, lax.ppermute(rows_all, "seq", [(i, i ^ 2) for i in range(count)])])
+        rows_all = after(rows_all, crossed)
         pairs = [(i * cols + i // 4, (i ^ 4) * cols + i // 4) for i in range(count)]
         far_rows = lax.ppermute(rows_all, ("seq", "col"), pairs)
         rows_all = jnp.where(lax.axis_index("seq") // 4 == col, rows_all, far_rows)
@@ -472,7 +475,7 @@
 
     parts = [sums[:, :own_rows]]
     if ring:
-        parts.append(after(lax.ppermute(sums[:, own_rows:], "seq", pair_swap), far_rows))
+        parts.append(crossed)
     out_tokens = pl.pallas_call(
         token_kernel,
         out_shape=shape((own_rows, width), BF16),

time: 104 us -> 103 us (level)
  the two profiles are of different devices: /device:TPU:0 before, /device:TPU:22 now
where the time goes in v11:
time: 103 us
  waiting for transfers between devices  49.8 us (48%)
  starting transfers between devices  26.2 us (25%)
  Pallas kernels  15.5 us (15%)
  local copies, waits for them, and re-layouts  7.66 us (7%)
  other arithmetic  2.41 us (2%)
    ppermute x3, waiting for transfers between devices, on_device(): lax.ppermute(here, 'seq', turn)  15.8 us
    ppermute x5, starting transfers between devices, along(): self.at[target] = lax.ppermute(self.at[source], ('grp', 'seq'), pairs)  8.27 us
    ppermute x5, waiting for transfers between devices, along(): self.at[target] = lax.ppermute(self.at[source], ('grp', 'seq'), pairs)  6.74 us
    pallas_call x1, Pallas kernels, on_device(): pl.pallas_call(functools.partial(conv_kernel, positions), out_shape=shape...  6.21 us
    ppermute x1, waiting for transfers between devices, on_device(): received = lax.ppermute(theirs, 'seq', pair_swap)  5.27 us
    ppermute x1, waiting for transfers between devices, on_device(): far_rows = lax.ppermute(rows_all, ('seq', 'col'), pairs)  4.4 us
    ppermute x1, waiting for transfers between devices, on_device(): crossed = lax.ppermute(sent, 'seq', pair_swap)  4.13 us
    ppermute x1, waiting for transfers between devices, on_device(): lax.ppermute(rows_all, 'seq', [(i, i ^ 2) for i in range(count)])  3.65 us
  transfers between devices with their start and end apart: 28, of which 16 were waited for; matrix products, arithmetic and copies ran while one was open for 7% of the time, Pallas kernels for 11%

profile of v11, /device:TPU:22, one launch (start us, length us, event | category | flops | bytes accessed | tf_op | source)
XLA Modules:
  0.0 102.6 jit_solution(4873381423664349497)
XLA Ops:
  0.7 0.9 copy-done
  1.6 1.1 %pad_maximum_fusion.1.refs_0_ = bf16[192,896]{1,0:T(8,128)(2,1)S(1)} fusion(bf16[192,192]{1,0:T(8,128)(2,1)S(1)} %constant_dynamic-slice_fusion.2, bf16[192,704]{1,0:T(8,128)(2,1)} %bitcast.15), kind=kLoop, calls=%fused_computation.2 | loop fusion | flops 688128 | bytes 688128 | tf_op jit(solution)/shard_map/concatenate | solution.py:298
  2.7 0.6 collective-permute-start.1
  3.3 1.6 %collective-permute-start = (bf16[192,896]{1,0:T(8,128)(2,1)S(1)}, bf16[192,896]{1,0:T(8,128)(2,1)S(1)}, u32[]{:S(2)}, u32[]{:S(2)}) collective-permute-start(bf16[192,896]{1,0:T(8,128)(2,1)S(1)} %pad_maximum_fusion.1.refs_0_), channel_id=1, source_target_pairs={{0,4},{2,6},{4,12},{6,14},{12,8},{14,10},{8,0},{10,2},{20,16},{22,... | collective-permute-start | bytes 1032200 | tf_op jit(solution)/shard_map/ppermute | solution.py:86
  4.9 1.1 %fusion.3 = (bf16[2,704]{0,1:T(8,128)(2,1)S(1)}, bf16[2,704]{0,1:T(8,128)(2,1)S(1)}) fusion(bf16[512,704]{0,1:T(8,128)(2,1)} %param.10), kind=kLoop, calls=%fused_computation.24 | loop fusion | bytes 11264 | tf_op jit(solution)/shard_map/slice | solution.py:325
  6.1 3.2 %collective-permute-start.2 = (bf16[2,704]{1,0:T(2,128)(2,1)S(1)}, bf16[2,704]{1,0:T(2,128)(2,1)S(1)}, u32[]{:S(2)}, u32[]{:S(2)}) collective-permute-start(bf16[2,704]{1,0:T(2,128)(2,1)S(1)} %copy.14), channel_id=1, source_target_pairs={{0,2},{2,4},{4,6},{6,8},{8,10},{10,12},{12,14},{1,3},{3,5},{5,7},{... | collective-permute-start | bytes 8456 | tf_op jit(solution)/shard_map/ppermute | solution.py:324
  9.4 2.7 %collective-permute-start.3 = (bf16[2,704]{1,0:T(2,128)(2,1)S(1)}, bf16[2,704]{1,0:T(2,128)(2,1)S(1)}, u32[]{:S(2)}, u32[]{:S(2)}) collective-permute-start(bf16[2,704]{1,0:T(2,128)(2,1)S(1)} %copy.15), channel_id=1, source_target_pairs={{2,0},{4,2},{6,4},{8,6},{10,8},{12,10},{14,12},{3,1},{5,3},{7,5},{... | collective-permute-start | bytes 8456 | tf_op jit(solution)/shard_map/ppermute | solution.py:325
  12.1 1.6 %constant_dynamic-slice_fusion.1 = (bf16[192,256]{1,0:T(8,128)(2,1)}, bf16[192,256]{1,0:T(8,128)(2,1)S(1)}) fusion(bf16[192,1024]{1,0:T(8,128)(2,1)} %param.15, s32[]{:T(128)S(6)} %select_n.44, s32[]{:T(128)S(6)} %select_n.46), kind=kLoop, calls=%fused_computation.22 | loop fusion | bytes 393224 | tf_op jit(solution)/shard_map/dynamic_slice | solution.py:311
  13.8 1.7 %dynamic-slice_bitcast_fusion.1 = (bf16[192,384]{1,0:T(8,128)(2,1)}, bf16[192,384]{1,0:T(8,128)(2,1)S(1)}) fusion(bf16[1536,192]{0,1:T(8,128)(2,1)} %param.17, s32[]{:T(128)S(6)} %select_n.45, s32[]{:T(128)S(6)} %select_n.47), kind=kLoop, calls=%fused_computation.5 | loop fusion | bytes 589832 | tf_op jit(solution)/shard_map/dynamic_slice | solution.py:312
  15.9 0.6 collective-permute-start.5
  16.5 0.7 reshape.10.gain_ref
  17.2 0.6 collective-permute-start.6
  17.8 1.5 %collective-permute-start.8 = (bf16[192,896]{1,0:T(8,128)(2,1)S(1)}, bf16[192,896]{1,0:T(8,128)(2,1)S(1)}, u32[]{:S(2)}, u32[]{:S(2)}) collective-permute-start(bf16[192,896]{1,0:T(8,128)(2,1)S(1)} %collective-permute-done.refs_2_), channel_id=1, source_target_pairs={{0,2},{2,0},{4,6},{6,4},{8,10},{10,8},{12,14},{14,12},{1,3},{3,1},... | collective-permute-start | bytes 1032200 | tf_op jit(solution)/shard_map/ppermute | solution.py:89
  19.4 1.0 %collective-permute-start.10 = (bf16[192,896]{1,0:T(8,128)(2,1)S(1)}, bf16[192,896]{1,0:T(8,128)(2,1)S(1)}, u32[]{:S(2)}, u32[]{:S(2)}) collective-permute-start(bf16[192,896]{1,0:T(8,128)(2,1)S(1)} %collective-permute-done.refs_2_), channel_id=1, source_target_pairs={{0,4},{2,6},{4,12},{6,14},{12,8},{14,10},{8,0},{10,2},{20,16},{22,... | collective-permute-start | bytes 1032200 | tf_op jit(solution)/shard_map/ppermute | solution.py:86
  20.4 1.1 %copy-done.2 = bf16[512,704]{0,1:T(8,128)(2,1)S(1)} copy-done((bf16[512,704]{0,1:T(8,128)(2,1)S(1)}, bf16[512,704]{0,1:T(8,128)(2,1)}, u32[]{:S(2)}) %copy-start.2) | copy-done | bytes 720920
  21.5 2.9 %act.1 = (bf16[640,1408]{1,0:T(8,128)(2,1)S(1)}, f32[128,704]{1,0:T(8,128)S(1)}) custom-call(bf16[704,512]{1,0:T(8,128)(2,1)S(1)} %bitcast.13, bf16[704,512]{1,0:T(8,128)(2,1)S(1)} %collective-permute-done.4.other_ref, f32[1,1408]{1,0:T(1,128)S(1)} %reshape.10.gain_ref), custom_call_target="tpu_custom_call" | custom-call | flops 922746880 | bytes 2883584 | tf_op jit(solution)/shard_map/act/pallas_call | solution.py:337
  24.4 6.2 %conv.1.pooled_ref = bf16[128,704]{1,0:T(8,128)(2,1)S(1)} custom-call(bf16[640,1408]{1,0:T(8,128)(2,1)S(1)} %get-tuple-element.22.windows_ref, f32[128,704]{1,0:T(8,128)S(1)} %get-tuple-element.23.residual_ref, bf16[16,1408]{1,0:T(8,128)(2,1)S(1)} %maximum_select_fusion.halo_ref, f32[1,1408]{1,0:T(1,128)S(1)} %reshape.10.gain_ref, bf16[5,704,1408]{2,1,0:T(8,128)(2,1)} %bitcast.14), custom_call_target="tpu_custom_call" | custom-call | flops 1268776960 | bytes 9912320 | tf_op jit(solution)/shard_map/conv/pallas_call | solution.py:352
  30.7 2.5 %collective-permute-start.11 = (bf16[192,896]{1,0:T(8,128)(2,1)S(1)}, bf16[192,896]{1,0:T(8,128)(2,1)S(1)}, u32[]{:S(2)}, u32[]{:S(2)}) collective-permute-start(bf16[192,896]{1,0:T(8,128)(2,1)S(1)} %collective-permute-done.8.refs_3_), channel_id=1, source_target_pairs={{0,4},{2,6},{4,12},{6,14},{12,8},{14,10},{8,0},{10,2},{20,16},{22,... | collective-permute-start | bytes 1032200 | tf_op jit(solution)/shard_map/ppermute | solution.py:86
  33.2 1.6 %collective-permute-start.7 = (bf16[192,640]{1,0:T(8,128)(2,1)S(1)}, bf16[192,640]{1,0:T(8,128)(2,1)}, u32[]{:S(2)}, u32[]{:S(2)}) collective-permute-start(bf16[192,640]{1,0:T(8,128)(2,1)S(1)} %pad_maximum_fusion.2), channel_id=1, source_target_pairs={{0,2},{2,0},{4,6},{6,4},{8,10},{10,8},{12,14},{14,12},{1,3},{3,1},... | collective-permute-start | bytes 737288 | tf_op jit(solution)/shard_map/ppermute | solution.py:368
  34.8 5.3 %collective-permute-done.7 = bf16[192,640]{1,0:T(8,128)(2,1)} collective-permute-done((bf16[192,640]{1,0:T(8,128)(2,1)S(1)}, bf16[192,640]{1,0:T(8,128)(2,1)}, u32[]{:S(2)}, u32[]{:S(2)}) %collective-permute-start.7) | collective-permute-done | bytes 245792 | tf_op jit(solution)/shard_map/ppermute | solution.py:368
  40.1 0.7 collective-permute-done.11.refs_7_
  40.8 1.3 %collective-permute-done.9.refs_5_ = bf16[192,896]{1,0:T(8,128)(2,1)S(1)} collective-permute-done((bf16[192,896]{1,0:T(8,128)(2,1)S(1)}, bf16[192,896]{1,0:T(8,128)(2,1)S(1)}, u32[]{:S(2)}, u32[]{:S(2)}) %collective-permute-start.9) | collective-permute-done | bytes 344096 | tf_op jit(solution)/shard_map/ppermute | solution.py:92
  42.1 1.0 embed.1
  43.2 1.1 %pad_maximum_fusion.refs_2_.refs_0_ = bf16[384,640]{1,0:T(8,128)(2,1)S(1)} fusion(bf16[192,640]{1,0:T(8,128)(2,1)} %collective-permute-done.7, bf16[192,384]{1,0:T(8,128)(2,1)S(1)} %copy-done.4, bf16[192,256]{1,0:T(8,128)(2,1)} %get-tuple-element.46), kind=kLoop, calls=%fused_computation.1 | loop fusion | flops 1474560 | bytes 983040 | tf_op jit(solution)/shard_map/concatenate | solution.py:370
  44.3 0.4 collective-permute-start.14
  45.0 0.6 keyvalue.1
  45.7 1.0 collective-permute-start.17
  46.6 1.1 %collective-permute-start.13 = (bf16[8,128,192]{2,1,0:T(8,128)(2,1)S(1)}, bf16[8,128,192]{2,1,0:T(8,128)(2,1)S(1)}, u32[]{:S(2)}, u32[]{:S(2)}) collective-permute-start(bf16[8,128,192]{2,1,0:T(8,128)(2,1)S(1)} %get-tuple-element.32.refs_0_), channel_id=1, source_target_pairs={{0,2},{2,0},{4,6},{6,4},{8,10},{10,8},{12,14},{14,12},{1,3},{3,1},... | collective-permute-start | bytes 1179656 | tf_op jit(solution)/shard_map/ppermute | solution.py:411
  47.8 2.6 %collective-permute-done.17 = bf16[192,128]{1,0:T(8,128)(2,1)S(1)} collective-permute-done((bf16[192,128]{1,0:T(8,128)(2,1)S(1)}, bf16[192,128]{1,0:T(8,128)(2,1)S(1)}, u32[]{:S(2)}, u32[]{:S(2)}) %collective-permute-start.17) | collective-permute-done | bytes 49184 | tf_op jit(solution)/shard_map/ppermute | solution.py:410
  50.4 2.3 %collective-permute-start.18 = (bf16[2,192,128]{2,1,0:T(8,128)(2,1)S(1)}, bf16[2,192,128]{2,1,0:T(8,128)(2,1)S(1)}, u32[]{:S(2)}, u32[]{:S(2)}) collective-permute-start(bf16[2,192,128]{2,1,0:T(8,128)(2,1)S(1)} %pad_maximum_fusion.3), channel_id=1, source_target_pairs={{0,4},{2,6},{4,12},{6,14},{12,8},{14,10},{8,0},{10,2},{1,5},{3,7},... | collective-permute-start | bytes 294920 | tf_op jit(solution)/shard_map/ppermute | solution.py:415
  52.6 0.6 collective-permute-start.20
  53.3 6.0 %collective-permute-done.14.refs_3_.refs_1_ = bf16[384,640]{1,0:T(8,128)(2,1)S(1)} collective-permute-done((bf16[384,640]{1,0:T(8,128)(2,1)S(1)}, bf16[384,640]{1,0:T(8,128)(2,1)S(1)}, u32[]{:S(2)}, u32[]{:S(2)}) %collective-permute-start.14) | collective-permute-done | bytes 491552 | tf_op jit(solution)/shard_map/ppermute | solution.py:86
  59.3 1.0 collective-permute-done.18
  60.3 2.7 %collective-permute-start.16 = (bf16[384,640]{1,0:T(8,128)(2,1)S(1)}, bf16[384,640]{1,0:T(8,128)(2,1)S(1)}, u32[]{:S(2)}, u32[]{:S(2)}) collective-permute-start(bf16[384,640]{1,0:T(8,128)(2,1)S(1)} %collective-permute-done.14.refs_3_.refs_1_), channel_id=1, source_target_pairs={{0,4},{2,6},{4,12},{6,14},{12,8},{14,10},{8,0},{10,2},{20,16},{22,... | collective-permute-start | bytes 1474568 | tf_op jit(solution)/shard_map/ppermute | solution.py:86
  63.0 0.6 collective-permute-done.19
  63.6 14.2 %collective-permute-done.20 = bf16[2,192,128]{2,1,0:T(8,128)(2,1)S(1)} collective-permute-done((bf16[2,192,128]{2,1,0:T(8,128)(2,1)S(1)}, bf16[2,192,128]{2,1,0:T(8,128)(2,1)S(1)}, u32[]{:S(2)}, u32[]{:S(2)}) %collective-permute-start.20) | collective-permute-done | bytes 98336 | tf_op jit(solution)/shard_map/ppermute | solution.py:415
  78.0 0.4 query.1.query_ref
  78.4 1.2 %collective-permute-done.21.other_ref = bf16[8,192,128]{2,1,0:T(8,128)(2,1)S(1)} collective-permute-done((bf16[8,192,128]{2,1,0:T(8,128)(2,1)S(1)}, bf16[8,192,128]{2,1,0:T(8,128)(2,1)S(1)}, u32[]{:S(2)}, u32[]{:S(2)}) %collective-permute-start.21) | collective-permute-done | bytes 393248 | tf_op jit(solution)/shard_map/ppermute | solution.py:418
  79.7 1.4 %attend.1.attended_ref = bf16[2,256,192]{2,1,0:T(8,128)(2,1)S(1)} custom-call(bf16[256,256]{1,0:T(8,128)(2,1)S(1)} %query.1.query_ref, bf16[8,192,128]{2,1,0:T(8,128)(2,1)S(1)} %constant_dynamic-update-slice_fusion.own_ref, bf16[8,192,128]{2,1,0:T(8,128)(2,1)S(1)} %collective-permute-done.21.other_ref), custom_call_target="tpu_custom_call" | custom-call | flops 167772160 | bytes 786432 | tf_op jit(solution)/shard_map/attend/pallas_call | solution.py:430
  81.1 1.4 %output.1 = (bf16[8,128,192]{2,1,0:T(8,128)(2,1)S(1)}, bf16[8,128,192]{2,1,0:T(8,128)(2,1)S(1)}, bf16[16,256]{1,0:T(8,128)(2,1)S(1)}) custom-call(bf16[2,256,192]{2,1,0:T(8,128)(2,1)S(1)} %attend.1.attended_ref, bf16[8,128,192]{2,1,0:T(8,128)(2,1)S(1)} %get-tuple-element.31.embedded_ref, bf16[1536,256]{1,0:T(8,128)(2,1)S(1)} %copy-done.1, ...), custom_call_target="tpu_custom_call" | custom-call | flops 301989888 | bytes 1179648 | tf_op jit(solution)/shard_map/output/pallas_call | solution.py:444
  82.8 3.4 %collective-permute-done.24 = bf16[16,256]{1,0:T(8,128)(2,1)S(1)} collective-permute-done((bf16[16,256]{1,0:T(8,128)(2,1)S(1)}, bf16[16,256]{1,0:T(8,128)(2,1)S(1)}, u32[]{:S(2)}, u32[]{:S(2)}) %collective-permute-start.24) | collective-permute-done | bytes 8224 | tf_op jit(solution)/shard_map/ppermute | solution.py:459
  86.8 0.6 collective-permute-done.25
  87.4 3.6 %collective-permute-done.26 = bf16[16,256]{1,0:T(8,128)(2,1)S(1)} collective-permute-done((bf16[16,256]{1,0:T(8,128)(2,1)S(1)}, bf16[16,256]{1,0:T(8,128)(2,1)S(1)}, u32[]{:S(2)}, u32[]{:S(2)}) %collective-permute-start.26) | collective-permute-done | bytes 8224 | tf_op jit(solution)/shard_map/ppermute | solution.py:468
  91.1 4.1 %collective-permute-done.23.refs_1_ = bf16[8,64,192]{2,1,0:T(8,128)(2,1)S(1)} collective-permute-done((bf16[8,64,192]{2,1,0:T(8,128)(2,1)S(1)}, bf16[8,64,192]{2,1,0:T(8,128)(2,1)S(1)}, u32[]{:S(2)}, u32[]{:S(2)}) %collective-permute-start.23) | collective-permute-done | bytes 196640 | tf_op jit(solution)/shard_map/ppermute | solution.py:466
  95.2 1.3 %collective-permute-start.27 = (bf16[32,256]{1,0:T(8,128)(2,1)S(1)}, bf16[32,256]{1,0:T(8,128)(2,1)S(1)}, u32[]{:S(2)}, u32[]{:S(2)}) collective-permute-start(bf16[32,256]{1,0:T(8,128)(2,1)S(1)} %pad_maximum_fusion.4), channel_id=1, source_target_pairs={{0,8},{2,10},{4,12},{6,14},{9,1},{11,3},{13,5},{15,7},{16,24},{18,... | collective-permute-start | bytes 49160 | tf_op jit(solution)/shard_map/ppermute | solution.py:471
  96.5 0.8 tokens.1
  97.3 4.4 %collective-permute-done.27 = bf16[32,256]{1,0:T(8,128)(2,1)S(1)} collective-permute-done((bf16[32,256]{1,0:T(8,128)(2,1)S(1)}, bf16[32,256]{1,0:T(8,128)(2,1)S(1)}, u32[]{:S(2)}, u32[]{:S(2)}) %collective-permute-start.27) | collective-permute-done | bytes 16416 | tf_op jit(solution)/shard_map/ppermute | solution.py:471
  101.7 0.8 pair.1
  (56 shorter events, 2.4 us)
Async XLA Ops:
  0.6 0.9 copy-start
  2.7 13.1 %collective-permute-start.1 = (bf16[192,896]{1,0:T(8,128)(2,1)S(1)}, bf16[192,896]{1,0:T(8,128)(2,1)S(1)}, u32[]{:S(2)}, u32[]{:S(2)}) collective-permute-start(bf16[192,896]{1,0:T(8,128)(2,1)S(1)} %pad_maximum_fusion.1.refs_0_), channel_id=1, source_target_pairs={{0,2},{2,0},{4,6},{6,4},{8,10},{10,8},{12,14},{14,12},{1,3},{3,1},... | collective-permute-start | bytes 1032200 | tf_op jit(solution)/shard_map/ppermute | solution.py:89
  3.3 12.6 %collective-permute-start = (bf16[192,896]{1,0:T(8,128)(2,1)S(1)}, bf16[192,896]{1,0:T(8,128)(2,1)S(1)}, u32[]{:S(2)}, u32[]{:S(2)}) collective-permute-start(bf16[192,896]{1,0:T(8,128)(2,1)S(1)} %pad_maximum_fusion.1.refs_0_), channel_id=1, source_target_pairs={{0,4},{2,6},{4,12},{6,14},{12,8},{14,10},{8,0},{10,2},{20,16},{22,... | collective-permute-start | bytes 1032200 | tf_op jit(solution)/shard_map/ppermute | solution.py:86
  6.1 9.4 %collective-permute-start.2 = (bf16[2,704]{1,0:T(2,128)(2,1)S(1)}, bf16[2,704]{1,0:T(2,128)(2,1)S(1)}, u32[]{:S(2)}, u32[]{:S(2)}) collective-permute-start(bf16[2,704]{1,0:T(2,128)(2,1)S(1)} %copy.14), channel_id=1, source_target_pairs={{0,2},{2,4},{4,6},{6,8},{8,10},{10,12},{12,14},{1,3},{3,5},{5,7},{... | collective-permute-start | bytes 8456 | tf_op jit(solution)/shard_map/ppermute | solution.py:324
  9.4 6.4 %collective-permute-start.3 = (bf16[2,704]{1,0:T(2,128)(2,1)S(1)}, bf16[2,704]{1,0:T(2,128)(2,1)S(1)}, u32[]{:S(2)}, u32[]{:S(2)}) collective-permute-start(bf16[2,704]{1,0:T(2,128)(2,1)S(1)} %copy.15), channel_id=1, source_target_pairs={{2,0},{4,2},{6,4},{8,6},{10,8},{12,10},{14,12},{3,1},{5,3},{7,5},{... | collective-permute-start | bytes 8456 | tf_op jit(solution)/shard_map/ppermute | solution.py:325
  13.8 29.4 %copy-start.5 = (f32[1536]{0:T(1024)S(1)}, f32[1536]{0:T(1024)}, u32[]{:S(2)}) copy-start(f32[1536]{0:T(1024)} %param.14) | copy-start | bytes 18436
  15.9 4.6 %collective-permute-start.4 = (bf16[704,512]{1,0:T(8,128)(2,1)}, bf16[704,512]{1,0:T(8,128)(2,1)S(1)}, u32[]{:S(2)}, u32[]{:S(2)}) collective-permute-start(bf16[704,512]{1,0:T(8,128)(2,1)} %bitcast.12), channel_id=1, source_target_pairs={{0,1},{1,0},{2,3},{3,2},{4,5},{5,4},{6,7},{7,6},{8,9},{9,8},{10,11... | collective-permute-start | bytes 2162696 | tf_op jit(solution)/shard_map/ppermute | solution.py:330
  15.9 3.4 %collective-permute-start.5 = (bf16[16,704]{1,0:T(8,128)(2,1)S(1)}, bf16[16,704]{1,0:T(8,128)(2,1)S(1)}, u32[]{:S(2)}, u32[]{:S(2)}) collective-permute-start(bf16[16,704]{1,0:T(8,128)(2,1)S(1)} %fusion.2), channel_id=1, source_target_pairs={{0,1},{1,0},{2,3},{3,2},{4,5},{5,4},{6,7},{7,6},{8,9},{9,8},{10,11... | collective-permute-start | bytes 67592 | tf_op jit(solution)/shard_map/ppermute | solution.py:332
  17.2 13.5 %collective-permute-start.6 = (bf16[192,896]{1,0:T(8,128)(2,1)S(1)}, bf16[192,896]{1,0:T(8,128)(2,1)S(1)}, u32[]{:S(2)}, u32[]{:S(2)}) collective-permute-start(bf16[192,896]{1,0:T(8,128)(2,1)S(1)} %collective-permute-done.refs_2_), channel_id=1, source_target_pairs={{0,16},{16,0},{1,17},{17,1},{2,18},{18,2},{3,19},{19,3},{4,20},{20... | collective-permute-start | bytes 1032200 | tf_op jit(solution)/shard_map/ppermute | solution.py:92
  17.8 12.9 %collective-permute-start.8 = (bf16[192,896]{1,0:T(8,128)(2,1)S(1)}, bf16[192,896]{1,0:T(8,128)(2,1)S(1)}, u32[]{:S(2)}, u32[]{:S(2)}) collective-permute-start(bf16[192,896]{1,0:T(8,128)(2,1)S(1)} %collective-permute-done.refs_2_), channel_id=1, source_target_pairs={{0,2},{2,0},{4,6},{6,4},{8,10},{10,8},{12,14},{14,12},{1,3},{3,1},... | collective-permute-start | bytes 1032200 | tf_op jit(solution)/shard_map/ppermute | solution.py:89
  19.4 15.4 %collective-permute-start.10 = (bf16[192,896]{1,0:T(8,128)(2,1)S(1)}, bf16[192,896]{1,0:T(8,128)(2,1)S(1)}, u32[]{:S(2)}, u32[]{:S(2)}) collective-permute-start(bf16[192,896]{1,0:T(8,128)(2,1)S(1)} %collective-permute-done.refs_2_), channel_id=1, source_target_pairs={{0,4},{2,6},{4,12},{6,14},{12,8},{14,10},{8,0},{10,2},{20,16},{22,... | collective-permute-start | bytes 1032200 | tf_op jit(solution)/shard_map/ppermute | solution.py:86
  20.4 1.1 %copy-start.2 = (bf16[512,704]{0,1:T(8,128)(2,1)S(1)}, bf16[512,704]{0,1:T(8,128)(2,1)}, u32[]{:S(2)}) copy-start(bf16[512,704]{0,1:T(8,128)(2,1)} %param.10) | copy-start | bytes 2162692
  24.4 18.8 %copy-start.4 = (bf16[192,384]{1,0:T(8,128)(2,1)S(1)}, bf16[192,384]{1,0:T(8,128)(2,1)}, u32[]{:S(2)}) copy-start(bf16[192,384]{1,0:T(8,128)(2,1)} %get-tuple-element.42) | copy-start | bytes 442372
  24.4 56.7 %copy-start.1 = (bf16[1536,256]{1,0:T(8,128)(2,1)S(1)}, bf16[1536,256]{1,0:T(8,128)(2,1)}, u32[]{:S(2)}) copy-start(bf16[1536,256]{1,0:T(8,128)(2,1)} %pair_weight_ref.1) | copy-start | bytes 2359300
  30.6 71.1 %copy-start.3 = (bf16[128,128]{1,0:T(8,128)(2,1)S(1)}, bf16[128,128]{1,0:T(8,128)(2,1)}, u32[]{:S(2)}) copy-start(bf16[128,128]{1,0:T(8,128)(2,1)} %weight_ref.1) | copy-start | bytes 98308
  30.7 10.1 %collective-permute-start.11 = (bf16[192,896]{1,0:T(8,128)(2,1)S(1)}, bf16[192,896]{1,0:T(8,128)(2,1)S(1)}, u32[]{:S(2)}, u32[]{:S(2)}) collective-permute-start(bf16[192,896]{1,0:T(8,128)(2,1)S(1)} %collective-permute-done.8.refs_3_), channel_id=1, source_target_pairs={{0,4},{2,6},{4,12},{6,14},{12,8},{14,10},{8,0},{10,2},{20,16},{22,... | collective-permute-start | bytes 1032200 | tf_op jit(solution)/shard_map/ppermute | solution.py:86
  33.2 8.9 %collective-permute-start.9 = (bf16[192,896]{1,0:T(8,128)(2,1)S(1)}, bf16[192,896]{1,0:T(8,128)(2,1)S(1)}, u32[]{:S(2)}, u32[]{:S(2)}) collective-permute-start(bf16[192,896]{1,0:T(8,128)(2,1)S(1)} %collective-permute-done.8.refs_3_), channel_id=1, source_target_pairs={{0,16},{16,0},{1,17},{17,1},{2,18},{18,2},{3,19},{19,3},{4,20},{20... | collective-permute-start | bytes 1032200 | tf_op jit(solution)/shard_map/ppermute | solution.py:92
  33.2 6.9 %collective-permute-start.7 = (bf16[192,640]{1,0:T(8,128)(2,1)S(1)}, bf16[192,640]{1,0:T(8,128)(2,1)}, u32[]{:S(2)}, u32[]{:S(2)}) collective-permute-start(bf16[192,640]{1,0:T(8,128)(2,1)S(1)} %pad_maximum_fusion.2), channel_id=1, source_target_pairs={{0,2},{2,0},{4,6},{6,4},{8,10},{10,8},{12,14},{14,12},{1,3},{3,1},... | collective-permute-start | bytes 737288 | tf_op jit(solution)/shard_map/ppermute | solution.py:368
  43.1 2.0 %collective-permute-start.12 = (bf16[8,128,192]{2,1,0:T(8,128)(2,1)S(1)}, bf16[8,128,192]{2,1,0:T(8,128)(2,1)S(1)}, u32[]{:S(2)}, u32[]{:S(2)}) collective-permute-start(bf16[8,128,192]{2,1,0:T(8,128)(2,1)S(1)} %get-tuple-element.29.part_ref), channel_id=1, source_target_pairs={{0,1},{1,0},{2,3},{3,2},{4,5},{5,4},{6,7},{7,6},{8,9},{9,8},{10,11... | collective-permute-start | bytes 1179656 | tf_op jit(solution)/shard_map/ppermute | solution.py:393
  44.3 15.0 %collective-permute-start.14 = (bf16[384,640]{1,0:T(8,128)(2,1)S(1)}, bf16[384,640]{1,0:T(8,128)(2,1)S(1)}, u32[]{:S(2)}, u32[]{:S(2)}) collective-permute-start(bf16[384,640]{1,0:T(8,128)(2,1)S(1)} %pad_maximum_fusion.refs_2_.refs_0_), channel_id=1, source_target_pairs={{0,4},{2,6},{4,12},{6,14},{12,8},{14,10},{8,0},{10,2},{20,16},{22,... | collective-permute-start | bytes 1474568 | tf_op jit(solution)/shard_map/ppermute | solution.py:86
  45.7 4.7 %collective-permute-start.17 = (bf16[192,128]{1,0:T(8,128)(2,1)S(1)}, bf16[192,128]{1,0:T(8,128)(2,1)S(1)}, u32[]{:S(2)}, u32[]{:S(2)}) collective-permute-start(bf16[192,128]{1,0:T(8,128)(2,1)S(1)} %get-tuple-element.34), channel_id=1, source_target_pairs={{0,2},{2,0},{4,6},{6,4},{8,10},{10,8},{12,14},{14,12},{1,3},{3,1},... | collective-permute-start | bytes 147464 | tf_op jit(solution)/shard_map/ppermute | solution.py:410
  46.6 31.3 %collective-permute-start.13 = (bf16[8,128,192]{2,1,0:T(8,128)(2,1)S(1)}, bf16[8,128,192]{2,1,0:T(8,128)(2,1)S(1)}, u32[]{:S(2)}, u32[]{:S(2)}) collective-permute-start(bf16[8,128,192]{2,1,0:T(8,128)(2,1)S(1)} %get-tuple-element.32.refs_0_), channel_id=1, source_target_pairs={{0,2},{2,0},{4,6},{6,4},{8,10},{10,8},{12,14},{14,12},{1,3},{3,1},... | collective-permute-start | bytes 1179656 | tf_op jit(solution)/shard_map/ppermute | solution.py:411
  50.4 9.9 %collective-permute-start.18 = (bf16[2,192,128]{2,1,0:T(8,128)(2,1)S(1)}, bf16[2,192,128]{2,1,0:T(8,128)(2,1)S(1)}, u32[]{:S(2)}, u32[]{:S(2)}) collective-permute-start(bf16[2,192,128]{2,1,0:T(8,128)(2,1)S(1)} %pad_maximum_fusion.3), channel_id=1, source_target_pairs={{0,4},{2,6},{4,12},{6,14},{12,8},{14,10},{8,0},{10,2},{1,5},{3,7},... | collective-permute-start | bytes 294920 | tf_op jit(solution)/shard_map/ppermute | solution.py:415
  52.6 11.0 %collective-permute-start.19 = (bf16[2,192,128]{2,1,0:T(8,128)(2,1)S(1)}, bf16[2,192,128]{2,1,0:T(8,128)(2,1)S(1)}, u32[]{:S(2)}, u32[]{:S(2)}) collective-permute-start(bf16[2,192,128]{2,1,0:T(8,128)(2,1)S(1)} %pad_maximum_fusion.3), channel_id=1, source_target_pairs={{4,0},{6,2},{12,4},{14,6},{8,12},{10,14},{0,8},{2,10},{5,1},{7,3},... | collective-permute-start | bytes 294920 | tf_op jit(solution)/shard_map/ppermute | solution.py:415
  52.6 25.2 %collective-permute-start.20 = (bf16[2,192,128]{2,1,0:T(8,128)(2,1)S(1)}, bf16[2,192,128]{2,1,0:T(8,128)(2,1)S(1)}, u32[]{:S(2)}, u32[]{:S(2)}) collective-permute-start(bf16[2,192,128]{2,1,0:T(8,128)(2,1)S(1)} %pad_maximum_fusion.3), channel_id=1, source_target_pairs={{0,12},{2,14},{4,8},{6,10},{12,0},{14,2},{8,4},{10,6},{1,13},{3,15... | collective-permute-start | bytes 294920 | tf_op jit(solution)/shard_map/ppermute | solution.py:415
  59.3 18.7 %collective-permute-start.15 = (bf16[384,640]{1,0:T(8,128)(2,1)S(1)}, bf16[384,640]{1,0:T(8,128)(2,1)S(1)}, u32[]{:S(2)}, u32[]{:S(2)}) collective-permute-start(bf16[384,640]{1,0:T(8,128)(2,1)S(1)} %collective-permute-done.14.refs_3_.refs_1_), channel_id=1, source_target_pairs={{0,16},{16,0},{1,17},{17,1},{2,18},{18,2},{3,19},{19,3},{4,20},{20... | collective-permute-start | bytes 1474568 | tf_op jit(solution)/shard_map/ppermute | solution.py:92
  60.3 17.7 %collective-permute-start.16 = (bf16[384,640]{1,0:T(8,128)(2,1)S(1)}, bf16[384,640]{1,0:T(8,128)(2,1)S(1)}, u32[]{:S(2)}, u32[]{:S(2)}) collective-permute-start(bf16[384,640]{1,0:T(8,128)(2,1)S(1)} %collective-permute-done.14.refs_3_.refs_1_), channel_id=1, source_target_pairs={{0,4},{2,6},{4,12},{6,14},{12,8},{14,10},{8,0},{10,2},{20,16},{22,... | collective-permute-start | bytes 1474568 | tf_op jit(solution)/shard_map/ppermute | solution.py:86
  77.9 1.8 %collective-permute-start.21 = (bf16[8,192,128]{2,1,0:T(8,128)(2,1)S(1)}, bf16[8,192,128]{2,1,0:T(8,128)(2,1)S(1)}, u32[]{:S(2)}, u32[]{:S(2)}) collective-permute-start(bf16[8,192,128]{2,1,0:T(8,128)(2,1)S(1)} %constant_dynamic-update-slice_fusion.own_ref), channel_id=1, source_target_pairs={{0,1},{1,0},{2,3},{3,2},{4,5},{5,4},{6,7},{7,6},{8,9},{9,8},{10,11... | collective-permute-start | bytes 1179656 | tf_op jit(solution)/shard_map/ppermute | solution.py:418
  82.5 3.7 %collective-permute-start.24 = (bf16[16,256]{1,0:T(8,128)(2,1)S(1)}, bf16[16,256]{1,0:T(8,128)(2,1)S(1)}, u32[]{:S(2)}, u32[]{:S(2)}) collective-permute-start(bf16[16,256]{1,0:T(8,128)(2,1)S(1)} %get-tuple-element.37), channel_id=1, source_target_pairs={{0,2},{2,0},{4,6},{6,4},{8,10},{10,8},{12,14},{14,12},{1,3},{3,1},... | collective-permute-start | bytes 24584 | tf_op jit(solution)/shard_map/ppermute | solution.py:459
  82.8 3.5 %collective-permute-start.22 = (bf16[8,128,192]{2,1,0:T(8,128)(2,1)S(1)}, bf16[8,128,192]{2,1,0:T(8,128)(2,1)S(1)}, u32[]{:S(2)}, u32[]{:S(2)}) collective-permute-start(bf16[8,128,192]{2,1,0:T(8,128)(2,1)S(1)} %get-tuple-element.36), channel_id=1, source_target_pairs={{0,1},{1,0},{2,3},{3,2},{4,5},{5,4},{6,7},{7,6},{8,9},{9,8},{10,11... | collective-permute-start | bytes 1179656 | tf_op jit(solution)/shard_map/ppermute | solution.py:462
  86.2 1.2 %collective-permute-start.25 = (bf16[16,256]{1,0:T(8,128)(2,1)S(1)}, bf16[16,256]{1,0:T(8,128)(2,1)S(1)}, u32[]{:S(2)}, u32[]{:S(2)}) collective-permute-start(bf16[16,256]{1,0:T(8,128)(2,1)S(1)} %add_convert_fusion.2), channel_id=1, source_target_pairs={{0,1},{1,0},{2,3},{3,2},{4,5},{5,4},{6,7},{7,6},{8,9},{9,8},{10,11... | collective-permute-start | bytes 24584 | tf_op jit(solution)/shard_map/ppermute | solution.py:461
  86.4 8.8 %collective-permute-start.23 = (bf16[8,64,192]{2,1,0:T(8,128)(2,1)S(1)}, bf16[8,64,192]{2,1,0:T(8,128)(2,1)S(1)}, u32[]{:S(2)}, u32[]{:S(2)}) collective-permute-start(bf16[8,64,192]{2,1,0:T(8,128)(2,1)S(1)} %get-tuple-element.44), channel_id=1, source_target_pairs={{0,2},{2,0},{4,6},{6,4},{8,10},{10,8},{12,14},{14,12},{1,3},{3,1},... | collective-permute-start | bytes 589832 | tf_op jit(solution)/shard_map/ppermute | solution.py:466
  87.4 3.7 %collective-permute-start.26 = (bf16[16,256]{1,0:T(8,128)(2,1)S(1)}, bf16[16,256]{1,0:T(8,128)(2,1)S(1)}, u32[]{:S(2)}, u32[]{:S(2)}) collective-permute-start(bf16[16,256]{1,0:T(8,128)(2,1)S(1)} %add_convert_fusion.1), channel_id=1, source_target_pairs={{0,4},{2,6},{4,0},{6,2},{8,12},{10,14},{12,8},{14,10},{1,5},{3,7},... | collective-permute-start | bytes 24584 | tf_op jit(solution)/shard_map/ppermute | solution.py:468
  95.2 6.5 %collective-permute-start.27 = (bf16[32,256]{1,0:T(8,128)(2,1)S(1)}, bf16[32,256]{1,0:T(8,128)(2,1)S(1)}, u32[]{:S(2)}, u32[]{:S(2)}) collective-permute-start(bf16[32,256]{1,0:T(8,128)(2,1)S(1)} %pad_maximum_fusion.4), channel_id=1, source_target_pairs={{0,8},{2,10},{4,12},{6,14},{9,1},{11,3},{13,5},{15,7},{16,24},{18,... | collective-permute-start | bytes 49160 | tf_op jit(solution)/shard_map/ppermute | solution.py:471

commit v12 on v11

--- a/solution.py
+++ b/solution.py
@@ -241,22 +241,19 @@
         weight = pair_weight_ref[pl.ds(pl.multiple_of(place * width, width), width)]
         projected = projected + dot_nn((pooled + first).astype(BF16), weight)
     pair_ref[...] = projected.astype(BF16)
-    own = keep_ref.shape[1] // sides
+    own = keep_ref.shape[0] // sides
     for i in range(sides):
-        rows = slice(i * own, (i + 1) * own)
-        keep_ref[:, rows] = whole[:, pl.ds(pl.multiple_of(i * tokens + col * own, own), own)]
-        give_ref[:, rows] = whole[:, pl.ds(pl.multiple_of(i * tokens + (1 - col) * own, own), own)]
+        for ref, core in ((keep_ref, col), (give_ref, 1 - col)):
+            rows = pl.ds(pl.multiple_of(i * tokens + core * own, own), own)
+            ref[i * own:(i + 1) * own] = jnp.concatenate([whole[s, rows] for s in range(whole.shape[0])], axis=1)
 
 
 def token_kernel(embedded_ref, *refs):
     parts, token_ref = refs[:-1], refs[-1]
     own = token_ref.shape[0]
     mine = pl.ds(pl.multiple_of(lax.axis_index("col") * own, own), own)
-    blocks = [
-        embedded_ref[s, mine].astype(F32) + sum(part[s].astype(F32) for part in parts)
-        for s in range(embedded_ref.shape[0])
-    ]
-    token_ref[...] = jnp.concatenate(blocks, axis=1).astype(BF16)
+    embedded = jnp.concatenate([embedded_ref[s, mine] for s in range(embedded_ref.shape[0])], axis=1)
+    token_ref[...] = (embedded.astype(F32) + sum(part[...].astype(F32) for part in parts)).astype(BF16)
 
 
 def pair_kernel(own_ref, all_ref, weight_ref, out_ref, columns_here):
@@ -370,10 +367,7 @@
         q = Blocks(jnp.concatenate([later_mine, received]), count)
         q.at["own"] = after(q.at["own"], e.at["far2"])
         q.along("own", "step")
-        q.along("step", "far")
-        q.between("step", "cross")
         embed_blocks = e.pieces()
-        later_blocks = [q.at[name] for name in ("own", "step", "cross", "far")]
     else:
         embed_blocks, later_blocks = (
             [lax.all_gather(x, "seq", axis=0, tiled=True)] for x in (embed_own, later_mine)
@@ -409,6 +403,10 @@
     if ring:
         here = jnp.stack([keyvalue, lax.ppermute(keyvalue, "seq", pair_swap)])
         both_normed.append(lax.ppermute(normed, "seq", pair_swap))
+        q.at["step"] = after(q.at["step"], both_normed[1])
+        q.along("step", "far")
+        q.between("step", "cross")
+        later_blocks = [q.at[name] for name in ("own", "step", "cross", "far")]
         onward = [(2 * RING[k] + i, 2 * RING[(k + 1) % 4] + i) for k in range(4) for i in range(2)]
         opposite = [(2 * RING[k] + i, 2 * RING[(k + 2) % 4] + i) for k in range(4) for i in range(2)]
         turns = [onward, [(j, i) for i, j in onward], opposite]
@@ -440,7 +438,7 @@
 
     out_width = rowcol_weight.shape[1]
     own_rows, pair_rows = tokens // cols, tokens // PAIR_POOL
-    kept = shape((pieces, sides * own_rows, block), BF16)
+    kept = shape((sides * own_rows, width), BF16)
     keep, give, part_pair = pl.pallas_call(
         functools.partial(output_kernel, sides, features),
         out_shape=(kept, kept, shape((sides * pair_rows, out_width), BF16)),
@@ -462,7 +460,7 @@
     sums = total(keep, lax.ppermute(give, "col", swap))
 
     if ring:
-        sent = sums[:, own_rows:]
+        sent = sums[own_rows:]
         crossed = lax.ppermute(sent, "seq", pair_swap)
         rows_all = after(projected, sent)
         rows_all = jnp.concatenate([rows_all, lax.ppermute(rows_all, "seq", [(i, i ^ 2) for i in range(count)])])
@@ -473,7 +471,7 @@
     else:
         rows_all = lax.all_gather(projected, "seq", axis=0, tiled=True)
 
-    parts = [sums[:, :own_rows]]
+    parts = [sums[:own_rows]]
     if ring:
         parts.append(crossed)
     out_tokens = pl.pallas_call(

time: 103 us -> 102 us (level)
  waiting for transfers between devices: 49.8 us -> 44.8 us
  starting transfers between devices: 26.2 us -> 29.8 us
    ppermute x5, waiting for transfers between devices: 6.74 us -> 0.7 us  [along(): self.at[target] = lax.ppermute(self.at[source], ('grp', 'seq'), pairs)]
    ppermute x3, starting transfers between devices: 0.66 us -> 3.76 us  [between(): self.at[target] = lax.ppermute(self.at[source], 'grp', [(0, 1), (1, 0)])]
    ppermute x3, waiting for transfers between devices: 15.8 us -> 17.6 us  [on_device(): lax.ppermute(here, 'seq', turn)]
    ppermute x1, waiting for transfers between devices: 4.13 us -> 2.71 us  [on_device(): crossed = lax.ppermute(sent, 'seq', pair_swap)]
  transfers between devices with their start and end apart: 28 -> 28, of which waited for: 16 -> 15; matrix products, arithmetic and copies ran while one was open for 7% -> 7% of each run, Pallas kernels for 11% -> 11%
where the time goes in v12:
time: 102 us; the launch traced here: 101 us
  waiting for transfers between devices  44.8 us (44%)
  starting transfers between devices  29.8 us (29%)
  Pallas kernels  15.6 us (15%)
  local copies, waits for them, and re-layouts  7.65 us (8%)
  other arithmetic  2.4 us (2%)
    ppermute x3, waiting for transfers between devices, on_device(): lax.ppermute(here, 'seq', turn)  17.6 us
    ppermute x5, starting transfers between devices, along(): self.at[target] = lax.ppermute(self.at[source], ('grp', 'seq'), pairs)  8.76 us
    pallas_call x1, Pallas kernels, on_device(): pl.pallas_call(functools.partial(conv_kernel, positions), out_shape=shape...  6.21 us
    ppermute x1, waiting for transfers between devices, on_device(): received = lax.ppermute(theirs, 'seq', pair_swap)  5.27 us
    ppermute x1, waiting for transfers between devices, on_device(): far_rows = lax.ppermute(rows_all, ('seq', 'col'), pairs)  4.41 us
    ppermute x3, starting transfers between devices, between(): self.at[target] = lax.ppermute(self.at[source], 'grp', [(0, 1), (1, 0)])  3.76 us
    ppermute x1, waiting for transfers between devices, on_device(): lax.ppermute(rows_all, 'seq', [(i, i ^ 2) for i in range(count)])  3.65 us
    ppermute x1, waiting for transfers between devices, on_device(): turned = lax.ppermute(part_pair, 'seq', pair_swap)  3.37 us
  transfers between devices with their start and end apart: 28, of which 15 were waited for; matrix products, arithmetic and copies ran while one was open for 7% of the time, Pallas kernels for 11%

profile of v12, /device:TPU:22, one launch (start us, length us, event | category | flops | bytes accessed | tf_op | source)
XLA Modules:
  0.0 101.2 jit_solution(17024953111472503007)
XLA Ops:
  0.7 0.9 copy-done
  1.6 1.1 %pad_maximum_fusion.1.refs_0_ = bf16[192,896]{1,0:T(8,128)(2,1)S(1)} fusion(bf16[192,192]{1,0:T(8,128)(2,1)S(1)} %constant_dynamic-slice_fusion.2, bf16[192,704]{1,0:T(8,128)(2,1)} %bitcast.15), kind=kLoop, calls=%fused_computation.2 | loop fusion | flops 688128 | bytes 688128 | tf_op jit(solution)/shard_map/concatenate | solution.py:295
  2.7 0.6 collective-permute-start.1
  3.3 1.6 %collective-permute-start = (bf16[192,896]{1,0:T(8,128)(2,1)S(1)}, bf16[192,896]{1,0:T(8,128)(2,1)S(1)}, u32[]{:S(2)}, u32[]{:S(2)}) collective-permute-start(bf16[192,896]{1,0:T(8,128)(2,1)S(1)} %pad_maximum_fusion.1.refs_0_), channel_id=1, source_target_pairs={{0,4},{2,6},{4,12},{6,14},{12,8},{14,10},{8,0},{10,2},{20,16},{22,... | collective-permute-start | bytes 1032200 | tf_op jit(solution)/shard_map/ppermute | solution.py:86
  4.9 1.1 %fusion.3 = (bf16[2,704]{0,1:T(8,128)(2,1)S(1)}, bf16[2,704]{0,1:T(8,128)(2,1)S(1)}) fusion(bf16[512,704]{0,1:T(8,128)(2,1)} %param.10), kind=kLoop, calls=%fused_computation.24 | loop fusion | bytes 11264 | tf_op jit(solution)/shard_map/slice | solution.py:322
  6.1 3.2 %collective-permute-start.2 = (bf16[2,704]{1,0:T(2,128)(2,1)S(1)}, bf16[2,704]{1,0:T(2,128)(2,1)S(1)}, u32[]{:S(2)}, u32[]{:S(2)}) collective-permute-start(bf16[2,704]{1,0:T(2,128)(2,1)S(1)} %copy.14), channel_id=1, source_target_pairs={{0,2},{2,4},{4,6},{6,8},{8,10},{10,12},{12,14},{1,3},{3,5},{5,7},{... | collective-permute-start | bytes 8456 | tf_op jit(solution)/shard_map/ppermute | solution.py:321
  9.4 2.7 %collective-permute-start.3 = (bf16[2,704]{1,0:T(2,128)(2,1)S(1)}, bf16[2,704]{1,0:T(2,128)(2,1)S(1)}, u32[]{:S(2)}, u32[]{:S(2)}) collective-permute-start(bf16[2,704]{1,0:T(2,128)(2,1)S(1)} %copy.15), channel_id=1, source_target_pairs={{2,0},{4,2},{6,4},{8,6},{10,8},{12,10},{14,12},{3,1},{5,3},{7,5},{... | collective-permute-start | bytes 8456 | tf_op jit(solution)/shard_map/ppermute | solution.py:322
  12.1 1.6 %constant_dynamic-slice_fusion.1 = (bf16[192,256]{1,0:T(8,128)(2,1)}, bf16[192,256]{1,0:T(8,128)(2,1)S(1)}) fusion(bf16[192,1024]{1,0:T(8,128)(2,1)} %param.15, s32[]{:T(128)S(6)} %select_n.44, s32[]{:T(128)S(6)} %select_n.46), kind=kLoop, calls=%fused_computation.22 | loop fusion | bytes 393224 | tf_op jit(solution)/shard_map/dynamic_slice | solution.py:308
  13.8 1.7 %dynamic-slice_bitcast_fusion.1 = (bf16[192,384]{1,0:T(8,128)(2,1)}, bf16[192,384]{1,0:T(8,128)(2,1)S(1)}) fusion(bf16[1536,192]{0,1:T(8,128)(2,1)} %param.17, s32[]{:T(128)S(6)} %select_n.45, s32[]{:T(128)S(6)} %select_n.47), kind=kLoop, calls=%fused_computation.5 | loop fusion | bytes 589832 | tf_op jit(solution)/shard_map/dynamic_slice | solution.py:309
  15.9 0.6 collective-permute-start.5
  16.5 0.7 reshape.10.gain_ref
  17.2 0.6 collective-permute-start.6
  17.8 1.5 %collective-permute-start.8 = (bf16[192,896]{1,0:T(8,128)(2,1)S(1)}, bf16[192,896]{1,0:T(8,128)(2,1)S(1)}, u32[]{:S(2)}, u32[]{:S(2)}) collective-permute-start(bf16[192,896]{1,0:T(8,128)(2,1)S(1)} %collective-permute-done.refs_2_), channel_id=1, source_target_pairs={{0,2},{2,0},{4,6},{6,4},{8,10},{10,8},{12,14},{14,12},{1,3},{3,1},... | collective-permute-start | bytes 1032200 | tf_op jit(solution)/shard_map/ppermute | solution.py:89
  19.4 1.0 %collective-permute-start.10 = (bf16[192,896]{1,0:T(8,128)(2,1)S(1)}, bf16[192,896]{1,0:T(8,128)(2,1)S(1)}, u32[]{:S(2)}, u32[]{:S(2)}) collective-permute-start(bf16[192,896]{1,0:T(8,128)(2,1)S(1)} %collective-permute-done.refs_2_), channel_id=1, source_target_pairs={{0,4},{2,6},{4,12},{6,14},{12,8},{14,10},{8,0},{10,2},{20,16},{22,... | collective-permute-start | bytes 1032200 | tf_op jit(solution)/shard_map/ppermute | solution.py:86
  20.4 1.1 %copy-done.2 = bf16[512,704]{0,1:T(8,128)(2,1)S(1)} copy-done((bf16[512,704]{0,1:T(8,128)(2,1)S(1)}, bf16[512,704]{0,1:T(8,128)(2,1)}, u32[]{:S(2)}) %copy-start.2) | copy-done | bytes 720920
  21.5 2.9 %act.1 = (bf16[640,1408]{1,0:T(8,128)(2,1)S(1)}, f32[128,704]{1,0:T(8,128)S(1)}) custom-call(bf16[704,512]{1,0:T(8,128)(2,1)S(1)} %bitcast.13, bf16[704,512]{1,0:T(8,128)(2,1)S(1)} %collective-permute-done.4.other_ref, f32[1,1408]{1,0:T(1,128)S(1)} %reshape.10.gain_ref), custom_call_target="tpu_custom_call" | custom-call | flops 922746880 | bytes 2883584 | tf_op jit(solution)/shard_map/act/pallas_call | solution.py:334
  24.4 6.2 %conv.1.pooled_ref = bf16[128,704]{1,0:T(8,128)(2,1)S(1)} custom-call(bf16[640,1408]{1,0:T(8,128)(2,1)S(1)} %get-tuple-element.23.windows_ref, f32[128,704]{1,0:T(8,128)S(1)} %get-tuple-element.24.residual_ref, bf16[16,1408]{1,0:T(8,128)(2,1)S(1)} %maximum_select_fusion.halo_ref, f32[1,1408]{1,0:T(1,128)S(1)} %reshape.10.gain_ref, bf16[5,704,1408]{2,1,0:T(8,128)(2,1)} %bitcast.14), custom_call_target="tpu_custom_call" | custom-call | flops 1268776960 | bytes 9912320 | tf_op jit(solution)/shard_map/conv/pallas_call | solution.py:349
  30.7 2.5 %collective-permute-start.11 = (bf16[192,896]{1,0:T(8,128)(2,1)S(1)}, bf16[192,896]{1,0:T(8,128)(2,1)S(1)}, u32[]{:S(2)}, u32[]{:S(2)}) collective-permute-start(bf16[192,896]{1,0:T(8,128)(2,1)S(1)} %collective-permute-done.8.refs_3_), channel_id=1, source_target_pairs={{0,4},{2,6},{4,12},{6,14},{12,8},{14,10},{8,0},{10,2},{20,16},{22,... | collective-permute-start | bytes 1032200 | tf_op jit(solution)/shard_map/ppermute | solution.py:86
  33.2 1.6 %collective-permute-start.7 = (bf16[192,640]{1,0:T(8,128)(2,1)S(1)}, bf16[192,640]{1,0:T(8,128)(2,1)}, u32[]{:S(2)}, u32[]{:S(2)}) collective-permute-start(bf16[192,640]{1,0:T(8,128)(2,1)S(1)} %pad_maximum_fusion.2), channel_id=1, source_target_pairs={{0,2},{2,0},{4,6},{6,4},{8,10},{10,8},{12,14},{14,12},{1,3},{3,1},... | collective-permute-start | bytes 737288 | tf_op jit(solution)/shard_map/ppermute | solution.py:365
  34.8 5.3 %collective-permute-done.7 = bf16[192,640]{1,0:T(8,128)(2,1)} collective-permute-done((bf16[192,640]{1,0:T(8,128)(2,1)S(1)}, bf16[192,640]{1,0:T(8,128)(2,1)}, u32[]{:S(2)}, u32[]{:S(2)}) %collective-permute-start.7) | collective-permute-done | bytes 245792 | tf_op jit(solution)/shard_map/ppermute | solution.py:365
  40.1 0.7 collective-permute-done.11.refs_7_
  40.8 1.3 %collective-permute-done.9.refs_5_ = bf16[192,896]{1,0:T(8,128)(2,1)S(1)} collective-permute-done((bf16[192,896]{1,0:T(8,128)(2,1)S(1)}, bf16[192,896]{1,0:T(8,128)(2,1)S(1)}, u32[]{:S(2)}, u32[]{:S(2)}) %collective-permute-start.9) | collective-permute-done | bytes 344096 | tf_op jit(solution)/shard_map/ppermute | solution.py:92
  42.1 1.0 embed.1
  43.2 1.1 %pad_maximum_fusion.refs_2_.refs_0_ = bf16[384,640]{1,0:T(8,128)(2,1)S(1)} fusion(bf16[192,640]{1,0:T(8,128)(2,1)} %collective-permute-done.7, bf16[192,384]{1,0:T(8,128)(2,1)S(1)} %copy-done.4, bf16[192,256]{1,0:T(8,128)(2,1)} %get-tuple-element.48), kind=kLoop, calls=%fused_computation.1 | loop fusion | flops 1474560 | bytes 983040 | tf_op jit(solution)/shard_map/concatenate | solution.py:367
  44.3 0.4 collective-permute-start.14
  45.0 0.6 keyvalue.1
  45.7 1.0 collective-permute-start.17
  46.6 1.1 %collective-permute-start.13 = (bf16[8,128,192]{2,1,0:T(8,128)(2,1)S(1)}, bf16[8,128,192]{2,1,0:T(8,128)(2,1)S(1)}, u32[]{:S(2)}, u32[]{:S(2)}) collective-permute-start(bf16[8,128,192]{2,1,0:T(8,128)(2,1)S(1)} %get-tuple-element.33.refs_0_), channel_id=1, source_target_pairs={{0,2},{2,0},{4,6},{6,4},{8,10},{10,8},{12,14},{14,12},{1,3},{3,1},... | collective-permute-start | bytes 1179656 | tf_op jit(solution)/shard_map/ppermute | solution.py:405
  47.8 2.6 %collective-permute-done.17 = bf16[192,128]{1,0:T(8,128)(2,1)S(1)} collective-permute-done((bf16[192,128]{1,0:T(8,128)(2,1)S(1)}, bf16[192,128]{1,0:T(8,128)(2,1)S(1)}, u32[]{:S(2)}, u32[]{:S(2)}) %collective-permute-start.17) | collective-permute-done | bytes 49184 | tf_op jit(solution)/shard_map/ppermute | solution.py:404
  50.4 2.3 %collective-permute-start.18 = (bf16[2,192,128]{2,1,0:T(8,128)(2,1)S(1)}, bf16[2,192,128]{2,1,0:T(8,128)(2,1)S(1)}, u32[]{:S(2)}, u32[]{:S(2)}) collective-permute-start(bf16[2,192,128]{2,1,0:T(8,128)(2,1)S(1)} %pad_maximum_fusion.3), channel_id=1, source_target_pairs={{0,4},{2,6},{4,12},{6,14},{12,8},{14,10},{8,0},{10,2},{1,5},{3,7},... | collective-permute-start | bytes 294920 | tf_op jit(solution)/shard_map/ppermute | solution.py:413
  52.6 0.6 collective-permute-start.20
  53.3 7.0 %collective-permute-done.18 = bf16[2,192,128]{2,1,0:T(8,128)(2,1)S(1)} collective-permute-done((bf16[2,192,128]{2,1,0:T(8,128)(2,1)S(1)}, bf16[2,192,128]{2,1,0:T(8,128)(2,1)S(1)}, u32[]{:S(2)}, u32[]{:S(2)}) %collective-permute-start.18) | collective-permute-done | bytes 98336 | tf_op jit(solution)/shard_map/ppermute | solution.py:413
  60.3 0.6 collective-permute-done.13.refs_1_
  60.9 3.1 %collective-permute-start.15 = (bf16[384,640]{1,0:T(8,128)(2,1)S(1)}, bf16[384,640]{1,0:T(8,128)(2,1)S(1)}, u32[]{:S(2)}, u32[]{:S(2)}) collective-permute-start(bf16[384,640]{1,0:T(8,128)(2,1)S(1)} %collective-permute-done.14.refs_3_.refs_1_), channel_id=1, source_target_pairs={{0,16},{16,0},{1,17},{17,1},{2,18},{18,2},{3,19},{19,3},{4,20},{20... | collective-permute-start | bytes 1474568 | tf_op jit(solution)/shard_map/ppermute | solution.py:92
  64.0 3.2 %collective-permute-start.16 = (bf16[384,640]{1,0:T(8,128)(2,1)S(1)}, bf16[384,640]{1,0:T(8,128)(2,1)S(1)}, u32[]{:S(2)}, u32[]{:S(2)}) collective-permute-start(bf16[384,640]{1,0:T(8,128)(2,1)S(1)} %collective-permute-done.14.refs_3_.refs_1_), channel_id=1, source_target_pairs={{0,4},{2,6},{4,12},{6,14},{12,8},{14,10},{8,0},{10,2},{20,16},{22,... | collective-permute-start | bytes 1474568 | tf_op jit(solution)/shard_map/ppermute | solution.py:86
  67.2 10.6 %collective-permute-done.20 = bf16[2,192,128]{2,1,0:T(8,128)(2,1)S(1)} collective-permute-done((bf16[2,192,128]{2,1,0:T(8,128)(2,1)S(1)}, bf16[2,192,128]{2,1,0:T(8,128)(2,1)S(1)}, u32[]{:S(2)}, u32[]{:S(2)}) %collective-permute-start.20) | collective-permute-done | bytes 98336 | tf_op jit(solution)/shard_map/ppermute | solution.py:413
  78.0 0.4 query.1.query_ref
  78.4 1.2 %collective-permute-done.21.other_ref = bf16[8,192,128]{2,1,0:T(8,128)(2,1)S(1)} collective-permute-done((bf16[8,192,128]{2,1,0:T(8,128)(2,1)S(1)}, bf16[8,192,128]{2,1,0:T(8,128)(2,1)S(1)}, u32[]{:S(2)}, u32[]{:S(2)}) %collective-permute-start.21) | collective-permute-done | bytes 393248 | tf_op jit(solution)/shard_map/ppermute | solution.py:416
  79.7 1.4 %attend.1.attended_ref = bf16[2,256,192]{2,1,0:T(8,128)(2,1)S(1)} custom-call(bf16[256,256]{1,0:T(8,128)(2,1)S(1)} %query.1.query_ref, bf16[8,192,128]{2,1,0:T(8,128)(2,1)S(1)} %constant_dynamic-update-slice_fusion.own_ref, bf16[8,192,128]{2,1,0:T(8,128)(2,1)S(1)} %collective-permute-done.21.other_ref), custom_call_target="tpu_custom_call" | custom-call | flops 167772160 | bytes 786432 | tf_op jit(solution)/shard_map/attend/pallas_call | solution.py:428
  81.1 1.4 %output.1 = (bf16[128,1536]{1,0:T(8,128)(2,1)S(1)}, bf16[128,1536]{1,0:T(8,128)(2,1)S(1)}, bf16[16,256]{1,0:T(8,128)(2,1)S(1)}) custom-call(bf16[2,256,192]{2,1,0:T(8,128)(2,1)S(1)} %attend.1.attended_ref, bf16[8,128,192]{2,1,0:T(8,128)(2,1)S(1)} %get-tuple-element.32.embedded_ref, bf16[1536,256]{1,0:T(8,128)(2,1)S(1)} %copy-done.1, ...), custom_call_target="tpu_custom_call" | custom-call | flops 301989888 | bytes 1179648 | tf_op jit(solution)/shard_map/output/pallas_call | solution.py:442
  82.9 3.4 %collective-permute-done.24 = bf16[16,256]{1,0:T(8,128)(2,1)S(1)} collective-permute-done((bf16[16,256]{1,0:T(8,128)(2,1)S(1)}, bf16[16,256]{1,0:T(8,128)(2,1)S(1)}, u32[]{:S(2)}, u32[]{:S(2)}) %collective-permute-start.24) | collective-permute-done | bytes 8224 | tf_op jit(solution)/shard_map/ppermute | solution.py:457
  86.9 0.6 collective-permute-done.25
  87.5 3.6 %collective-permute-done.26 = bf16[16,256]{1,0:T(8,128)(2,1)S(1)} collective-permute-done((bf16[16,256]{1,0:T(8,128)(2,1)S(1)}, bf16[16,256]{1,0:T(8,128)(2,1)S(1)}, u32[]{:S(2)}, u32[]{:S(2)}) %collective-permute-start.26) | collective-permute-done | bytes 8224 | tf_op jit(solution)/shard_map/ppermute | solution.py:466
  91.2 2.7 %collective-permute-done.23.refs_1_ = bf16[64,1536]{1,0:T(8,128)(2,1)S(1)} collective-permute-done((bf16[64,1536]{1,0:T(8,128)(2,1)S(1)}, bf16[64,1536]{1,0:T(8,128)(2,1)S(1)}, u32[]{:S(2)}, u32[]{:S(2)}) %collective-permute-start.23) | collective-permute-done | bytes 196640 | tf_op jit(solution)/shard_map/ppermute | solution.py:464
  93.9 1.3 %collective-permute-start.27 = (bf16[32,256]{1,0:T(8,128)(2,1)S(1)}, bf16[32,256]{1,0:T(8,128)(2,1)S(1)}, u32[]{:S(2)}, u32[]{:S(2)}) collective-permute-start(bf16[32,256]{1,0:T(8,128)(2,1)S(1)} %pad_maximum_fusion.4), channel_id=1, source_target_pairs={{0,8},{2,10},{4,12},{6,14},{9,1},{11,3},{13,5},{15,7},{16,24},{18,... | collective-permute-start | bytes 49160 | tf_op jit(solution)/shard_map/ppermute | solution.py:469
  95.2 0.8 tokens.1
  96.0 4.4 %collective-permute-done.27 = bf16[32,256]{1,0:T(8,128)(2,1)S(1)} collective-permute-done((bf16[32,256]{1,0:T(8,128)(2,1)S(1)}, bf16[32,256]{1,0:T(8,128)(2,1)S(1)}, u32[]{:S(2)}, u32[]{:S(2)}) %collective-permute-start.27) | collective-permute-done | bytes 16416 | tf_op jit(solution)/shard_map/ppermute | solution.py:469
  100.4 0.8 pair.1
  (56 shorter events, 2.5 us)
Async XLA Ops:
  0.6 0.9 copy-start
  2.7 13.1 %collective-permute-start.1 = (bf16[192,896]{1,0:T(8,128)(2,1)S(1)}, bf16[192,896]{1,0:T(8,128)(2,1)S(1)}, u32[]{:S(2)}, u32[]{:S(2)}) collective-permute-start(bf16[192,896]{1,0:T(8,128)(2,1)S(1)} %pad_maximum_fusion.1.refs_0_), channel_id=1, source_target_pairs={{0,2},{2,0},{4,6},{6,4},{8,10},{10,8},{12,14},{14,12},{1,3},{3,1},... | collective-permute-start | bytes 1032200 | tf_op jit(solution)/shard_map/ppermute | solution.py:89
  3.3 12.6 %collective-permute-start = (bf16[192,896]{1,0:T(8,128)(2,1)S(1)}, bf16[192,896]{1,0:T(8,128)(2,1)S(1)}, u32[]{:S(2)}, u32[]{:S(2)}) collective-permute-start(bf16[192,896]{1,0:T(8,128)(2,1)S(1)} %pad_maximum_fusion.1.refs_0_), channel_id=1, source_target_pairs={{0,4},{2,6},{4,12},{6,14},{12,8},{14,10},{8,0},{10,2},{20,16},{22,... | collective-permute-start | bytes 1032200 | tf_op jit(solution)/shard_map/ppermute | solution.py:86
  6.1 9.4 %collective-permute-start.2 = (bf16[2,704]{1,0:T(2,128)(2,1)S(1)}, bf16[2,704]{1,0:T(2,128)(2,1)S(1)}, u32[]{:S(2)}, u32[]{:S(2)}) collective-permute-start(bf16[2,704]{1,0:T(2,128)(2,1)S(1)} %copy.14), channel_id=1, source_target_pairs={{0,2},{2,4},{4,6},{6,8},{8,10},{10,12},{12,14},{1,3},{3,5},{5,7},{... | collective-permute-start | bytes 8456 | tf_op jit(solution)/shard_map/ppermute | solution.py:321
  9.4 6.4 %collective-permute-start.3 = (bf16[2,704]{1,0:T(2,128)(2,1)S(1)}, bf16[2,704]{1,0:T(2,128)(2,1)S(1)}, u32[]{:S(2)}, u32[]{:S(2)}) collective-permute-start(bf16[2,704]{1,0:T(2,128)(2,1)S(1)} %copy.15), channel_id=1, source_target_pairs={{2,0},{4,2},{6,4},{8,6},{10,8},{12,10},{14,12},{3,1},{5,3},{7,5},{... | collective-permute-start | bytes 8456 | tf_op jit(solution)/shard_map/ppermute | solution.py:322
  13.8 29.4 %copy-start.5 = (f32[1536]{0:T(1024)S(1)}, f32[1536]{0:T(1024)}, u32[]{:S(2)}) copy-start(f32[1536]{0:T(1024)} %param.14) | copy-start | bytes 18436
  15.9 4.6 %collective-permute-start.4 = (bf16[704,512]{1,0:T(8,128)(2,1)}, bf16[704,512]{1,0:T(8,128)(2,1)S(1)}, u32[]{:S(2)}, u32[]{:S(2)}) collective-permute-start(bf16[704,512]{1,0:T(8,128)(2,1)} %bitcast.12), channel_id=1, source_target_pairs={{0,1},{1,0},{2,3},{3,2},{4,5},{5,4},{6,7},{7,6},{8,9},{9,8},{10,11... | collective-permute-start | bytes 2162696 | tf_op jit(solution)/shard_map/ppermute | solution.py:327
  15.9 3.4 %collective-permute-start.5 = (bf16[16,704]{1,0:T(8,128)(2,1)S(1)}, bf16[16,704]{1,0:T(8,128)(2,1)S(1)}, u32[]{:S(2)}, u32[]{:S(2)}) collective-permute-start(bf16[16,704]{1,0:T(8,128)(2,1)S(1)} %fusion.2), channel_id=1, source_target_pairs={{0,1},{1,0},{2,3},{3,2},{4,5},{5,4},{6,7},{7,6},{8,9},{9,8},{10,11... | collective-permute-start | bytes 67592 | tf_op jit(solution)/shard_map/ppermute | solution.py:329
  17.2 13.5 %collective-permute-start.6 = (bf16[192,896]{1,0:T(8,128)(2,1)S(1)}, bf16[192,896]{1,0:T(8,128)(2,1)S(1)}, u32[]{:S(2)}, u32[]{:S(2)}) collective-permute-start(bf16[192,896]{1,0:T(8,128)(2,1)S(1)} %collective-permute-done.refs_2_), channel_id=1, source_target_pairs={{0,16},{16,0},{1,17},{17,1},{2,18},{18,2},{3,19},{19,3},{4,20},{20... | collective-permute-start | bytes 1032200 | tf_op jit(solution)/shard_map/ppermute | solution.py:92
  17.8 12.9 %collective-permute-start.8 = (bf16[192,896]{1,0:T(8,128)(2,1)S(1)}, bf16[192,896]{1,0:T(8,128)(2,1)S(1)}, u32[]{:S(2)}, u32[]{:S(2)}) collective-permute-start(bf16[192,896]{1,0:T(8,128)(2,1)S(1)} %collective-permute-done.refs_2_), channel_id=1, source_target_pairs={{0,2},{2,0},{4,6},{6,4},{8,10},{10,8},{12,14},{14,12},{1,3},{3,1},... | collective-permute-start | bytes 1032200 | tf_op jit(solution)/shard_map/ppermute | solution.py:89
  19.4 15.4 %collective-permute-start.10 = (bf16[192,896]{1,0:T(8,128)(2,1)S(1)}, bf16[192,896]{1,0:T(8,128)(2,1)S(1)}, u32[]{:S(2)}, u32[]{:S(2)}) collective-permute-start(bf16[192,896]{1,0:T(8,128)(2,1)S(1)} %collective-permute-done.refs_2_), channel_id=1, source_target_pairs={{0,4},{2,6},{4,12},{6,14},{12,8},{14,10},{8,0},{10,2},{20,16},{22,... | collective-permute-start | bytes 1032200 | tf_op jit(solution)/shard_map/ppermute | solution.py:86
  20.4 1.1 %copy-start.2 = (bf16[512,704]{0,1:T(8,128)(2,1)S(1)}, bf16[512,704]{0,1:T(8,128)(2,1)}, u32[]{:S(2)}) copy-start(bf16[512,704]{0,1:T(8,128)(2,1)} %param.10) | copy-start | bytes 2162692
  24.4 18.8 %copy-start.4 = (bf16[192,384]{1,0:T(8,128)(2,1)S(1)}, bf16[192,384]{1,0:T(8,128)(2,1)}, u32[]{:S(2)}) copy-start(bf16[192,384]{1,0:T(8,128)(2,1)} %get-tuple-element.44) | copy-start | bytes 442372
  24.4 56.7 %copy-start.1 = (bf16[1536,256]{1,0:T(8,128)(2,1)S(1)}, bf16[1536,256]{1,0:T(8,128)(2,1)}, u32[]{:S(2)}) copy-start(bf16[1536,256]{1,0:T(8,128)(2,1)} %pair_weight_ref.1) | copy-start | bytes 2359300
  30.6 69.8 %copy-start.3 = (bf16[128,128]{1,0:T(8,128)(2,1)S(1)}, bf16[128,128]{1,0:T(8,128)(2,1)}, u32[]{:S(2)}) copy-start(bf16[128,128]{1,0:T(8,128)(2,1)} %weight_ref.1) | copy-start | bytes 98308
  30.7 10.1 %collective-permute-start.11 = (bf16[192,896]{1,0:T(8,128)(2,1)S(1)}, bf16[192,896]{1,0:T(8,128)(2,1)S(1)}, u32[]{:S(2)}, u32[]{:S(2)}) collective-permute-start(bf16[192,896]{1,0:T(8,128)(2,1)S(1)} %collective-permute-done.8.refs_3_), channel_id=1, source_target_pairs={{0,4},{2,6},{4,12},{6,14},{12,8},{14,10},{8,0},{10,2},{20,16},{22,... | collective-permute-start | bytes 1032200 | tf_op jit(solution)/shard_map/ppermute | solution.py:86
  33.2 8.9 %collective-permute-start.9 = (bf16[192,896]{1,0:T(8,128)(2,1)S(1)}, bf16[192,896]{1,0:T(8,128)(2,1)S(1)}, u32[]{:S(2)}, u32[]{:S(2)}) collective-permute-start(bf16[192,896]{1,0:T(8,128)(2,1)S(1)} %collective-permute-done.8.refs_3_), channel_id=1, source_target_pairs={{0,16},{16,0},{1,17},{17,1},{2,18},{18,2},{3,19},{19,3},{4,20},{20... | collective-permute-start | bytes 1032200 | tf_op jit(solution)/shard_map/ppermute | solution.py:92
  33.2 6.9 %collective-permute-start.7 = (bf16[192,640]{1,0:T(8,128)(2,1)S(1)}, bf16[192,640]{1,0:T(8,128)(2,1)}, u32[]{:S(2)}, u32[]{:S(2)}) collective-permute-start(bf16[192,640]{1,0:T(8,128)(2,1)S(1)} %pad_maximum_fusion.2), channel_id=1, source_target_pairs={{0,2},{2,0},{4,6},{6,4},{8,10},{10,8},{12,14},{14,12},{1,3},{3,1},... | collective-permute-start | bytes 737288 | tf_op jit(solution)/shard_map/ppermute | solution.py:365
  43.1 2.0 %collective-permute-start.12 = (bf16[8,128,192]{2,1,0:T(8,128)(2,1)S(1)}, bf16[8,128,192]{2,1,0:T(8,128)(2,1)S(1)}, u32[]{:S(2)}, u32[]{:S(2)}) collective-permute-start(bf16[8,128,192]{2,1,0:T(8,128)(2,1)S(1)} %get-tuple-element.30.part_ref), channel_id=1, source_target_pairs={{0,1},{1,0},{2,3},{3,2},{4,5},{5,4},{6,7},{7,6},{8,9},{9,8},{10,11... | collective-permute-start | bytes 1179656 | tf_op jit(solution)/shard_map/ppermute | solution.py:387
  44.3 16.0 %collective-permute-start.14 = (bf16[384,640]{1,0:T(8,128)(2,1)S(1)}, bf16[384,640]{1,0:T(8,128)(2,1)S(1)}, u32[]{:S(2)}, u32[]{:S(2)}) collective-permute-start(bf16[384,640]{1,0:T(8,128)(2,1)S(1)} %pad_maximum_fusion.refs_2_.refs_0_), channel_id=1, source_target_pairs={{0,4},{2,6},{4,12},{6,14},{12,8},{14,10},{8,0},{10,2},{20,16},{22,... | collective-permute-start | bytes 1474568 | tf_op jit(solution)/shard_map/ppermute | solution.py:86
  45.7 4.7 %collective-permute-start.17 = (bf16[192,128]{1,0:T(8,128)(2,1)S(1)}, bf16[192,128]{1,0:T(8,128)(2,1)S(1)}, u32[]{:S(2)}, u32[]{:S(2)}) collective-permute-start(bf16[192,128]{1,0:T(8,128)(2,1)S(1)} %get-tuple-element.36), channel_id=1, source_target_pairs={{0,2},{2,0},{4,6},{6,4},{8,10},{10,8},{12,14},{14,12},{1,3},{3,1},... | collective-permute-start | bytes 147464 | tf_op jit(solution)/shard_map/ppermute | solution.py:404
  46.6 14.3 %collective-permute-start.13 = (bf16[8,128,192]{2,1,0:T(8,128)(2,1)S(1)}, bf16[8,128,192]{2,1,0:T(8,128)(2,1)S(1)}, u32[]{:S(2)}, u32[]{:S(2)}) collective-permute-start(bf16[8,128,192]{2,1,0:T(8,128)(2,1)S(1)} %get-tuple-element.33.refs_0_), channel_id=1, source_target_pairs={{0,2},{2,0},{4,6},{6,4},{8,10},{10,8},{12,14},{14,12},{1,3},{3,1},... | collective-permute-start | bytes 1179656 | tf_op jit(solution)/shard_map/ppermute | solution.py:405
  50.4 9.9 %collective-permute-start.18 = (bf16[2,192,128]{2,1,0:T(8,128)(2,1)S(1)}, bf16[2,192,128]{2,1,0:T(8,128)(2,1)S(1)}, u32[]{:S(2)}, u32[]{:S(2)}) collective-permute-start(bf16[2,192,128]{2,1,0:T(8,128)(2,1)S(1)} %pad_maximum_fusion.3), channel_id=1, source_target_pairs={{0,4},{2,6},{4,12},{6,14},{12,8},{14,10},{8,0},{10,2},{1,5},{3,7},... | collective-permute-start | bytes 294920 | tf_op jit(solution)/shard_map/ppermute | solution.py:413
  52.6 14.6 %collective-permute-start.19 = (bf16[2,192,128]{2,1,0:T(8,128)(2,1)S(1)}, bf16[2,192,128]{2,1,0:T(8,128)(2,1)S(1)}, u32[]{:S(2)}, u32[]{:S(2)}) collective-permute-start(bf16[2,192,128]{2,1,0:T(8,128)(2,1)S(1)} %pad_maximum_fusion.3), channel_id=1, source_target_pairs={{4,0},{6,2},{12,4},{14,6},{8,12},{10,14},{0,8},{2,10},{5,1},{7,3},... | collective-permute-start | bytes 294920 | tf_op jit(solution)/shard_map/ppermute | solution.py:413
  52.6 25.2 %collective-permute-start.20 = (bf16[2,192,128]{2,1,0:T(8,128)(2,1)S(1)}, bf16[2,192,128]{2,1,0:T(8,128)(2,1)S(1)}, u32[]{:S(2)}, u32[]{:S(2)}) collective-permute-start(bf16[2,192,128]{2,1,0:T(8,128)(2,1)S(1)} %pad_maximum_fusion.3), channel_id=1, source_target_pairs={{0,12},{2,14},{4,8},{6,10},{12,0},{14,2},{8,4},{10,6},{1,13},{3,15... | collective-permute-start | bytes 294920 | tf_op jit(solution)/shard_map/ppermute | solution.py:413
  60.9 17.1 %collective-permute-start.15 = (bf16[384,640]{1,0:T(8,128)(2,1)S(1)}, bf16[384,640]{1,0:T(8,128)(2,1)S(1)}, u32[]{:S(2)}, u32[]{:S(2)}) collective-permute-start(bf16[384,640]{1,0:T(8,128)(2,1)S(1)} %collective-permute-done.14.refs_3_.refs_1_), channel_id=1, source_target_pairs={{0,16},{16,0},{1,17},{17,1},{2,18},{18,2},{3,19},{19,3},{4,20},{20... | collective-permute-start | bytes 1474568 | tf_op jit(solution)/shard_map/ppermute | solution.py:92
  64.0 13.9 %collective-permute-start.16 = (bf16[384,640]{1,0:T(8,128)(2,1)S(1)}, bf16[384,640]{1,0:T(8,128)(2,1)S(1)}, u32[]{:S(2)}, u32[]{:S(2)}) collective-permute-start(bf16[384,640]{1,0:T(8,128)(2,1)S(1)} %collective-permute-done.14.refs_3_.refs_1_), channel_id=1, source_target_pairs={{0,4},{2,6},{4,12},{6,14},{12,8},{14,10},{8,0},{10,2},{20,16},{22,... | collective-permute-start | bytes 1474568 | tf_op jit(solution)/shard_map/ppermute | solution.py:86
  77.9 1.8 %collective-permute-start.21 = (bf16[8,192,128]{2,1,0:T(8,128)(2,1)S(1)}, bf16[8,192,128]{2,1,0:T(8,128)(2,1)S(1)}, u32[]{:S(2)}, u32[]{:S(2)}) collective-permute-start(bf16[8,192,128]{2,1,0:T(8,128)(2,1)S(1)} %constant_dynamic-update-slice_fusion.own_ref), channel_id=1, source_target_pairs={{0,1},{1,0},{2,3},{3,2},{4,5},{5,4},{6,7},{7,6},{8,9},{9,8},{10,11... | collective-permute-start | bytes 1179656 | tf_op jit(solution)/shard_map/ppermute | solution.py:416
  82.5 3.7 %collective-permute-start.24 = (bf16[16,256]{1,0:T(8,128)(2,1)S(1)}, bf16[16,256]{1,0:T(8,128)(2,1)S(1)}, u32[]{:S(2)}, u32[]{:S(2)}) collective-permute-start(bf16[16,256]{1,0:T(8,128)(2,1)S(1)} %get-tuple-element.39), channel_id=1, source_target_pairs={{0,2},{2,0},{4,6},{6,4},{8,10},{10,8},{12,14},{14,12},{1,3},{3,1},... | collective-permute-start | bytes 24584 | tf_op jit(solution)/shard_map/ppermute | solution.py:457
  82.9 3.5 %collective-permute-start.22 = (bf16[128,1536]{1,0:T(8,128)(2,1)S(1)}, bf16[128,1536]{1,0:T(8,128)(2,1)S(1)}, u32[]{:S(2)}, u32[]{:S(2)}) collective-permute-start(bf16[128,1536]{1,0:T(8,128)(2,1)S(1)} %get-tuple-element.38), channel_id=1, source_target_pairs={{0,1},{1,0},{2,3},{3,2},{4,5},{5,4},{6,7},{7,6},{8,9},{9,8},{10,11... | collective-permute-start | bytes 1179656 | tf_op jit(solution)/shard_map/ppermute | solution.py:460
  86.3 1.2 %collective-permute-start.25 = (bf16[16,256]{1,0:T(8,128)(2,1)S(1)}, bf16[16,256]{1,0:T(8,128)(2,1)S(1)}, u32[]{:S(2)}, u32[]{:S(2)}) collective-permute-start(bf16[16,256]{1,0:T(8,128)(2,1)S(1)} %add_convert_fusion.2), channel_id=1, source_target_pairs={{0,1},{1,0},{2,3},{3,2},{4,5},{5,4},{6,7},{7,6},{8,9},{9,8},{10,11... | collective-permute-start | bytes 24584 | tf_op jit(solution)/shard_map/ppermute | solution.py:459
  86.5 7.4 %collective-permute-start.23 = (bf16[64,1536]{1,0:T(8,128)(2,1)S(1)}, bf16[64,1536]{1,0:T(8,128)(2,1)S(1)}, u32[]{:S(2)}, u32[]{:S(2)}) collective-permute-start(bf16[64,1536]{1,0:T(8,128)(2,1)S(1)} %get-tuple-element.46), channel_id=1, source_target_pairs={{0,2},{2,0},{4,6},{6,4},{8,10},{10,8},{12,14},{14,12},{1,3},{3,1},... | collective-permute-start | bytes 589832 | tf_op jit(solution)/shard_map/ppermute | solution.py:464
  87.5 3.7 %collective-permute-start.26 = (bf16[16,256]{1,0:T(8,128)(2,1)S(1)}, bf16[16,256]{1,0:T(8,128)(2,1)S(1)}, u32[]{:S(2)}, u32[]{:S(2)}) collective-permute-start(bf16[16,256]{1,0:T(8,128)(2,1)S(1)} %add_convert_fusion.1), channel_id=1, source_target_pairs={{0,4},{2,6},{4,0},{6,2},{8,12},{10,14},{12,8},{14,10},{1,5},{3,7},... | collective-permute-start | bytes 24584 | tf_op jit(solution)/shard_map/ppermute | solution.py:466
  93.9 6.5 %collective-permute-start.27 = (bf16[32,256]{1,0:T(8,128)(2,1)S(1)}, bf16[32,256]{1,0:T(8,128)(2,1)S(1)}, u32[]{:S(2)}, u32[]{:S(2)}) collective-permute-start(bf16[32,256]{1,0:T(8,128)(2,1)S(1)} %pad_maximum_fusion.4), channel_id=1, source_target_pairs={{0,8},{2,10},{4,12},{6,14},{9,1},{11,3},{13,5},{15,7},{16,24},{18,... | collective-permute-start | bytes 49160 | tf_op jit(solution)/shard_map/ppermute | solution.py:469

commit v13 on v12

--- a/solution.py
+++ b/solution.py
@@ -401,16 +401,15 @@
     )(part, other_part, attn_gain.reshape(pieces, 1, block), keyvalue_blocks)
     both_normed = [normed]
     if ring:
-        here = jnp.stack([keyvalue, lax.ppermute(keyvalue, "seq", pair_swap)])
+        turns = [[(2 * RING[k] + i, 2 * RING[(k + t) % 4] + i) for k in range(4) for i in range(2)] for t in (1, 3, 2)]
+        turned = [lax.ppermute(keyvalue, "seq", turn) for turn in turns]
         both_normed.append(lax.ppermute(normed, "seq", pair_swap))
         q.at["step"] = after(q.at["step"], both_normed[1])
         q.along("step", "far")
         q.between("step", "cross")
         later_blocks = [q.at[name] for name in ("own", "step", "cross", "far")]
-        onward = [(2 * RING[k] + i, 2 * RING[(k + 1) % 4] + i) for k in range(4) for i in range(2)]
-        opposite = [(2 * RING[k] + i, 2 * RING[(k + 2) % 4] + i) for k in range(4) for i in range(2)]
-        turns = [onward, [(j, i) for i, j in onward], opposite]
-        gathered = jnp.concatenate([here] + [lax.ppermute(here, "seq", turn) for turn in turns])
+        row = jnp.stack([keyvalue] + after(turned, q.at["step"]))
+        gathered = jnp.concatenate([row, lax.ppermute(row, "seq", pair_swap)])
     else:
         gathered = lax.all_gather(keyvalue, "seq", axis=0)
     gathered_other = lax.ppermute(gathered, "col", swap)

time: 102 us -> 101 us (level)
  the two profiles are of different devices: /device:TPU:22 before, /device:TPU:0 now
where the time goes in v13:
time: 101 us; the launch traced here: 100 us
  waiting for transfers between devices  40.8 us (40%)
  starting transfers between devices  31.5 us (31%)
  Pallas kernels  17.4 us (17%)
  local copies, waits for them, and re-layouts  8.2 us (8%)
  other arithmetic  1.41 us (1%)
    ppermute x5, starting transfers between devices, along(): self.at[target] = lax.ppermute(self.at[source], ('grp', 'seq'), pairs)  8.47 us
    ppermute x1, waiting for transfers between devices, on_device(): received = lax.ppermute(theirs, 'seq', pair_swap)  6.5 us
    pallas_call x1, Pallas kernels, on_device(): pl.pallas_call(functools.partial(conv_kernel, positions), out_shape=shape...  6.2 us
    ppermute x5, waiting for transfers between devices, along(): self.at[target] = lax.ppermute(self.at[source], ('grp', 'seq'), pairs)  5.62 us
    ppermute x3, starting transfers between devices, on_device(): turned = [lax.ppermute(keyvalue, 'seq', turn) for turn in turns]  5.52 us
    ppermute x3, waiting for transfers between devices, between(): self.at[target] = lax.ppermute(self.at[source], 'grp', [(0, 1), (1, 0)])  5.26 us
    ppermute x1, waiting for transfers between devices, on_device(): gathered = jnp.concatenate([row, lax.ppermute(row, 'seq', pair_swap)])  5.03 us
    ppermute x1, waiting for transfers between devices, on_device(): both_normed.append(lax.ppermute(normed, 'seq', pair_swap))  4.57 us
  transfers between devices with their start and end apart: 28, of which 14 were waited for; matrix products, arithmetic and copies ran while one was open for 5% of the time, Pallas kernels for 12%

profile of v13, /device:TPU:0, one launch (start us, length us, event | category | flops | bytes accessed | tf_op | source)
XLA Modules:
  0.0 100.2 jit_solution(14061295104039994396)
XLA Ops:
  0.7 0.9 copy-done
  1.6 1.1 %pad_maximum_fusion.1.refs_0_ = bf16[192,896]{1,0:T(8,128)(2,1)S(1)} fusion(bf16[192,192]{1,0:T(8,128)(2,1)S(1)} %constant_dynamic-slice_fusion.2, bf16[192,704]{1,0:T(8,128)(2,1)} %bitcast.19), kind=kLoop, calls=%fused_computation.2 | loop fusion | flops 688128 | bytes 688128 | tf_op jit(solution)/shard_map/concatenate | solution.py:295
  2.7 3.1 %collective-permute-start = (bf16[192,896]{1,0:T(8,128)(2,1)S(1)}, bf16[192,896]{1,0:T(8,128)(2,1)S(1)}, u32[]{:S(2)}, u32[]{:S(2)}) collective-permute-start(bf16[192,896]{1,0:T(8,128)(2,1)S(1)} %pad_maximum_fusion.1.refs_0_), channel_id=1, source_target_pairs={{0,4},{2,6},{4,12},{6,14},{12,8},{14,10},{8,0},{10,2},{20,16},{22,... | collective-permute-start | bytes 1032200 | tf_op jit(solution)/shard_map/ppermute | solution.py:86
  5.8 1.5 %collective-permute-start.1 = (bf16[192,896]{1,0:T(8,128)(2,1)S(1)}, bf16[192,896]{1,0:T(8,128)(2,1)S(1)}, u32[]{:S(2)}, u32[]{:S(2)}) collective-permute-start(bf16[192,896]{1,0:T(8,128)(2,1)S(1)} %pad_maximum_fusion.1.refs_0_), channel_id=1, source_target_pairs={{0,2},{2,0},{4,6},{6,4},{8,10},{10,8},{12,14},{14,12},{1,3},{3,1},... | collective-permute-start | bytes 1032200 | tf_op jit(solution)/shard_map/ppermute | solution.py:89
  7.3 1.1 %fusion.3 = (bf16[2,704]{0,1:T(8,128)(2,1)S(1)}, bf16[2,704]{0,1:T(8,128)(2,1)S(1)}) fusion(bf16[512,704]{0,1:T(8,128)(2,1)} %param.10), kind=kLoop, calls=%fused_computation.24 | loop fusion | bytes 11264 | tf_op jit(solution)/shard_map/slice | solution.py:322
  8.6 2.4 %collective-permute-start.2 = (bf16[2,704]{1,0:T(2,128)(2,1)S(1)}, bf16[2,704]{1,0:T(2,128)(2,1)S(1)}, u32[]{:S(2)}, u32[]{:S(2)}) collective-permute-start(bf16[2,704]{1,0:T(2,128)(2,1)S(1)} %copy.14), channel_id=1, source_target_pairs={{0,2},{2,4},{4,6},{6,8},{8,10},{10,12},{12,14},{1,3},{3,5},{5,7},{... | collective-permute-start | bytes 8456 | tf_op jit(solution)/shard_map/ppermute | solution.py:321
  11.1 1.3 %collective-permute-start.3 = (bf16[2,704]{1,0:T(2,128)(2,1)S(1)}, bf16[2,704]{1,0:T(2,128)(2,1)S(1)}, u32[]{:S(2)}, u32[]{:S(2)}) collective-permute-start(bf16[2,704]{1,0:T(2,128)(2,1)S(1)} %copy.15), channel_id=1, source_target_pairs={{2,0},{4,2},{6,4},{8,6},{10,8},{12,10},{14,12},{3,1},{5,3},{7,5},{... | collective-permute-start | bytes 8456 | tf_op jit(solution)/shard_map/ppermute | solution.py:322
  12.5 1.0 constant_dynamic-slice_fusion.1
  13.4 1.0 %dynamic-slice_bitcast_fusion.1 = (bf16[192,384]{1,0:T(8,128)(2,1)S(1)}, bf16[192,384]{1,0:T(8,128)(2,1)S(1)}) fusion(bf16[1536,192]{0,1:T(8,128)(2,1)} %param.17, s32[]{:T(128)S(6)} %select_n.45, s32[]{:T(128)S(6)} %select_n.47), kind=kLoop, calls=%fused_computation.6 | loop fusion | bytes 589832 | tf_op jit(solution)/shard_map/dynamic_slice | solution.py:309
  14.5 3.7 %collective-permute-done.3 = bf16[2,704]{1,0:T(2,128)(2,1)S(1)} collective-permute-done((bf16[2,704]{1,0:T(2,128)(2,1)S(1)}, bf16[2,704]{1,0:T(2,128)(2,1)S(1)}, u32[]{:S(2)}, u32[]{:S(2)}) %collective-permute-start.3) | collective-permute-done | bytes 2848 | tf_op jit(solution)/shard_map/ppermute | solution.py:322
  18.8 0.7 reshape.10.gain_ref
  19.5 1.0 collective-permute-start.6
  20.4 1.9 %collective-permute-start.8 = (bf16[192,896]{1,0:T(8,128)(2,1)S(1)}, bf16[192,896]{1,0:T(8,128)(2,1)S(1)}, u32[]{:S(2)}, u32[]{:S(2)}) collective-permute-start(bf16[192,896]{1,0:T(8,128)(2,1)S(1)} %collective-permute-done.refs_2_), channel_id=1, source_target_pairs={{0,2},{2,0},{4,6},{6,4},{8,10},{10,8},{12,14},{14,12},{1,3},{3,1},... | collective-permute-start | bytes 1032200 | tf_op jit(solution)/shard_map/ppermute | solution.py:89
  22.5 2.1 %collective-permute-start.10 = (bf16[192,896]{1,0:T(8,128)(2,1)S(1)}, bf16[192,896]{1,0:T(8,128)(2,1)S(1)}, u32[]{:S(2)}, u32[]{:S(2)}) collective-permute-start(bf16[192,896]{1,0:T(8,128)(2,1)S(1)} %collective-permute-done.refs_2_), channel_id=1, source_target_pairs={{0,4},{2,6},{4,12},{6,14},{12,8},{14,10},{8,0},{10,2},{20,16},{22,... | collective-permute-start | bytes 1032200 | tf_op jit(solution)/shard_map/ppermute | solution.py:86
  24.6 1.1 %copy-done.4 = bf16[512,704]{0,1:T(8,128)(2,1)S(1)} copy-done((bf16[512,704]{0,1:T(8,128)(2,1)S(1)}, bf16[512,704]{0,1:T(8,128)(2,1)}, u32[]{:S(2)}) %copy-start.4) | copy-done | bytes 720920
  25.7 2.8 %act.1 = (bf16[640,1408]{1,0:T(8,128)(2,1)S(1)}, f32[128,704]{1,0:T(8,128)S(1)}) custom-call(bf16[704,512]{1,0:T(8,128)(2,1)S(1)} %bitcast.17, bf16[704,512]{1,0:T(8,128)(2,1)S(1)} %collective-permute-done.4.other_ref, f32[1,1408]{1,0:T(1,128)S(1)} %reshape.10.gain_ref), custom_call_target="tpu_custom_call" | custom-call | flops 922746880 | bytes 2883584 | tf_op jit(solution)/shard_map/act/pallas_call | solution.py:334
  28.6 6.2 %conv.1.pooled_ref = bf16[128,704]{1,0:T(8,128)(2,1)S(1)} custom-call(bf16[640,1408]{1,0:T(8,128)(2,1)S(1)} %get-tuple-element.26.windows_ref, f32[128,704]{1,0:T(8,128)S(1)} %get-tuple-element.27.residual_ref, bf16[16,1408]{1,0:T(8,128)(2,1)S(1)} %maximum_select_fusion.halo_ref, f32[1,1408]{1,0:T(1,128)S(1)} %reshape.10.gain_ref, bf16[5,704,1408]{2,1,0:T(8,128)(2,1)} %bitcast.18), custom_call_target="tpu_custom_call" | custom-call | flops 1268776960 | bytes 9912320 | tf_op jit(solution)/shard_map/conv/pallas_call | solution.py:349
  35.3 1.6 %collective-permute-start.11 = (bf16[192,896]{1,0:T(8,128)(2,1)S(1)}, bf16[192,896]{1,0:T(8,128)(2,1)S(1)}, u32[]{:S(2)}, u32[]{:S(2)}) collective-permute-start(bf16[192,896]{1,0:T(8,128)(2,1)S(1)} %collective-permute-done.8.refs_3_), channel_id=1, source_target_pairs={{0,4},{2,6},{4,12},{6,14},{12,8},{14,10},{8,0},{10,2},{20,16},{22,... | collective-permute-start | bytes 1032200 | tf_op jit(solution)/shard_map/ppermute | solution.py:86
  36.9 6.5 %collective-permute-done.7 = bf16[192,640]{1,0:T(8,128)(2,1)S(1)} collective-permute-done((bf16[192,640]{1,0:T(8,128)(2,1)S(1)}, bf16[192,640]{1,0:T(8,128)(2,1)S(1)}, u32[]{:S(2)}, u32[]{:S(2)}) %collective-permute-start.7) | collective-permute-done | bytes 245792 | tf_op jit(solution)/shard_map/ppermute | solution.py:365
  44.0 1.0 %collective-permute-done.11.refs_7_ = bf16[192,896]{1,0:T(8,128)(2,1)S(1)} collective-permute-done((bf16[192,896]{1,0:T(8,128)(2,1)S(1)}, bf16[192,896]{1,0:T(8,128)(2,1)S(1)}, u32[]{:S(2)}, u32[]{:S(2)}) %collective-permute-start.11) | collective-permute-done | bytes 344096 | tf_op jit(solution)/shard_map/ppermute | solution.py:86
  45.1 1.8 %embed.1 = (bf16[8,128,192]{2,1,0:T(8,128)(2,1)}, bf16[8,192,192]{2,1,0:T(8,128)(2,1)S(1)}) custom-call(bf16[128,704]{1,0:T(8,128)(2,1)S(1)} %conv.1.pooled_ref, bf16[192,896]{1,0:T(8,128)(2,1)S(1)} %pad_maximum_fusion.1.refs_0_, bf16[192,896]{1,0:T(8,128)(2,1)S(1)} %collective-permute-done.1.refs_1_, bf16[192,896]{1,0:T(8,128)(2,1)S(1)} %collective-permute-done.refs_2_, ...), custom_call_target="tpu_custom_call" | custom-call | flops 276824064 | bytes 2162688 | tf_op jit(solution)/shard_map/embed/pallas_call | solution.py:378
  46.9 0.7 collective-permute-start.14
  47.7 1.3 %collective-permute-done.12.other_ref = bf16[8,128,192]{2,1,0:T(8,128)(2,1)S(1)} collective-permute-done((bf16[8,128,192]{2,1,0:T(8,128)(2,1)}, bf16[8,128,192]{2,1,0:T(8,128)(2,1)S(1)}, u32[]{:S(2)}, u32[]{:S(2)}) %collective-permute-start.12) | collective-permute-done | bytes 393248 | tf_op jit(solution)/shard_map/ppermute | solution.py:387
  49.0 0.8 copy-done.2
  49.8 1.0 %copy-done.3 = bf16[8,128,192]{2,1,0:T(8,128)(2,1)S(1)} copy-done((bf16[8,128,192]{2,1,0:T(8,128)(2,1)S(1)}, bf16[8,128,192]{2,1,0:T(8,128)(2,1)}, u32[]{:S(2)}) %copy-start.3) | copy-done | bytes 393240
  50.8 1.7 %keyvalue.1 = (bf16[192,128]{1,0:T(8,128)(2,1)S(1)}, bf16[8,128,192]{2,1,0:T(8,128)(2,1)S(1)}, bf16[8,128,192]{2,1,0:T(8,128)(2,1)S(1)}) custom-call(bf16[8,128,192]{2,1,0:T(8,128)(2,1)} %get-tuple-element.33.part_ref, bf16[8,128,192]{2,1,0:T(8,128)(2,1)S(1)} %copy-done.3, f32[8,1,192]{2,1,0:T(1,128)S(1)} %reshape.11.gain_ref, ...), custom_call_target="tpu_custom_call" | custom-call | flops 75497472 | bytes 589824 | tf_op jit(solution)/shard_map/keyvalue/pallas_call | solution.py:389
  52.5 1.0 %collective-permute-start.13 = (bf16[8,128,192]{2,1,0:T(8,128)(2,1)S(1)}, bf16[8,128,192]{2,1,0:T(8,128)(2,1)S(1)}, u32[]{:S(2)}, u32[]{:S(2)}) collective-permute-start(bf16[8,128,192]{2,1,0:T(8,128)(2,1)S(1)} %get-tuple-element.36.refs_0_), channel_id=1, source_target_pairs={{0,2},{2,0},{4,6},{6,4},{8,10},{10,8},{12,14},{14,12},{1,3},{3,1},... | collective-permute-start | bytes 1179656 | tf_op jit(solution)/shard_map/ppermute | solution.py:406
  53.5 1.2 %collective-permute-start.17 = (bf16[192,128]{1,0:T(8,128)(2,1)S(1)}, bf16[192,128]{1,0:T(8,128)(2,1)S(1)}, u32[]{:S(2)}, u32[]{:S(2)}) collective-permute-start(bf16[192,128]{1,0:T(8,128)(2,1)S(1)} %get-tuple-element.39), channel_id=1, source_target_pairs={{0,4},{2,6},{4,12},{6,14},{12,8},{14,10},{8,0},{10,2},{1,5},{3,7},... | collective-permute-start | bytes 147464 | tf_op jit(solution)/shard_map/ppermute | solution.py:405
  54.7 1.7 %collective-permute-start.18 = (bf16[192,128]{1,0:T(8,128)(2,1)S(1)}, bf16[192,128]{1,0:T(8,128)(2,1)S(1)}, u32[]{:S(2)}, u32[]{:S(2)}) collective-permute-start(bf16[192,128]{1,0:T(8,128)(2,1)S(1)} %get-tuple-element.39), channel_id=1, source_target_pairs={{0,8},{2,10},{4,0},{6,2},{12,4},{14,6},{8,12},{10,14},{1,9},{3,11}... | collective-permute-start | bytes 147464 | tf_op jit(solution)/shard_map/ppermute | solution.py:405
  56.4 2.6 %collective-permute-start.19 = (bf16[192,128]{1,0:T(8,128)(2,1)S(1)}, bf16[192,128]{1,0:T(8,128)(2,1)S(1)}, u32[]{:S(2)}, u32[]{:S(2)}) collective-permute-start(bf16[192,128]{1,0:T(8,128)(2,1)S(1)} %get-tuple-element.39), channel_id=1, source_target_pairs={{0,12},{2,14},{4,8},{6,10},{12,0},{14,2},{8,4},{10,6},{1,13},{3,15... | collective-permute-start | bytes 147464 | tf_op jit(solution)/shard_map/ppermute | solution.py:405
  59.0 2.9 %collective-permute-done.14.refs_3_.refs_1_ = bf16[384,640]{1,0:T(8,128)(2,1)S(1)} collective-permute-done((bf16[384,640]{1,0:T(8,128)(2,1)S(1)}, bf16[384,640]{1,0:T(8,128)(2,1)S(1)}, u32[]{:S(2)}, u32[]{:S(2)}) %collective-permute-start.14) | collective-permute-done | bytes 491552 | tf_op jit(solution)/shard_map/ppermute | solution.py:86
  61.9 4.6 %collective-permute-done.13.refs_1_ = bf16[8,128,192]{2,1,0:T(8,128)(2,1)S(1)} collective-permute-done((bf16[8,128,192]{2,1,0:T(8,128)(2,1)S(1)}, bf16[8,128,192]{2,1,0:T(8,128)(2,1)S(1)}, u32[]{:S(2)}, u32[]{:S(2)}) %collective-permute-start.13) | collective-permute-done | bytes 393248 | tf_op jit(solution)/shard_map/ppermute | solution.py:406
  66.5 0.9 collective-permute-start.15
  67.4 1.0 collective-permute-start.16
  68.5 0.7 collective-permute-start.20
  69.2 5.0 %collective-permute-done.20 = bf16[4,192,128]{2,1,0:T(8,128)(2,1)S(1)} collective-permute-done((bf16[4,192,128]{2,1,0:T(8,128)(2,1)S(1)}, bf16[4,192,128]{2,1,0:T(8,128)(2,1)S(1)}, u32[]{:S(2)}, u32[]{:S(2)}) %collective-permute-start.20) | collective-permute-done | bytes 196640 | tf_op jit(solution)/shard_map/ppermute | solution.py:412
  74.4 4.6 %collective-permute-done.15.refs_4_.refs_2_ = bf16[384,640]{1,0:T(8,128)(2,1)S(1)} collective-permute-done((bf16[384,640]{1,0:T(8,128)(2,1)S(1)}, bf16[384,640]{1,0:T(8,128)(2,1)S(1)}, u32[]{:S(2)}, u32[]{:S(2)}) %collective-permute-start.15) | collective-permute-done | bytes 491552 | tf_op jit(solution)/shard_map/ppermute | solution.py:92
  78.9 1.6 %collective-permute-done.16.refs_5_.refs_3_ = bf16[384,640]{1,0:T(8,128)(2,1)S(1)} collective-permute-done((bf16[384,640]{1,0:T(8,128)(2,1)S(1)}, bf16[384,640]{1,0:T(8,128)(2,1)S(1)}, u32[]{:S(2)}, u32[]{:S(2)}) %collective-permute-start.16) | collective-permute-done | bytes 491552 | tf_op jit(solution)/shard_map/ppermute | solution.py:86
  81.0 1.4 %attend.1.attended_ref = bf16[2,256,192]{2,1,0:T(8,128)(2,1)S(1)} custom-call(bf16[256,256]{1,0:T(8,128)(2,1)S(1)} %query.1.query_ref, bf16[8,192,128]{2,1,0:T(8,128)(2,1)S(1)} %constant_dynamic-update-slice_fusion.own_ref, bf16[8,192,128]{2,1,0:T(8,128)(2,1)S(1)} %collective-permute-done.21.other_ref), custom_call_target="tpu_custom_call" | custom-call | flops 167772160 | bytes 786432 | tf_op jit(solution)/shard_map/attend/pallas_call | solution.py:427
  82.5 1.4 %output.1 = (bf16[128,1536]{1,0:T(8,128)(2,1)S(1)}, bf16[128,1536]{1,0:T(8,128)(2,1)S(1)}, bf16[16,256]{1,0:T(8,128)(2,1)S(1)}) custom-call(bf16[2,256,192]{2,1,0:T(8,128)(2,1)S(1)} %attend.1.attended_ref, bf16[8,128,192]{2,1,0:T(8,128)(2,1)S(1)} %get-tuple-element.35.embedded_ref, bf16[1536,256]{1,0:T(8,128)(2,1)S(1)} %copy-done.1, ...), custom_call_target="tpu_custom_call" | custom-call | flops 301989888 | bytes 1179648 | tf_op jit(solution)/shard_map/output/pallas_call | solution.py:441
  83.9 1.4 %collective-permute-start.24 = (bf16[16,256]{1,0:T(8,128)(2,1)S(1)}, bf16[16,256]{1,0:T(8,128)(2,1)S(1)}, u32[]{:S(2)}, u32[]{:S(2)}) collective-permute-start(bf16[16,256]{1,0:T(8,128)(2,1)S(1)} %get-tuple-element.45), channel_id=1, source_target_pairs={{0,2},{2,0},{4,6},{6,4},{8,10},{10,8},{12,14},{14,12},{1,3},{3,1},... | collective-permute-start | bytes 24584 | tf_op jit(solution)/shard_map/ppermute | solution.py:456
  85.3 2.3 %collective-permute-done.24 = bf16[16,256]{1,0:T(8,128)(2,1)S(1)} collective-permute-done((bf16[16,256]{1,0:T(8,128)(2,1)S(1)}, bf16[16,256]{1,0:T(8,128)(2,1)S(1)}, u32[]{:S(2)}, u32[]{:S(2)}) %collective-permute-start.24) | collective-permute-done | bytes 8224 | tf_op jit(solution)/shard_map/ppermute | solution.py:456
  87.9 1.4 %collective-permute-start.23 = (bf16[64,1536]{1,0:T(8,128)(2,1)S(1)}, bf16[64,1536]{1,0:T(8,128)(2,1)S(1)}, u32[]{:S(2)}, u32[]{:S(2)}) collective-permute-start(bf16[64,1536]{1,0:T(8,128)(2,1)S(1)} %get-tuple-element.52), channel_id=1, source_target_pairs={{0,2},{2,0},{4,6},{6,4},{8,10},{10,8},{12,14},{14,12},{1,3},{3,1},... | collective-permute-start | bytes 589832 | tf_op jit(solution)/shard_map/ppermute | solution.py:463
  89.3 3.6 %collective-permute-done.26 = bf16[16,256]{1,0:T(8,128)(2,1)S(1)} collective-permute-done((bf16[16,256]{1,0:T(8,128)(2,1)S(1)}, bf16[16,256]{1,0:T(8,128)(2,1)S(1)}, u32[]{:S(2)}, u32[]{:S(2)}) %collective-permute-start.26) | collective-permute-done | bytes 8224 | tf_op jit(solution)/shard_map/ppermute | solution.py:465
  92.9 2.3 %collective-permute-done.23.refs_1_ = bf16[64,1536]{1,0:T(8,128)(2,1)S(1)} collective-permute-done((bf16[64,1536]{1,0:T(8,128)(2,1)S(1)}, bf16[64,1536]{1,0:T(8,128)(2,1)S(1)}, u32[]{:S(2)}, u32[]{:S(2)}) %collective-permute-start.23) | collective-permute-done | bytes 196640 | tf_op jit(solution)/shard_map/ppermute | solution.py:463
  95.3 2.7 %collective-permute-start.27 = (bf16[32,256]{1,0:T(8,128)(2,1)S(1)}, bf16[32,256]{1,0:T(8,128)(2,1)S(1)}, u32[]{:S(2)}, u32[]{:S(2)}) collective-permute-start(bf16[32,256]{1,0:T(8,128)(2,1)S(1)} %pad_maximum_fusion.4), channel_id=1, source_target_pairs={{0,8},{2,10},{4,12},{6,14},{9,1},{11,3},{13,5},{15,7},{16,24},{18,... | collective-permute-start | bytes 49160 | tf_op jit(solution)/shard_map/ppermute | solution.py:468
  98.0 0.8 tokens.1
  99.4 0.8 pair.1
  (58 shorter events, 3.8 us)
Async XLA Ops:
  0.6 0.9 copy-start
  2.7 15.4 %collective-permute-start = (bf16[192,896]{1,0:T(8,128)(2,1)S(1)}, bf16[192,896]{1,0:T(8,128)(2,1)S(1)}, u32[]{:S(2)}, u32[]{:S(2)}) collective-permute-start(bf16[192,896]{1,0:T(8,128)(2,1)S(1)} %pad_maximum_fusion.1.refs_0_), channel_id=1, source_target_pairs={{0,4},{2,6},{4,12},{6,14},{12,8},{14,10},{8,0},{10,2},{20,16},{22,... | collective-permute-start | bytes 1032200 | tf_op jit(solution)/shard_map/ppermute | solution.py:86
  5.8 12.4 %collective-permute-start.1 = (bf16[192,896]{1,0:T(8,128)(2,1)S(1)}, bf16[192,896]{1,0:T(8,128)(2,1)S(1)}, u32[]{:S(2)}, u32[]{:S(2)}) collective-permute-start(bf16[192,896]{1,0:T(8,128)(2,1)S(1)} %pad_maximum_fusion.1.refs_0_), channel_id=1, source_target_pairs={{0,2},{2,0},{4,6},{6,4},{8,10},{10,8},{12,14},{14,12},{1,3},{3,1},... | collective-permute-start | bytes 1032200 | tf_op jit(solution)/shard_map/ppermute | solution.py:89
  8.6 5.9 %collective-permute-start.2 = (bf16[2,704]{1,0:T(2,128)(2,1)S(1)}, bf16[2,704]{1,0:T(2,128)(2,1)S(1)}, u32[]{:S(2)}, u32[]{:S(2)}) collective-permute-start(bf16[2,704]{1,0:T(2,128)(2,1)S(1)} %copy.14), channel_id=1, source_target_pairs={{0,2},{2,4},{4,6},{6,8},{8,10},{10,12},{12,14},{1,3},{3,5},{5,7},{... | collective-permute-start | bytes 8456 | tf_op jit(solution)/shard_map/ppermute | solution.py:321
  11.1 7.0 %collective-permute-start.3 = (bf16[2,704]{1,0:T(2,128)(2,1)S(1)}, bf16[2,704]{1,0:T(2,128)(2,1)S(1)}, u32[]{:S(2)}, u32[]{:S(2)}) collective-permute-start(bf16[2,704]{1,0:T(2,128)(2,1)S(1)} %copy.15), channel_id=1, source_target_pairs={{2,0},{4,2},{6,4},{8,6},{10,8},{12,10},{14,12},{3,1},{5,3},{7,5},{... | collective-permute-start | bytes 8456 | tf_op jit(solution)/shard_map/ppermute | solution.py:322
  18.2 6.4 %collective-permute-start.4 = (bf16[704,512]{1,0:T(8,128)(2,1)}, bf16[704,512]{1,0:T(8,128)(2,1)S(1)}, u32[]{:S(2)}, u32[]{:S(2)}) collective-permute-start(bf16[704,512]{1,0:T(8,128)(2,1)} %bitcast.16), channel_id=1, source_target_pairs={{0,1},{1,0},{2,3},{3,2},{4,5},{5,4},{6,7},{7,6},{8,9},{9,8},{10,11... | collective-permute-start | bytes 2162696 | tf_op jit(solution)/shard_map/ppermute | solution.py:327
  18.2 29.4 %copy-start.6 = (f32[1536]{0:T(1024)S(1)}, f32[1536]{0:T(1024)}, u32[]{:S(2)}) copy-start(f32[1536]{0:T(1024)} %param.14) | copy-start | bytes 18436
  18.2 4.2 %collective-permute-start.5 = (bf16[16,704]{1,0:T(8,128)(2,1)S(1)}, bf16[16,704]{1,0:T(8,128)(2,1)S(1)}, u32[]{:S(2)}, u32[]{:S(2)}) collective-permute-start(bf16[16,704]{1,0:T(8,128)(2,1)S(1)} %fusion.2), channel_id=1, source_target_pairs={{0,1},{1,0},{2,3},{3,2},{4,5},{5,4},{6,7},{7,6},{8,9},{9,8},{10,11... | collective-permute-start | bytes 67592 | tf_op jit(solution)/shard_map/ppermute | solution.py:329
  19.5 15.3 %collective-permute-start.6 = (bf16[192,896]{1,0:T(8,128)(2,1)S(1)}, bf16[192,896]{1,0:T(8,128)(2,1)S(1)}, u32[]{:S(2)}, u32[]{:S(2)}) collective-permute-start(bf16[192,896]{1,0:T(8,128)(2,1)S(1)} %collective-permute-done.refs_2_), channel_id=1, source_target_pairs={{0,16},{16,0},{1,17},{17,1},{2,18},{18,2},{3,19},{19,3},{4,20},{20... | collective-permute-start | bytes 1032200 | tf_op jit(solution)/shard_map/ppermute | solution.py:92
  20.4 14.4 %collective-permute-start.8 = (bf16[192,896]{1,0:T(8,128)(2,1)S(1)}, bf16[192,896]{1,0:T(8,128)(2,1)S(1)}, u32[]{:S(2)}, u32[]{:S(2)}) collective-permute-start(bf16[192,896]{1,0:T(8,128)(2,1)S(1)} %collective-permute-done.refs_2_), channel_id=1, source_target_pairs={{0,2},{2,0},{4,6},{6,4},{8,10},{10,8},{12,14},{14,12},{1,3},{3,1},... | collective-permute-start | bytes 1032200 | tf_op jit(solution)/shard_map/ppermute | solution.py:89
  22.5 14.4 %collective-permute-start.10 = (bf16[192,896]{1,0:T(8,128)(2,1)S(1)}, bf16[192,896]{1,0:T(8,128)(2,1)S(1)}, u32[]{:S(2)}, u32[]{:S(2)}) collective-permute-start(bf16[192,896]{1,0:T(8,128)(2,1)S(1)} %collective-permute-done.refs_2_), channel_id=1, source_target_pairs={{0,4},{2,6},{4,12},{6,14},{12,8},{14,10},{8,0},{10,2},{20,16},{22,... | collective-permute-start | bytes 1032200 | tf_op jit(solution)/shard_map/ppermute | solution.py:86
  24.6 1.1 %copy-start.4 = (bf16[512,704]{0,1:T(8,128)(2,1)S(1)}, bf16[512,704]{0,1:T(8,128)(2,1)}, u32[]{:S(2)}) copy-start(bf16[512,704]{0,1:T(8,128)(2,1)} %param.10) | copy-start | bytes 2162692
  28.5 53.9 %copy-start.1 = (bf16[1536,256]{1,0:T(8,128)(2,1)S(1)}, bf16[1536,256]{1,0:T(8,128)(2,1)}, u32[]{:S(2)}) copy-start(bf16[1536,256]{1,0:T(8,128)(2,1)} %pair_weight_ref.1) | copy-start | bytes 2359300
  34.8 64.7 %copy-start.5 = (bf16[128,128]{1,0:T(8,128)(2,1)S(1)}, bf16[128,128]{1,0:T(8,128)(2,1)}, u32[]{:S(2)}) copy-start(bf16[128,128]{1,0:T(8,128)(2,1)} %weight_ref.1) | copy-start | bytes 98308
  34.8 9.2 %collective-permute-start.9 = (bf16[192,896]{1,0:T(8,128)(2,1)S(1)}, bf16[192,896]{1,0:T(8,128)(2,1)S(1)}, u32[]{:S(2)}, u32[]{:S(2)}) collective-permute-start(bf16[192,896]{1,0:T(8,128)(2,1)S(1)} %collective-permute-done.8.refs_3_), channel_id=1, source_target_pairs={{0,16},{16,0},{1,17},{17,1},{2,18},{18,2},{3,19},{19,3},{4,20},{20... | collective-permute-start | bytes 1032200 | tf_op jit(solution)/shard_map/ppermute | solution.py:92
  35.3 9.8 %collective-permute-start.11 = (bf16[192,896]{1,0:T(8,128)(2,1)S(1)}, bf16[192,896]{1,0:T(8,128)(2,1)S(1)}, u32[]{:S(2)}, u32[]{:S(2)}) collective-permute-start(bf16[192,896]{1,0:T(8,128)(2,1)S(1)} %collective-permute-done.8.refs_3_), channel_id=1, source_target_pairs={{0,4},{2,6},{4,12},{6,14},{12,8},{14,10},{8,0},{10,2},{20,16},{22,... | collective-permute-start | bytes 1032200 | tf_op jit(solution)/shard_map/ppermute | solution.py:86
  36.9 6.5 %collective-permute-start.7 = (bf16[192,640]{1,0:T(8,128)(2,1)S(1)}, bf16[192,640]{1,0:T(8,128)(2,1)S(1)}, u32[]{:S(2)}, u32[]{:S(2)}) collective-permute-start(bf16[192,640]{1,0:T(8,128)(2,1)S(1)} %pad_maximum_fusion.2), channel_id=1, source_target_pairs={{0,2},{2,0},{4,6},{6,4},{8,10},{10,8},{12,14},{14,12},{1,3},{3,1},... | collective-permute-start | bytes 737288 | tf_op jit(solution)/shard_map/ppermute | solution.py:365
  46.8 2.1 %collective-permute-start.12 = (bf16[8,128,192]{2,1,0:T(8,128)(2,1)}, bf16[8,128,192]{2,1,0:T(8,128)(2,1)S(1)}, u32[]{:S(2)}, u32[]{:S(2)}) collective-permute-start(bf16[8,128,192]{2,1,0:T(8,128)(2,1)} %get-tuple-element.33.part_ref), channel_id=1, source_target_pairs={{0,1},{1,0},{2,3},{3,2},{4,5},{5,4},{6,7},{7,6},{8,9},{9,8},{10,11... | collective-permute-start | bytes 1179656 | tf_op jit(solution)/shard_map/ppermute | solution.py:387
  46.9 15.1 %collective-permute-start.14 = (bf16[384,640]{1,0:T(8,128)(2,1)S(1)}, bf16[384,640]{1,0:T(8,128)(2,1)S(1)}, u32[]{:S(2)}, u32[]{:S(2)}) collective-permute-start(bf16[384,640]{1,0:T(8,128)(2,1)S(1)} %pad_maximum_fusion.refs_2_.refs_0_), channel_id=1, source_target_pairs={{0,4},{2,6},{4,12},{6,14},{12,8},{14,10},{8,0},{10,2},{20,16},{22,... | collective-permute-start | bytes 1474568 | tf_op jit(solution)/shard_map/ppermute | solution.py:86
  48.9 0.8 copy-start.2
  49.8 1.0 %copy-start.3 = (bf16[8,128,192]{2,1,0:T(8,128)(2,1)S(1)}, bf16[8,128,192]{2,1,0:T(8,128)(2,1)}, u32[]{:S(2)}) copy-start(bf16[8,128,192]{2,1,0:T(8,128)(2,1)} %copy-done.2) | copy-start | bytes 1179652
  52.5 14.0 %collective-permute-start.13 = (bf16[8,128,192]{2,1,0:T(8,128)(2,1)S(1)}, bf16[8,128,192]{2,1,0:T(8,128)(2,1)S(1)}, u32[]{:S(2)}, u32[]{:S(2)}) collective-permute-start(bf16[8,128,192]{2,1,0:T(8,128)(2,1)S(1)} %get-tuple-element.36.refs_0_), channel_id=1, source_target_pairs={{0,2},{2,0},{4,6},{6,4},{8,10},{10,8},{12,14},{14,12},{1,3},{3,1},... | collective-permute-start | bytes 1179656 | tf_op jit(solution)/shard_map/ppermute | solution.py:406
  53.5 15.0 %collective-permute-start.17 = (bf16[192,128]{1,0:T(8,128)(2,1)S(1)}, bf16[192,128]{1,0:T(8,128)(2,1)S(1)}, u32[]{:S(2)}, u32[]{:S(2)}) collective-permute-start(bf16[192,128]{1,0:T(8,128)(2,1)S(1)} %get-tuple-element.39), channel_id=1, source_target_pairs={{0,4},{2,6},{4,12},{6,14},{12,8},{14,10},{8,0},{10,2},{1,5},{3,7},... | collective-permute-start | bytes 147464 | tf_op jit(solution)/shard_map/ppermute | solution.py:405
  54.7 13.7 %collective-permute-start.18 = (bf16[192,128]{1,0:T(8,128)(2,1)S(1)}, bf16[192,128]{1,0:T(8,128)(2,1)S(1)}, u32[]{:S(2)}, u32[]{:S(2)}) collective-permute-start(bf16[192,128]{1,0:T(8,128)(2,1)S(1)} %get-tuple-element.39), channel_id=1, source_target_pairs={{0,8},{2,10},{4,0},{6,2},{12,4},{14,6},{8,12},{10,14},{1,9},{3,11}... | collective-permute-start | bytes 147464 | tf_op jit(solution)/shard_map/ppermute | solution.py:405
  56.4 12.0 %collective-permute-start.19 = (bf16[192,128]{1,0:T(8,128)(2,1)S(1)}, bf16[192,128]{1,0:T(8,128)(2,1)S(1)}, u32[]{:S(2)}, u32[]{:S(2)}) collective-permute-start(bf16[192,128]{1,0:T(8,128)(2,1)S(1)} %get-tuple-element.39), channel_id=1, source_target_pairs={{0,12},{2,14},{4,8},{6,10},{12,0},{14,2},{8,4},{10,6},{1,13},{3,15... | collective-permute-start | bytes 147464 | tf_op jit(solution)/shard_map/ppermute | solution.py:405
  66.5 12.4 %collective-permute-start.15 = (bf16[384,640]{1,0:T(8,128)(2,1)S(1)}, bf16[384,640]{1,0:T(8,128)(2,1)S(1)}, u32[]{:S(2)}, u32[]{:S(2)}) collective-permute-start(bf16[384,640]{1,0:T(8,128)(2,1)S(1)} %collective-permute-done.14.refs_3_.refs_1_), channel_id=1, source_target_pairs={{0,16},{16,0},{1,17},{17,1},{2,18},{18,2},{3,19},{19,3},{4,20},{20... | collective-permute-start | bytes 1474568 | tf_op jit(solution)/shard_map/ppermute | solution.py:92
  67.4 13.2 %collective-permute-start.16 = (bf16[384,640]{1,0:T(8,128)(2,1)S(1)}, bf16[384,640]{1,0:T(8,128)(2,1)S(1)}, u32[]{:S(2)}, u32[]{:S(2)}) collective-permute-start(bf16[384,640]{1,0:T(8,128)(2,1)S(1)} %collective-permute-done.14.refs_3_.refs_1_), channel_id=1, source_target_pairs={{0,4},{2,6},{4,12},{6,14},{12,8},{14,10},{8,0},{10,2},{20,16},{22,... | collective-permute-start | bytes 1474568 | tf_op jit(solution)/shard_map/ppermute | solution.py:86
  68.5 5.7 %collective-permute-start.20 = (bf16[4,192,128]{2,1,0:T(8,128)(2,1)S(1)}, bf16[4,192,128]{2,1,0:T(8,128)(2,1)S(1)}, u32[]{:S(2)}, u32[]{:S(2)}) collective-permute-start(bf16[4,192,128]{2,1,0:T(8,128)(2,1)S(1)} %pad_maximum_fusion.3), channel_id=1, source_target_pairs={{0,2},{2,0},{4,6},{6,4},{8,10},{10,8},{12,14},{14,12},{1,3},{3,1},... | collective-permute-start | bytes 589832 | tf_op jit(solution)/shard_map/ppermute | solution.py:412
  74.3 6.7 %collective-permute-start.21 = (bf16[8,192,128]{2,1,0:T(8,128)(2,1)S(1)}, bf16[8,192,128]{2,1,0:T(8,128)(2,1)S(1)}, u32[]{:S(2)}, u32[]{:S(2)}) collective-permute-start(bf16[8,192,128]{2,1,0:T(8,128)(2,1)S(1)} %constant_dynamic-update-slice_fusion.own_ref), channel_id=1, source_target_pairs={{0,1},{1,0},{2,3},{3,2},{4,5},{5,4},{6,7},{7,6},{8,9},{9,8},{10,11... | collective-permute-start | bytes 1179656 | tf_op jit(solution)/shard_map/ppermute | solution.py:415
  83.9 3.7 %collective-permute-start.24 = (bf16[16,256]{1,0:T(8,128)(2,1)S(1)}, bf16[16,256]{1,0:T(8,128)(2,1)S(1)}, u32[]{:S(2)}, u32[]{:S(2)}) collective-permute-start(bf16[16,256]{1,0:T(8,128)(2,1)S(1)} %get-tuple-element.45), channel_id=1, source_target_pairs={{0,2},{2,0},{4,6},{6,4},{8,10},{10,8},{12,14},{14,12},{1,3},{3,1},... | collective-permute-start | bytes 24584 | tf_op jit(solution)/shard_map/ppermute | solution.py:456
  85.3 2.4 %collective-permute-start.22 = (bf16[128,1536]{1,0:T(8,128)(2,1)S(1)}, bf16[128,1536]{1,0:T(8,128)(2,1)S(1)}, u32[]{:S(2)}, u32[]{:S(2)}) collective-permute-start(bf16[128,1536]{1,0:T(8,128)(2,1)S(1)} %get-tuple-element.44), channel_id=1, source_target_pairs={{0,1},{1,0},{2,3},{3,2},{4,5},{5,4},{6,7},{7,6},{8,9},{9,8},{10,11... | collective-permute-start | bytes 1179656 | tf_op jit(solution)/shard_map/ppermute | solution.py:459
  87.6 1.6 %collective-permute-start.25 = (bf16[16,256]{1,0:T(8,128)(2,1)S(1)}, bf16[16,256]{1,0:T(8,128)(2,1)S(1)}, u32[]{:S(2)}, u32[]{:S(2)}) collective-permute-start(bf16[16,256]{1,0:T(8,128)(2,1)S(1)} %add_convert_fusion.2), channel_id=1, source_target_pairs={{0,1},{1,0},{2,3},{3,2},{4,5},{5,4},{6,7},{7,6},{8,9},{9,8},{10,11... | collective-permute-start | bytes 24584 | tf_op jit(solution)/shard_map/ppermute | solution.py:458
  87.9 7.4 %collective-permute-start.23 = (bf16[64,1536]{1,0:T(8,128)(2,1)S(1)}, bf16[64,1536]{1,0:T(8,128)(2,1)S(1)}, u32[]{:S(2)}, u32[]{:S(2)}) collective-permute-start(bf16[64,1536]{1,0:T(8,128)(2,1)S(1)} %get-tuple-element.52), channel_id=1, source_target_pairs={{0,2},{2,0},{4,6},{6,4},{8,10},{10,8},{12,14},{14,12},{1,3},{3,1},... | collective-permute-start | bytes 589832 | tf_op jit(solution)/shard_map/ppermute | solution.py:463
  89.3 3.7 %collective-permute-start.26 = (bf16[16,256]{1,0:T(8,128)(2,1)S(1)}, bf16[16,256]{1,0:T(8,128)(2,1)S(1)}, u32[]{:S(2)}, u32[]{:S(2)}) collective-permute-start(bf16[16,256]{1,0:T(8,128)(2,1)S(1)} %add_convert_fusion.1), channel_id=1, source_target_pairs={{0,4},{2,6},{4,0},{6,2},{8,12},{10,14},{12,8},{14,10},{1,5},{3,7},... | collective-permute-start | bytes 24584 | tf_op jit(solution)/shard_map/ppermute | solution.py:465
  95.3 4.2 %collective-permute-start.27 = (bf16[32,256]{1,0:T(8,128)(2,1)S(1)}, bf16[32,256]{1,0:T(8,128)(2,1)S(1)}, u32[]{:S(2)}, u32[]{:S(2)}) collective-permute-start(bf16[32,256]{1,0:T(8,128)(2,1)S(1)} %pad_maximum_fusion.4), channel_id=1, source_target_pairs={{0,8},{2,10},{4,12},{6,14},{9,1},{11,3},{13,5},{15,7},{16,24},{18,... | collective-permute-start | bytes 49160 | tf_op jit(solution)/shard_map/ppermute | solution.py:468

commit v14 on v13

--- a/solution.py
+++ b/solution.py
@@ -404,7 +404,6 @@
         turns = [[(2 * RING[k] + i, 2 * RING[(k + t) % 4] + i) for k in range(4) for i in range(2)] for t in (1, 3, 2)]
         turned = [lax.ppermute(keyvalue, "seq", turn) for turn in turns]
         both_normed.append(lax.ppermute(normed, "seq", pair_swap))
-        q.at["step"] = after(q.at["step"], both_normed[1])
         q.along("step", "far")
         q.between("step", "cross")
         later_blocks = [q.at[name] for name in ("own", "step", "cross", "far")]

time: 101 us -> 102 us (level)
    ppermute x3, waiting for transfers between devices: 0.01 us -> 6.06 us  [on_device(): turned = [lax.ppermute(keyvalue, 'seq', turn) for turn in turns]]
    ppermute x1, waiting for transfers between devices: 4.57 us -> 0.01 us  [on_device(): both_normed.append(lax.ppermute(normed, 'seq', pair_swap))]
    ppermute x5, waiting for transfers between devices: 5.62 us -> 3.32 us  [along(): self.at[target] = lax.ppermute(self.at[source], ('grp', 'seq'), pairs)]
    ppermute x1, waiting for transfers between devices: 5.03 us -> 6.66 us  [on_device(): gathered = jnp.concatenate([row, lax.ppermute(row, 'seq', pair_swap)])]
    ppermute x3, waiting for transfers between devices: 5.26 us -> 3.99 us  [between(): self.at[target] = lax.ppermute(self.at[source], 'grp', [(0, 1), (1, 0)])]
  transfers between devices with their start and end apart: 28 -> 28, of which waited for: 14 -> 14; matrix products, arithmetic and copies ran while one was open for 5% -> 4% of each run, Pallas kernels for 12% -> 12%
where the time goes in v14:
time: 102 us; the launch traced here: 101 us
  waiting for transfers between devices  40.8 us (40%)
  starting transfers between devices  32.5 us (32%)
  Pallas kernels  17.4 us (17%)
  local copies, waits for them, and re-layouts  8.2 us (8%)
  other arithmetic  1.41 us (1%)
    ppermute x5, starting transfers between devices, along(): self.at[target] = lax.ppermute(self.at[source], ('grp', 'seq'), pairs)  9.01 us
    ppermute x1, waiting for transfers between devices, on_device(): gathered = jnp.concatenate([row, lax.ppermute(row, 'seq', pair_swap)])  6.66 us
    ppermute x1, waiting for transfers between devices, on_device(): received = lax.ppermute(theirs, 'seq', pair_swap)  6.5 us
    pallas_call x1, Pallas kernels, on_device(): pl.pallas_call(functools.partial(conv_kernel, positions), out_shape=shape...  6.2 us
    ppermute x3, waiting for transfers between devices, on_device(): turned = [lax.ppermute(keyvalue, 'seq', turn) for turn in turns]  6.06 us
    ppermute x3, starting transfers between devices, on_device(): turned = [lax.ppermute(keyvalue, 'seq', turn) for turn in turns]  5.2 us
    unnamed x20, local copies, waits for them, and re-layouts  4.15 us
    ppermute x3, waiting for transfers between devices, between(): self.at[target] = lax.ppermute(self.at[source], 'grp', [(0, 1), (1, 0)])  3.99 us
  transfers between devices with their start and end apart: 28, of which 14 were waited for; matrix products, arithmetic and copies ran while one was open for 4% of the time, Pallas kernels for 12%

profile of v14, /device:TPU:0, one launch (start us, length us, event | category | flops | bytes accessed | tf_op | source)
XLA Modules:
  0.0 101.3 jit_solution(729121160447319039)
XLA Ops:
  0.7 0.9 copy-done
  1.6 1.1 %pad_maximum_fusion.1.refs_0_ = bf16[192,896]{1,0:T(8,128)(2,1)S(1)} fusion(bf16[192,192]{1,0:T(8,128)(2,1)S(1)} %constant_dynamic-slice_fusion.2, bf16[192,704]{1,0:T(8,128)(2,1)} %bitcast.19), kind=kLoop, calls=%fused_computation.2 | loop fusion | flops 688128 | bytes 688128 | tf_op jit(solution)/shard_map/concatenate | solution.py:295
  2.7 3.1 %collective-permute-start = (bf16[192,896]{1,0:T(8,128)(2,1)S(1)}, bf16[192,896]{1,0:T(8,128)(2,1)S(1)}, u32[]{:S(2)}, u32[]{:S(2)}) collective-permute-start(bf16[192,896]{1,0:T(8,128)(2,1)S(1)} %pad_maximum_fusion.1.refs_0_), channel_id=1, source_target_pairs={{0,4},{2,6},{4,12},{6,14},{12,8},{14,10},{8,0},{10,2},{20,16},{22,... | collective-permute-start | bytes 1032200 | tf_op jit(solution)/shard_map/ppermute | solution.py:86
  5.8 1.5 %collective-permute-start.1 = (bf16[192,896]{1,0:T(8,128)(2,1)S(1)}, bf16[192,896]{1,0:T(8,128)(2,1)S(1)}, u32[]{:S(2)}, u32[]{:S(2)}) collective-permute-start(bf16[192,896]{1,0:T(8,128)(2,1)S(1)} %pad_maximum_fusion.1.refs_0_), channel_id=1, source_target_pairs={{0,2},{2,0},{4,6},{6,4},{8,10},{10,8},{12,14},{14,12},{1,3},{3,1},... | collective-permute-start | bytes 1032200 | tf_op jit(solution)/shard_map/ppermute | solution.py:89
  7.3 1.1 %fusion.3 = (bf16[2,704]{0,1:T(8,128)(2,1)S(1)}, bf16[2,704]{0,1:T(8,128)(2,1)S(1)}) fusion(bf16[512,704]{0,1:T(8,128)(2,1)} %param.10), kind=kLoop, calls=%fused_computation.24 | loop fusion | bytes 11264 | tf_op jit(solution)/shard_map/slice | solution.py:322
  8.6 2.4 %collective-permute-start.2 = (bf16[2,704]{1,0:T(2,128)(2,1)S(1)}, bf16[2,704]{1,0:T(2,128)(2,1)S(1)}, u32[]{:S(2)}, u32[]{:S(2)}) collective-permute-start(bf16[2,704]{1,0:T(2,128)(2,1)S(1)} %copy.14), channel_id=1, source_target_pairs={{0,2},{2,4},{4,6},{6,8},{8,10},{10,12},{12,14},{1,3},{3,5},{5,7},{... | collective-permute-start | bytes 8456 | tf_op jit(solution)/shard_map/ppermute | solution.py:321
  11.1 1.3 %collective-permute-start.3 = (bf16[2,704]{1,0:T(2,128)(2,1)S(1)}, bf16[2,704]{1,0:T(2,128)(2,1)S(1)}, u32[]{:S(2)}, u32[]{:S(2)}) collective-permute-start(bf16[2,704]{1,0:T(2,128)(2,1)S(1)} %copy.15), channel_id=1, source_target_pairs={{2,0},{4,2},{6,4},{8,6},{10,8},{12,10},{14,12},{3,1},{5,3},{7,5},{... | collective-permute-start | bytes 8456 | tf_op jit(solution)/shard_map/ppermute | solution.py:322
  12.5 1.0 constant_dynamic-slice_fusion.1
  13.4 1.0 %dynamic-slice_bitcast_fusion.1 = (bf16[192,384]{1,0:T(8,128)(2,1)S(1)}, bf16[192,384]{1,0:T(8,128)(2,1)S(1)}) fusion(bf16[1536,192]{0,1:T(8,128)(2,1)} %param.17, s32[]{:T(128)S(6)} %select_n.45, s32[]{:T(128)S(6)} %select_n.47), kind=kLoop, calls=%fused_computation.6 | loop fusion | bytes 589832 | tf_op jit(solution)/shard_map/dynamic_slice | solution.py:309
  14.5 3.7 %collective-permute-done.3 = bf16[2,704]{1,0:T(2,128)(2,1)S(1)} collective-permute-done((bf16[2,704]{1,0:T(2,128)(2,1)S(1)}, bf16[2,704]{1,0:T(2,128)(2,1)S(1)}, u32[]{:S(2)}, u32[]{:S(2)}) %collective-permute-start.3) | collective-permute-done | bytes 2848 | tf_op jit(solution)/shard_map/ppermute | solution.py:322
  18.8 0.7 reshape.10.gain_ref
  19.5 1.0 collective-permute-start.6
  20.4 1.9 %collective-permute-start.8 = (bf16[192,896]{1,0:T(8,128)(2,1)S(1)}, bf16[192,896]{1,0:T(8,128)(2,1)S(1)}, u32[]{:S(2)}, u32[]{:S(2)}) collective-permute-start(bf16[192,896]{1,0:T(8,128)(2,1)S(1)} %collective-permute-done.refs_2_), channel_id=1, source_target_pairs={{0,2},{2,0},{4,6},{6,4},{8,10},{10,8},{12,14},{14,12},{1,3},{3,1},... | collective-permute-start | bytes 1032200 | tf_op jit(solution)/shard_map/ppermute | solution.py:89
  22.5 2.1 %collective-permute-start.10 = (bf16[192,896]{1,0:T(8,128)(2,1)S(1)}, bf16[192,896]{1,0:T(8,128)(2,1)S(1)}, u32[]{:S(2)}, u32[]{:S(2)}) collective-permute-start(bf16[192,896]{1,0:T(8,128)(2,1)S(1)} %collective-permute-done.refs_2_), channel_id=1, source_target_pairs={{0,4},{2,6},{4,12},{6,14},{12,8},{14,10},{8,0},{10,2},{20,16},{22,... | collective-permute-start | bytes 1032200 | tf_op jit(solution)/shard_map/ppermute | solution.py:86
  24.6 1.1 %copy-done.4 = bf16[512,704]{0,1:T(8,128)(2,1)S(1)} copy-done((bf16[512,704]{0,1:T(8,128)(2,1)S(1)}, bf16[512,704]{0,1:T(8,128)(2,1)}, u32[]{:S(2)}) %copy-start.4) | copy-done | bytes 720920
  25.7 2.8 %act.1 = (bf16[640,1408]{1,0:T(8,128)(2,1)S(1)}, f32[128,704]{1,0:T(8,128)S(1)}) custom-call(bf16[704,512]{1,0:T(8,128)(2,1)S(1)} %bitcast.17, bf16[704,512]{1,0:T(8,128)(2,1)S(1)} %collective-permute-done.4.other_ref, f32[1,1408]{1,0:T(1,128)S(1)} %reshape.10.gain_ref), custom_call_target="tpu_custom_call" | custom-call | flops 922746880 | bytes 2883584 | tf_op jit(solution)/shard_map/act/pallas_call | solution.py:334
  28.6 6.2 %conv.1.pooled_ref = bf16[128,704]{1,0:T(8,128)(2,1)S(1)} custom-call(bf16[640,1408]{1,0:T(8,128)(2,1)S(1)} %get-tuple-element.25.windows_ref, f32[128,704]{1,0:T(8,128)S(1)} %get-tuple-element.26.residual_ref, bf16[16,1408]{1,0:T(8,128)(2,1)S(1)} %maximum_select_fusion.halo_ref, f32[1,1408]{1,0:T(1,128)S(1)} %reshape.10.gain_ref, bf16[5,704,1408]{2,1,0:T(8,128)(2,1)} %bitcast.18), custom_call_target="tpu_custom_call" | custom-call | flops 1268776960 | bytes 9912320 | tf_op jit(solution)/shard_map/conv/pallas_call | solution.py:349
  35.3 1.6 %collective-permute-start.11 = (bf16[192,896]{1,0:T(8,128)(2,1)S(1)}, bf16[192,896]{1,0:T(8,128)(2,1)S(1)}, u32[]{:S(2)}, u32[]{:S(2)}) collective-permute-start(bf16[192,896]{1,0:T(8,128)(2,1)S(1)} %collective-permute-done.8.refs_3_), channel_id=1, source_target_pairs={{0,4},{2,6},{4,12},{6,14},{12,8},{14,10},{8,0},{10,2},{20,16},{22,... | collective-permute-start | bytes 1032200 | tf_op jit(solution)/shard_map/ppermute | solution.py:86
  36.9 6.5 %collective-permute-done.7 = bf16[192,640]{1,0:T(8,128)(2,1)S(1)} collective-permute-done((bf16[192,640]{1,0:T(8,128)(2,1)S(1)}, bf16[192,640]{1,0:T(8,128)(2,1)S(1)}, u32[]{:S(2)}, u32[]{:S(2)}) %collective-permute-start.7) | collective-permute-done | bytes 245792 | tf_op jit(solution)/shard_map/ppermute | solution.py:365
  44.0 1.0 %collective-permute-done.11.refs_7_ = bf16[192,896]{1,0:T(8,128)(2,1)S(1)} collective-permute-done((bf16[192,896]{1,0:T(8,128)(2,1)S(1)}, bf16[192,896]{1,0:T(8,128)(2,1)S(1)}, u32[]{:S(2)}, u32[]{:S(2)}) %collective-permute-start.11) | collective-permute-done | bytes 344096 | tf_op jit(solution)/shard_map/ppermute | solution.py:86
  45.1 1.8 %embed.1 = (bf16[8,128,192]{2,1,0:T(8,128)(2,1)}, bf16[8,192,192]{2,1,0:T(8,128)(2,1)S(1)}) custom-call(bf16[128,704]{1,0:T(8,128)(2,1)S(1)} %conv.1.pooled_ref, bf16[192,896]{1,0:T(8,128)(2,1)S(1)} %pad_maximum_fusion.1.refs_0_, bf16[192,896]{1,0:T(8,128)(2,1)S(1)} %collective-permute-done.1.refs_1_, bf16[192,896]{1,0:T(8,128)(2,1)S(1)} %collective-permute-done.refs_2_, ...), custom_call_target="tpu_custom_call" | custom-call | flops 276824064 | bytes 2162688 | tf_op jit(solution)/shard_map/embed/pallas_call | solution.py:378
  46.9 0.7 collective-permute-start.14
  47.7 1.3 %collective-permute-done.12.other_ref = bf16[8,128,192]{2,1,0:T(8,128)(2,1)S(1)} collective-permute-done((bf16[8,128,192]{2,1,0:T(8,128)(2,1)}, bf16[8,128,192]{2,1,0:T(8,128)(2,1)S(1)}, u32[]{:S(2)}, u32[]{:S(2)}) %collective-permute-start.12) | collective-permute-done | bytes 393248 | tf_op jit(solution)/shard_map/ppermute | solution.py:387
  49.0 0.8 copy-done.2
  49.8 1.0 %copy-done.3 = bf16[8,128,192]{2,1,0:T(8,128)(2,1)S(1)} copy-done((bf16[8,128,192]{2,1,0:T(8,128)(2,1)S(1)}, bf16[8,128,192]{2,1,0:T(8,128)(2,1)}, u32[]{:S(2)}) %copy-start.3) | copy-done | bytes 393240
  50.8 1.7 %keyvalue.1 = (bf16[192,128]{1,0:T(8,128)(2,1)S(1)}, bf16[8,128,192]{2,1,0:T(8,128)(2,1)S(1)}, bf16[8,128,192]{2,1,0:T(8,128)(2,1)S(1)}) custom-call(bf16[8,128,192]{2,1,0:T(8,128)(2,1)} %get-tuple-element.32.part_ref, bf16[8,128,192]{2,1,0:T(8,128)(2,1)S(1)} %copy-done.3, f32[8,1,192]{2,1,0:T(1,128)S(1)} %reshape.11.gain_ref, ...), custom_call_target="tpu_custom_call" | custom-call | flops 75497472 | bytes 589824 | tf_op jit(solution)/shard_map/keyvalue/pallas_call | solution.py:389
  52.5 0.9 collective-permute-start.17
  53.4 2.1 %collective-permute-start.18 = (bf16[192,128]{1,0:T(8,128)(2,1)S(1)}, bf16[192,128]{1,0:T(8,128)(2,1)S(1)}, u32[]{:S(2)}, u32[]{:S(2)}) collective-permute-start(bf16[192,128]{1,0:T(8,128)(2,1)S(1)} %get-tuple-element.37), channel_id=1, source_target_pairs={{0,8},{2,10},{4,0},{6,2},{12,4},{14,6},{8,12},{10,14},{1,9},{3,11}... | collective-permute-start | bytes 147464 | tf_op jit(solution)/shard_map/ppermute | solution.py:405
  55.5 2.2 %collective-permute-start.19 = (bf16[192,128]{1,0:T(8,128)(2,1)S(1)}, bf16[192,128]{1,0:T(8,128)(2,1)S(1)}, u32[]{:S(2)}, u32[]{:S(2)}) collective-permute-start(bf16[192,128]{1,0:T(8,128)(2,1)S(1)} %get-tuple-element.37), channel_id=1, source_target_pairs={{0,12},{2,14},{4,8},{6,10},{12,0},{14,2},{8,4},{10,6},{1,13},{3,15... | collective-permute-start | bytes 147464 | tf_op jit(solution)/shard_map/ppermute | solution.py:405
  57.7 1.3 %collective-permute-start.13 = (bf16[8,128,192]{2,1,0:T(8,128)(2,1)S(1)}, bf16[8,128,192]{2,1,0:T(8,128)(2,1)S(1)}, u32[]{:S(2)}, u32[]{:S(2)}) collective-permute-start(bf16[8,128,192]{2,1,0:T(8,128)(2,1)S(1)} %get-tuple-element.35.refs_0_), channel_id=1, source_target_pairs={{0,2},{2,0},{4,6},{6,4},{8,10},{10,8},{12,14},{14,12},{1,3},{3,1},... | collective-permute-start | bytes 1179656 | tf_op jit(solution)/shard_map/ppermute | solution.py:406
  59.0 6.1 %collective-permute-done.17 = bf16[192,128]{1,0:T(8,128)(2,1)S(1)} collective-permute-done((bf16[192,128]{1,0:T(8,128)(2,1)S(1)}, bf16[192,128]{1,0:T(8,128)(2,1)S(1)}, u32[]{:S(2)}, u32[]{:S(2)}) %collective-permute-start.17) | collective-permute-done | bytes 49184 | tf_op jit(solution)/shard_map/ppermute | solution.py:405
  65.1 1.0 collective-permute-start.20
  66.1 0.7 collective-permute-start.15
  66.8 1.5 %collective-permute-start.16 = (bf16[384,640]{1,0:T(8,128)(2,1)S(1)}, bf16[384,640]{1,0:T(8,128)(2,1)S(1)}, u32[]{:S(2)}, u32[]{:S(2)}) collective-permute-start(bf16[384,640]{1,0:T(8,128)(2,1)S(1)} %collective-permute-done.14.refs_3_.refs_1_), channel_id=1, source_target_pairs={{0,4},{2,6},{4,12},{6,14},{12,8},{14,10},{8,0},{10,2},{20,16},{22,... | collective-permute-start | bytes 1474568 | tf_op jit(solution)/shard_map/ppermute | solution.py:86
  68.4 6.7 %collective-permute-done.20 = bf16[4,192,128]{2,1,0:T(8,128)(2,1)S(1)} collective-permute-done((bf16[4,192,128]{2,1,0:T(8,128)(2,1)S(1)}, bf16[4,192,128]{2,1,0:T(8,128)(2,1)S(1)}, u32[]{:S(2)}, u32[]{:S(2)}) %collective-permute-start.20) | collective-permute-done | bytes 196640 | tf_op jit(solution)/shard_map/ppermute | solution.py:411
  75.1 3.3 %collective-permute-done.15.refs_4_.refs_2_ = bf16[384,640]{1,0:T(8,128)(2,1)S(1)} collective-permute-done((bf16[384,640]{1,0:T(8,128)(2,1)S(1)}, bf16[384,640]{1,0:T(8,128)(2,1)S(1)}, u32[]{:S(2)}, u32[]{:S(2)}) %collective-permute-start.15) | collective-permute-done | bytes 491552 | tf_op jit(solution)/shard_map/ppermute | solution.py:92
  78.5 2.3 %collective-permute-done.16.refs_5_.refs_3_ = bf16[384,640]{1,0:T(8,128)(2,1)S(1)} collective-permute-done((bf16[384,640]{1,0:T(8,128)(2,1)S(1)}, bf16[384,640]{1,0:T(8,128)(2,1)S(1)}, u32[]{:S(2)}, u32[]{:S(2)}) %collective-permute-start.16) | collective-permute-done | bytes 491552 | tf_op jit(solution)/shard_map/ppermute | solution.py:86
  81.2 1.4 %attend.1.attended_ref = bf16[2,256,192]{2,1,0:T(8,128)(2,1)S(1)} custom-call(bf16[256,256]{1,0:T(8,128)(2,1)S(1)} %query.1.query_ref, bf16[8,192,128]{2,1,0:T(8,128)(2,1)S(1)} %constant_dynamic-update-slice_fusion.own_ref, bf16[8,192,128]{2,1,0:T(8,128)(2,1)S(1)} %collective-permute-done.21.other_ref), custom_call_target="tpu_custom_call" | custom-call | flops 167772160 | bytes 786432 | tf_op jit(solution)/shard_map/attend/pallas_call | solution.py:426
  82.6 1.4 %output.1 = (bf16[128,1536]{1,0:T(8,128)(2,1)S(1)}, bf16[128,1536]{1,0:T(8,128)(2,1)S(1)}, bf16[16,256]{1,0:T(8,128)(2,1)S(1)}) custom-call(bf16[2,256,192]{2,1,0:T(8,128)(2,1)S(1)} %attend.1.attended_ref, bf16[8,128,192]{2,1,0:T(8,128)(2,1)S(1)} %get-tuple-element.34.embedded_ref, bf16[1536,256]{1,0:T(8,128)(2,1)S(1)} %copy-done.1, ...), custom_call_target="tpu_custom_call" | custom-call | flops 301989888 | bytes 1179648 | tf_op jit(solution)/shard_map/output/pallas_call | solution.py:440
  84.1 0.8 collective-permute-start.24
  84.9 2.9 %collective-permute-done.24 = bf16[16,256]{1,0:T(8,128)(2,1)S(1)} collective-permute-done((bf16[16,256]{1,0:T(8,128)(2,1)S(1)}, bf16[16,256]{1,0:T(8,128)(2,1)S(1)}, u32[]{:S(2)}, u32[]{:S(2)}) %collective-permute-start.24) | collective-permute-done | bytes 8224 | tf_op jit(solution)/shard_map/ppermute | solution.py:455
  88.0 0.8 collective-permute-start.23
  89.0 0.7 collective-permute-start.26
  89.7 2.9 %collective-permute-done.26 = bf16[16,256]{1,0:T(8,128)(2,1)S(1)} collective-permute-done((bf16[16,256]{1,0:T(8,128)(2,1)S(1)}, bf16[16,256]{1,0:T(8,128)(2,1)S(1)}, u32[]{:S(2)}, u32[]{:S(2)}) %collective-permute-start.26) | collective-permute-done | bytes 8224 | tf_op jit(solution)/shard_map/ppermute | solution.py:464
  92.7 2.7 %collective-permute-done.23.refs_1_ = bf16[64,1536]{1,0:T(8,128)(2,1)S(1)} collective-permute-done((bf16[64,1536]{1,0:T(8,128)(2,1)S(1)}, bf16[64,1536]{1,0:T(8,128)(2,1)S(1)}, u32[]{:S(2)}, u32[]{:S(2)}) %collective-permute-start.23) | collective-permute-done | bytes 196640 | tf_op jit(solution)/shard_map/ppermute | solution.py:462
  95.4 3.6 %collective-permute-start.27 = (bf16[32,256]{1,0:T(8,128)(2,1)S(1)}, bf16[32,256]{1,0:T(8,128)(2,1)S(1)}, u32[]{:S(2)}, u32[]{:S(2)}) collective-permute-start(bf16[32,256]{1,0:T(8,128)(2,1)S(1)} %pad_maximum_fusion.4), channel_id=1, source_target_pairs={{0,8},{2,10},{4,12},{6,14},{9,1},{11,3},{13,5},{15,7},{16,24},{18,... | collective-permute-start | bytes 49160 | tf_op jit(solution)/shard_map/ppermute | solution.py:467
  99.1 0.8 tokens.1
  100.5 0.8 pair.1
  (58 shorter events, 4.0 us)
Async XLA Ops:
  0.6 0.9 copy-start
  2.7 15.4 %collective-permute-start = (bf16[192,896]{1,0:T(8,128)(2,1)S(1)}, bf16[192,896]{1,0:T(8,128)(2,1)S(1)}, u32[]{:S(2)}, u32[]{:S(2)}) collective-permute-start(bf16[192,896]{1,0:T(8,128)(2,1)S(1)} %pad_maximum_fusion.1.refs_0_), channel_id=1, source_target_pairs={{0,4},{2,6},{4,12},{6,14},{12,8},{14,10},{8,0},{10,2},{20,16},{22,... | collective-permute-start | bytes 1032200 | tf_op jit(solution)/shard_map/ppermute | solution.py:86
  5.8 12.4 %collective-permute-start.1 = (bf16[192,896]{1,0:T(8,128)(2,1)S(1)}, bf16[192,896]{1,0:T(8,128)(2,1)S(1)}, u32[]{:S(2)}, u32[]{:S(2)}) collective-permute-start(bf16[192,896]{1,0:T(8,128)(2,1)S(1)} %pad_maximum_fusion.1.refs_0_), channel_id=1, source_target_pairs={{0,2},{2,0},{4,6},{6,4},{8,10},{10,8},{12,14},{14,12},{1,3},{3,1},... | collective-permute-start | bytes 1032200 | tf_op jit(solution)/shard_map/ppermute | solution.py:89
  8.6 5.9 %collective-permute-start.2 = (bf16[2,704]{1,0:T(2,128)(2,1)S(1)}, bf16[2,704]{1,0:T(2,128)(2,1)S(1)}, u32[]{:S(2)}, u32[]{:S(2)}) collective-permute-start(bf16[2,704]{1,0:T(2,128)(2,1)S(1)} %copy.14), channel_id=1, source_target_pairs={{0,2},{2,4},{4,6},{6,8},{8,10},{10,12},{12,14},{1,3},{3,5},{5,7},{... | collective-permute-start | bytes 8456 | tf_op jit(solution)/shard_map/ppermute | solution.py:321
  11.1 7.0 %collective-permute-start.3 = (bf16[2,704]{1,0:T(2,128)(2,1)S(1)}, bf16[2,704]{1,0:T(2,128)(2,1)S(1)}, u32[]{:S(2)}, u32[]{:S(2)}) collective-permute-start(bf16[2,704]{1,0:T(2,128)(2,1)S(1)} %copy.15), channel_id=1, source_target_pairs={{2,0},{4,2},{6,4},{8,6},{10,8},{12,10},{14,12},{3,1},{5,3},{7,5},{... | collective-permute-start | bytes 8456 | tf_op jit(solution)/shard_map/ppermute | solution.py:322
  18.2 6.4 %collective-permute-start.4 = (bf16[704,512]{1,0:T(8,128)(2,1)}, bf16[704,512]{1,0:T(8,128)(2,1)S(1)}, u32[]{:S(2)}, u32[]{:S(2)}) collective-permute-start(bf16[704,512]{1,0:T(8,128)(2,1)} %bitcast.16), channel_id=1, source_target_pairs={{0,1},{1,0},{2,3},{3,2},{4,5},{5,4},{6,7},{7,6},{8,9},{9,8},{10,11... | collective-permute-start | bytes 2162696 | tf_op jit(solution)/shard_map/ppermute | solution.py:327
  18.2 29.4 %copy-start.6 = (f32[1536]{0:T(1024)S(1)}, f32[1536]{0:T(1024)}, u32[]{:S(2)}) copy-start(f32[1536]{0:T(1024)} %param.14) | copy-start | bytes 18436
  18.2 4.2 %collective-permute-start.5 = (bf16[16,704]{1,0:T(8,128)(2,1)S(1)}, bf16[16,704]{1,0:T(8,128)(2,1)S(1)}, u32[]{:S(2)}, u32[]{:S(2)}) collective-permute-start(bf16[16,704]{1,0:T(8,128)(2,1)S(1)} %fusion.2), channel_id=1, source_target_pairs={{0,1},{1,0},{2,3},{3,2},{4,5},{5,4},{6,7},{7,6},{8,9},{9,8},{10,11... | collective-permute-start | bytes 67592 | tf_op jit(solution)/shard_map/ppermute | solution.py:329
  19.5 15.3 %collective-permute-start.6 = (bf16[192,896]{1,0:T(8,128)(2,1)S(1)}, bf16[192,896]{1,0:T(8,128)(2,1)S(1)}, u32[]{:S(2)}, u32[]{:S(2)}) collective-permute-start(bf16[192,896]{1,0:T(8,128)(2,1)S(1)} %collective-permute-done.refs_2_), channel_id=1, source_target_pairs={{0,16},{16,0},{1,17},{17,1},{2,18},{18,2},{3,19},{19,3},{4,20},{20... | collective-permute-start | bytes 1032200 | tf_op jit(solution)/shard_map/ppermute | solution.py:92
  20.4 14.4 %collective-permute-start.8 = (bf16[192,896]{1,0:T(8,128)(2,1)S(1)}, bf16[192,896]{1,0:T(8,128)(2,1)S(1)}, u32[]{:S(2)}, u32[]{:S(2)}) collective-permute-start(bf16[192,896]{1,0:T(8,128)(2,1)S(1)} %collective-permute-done.refs_2_), channel_id=1, source_target_pairs={{0,2},{2,0},{4,6},{6,4},{8,10},{10,8},{12,14},{14,12},{1,3},{3,1},... | collective-permute-start | bytes 1032200 | tf_op jit(solution)/shard_map/ppermute | solution.py:89
  22.5 14.4 %collective-permute-start.10 = (bf16[192,896]{1,0:T(8,128)(2,1)S(1)}, bf16[192,896]{1,0:T(8,128)(2,1)S(1)}, u32[]{:S(2)}, u32[]{:S(2)}) collective-permute-start(bf16[192,896]{1,0:T(8,128)(2,1)S(1)} %collective-permute-done.refs_2_), channel_id=1, source_target_pairs={{0,4},{2,6},{4,12},{6,14},{12,8},{14,10},{8,0},{10,2},{20,16},{22,... | collective-permute-start | bytes 1032200 | tf_op jit(solution)/shard_map/ppermute | solution.py:86
  24.6 1.1 %copy-start.4 = (bf16[512,704]{0,1:T(8,128)(2,1)S(1)}, bf16[512,704]{0,1:T(8,128)(2,1)}, u32[]{:S(2)}) copy-start(bf16[512,704]{0,1:T(8,128)(2,1)} %param.10) | copy-start | bytes 2162692
  28.5 54.1 %copy-start.1 = (bf16[1536,256]{1,0:T(8,128)(2,1)S(1)}, bf16[1536,256]{1,0:T(8,128)(2,1)}, u32[]{:S(2)}) copy-start(bf16[1536,256]{1,0:T(8,128)(2,1)} %pair_weight_ref.1) | copy-start | bytes 2359300
  34.8 65.7 %copy-start.5 = (bf16[128,128]{1,0:T(8,128)(2,1)S(1)}, bf16[128,128]{1,0:T(8,128)(2,1)}, u32[]{:S(2)}) copy-start(bf16[128,128]{1,0:T(8,128)(2,1)} %weight_ref.1) | copy-start | bytes 98308
  34.8 9.2 %collective-permute-start.9 = (bf16[192,896]{1,0:T(8,128)(2,1)S(1)}, bf16[192,896]{1,0:T(8,128)(2,1)S(1)}, u32[]{:S(2)}, u32[]{:S(2)}) collective-permute-start(bf16[192,896]{1,0:T(8,128)(2,1)S(1)} %collective-permute-done.8.refs_3_), channel_id=1, source_target_pairs={{0,16},{16,0},{1,17},{17,1},{2,18},{18,2},{3,19},{19,3},{4,20},{20... | collective-permute-start | bytes 1032200 | tf_op jit(solution)/shard_map/ppermute | solution.py:92
  35.3 9.8 %collective-permute-start.11 = (bf16[192,896]{1,0:T(8,128)(2,1)S(1)}, bf16[192,896]{1,0:T(8,128)(2,1)S(1)}, u32[]{:S(2)}, u32[]{:S(2)}) collective-permute-start(bf16[192,896]{1,0:T(8,128)(2,1)S(1)} %collective-permute-done.8.refs_3_), channel_id=1, source_target_pairs={{0,4},{2,6},{4,12},{6,14},{12,8},{14,10},{8,0},{10,2},{20,16},{22,... | collective-permute-start | bytes 1032200 | tf_op jit(solution)/shard_map/ppermute | solution.py:86
  36.9 6.5 %collective-permute-start.7 = (bf16[192,640]{1,0:T(8,128)(2,1)S(1)}, bf16[192,640]{1,0:T(8,128)(2,1)S(1)}, u32[]{:S(2)}, u32[]{:S(2)}) collective-permute-start(bf16[192,640]{1,0:T(8,128)(2,1)S(1)} %pad_maximum_fusion.2), channel_id=1, source_target_pairs={{0,2},{2,0},{4,6},{6,4},{8,10},{10,8},{12,14},{14,12},{1,3},{3,1},... | collective-permute-start | bytes 737288 | tf_op jit(solution)/shard_map/ppermute | solution.py:365
  46.8 2.1 %collective-permute-start.12 = (bf16[8,128,192]{2,1,0:T(8,128)(2,1)}, bf16[8,128,192]{2,1,0:T(8,128)(2,1)S(1)}, u32[]{:S(2)}, u32[]{:S(2)}) collective-permute-start(bf16[8,128,192]{2,1,0:T(8,128)(2,1)} %get-tuple-element.32.part_ref), channel_id=1, source_target_pairs={{0,1},{1,0},{2,3},{3,2},{4,5},{5,4},{6,7},{7,6},{8,9},{9,8},{10,11... | collective-permute-start | bytes 1179656 | tf_op jit(solution)/shard_map/ppermute | solution.py:387
  46.9 18.2 %collective-permute-start.14 = (bf16[384,640]{1,0:T(8,128)(2,1)S(1)}, bf16[384,640]{1,0:T(8,128)(2,1)S(1)}, u32[]{:S(2)}, u32[]{:S(2)}) collective-permute-start(bf16[384,640]{1,0:T(8,128)(2,1)S(1)} %pad_maximum_fusion.refs_2_.refs_0_), channel_id=1, source_target_pairs={{0,4},{2,6},{4,12},{6,14},{12,8},{14,10},{8,0},{10,2},{20,16},{22,... | collective-permute-start | bytes 1474568 | tf_op jit(solution)/shard_map/ppermute | solution.py:86
  48.9 0.8 copy-start.2
  49.8 1.0 %copy-start.3 = (bf16[8,128,192]{2,1,0:T(8,128)(2,1)S(1)}, bf16[8,128,192]{2,1,0:T(8,128)(2,1)}, u32[]{:S(2)}) copy-start(bf16[8,128,192]{2,1,0:T(8,128)(2,1)} %copy-done.2) | copy-start | bytes 1179652
  52.5 12.6 %collective-permute-start.17 = (bf16[192,128]{1,0:T(8,128)(2,1)S(1)}, bf16[192,128]{1,0:T(8,128)(2,1)S(1)}, u32[]{:S(2)}, u32[]{:S(2)}) collective-permute-start(bf16[192,128]{1,0:T(8,128)(2,1)S(1)} %get-tuple-element.37), channel_id=1, source_target_pairs={{0,4},{2,6},{4,12},{6,14},{12,8},{14,10},{8,0},{10,2},{1,5},{3,7},... | collective-permute-start | bytes 147464 | tf_op jit(solution)/shard_map/ppermute | solution.py:405
  53.4 11.7 %collective-permute-start.18 = (bf16[192,128]{1,0:T(8,128)(2,1)S(1)}, bf16[192,128]{1,0:T(8,128)(2,1)S(1)}, u32[]{:S(2)}, u32[]{:S(2)}) collective-permute-start(bf16[192,128]{1,0:T(8,128)(2,1)S(1)} %get-tuple-element.37), channel_id=1, source_target_pairs={{0,8},{2,10},{4,0},{6,2},{12,4},{14,6},{8,12},{10,14},{1,9},{3,11}... | collective-permute-start | bytes 147464 | tf_op jit(solution)/shard_map/ppermute | solution.py:405
  55.5 9.6 %collective-permute-start.19 = (bf16[192,128]{1,0:T(8,128)(2,1)S(1)}, bf16[192,128]{1,0:T(8,128)(2,1)S(1)}, u32[]{:S(2)}, u32[]{:S(2)}) collective-permute-start(bf16[192,128]{1,0:T(8,128)(2,1)S(1)} %get-tuple-element.37), channel_id=1, source_target_pairs={{0,12},{2,14},{4,8},{6,10},{12,0},{14,2},{8,4},{10,6},{1,13},{3,15... | collective-permute-start | bytes 147464 | tf_op jit(solution)/shard_map/ppermute | solution.py:405
  57.7 17.5 %collective-permute-start.13 = (bf16[8,128,192]{2,1,0:T(8,128)(2,1)S(1)}, bf16[8,128,192]{2,1,0:T(8,128)(2,1)S(1)}, u32[]{:S(2)}, u32[]{:S(2)}) collective-permute-start(bf16[8,128,192]{2,1,0:T(8,128)(2,1)S(1)} %get-tuple-element.35.refs_0_), channel_id=1, source_target_pairs={{0,2},{2,0},{4,6},{6,4},{8,10},{10,8},{12,14},{14,12},{1,3},{3,1},... | collective-permute-start | bytes 1179656 | tf_op jit(solution)/shard_map/ppermute | solution.py:406
  65.1 9.9 %collective-permute-start.20 = (bf16[4,192,128]{2,1,0:T(8,128)(2,1)S(1)}, bf16[4,192,128]{2,1,0:T(8,128)(2,1)S(1)}, u32[]{:S(2)}, u32[]{:S(2)}) collective-permute-start(bf16[4,192,128]{2,1,0:T(8,128)(2,1)S(1)} %pad_maximum_fusion.3), channel_id=1, source_target_pairs={{0,2},{2,0},{4,6},{6,4},{8,10},{10,8},{12,14},{14,12},{1,3},{3,1},... | collective-permute-start | bytes 589832 | tf_op jit(solution)/shard_map/ppermute | solution.py:411
  66.1 12.3 %collective-permute-start.15 = (bf16[384,640]{1,0:T(8,128)(2,1)S(1)}, bf16[384,640]{1,0:T(8,128)(2,1)S(1)}, u32[]{:S(2)}, u32[]{:S(2)}) collective-permute-start(bf16[384,640]{1,0:T(8,128)(2,1)S(1)} %collective-permute-done.14.refs_3_.refs_1_), channel_id=1, source_target_pairs={{0,16},{16,0},{1,17},{17,1},{2,18},{18,2},{3,19},{19,3},{4,20},{20... | collective-permute-start | bytes 1474568 | tf_op jit(solution)/shard_map/ppermute | solution.py:92
  66.8 13.9 %collective-permute-start.16 = (bf16[384,640]{1,0:T(8,128)(2,1)S(1)}, bf16[384,640]{1,0:T(8,128)(2,1)S(1)}, u32[]{:S(2)}, u32[]{:S(2)}) collective-permute-start(bf16[384,640]{1,0:T(8,128)(2,1)S(1)} %collective-permute-done.14.refs_3_.refs_1_), channel_id=1, source_target_pairs={{0,4},{2,6},{4,12},{6,14},{12,8},{14,10},{8,0},{10,2},{20,16},{22,... | collective-permute-start | bytes 1474568 | tf_op jit(solution)/shard_map/ppermute | solution.py:86
  75.1 6.1 %collective-permute-start.21 = (bf16[8,192,128]{2,1,0:T(8,128)(2,1)S(1)}, bf16[8,192,128]{2,1,0:T(8,128)(2,1)S(1)}, u32[]{:S(2)}, u32[]{:S(2)}) collective-permute-start(bf16[8,192,128]{2,1,0:T(8,128)(2,1)S(1)} %constant_dynamic-update-slice_fusion.own_ref), channel_id=1, source_target_pairs={{0,1},{1,0},{2,3},{3,2},{4,5},{5,4},{6,7},{7,6},{8,9},{9,8},{10,11... | collective-permute-start | bytes 1179656 | tf_op jit(solution)/shard_map/ppermute | solution.py:414
  84.1 3.7 %collective-permute-start.24 = (bf16[16,256]{1,0:T(8,128)(2,1)S(1)}, bf16[16,256]{1,0:T(8,128)(2,1)S(1)}, u32[]{:S(2)}, u32[]{:S(2)}) collective-permute-start(bf16[16,256]{1,0:T(8,128)(2,1)S(1)} %get-tuple-element.43), channel_id=1, source_target_pairs={{0,2},{2,0},{4,6},{6,4},{8,10},{10,8},{12,14},{14,12},{1,3},{3,1},... | collective-permute-start | bytes 24584 | tf_op jit(solution)/shard_map/ppermute | solution.py:455
  84.8 3.0 %collective-permute-start.22 = (bf16[128,1536]{1,0:T(8,128)(2,1)S(1)}, bf16[128,1536]{1,0:T(8,128)(2,1)S(1)}, u32[]{:S(2)}, u32[]{:S(2)}) collective-permute-start(bf16[128,1536]{1,0:T(8,128)(2,1)S(1)} %get-tuple-element.42), channel_id=1, source_target_pairs={{0,1},{1,0},{2,3},{3,2},{4,5},{5,4},{6,7},{7,6},{8,9},{9,8},{10,11... | collective-permute-start | bytes 1179656 | tf_op jit(solution)/shard_map/ppermute | solution.py:458
  87.8 1.2 %collective-permute-start.25 = (bf16[16,256]{1,0:T(8,128)(2,1)S(1)}, bf16[16,256]{1,0:T(8,128)(2,1)S(1)}, u32[]{:S(2)}, u32[]{:S(2)}) collective-permute-start(bf16[16,256]{1,0:T(8,128)(2,1)S(1)} %add_convert_fusion.2), channel_id=1, source_target_pairs={{0,1},{1,0},{2,3},{3,2},{4,5},{5,4},{6,7},{7,6},{8,9},{9,8},{10,11... | collective-permute-start | bytes 24584 | tf_op jit(solution)/shard_map/ppermute | solution.py:457
  88.0 7.4 %collective-permute-start.23 = (bf16[64,1536]{1,0:T(8,128)(2,1)S(1)}, bf16[64,1536]{1,0:T(8,128)(2,1)S(1)}, u32[]{:S(2)}, u32[]{:S(2)}) collective-permute-start(bf16[64,1536]{1,0:T(8,128)(2,1)S(1)} %get-tuple-element.50), channel_id=1, source_target_pairs={{0,2},{2,0},{4,6},{6,4},{8,10},{10,8},{12,14},{14,12},{1,3},{3,1},... | collective-permute-start | bytes 589832 | tf_op jit(solution)/shard_map/ppermute | solution.py:462
  89.0 3.7 %collective-permute-start.26 = (bf16[16,256]{1,0:T(8,128)(2,1)S(1)}, bf16[16,256]{1,0:T(8,128)(2,1)S(1)}, u32[]{:S(2)}, u32[]{:S(2)}) collective-permute-start(bf16[16,256]{1,0:T(8,128)(2,1)S(1)} %add_convert_fusion.1), channel_id=1, source_target_pairs={{0,4},{2,6},{4,0},{6,2},{8,12},{10,14},{12,8},{14,10},{1,5},{3,7},... | collective-permute-start | bytes 24584 | tf_op jit(solution)/shard_map/ppermute | solution.py:464
  95.4 5.1 %collective-permute-start.27 = (bf16[32,256]{1,0:T(8,128)(2,1)S(1)}, bf16[32,256]{1,0:T(8,128)(2,1)S(1)}, u32[]{:S(2)}, u32[]{:S(2)}) collective-permute-start(bf16[32,256]{1,0:T(8,128)(2,1)S(1)} %pad_maximum_fusion.4), channel_id=1, source_target_pairs={{0,8},{2,10},{4,12},{6,14},{9,1},{11,3},{13,5},{15,7},{16,24},{18,... | collective-permute-start | bytes 49160 | tf_op jit(solution)/shard_map/ppermute | solution.py:467

commit v15 on v13

--- a/solution.py
+++ b/solution.py
@@ -173,7 +173,7 @@
         rest_ref[owner] = ref[:, half:]
 
 
-def keyvalue_kernel(part_ref, other_ref, gain_ref, weight_ref, kv_ref, normed_ref, embedded_ref):
+def keyvalue_kernel(part_ref, other_ref, gain_ref, weight_ref, kv_ref, normed_ref, embedded_ref, *send_ref):
     count, _, width = part_ref.shape
     e = (part_ref[...].astype(F32) + other_ref[...].astype(F32)).astype(BF16)
     embedded_ref[...] = e
@@ -186,6 +186,8 @@
         total = total + dot_nn(normed_ref[s], weight_ref[s])
     kv = total.T.astype(BF16)
     kv_ref[...] = kv
+    for ref in send_ref:
+        ref[...] = jnp.concatenate([normed_ref[s] for s in range(count)], axis=1)
 
 
 def later_blocks_of(refs):
@@ -198,9 +200,13 @@
 
 
 def query_kernel(sides, *refs):
-    normed, pieces, query_ref = refs[:sides], refs[sides:-1], refs[-1]
+    normed, pieces, query_ref = list(refs[:sides]), refs[sides:-sides], refs[-sides]
     features = query_ref.shape[1]
-    tokens = normed[0].shape[1]
+    count, tokens, width = normed[0].shape
+    if sides > 1:
+        for s in range(count):
+            refs[-1][s] = normed[1][:, s * width:(s + 1) * width]
+        normed[1] = refs[-1]
     totals = [0.0] * sides
     for ref, rows, place in later_blocks_of(pieces):
         weight = ref[rows, :features]
@@ -386,15 +392,15 @@
     )(pooled, *embed_blocks)
     other_part = lax.ppermute(part, "col", swap)
 
-    keyvalue, normed, embedded = pl.pallas_call(
+    keyvalue, normed, embedded, *sending = pl.pallas_call(
         keyvalue_kernel,
         out_shape=(
             shape((DV, tokens), BF16),
             shape((pieces, tokens, block), BF16),
             shape((pieces, tokens, block), BF16),
-        ),
+        ) + (shape((tokens, width), BF16),) * (sides - 1),
         in_specs=vspec(4),
-        out_specs=vspec(3),
+        out_specs=vspec(2 + sides),
         compiler_params=params(16),
         cost_estimate=cost(2 * tokens * width * DV, 2 * width * DV),
         name="keyvalue",
@@ -403,7 +409,7 @@
     if ring:
         turns = [[(2 * RING[k] + i, 2 * RING[(k + t) % 4] + i) for k in range(4) for i in range(2)] for t in (1, 3, 2)]
         turned = [lax.ppermute(keyvalue, "seq", turn) for turn in turns]
-        both_normed.append(lax.ppermute(normed, "seq", pair_swap))
+        both_normed.append(lax.ppermute(sending[0], "seq", pair_swap))
         q.at["step"] = after(q.at["step"], both_normed[1])
         q.along("step", "far")
         q.between("step", "cross")
@@ -419,6 +425,7 @@
         out_shape=shape((sides * tokens, features), BF16),
         in_specs=vspec(sides + len(later_blocks)),
         out_specs=pl.BlockSpec(memory_space=VMEM),
+        scratch_shapes=[pltpu.VMEM((pieces, tokens, block), BF16)] * (sides - 1),
         compiler_params=params(12),
         cost_estimate=cost(2 * sides * tokens * width * features, 2 * width * features),
         name="query",

time: 101 us -> 98.6 us (0.976)
  waiting for transfers between devices: 40.8 us -> 38 us
    ppermute x1, waiting for transfers between devices: 4.57 us -> 1.81 us  [on_device(): both_normed.append(lax.ppermute(sending[0], 'seq', pair_swap))]
where the time goes in v15:
time: 98.6 us; the launch traced here: 97.6 us
  waiting for transfers between devices  38 us (39%)
  starting transfers between devices  31.5 us (32%)
  Pallas kernels  17.6 us (18%)
  local copies, waits for them, and re-layouts  8.2 us (8%)
  other arithmetic  1.41 us (1%)
    ppermute x5, starting transfers between devices, along(): self.at[target] = lax.ppermute(self.at[source], ('grp', 'seq'), pairs)  8.47 us
    ppermute x1, waiting for transfers between devices, on_device(): received = lax.ppermute(theirs, 'seq', pair_swap)  6.5 us
    pallas_call x1, Pallas kernels, on_device(): pl.pallas_call(functools.partial(conv_kernel, positions), out_shape=shape...  6.2 us
    ppermute x5, waiting for transfers between devices, along(): self.at[target] = lax.ppermute(self.at[source], ('grp', 'seq'), pairs)  5.57 us
    ppermute x3, starting transfers between devices, on_device(): turned = [lax.ppermute(keyvalue, 'seq', turn) for turn in turns]  5.52 us
    ppermute x3, waiting for transfers between devices, between(): self.at[target] = lax.ppermute(self.at[source], 'grp', [(0, 1), (1, 0)])  5.25 us
    ppermute x1, waiting for transfers between devices, on_device(): gathered = jnp.concatenate([row, lax.ppermute(row, 'seq', pair_swap)])  5.03 us
    unnamed x20, local copies, waits for them, and re-layouts  4.15 us
  transfers between devices with their start and end apart: 28, of which 14 were waited for; matrix products, arithmetic and copies ran while one was open for 5% of the time, Pallas kernels for 12%

profile of v15, /device:TPU:0, one launch (start us, length us, event | category | flops | bytes accessed | tf_op | source)
XLA Modules:
  0.0 97.6 jit_solution(1108067983829660686)
XLA Ops:
  0.7 0.9 copy-done
  1.6 1.1 %pad_maximum_fusion.1.refs_0_ = bf16[192,896]{1,0:T(8,128)(2,1)S(1)} fusion(bf16[192,192]{1,0:T(8,128)(2,1)S(1)} %constant_dynamic-slice_fusion.2, bf16[192,704]{1,0:T(8,128)(2,1)} %bitcast.19), kind=kLoop, calls=%fused_computation.2 | loop fusion | flops 688128 | bytes 688128 | tf_op jit(solution)/shard_map/concatenate | solution.py:301
  2.7 3.1 %collective-permute-start = (bf16[192,896]{1,0:T(8,128)(2,1)S(1)}, bf16[192,896]{1,0:T(8,128)(2,1)S(1)}, u32[]{:S(2)}, u32[]{:S(2)}) collective-permute-start(bf16[192,896]{1,0:T(8,128)(2,1)S(1)} %pad_maximum_fusion.1.refs_0_), channel_id=1, source_target_pairs={{0,4},{2,6},{4,12},{6,14},{12,8},{14,10},{8,0},{10,2},{20,16},{22,... | collective-permute-start | bytes 1032200 | tf_op jit(solution)/shard_map/ppermute | solution.py:86
  5.8 1.5 %collective-permute-start.1 = (bf16[192,896]{1,0:T(8,128)(2,1)S(1)}, bf16[192,896]{1,0:T(8,128)(2,1)S(1)}, u32[]{:S(2)}, u32[]{:S(2)}) collective-permute-start(bf16[192,896]{1,0:T(8,128)(2,1)S(1)} %pad_maximum_fusion.1.refs_0_), channel_id=1, source_target_pairs={{0,2},{2,0},{4,6},{6,4},{8,10},{10,8},{12,14},{14,12},{1,3},{3,1},... | collective-permute-start | bytes 1032200 | tf_op jit(solution)/shard_map/ppermute | solution.py:89
  7.3 1.1 %fusion.3 = (bf16[2,704]{0,1:T(8,128)(2,1)S(1)}, bf16[2,704]{0,1:T(8,128)(2,1)S(1)}) fusion(bf16[512,704]{0,1:T(8,128)(2,1)} %param.10), kind=kLoop, calls=%fused_computation.24 | loop fusion | bytes 11264 | tf_op jit(solution)/shard_map/slice | solution.py:328
  8.6 2.4 %collective-permute-start.2 = (bf16[2,704]{1,0:T(2,128)(2,1)S(1)}, bf16[2,704]{1,0:T(2,128)(2,1)S(1)}, u32[]{:S(2)}, u32[]{:S(2)}) collective-permute-start(bf16[2,704]{1,0:T(2,128)(2,1)S(1)} %copy.14), channel_id=1, source_target_pairs={{0,2},{2,4},{4,6},{6,8},{8,10},{10,12},{12,14},{1,3},{3,5},{5,7},{... | collective-permute-start | bytes 8456 | tf_op jit(solution)/shard_map/ppermute | solution.py:327
  11.1 1.3 %collective-permute-start.3 = (bf16[2,704]{1,0:T(2,128)(2,1)S(1)}, bf16[2,704]{1,0:T(2,128)(2,1)S(1)}, u32[]{:S(2)}, u32[]{:S(2)}) collective-permute-start(bf16[2,704]{1,0:T(2,128)(2,1)S(1)} %copy.15), channel_id=1, source_target_pairs={{2,0},{4,2},{6,4},{8,6},{10,8},{12,10},{14,12},{3,1},{5,3},{7,5},{... | collective-permute-start | bytes 8456 | tf_op jit(solution)/shard_map/ppermute | solution.py:328
  12.5 1.0 constant_dynamic-slice_fusion.1
  13.4 1.0 %dynamic-slice_bitcast_fusion.1 = (bf16[192,384]{1,0:T(8,128)(2,1)S(1)}, bf16[192,384]{1,0:T(8,128)(2,1)S(1)}) fusion(bf16[1536,192]{0,1:T(8,128)(2,1)} %param.17, s32[]{:T(128)S(6)} %select_n.45, s32[]{:T(128)S(6)} %select_n.47), kind=kLoop, calls=%fused_computation.6 | loop fusion | bytes 589832 | tf_op jit(solution)/shard_map/dynamic_slice | solution.py:315
  14.5 3.7 %collective-permute-done.3 = bf16[2,704]{1,0:T(2,128)(2,1)S(1)} collective-permute-done((bf16[2,704]{1,0:T(2,128)(2,1)S(1)}, bf16[2,704]{1,0:T(2,128)(2,1)S(1)}, u32[]{:S(2)}, u32[]{:S(2)}) %collective-permute-start.3) | collective-permute-done | bytes 2848 | tf_op jit(solution)/shard_map/ppermute | solution.py:328
  18.8 0.7 reshape.10.gain_ref
  19.5 1.0 collective-permute-start.6
  20.4 1.9 %collective-permute-start.8 = (bf16[192,896]{1,0:T(8,128)(2,1)S(1)}, bf16[192,896]{1,0:T(8,128)(2,1)S(1)}, u32[]{:S(2)}, u32[]{:S(2)}) collective-permute-start(bf16[192,896]{1,0:T(8,128)(2,1)S(1)} %collective-permute-done.refs_2_), channel_id=1, source_target_pairs={{0,2},{2,0},{4,6},{6,4},{8,10},{10,8},{12,14},{14,12},{1,3},{3,1},... | collective-permute-start | bytes 1032200 | tf_op jit(solution)/shard_map/ppermute | solution.py:89
  22.5 2.1 %collective-permute-start.10 = (bf16[192,896]{1,0:T(8,128)(2,1)S(1)}, bf16[192,896]{1,0:T(8,128)(2,1)S(1)}, u32[]{:S(2)}, u32[]{:S(2)}) collective-permute-start(bf16[192,896]{1,0:T(8,128)(2,1)S(1)} %collective-permute-done.refs_2_), channel_id=1, source_target_pairs={{0,4},{2,6},{4,12},{6,14},{12,8},{14,10},{8,0},{10,2},{20,16},{22,... | collective-permute-start | bytes 1032200 | tf_op jit(solution)/shard_map/ppermute | solution.py:86
  24.6 1.1 %copy-done.4 = bf16[512,704]{0,1:T(8,128)(2,1)S(1)} copy-done((bf16[512,704]{0,1:T(8,128)(2,1)S(1)}, bf16[512,704]{0,1:T(8,128)(2,1)}, u32[]{:S(2)}) %copy-start.4) | copy-done | bytes 720920
  25.7 2.8 %act.1 = (bf16[640,1408]{1,0:T(8,128)(2,1)S(1)}, f32[128,704]{1,0:T(8,128)S(1)}) custom-call(bf16[704,512]{1,0:T(8,128)(2,1)S(1)} %bitcast.17, bf16[704,512]{1,0:T(8,128)(2,1)S(1)} %collective-permute-done.4.other_ref, f32[1,1408]{1,0:T(1,128)S(1)} %reshape.10.gain_ref), custom_call_target="tpu_custom_call" | custom-call | flops 922746880 | bytes 2883584 | tf_op jit(solution)/shard_map/act/pallas_call | solution.py:340
  28.6 6.2 %conv.1.pooled_ref = bf16[128,704]{1,0:T(8,128)(2,1)S(1)} custom-call(bf16[640,1408]{1,0:T(8,128)(2,1)S(1)} %get-tuple-element.27.windows_ref, f32[128,704]{1,0:T(8,128)S(1)} %get-tuple-element.28.residual_ref, bf16[16,1408]{1,0:T(8,128)(2,1)S(1)} %maximum_select_fusion.halo_ref, f32[1,1408]{1,0:T(1,128)S(1)} %reshape.10.gain_ref, bf16[5,704,1408]{2,1,0:T(8,128)(2,1)} %bitcast.18), custom_call_target="tpu_custom_call" | custom-call | flops 1268776960 | bytes 9912320 | tf_op jit(solution)/shard_map/conv/pallas_call | solution.py:355
  35.3 1.6 %collective-permute-start.11 = (bf16[192,896]{1,0:T(8,128)(2,1)S(1)}, bf16[192,896]{1,0:T(8,128)(2,1)S(1)}, u32[]{:S(2)}, u32[]{:S(2)}) collective-permute-start(bf16[192,896]{1,0:T(8,128)(2,1)S(1)} %collective-permute-done.8.refs_3_), channel_id=1, source_target_pairs={{0,4},{2,6},{4,12},{6,14},{12,8},{14,10},{8,0},{10,2},{20,16},{22,... | collective-permute-start | bytes 1032200 | tf_op jit(solution)/shard_map/ppermute | solution.py:86
  36.9 6.5 %collective-permute-done.7 = bf16[192,640]{1,0:T(8,128)(2,1)S(1)} collective-permute-done((bf16[192,640]{1,0:T(8,128)(2,1)S(1)}, bf16[192,640]{1,0:T(8,128)(2,1)S(1)}, u32[]{:S(2)}, u32[]{:S(2)}) %collective-permute-start.7) | collective-permute-done | bytes 245792 | tf_op jit(solution)/shard_map/ppermute | solution.py:371
  44.0 1.0 %collective-permute-done.11.refs_7_ = bf16[192,896]{1,0:T(8,128)(2,1)S(1)} collective-permute-done((bf16[192,896]{1,0:T(8,128)(2,1)S(1)}, bf16[192,896]{1,0:T(8,128)(2,1)S(1)}, u32[]{:S(2)}, u32[]{:S(2)}) %collective-permute-start.11) | collective-permute-done | bytes 344096 | tf_op jit(solution)/shard_map/ppermute | solution.py:86
  45.1 1.8 %embed.1 = (bf16[8,128,192]{2,1,0:T(8,128)(2,1)}, bf16[8,192,192]{2,1,0:T(8,128)(2,1)S(1)}) custom-call(bf16[128,704]{1,0:T(8,128)(2,1)S(1)} %conv.1.pooled_ref, bf16[192,896]{1,0:T(8,128)(2,1)S(1)} %pad_maximum_fusion.1.refs_0_, bf16[192,896]{1,0:T(8,128)(2,1)S(1)} %collective-permute-done.1.refs_1_, bf16[192,896]{1,0:T(8,128)(2,1)S(1)} %collective-permute-done.refs_2_, ...), custom_call_target="tpu_custom_call" | custom-call | flops 276824064 | bytes 2162688 | tf_op jit(solution)/shard_map/embed/pallas_call | solution.py:384
  46.9 0.7 collective-permute-start.14
  47.7 1.3 %collective-permute-done.12.other_ref = bf16[8,128,192]{2,1,0:T(8,128)(2,1)S(1)} collective-permute-done((bf16[8,128,192]{2,1,0:T(8,128)(2,1)}, bf16[8,128,192]{2,1,0:T(8,128)(2,1)S(1)}, u32[]{:S(2)}, u32[]{:S(2)}) %collective-permute-start.12) | collective-permute-done | bytes 393248 | tf_op jit(solution)/shard_map/ppermute | solution.py:393
  49.0 0.8 copy-done.2
  49.8 1.0 %copy-done.3 = bf16[8,128,192]{2,1,0:T(8,128)(2,1)S(1)} copy-done((bf16[8,128,192]{2,1,0:T(8,128)(2,1)S(1)}, bf16[8,128,192]{2,1,0:T(8,128)(2,1)}, u32[]{:S(2)}) %copy-start.3) | copy-done | bytes 393240
  50.8 1.7 %keyvalue.1 = (bf16[192,128]{1,0:T(8,128)(2,1)S(1)}, bf16[8,128,192]{2,1,0:T(8,128)(2,1)S(1)}, bf16[8,128,192]{2,1,0:T(8,128)(2,1)S(1)}, bf16[128,1536]{1,0:T(8,128)(2,1)S(1)}) custom-call(bf16[8,128,192]{2,1,0:T(8,128)(2,1)} %get-tuple-element.34.part_ref, bf16[8,128,192]{2,1,0:T(8,128)(2,1)S(1)} %copy-done.3, f32[8,1,192]{2,1,0:T(1,128)S(1)} %reshape.11.gain_ref, ...), custom_call_target="tpu_custom_call" | custom-call | flops 75497472 | bytes 589824 | tf_op jit(solution)/shard_map/keyvalue/pallas_call | solution.py:395
  52.5 1.0 %collective-permute-start.13 = (bf16[128,1536]{1,0:T(8,128)(2,1)S(1)}, bf16[128,1536]{1,0:T(8,128)(2,1)S(1)}, u32[]{:S(2)}, u32[]{:S(2)}) collective-permute-start(bf16[128,1536]{1,0:T(8,128)(2,1)S(1)} %get-tuple-element.38), channel_id=1, source_target_pairs={{0,2},{2,0},{4,6},{6,4},{8,10},{10,8},{12,14},{14,12},{1,3},{3,1},... | collective-permute-start | bytes 1179656 | tf_op jit(solution)/shard_map/ppermute | solution.py:412
  53.5 1.2 %collective-permute-start.17 = (bf16[192,128]{1,0:T(8,128)(2,1)S(1)}, bf16[192,128]{1,0:T(8,128)(2,1)S(1)}, u32[]{:S(2)}, u32[]{:S(2)}) collective-permute-start(bf16[192,128]{1,0:T(8,128)(2,1)S(1)} %get-tuple-element.41), channel_id=1, source_target_pairs={{0,4},{2,6},{4,12},{6,14},{12,8},{14,10},{8,0},{10,2},{1,5},{3,7},... | collective-permute-start | bytes 147464 | tf_op jit(solution)/shard_map/ppermute | solution.py:411
  54.8 1.7 %collective-permute-start.18 = (bf16[192,128]{1,0:T(8,128)(2,1)S(1)}, bf16[192,128]{1,0:T(8,128)(2,1)S(1)}, u32[]{:S(2)}, u32[]{:S(2)}) collective-permute-start(bf16[192,128]{1,0:T(8,128)(2,1)S(1)} %get-tuple-element.41), channel_id=1, source_target_pairs={{0,8},{2,10},{4,0},{6,2},{12,4},{14,6},{8,12},{10,14},{1,9},{3,11}... | collective-permute-start | bytes 147464 | tf_op jit(solution)/shard_map/ppermute | solution.py:411
  56.5 2.6 %collective-permute-start.19 = (bf16[192,128]{1,0:T(8,128)(2,1)S(1)}, bf16[192,128]{1,0:T(8,128)(2,1)S(1)}, u32[]{:S(2)}, u32[]{:S(2)}) collective-permute-start(bf16[192,128]{1,0:T(8,128)(2,1)S(1)} %get-tuple-element.41), channel_id=1, source_target_pairs={{0,12},{2,14},{4,8},{6,10},{12,0},{14,2},{8,4},{10,6},{1,13},{3,15... | collective-permute-start | bytes 147464 | tf_op jit(solution)/shard_map/ppermute | solution.py:411
  59.1 2.9 %collective-permute-done.14.refs_3_.refs_1_ = bf16[384,640]{1,0:T(8,128)(2,1)S(1)} collective-permute-done((bf16[384,640]{1,0:T(8,128)(2,1)S(1)}, bf16[384,640]{1,0:T(8,128)(2,1)S(1)}, u32[]{:S(2)}, u32[]{:S(2)}) %collective-permute-start.14) | collective-permute-done | bytes 491552 | tf_op jit(solution)/shard_map/ppermute | solution.py:86
  61.9 1.8 %collective-permute-done.13.refs_1_ = bf16[128,1536]{1,0:T(8,128)(2,1)S(1)} collective-permute-done((bf16[128,1536]{1,0:T(8,128)(2,1)S(1)}, bf16[128,1536]{1,0:T(8,128)(2,1)S(1)}, u32[]{:S(2)}, u32[]{:S(2)}) %collective-permute-start.13) | collective-permute-done | bytes 393248 | tf_op jit(solution)/shard_map/ppermute | solution.py:412
  63.8 0.9 collective-permute-start.15
  64.7 1.0 %collective-permute-start.16 = (bf16[384,640]{1,0:T(8,128)(2,1)S(1)}, bf16[384,640]{1,0:T(8,128)(2,1)S(1)}, u32[]{:S(2)}, u32[]{:S(2)}) collective-permute-start(bf16[384,640]{1,0:T(8,128)(2,1)S(1)} %collective-permute-done.14.refs_3_.refs_1_), channel_id=1, source_target_pairs={{0,4},{2,6},{4,12},{6,14},{12,8},{14,10},{8,0},{10,2},{20,16},{22,... | collective-permute-start | bytes 1474568 | tf_op jit(solution)/shard_map/ppermute | solution.py:86
  65.8 0.7 collective-permute-start.20
  66.5 5.0 %collective-permute-done.20 = bf16[4,192,128]{2,1,0:T(8,128)(2,1)S(1)} collective-permute-done((bf16[4,192,128]{2,1,0:T(8,128)(2,1)S(1)}, bf16[4,192,128]{2,1,0:T(8,128)(2,1)S(1)}, u32[]{:S(2)}, u32[]{:S(2)}) %collective-permute-start.20) | collective-permute-done | bytes 196640 | tf_op jit(solution)/shard_map/ppermute | solution.py:418
  71.6 4.6 %collective-permute-done.15.refs_4_.refs_2_ = bf16[384,640]{1,0:T(8,128)(2,1)S(1)} collective-permute-done((bf16[384,640]{1,0:T(8,128)(2,1)S(1)}, bf16[384,640]{1,0:T(8,128)(2,1)S(1)}, u32[]{:S(2)}, u32[]{:S(2)}) %collective-permute-start.15) | collective-permute-done | bytes 491552 | tf_op jit(solution)/shard_map/ppermute | solution.py:92
  76.2 1.6 %collective-permute-done.16.refs_5_.refs_3_ = bf16[384,640]{1,0:T(8,128)(2,1)S(1)} collective-permute-done((bf16[384,640]{1,0:T(8,128)(2,1)S(1)}, bf16[384,640]{1,0:T(8,128)(2,1)S(1)}, u32[]{:S(2)}, u32[]{:S(2)}) %collective-permute-start.16) | collective-permute-done | bytes 491552 | tf_op jit(solution)/shard_map/ppermute | solution.py:86
  78.4 1.4 %attend.1.attended_ref = bf16[2,256,192]{2,1,0:T(8,128)(2,1)S(1)} custom-call(bf16[256,256]{1,0:T(8,128)(2,1)S(1)} %query.1.query_ref, bf16[8,192,128]{2,1,0:T(8,128)(2,1)S(1)} %constant_dynamic-update-slice_fusion.own_ref, bf16[8,192,128]{2,1,0:T(8,128)(2,1)S(1)} %collective-permute-done.21.other_ref), custom_call_target="tpu_custom_call" | custom-call | flops 167772160 | bytes 786432 | tf_op jit(solution)/shard_map/attend/pallas_call | solution.py:434
  79.9 1.4 %output.1 = (bf16[128,1536]{1,0:T(8,128)(2,1)S(1)}, bf16[128,1536]{1,0:T(8,128)(2,1)S(1)}, bf16[16,256]{1,0:T(8,128)(2,1)S(1)}) custom-call(bf16[2,256,192]{2,1,0:T(8,128)(2,1)S(1)} %attend.1.attended_ref, bf16[8,128,192]{2,1,0:T(8,128)(2,1)S(1)} %get-tuple-element.36.embedded_ref, bf16[1536,256]{1,0:T(8,128)(2,1)S(1)} %copy-done.1, ...), custom_call_target="tpu_custom_call" | custom-call | flops 301989888 | bytes 1179648 | tf_op jit(solution)/shard_map/output/pallas_call | solution.py:448
  81.3 1.4 %collective-permute-start.24 = (bf16[16,256]{1,0:T(8,128)(2,1)S(1)}, bf16[16,256]{1,0:T(8,128)(2,1)S(1)}, u32[]{:S(2)}, u32[]{:S(2)}) collective-permute-start(bf16[16,256]{1,0:T(8,128)(2,1)S(1)} %get-tuple-element.47), channel_id=1, source_target_pairs={{0,2},{2,0},{4,6},{6,4},{8,10},{10,8},{12,14},{14,12},{1,3},{3,1},... | collective-permute-start | bytes 24584 | tf_op jit(solution)/shard_map/ppermute | solution.py:463
  82.6 2.3 %collective-permute-done.24 = bf16[16,256]{1,0:T(8,128)(2,1)S(1)} collective-permute-done((bf16[16,256]{1,0:T(8,128)(2,1)S(1)}, bf16[16,256]{1,0:T(8,128)(2,1)S(1)}, u32[]{:S(2)}, u32[]{:S(2)}) %collective-permute-start.24) | collective-permute-done | bytes 8224 | tf_op jit(solution)/shard_map/ppermute | solution.py:463
  85.3 1.4 %collective-permute-start.23 = (bf16[64,1536]{1,0:T(8,128)(2,1)S(1)}, bf16[64,1536]{1,0:T(8,128)(2,1)S(1)}, u32[]{:S(2)}, u32[]{:S(2)}) collective-permute-start(bf16[64,1536]{1,0:T(8,128)(2,1)S(1)} %get-tuple-element.54), channel_id=1, source_target_pairs={{0,2},{2,0},{4,6},{6,4},{8,10},{10,8},{12,14},{14,12},{1,3},{3,1},... | collective-permute-start | bytes 589832 | tf_op jit(solution)/shard_map/ppermute | solution.py:470
  86.6 3.6 %collective-permute-done.26 = bf16[16,256]{1,0:T(8,128)(2,1)S(1)} collective-permute-done((bf16[16,256]{1,0:T(8,128)(2,1)S(1)}, bf16[16,256]{1,0:T(8,128)(2,1)S(1)}, u32[]{:S(2)}, u32[]{:S(2)}) %collective-permute-start.26) | collective-permute-done | bytes 8224 | tf_op jit(solution)/shard_map/ppermute | solution.py:472
  90.3 2.3 %collective-permute-done.23.refs_1_ = bf16[64,1536]{1,0:T(8,128)(2,1)S(1)} collective-permute-done((bf16[64,1536]{1,0:T(8,128)(2,1)S(1)}, bf16[64,1536]{1,0:T(8,128)(2,1)S(1)}, u32[]{:S(2)}, u32[]{:S(2)}) %collective-permute-start.23) | collective-permute-done | bytes 196640 | tf_op jit(solution)/shard_map/ppermute | solution.py:470
  92.6 2.7 %collective-permute-start.27 = (bf16[32,256]{1,0:T(8,128)(2,1)S(1)}, bf16[32,256]{1,0:T(8,128)(2,1)S(1)}, u32[]{:S(2)}, u32[]{:S(2)}) collective-permute-start(bf16[32,256]{1,0:T(8,128)(2,1)S(1)} %pad_maximum_fusion.4), channel_id=1, source_target_pairs={{0,8},{2,10},{4,12},{6,14},{9,1},{11,3},{13,5},{15,7},{16,24},{18,... | collective-permute-start | bytes 49160 | tf_op jit(solution)/shard_map/ppermute | solution.py:475
  95.4 0.8 tokens.1
  96.8 0.8 pair.1
  (58 shorter events, 3.9 us)
Async XLA Ops:
  0.6 0.9 copy-start
  2.7 15.4 %collective-permute-start = (bf16[192,896]{1,0:T(8,128)(2,1)S(1)}, bf16[192,896]{1,0:T(8,128)(2,1)S(1)}, u32[]{:S(2)}, u32[]{:S(2)}) collective-permute-start(bf16[192,896]{1,0:T(8,128)(2,1)S(1)} %pad_maximum_fusion.1.refs_0_), channel_id=1, source_target_pairs={{0,4},{2,6},{4,12},{6,14},{12,8},{14,10},{8,0},{10,2},{20,16},{22,... | collective-permute-start | bytes 1032200 | tf_op jit(solution)/shard_map/ppermute | solution.py:86
  5.8 12.4 %collective-permute-start.1 = (bf16[192,896]{1,0:T(8,128)(2,1)S(1)}, bf16[192,896]{1,0:T(8,128)(2,1)S(1)}, u32[]{:S(2)}, u32[]{:S(2)}) collective-permute-start(bf16[192,896]{1,0:T(8,128)(2,1)S(1)} %pad_maximum_fusion.1.refs_0_), channel_id=1, source_target_pairs={{0,2},{2,0},{4,6},{6,4},{8,10},{10,8},{12,14},{14,12},{1,3},{3,1},... | collective-permute-start | bytes 1032200 | tf_op jit(solution)/shard_map/ppermute | solution.py:89
  8.6 5.9 %collective-permute-start.2 = (bf16[2,704]{1,0:T(2,128)(2,1)S(1)}, bf16[2,704]{1,0:T(2,128)(2,1)S(1)}, u32[]{:S(2)}, u32[]{:S(2)}) collective-permute-start(bf16[2,704]{1,0:T(2,128)(2,1)S(1)} %copy.14), channel_id=1, source_target_pairs={{0,2},{2,4},{4,6},{6,8},{8,10},{10,12},{12,14},{1,3},{3,5},{5,7},{... | collective-permute-start | bytes 8456 | tf_op jit(solution)/shard_map/ppermute | solution.py:327
  11.1 7.0 %collective-permute-start.3 = (bf16[2,704]{1,0:T(2,128)(2,1)S(1)}, bf16[2,704]{1,0:T(2,128)(2,1)S(1)}, u32[]{:S(2)}, u32[]{:S(2)}) collective-permute-start(bf16[2,704]{1,0:T(2,128)(2,1)S(1)} %copy.15), channel_id=1, source_target_pairs={{2,0},{4,2},{6,4},{8,6},{10,8},{12,10},{14,12},{3,1},{5,3},{7,5},{... | collective-permute-start | bytes 8456 | tf_op jit(solution)/shard_map/ppermute | solution.py:328
  18.2 6.4 %collective-permute-start.4 = (bf16[704,512]{1,0:T(8,128)(2,1)}, bf16[704,512]{1,0:T(8,128)(2,1)S(1)}, u32[]{:S(2)}, u32[]{:S(2)}) collective-permute-start(bf16[704,512]{1,0:T(8,128)(2,1)} %bitcast.16), channel_id=1, source_target_pairs={{0,1},{1,0},{2,3},{3,2},{4,5},{5,4},{6,7},{7,6},{8,9},{9,8},{10,11... | collective-permute-start | bytes 2162696 | tf_op jit(solution)/shard_map/ppermute | solution.py:333
  18.2 29.4 %copy-start.6 = (f32[1536]{0:T(1024)S(1)}, f32[1536]{0:T(1024)}, u32[]{:S(2)}) copy-start(f32[1536]{0:T(1024)} %param.14) | copy-start | bytes 18436
  18.2 4.2 %collective-permute-start.5 = (bf16[16,704]{1,0:T(8,128)(2,1)S(1)}, bf16[16,704]{1,0:T(8,128)(2,1)S(1)}, u32[]{:S(2)}, u32[]{:S(2)}) collective-permute-start(bf16[16,704]{1,0:T(8,128)(2,1)S(1)} %fusion.2), channel_id=1, source_target_pairs={{0,1},{1,0},{2,3},{3,2},{4,5},{5,4},{6,7},{7,6},{8,9},{9,8},{10,11... | collective-permute-start | bytes 67592 | tf_op jit(solution)/shard_map/ppermute | solution.py:335
  19.5 15.3 %collective-permute-start.6 = (bf16[192,896]{1,0:T(8,128)(2,1)S(1)}, bf16[192,896]{1,0:T(8,128)(2,1)S(1)}, u32[]{:S(2)}, u32[]{:S(2)}) collective-permute-start(bf16[192,896]{1,0:T(8,128)(2,1)S(1)} %collective-permute-done.refs_2_), channel_id=1, source_target_pairs={{0,16},{16,0},{1,17},{17,1},{2,18},{18,2},{3,19},{19,3},{4,20},{20... | collective-permute-start | bytes 1032200 | tf_op jit(solution)/shard_map/ppermute | solution.py:92
  20.4 14.4 %collective-permute-start.8 = (bf16[192,896]{1,0:T(8,128)(2,1)S(1)}, bf16[192,896]{1,0:T(8,128)(2,1)S(1)}, u32[]{:S(2)}, u32[]{:S(2)}) collective-permute-start(bf16[192,896]{1,0:T(8,128)(2,1)S(1)} %collective-permute-done.refs_2_), channel_id=1, source_target_pairs={{0,2},{2,0},{4,6},{6,4},{8,10},{10,8},{12,14},{14,12},{1,3},{3,1},... | collective-permute-start | bytes 1032200 | tf_op jit(solution)/shard_map/ppermute | solution.py:89
  22.5 14.4 %collective-permute-start.10 = (bf16[192,896]{1,0:T(8,128)(2,1)S(1)}, bf16[192,896]{1,0:T(8,128)(2,1)S(1)}, u32[]{:S(2)}, u32[]{:S(2)}) collective-permute-start(bf16[192,896]{1,0:T(8,128)(2,1)S(1)} %collective-permute-done.refs_2_), channel_id=1, source_target_pairs={{0,4},{2,6},{4,12},{6,14},{12,8},{14,10},{8,0},{10,2},{20,16},{22,... | collective-permute-start | bytes 1032200 | tf_op jit(solution)/shard_map/ppermute | solution.py:86
  24.6 1.1 %copy-start.4 = (bf16[512,704]{0,1:T(8,128)(2,1)S(1)}, bf16[512,704]{0,1:T(8,128)(2,1)}, u32[]{:S(2)}) copy-start(bf16[512,704]{0,1:T(8,128)(2,1)} %param.10) | copy-start | bytes 2162692
  28.5 51.3 %copy-start.1 = (bf16[1536,256]{1,0:T(8,128)(2,1)S(1)}, bf16[1536,256]{1,0:T(8,128)(2,1)}, u32[]{:S(2)}) copy-start(bf16[1536,256]{1,0:T(8,128)(2,1)} %pair_weight_ref.1) | copy-start | bytes 2359300
  34.8 62.0 %copy-start.5 = (bf16[128,128]{1,0:T(8,128)(2,1)S(1)}, bf16[128,128]{1,0:T(8,128)(2,1)}, u32[]{:S(2)}) copy-start(bf16[128,128]{1,0:T(8,128)(2,1)} %weight_ref.1) | copy-start | bytes 98308
  34.8 9.2 %collective-permute-start.9 = (bf16[192,896]{1,0:T(8,128)(2,1)S(1)}, bf16[192,896]{1,0:T(8,128)(2,1)S(1)}, u32[]{:S(2)}, u32[]{:S(2)}) collective-permute-start(bf16[192,896]{1,0:T(8,128)(2,1)S(1)} %collective-permute-done.8.refs_3_), channel_id=1, source_target_pairs={{0,16},{16,0},{1,17},{17,1},{2,18},{18,2},{3,19},{19,3},{4,20},{20... | collective-permute-start | bytes 1032200 | tf_op jit(solution)/shard_map/ppermute | solution.py:92
  35.3 9.8 %collective-permute-start.11 = (bf16[192,896]{1,0:T(8,128)(2,1)S(1)}, bf16[192,896]{1,0:T(8,128)(2,1)S(1)}, u32[]{:S(2)}, u32[]{:S(2)}) collective-permute-start(bf16[192,896]{1,0:T(8,128)(2,1)S(1)} %collective-permute-done.8.refs_3_), channel_id=1, source_target_pairs={{0,4},{2,6},{4,12},{6,14},{12,8},{14,10},{8,0},{10,2},{20,16},{22,... | collective-permute-start | bytes 1032200 | tf_op jit(solution)/shard_map/ppermute | solution.py:86
  36.9 6.5 %collective-permute-start.7 = (bf16[192,640]{1,0:T(8,128)(2,1)S(1)}, bf16[192,640]{1,0:T(8,128)(2,1)S(1)}, u32[]{:S(2)}, u32[]{:S(2)}) collective-permute-start(bf16[192,640]{1,0:T(8,128)(2,1)S(1)} %pad_maximum_fusion.2), channel_id=1, source_target_pairs={{0,2},{2,0},{4,6},{6,4},{8,10},{10,8},{12,14},{14,12},{1,3},{3,1},... | collective-permute-start | bytes 737288 | tf_op jit(solution)/shard_map/ppermute | solution.py:371
  46.8 2.1 %collective-permute-start.12 = (bf16[8,128,192]{2,1,0:T(8,128)(2,1)}, bf16[8,128,192]{2,1,0:T(8,128)(2,1)S(1)}, u32[]{:S(2)}, u32[]{:S(2)}) collective-permute-start(bf16[8,128,192]{2,1,0:T(8,128)(2,1)} %get-tuple-element.34.part_ref), channel_id=1, source_target_pairs={{0,1},{1,0},{2,3},{3,2},{4,5},{5,4},{6,7},{7,6},{8,9},{9,8},{10,11... | collective-permute-start | bytes 1179656 | tf_op jit(solution)/shard_map/ppermute | solution.py:393
  46.9 15.1 %collective-permute-start.14 = (bf16[384,640]{1,0:T(8,128)(2,1)S(1)}, bf16[384,640]{1,0:T(8,128)(2,1)S(1)}, u32[]{:S(2)}, u32[]{:S(2)}) collective-permute-start(bf16[384,640]{1,0:T(8,128)(2,1)S(1)} %pad_maximum_fusion.refs_2_.refs_0_), channel_id=1, source_target_pairs={{0,4},{2,6},{4,12},{6,14},{12,8},{14,10},{8,0},{10,2},{20,16},{22,... | collective-permute-start | bytes 1474568 | tf_op jit(solution)/shard_map/ppermute | solution.py:86
  48.9 0.8 copy-start.2
  49.8 1.0 %copy-start.3 = (bf16[8,128,192]{2,1,0:T(8,128)(2,1)S(1)}, bf16[8,128,192]{2,1,0:T(8,128)(2,1)}, u32[]{:S(2)}) copy-start(bf16[8,128,192]{2,1,0:T(8,128)(2,1)} %copy-done.2) | copy-start | bytes 1179652
  52.5 11.2 %collective-permute-start.13 = (bf16[128,1536]{1,0:T(8,128)(2,1)S(1)}, bf16[128,1536]{1,0:T(8,128)(2,1)S(1)}, u32[]{:S(2)}, u32[]{:S(2)}) collective-permute-start(bf16[128,1536]{1,0:T(8,128)(2,1)S(1)} %get-tuple-element.38), channel_id=1, source_target_pairs={{0,2},{2,0},{4,6},{6,4},{8,10},{10,8},{12,14},{14,12},{1,3},{3,1},... | collective-permute-start | bytes 1179656 | tf_op jit(solution)/shard_map/ppermute | solution.py:412
  53.5 12.1 %collective-permute-start.17 = (bf16[192,128]{1,0:T(8,128)(2,1)S(1)}, bf16[192,128]{1,0:T(8,128)(2,1)S(1)}, u32[]{:S(2)}, u32[]{:S(2)}) collective-permute-start(bf16[192,128]{1,0:T(8,128)(2,1)S(1)} %get-tuple-element.41), channel_id=1, source_target_pairs={{0,4},{2,6},{4,12},{6,14},{12,8},{14,10},{8,0},{10,2},{1,5},{3,7},... | collective-permute-start | bytes 147464 | tf_op jit(solution)/shard_map/ppermute | solution.py:411
  54.8 10.9 %collective-permute-start.18 = (bf16[192,128]{1,0:T(8,128)(2,1)S(1)}, bf16[192,128]{1,0:T(8,128)(2,1)S(1)}, u32[]{:S(2)}, u32[]{:S(2)}) collective-permute-start(bf16[192,128]{1,0:T(8,128)(2,1)S(1)} %get-tuple-element.41), channel_id=1, source_target_pairs={{0,8},{2,10},{4,0},{6,2},{12,4},{14,6},{8,12},{10,14},{1,9},{3,11}... | collective-permute-start | bytes 147464 | tf_op jit(solution)/shard_map/ppermute | solution.py:411
  56.5 9.2 %collective-permute-start.19 = (bf16[192,128]{1,0:T(8,128)(2,1)S(1)}, bf16[192,128]{1,0:T(8,128)(2,1)S(1)}, u32[]{:S(2)}, u32[]{:S(2)}) collective-permute-start(bf16[192,128]{1,0:T(8,128)(2,1)S(1)} %get-tuple-element.41), channel_id=1, source_target_pairs={{0,12},{2,14},{4,8},{6,10},{12,0},{14,2},{8,4},{10,6},{1,13},{3,15... | collective-permute-start | bytes 147464 | tf_op jit(solution)/shard_map/ppermute | solution.py:411
  63.8 12.4 %collective-permute-start.15 = (bf16[384,640]{1,0:T(8,128)(2,1)S(1)}, bf16[384,640]{1,0:T(8,128)(2,1)S(1)}, u32[]{:S(2)}, u32[]{:S(2)}) collective-permute-start(bf16[384,640]{1,0:T(8,128)(2,1)S(1)} %collective-permute-done.14.refs_3_.refs_1_), channel_id=1, source_target_pairs={{0,16},{16,0},{1,17},{17,1},{2,18},{18,2},{3,19},{19,3},{4,20},{20... | collective-permute-start | bytes 1474568 | tf_op jit(solution)/shard_map/ppermute | solution.py:92
  64.7 13.2 %collective-permute-start.16 = (bf16[384,640]{1,0:T(8,128)(2,1)S(1)}, bf16[384,640]{1,0:T(8,128)(2,1)S(1)}, u32[]{:S(2)}, u32[]{:S(2)}) collective-permute-start(bf16[384,640]{1,0:T(8,128)(2,1)S(1)} %collective-permute-done.14.refs_3_.refs_1_), channel_id=1, source_target_pairs={{0,4},{2,6},{4,12},{6,14},{12,8},{14,10},{8,0},{10,2},{20,16},{22,... | collective-permute-start | bytes 1474568 | tf_op jit(solution)/shard_map/ppermute | solution.py:86
  65.8 5.7 %collective-permute-start.20 = (bf16[4,192,128]{2,1,0:T(8,128)(2,1)S(1)}, bf16[4,192,128]{2,1,0:T(8,128)(2,1)S(1)}, u32[]{:S(2)}, u32[]{:S(2)}) collective-permute-start(bf16[4,192,128]{2,1,0:T(8,128)(2,1)S(1)} %pad_maximum_fusion.3), channel_id=1, source_target_pairs={{0,2},{2,0},{4,6},{6,4},{8,10},{10,8},{12,14},{14,12},{1,3},{3,1},... | collective-permute-start | bytes 589832 | tf_op jit(solution)/shard_map/ppermute | solution.py:418
  71.5 6.9 %collective-permute-start.21 = (bf16[8,192,128]{2,1,0:T(8,128)(2,1)S(1)}, bf16[8,192,128]{2,1,0:T(8,128)(2,1)S(1)}, u32[]{:S(2)}, u32[]{:S(2)}) collective-permute-start(bf16[8,192,128]{2,1,0:T(8,128)(2,1)S(1)} %constant_dynamic-update-slice_fusion.own_ref), channel_id=1, source_target_pairs={{0,1},{1,0},{2,3},{3,2},{4,5},{5,4},{6,7},{7,6},{8,9},{9,8},{10,11... | collective-permute-start | bytes 1179656 | tf_op jit(solution)/shard_map/ppermute | solution.py:421
  81.3 3.7 %collective-permute-start.24 = (bf16[16,256]{1,0:T(8,128)(2,1)S(1)}, bf16[16,256]{1,0:T(8,128)(2,1)S(1)}, u32[]{:S(2)}, u32[]{:S(2)}) collective-permute-start(bf16[16,256]{1,0:T(8,128)(2,1)S(1)} %get-tuple-element.47), channel_id=1, source_target_pairs={{0,2},{2,0},{4,6},{6,4},{8,10},{10,8},{12,14},{14,12},{1,3},{3,1},... | collective-permute-start | bytes 24584 | tf_op jit(solution)/shard_map/ppermute | solution.py:463
  82.6 2.4 %collective-permute-start.22 = (bf16[128,1536]{1,0:T(8,128)(2,1)S(1)}, bf16[128,1536]{1,0:T(8,128)(2,1)S(1)}, u32[]{:S(2)}, u32[]{:S(2)}) collective-permute-start(bf16[128,1536]{1,0:T(8,128)(2,1)S(1)} %get-tuple-element.46), channel_id=1, source_target_pairs={{0,1},{1,0},{2,3},{3,2},{4,5},{5,4},{6,7},{7,6},{8,9},{9,8},{10,11... | collective-permute-start | bytes 1179656 | tf_op jit(solution)/shard_map/ppermute | solution.py:466
  85.0 1.6 %collective-permute-start.25 = (bf16[16,256]{1,0:T(8,128)(2,1)S(1)}, bf16[16,256]{1,0:T(8,128)(2,1)S(1)}, u32[]{:S(2)}, u32[]{:S(2)}) collective-permute-start(bf16[16,256]{1,0:T(8,128)(2,1)S(1)} %add_convert_fusion.2), channel_id=1, source_target_pairs={{0,1},{1,0},{2,3},{3,2},{4,5},{5,4},{6,7},{7,6},{8,9},{9,8},{10,11... | collective-permute-start | bytes 24584 | tf_op jit(solution)/shard_map/ppermute | solution.py:465
  85.3 7.4 %collective-permute-start.23 = (bf16[64,1536]{1,0:T(8,128)(2,1)S(1)}, bf16[64,1536]{1,0:T(8,128)(2,1)S(1)}, u32[]{:S(2)}, u32[]{:S(2)}) collective-permute-start(bf16[64,1536]{1,0:T(8,128)(2,1)S(1)} %get-tuple-element.54), channel_id=1, source_target_pairs={{0,2},{2,0},{4,6},{6,4},{8,10},{10,8},{12,14},{14,12},{1,3},{3,1},... | collective-permute-start | bytes 589832 | tf_op jit(solution)/shard_map/ppermute | solution.py:470
  86.6 3.7 %collective-permute-start.26 = (bf16[16,256]{1,0:T(8,128)(2,1)S(1)}, bf16[16,256]{1,0:T(8,128)(2,1)S(1)}, u32[]{:S(2)}, u32[]{:S(2)}) collective-permute-start(bf16[16,256]{1,0:T(8,128)(2,1)S(1)} %add_convert_fusion.1), channel_id=1, source_target_pairs={{0,4},{2,6},{4,0},{6,2},{8,12},{10,14},{12,8},{14,10},{1,5},{3,7},... | collective-permute-start | bytes 24584 | tf_op jit(solution)/shard_map/ppermute | solution.py:472
  92.6 4.2 %collective-permute-start.27 = (bf16[32,256]{1,0:T(8,128)(2,1)S(1)}, bf16[32,256]{1,0:T(8,128)(2,1)S(1)}, u32[]{:S(2)}, u32[]{:S(2)}) collective-permute-start(bf16[32,256]{1,0:T(8,128)(2,1)S(1)} %pad_maximum_fusion.4), channel_id=1, source_target_pairs={{0,8},{2,10},{4,12},{6,14},{9,1},{11,3},{13,5},{15,7},{16,24},{18,... | collective-permute-start | bytes 49160 | tf_op jit(solution)/shard_map/ppermute | solution.py:475

commit v16 on v15

--- a/solution.py
+++ b/solution.py
@@ -343,7 +343,7 @@
         in_specs=vspec(3),
         out_specs=vspec(2),
         scratch_shapes=[pltpu.VMEM((channels, positions), BF16), pltpu.VMEM((channels, 8), F32)],
-        compiler_params=params(20),
+        compiler_params=params(12),
         cost_estimate=cost(2 * taps * tokens * channels * positions, 4 * channels * positions),
         name="act",
     )(signal_t, other_t, gain_row)
@@ -401,7 +401,7 @@
         ) + (shape((tokens, width), BF16),) * (sides - 1),
         in_specs=vspec(4),
         out_specs=vspec(2 + sides),
-        compiler_params=params(16),
+        compiler_params=params(12),
         cost_estimate=cost(2 * tokens * width * DV, 2 * width * DV),
         name="keyvalue",
     )(part, other_part, attn_gain.reshape(pieces, 1, block), keyvalue_blocks)
@@ -451,7 +451,7 @@
         in_specs=vspec(3 + len(later_blocks)),
         out_specs=vspec(3),
         scratch_shapes=[pltpu.VMEM((pieces, sides * tokens, block), BF16)],
-        compiler_params=params(16),
+        compiler_params=params(12),
         cost_estimate=cost(2 * sides * tokens * heads * DV * width, 2 * heads * DV * width),
         name="output",
     )(attended, embedded, rowcol_weight, *later_blocks)
@@ -498,7 +498,7 @@
         in_specs=vspec(3),
         out_specs=pl.BlockSpec(memory_space=VMEM),
         scratch_shapes=[pltpu.VMEM((span, pair_features), F32)],
-        compiler_params=params(16),
+        compiler_params=params(12),
         cost_estimate=cost(2 * pair_rows * span * pair_features**2, 2 * pair_rows * span * pair_features),
         name="pair",
     )(projected[:pair_rows], rows_all, pair_weight)

time: 98.6 us -> 98.5 us (level)
  no operation moved by 1% of the time
where the time goes in v16:
time: 98.5 us; the launch traced here: 97.6 us
  waiting for transfers between devices  38 us (39%)
  starting transfers between devices  31.5 us (32%)
  Pallas kernels  17.6 us (18%)
  local copies, waits for them, and re-layouts  8.2 us (8%)
  other arithmetic  1.38 us (1%)
  between operations  0.99 us (1%)
    ppermute x5, starting transfers between devices, along(): self.at[target] = lax.ppermute(self.at[source], ('grp', 'seq'), pairs)  8.47 us
    ppermute x1, waiting for transfers between devices, on_device(): received = lax.ppermute(theirs, 'seq', pair_swap)  6.5 us
    pallas_call x1, Pallas kernels, on_device(): pl.pallas_call(functools.partial(conv_kernel, positions), out_shape=shape...  6.2 us
    ppermute x5, waiting for transfers between devices, along(): self.at[target] = lax.ppermute(self.at[source], ('grp', 'seq'), pairs)  5.57 us
    ppermute x3, starting transfers between devices, on_device(): turned = [lax.ppermute(keyvalue, 'seq', turn) for turn in turns]  5.52 us
    ppermute x3, waiting for transfers between devices, between(): self.at[target] = lax.ppermute(self.at[source], 'grp', [(0, 1), (1, 0)])  5.25 us
    ppermute x1, waiting for transfers between devices, on_device(): gathered = jnp.concatenate([row, lax.ppermute(row, 'seq', pair_swap)])  5.03 us
    unnamed x20, local copies, waits for them, and re-layouts  4.15 us
  transfers between devices with their start and end apart: 28, of which 14 were waited for; matrix products, arithmetic and copies ran while one was open for 5% of the time, Pallas kernels for 12%

profile of v16, /device:TPU:0, one launch (start us, length us, event | category | flops | bytes accessed | tf_op | source)
XLA Modules:
  0.0 97.6 jit_solution(11370439142000019740)
XLA Ops:
  0.7 0.9 copy-done
  1.6 1.1 %pad_maximum_fusion.1.refs_0_ = bf16[192,896]{1,0:T(8,128)(2,1)S(1)} fusion(bf16[192,192]{1,0:T(8,128)(2,1)S(1)} %constant_dynamic-slice_fusion.2, bf16[192,704]{1,0:T(8,128)(2,1)} %bitcast.19), kind=kLoop, calls=%fused_computation.2 | loop fusion | flops 688128 | bytes 688128 | tf_op jit(solution)/shard_map/concatenate | solution.py:301
  2.7 3.1 %collective-permute-start = (bf16[192,896]{1,0:T(8,128)(2,1)S(1)}, bf16[192,896]{1,0:T(8,128)(2,1)S(1)}, u32[]{:S(2)}, u32[]{:S(2)}) collective-permute-start(bf16[192,896]{1,0:T(8,128)(2,1)S(1)} %pad_maximum_fusion.1.refs_0_), channel_id=1, source_target_pairs={{0,4},{2,6},{4,12},{6,14},{12,8},{14,10},{8,0},{10,2},{20,16},{22,... | collective-permute-start | bytes 1032200 | tf_op jit(solution)/shard_map/ppermute | solution.py:86
  5.8 1.5 %collective-permute-start.1 = (bf16[192,896]{1,0:T(8,128)(2,1)S(1)}, bf16[192,896]{1,0:T(8,128)(2,1)S(1)}, u32[]{:S(2)}, u32[]{:S(2)}) collective-permute-start(bf16[192,896]{1,0:T(8,128)(2,1)S(1)} %pad_maximum_fusion.1.refs_0_), channel_id=1, source_target_pairs={{0,2},{2,0},{4,6},{6,4},{8,10},{10,8},{12,14},{14,12},{1,3},{3,1},... | collective-permute-start | bytes 1032200 | tf_op jit(solution)/shard_map/ppermute | solution.py:89
  7.3 1.1 %fusion.3 = (bf16[2,704]{0,1:T(8,128)(2,1)S(1)}, bf16[2,704]{0,1:T(8,128)(2,1)S(1)}) fusion(bf16[512,704]{0,1:T(8,128)(2,1)} %param.10), kind=kLoop, calls=%fused_computation.24 | loop fusion | bytes 11264 | tf_op jit(solution)/shard_map/slice | solution.py:328
  8.6 2.4 %collective-permute-start.2 = (bf16[2,704]{1,0:T(2,128)(2,1)S(1)}, bf16[2,704]{1,0:T(2,128)(2,1)S(1)}, u32[]{:S(2)}, u32[]{:S(2)}) collective-permute-start(bf16[2,704]{1,0:T(2,128)(2,1)S(1)} %copy.14), channel_id=1, source_target_pairs={{0,2},{2,4},{4,6},{6,8},{8,10},{10,12},{12,14},{1,3},{3,5},{5,7},{... | collective-permute-start | bytes 8456 | tf_op jit(solution)/shard_map/ppermute | solution.py:327
  11.1 1.3 %collective-permute-start.3 = (bf16[2,704]{1,0:T(2,128)(2,1)S(1)}, bf16[2,704]{1,0:T(2,128)(2,1)S(1)}, u32[]{:S(2)}, u32[]{:S(2)}) collective-permute-start(bf16[2,704]{1,0:T(2,128)(2,1)S(1)} %copy.15), channel_id=1, source_target_pairs={{2,0},{4,2},{6,4},{8,6},{10,8},{12,10},{14,12},{3,1},{5,3},{7,5},{... | collective-permute-start | bytes 8456 | tf_op jit(solution)/shard_map/ppermute | solution.py:328
  12.5 1.0 constant_dynamic-slice_fusion.1
  13.4 1.0 %dynamic-slice_bitcast_fusion.1 = (bf16[192,384]{1,0:T(8,128)(2,1)S(1)}, bf16[192,384]{1,0:T(8,128)(2,1)S(1)}) fusion(bf16[1536,192]{0,1:T(8,128)(2,1)} %param.17, s32[]{:T(128)S(6)} %select_n.45, s32[]{:T(128)S(6)} %select_n.47), kind=kLoop, calls=%fused_computation.6 | loop fusion | bytes 589832 | tf_op jit(solution)/shard_map/dynamic_slice | solution.py:315
  14.5 3.7 %collective-permute-done.3 = bf16[2,704]{1,0:T(2,128)(2,1)S(1)} collective-permute-done((bf16[2,704]{1,0:T(2,128)(2,1)S(1)}, bf16[2,704]{1,0:T(2,128)(2,1)S(1)}, u32[]{:S(2)}, u32[]{:S(2)}) %collective-permute-start.3) | collective-permute-done | bytes 2848 | tf_op jit(solution)/shard_map/ppermute | solution.py:328
  18.8 0.7 reshape.10.gain_ref
  19.5 1.0 collective-permute-start.6
  20.4 1.9 %collective-permute-start.8 = (bf16[192,896]{1,0:T(8,128)(2,1)S(1)}, bf16[192,896]{1,0:T(8,128)(2,1)S(1)}, u32[]{:S(2)}, u32[]{:S(2)}) collective-permute-start(bf16[192,896]{1,0:T(8,128)(2,1)S(1)} %collective-permute-done.refs_2_), channel_id=1, source_target_pairs={{0,2},{2,0},{4,6},{6,4},{8,10},{10,8},{12,14},{14,12},{1,3},{3,1},... | collective-permute-start | bytes 1032200 | tf_op jit(solution)/shard_map/ppermute | solution.py:89
  22.5 2.1 %collective-permute-start.10 = (bf16[192,896]{1,0:T(8,128)(2,1)S(1)}, bf16[192,896]{1,0:T(8,128)(2,1)S(1)}, u32[]{:S(2)}, u32[]{:S(2)}) collective-permute-start(bf16[192,896]{1,0:T(8,128)(2,1)S(1)} %collective-permute-done.refs_2_), channel_id=1, source_target_pairs={{0,4},{2,6},{4,12},{6,14},{12,8},{14,10},{8,0},{10,2},{20,16},{22,... | collective-permute-start | bytes 1032200 | tf_op jit(solution)/shard_map/ppermute | solution.py:86
  24.6 1.1 %copy-done.4 = bf16[512,704]{0,1:T(8,128)(2,1)S(1)} copy-done((bf16[512,704]{0,1:T(8,128)(2,1)S(1)}, bf16[512,704]{0,1:T(8,128)(2,1)}, u32[]{:S(2)}) %copy-start.4) | copy-done | bytes 720920
  25.7 2.8 %act.1 = (bf16[640,1408]{1,0:T(8,128)(2,1)S(1)}, f32[128,704]{1,0:T(8,128)S(1)}) custom-call(bf16[704,512]{1,0:T(8,128)(2,1)S(1)} %bitcast.17, bf16[704,512]{1,0:T(8,128)(2,1)S(1)} %collective-permute-done.4.other_ref, f32[1,1408]{1,0:T(1,128)S(1)} %reshape.10.gain_ref), custom_call_target="tpu_custom_call" | custom-call | flops 922746880 | bytes 2883584 | tf_op jit(solution)/shard_map/act/pallas_call | solution.py:340
  28.6 6.2 %conv.1.pooled_ref = bf16[128,704]{1,0:T(8,128)(2,1)S(1)} custom-call(bf16[640,1408]{1,0:T(8,128)(2,1)S(1)} %get-tuple-element.27.windows_ref, f32[128,704]{1,0:T(8,128)S(1)} %get-tuple-element.28.residual_ref, bf16[16,1408]{1,0:T(8,128)(2,1)S(1)} %maximum_select_fusion.halo_ref, f32[1,1408]{1,0:T(1,128)S(1)} %reshape.10.gain_ref, bf16[5,704,1408]{2,1,0:T(8,128)(2,1)} %bitcast.18), custom_call_target="tpu_custom_call" | custom-call | flops 1268776960 | bytes 9912320 | tf_op jit(solution)/shard_map/conv/pallas_call | solution.py:355
  35.3 1.6 %collective-permute-start.11 = (bf16[192,896]{1,0:T(8,128)(2,1)S(1)}, bf16[192,896]{1,0:T(8,128)(2,1)S(1)}, u32[]{:S(2)}, u32[]{:S(2)}) collective-permute-start(bf16[192,896]{1,0:T(8,128)(2,1)S(1)} %collective-permute-done.8.refs_3_), channel_id=1, source_target_pairs={{0,4},{2,6},{4,12},{6,14},{12,8},{14,10},{8,0},{10,2},{20,16},{22,... | collective-permute-start | bytes 1032200 | tf_op jit(solution)/shard_map/ppermute | solution.py:86
  36.9 6.5 %collective-permute-done.7 = bf16[192,640]{1,0:T(8,128)(2,1)S(1)} collective-permute-done((bf16[192,640]{1,0:T(8,128)(2,1)S(1)}, bf16[192,640]{1,0:T(8,128)(2,1)S(1)}, u32[]{:S(2)}, u32[]{:S(2)}) %collective-permute-start.7) | collective-permute-done | bytes 245792 | tf_op jit(solution)/shard_map/ppermute | solution.py:371
  44.0 1.0 %collective-permute-done.11.refs_7_ = bf16[192,896]{1,0:T(8,128)(2,1)S(1)} collective-permute-done((bf16[192,896]{1,0:T(8,128)(2,1)S(1)}, bf16[192,896]{1,0:T(8,128)(2,1)S(1)}, u32[]{:S(2)}, u32[]{:S(2)}) %collective-permute-start.11) | collective-permute-done | bytes 344096 | tf_op jit(solution)/shard_map/ppermute | solution.py:86
  45.1 1.8 %embed.1 = (bf16[8,128,192]{2,1,0:T(8,128)(2,1)}, bf16[8,192,192]{2,1,0:T(8,128)(2,1)S(1)}) custom-call(bf16[128,704]{1,0:T(8,128)(2,1)S(1)} %conv.1.pooled_ref, bf16[192,896]{1,0:T(8,128)(2,1)S(1)} %pad_maximum_fusion.1.refs_0_, bf16[192,896]{1,0:T(8,128)(2,1)S(1)} %collective-permute-done.1.refs_1_, bf16[192,896]{1,0:T(8,128)(2,1)S(1)} %collective-permute-done.refs_2_, ...), custom_call_target="tpu_custom_call" | custom-call | flops 276824064 | bytes 2162688 | tf_op jit(solution)/shard_map/embed/pallas_call | solution.py:384
  46.9 0.7 collective-permute-start.14
  47.7 1.3 %collective-permute-done.12.other_ref = bf16[8,128,192]{2,1,0:T(8,128)(2,1)S(1)} collective-permute-done((bf16[8,128,192]{2,1,0:T(8,128)(2,1)}, bf16[8,128,192]{2,1,0:T(8,128)(2,1)S(1)}, u32[]{:S(2)}, u32[]{:S(2)}) %collective-permute-start.12) | collective-permute-done | bytes 393248 | tf_op jit(solution)/shard_map/ppermute | solution.py:393
  49.0 0.8 copy-done.2
  49.8 1.0 %copy-done.3 = bf16[8,128,192]{2,1,0:T(8,128)(2,1)S(1)} copy-done((bf16[8,128,192]{2,1,0:T(8,128)(2,1)S(1)}, bf16[8,128,192]{2,1,0:T(8,128)(2,1)}, u32[]{:S(2)}) %copy-start.3) | copy-done | bytes 393240
  50.8 1.7 %keyvalue.1 = (bf16[192,128]{1,0:T(8,128)(2,1)S(1)}, bf16[8,128,192]{2,1,0:T(8,128)(2,1)S(1)}, bf16[8,128,192]{2,1,0:T(8,128)(2,1)S(1)}, bf16[128,1536]{1,0:T(8,128)(2,1)S(1)}) custom-call(bf16[8,128,192]{2,1,0:T(8,128)(2,1)} %get-tuple-element.34.part_ref, bf16[8,128,192]{2,1,0:T(8,128)(2,1)S(1)} %copy-done.3, f32[8,1,192]{2,1,0:T(1,128)S(1)} %reshape.11.gain_ref, ...), custom_call_target="tpu_custom_call" | custom-call | flops 75497472 | bytes 589824 | tf_op jit(solution)/shard_map/keyvalue/pallas_call | solution.py:395
  52.5 1.0 %collective-permute-start.13 = (bf16[128,1536]{1,0:T(8,128)(2,1)S(1)}, bf16[128,1536]{1,0:T(8,128)(2,1)S(1)}, u32[]{:S(2)}, u32[]{:S(2)}) collective-permute-start(bf16[128,1536]{1,0:T(8,128)(2,1)S(1)} %get-tuple-element.38), channel_id=1, source_target_pairs={{0,2},{2,0},{4,6},{6,4},{8,10},{10,8},{12,14},{14,12},{1,3},{3,1},... | collective-permute-start | bytes 1179656 | tf_op jit(solution)/shard_map/ppermute | solution.py:412
  53.5 1.2 %collective-permute-start.17 = (bf16[192,128]{1,0:T(8,128)(2,1)S(1)}, bf16[192,128]{1,0:T(8,128)(2,1)S(1)}, u32[]{:S(2)}, u32[]{:S(2)}) collective-permute-start(bf16[192,128]{1,0:T(8,128)(2,1)S(1)} %get-tuple-element.41), channel_id=1, source_target_pairs={{0,4},{2,6},{4,12},{6,14},{12,8},{14,10},{8,0},{10,2},{1,5},{3,7},... | collective-permute-start | bytes 147464 | tf_op jit(solution)/shard_map/ppermute | solution.py:411
  54.8 1.7 %collective-permute-start.18 = (bf16[192,128]{1,0:T(8,128)(2,1)S(1)}, bf16[192,128]{1,0:T(8,128)(2,1)S(1)}, u32[]{:S(2)}, u32[]{:S(2)}) collective-permute-start(bf16[192,128]{1,0:T(8,128)(2,1)S(1)} %get-tuple-element.41), channel_id=1, source_target_pairs={{0,8},{2,10},{4,0},{6,2},{12,4},{14,6},{8,12},{10,14},{1,9},{3,11}... | collective-permute-start | bytes 147464 | tf_op jit(solution)/shard_map/ppermute | solution.py:411
  56.5 2.6 %collective-permute-start.19 = (bf16[192,128]{1,0:T(8,128)(2,1)S(1)}, bf16[192,128]{1,0:T(8,128)(2,1)S(1)}, u32[]{:S(2)}, u32[]{:S(2)}) collective-permute-start(bf16[192,128]{1,0:T(8,128)(2,1)S(1)} %get-tuple-element.41), channel_id=1, source_target_pairs={{0,12},{2,14},{4,8},{6,10},{12,0},{14,2},{8,4},{10,6},{1,13},{3,15... | collective-permute-start | bytes 147464 | tf_op jit(solution)/shard_map/ppermute | solution.py:411
  59.1 2.9 %collective-permute-done.14.refs_3_.refs_1_ = bf16[384,640]{1,0:T(8,128)(2,1)S(1)} collective-permute-done((bf16[384,640]{1,0:T(8,128)(2,1)S(1)}, bf16[384,640]{1,0:T(8,128)(2,1)S(1)}, u32[]{:S(2)}, u32[]{:S(2)}) %collective-permute-start.14) | collective-permute-done | bytes 491552 | tf_op jit(solution)/shard_map/ppermute | solution.py:86
  61.9 1.8 %collective-permute-done.13.refs_1_ = bf16[128,1536]{1,0:T(8,128)(2,1)S(1)} collective-permute-done((bf16[128,1536]{1,0:T(8,128)(2,1)S(1)}, bf16[128,1536]{1,0:T(8,128)(2,1)S(1)}, u32[]{:S(2)}, u32[]{:S(2)}) %collective-permute-start.13) | collective-permute-done | bytes 393248 | tf_op jit(solution)/shard_map/ppermute | solution.py:412
  63.8 0.9 collective-permute-start.15
  64.7 1.0 %collective-permute-start.16 = (bf16[384,640]{1,0:T(8,128)(2,1)S(1)}, bf16[384,640]{1,0:T(8,128)(2,1)S(1)}, u32[]{:S(2)}, u32[]{:S(2)}) collective-permute-start(bf16[384,640]{1,0:T(8,128)(2,1)S(1)} %collective-permute-done.14.refs_3_.refs_1_), channel_id=1, source_target_pairs={{0,4},{2,6},{4,12},{6,14},{12,8},{14,10},{8,0},{10,2},{20,16},{22,... | collective-permute-start | bytes 1474568 | tf_op jit(solution)/shard_map/ppermute | solution.py:86
  65.8 0.7 collective-permute-start.20
  66.5 5.0 %collective-permute-done.20 = bf16[4,192,128]{2,1,0:T(8,128)(2,1)S(1)} collective-permute-done((bf16[4,192,128]{2,1,0:T(8,128)(2,1)S(1)}, bf16[4,192,128]{2,1,0:T(8,128)(2,1)S(1)}, u32[]{:S(2)}, u32[]{:S(2)}) %collective-permute-start.20) | collective-permute-done | bytes 196640 | tf_op jit(solution)/shard_map/ppermute | solution.py:418
  71.6 4.6 %collective-permute-done.15.refs_4_.refs_2_ = bf16[384,640]{1,0:T(8,128)(2,1)S(1)} collective-permute-done((bf16[384,640]{1,0:T(8,128)(2,1)S(1)}, bf16[384,640]{1,0:T(8,128)(2,1)S(1)}, u32[]{:S(2)}, u32[]{:S(2)}) %collective-permute-start.15) | collective-permute-done | bytes 491552 | tf_op jit(solution)/shard_map/ppermute | solution.py:92
  76.2 1.6 %collective-permute-done.16.refs_5_.refs_3_ = bf16[384,640]{1,0:T(8,128)(2,1)S(1)} collective-permute-done((bf16[384,640]{1,0:T(8,128)(2,1)S(1)}, bf16[384,640]{1,0:T(8,128)(2,1)S(1)}, u32[]{:S(2)}, u32[]{:S(2)}) %collective-permute-start.16) | collective-permute-done | bytes 491552 | tf_op jit(solution)/shard_map/ppermute | solution.py:86
  78.4 1.4 %attend.1.attended_ref = bf16[2,256,192]{2,1,0:T(8,128)(2,1)S(1)} custom-call(bf16[256,256]{1,0:T(8,128)(2,1)S(1)} %query.1.query_ref, bf16[8,192,128]{2,1,0:T(8,128)(2,1)S(1)} %constant_dynamic-update-slice_fusion.own_ref, bf16[8,192,128]{2,1,0:T(8,128)(2,1)S(1)} %collective-permute-done.21.other_ref), custom_call_target="tpu_custom_call" | custom-call | flops 167772160 | bytes 786432 | tf_op jit(solution)/shard_map/attend/pallas_call | solution.py:434
  79.9 1.4 %output.1 = (bf16[128,1536]{1,0:T(8,128)(2,1)S(1)}, bf16[128,1536]{1,0:T(8,128)(2,1)S(1)}, bf16[16,256]{1,0:T(8,128)(2,1)S(1)}) custom-call(bf16[2,256,192]{2,1,0:T(8,128)(2,1)S(1)} %attend.1.attended_ref, bf16[8,128,192]{2,1,0:T(8,128)(2,1)S(1)} %get-tuple-element.36.embedded_ref, bf16[1536,256]{1,0:T(8,128)(2,1)S(1)} %copy-done.1, ...), custom_call_target="tpu_custom_call" | custom-call | flops 301989888 | bytes 1179648 | tf_op jit(solution)/shard_map/output/pallas_call | solution.py:448
  81.3 1.4 %collective-permute-start.24 = (bf16[16,256]{1,0:T(8,128)(2,1)S(1)}, bf16[16,256]{1,0:T(8,128)(2,1)S(1)}, u32[]{:S(2)}, u32[]{:S(2)}) collective-permute-start(bf16[16,256]{1,0:T(8,128)(2,1)S(1)} %get-tuple-element.47), channel_id=1, source_target_pairs={{0,2},{2,0},{4,6},{6,4},{8,10},{10,8},{12,14},{14,12},{1,3},{3,1},... | collective-permute-start | bytes 24584 | tf_op jit(solution)/shard_map/ppermute | solution.py:463
  82.6 2.3 %collective-permute-done.24 = bf16[16,256]{1,0:T(8,128)(2,1)S(1)} collective-permute-done((bf16[16,256]{1,0:T(8,128)(2,1)S(1)}, bf16[16,256]{1,0:T(8,128)(2,1)S(1)}, u32[]{:S(2)}, u32[]{:S(2)}) %collective-permute-start.24) | collective-permute-done | bytes 8224 | tf_op jit(solution)/shard_map/ppermute | solution.py:463
  85.2 1.4 %collective-permute-start.23 = (bf16[64,1536]{1,0:T(8,128)(2,1)S(1)}, bf16[64,1536]{1,0:T(8,128)(2,1)S(1)}, u32[]{:S(2)}, u32[]{:S(2)}) collective-permute-start(bf16[64,1536]{1,0:T(8,128)(2,1)S(1)} %get-tuple-element.54), channel_id=1, source_target_pairs={{0,2},{2,0},{4,6},{6,4},{8,10},{10,8},{12,14},{14,12},{1,3},{3,1},... | collective-permute-start | bytes 589832 | tf_op jit(solution)/shard_map/ppermute | solution.py:470
  86.6 3.6 %collective-permute-done.26 = bf16[16,256]{1,0:T(8,128)(2,1)S(1)} collective-permute-done((bf16[16,256]{1,0:T(8,128)(2,1)S(1)}, bf16[16,256]{1,0:T(8,128)(2,1)S(1)}, u32[]{:S(2)}, u32[]{:S(2)}) %collective-permute-start.26) | collective-permute-done | bytes 8224 | tf_op jit(solution)/shard_map/ppermute | solution.py:472
  90.3 2.3 %collective-permute-done.23.refs_1_ = bf16[64,1536]{1,0:T(8,128)(2,1)S(1)} collective-permute-done((bf16[64,1536]{1,0:T(8,128)(2,1)S(1)}, bf16[64,1536]{1,0:T(8,128)(2,1)S(1)}, u32[]{:S(2)}, u32[]{:S(2)}) %collective-permute-start.23) | collective-permute-done | bytes 196640 | tf_op jit(solution)/shard_map/ppermute | solution.py:470
  92.6 2.7 %collective-permute-start.27 = (bf16[32,256]{1,0:T(8,128)(2,1)S(1)}, bf16[32,256]{1,0:T(8,128)(2,1)S(1)}, u32[]{:S(2)}, u32[]{:S(2)}) collective-permute-start(bf16[32,256]{1,0:T(8,128)(2,1)S(1)} %pad_maximum_fusion.4), channel_id=1, source_target_pairs={{0,8},{2,10},{4,12},{6,14},{9,1},{11,3},{13,5},{15,7},{16,24},{18,... | collective-permute-start | bytes 49160 | tf_op jit(solution)/shard_map/ppermute | solution.py:475
  95.3 0.8 tokens.1
  96.8 0.8 pair.1
  (58 shorter events, 3.9 us)
Async XLA Ops:
  0.6 0.9 copy-start
  2.7 15.4 %collective-permute-start = (bf16[192,896]{1,0:T(8,128)(2,1)S(1)}, bf16[192,896]{1,0:T(8,128)(2,1)S(1)}, u32[]{:S(2)}, u32[]{:S(2)}) collective-permute-start(bf16[192,896]{1,0:T(8,128)(2,1)S(1)} %pad_maximum_fusion.1.refs_0_), channel_id=1, source_target_pairs={{0,4},{2,6},{4,12},{6,14},{12,8},{14,10},{8,0},{10,2},{20,16},{22,... | collective-permute-start | bytes 1032200 | tf_op jit(solution)/shard_map/ppermute | solution.py:86
  5.8 12.4 %collective-permute-start.1 = (bf16[192,896]{1,0:T(8,128)(2,1)S(1)}, bf16[192,896]{1,0:T(8,128)(2,1)S(1)}, u32[]{:S(2)}, u32[]{:S(2)}) collective-permute-start(bf16[192,896]{1,0:T(8,128)(2,1)S(1)} %pad_maximum_fusion.1.refs_0_), channel_id=1, source_target_pairs={{0,2},{2,0},{4,6},{6,4},{8,10},{10,8},{12,14},{14,12},{1,3},{3,1},... | collective-permute-start | bytes 1032200 | tf_op jit(solution)/shard_map/ppermute | solution.py:89
  8.6 5.9 %collective-permute-start.2 = (bf16[2,704]{1,0:T(2,128)(2,1)S(1)}, bf16[2,704]{1,0:T(2,128)(2,1)S(1)}, u32[]{:S(2)}, u32[]{:S(2)}) collective-permute-start(bf16[2,704]{1,0:T(2,128)(2,1)S(1)} %copy.14), channel_id=1, source_target_pairs={{0,2},{2,4},{4,6},{6,8},{8,10},{10,12},{12,14},{1,3},{3,5},{5,7},{... | collective-permute-start | bytes 8456 | tf_op jit(solution)/shard_map/ppermute | solution.py:327
  11.1 7.0 %collective-permute-start.3 = (bf16[2,704]{1,0:T(2,128)(2,1)S(1)}, bf16[2,704]{1,0:T(2,128)(2,1)S(1)}, u32[]{:S(2)}, u32[]{:S(2)}) collective-permute-start(bf16[2,704]{1,0:T(2,128)(2,1)S(1)} %copy.15), channel_id=1, source_target_pairs={{2,0},{4,2},{6,4},{8,6},{10,8},{12,10},{14,12},{3,1},{5,3},{7,5},{... | collective-permute-start | bytes 8456 | tf_op jit(solution)/shard_map/ppermute | solution.py:328
  18.2 6.4 %collective-permute-start.4 = (bf16[704,512]{1,0:T(8,128)(2,1)}, bf16[704,512]{1,0:T(8,128)(2,1)S(1)}, u32[]{:S(2)}, u32[]{:S(2)}) collective-permute-start(bf16[704,512]{1,0:T(8,128)(2,1)} %bitcast.16), channel_id=1, source_target_pairs={{0,1},{1,0},{2,3},{3,2},{4,5},{5,4},{6,7},{7,6},{8,9},{9,8},{10,11... | collective-permute-start | bytes 2162696 | tf_op jit(solution)/shard_map/ppermute | solution.py:333
  18.2 29.4 %copy-start.6 = (f32[1536]{0:T(1024)S(1)}, f32[1536]{0:T(1024)}, u32[]{:S(2)}) copy-start(f32[1536]{0:T(1024)} %param.14) | copy-start | bytes 18436
  18.2 4.2 %collective-permute-start.5 = (bf16[16,704]{1,0:T(8,128)(2,1)S(1)}, bf16[16,704]{1,0:T(8,128)(2,1)S(1)}, u32[]{:S(2)}, u32[]{:S(2)}) collective-permute-start(bf16[16,704]{1,0:T(8,128)(2,1)S(1)} %fusion.2), channel_id=1, source_target_pairs={{0,1},{1,0},{2,3},{3,2},{4,5},{5,4},{6,7},{7,6},{8,9},{9,8},{10,11... | collective-permute-start | bytes 67592 | tf_op jit(solution)/shard_map/ppermute | solution.py:335
  19.5 15.3 %collective-permute-start.6 = (bf16[192,896]{1,0:T(8,128)(2,1)S(1)}, bf16[192,896]{1,0:T(8,128)(2,1)S(1)}, u32[]{:S(2)}, u32[]{:S(2)}) collective-permute-start(bf16[192,896]{1,0:T(8,128)(2,1)S(1)} %collective-permute-done.refs_2_), channel_id=1, source_target_pairs={{0,16},{16,0},{1,17},{17,1},{2,18},{18,2},{3,19},{19,3},{4,20},{20... | collective-permute-start | bytes 1032200 | tf_op jit(solution)/shard_map/ppermute | solution.py:92
  20.4 14.4 %collective-permute-start.8 = (bf16[192,896]{1,0:T(8,128)(2,1)S(1)}, bf16[192,896]{1,0:T(8,128)(2,1)S(1)}, u32[]{:S(2)}, u32[]{:S(2)}) collective-permute-start(bf16[192,896]{1,0:T(8,128)(2,1)S(1)} %collective-permute-done.refs_2_), channel_id=1, source_target_pairs={{0,2},{2,0},{4,6},{6,4},{8,10},{10,8},{12,14},{14,12},{1,3},{3,1},... | collective-permute-start | bytes 1032200 | tf_op jit(solution)/shard_map/ppermute | solution.py:89
  22.5 14.4 %collective-permute-start.10 = (bf16[192,896]{1,0:T(8,128)(2,1)S(1)}, bf16[192,896]{1,0:T(8,128)(2,1)S(1)}, u32[]{:S(2)}, u32[]{:S(2)}) collective-permute-start(bf16[192,896]{1,0:T(8,128)(2,1)S(1)} %collective-permute-done.refs_2_), channel_id=1, source_target_pairs={{0,4},{2,6},{4,12},{6,14},{12,8},{14,10},{8,0},{10,2},{20,16},{22,... | collective-permute-start | bytes 1032200 | tf_op jit(solution)/shard_map/ppermute | solution.py:86
  24.6 1.1 %copy-start.4 = (bf16[512,704]{0,1:T(8,128)(2,1)S(1)}, bf16[512,704]{0,1:T(8,128)(2,1)}, u32[]{:S(2)}) copy-start(bf16[512,704]{0,1:T(8,128)(2,1)} %param.10) | copy-start | bytes 2162692
  28.5 51.3 %copy-start.1 = (bf16[1536,256]{1,0:T(8,128)(2,1)S(1)}, bf16[1536,256]{1,0:T(8,128)(2,1)}, u32[]{:S(2)}) copy-start(bf16[1536,256]{1,0:T(8,128)(2,1)} %pair_weight_ref.1) | copy-start | bytes 2359300
  34.8 62.0 %copy-start.5 = (bf16[128,128]{1,0:T(8,128)(2,1)S(1)}, bf16[128,128]{1,0:T(8,128)(2,1)}, u32[]{:S(2)}) copy-start(bf16[128,128]{1,0:T(8,128)(2,1)} %weight_ref.1) | copy-start | bytes 98308
  34.8 9.2 %collective-permute-start.9 = (bf16[192,896]{1,0:T(8,128)(2,1)S(1)}, bf16[192,896]{1,0:T(8,128)(2,1)S(1)}, u32[]{:S(2)}, u32[]{:S(2)}) collective-permute-start(bf16[192,896]{1,0:T(8,128)(2,1)S(1)} %collective-permute-done.8.refs_3_), channel_id=1, source_target_pairs={{0,16},{16,0},{1,17},{17,1},{2,18},{18,2},{3,19},{19,3},{4,20},{20... | collective-permute-start | bytes 1032200 | tf_op jit(solution)/shard_map/ppermute | solution.py:92
  35.3 9.8 %collective-permute-start.11 = (bf16[192,896]{1,0:T(8,128)(2,1)S(1)}, bf16[192,896]{1,0:T(8,128)(2,1)S(1)}, u32[]{:S(2)}, u32[]{:S(2)}) collective-permute-start(bf16[192,896]{1,0:T(8,128)(2,1)S(1)} %collective-permute-done.8.refs_3_), channel_id=1, source_target_pairs={{0,4},{2,6},{4,12},{6,14},{12,8},{14,10},{8,0},{10,2},{20,16},{22,... | collective-permute-start | bytes 1032200 | tf_op jit(solution)/shard_map/ppermute | solution.py:86
  36.9 6.5 %collective-permute-start.7 = (bf16[192,640]{1,0:T(8,128)(2,1)S(1)}, bf16[192,640]{1,0:T(8,128)(2,1)S(1)}, u32[]{:S(2)}, u32[]{:S(2)}) collective-permute-start(bf16[192,640]{1,0:T(8,128)(2,1)S(1)} %pad_maximum_fusion.2), channel_id=1, source_target_pairs={{0,2},{2,0},{4,6},{6,4},{8,10},{10,8},{12,14},{14,12},{1,3},{3,1},... | collective-permute-start | bytes 737288 | tf_op jit(solution)/shard_map/ppermute | solution.py:371
  46.8 2.1 %collective-permute-start.12 = (bf16[8,128,192]{2,1,0:T(8,128)(2,1)}, bf16[8,128,192]{2,1,0:T(8,128)(2,1)S(1)}, u32[]{:S(2)}, u32[]{:S(2)}) collective-permute-start(bf16[8,128,192]{2,1,0:T(8,128)(2,1)} %get-tuple-element.34.part_ref), channel_id=1, source_target_pairs={{0,1},{1,0},{2,3},{3,2},{4,5},{5,4},{6,7},{7,6},{8,9},{9,8},{10,11... | collective-permute-start | bytes 1179656 | tf_op jit(solution)/shard_map/ppermute | solution.py:393
  46.9 15.1 %collective-permute-start.14 = (bf16[384,640]{1,0:T(8,128)(2,1)S(1)}, bf16[384,640]{1,0:T(8,128)(2,1)S(1)}, u32[]{:S(2)}, u32[]{:S(2)}) collective-permute-start(bf16[384,640]{1,0:T(8,128)(2,1)S(1)} %pad_maximum_fusion.refs_2_.refs_0_), channel_id=1, source_target_pairs={{0,4},{2,6},{4,12},{6,14},{12,8},{14,10},{8,0},{10,2},{20,16},{22,... | collective-permute-start | bytes 1474568 | tf_op jit(solution)/shard_map/ppermute | solution.py:86
  48.9 0.8 copy-start.2
  49.8 1.0 %copy-start.3 = (bf16[8,128,192]{2,1,0:T(8,128)(2,1)S(1)}, bf16[8,128,192]{2,1,0:T(8,128)(2,1)}, u32[]{:S(2)}) copy-start(bf16[8,128,192]{2,1,0:T(8,128)(2,1)} %copy-done.2) | copy-start | bytes 1179652
  52.5 11.2 %collective-permute-start.13 = (bf16[128,1536]{1,0:T(8,128)(2,1)S(1)}, bf16[128,1536]{1,0:T(8,128)(2,1)S(1)}, u32[]{:S(2)}, u32[]{:S(2)}) collective-permute-start(bf16[128,1536]{1,0:T(8,128)(2,1)S(1)} %get-tuple-element.38), channel_id=1, source_target_pairs={{0,2},{2,0},{4,6},{6,4},{8,10},{10,8},{12,14},{14,12},{1,3},{3,1},... | collective-permute-start | bytes 1179656 | tf_op jit(solution)/shard_map/ppermute | solution.py:412
  53.5 12.1 %collective-permute-start.17 = (bf16[192,128]{1,0:T(8,128)(2,1)S(1)}, bf16[192,128]{1,0:T(8,128)(2,1)S(1)}, u32[]{:S(2)}, u32[]{:S(2)}) collective-permute-start(bf16[192,128]{1,0:T(8,128)(2,1)S(1)} %get-tuple-element.41), channel_id=1, source_target_pairs={{0,4},{2,6},{4,12},{6,14},{12,8},{14,10},{8,0},{10,2},{1,5},{3,7},... | collective-permute-start | bytes 147464 | tf_op jit(solution)/shard_map/ppermute | solution.py:411
  54.8 10.9 %collective-permute-start.18 = (bf16[192,128]{1,0:T(8,128)(2,1)S(1)}, bf16[192,128]{1,0:T(8,128)(2,1)S(1)}, u32[]{:S(2)}, u32[]{:S(2)}) collective-permute-start(bf16[192,128]{1,0:T(8,128)(2,1)S(1)} %get-tuple-element.41), channel_id=1, source_target_pairs={{0,8},{2,10},{4,0},{6,2},{12,4},{14,6},{8,12},{10,14},{1,9},{3,11}... | collective-permute-start | bytes 147464 | tf_op jit(solution)/shard_map/ppermute | solution.py:411
  56.5 9.2 %collective-permute-start.19 = (bf16[192,128]{1,0:T(8,128)(2,1)S(1)}, bf16[192,128]{1,0:T(8,128)(2,1)S(1)}, u32[]{:S(2)}, u32[]{:S(2)}) collective-permute-start(bf16[192,128]{1,0:T(8,128)(2,1)S(1)} %get-tuple-element.41), channel_id=1, source_target_pairs={{0,12},{2,14},{4,8},{6,10},{12,0},{14,2},{8,4},{10,6},{1,13},{3,15... | collective-permute-start | bytes 147464 | tf_op jit(solution)/shard_map/ppermute | solution.py:411
  63.8 12.4 %collective-permute-start.15 = (bf16[384,640]{1,0:T(8,128)(2,1)S(1)}, bf16[384,640]{1,0:T(8,128)(2,1)S(1)}, u32[]{:S(2)}, u32[]{:S(2)}) collective-permute-start(bf16[384,640]{1,0:T(8,128)(2,1)S(1)} %collective-permute-done.14.refs_3_.refs_1_), channel_id=1, source_target_pairs={{0,16},{16,0},{1,17},{17,1},{2,18},{18,2},{3,19},{19,3},{4,20},{20... | collective-permute-start | bytes 1474568 | tf_op jit(solution)/shard_map/ppermute | solution.py:92
  64.7 13.2 %collective-permute-start.16 = (bf16[384,640]{1,0:T(8,128)(2,1)S(1)}, bf16[384,640]{1,0:T(8,128)(2,1)S(1)}, u32[]{:S(2)}, u32[]{:S(2)}) collective-permute-start(bf16[384,640]{1,0:T(8,128)(2,1)S(1)} %collective-permute-done.14.refs_3_.refs_1_), channel_id=1, source_target_pairs={{0,4},{2,6},{4,12},{6,14},{12,8},{14,10},{8,0},{10,2},{20,16},{22,... | collective-permute-start | bytes 1474568 | tf_op jit(solution)/shard_map/ppermute | solution.py:86
  65.8 5.7 %collective-permute-start.20 = (bf16[4,192,128]{2,1,0:T(8,128)(2,1)S(1)}, bf16[4,192,128]{2,1,0:T(8,128)(2,1)S(1)}, u32[]{:S(2)}, u32[]{:S(2)}) collective-permute-start(bf16[4,192,128]{2,1,0:T(8,128)(2,1)S(1)} %pad_maximum_fusion.3), channel_id=1, source_target_pairs={{0,2},{2,0},{4,6},{6,4},{8,10},{10,8},{12,14},{14,12},{1,3},{3,1},... | collective-permute-start | bytes 589832 | tf_op jit(solution)/shard_map/ppermute | solution.py:418
  71.5 6.9 %collective-permute-start.21 = (bf16[8,192,128]{2,1,0:T(8,128)(2,1)S(1)}, bf16[8,192,128]{2,1,0:T(8,128)(2,1)S(1)}, u32[]{:S(2)}, u32[]{:S(2)}) collective-permute-start(bf16[8,192,128]{2,1,0:T(8,128)(2,1)S(1)} %constant_dynamic-update-slice_fusion.own_ref), channel_id=1, source_target_pairs={{0,1},{1,0},{2,3},{3,2},{4,5},{5,4},{6,7},{7,6},{8,9},{9,8},{10,11... | collective-permute-start | bytes 1179656 | tf_op jit(solution)/shard_map/ppermute | solution.py:421
  81.3 3.7 %collective-permute-start.24 = (bf16[16,256]{1,0:T(8,128)(2,1)S(1)}, bf16[16,256]{1,0:T(8,128)(2,1)S(1)}, u32[]{:S(2)}, u32[]{:S(2)}) collective-permute-start(bf16[16,256]{1,0:T(8,128)(2,1)S(1)} %get-tuple-element.47), channel_id=1, source_target_pairs={{0,2},{2,0},{4,6},{6,4},{8,10},{10,8},{12,14},{14,12},{1,3},{3,1},... | collective-permute-start | bytes 24584 | tf_op jit(solution)/shard_map/ppermute | solution.py:463
  82.6 2.4 %collective-permute-start.22 = (bf16[128,1536]{1,0:T(8,128)(2,1)S(1)}, bf16[128,1536]{1,0:T(8,128)(2,1)S(1)}, u32[]{:S(2)}, u32[]{:S(2)}) collective-permute-start(bf16[128,1536]{1,0:T(8,128)(2,1)S(1)} %get-tuple-element.46), channel_id=1, source_target_pairs={{0,1},{1,0},{2,3},{3,2},{4,5},{5,4},{6,7},{7,6},{8,9},{9,8},{10,11... | collective-permute-start | bytes 1179656 | tf_op jit(solution)/shard_map/ppermute | solution.py:466
  85.0 1.6 %collective-permute-start.25 = (bf16[16,256]{1,0:T(8,128)(2,1)S(1)}, bf16[16,256]{1,0:T(8,128)(2,1)S(1)}, u32[]{:S(2)}, u32[]{:S(2)}) collective-permute-start(bf16[16,256]{1,0:T(8,128)(2,1)S(1)} %add_convert_fusion.2), channel_id=1, source_target_pairs={{0,1},{1,0},{2,3},{3,2},{4,5},{5,4},{6,7},{7,6},{8,9},{9,8},{10,11... | collective-permute-start | bytes 24584 | tf_op jit(solution)/shard_map/ppermute | solution.py:465
  85.2 7.4 %collective-permute-start.23 = (bf16[64,1536]{1,0:T(8,128)(2,1)S(1)}, bf16[64,1536]{1,0:T(8,128)(2,1)S(1)}, u32[]{:S(2)}, u32[]{:S(2)}) collective-permute-start(bf16[64,1536]{1,0:T(8,128)(2,1)S(1)} %get-tuple-element.54), channel_id=1, source_target_pairs={{0,2},{2,0},{4,6},{6,4},{8,10},{10,8},{12,14},{14,12},{1,3},{3,1},... | collective-permute-start | bytes 589832 | tf_op jit(solution)/shard_map/ppermute | solution.py:470
  86.6 3.7 %collective-permute-start.26 = (bf16[16,256]{1,0:T(8,128)(2,1)S(1)}, bf16[16,256]{1,0:T(8,128)(2,1)S(1)}, u32[]{:S(2)}, u32[]{:S(2)}) collective-permute-start(bf16[16,256]{1,0:T(8,128)(2,1)S(1)} %add_convert_fusion.1), channel_id=1, source_target_pairs={{0,4},{2,6},{4,0},{6,2},{8,12},{10,14},{12,8},{14,10},{1,5},{3,7},... | collective-permute-start | bytes 24584 | tf_op jit(solution)/shard_map/ppermute | solution.py:472
  92.6 4.2 %collective-permute-start.27 = (bf16[32,256]{1,0:T(8,128)(2,1)S(1)}, bf16[32,256]{1,0:T(8,128)(2,1)S(1)}, u32[]{:S(2)}, u32[]{:S(2)}) collective-permute-start(bf16[32,256]{1,0:T(8,128)(2,1)S(1)} %pad_maximum_fusion.4), channel_id=1, source_target_pairs={{0,8},{2,10},{4,12},{6,14},{9,1},{11,3},{13,5},{15,7},{16,24},{18,... | collective-permute-start | bytes 49160 | tf_op jit(solution)/shard_map/ppermute | solution.py:475
